TPU v7x, 32 devices: a whole 2x2x4 slice. The times are simulated.
32 devices in a mesh: rep: 8 (over z, core), shard: 4 (over y, x).
Axes of the slice: x: 2, y: 2, z: 4, core: 2. Of those that a mesh axis runs over, the one named last changes fastest.
Arguments:
- inputs: bfloat16 [8, 512, 8192], P('rep', 'shard'), may hold values from -6 to 6
- target: bfloat16 [8, 512, 512], P('rep', 'shard'), may hold values from -6 to 6
- weights: bfloat16 [8, 8192, 512], P('rep', 'shard'), may hold values from -0.0625 to 0.0625
- feedback: bfloat16 [8, 8192, 512], P('rep', 'shard'), may hold values from -6 to 6
- counts: int32 [8, 4], P('rep', 'shard'), may hold values from 16 to 128, as said below
- blocks: int32 [8, 4, 128], P('rep', 'shard'), may hold values from 0 to 8191, as said below
Outputs:
- outer_update: float32 [8192, 512], P('shard')
- new_feedback: bfloat16 [8, 8192, 512], P('rep', 'shard')
Inputs may be any that keep to these rules, and one draw needn't show every extreme that they name: `counts`: in every shard index some replica keeps exactly 128 blocks. The 128 slots of one device hold distinct block numbers; only the first counts slots are kept; the others hold block numbers that this device does not keep (other replicas may keep them). All replicas of one shard index draw all their slots from a common set of 512 blocks.
All inputs are finite; a program needn't handle non-finite values.
Results may differ from a plain program's by a relative error of at most 0.0034.
Values may be sent and summed in bfloat16 or wider, within the bound.
No kernel may reach another device: no remote copies, remote signals or barrier semaphores. Data moves between devices by JAX's collectives and lax.ppermute only.
A program may use at most 64 MiB of HBM per device.

v0:
```python
import jax
import jax.numpy as jnp
from jax import lax
from jax.sharding import PartitionSpec as P


def on_device(inputs, target, weights, feedback, counts, blocks):
    tokens = inputs[0]
    rows_w = weights[0]
    tok_dev = tokens.shape[0]
    n_rep = lax.axis_size("rep")
    columns = lax.all_to_all(tokens, "shard", split_axis=1, concat_axis=0, tiled=True)
    window = tokens
    key_proj = jnp.dot(
        window,
        lax.all_gather(rows_w, "shard", axis=0, tiled=True),
        preferred_element_type=jnp.float32,
    )
    slopes = ((key_proj - target[0].astype(jnp.float32)) / tok_dev).astype(jnp.bfloat16)
    window = columns
    gradient = lax.dot_general(
        window,
        lax.all_gather(slopes, "shard", axis=0, tiled=True),
        (((0,), (0,)), ((), ())),
        preferred_element_type=jnp.float32,
    )
    pseudo = gradient + feedback[0].astype(jnp.float32)
    flattened = pseudo.reshape(-1, 128)
    n_blocks = flattened.shape[0]
    slot_list = blocks[0, 0]
    slot_total = slot_list.shape[0]
    in_use = (jnp.arange(slot_total, dtype=jnp.int32) < counts[0, 0]).astype(jnp.float32)
    chosen_values = flattened[slot_list] * in_use[:, None]
    kept_mask = jnp.zeros((n_blocks,), jnp.float32).at[slot_list].add(in_use)
    residue = jnp.where(kept_mask[:, None] > 0, jnp.zeros_like(flattened), flattened)
    new_feedback = residue.reshape(rows_w.shape).astype(jnp.bfloat16)
    all_values, all_slots = (
        lax.all_gather(chosen_values, "rep", axis=0, tiled=True),
        lax.all_gather(slot_list.astype(jnp.float32), "rep", axis=0, tiled=True),
    )
    summed = jnp.zeros((n_blocks, 128), jnp.float32).at[all_slots.astype(jnp.int32)].add(all_values)
    outer_update = (summed / n_rep).reshape(rows_w.shape)
    return (outer_update, new_feedback[None])


def solution(mesh):
    placed = (
        P("rep", "shard", None),
        P("rep", "shard", None),
        P("rep", "shard", None),
        P("rep", "shard", None),
        P("rep", "shard"),
        P("rep", "shard", None),
    )
    return jax.shard_map(
        on_device,
        mesh=mesh,
        in_specs=placed,
        out_specs=(P("shard", None), P("rep", "shard", None)),
        check_vma=False,
    )
```

profile of v0, /device:TPU:1, one launch (start us, length us, event | category | flops | bytes accessed | tf_op | source)
XLA Modules:
  0.0 191.7 jit_solution(17572817173326428322)
XLA Ops:
  7.2 0.0 all-gather.4.cloned.1.call-start
  7.2 0.7 all-gather.4.cloned.1.call-update
  7.9 0.0 copy-start.4
  7.9 4.1 %copy.14 = bf16[1,128,8192]{1,2,0:T(8,128)(2,1)} copy(bf16[1,128,8192]{2,1,0:T(8,128)(2,1)} %param.6) | data formatting | bytes 4194304 | tf_op args[0]
  12.0 4.5 %all-to-all-start = ((bf16[128,4,2048]{0,2,1:T(8,128)(2,1)}), bf16[128,4,2048]{0,2,1:T(8,128)(2,1)}, u32[]{:S(2)}, u32[]{:S(2)}) async-start(bf16[128,4,2048]{0,2,1:T(8,128)(2,1)} %bitcast.4), calls=%async_computation | async-start | bytes 4194304 | tf_op jit(solution)/shard_map/all_to_all | solution.py:12
  17.1 0.0 copy-done.4
  17.1 13.2 %all-gather = f32[1,1,1024]{2,1,0:T(1,128)S(1)} all-gather(f32[1,1,128]{2,1,0:T(1,128)S(1)} %convert_element_type.34), channel_id=2, replica_groups=mesh['rep'=8,'shard'=4] {'rep'}, dimensions={2}, use_global_device_ids=true | all-gather | bytes 4608 | tf_op jit(solution)/shard_map/all_gather | solution.py:39
  30.4 1.3 scatter_custom_fusion.1
  31.7 1.1 broadcast_in_dim.27
  32.9 0.4 copy.18
  33.2 0.0 copy-start
  33.2 0.0 copy-start.3
  33.2 4.1 %copy.16 = bf16[1,2048,512]{1,2,0:T(8,128)(2,1)} copy(bf16[1,2048,512]{2,1,0:T(8,128)(2,1)} %param.9) | data formatting | bytes 4194304 | tf_op args[3]
  37.3 21.9 %all-to-all-done = bf16[128,4,2048]{0,2,1:T(8,128)(2,1)} async-done(((bf16[128,4,2048]{0,2,1:T(8,128)(2,1)}), bf16[128,4,2048]{0,2,1:T(8,128)(2,1)}, u32[]{:S(2)}, u32[]{:S(2)}) %all-to-all-start) | async-done | bytes 2097184 | tf_op jit(solution)/shard_map/all_to_all | solution.py:12
  59.2 3.9 %copy.15 = bf16[4,128,2048]{2,1,0:T(8,128)(2,1)} copy(bf16[4,128,2048]{1,2,0:T(8,128)(2,1)} %bitcast.5) | data formatting | bytes 4194304 | tf_op jit(solution)/shard_map/all_to_all | solution.py:12
  63.2 54.9 %all-gather.4.cloned.1.call-done = bf16[1,8192,512]{2,1,0:T(8,128)(2,1)} async-done(((bf16[1,2048,512]{2,1,0:T(8,128)(2,1)}), bf16[1,8192,512]{2,1,0:T(8,128)(2,1)}) %all-gather.4.cloned.1.call-update) | async-done | bytes 8388624 | tf_op jit(solution)/shard_map/all_gather | solution.py:16
  118.1 0.0 copy-done
  118.1 0.0 copy-done.3
  118.1 4.8 %fusion.15 = bf16[128,512]{1,0:T(8,128)(2,1)S(1)} fusion(bf16[1,8192,512]{2,1,0:T(8,128)(2,1)} %all-gather.4.cloned.1.call-done, bf16[1,128,8192]{2,1,0:T(8,128)(2,1)S(1)} %copy-done, bf16[1,128,512]{2,1,0:T(8,128)(2,1)S(1)} %copy-done.3), kind=kOutput, calls=%fused_computation.13 | convolution fusion | flops 1074003968 | bytes 10747904 | tf_op jit(solution)/shard_map/dot_general | solution.py:14
  122.9 8.0 %all_gather.14 = bf16[512,512]{1,0:T(8,128)(2,1)S(1)} all-gather(bf16[128,512]{1,0:T(8,128)(2,1)S(1)} %fusion.15), channel_id=1, replica_groups=mesh['rep'=8,'shard'=4] {'shard'}, dimensions={0}, use_global_device_ids=true | all-gather | bytes 655360 | tf_op jit(solution)/shard_map/all_gather | solution.py:23
  130.9 0.0 copy-done.1
  130.9 0.0 copy-done.2
  130.9 3.5 %select_convert_fusion = (bf16[2048,512]{0,1:T(8,128)(2,1)S(1)}, f32[2048,512]{0,1:T(8,128)}) fusion(pred[2048,4]{0,1:T(4,128)(4,1)S(1)} %copy.18, bf16[1,2048,512]{1,2,0:T(8,128)(2,1)S(1)} %copy-done.1, bf16[512,512]{1,0:T(8,128)(2,1)S(1)} %all_gather.14, bf16[512,2048]{1,0:T(8,128)(2,1)S(1)} %bitcast.41), kind=kOutput, calls=%fused_computation.6 | convolution fusion | flops 1076887552 | bytes 11018240 | tf_op jit(solution)/shard_map/dot_general | solution.py:21
  134.4 2.5 %copy.19 = bf16[1,2048,512]{2,1,0:T(8,128)(2,1)} copy(bf16[1,2048,512]{1,2,0:T(8,128)(2,1)S(1)} %bitcast.42) | data formatting | bytes 4194304
  136.9 5.3 %copy.17 = f32[2048,512]{1,0:T(8,128)} copy(f32[2048,512]{0,1:T(8,128)} %get-tuple-element.9) | data formatting | bytes 8388608 | tf_op jit(solution)/shard_map/add | solution.py:27
  142.2 4.7 %reshape.58 = f32[8192,128]{1,0:T(8,128)} reshape(f32[2048,512]{1,0:T(8,128)} %copy.17) | data formatting | bytes 8388608 | tf_op jit(solution)/shard_map/reshape | solution.py:28
  146.9 2.8 %gather_fusion = f32[128,128]{1,0:T(8,128)S(1)} fusion(f32[8192,128]{1,0:T(8,128)} %reshape.58, s32[1024]{0:T(1024)S(1)} %pad_clamp_fusion), kind=kCustom, calls=%fused_computation | custom fusion | bytes 131584 | tf_op jit(solution)/shard_map/gather | solution.py:33
  149.8 0.1 broadcast_multiply_fusion.1
  149.8 17.4 %all_gather.15 = f32[1024,128]{1,0:T(8,128)S(1)} all-gather(f32[128,128]{1,0:T(8,128)S(1)} %broadcast_multiply_fusion.1), channel_id=1, replica_groups=mesh['rep'=8,'shard'=4] {'rep'}, dimensions={0}, use_global_device_ids=true | all-gather | bytes 589824 | tf_op jit(solution)/shard_map/all_gather | solution.py:38
  167.3 8.2 %scatter_custom_fusion = f32[8192,128]{1,0:T(8,128)} fusion(s32[1024]{0:T(1024)S(1)} %compare_select_fusion, f32[1024,128]{1,0:T(8,128)S(1)} %all_gather.15, f32[]{:T(128)} %constant.5.clone.1), kind=kCustom, calls=%fused_computation.9 | custom fusion | flops 131072 | bytes 4194308 | tf_op jit(solution)/shard_map/scatter-add | solution.py:41
  175.5 4.4 %broadcast_multiply_fusion = f32[8192,128]{1,0:T(8,128)} fusion(f32[8192,128]{1,0:T(8,128)} %scatter_custom_fusion), kind=kLoop, calls=%fused_computation.8 | loop fusion | flops 1048576 | bytes 8388608 | tf_op jit(solution)/shard_map/div | solution.py:42
  179.9 4.9 %reshape.59 = f32[2048,512]{1,0:T(8,128)} reshape(f32[8192,128]{1,0:T(8,128)} %broadcast_multiply_fusion) | data formatting | bytes 8388608 | tf_op jit(solution)/shard_map/reshape | solution.py:42
  (9 shorter events, 0.0 us)
Async XLA Ops:
  7.2 110.9 %all-gather.4.cloned.1.call-start = ((), (), s32[]{:S(2)}) async-start(), calls=%async_computation.1 | async-start | bytes 10485760 | tf_op jit(solution)/shard_map/all_gather | solution.py:16
  7.9 9.2 %copy-start.4 = (s32[1,1,128]{2,1,0:T(1,128)S(1)}, s32[1,1,128]{2,1,0:T(1,128)}, u32[]{:S(2)}) copy-start(s32[1,1,128]{2,1,0:T(1,128)} %param.11) | copy-start | bytes 1540
  12.0 47.3 %all-to-all-start = ((bf16[128,4,2048]{0,2,1:T(8,128)(2,1)}), bf16[128,4,2048]{0,2,1:T(8,128)(2,1)}, u32[]{:S(2)}, u32[]{:S(2)}) async-start(bf16[128,4,2048]{0,2,1:T(8,128)(2,1)} %bitcast.4), calls=%async_computation | async-start | bytes 4194304 | tf_op jit(solution)/shard_map/all_to_all | solution.py:12
  33.2 84.9 %copy-start = (bf16[1,128,8192]{2,1,0:T(8,128)(2,1)S(1)}, bf16[1,128,8192]{2,1,0:T(8,128)(2,1)}, u32[]{:S(2)}) copy-start(bf16[1,128,8192]{2,1,0:T(8,128)(2,1)} %param.6) | copy-start | bytes 6291460
  33.2 84.9 %copy-start.3 = (bf16[1,128,512]{2,1,0:T(8,128)(2,1)S(1)}, bf16[1,128,512]{2,1,0:T(8,128)(2,1)}, u32[]{:S(2)}) copy-start(bf16[1,128,512]{2,1,0:T(8,128)(2,1)} %param.7) | copy-start | bytes 393220
  118.1 12.8 %copy-start.1 = (bf16[1,2048,512]{1,2,0:T(8,128)(2,1)S(1)}, bf16[1,2048,512]{1,2,0:T(8,128)(2,1)}, u32[]{:S(2)}) copy-start(bf16[1,2048,512]{1,2,0:T(8,128)(2,1)} %copy.16) | copy-start | bytes 6291460
  118.1 12.8 %copy-start.2 = (bf16[4,128,2048]{2,1,0:T(8,128)(2,1)S(1)}, bf16[4,128,2048]{2,1,0:T(8,128)(2,1)}, u32[]{:S(2)}) copy-start(bf16[4,128,2048]{2,1,0:T(8,128)(2,1)} %copy.15) | copy-start | bytes 6291460
Sparse Core Ops, SparseCore 0:
  9.8 108.2 all-gather.3
where the time goes:
time: 192 us
  waiting for transfers between devices  77.6 us (40%)
  blocking collectives  38.6 us (20%)
  local copies, waits for them, and re-layouts  33.9 us (18%)
  between operations  14.8 us (8%)
  other arithmetic  14 us (7%)
  matrix products  8.25 us (4%)
  starting transfers between devices  4.53 us (2%)
    all_gather x1, waiting for transfers between devices, on_device(): lax.all_gather(rows_w, 'shard', axis=0, tiled=True)  54.9 us
    all_to_all x1, waiting for transfers between devices, on_device(): lax.all_to_all(tokens, 'shard', split_axis=1, concat_axis=0, tiled=True)  21.9 us
    all_gather x1, blocking collectives, on_device(): lax.all_gather(chosen_values, 'rep', axis=0, tiled=True)  17.4 us
    all_gather x1, blocking collectives, on_device(): lax.all_gather(slot_list.astype(jnp.float32), 'rep', axis=0, tiled=True)  13.2 us
    unnamed x13, local copies, waits for them, and re-layouts  10.6 us
    scatter-add x1, other arithmetic, on_device(): jnp.zeros((n_blocks, 128), jnp.float32).at[all_slots.astype(jnp.int32)]  8.25 us
    all_gather x1, blocking collectives, on_device(): lax.all_gather(slopes, 'shard', axis=0, tiled=True)  7.98 us
    add x1, local copies, waits for them, and re-layouts, on_device(): pseudo = gradient + feedback[0].astype(jnp.float32)  5.35 us
  transfers between devices with their start and end apart: 2, of which 2 were waited for; matrix products, arithmetic and copies ran while one was open for 8% of the time, Pallas kernels for 0%

commit v1 on v0

v1 whole, which is shorter than its diff:
```python
import functools

import jax
import jax.numpy as jnp
from jax import lax
from jax.experimental import pallas as pl
from jax.experimental.pallas import tpu as pltpu
from jax.sharding import PartitionSpec as P

LANES = 128
CHUNKS = 1
MIB = 1024 * 1024


def params(mib):
    return pltpu.CompilerParams(vmem_limit_bytes=mib * MIB)


def cost(flops, nbytes):
    return pl.CostEstimate(flops=int(flops), bytes_accessed=int(nbytes), transcendentals=0)


def swap(x, axis, n, d):
    return lax.ppermute(x, axis, [(i, i ^ d) for i in range(n)])


def project_kernel(*refs):
    n = (len(refs) - 2) // 2
    pieces, w, outs, x = refs[:n], refs[n], refs[n + 1 : 2 * n + 1], refs[-1]
    rows = pieces[0].shape[0]
    for d in range(n):
        x[d * rows : (d + 1) * rows, :] = pieces[d][...]
    full = jnp.dot(x[...], w[...], preferred_element_type=jnp.float32)
    for d in range(n):
        outs[d][...] = full[d * rows : (d + 1) * rows, :].astype(outs[d].dtype)


def project(pieces, w):
    n = len(pieces)
    rows, depth = pieces[0].shape
    kw = w.shape[1]
    return pl.pallas_call(
        project_kernel,
        out_shape=[
            jax.ShapeDtypeStruct((rows, kw), jnp.float32 if d == 0 else jnp.bfloat16)
            for d in range(n)
        ],
        scratch_shapes=[pltpu.VMEM((n * rows, depth), jnp.bfloat16)],
        compiler_params=params(24),
        cost_estimate=cost(2 * n * rows * depth * kw, 2 * depth * (n * rows + kw)),
        name="project",
    )(*pieces, w)


def pick_columns(wide, column):
    out = jnp.zeros((wide.shape[0], LANES), jnp.float32)
    for c in range(wide.shape[1] // LANES):
        out += jnp.where(column == c, wide[:, c * LANES : (c + 1) * LANES], 0.0)
    return out


def prepare_kernel(per_row, *refs):
    pieces, (slots, fb, xg, fbk, x) = refs[:-5], refs[-5:]
    rows, depth = pieces[0].shape
    for d in range(len(pieces)):
        x[d * rows : (d + 1) * rows, :] = pieces[d][...]
    cap = slots.shape[0]
    slot = slots[...]
    hot = slot // per_row == lax.broadcasted_iota(jnp.int32, (cap, depth), 1)
    hot = hot.astype(jnp.float32).astype(jnp.bfloat16)
    xg[...] = lax.dot_general(
        hot, x[...], (((1,), (1,)), ((), ())), preferred_element_type=jnp.float32
    ).astype(jnp.bfloat16)
    wide = jnp.dot(hot, fb[...], preferred_element_type=jnp.float32)
    fbk[...] = pick_columns(wide, slot % per_row)


def prepare(pieces, slots, fb):
    n = len(pieces)
    rows, depth = pieces[0].shape
    cap = slots.shape[0]
    kw = fb.shape[1]
    return pl.pallas_call(
        functools.partial(prepare_kernel, kw // LANES),
        out_shape=[
            jax.ShapeDtypeStruct((cap, n * rows), jnp.bfloat16),
            jax.ShapeDtypeStruct((cap, LANES), jnp.float32),
        ],
        scratch_shapes=[pltpu.VMEM((n * rows, depth), jnp.bfloat16)],
        compiler_params=params(24),
        cost_estimate=cost(2 * cap * depth * (n * rows + kw), 2 * depth * (n * rows + kw)),
        name="prepare",
    )(*pieces, slots, fb)


def kept_kernel(per_row, *refs):
    parts, (xg, fbk, slots, slot_row, count, out, s) = refs[:-7], refs[-7:]
    rows = parts[0].shape[0]
    cap = xg.shape[0]
    for d in range(len(parts)):
        s[d * rows : (d + 1) * rows, :] = parts[d][...]
    wide = jnp.dot(xg[...], s[...], preferred_element_type=jnp.float32)
    value = pick_columns(wide, slots[...] % per_row) + fbk[...]
    used = lax.broadcasted_iota(jnp.int32, (cap, LANES), 0) < count[0, 0]
    out[:cap, :] = jnp.where(used, value, 0.0).astype(jnp.bfloat16)
    tail = out.shape[0] - cap
    number = jnp.broadcast_to(slot_row[...], (tail, cap))
    line = lax.broadcasted_iota(jnp.int32, (tail, cap), 0)
    number = jnp.where(line == 0, number // LANES, number % LANES)
    out[cap:, :] = number.astype(jnp.float32).astype(jnp.bfloat16)


def kept(parts, xg, fbk, slots, slot_row, count):
    cap = slots.shape[0]
    rows, kw = parts[0].shape
    vmem = pl.BlockSpec(memory_space=pltpu.VMEM)
    return pl.pallas_call(
        functools.partial(kept_kernel, kw // LANES),
        out_shape=jax.ShapeDtypeStruct((cap + 16, LANES), jnp.bfloat16),
        in_specs=[vmem] * (len(parts) + 4) + [pl.BlockSpec(memory_space=pltpu.SMEM)],
        scratch_shapes=[pltpu.VMEM((len(parts) * rows, kw), jnp.bfloat16)],
        compiler_params=params(8),
        cost_estimate=cost(2 * cap * len(parts) * rows * kw, 2 * len(parts) * rows * kw),
        name="kept",
    )(*parts, xg, fbk, slots, slot_row, count)


def residue_kernel(n, per_row, *refs):
    pieces, parts = refs[:n], refs[n : 2 * n]
    fb, slots, slot_row, count, out, x, s = refs[2 * n :]
    step = pl.program_id(0)
    rows = pieces[0].shape[0]
    cap = slots.shape[0]
    tile, kw = out.shape

    @pl.when(step == 0)
    def _():
        for d in range(n):
            s[d * rows : (d + 1) * rows, :] = parts[d][...]

    for d in range(n):
        x[d * rows : (d + 1) * rows, :] = pieces[d][...]
    gradient = lax.dot_general(
        x[...], s[...], (((0,), (0,)), ((), ())), preferred_element_type=jnp.float32
    )
    pseudo = gradient + fb[...].astype(jnp.float32)
    line = lax.broadcasted_iota(jnp.int32, (tile, cap), 0) + step * tile
    hot = (slot_row[...] // per_row == line).astype(jnp.float32).astype(jnp.bfloat16)
    used = lax.broadcasted_iota(jnp.int32, (cap, kw), 0) < count[0, 0]
    group = lax.broadcasted_iota(jnp.int32, (cap, kw), 1) // LANES
    mark = jnp.where(used & (slots[...] % per_row == group), 1.0, 0.0).astype(jnp.bfloat16)
    mask = jnp.dot(hot, mark, preferred_element_type=jnp.float32)
    out[...] = jnp.where(mask > 0, 0.0, pseudo).astype(jnp.bfloat16)


def residue(pieces, parts, fb, slots, slot_row, count):
    n = len(pieces)
    rows, depth = pieces[0].shape
    kw = fb.shape[1]
    tile = min(depth, 512)
    full = lambda a: pl.BlockSpec(a.shape, lambda i: (0, 0))
    return pl.pallas_call(
        functools.partial(residue_kernel, n, kw // LANES),
        grid=(depth // tile,),
        out_shape=jax.ShapeDtypeStruct((depth, kw), jnp.bfloat16),
        in_specs=[pl.BlockSpec((rows, tile), lambda i: (0, i))] * n
        + [full(parts[0])] * n
        + [pl.BlockSpec((tile, kw), lambda i: (i, 0)), full(slots), full(slot_row)]
        + [pl.BlockSpec(memory_space=pltpu.SMEM)],
        out_specs=pl.BlockSpec((tile, kw), lambda i: (i, 0)),
        scratch_shapes=[
            pltpu.VMEM((n * rows, tile), jnp.bfloat16),
            pltpu.VMEM((n * rows, kw), jnp.bfloat16),
        ],
        compiler_params=params(24),
        cost_estimate=cost(2 * n * rows * depth * kw, 2 * depth * (n * rows + 2 * kw)),
        name="residue",
    )(*pieces, *parts, fb, slots, slot_row, count)


def outer_kernel(n, per_row, *refs):
    messages, (out, wide, lines) = refs[:n], refs[n:]
    step = pl.program_id(0)
    cap = messages[0].shape[0] - 16
    tile, kw = out.shape

    @pl.when(step == 0)
    def _():
        for k in range(n):
            tail = messages[k][cap:, :].astype(jnp.float32)
            number = (tail[0:1, :] * LANES + tail[1:2, :]).astype(jnp.int32)
            lines[:, k * cap : (k + 1) * cap] = jnp.broadcast_to(number // per_row, (8, cap))
            column = jnp.broadcast_to((number % per_row).astype(jnp.float32), (LANES, cap)).T
            value = messages[k][:cap, :].astype(jnp.float32)
            for c in range(per_row):
                wide[k * cap : (k + 1) * cap, c * LANES : (c + 1) * LANES] = jnp.where(
                    column == c, value, 0.0
                ).astype(jnp.bfloat16)

    line = lax.broadcasted_iota(jnp.int32, (tile, n * cap), 0) + step * tile
    hot = (lines[0:1, :] == line).astype(jnp.float32).astype(jnp.bfloat16)
    out[...] = jnp.dot(hot, wide[...], preferred_element_type=jnp.float32) / n


def outer(messages, depth, kw):
    n = len(messages)
    cap = messages[0].shape[0] - 16
    tile = min(depth, 256)
    return pl.pallas_call(
        functools.partial(outer_kernel, n, kw // LANES),
        grid=(depth // tile,),
        out_shape=jax.ShapeDtypeStruct((depth, kw), jnp.float32),
        in_specs=[pl.BlockSpec(messages[0].shape, lambda i: (0, 0))] * n,
        out_specs=pl.BlockSpec((tile, kw), lambda i: (i, 0)),
        scratch_shapes=[
            pltpu.VMEM((n * cap, kw), jnp.bfloat16),
            pltpu.VMEM((8, n * cap), jnp.int32),
        ],
        compiler_params=params(24),
        cost_estimate=cost(2 * n * cap * depth * kw, 4 * depth * kw),
        name="outer",
    )(*messages)


def on_device(inputs, target, weights, feedback, counts, blocks):
    tokens, w, fb = inputs[0], weights[0], feedback[0]
    n_shard, n_rep = lax.axis_size("shard"), lax.axis_size("rep")
    me = lax.axis_index("shard")
    tok_dev = tokens.shape[0]
    depth, kw = w.shape
    rows = tok_dev // CHUNKS
    slot_row = blocks[0]
    slots = blocks.reshape(-1, 1)

    pieces = []
    for c in range(CHUNKS):
        mine = [
            lax.dynamic_slice(tokens, (c * rows, (me ^ d) * depth), (rows, depth))
            for d in range(n_shard)
        ]
        pieces.append(mine[:1] + [swap(mine[d], "shard", n_shard, d) for d in range(1, n_shard)])
    parts = []
    for c in range(CHUNKS):
        products = project(pieces[c], w)
        key_proj = products[0]
        for d in range(1, n_shard):
            key_proj = key_proj + swap(products[d], "shard", n_shard, d).astype(jnp.float32)
        goal = target[0, c * rows : (c + 1) * rows].astype(jnp.float32)
        slope = ((key_proj - goal) / tok_dev).astype(jnp.bfloat16)
        parts += [slope] + [swap(slope, "shard", n_shard, d) for d in range(1, n_shard)]
    pieces = [p for chunk in pieces for p in chunk]
    xg, fbk = prepare(pieces, slots, fb)
    message = kept(parts, xg, fbk, slots, slot_row, counts)
    messages = [message] + [swap(message, "rep", n_rep, d) for d in range(1, n_rep)]
    new_feedback = residue(pieces, parts, fb, slots, slot_row, counts)
    return outer(messages, depth, kw), new_feedback[None]


def solution(mesh):
    placed = (
        P("rep", "shard", None),
        P("rep", "shard", None),
        P("rep", "shard", None),
        P("rep", "shard", None),
        P("rep", "shard"),
        P("rep", "shard", None),
    )
    return jax.shard_map(
        on_device,
        mesh=mesh,
        in_specs=placed,
        out_specs=(P("shard", None), P("rep", "shard", None)),
        check_vma=False,
    )
```

time: 192 us -> 69.2 us (0.36)
  waiting for transfers between devices: 77.6 us -> 30.6 us
  blocking collectives: 38.6 us -> 0 us
  local copies, waits for them, and re-layouts: 33.9 us -> 4.04 us
  starting transfers between devices: 4.53 us -> 18.6 us
  other arithmetic: 14 us -> 0.09 us
  Pallas kernels: 0 us -> 13.9 us
  between operations: 14.8 us -> 1.44 us
  matrix products: 8.25 us -> 0 us
    all_gather x1 -> x0, waiting for transfers between devices: 54.9 us -> none  [on_device(): lax.all_gather(rows_w, 'shard', axis=0, tiled=True)]
    all_gather x3 -> x0, blocking collectives: 38.6 us -> none  [the longest x1 17.4 us: on_device(): lax.all_gather(chosen_values, 'rep', axis=0, tiled=True)]
    ppermute x0 -> x16, waiting for transfers between devices: none -> 30.6 us  [swap(): return lax.ppermute(x, axis, [(i, i ^ d) for i in range(n)])]
    all_to_all x1 -> x0, waiting for transfers between devices: 21.9 us -> none  [on_device(): lax.all_to_all(tokens, 'shard', split_axis=1, concat_axis=0, tiled=True)]
    ppermute x0 -> x16, starting transfers between devices: none -> 18.6 us  [swap(): return lax.ppermute(x, axis, [(i, i ^ d) for i in range(n)])]
    pallas_call x0 -> x5, Pallas kernels: none -> 13.9 us  [the longest x1 5.74 us: outer(): pl.pallas_call(functools.partial(outer_kernel, n, kw // LANES), grid=(dep...]
    reshape x2 -> x1, local copies, waits for them, and re-layouts: 9.64 us -> 0.11 us  [on_device(): slots = blocks.reshape(-1, 1)]
    scatter-add x2 -> x0, other arithmetic: 9.52 us -> none  [the longest x1 8.25 us: on_device(): jnp.zeros((n_blocks, 128), jnp.float32).at[all_slots.astype(jnp.int32)]]
  transfers between devices with their start and end apart: 2 -> 16, of which waited for: 2 -> 8; matrix products, arithmetic and copies ran while one was open for 8% -> 0% of each run, Pallas kernels for 0% -> 8%
where the time goes in v1:
time: 69.2 us; the launch traced here: 68.8 us
  waiting for transfers between devices  30.6 us (44%)
  starting transfers between devices  18.6 us (27%)
  Pallas kernels  13.9 us (20%)
  local copies, waits for them, and re-layouts  4.04 us (6%)
  between operations  1.44 us (2%)
    ppermute x16, waiting for transfers between devices, swap(): return lax.ppermute(x, axis, [(i, i ^ d) for i in range(n)])  30.6 us
    ppermute x16, starting transfers between devices, swap(): return lax.ppermute(x, axis, [(i, i ^ d) for i in range(n)])  18.6 us
    pallas_call x1, Pallas kernels, outer(): pl.pallas_call(functools.partial(outer_kernel, n, kw // LANES), grid=(dep...  5.74 us
    pallas_call x1, Pallas kernels, residue(): pl.pallas_call(functools.partial(residue_kernel, n, kw // LANES), grid=(d...  4.59 us
    unnamed x16, local copies, waits for them, and re-layouts  2.1 us
    dynamic_slice x1, local copies, waits for them, and re-layouts, on_device(): lax.dynamic_slice(tokens, (c * rows, (me ^ d) * depth), (rows, depth))  1.82 us
  transfers between devices with their start and end apart: 16, of which 8 were waited for; matrix products, arithmetic and copies ran while one was open for 0% of the time, Pallas kernels for 8%

profile of v1, /device:TPU:1, one launch (start us, length us, event | category | flops | bytes accessed | tf_op | source)
XLA Modules:
  0.0 68.8 jit_solution(9711024780285147692)
XLA Ops:
  0.7 1.8 %dynamic-slice_bitcast_fusion = (bf16[128,2048]{1,0:T(8,128)(2,1)S(1)}, bf16[128,2048]{1,0:T(8,128)(2,1)S(1)}, bf16[128,2048]{1,0:T(8,128)(2,1)S(1)}, bf16[128,2048]{1,0:T(8,128)(2,1)S(1)}) fusion(bf16[1,128,8192]{2,1,0:T(8,128)(2,1)} %param.6, s32[]{:T(128)S(6)} %select_n.15, s32[]{:T(128)S(6)} %select_n.13, s32[]{:T(128)S(6)} %select_n.12, s32[]{:T(128)S(6)} %select_n.14), kind=kLoop, calls=%fused_computation | loop fusion | bytes 4194320 | tf_op jit(solution)/shard_map/dynamic_slice | solution.py:238
  2.5 3.1 %collective-permute-start.2 = (bf16[128,2048]{1,0:T(8,128)(2,1)S(1)}, bf16[128,2048]{1,0:T(8,128)(2,1)S(1)}, u32[]{:S(2)}, u32[]{:S(2)}) collective-permute-start(bf16[128,2048]{1,0:T(8,128)(2,1)S(1)} %get-tuple-element.14), channel_id=1, source_target_pairs={{0,3},{1,2},{2,1},{3,0},{4,7},{5,6},{6,5},{7,4},{8,11},{9,10},{10,... | collective-permute-start | bytes 1572872 | tf_op jit(solution)/shard_map/ppermute | solution.py:24
  5.5 0.3 collective-permute-start
  5.8 0.1 collective-permute-start.1
  5.9 11.3 %collective-permute-done.2.refs_3_ = bf16[128,2048]{1,0:T(8,128)(2,1)S(1)} collective-permute-done((bf16[128,2048]{1,0:T(8,128)(2,1)S(1)}, bf16[128,2048]{1,0:T(8,128)(2,1)S(1)}, u32[]{:S(2)}, u32[]{:S(2)}) %collective-permute-start.2) | collective-permute-done | bytes 524320 | tf_op jit(solution)/shard_map/ppermute | solution.py:24
  17.2 11.2 %collective-permute-done.refs_1_ = bf16[128,2048]{1,0:T(8,128)(2,1)S(1)} collective-permute-done((bf16[128,2048]{1,0:T(8,128)(2,1)S(1)}, bf16[128,2048]{1,0:T(8,128)(2,1)S(1)}, u32[]{:S(2)}, u32[]{:S(2)}) %collective-permute-start) | collective-permute-done | bytes 524320 | tf_op jit(solution)/shard_map/ppermute | solution.py:24
  28.4 0.8 %collective-permute-done.1.refs_2_ = bf16[128,2048]{1,0:T(8,128)(2,1)S(1)} collective-permute-done((bf16[128,2048]{1,0:T(8,128)(2,1)S(1)}, bf16[128,2048]{1,0:T(8,128)(2,1)S(1)}, u32[]{:S(2)}, u32[]{:S(2)}) %collective-permute-start.1) | collective-permute-done | bytes 524320 | tf_op jit(solution)/shard_map/ppermute | solution.py:24
  29.2 1.2 %project.1 = (f32[128,512]{1,0:T(8,128)S(1)}, bf16[128,512]{1,0:T(8,128)(2,1)S(1)}, bf16[128,512]{1,0:T(8,128)(2,1)S(1)}, bf16[128,512]{1,0:T(8,128)(2,1)S(1)}) custom-call(bf16[128,2048]{1,0:T(8,128)(2,1)S(1)} %get-tuple-element.16.refs_0_, bf16[128,2048]{1,0:T(8,128)(2,1)S(1)} %collective-permute-done.refs_1_, ...), custom_call_target="tpu_custom_call" | custom-call | flops 1073741824 | bytes 4194304 | tf_op jit(solution)/shard_map/project/pallas_call | solution.py:42
  30.5 1.5 %collective-permute-start.3 = (bf16[128,512]{1,0:T(8,128)(2,1)S(1)}, bf16[128,512]{1,0:T(8,128)(2,1)S(1)}, u32[]{:S(2)}, u32[]{:S(2)}) collective-permute-start(bf16[128,512]{1,0:T(8,128)(2,1)S(1)} %get-tuple-element.9), channel_id=1, source_target_pairs={{0,1},{1,0},{2,3},{3,2},{4,5},{5,4},{6,7},{7,6},{8,9},{9,8},{10,11... | collective-permute-start | bytes 393224 | tf_op jit(solution)/shard_map/ppermute | solution.py:24
  31.9 1.2 %collective-permute-start.4 = (bf16[128,512]{1,0:T(8,128)(2,1)S(1)}, bf16[128,512]{1,0:T(8,128)(2,1)S(1)}, u32[]{:S(2)}, u32[]{:S(2)}) collective-permute-start(bf16[128,512]{1,0:T(8,128)(2,1)S(1)} %get-tuple-element.10), channel_id=1, source_target_pairs={{0,2},{1,3},{2,0},{3,1},{4,6},{5,7},{6,4},{7,5},{8,10},{9,11},{10,... | collective-permute-start | bytes 393224 | tf_op jit(solution)/shard_map/ppermute | solution.py:24
  33.2 0.0 collective-permute-start.5
  33.2 1.5 %collective-permute-done.3 = bf16[128,512]{1,0:T(8,128)(2,1)S(1)} collective-permute-done((bf16[128,512]{1,0:T(8,128)(2,1)S(1)}, bf16[128,512]{1,0:T(8,128)(2,1)S(1)}, u32[]{:S(2)}, u32[]{:S(2)}) %collective-permute-start.3) | collective-permute-done | bytes 131104 | tf_op jit(solution)/shard_map/ppermute | solution.py:24
  34.7 1.3 %collective-permute-done.4 = bf16[128,512]{1,0:T(8,128)(2,1)S(1)} collective-permute-done((bf16[128,512]{1,0:T(8,128)(2,1)S(1)}, bf16[128,512]{1,0:T(8,128)(2,1)S(1)}, u32[]{:S(2)}, u32[]{:S(2)}) %collective-permute-start.4) | collective-permute-done | bytes 131104 | tf_op jit(solution)/shard_map/ppermute | solution.py:24
  36.1 2.8 %collective-permute-done.5 = bf16[128,512]{1,0:T(8,128)(2,1)S(1)} collective-permute-done((bf16[128,512]{1,0:T(8,128)(2,1)S(1)}, bf16[128,512]{1,0:T(8,128)(2,1)S(1)}, u32[]{:S(2)}, u32[]{:S(2)}) %collective-permute-start.5) | collective-permute-done | bytes 131104 | tf_op jit(solution)/shard_map/ppermute | solution.py:24
  38.9 0.1 fusion.1.refs_0_.refs_4_
  39.0 1.2 %collective-permute-start.8 = (bf16[128,512]{1,0:T(8,128)(2,1)S(1)}, bf16[128,512]{1,0:T(8,128)(2,1)S(1)}, u32[]{:S(2)}, u32[]{:S(2)}) collective-permute-start(bf16[128,512]{1,0:T(8,128)(2,1)S(1)} %fusion.1.refs_0_.refs_4_), channel_id=1, source_target_pairs={{0,3},{1,2},{2,1},{3,0},{4,7},{5,6},{6,5},{7,4},{8,11},{9,10},{10,... | collective-permute-start | bytes 393224 | tf_op jit(solution)/shard_map/ppermute | solution.py:24
  40.2 1.4 %collective-permute-start.7 = (bf16[128,512]{1,0:T(8,128)(2,1)S(1)}, bf16[128,512]{1,0:T(8,128)(2,1)}, u32[]{:S(2)}, u32[]{:S(2)}) collective-permute-start(bf16[128,512]{1,0:T(8,128)(2,1)S(1)} %fusion.1.refs_0_.refs_4_), channel_id=1, source_target_pairs={{0,2},{1,3},{2,0},{3,1},{4,6},{5,7},{6,4},{7,5},{8,10},{9,11},{10,... | collective-permute-start | bytes 393224 | tf_op jit(solution)/shard_map/ppermute | solution.py:24
  41.6 0.1 collective-permute-start.6
  42.4 0.1 copy.8.refs_4_.refs_6_.refs_9_
  42.5 1.0 %copy-done.2 = bf16[128,2048]{1,0:T(8,128)(2,1)S(1)} copy-done((bf16[128,2048]{1,0:T(8,128)(2,1)S(1)}, bf16[128,2048]{1,0:T(8,128)(2,1)}, u32[]{:S(2)}) %copy-start.2) | copy-done | bytes 524312
  43.5 1.0 %copy-done.4 = bf16[128,2048]{1,0:T(8,128)(2,1)S(1)} copy-done((bf16[128,2048]{1,0:T(8,128)(2,1)S(1)}, bf16[128,2048]{1,0:T(8,128)(2,1)}, u32[]{:S(2)}) %copy-start.4) | copy-done | bytes 524312
  44.6 1.2 %prepare.1 = (bf16[128,512]{1,0:T(8,128)(2,1)S(1)}, f32[128,128]{1,0:T(8,128)S(1)}) custom-call(bf16[128,2048]{1,0:T(8,128)(2,1)S(1)} %get-tuple-element.16.refs_0_, bf16[128,2048]{1,0:T(8,128)(2,1)S(1)} %copy-done.2, bf16[128,2048]{1,0:T(8,128)(2,1)S(1)} %copy-done.4, bf16[128,2048]{1,0:T(8,128)(2,1)S(1)} %collective-permute-done.2.refs_3_, ...), custom_call_target="tpu_custom_call" | custom-call | flops 536870912 | bytes 4194304 | tf_op jit(solution)/shard_map/prepare/pallas_call | solution.py:83
  45.7 1.5 %collective-permute-done.7.refs_2_.refs_6_ = bf16[128,512]{1,0:T(8,128)(2,1)} collective-permute-done((bf16[128,512]{1,0:T(8,128)(2,1)S(1)}, bf16[128,512]{1,0:T(8,128)(2,1)}, u32[]{:S(2)}, u32[]{:S(2)}) %collective-permute-start.7) | collective-permute-done | bytes 131104 | tf_op jit(solution)/shard_map/ppermute | solution.py:24
  47.2 1.2 %kept.1.refs_0_ = bf16[144,128]{1,0:T(8,128)(2,1)S(1)} custom-call(bf16[128,512]{1,0:T(8,128)(2,1)S(1)} %fusion.1.refs_0_.refs_4_, bf16[128,512]{1,0:T(8,128)(2,1)} %collective-permute-done.6.refs_1_.refs_5_, bf16[128,512]{1,0:T(8,128)(2,1)} %collective-permute-done.7.refs_2_.refs_6_, bf16[128,512]{1,0:T(8,128)(2,1)S(1)} %collective-permute-done.8.refs_3_.refs_7_, ...), custom_call_target="tpu_custom_call" | custom-call | flops 67108864 | bytes 524288 | tf_op jit(solution)/shard_map/kept/pallas_call | solution.py:117
  48.4 5.1 %collective-permute-start.15 = (bf16[144,128]{1,0:T(8,128)(2,1)S(1)}, bf16[144,128]{1,0:T(8,128)(2,1)S(1)}, u32[]{:S(2)}, u32[]{:S(2)}) collective-permute-start(bf16[144,128]{1,0:T(8,128)(2,1)S(1)} %kept.1.refs_0_), channel_id=1, source_target_pairs={{0,28},{4,24},{8,20},{12,16},{16,12},{20,8},{24,4},{28,0},{1,29},{... | collective-permute-start | bytes 110600 | tf_op jit(solution)/shard_map/ppermute | solution.py:24
  53.5 2.7 %collective-permute-start.12 = (bf16[144,128]{1,0:T(8,128)(2,1)S(1)}, bf16[144,128]{1,0:T(8,128)(2,1)S(1)}, u32[]{:S(2)}, u32[]{:S(2)}) collective-permute-start(bf16[144,128]{1,0:T(8,128)(2,1)S(1)} %kept.1.refs_0_), channel_id=1, source_target_pairs={{0,16},{4,20},{8,24},{12,28},{16,0},{20,4},{24,8},{28,12},{1,17},{... | collective-permute-start | bytes 110600 | tf_op jit(solution)/shard_map/ppermute | solution.py:24
  56.3 1.1 %collective-permute-start.11 = (bf16[144,128]{1,0:T(8,128)(2,1)S(1)}, bf16[144,128]{1,0:T(8,128)(2,1)S(1)}, u32[]{:S(2)}, u32[]{:S(2)}) collective-permute-start(bf16[144,128]{1,0:T(8,128)(2,1)S(1)} %kept.1.refs_0_), channel_id=1, source_target_pairs={{0,12},{4,8},{8,4},{12,0},{16,28},{20,24},{24,20},{28,16},{1,13},{... | collective-permute-start | bytes 110600 | tf_op jit(solution)/shard_map/ppermute | solution.py:24
  57.4 0.6 collective-permute-start.10
  57.9 0.2 collective-permute-done.14.refs_6_
  58.2 0.2 collective-permute-start.9
  58.4 4.6 %residue.1 = bf16[2048,512]{1,0:T(8,128)(2,1)} custom-call(bf16[128,2048]{1,0:T(8,128)(2,1)S(1)} %get-tuple-element.16.refs_0_, bf16[128,2048]{1,0:T(8,128)(2,1)S(1)} %copy-done.2, bf16[128,2048]{1,0:T(8,128)(2,1)S(1)} %copy-done.4, bf16[128,2048]{1,0:T(8,128)(2,1)S(1)} %collective-permute-done.2.refs_3_, bf16[128,512]{1,0:T(8,128)(2,1)S(1)} %fusion.1.refs_0_.refs_4_, ...), custom_call_target="tpu_custom_call" | custom-call | flops 1073741824 | bytes 6291456 | tf_op jit(solution)/shard_map/residue/pallas_call | solution.py:162
  63.0 5.7 %outer.1 = f32[2048,512]{1,0:T(8,128)} custom-call(bf16[144,128]{1,0:T(8,128)(2,1)S(1)} %kept.1.refs_0_, bf16[144,128]{1,0:T(8,128)(2,1)S(1)} %collective-permute-done.9.refs_1_, bf16[144,128]{1,0:T(8,128)(2,1)S(1)} %collective-permute-done.10.refs_2_, bf16[144,128]{1,0:T(8,128)(2,1)S(1)} %collective-permute-done.11.refs_3_, ...), custom_call_target="tpu_custom_call" | custom-call | flops 2147483648 | bytes 4194304 | tf_op jit(solution)/shard_map/outer/pallas_call | solution.py:209
  (24 shorter events, 0.1 us)
Async XLA Ops:
  0.7 28.5 %copy-start.5 = (bf16[1,2048,512]{2,1,0:T(8,128)(2,1)S(1)}, bf16[1,2048,512]{2,1,0:T(8,128)(2,1)}, u32[]{:S(2)}) copy-start(bf16[1,2048,512]{2,1,0:T(8,128)(2,1)} %param.8) | copy-start | bytes 6291460
  2.5 14.8 %collective-permute-start.2 = (bf16[128,2048]{1,0:T(8,128)(2,1)S(1)}, bf16[128,2048]{1,0:T(8,128)(2,1)S(1)}, u32[]{:S(2)}, u32[]{:S(2)}) collective-permute-start(bf16[128,2048]{1,0:T(8,128)(2,1)S(1)} %get-tuple-element.14), channel_id=1, source_target_pairs={{0,3},{1,2},{2,1},{3,0},{4,7},{5,6},{6,5},{7,4},{8,11},{9,10},{10,... | collective-permute-start | bytes 1572872 | tf_op jit(solution)/shard_map/ppermute | solution.py:24
  5.5 22.9 %collective-permute-start = (bf16[128,2048]{1,0:T(8,128)(2,1)S(1)}, bf16[128,2048]{1,0:T(8,128)(2,1)S(1)}, u32[]{:S(2)}, u32[]{:S(2)}) collective-permute-start(bf16[128,2048]{1,0:T(8,128)(2,1)S(1)} %get-tuple-element.15), channel_id=1, source_target_pairs={{0,1},{1,0},{2,3},{3,2},{4,5},{5,4},{6,7},{7,6},{8,9},{9,8},{10,11... | collective-permute-start | bytes 1572872 | tf_op jit(solution)/shard_map/ppermute | solution.py:24
  5.8 23.4 %collective-permute-start.1 = (bf16[128,2048]{1,0:T(8,128)(2,1)S(1)}, bf16[128,2048]{1,0:T(8,128)(2,1)S(1)}, u32[]{:S(2)}, u32[]{:S(2)}) collective-permute-start(bf16[128,2048]{1,0:T(8,128)(2,1)S(1)} %get-tuple-element.17), channel_id=1, source_target_pairs={{0,2},{1,3},{2,0},{3,1},{4,6},{5,7},{6,4},{7,5},{8,10},{9,11},{10,... | collective-permute-start | bytes 1572872 | tf_op jit(solution)/shard_map/ppermute | solution.py:24
  28.4 2.0 %copy-start.1 = (bf16[128,2048]{1,0:T(8,128)(2,1)}, bf16[128,2048]{1,0:T(8,128)(2,1)S(1)}, u32[]{:S(2)}) copy-start(bf16[128,2048]{1,0:T(8,128)(2,1)S(1)} %collective-permute-done.refs_1_) | copy-start | bytes 1572868
  29.2 1.3 %copy-start.3 = (bf16[128,2048]{1,0:T(8,128)(2,1)}, bf16[128,2048]{1,0:T(8,128)(2,1)S(1)}, u32[]{:S(2)}) copy-start(bf16[128,2048]{1,0:T(8,128)(2,1)S(1)} %collective-permute-done.1.refs_2_) | copy-start | bytes 1572868
  29.2 9.7 %copy-start.7 = (bf16[1,128,512]{2,1,0:T(8,128)(2,1)S(1)}, bf16[1,128,512]{2,1,0:T(8,128)(2,1)}, u32[]{:S(2)}) copy-start(bf16[1,128,512]{2,1,0:T(8,128)(2,1)} %param.7) | copy-start | bytes 393220
  29.2 13.2 %copy-start.6 = (s32[1,1,128]{2,1,0:T(1,128)S(1)}, s32[1,1,128]{2,1,0:T(1,128)}, u32[]{:S(2)}) copy-start(s32[1,1,128]{2,1,0:T(1,128)} %param.11) | copy-start | bytes 1540
  29.2 13.3 %copy-start = (bf16[1,2048,512]{2,1,0:T(8,128)(2,1)S(1)}, bf16[1,2048,512]{2,1,0:T(8,128)(2,1)}, u32[]{:S(2)}) copy-start(bf16[1,2048,512]{2,1,0:T(8,128)(2,1)} %param.9) | copy-start | bytes 6291460
  30.5 4.3 %collective-permute-start.3 = (bf16[128,512]{1,0:T(8,128)(2,1)S(1)}, bf16[128,512]{1,0:T(8,128)(2,1)S(1)}, u32[]{:S(2)}, u32[]{:S(2)}) collective-permute-start(bf16[128,512]{1,0:T(8,128)(2,1)S(1)} %get-tuple-element.9), channel_id=1, source_target_pairs={{0,1},{1,0},{2,3},{3,2},{4,5},{5,4},{6,7},{7,6},{8,9},{9,8},{10,11... | collective-permute-start | bytes 393224 | tf_op jit(solution)/shard_map/ppermute | solution.py:24
  31.9 4.1 %collective-permute-start.4 = (bf16[128,512]{1,0:T(8,128)(2,1)S(1)}, bf16[128,512]{1,0:T(8,128)(2,1)S(1)}, u32[]{:S(2)}, u32[]{:S(2)}) collective-permute-start(bf16[128,512]{1,0:T(8,128)(2,1)S(1)} %get-tuple-element.10), channel_id=1, source_target_pairs={{0,2},{1,3},{2,0},{3,1},{4,6},{5,7},{6,4},{7,5},{8,10},{9,11},{10,... | collective-permute-start | bytes 393224 | tf_op jit(solution)/shard_map/ppermute | solution.py:24
  33.2 5.7 %collective-permute-start.5 = (bf16[128,512]{1,0:T(8,128)(2,1)S(1)}, bf16[128,512]{1,0:T(8,128)(2,1)S(1)}, u32[]{:S(2)}, u32[]{:S(2)}) collective-permute-start(bf16[128,512]{1,0:T(8,128)(2,1)S(1)} %get-tuple-element.11), channel_id=1, source_target_pairs={{0,3},{1,2},{2,1},{3,0},{4,7},{5,6},{6,5},{7,4},{8,11},{9,10},{10,... | collective-permute-start | bytes 393224 | tf_op jit(solution)/shard_map/ppermute | solution.py:24
  39.0 6.7 %collective-permute-start.8 = (bf16[128,512]{1,0:T(8,128)(2,1)S(1)}, bf16[128,512]{1,0:T(8,128)(2,1)S(1)}, u32[]{:S(2)}, u32[]{:S(2)}) collective-permute-start(bf16[128,512]{1,0:T(8,128)(2,1)S(1)} %fusion.1.refs_0_.refs_4_), channel_id=1, source_target_pairs={{0,3},{1,2},{2,1},{3,0},{4,7},{5,6},{6,5},{7,4},{8,11},{9,10},{10,... | collective-permute-start | bytes 393224 | tf_op jit(solution)/shard_map/ppermute | solution.py:24
  40.2 7.0 %collective-permute-start.7 = (bf16[128,512]{1,0:T(8,128)(2,1)S(1)}, bf16[128,512]{1,0:T(8,128)(2,1)}, u32[]{:S(2)}, u32[]{:S(2)}) collective-permute-start(bf16[128,512]{1,0:T(8,128)(2,1)S(1)} %fusion.1.refs_0_.refs_4_), channel_id=1, source_target_pairs={{0,2},{1,3},{2,0},{3,1},{4,6},{5,7},{6,4},{7,5},{8,10},{9,11},{10,... | collective-permute-start | bytes 393224 | tf_op jit(solution)/shard_map/ppermute | solution.py:24
  41.6 5.6 %collective-permute-start.6 = (bf16[128,512]{1,0:T(8,128)(2,1)S(1)}, bf16[128,512]{1,0:T(8,128)(2,1)}, u32[]{:S(2)}, u32[]{:S(2)}) collective-permute-start(bf16[128,512]{1,0:T(8,128)(2,1)S(1)} %fusion.1.refs_0_.refs_4_), channel_id=1, source_target_pairs={{0,1},{1,0},{2,3},{3,2},{4,5},{5,4},{6,7},{7,6},{8,9},{9,8},{10,11... | collective-permute-start | bytes 393224 | tf_op jit(solution)/shard_map/ppermute | solution.py:24
  42.5 1.0 %copy-start.2 = (bf16[128,2048]{1,0:T(8,128)(2,1)S(1)}, bf16[128,2048]{1,0:T(8,128)(2,1)}, u32[]{:S(2)}) copy-start(bf16[128,2048]{1,0:T(8,128)(2,1)} %copy-done.1) | copy-start | bytes 1572868
  43.5 1.0 %copy-start.4 = (bf16[128,2048]{1,0:T(8,128)(2,1)S(1)}, bf16[128,2048]{1,0:T(8,128)(2,1)}, u32[]{:S(2)}) copy-start(bf16[128,2048]{1,0:T(8,128)(2,1)} %copy-done.3) | copy-start | bytes 1572868
  48.4 8.9 %collective-permute-start.15 = (bf16[144,128]{1,0:T(8,128)(2,1)S(1)}, bf16[144,128]{1,0:T(8,128)(2,1)S(1)}, u32[]{:S(2)}, u32[]{:S(2)}) collective-permute-start(bf16[144,128]{1,0:T(8,128)(2,1)S(1)} %kept.1.refs_0_), channel_id=1, source_target_pairs={{0,28},{4,24},{8,20},{12,16},{16,12},{20,8},{24,4},{28,0},{1,29},{... | collective-permute-start | bytes 110600 | tf_op jit(solution)/shard_map/ppermute | solution.py:24
  53.5 4.6 %collective-permute-start.14 = (bf16[144,128]{1,0:T(8,128)(2,1)S(1)}, bf16[144,128]{1,0:T(8,128)(2,1)S(1)}, u32[]{:S(2)}, u32[]{:S(2)}) collective-permute-start(bf16[144,128]{1,0:T(8,128)(2,1)S(1)} %kept.1.refs_0_), channel_id=1, source_target_pairs={{0,24},{4,28},{8,16},{12,20},{16,8},{20,12},{24,0},{28,4},{1,25},{... | collective-permute-start | bytes 110600 | tf_op jit(solution)/shard_map/ppermute | solution.py:24
  53.5 9.5 %collective-permute-start.13 = (bf16[144,128]{1,0:T(8,128)(2,1)S(1)}, bf16[144,128]{1,0:T(8,128)(2,1)S(1)}, u32[]{:S(2)}, u32[]{:S(2)}) collective-permute-start(bf16[144,128]{1,0:T(8,128)(2,1)S(1)} %kept.1.refs_0_), channel_id=1, source_target_pairs={{0,20},{4,16},{8,28},{12,24},{16,4},{20,0},{24,12},{28,8},{1,21},{... | collective-permute-start | bytes 110600 | tf_op jit(solution)/shard_map/ppermute | solution.py:24
  53.5 9.5 %collective-permute-start.12 = (bf16[144,128]{1,0:T(8,128)(2,1)S(1)}, bf16[144,128]{1,0:T(8,128)(2,1)S(1)}, u32[]{:S(2)}, u32[]{:S(2)}) collective-permute-start(bf16[144,128]{1,0:T(8,128)(2,1)S(1)} %kept.1.refs_0_), channel_id=1, source_target_pairs={{0,16},{4,20},{8,24},{12,28},{16,0},{20,4},{24,8},{28,12},{1,17},{... | collective-permute-start | bytes 110600 | tf_op jit(solution)/shard_map/ppermute | solution.py:24
  56.3 6.8 %collective-permute-start.11 = (bf16[144,128]{1,0:T(8,128)(2,1)S(1)}, bf16[144,128]{1,0:T(8,128)(2,1)S(1)}, u32[]{:S(2)}, u32[]{:S(2)}) collective-permute-start(bf16[144,128]{1,0:T(8,128)(2,1)S(1)} %kept.1.refs_0_), channel_id=1, source_target_pairs={{0,12},{4,8},{8,4},{12,0},{16,28},{20,24},{24,20},{28,16},{1,13},{... | collective-permute-start | bytes 110600 | tf_op jit(solution)/shard_map/ppermute | solution.py:24
  57.4 5.6 %collective-permute-start.10 = (bf16[144,128]{1,0:T(8,128)(2,1)S(1)}, bf16[144,128]{1,0:T(8,128)(2,1)S(1)}, u32[]{:S(2)}, u32[]{:S(2)}) collective-permute-start(bf16[144,128]{1,0:T(8,128)(2,1)S(1)} %kept.1.refs_0_), channel_id=1, source_target_pairs={{0,8},{4,12},{8,0},{12,4},{16,24},{20,28},{24,16},{28,20},{1,9},{5... | collective-permute-start | bytes 110600 | tf_op jit(solution)/shard_map/ppermute | solution.py:24
  58.2 4.9 %collective-permute-start.9 = (bf16[144,128]{1,0:T(8,128)(2,1)S(1)}, bf16[144,128]{1,0:T(8,128)(2,1)S(1)}, u32[]{:S(2)}, u32[]{:S(2)}) collective-permute-start(bf16[144,128]{1,0:T(8,128)(2,1)S(1)} %kept.1.refs_0_), channel_id=1, source_target_pairs={{0,4},{4,0},{8,12},{12,8},{16,20},{20,16},{24,28},{28,24},{1,5},{5... | collective-permute-start | bytes 110600 | tf_op jit(solution)/shard_map/ppermute | solution.py:24

commit v2 on v1

v2 whole, which is shorter than its diff:
```python
import functools

import jax
import jax.numpy as jnp
from jax import lax
from jax.experimental import pallas as pl
from jax.experimental.pallas import tpu as pltpu
from jax.sharding import PartitionSpec as P

LANES = 128
CHUNKS = (4, 4)
ANY = pl.BlockSpec(memory_space=pl.ANY)
VMEM = pl.BlockSpec(memory_space=pltpu.VMEM)
SMEM = pl.BlockSpec(memory_space=pltpu.SMEM)
MIB = 1024 * 1024


def params(mib):
    return pltpu.CompilerParams(vmem_limit_bytes=mib * MIB)


def cost(flops, nbytes):
    return pl.CostEstimate(flops=int(flops), bytes_accessed=int(nbytes), transcendentals=0)


def swap(x, axis, n, d):
    return lax.ppermute(x, axis, [(i, i ^ d) for i in range(n)])


def project_kernel(n, *refs):
    pieces, w, outs, x = refs[:n], refs[n], refs[-n - 1 : -1], refs[-1]
    rows = x.shape[0] // n
    for d in range(n):
        x[d * rows : (d + 1) * rows, :] = pieces[d][...]
    full = jnp.dot(x[...], w[...], preferred_element_type=jnp.float32)
    for d in range(n):
        outs[d][...] = full[d * rows : (d + 1) * rows, :].astype(outs[d].dtype)


def project(pieces, w, after):
    n = len(pieces)
    rows, depth = pieces[0].shape
    kw = w.shape[1]
    result = pl.pallas_call(
        functools.partial(project_kernel, n),
        out_shape=[
            jax.ShapeDtypeStruct((rows, kw), jnp.float32 if d == 0 else jnp.bfloat16)
            for d in range(n)
        ]
        + [jax.ShapeDtypeStruct((n * rows, depth), jnp.bfloat16)],
        in_specs=[VMEM] * (n + 1) + [ANY] * len(after),
        compiler_params=params(24),
        cost_estimate=cost(2 * n * rows * depth * kw, 2 * depth * (n * rows + kw)),
        name="project",
    )(*pieces, w, *after)
    return result[:n], result[n]


def slope_kernel(low, tok_dev, *refs):
    products, goal, out = refs[:-3], refs[-3], refs[-1]
    key_proj = products[0][...]
    for product in products[1:]:
        key_proj += product[...].astype(jnp.float32)
    goal = goal[low : low + out.shape[0], :].astype(jnp.float32)
    out[...] = ((key_proj - goal) / tok_dev).astype(jnp.bfloat16)


def slope(products, goal, low, after):
    return pl.pallas_call(
        functools.partial(slope_kernel, low, goal.shape[0]),
        out_shape=jax.ShapeDtypeStruct(products[0].shape, jnp.bfloat16),
        in_specs=[VMEM] * (len(products) + 1) + [ANY],
        compiler_params=params(8),
        cost_estimate=cost(4 * products[0].size, 12 * products[0].size),
        name="slope",
    )(*products, goal, after)


def pick_columns(wide, column):
    out = jnp.zeros((wide.shape[0], LANES), jnp.float32)
    for c in range(wide.shape[1] // LANES):
        out += jnp.where(column == c, wide[:, c * LANES : (c + 1) * LANES], 0.0)
    return out


def early_kernel(per_row, slots, slot_row, count, fb, fbk, keep):
    depth, kw = fb.shape
    cap = slots.shape[0]
    slot = slots[...]
    hot = slot // per_row == lax.broadcasted_iota(jnp.int32, (cap, depth), 1)
    hot = hot.astype(jnp.float32).astype(jnp.bfloat16)
    used = lax.broadcasted_iota(jnp.int32, (cap, 1), 0) < count[0, 0]
    wide = jnp.dot(hot, fb[...], preferred_element_type=jnp.float32)
    fbk[...] = jnp.where(used, pick_columns(wide, slot % per_row), 0.0)
    group = lax.broadcasted_iota(jnp.int32, (cap, kw), 1) // LANES
    mark = jnp.where(used & (slot % per_row == group), 1.0, 0.0).astype(jnp.bfloat16)
    tile = min(depth, 512)
    for t in range(depth // tile):
        line = lax.broadcasted_iota(jnp.int32, (tile, cap), 0) + t * tile
        hot = (slot_row[...] // per_row == line).astype(jnp.float32).astype(jnp.bfloat16)
        mask = jnp.dot(hot, mark, preferred_element_type=jnp.float32)
        keep[t * tile : (t + 1) * tile, :] = (1.0 - mask).astype(jnp.bfloat16)


def early(slots, slot_row, count, fb):
    depth, kw = fb.shape
    cap = slots.shape[0]
    return pl.pallas_call(
        functools.partial(early_kernel, kw // LANES),
        out_shape=[
            jax.ShapeDtypeStruct((cap, LANES), jnp.float32),
            jax.ShapeDtypeStruct((depth, kw), jnp.bfloat16),
        ],
        in_specs=[VMEM, VMEM, SMEM, VMEM],
        compiler_params=params(24),
        cost_estimate=cost(4 * cap * depth * kw, 4 * depth * kw),
        name="early",
    )(slots, slot_row, count, fb)


def prepare_kernel(per_row, x, slots, count, after, xg, xt):
    depth = x.shape[1]
    cap = slots.shape[0]
    used = lax.broadcasted_iota(jnp.int32, (cap, 1), 0) < count[0, 0]
    line = jnp.where(used, slots[...] // per_row, depth)
    hot = line == lax.broadcasted_iota(jnp.int32, (cap, depth), 1)
    hot = hot.astype(jnp.float32).astype(jnp.bfloat16)
    xg[...] = lax.dot_general(
        hot, x[...], (((1,), (1,)), ((), ())), preferred_element_type=jnp.float32
    ).astype(jnp.bfloat16)
    xt[...] = x[...].T


def prepare(x, slots, count, per_row, after):
    rows, depth = x.shape
    cap = slots.shape[0]
    return pl.pallas_call(
        functools.partial(prepare_kernel, per_row),
        out_shape=[
            jax.ShapeDtypeStruct((cap, rows), jnp.bfloat16),
            jax.ShapeDtypeStruct((depth, rows), jnp.bfloat16),
        ],
        in_specs=[VMEM, VMEM, SMEM, ANY],
        compiler_params=params(24),
        cost_estimate=cost(2 * cap * depth * rows, 4 * depth * rows),
        name="prepare",
    )(x, slots, count, after)


def stack(parts, s):
    rows = parts[0].shape[0]
    for d in range(len(parts)):
        s[d * rows : (d + 1) * rows, :] = parts[d][...]
    return s[...]


def kept_kernel(per_row, n, *refs):
    chunks = (len(refs) - 4) // (n + 2)
    parts, xgs = refs[: n * chunks], refs[n * chunks : (n + 1) * chunks]
    fbk, slots, slot_row, out = refs[(n + 1) * chunks : (n + 1) * chunks + 4]
    scratch = refs[(n + 1) * chunks + 4 :]
    cap = slots.shape[0]
    wide = 0.0
    for c in range(chunks):
        s = stack(parts[c * n : (c + 1) * n], scratch[c])
        wide += jnp.dot(xgs[c][...], s, preferred_element_type=jnp.float32)
    value = pick_columns(wide, slots[...] % per_row) + fbk[...]
    out[:cap, :] = value.astype(jnp.bfloat16)
    tail = out.shape[0] - cap
    number = jnp.broadcast_to(slot_row[...], (tail, cap))
    line = lax.broadcasted_iota(jnp.int32, (tail, cap), 0)
    number = jnp.where(line == 0, number // LANES, number % LANES)
    out[cap:, :] = number.astype(jnp.float32).astype(jnp.bfloat16)


def kept(parts, xgs, fbk, slots, slot_row):
    cap = slots.shape[0]
    n, kw = len(parts[0]), parts[0][0].shape[1]
    total = sum(xg.shape[1] for xg in xgs)
    return pl.pallas_call(
        functools.partial(kept_kernel, kw // LANES, n),
        out_shape=jax.ShapeDtypeStruct((cap + 16, LANES), jnp.bfloat16),
        scratch_shapes=[pltpu.VMEM((xg.shape[1], kw), jnp.bfloat16) for xg in xgs],
        compiler_params=params(8),
        cost_estimate=cost(2 * cap * total * kw, 2 * total * kw),
        name="kept",
    )(*sum(parts, []), *xgs, fbk, slots, slot_row)


def residue_kernel(n, *refs):
    chunks = (len(refs) - 3) // (n + 2)
    parts, xts = refs[: n * chunks], refs[n * chunks : (n + 1) * chunks]
    fb, keep, out = refs[(n + 1) * chunks : (n + 1) * chunks + 3]
    scratch = refs[(n + 1) * chunks + 3 :]

    @pl.when(pl.program_id(0) == 0)
    def _():
        for c in range(chunks):
            stack(parts[c * n : (c + 1) * n], scratch[c])

    pseudo = fb[...].astype(jnp.float32)
    for c in range(chunks):
        pseudo += jnp.dot(xts[c][...], scratch[c][...], preferred_element_type=jnp.float32)
    out[...] = jnp.where(keep[...] > 0, pseudo, 0.0).astype(jnp.bfloat16)


def residue(parts, xts, fb, keep):
    depth, kw = fb.shape
    n = len(parts[0])
    total = sum(xt.shape[1] for xt in xts)
    tile = min(depth, 512)
    rows = pl.BlockSpec((tile, kw), lambda i: (i, 0))
    flat = sum(parts, [])
    return pl.pallas_call(
        functools.partial(residue_kernel, n),
        grid=(depth // tile,),
        out_shape=jax.ShapeDtypeStruct((depth, kw), jnp.bfloat16),
        in_specs=[pl.BlockSpec(p.shape, lambda i: (0, 0)) for p in flat]
        + [pl.BlockSpec((tile, xt.shape[1]), lambda i: (i, 0)) for xt in xts]
        + [rows, rows],
        out_specs=rows,
        scratch_shapes=[pltpu.VMEM((xt.shape[1], kw), jnp.bfloat16) for xt in xts],
        compiler_params=params(24),
        cost_estimate=cost(2 * total * depth * kw, 2 * depth * (total + 3 * kw)),
        name="residue",
    )(*flat, *xts, fb, keep)


def outer_kernel(n, per_row, *refs):
    messages, (out, wide, lines) = refs[:n], refs[n:]
    step = pl.program_id(0)
    cap = messages[0].shape[0] - 16
    tile, kw = out.shape

    @pl.when(step == 0)
    def _():
        for k in range(n):
            tail = messages[k][cap:, :].astype(jnp.float32)
            number = (tail[0:1, :] * LANES + tail[1:2, :]).astype(jnp.int32)
            lines[:, k * cap : (k + 1) * cap] = jnp.broadcast_to(number // per_row, (8, cap))
            column = jnp.broadcast_to((number % per_row).astype(jnp.float32), (LANES, cap)).T
            value = messages[k][:cap, :].astype(jnp.float32)
            for c in range(per_row):
                wide[k * cap : (k + 1) * cap, c * LANES : (c + 1) * LANES] = jnp.where(
                    column == c, value, 0.0
                ).astype(jnp.bfloat16)

    line = lax.broadcasted_iota(jnp.int32, (tile, n * cap), 0) + step * tile
    hot = (lines[0:1, :] == line).astype(jnp.float32).astype(jnp.bfloat16)
    out[...] = jnp.dot(hot, wide[...], preferred_element_type=jnp.float32) / n


def outer(messages, depth, kw):
    n = len(messages)
    cap = messages[0].shape[0] - 16
    tile = min(depth, 512)
    return pl.pallas_call(
        functools.partial(outer_kernel, n, kw // LANES),
        grid=(depth // tile,),
        out_shape=jax.ShapeDtypeStruct((depth, kw), jnp.float32),
        in_specs=[pl.BlockSpec(messages[0].shape, lambda i: (0, 0))] * n,
        out_specs=pl.BlockSpec((tile, kw), lambda i: (i, 0)),
        scratch_shapes=[
            pltpu.VMEM((n * cap, kw), jnp.bfloat16),
            pltpu.VMEM((8, n * cap), jnp.int32),
        ],
        compiler_params=params(24),
        cost_estimate=cost(2 * n * cap * depth * kw, 4 * depth * kw),
        name="outer",
    )(*messages)


def on_device(inputs, target, weights, feedback, counts, blocks):
    tokens, w, fb = inputs[0], weights[0], feedback[0]
    n_shard, n_rep = lax.axis_size("shard"), lax.axis_size("rep")
    me = lax.axis_index("shard")
    tok_dev = tokens.shape[0]
    depth, kw = w.shape
    slot_row = blocks[0]
    slots = blocks.reshape(-1, 1)

    pieces, parts, xgs, xts, spans = [], [], [], [], []
    start = 0
    for share in CHUNKS:
        rows = tok_dev * share // sum(CHUNKS)
        mine = [
            lax.dynamic_slice(tokens, (start, (me ^ d) * depth), (rows, depth))
            for d in range(n_shard)
        ]
        moved = [swap(mine[d], "shard", n_shard, d) for d in range(1, n_shard)]
        pieces.append(mine[:1] + moved)
        spans.append(start)
        start += rows
    fbk, keep = early(slots, slot_row, counts, fb)
    after = []
    for c, low in enumerate(spans):
        products, x = project(pieces[c], w, after)
        moved = [swap(products[d], "shard", n_shard, d) for d in range(1, n_shard)]
        xg, xt = prepare(x, slots, counts, kw // LANES, products[1])
        xgs.append(xg)
        xts.append(xt)
        mine = slope([products[0]] + moved, target[0], low, xt)
        parts.append([mine] + [swap(mine, "shard", n_shard, d) for d in range(1, n_shard)])
        after = [keep] + parts[-1]
    message = kept(parts, xgs, fbk, slots, slot_row)
    messages = [message] + [swap(message, "rep", n_rep, d) for d in range(1, n_rep)]
    new_feedback = residue(parts, xts, fb, keep)
    return outer(messages, depth, kw), new_feedback[None]


def solution(mesh):
    placed = (
        P("rep", "shard", None),
        P("rep", "shard", None),
        P("rep", "shard", None),
        P("rep", "shard", None),
        P("rep", "shard"),
        P("rep", "shard", None),
    )
    return jax.shard_map(
        on_device,
        mesh=mesh,
        in_specs=placed,
        out_specs=(P("shard", None), P("rep", "shard", None)),
        check_vma=False,
    )
```

time: 69.2 us -> 81.9 us (1.18)
  starting transfers between devices: 18.6 us -> 34.1 us
  waiting for transfers between devices: 30.6 us -> 24.7 us
  local copies, waits for them, and re-layouts: 4.04 us -> 6.87 us
    ppermute x16 -> x25, starting transfers between devices: 18.6 us -> 34.1 us  [swap(): return lax.ppermute(x, axis, [(i, i ^ d) for i in range(n)])]
    ppermute x16 -> x25, waiting for transfers between devices: 30.6 us -> 24.7 us  [swap(): return lax.ppermute(x, axis, [(i, i ^ d) for i in range(n)])]
    unnamed x16 -> x20, local copies, waits for them, and re-layouts: 2.1 us -> 4.1 us
    pallas_call x4 -> x9, Pallas kernels: 8.2 us -> 9.69 us  [the longest x2 3.19 us: project(): pl.pallas_call(functools.partial(project_kernel, n), out_shape=[jax.Shape...]
    pallas_call x1, Pallas kernels: 5.74 us -> 4.43 us  [outer(): pl.pallas_call(functools.partial(outer_kernel, n, kw // LANES), grid=(dep...]
    dynamic_slice x1, local copies, waits for them, and re-layouts: 1.82 us -> 2.66 us  [on_device(): lax.dynamic_slice(tokens, (start, (me ^ d) * depth), (rows, depth))]
  transfers between devices with their start and end apart: 16 -> 25, of which waited for: 8 -> 14; matrix products, arithmetic and copies ran while one was open for 0% -> 0% of each run, Pallas kernels for 8% -> 9%
where the time goes in v2:
time: 81.9 us; the launch traced here: 81.2 us
  starting transfers between devices  34.1 us (42%)
  waiting for transfers between devices  24.7 us (30%)
  Pallas kernels  14.1 us (17%)
  local copies, waits for them, and re-layouts  6.87 us (8%)
  between operations  1.43 us (2%)
    ppermute x25, starting transfers between devices, swap(): return lax.ppermute(x, axis, [(i, i ^ d) for i in range(n)])  34.1 us
    ppermute x25, waiting for transfers between devices, swap(): return lax.ppermute(x, axis, [(i, i ^ d) for i in range(n)])  24.7 us
    pallas_call x1, Pallas kernels, outer(): pl.pallas_call(functools.partial(outer_kernel, n, kw // LANES), grid=(dep...  4.43 us
    unnamed x20, local copies, waits for them, and re-layouts  4.1 us
    pallas_call x2, Pallas kernels, project(): pl.pallas_call(functools.partial(project_kernel, n), out_shape=[jax.Shape...  3.19 us
    pallas_call x1, Pallas kernels, residue(): pl.pallas_call(functools.partial(residue_kernel, n), grid=(depth // tile,...  3.16 us
    dynamic_slice x1, local copies, waits for them, and re-layouts, on_device(): lax.dynamic_slice(tokens, (start, (me ^ d) * depth), (rows, depth))  2.66 us
  transfers between devices with their start and end apart: 25, of which 14 were waited for; matrix products, arithmetic and copies ran while one was open for 0% of the time, Pallas kernels for 9%

profile of v2, /device:TPU:1, one launch (start us, length us, event | category | flops | bytes accessed | tf_op | source)
XLA Modules:
  0.0 81.2 jit_solution(13685220828887632989)
XLA Ops:
  0.7 2.7 %dynamic-slice_bitcast_fusion = (bf16[64,2048]{1,0:T(8,128)(2,1)}, bf16[64,2048]{1,0:T(8,128)(2,1)}, bf16[64,2048]{1,0:T(8,128)(2,1)S(1)}, bf16[64,2048]{1,0:T(8...) fusion(bf16[1,128,8192]{2,1,0:T(8,128)(2,1)} %param.6, ...), kind=kLoop, calls=%fused_computation | loop fusion | bytes 4194320 | tf_op jit(solution)/shard_map/dynamic_slice | solution.py:287
  3.3 3.0 %collective-permute-start.2 = (bf16[64,2048]{1,0:T(8,128)(2,1)S(1)}, bf16[64,2048]{1,0:T(8,128)(2,1)S(1)}, u32[]{:S(2)}, u32[]{:S(2)}) collective-permute-start(bf16[64,2048]{1,0:T(8,128)(2,1)S(1)} %get-tuple-element.37), channel_id=1, source_target_pairs={{0,3},{1,2},{2,1},{3,0},{4,7},{5,6},{6,5},{7,4},{8,11},{9,10},{10,... | collective-permute-start | bytes 786440 | tf_op jit(solution)/shard_map/ppermute | solution.py:27
  6.7 2.3 %collective-permute-start.11 = (bf16[64,2048]{1,0:T(8,128)(2,1)}, bf16[64,2048]{1,0:T(8,128)(2,1)}, u32[]{:S(2)}, u32[]{:S(2)}) collective-permute-start(bf16[64,2048]{1,0:T(8,128)(2,1)} %get-tuple-element.34), channel_id=1, source_target_pairs={{0,3},{1,2},{2,1},{3,0},{4,7},{5,6},{6,5},{7,4},{8,11},{9,10},{10,... | collective-permute-start | bytes 786440 | tf_op jit(solution)/shard_map/ppermute | solution.py:27
  9.2 3.2 %collective-permute-done.2.refs_3_ = bf16[64,2048]{1,0:T(8,128)(2,1)S(1)} collective-permute-done((bf16[64,2048]{1,0:T(8,128)(2,1)S(1)}, bf16[64,2048]{1,0:T(8,128)(2,1)S(1)}, u32[]{:S(2)}, u32[]{:S(2)}) %collective-permute-start.2) | collective-permute-done | bytes 262176 | tf_op jit(solution)/shard_map/ppermute | solution.py:27
  12.4 1.1 %collective-permute-start.10 = (bf16[64,2048]{1,0:T(8,128)(2,1)}, bf16[64,2048]{1,0:T(8,128)(2,1)}, u32[]{:S(2)}, u32[]{:S(2)}) collective-permute-start(bf16[64,2048]{1,0:T(8,128)(2,1)} %get-tuple-element.41), channel_id=1, source_target_pairs={{0,2},{1,3},{2,0},{3,1},{4,6},{5,7},{6,4},{7,5},{8,10},{9,11},{10,... | collective-permute-start | bytes 786440 | tf_op jit(solution)/shard_map/ppermute | solution.py:27
  13.5 5.9 %collective-permute-done.1.refs_2_ = bf16[64,2048]{1,0:T(8,128)(2,1)S(1)} collective-permute-done((bf16[64,2048]{1,0:T(8,128)(2,1)S(1)}, bf16[64,2048]{1,0:T(8,128)(2,1)S(1)}, u32[]{:S(2)}, u32[]{:S(2)}) %collective-permute-start.1) | collective-permute-done | bytes 262176 | tf_op jit(solution)/shard_map/ppermute | solution.py:27
  19.4 1.3 %project.2 = (f32[64,512]{1,0:T(8,128)S(1)}, bf16[64,512]{1,0:T(8,128)(2,1)S(1)}, bf16[64,512]{1,0:T(8,128)(2,1)S(1)}, bf16[64,512]{1,0:T(8,128)(2,1)}, bf16[256,2048]{1,0:T(8,128)(2,1)S(1)}) custom-call(bf16[64,2048]{1,0:T(8,128)(2,1)S(1)} %get-tuple-element.40.refs_0_, bf16[64,2048]{1,0:T(8,128)(2,1)S(1)} %collective-permute-done.refs_1_, ...), custom_call_target="tpu_custom_call" | custom-call | flops 536870912 | bytes 3145728 | tf_op jit(solution)/shard_map/project/pallas_call | solution.py:44
  21.4 1.8 %collective-permute-start.4 = (bf16[64,512]{1,0:T(8,128)(2,1)S(1)}, bf16[64,512]{1,0:T(8,128)(2,1)S(1)}, u32[]{:S(2)}, u32[]{:S(2)}) collective-permute-start(bf16[64,512]{1,0:T(8,128)(2,1)S(1)} %get-tuple-element.20), channel_id=1, source_target_pairs={{0,2},{1,3},{2,0},{3,1},{4,6},{5,7},{6,4},{7,5},{8,10},{9,11},{10,... | collective-permute-start | bytes 196616 | tf_op jit(solution)/shard_map/ppermute | solution.py:27
  23.1 1.2 %collective-permute-start.5 = (bf16[64,512]{1,0:T(8,128)(2,1)}, bf16[64,512]{1,0:T(8,128)(2,1)}, u32[]{:S(2)}, u32[]{:S(2)}) collective-permute-start(bf16[64,512]{1,0:T(8,128)(2,1)} %get-tuple-element.21), channel_id=1, source_target_pairs={{0,3},{1,2},{2,1},{3,0},{4,7},{5,6},{6,5},{7,4},{8,11},{9,10},{10,... | collective-permute-start | bytes 196616 | tf_op jit(solution)/shard_map/ppermute | solution.py:27
  24.3 8.4 %collective-permute-done.4.refs_2_ = bf16[64,512]{1,0:T(8,128)(2,1)S(1)} collective-permute-done((bf16[64,512]{1,0:T(8,128)(2,1)S(1)}, bf16[64,512]{1,0:T(8,128)(2,1)S(1)}, u32[]{:S(2)}, u32[]{:S(2)}) %collective-permute-start.4) | collective-permute-done | bytes 65568 | tf_op jit(solution)/shard_map/ppermute | solution.py:27
  33.4 1.4 %collective-permute-start.3 = (bf16[64,512]{1,0:T(8,128)(2,1)S(1)}, bf16[64,512]{1,0:T(8,128)(2,1)}, u32[]{:S(2)}, u32[]{:S(2)}) collective-permute-start(bf16[64,512]{1,0:T(8,128)(2,1)S(1)} %get-tuple-element.19.after), channel_id=1, source_target_pairs={{0,1},{1,0},{2,3},{3,2},{4,5},{5,4},{6,7},{7,6},{8,9},{9,8},{10,11... | collective-permute-start | bytes 196616 | tf_op jit(solution)/shard_map/ppermute | solution.py:27
  36.6 1.1 %copy-done.3 = bf16[1,128,512]{2,1,0:T(8,128)(2,1)S(1)} copy-done((bf16[1,128,512]{2,1,0:T(8,128)(2,1)S(1)}, bf16[1,128,512]{2,1,0:T(8,128)(2,1)}, u32[]{:S(2)}) %copy-start.3) | copy-done | bytes 131096
  37.6 0.9 %copy-done.6 = f32[64,512]{1,0:T(8,128)S(1)} copy-done((f32[64,512]{1,0:T(8,128)S(1)}, f32[64,512]{1,0:T(8,128)}, u32[]{:S(2)}) %copy-start.6) | copy-done | bytes 131096
  38.5 0.8 %copy-done.8 = bf16[64,512]{1,0:T(8,128)(2,1)S(1)} copy-done((bf16[64,512]{1,0:T(8,128)(2,1)S(1)}, bf16[64,512]{1,0:T(8,128)(2,1)}, u32[]{:S(2)}) %copy-start.8) | copy-done | bytes 65560
  39.4 0.9 %slope.2.refs_6_.refs_0_ = bf16[64,512]{1,0:T(8,128)(2,1)S(1)} custom-call(f32[64,512]{1,0:T(8,128)S(1)} %copy-done.6, bf16[64,512]{1,0:T(8,128)(2,1)} %collective-permute-done.3.refs_1_, bf16[64,512]{1,0:T(8,128)(2,1)S(1)} %copy-done.8, bf16[64,512]{1,0:T(8,128)(2,1)} %collective-permute-done.5.refs_3_, bf16[128,512]{1,0:T(8,128)(2,1)S(1)} %bitcast.26, ...), custom_call_target="tpu_custom_call" | custom-call | flops 131072 | bytes 393216 | tf_op jit(solution)/shard_map/slope/pallas_call | solution.py:69
  40.3 1.3 %collective-permute-start.8 = (bf16[64,512]{1,0:T(8,128)(2,1)S(1)}, bf16[64,512]{1,0:T(8,128)(2,1)S(1)}, u32[]{:S(2)}, u32[]{:S(2)}) collective-permute-start(bf16[64,512]{1,0:T(8,128)(2,1)S(1)} %slope.2.refs_6_.refs_0_), channel_id=1, source_target_pairs={{0,3},{1,2},{2,1},{3,0},{4,7},{5,6},{6,5},{7,4},{8,11},{9,10},{10,... | collective-permute-start | bytes 196616 | tf_op jit(solution)/shard_map/ppermute | solution.py:27
  41.6 1.2 %collective-permute-start.7 = (bf16[64,512]{1,0:T(8,128)(2,1)S(1)}, bf16[64,512]{1,0:T(8,128)(2,1)S(1)}, u32[]{:S(2)}, u32[]{:S(2)}) collective-permute-start(bf16[64,512]{1,0:T(8,128)(2,1)S(1)} %slope.2.refs_6_.refs_0_), channel_id=1, source_target_pairs={{0,2},{1,3},{2,0},{3,1},{4,6},{5,7},{6,4},{7,5},{8,10},{9,11},{10,... | collective-permute-start | bytes 196616 | tf_op jit(solution)/shard_map/ppermute | solution.py:27
  43.0 1.0 %early.1 = (f32[128,128]{1,0:T(8,128)S(1)}, bf16[2048,512]{1,0:T(8,128)(2,1)S(1)}) custom-call(s32[128,1]{1,0:T(8,128)S(1)} %copy.8.slots.refs_11_, s32[1,128]{1,0:T(1,128)S(1)} %bitcast.29, s32[1,1]{1,0:T(1,128)S(6)} %copy.12.count, bf16[2048,512]{1,0:T(8,128)(2,1)S(1)} %bitcast.22), custom_call_target="tpu_custom_call" | custom-call | flops 536870912 | bytes 4194304 | tf_op jit(solution)/shard_map/early/pallas_call | solution.py:108
  45.1 1.2 %collective-permute-done.6.refs_7_.refs_1_ = bf16[64,512]{1,0:T(8,128)(2,1)S(1)} collective-permute-done((bf16[64,512]{1,0:T(8,128)(2,1)S(1)}, bf16[64,512]{1,0:T(8,128)(2,1)S(1)}, u32[]{:S(2)}, u32[]{:S(2)}) %collective-permute-start.6) | collective-permute-done | bytes 65568 | tf_op jit(solution)/shard_map/ppermute | solution.py:27
  46.3 1.8 %project.3 = (f32[64,512]{1,0:T(8,128)S(1)}, bf16[64,512]{1,0:T(8,128)(2,1)S(1)}, bf16[64,512]{1,0:T(8,128)(2,1)S(1)}, bf16[64,512]{1,0:T(8,128)(2,1)S(1)}, bf16[256,2048]{1,0:T(8,128)(2,1)S(1)}) custom-call(bf16[64,2048]{1,0:T(8,128)(2,1)S(1)} %get-tuple-element.36.refs_0_, bf16[64,2048]{1,0:T(8,128)(2,1)} %collective-permute-done.9.refs_1_, ...), custom_call_target="tpu_custom_call" | custom-call | flops 536870912 | bytes 3145728 | tf_op jit(solution)/shard_map/project/pallas_call | solution.py:44
  48.4 1.2 %collective-permute-start.14 = (bf16[64,512]{1,0:T(8,128)(2,1)S(1)}, bf16[64,512]{1,0:T(8,128)(2,1)S(1)}, u32[]{:S(2)}, u32[]{:S(2)}) collective-permute-start(bf16[64,512]{1,0:T(8,128)(2,1)S(1)} %get-tuple-element.28), channel_id=1, source_target_pairs={{0,3},{1,2},{2,1},{3,0},{4,7},{5,6},{6,5},{7,4},{8,11},{9,10},{10,... | collective-permute-start | bytes 196616 | tf_op jit(solution)/shard_map/ppermute | solution.py:27
  49.6 1.3 %collective-permute-start.12 = (bf16[64,512]{1,0:T(8,128)(2,1)S(1)}, bf16[64,512]{1,0:T(8,128)(2,1)S(1)}, u32[]{:S(2)}, u32[]{:S(2)}) collective-permute-start(bf16[64,512]{1,0:T(8,128)(2,1)S(1)} %get-tuple-element.26.after), channel_id=1, source_target_pairs={{0,1},{1,0},{2,3},{3,2},{4,5},{5,4},{6,7},{7,6},{8,9},{9,8},{10,11... | collective-permute-start | bytes 196616 | tf_op jit(solution)/shard_map/ppermute | solution.py:27
  51.5 1.0 %collective-permute-done.14.refs_3_ = bf16[64,512]{1,0:T(8,128)(2,1)S(1)} collective-permute-done((bf16[64,512]{1,0:T(8,128)(2,1)S(1)}, bf16[64,512]{1,0:T(8,128)(2,1)S(1)}, u32[]{:S(2)}, u32[]{:S(2)}) %collective-permute-start.14) | collective-permute-done | bytes 65568 | tf_op jit(solution)/shard_map/ppermute | solution.py:27
  52.4 0.8 collective-permute-done.12.refs_1_
  53.3 1.3 %collective-permute-start.17 = (bf16[64,512]{1,0:T(8,128)(2,1)S(1)}, bf16[64,512]{1,0:T(8,128)(2,1)S(1)}, u32[]{:S(2)}, u32[]{:S(2)}) collective-permute-start(bf16[64,512]{1,0:T(8,128)(2,1)S(1)} %slope.3.refs_4_), channel_id=1, source_target_pairs={{0,3},{1,2},{2,1},{3,0},{4,7},{5,6},{6,5},{7,4},{8,11},{9,10},{10,... | collective-permute-start | bytes 196616 | tf_op jit(solution)/shard_map/ppermute | solution.py:27
  56.0 1.8 %collective-permute-done.17.refs_7_ = bf16[64,512]{1,0:T(8,128)(2,1)S(1)} collective-permute-done((bf16[64,512]{1,0:T(8,128)(2,1)S(1)}, bf16[64,512]{1,0:T(8,128)(2,1)S(1)}, u32[]{:S(2)}, u32[]{:S(2)}) %collective-permute-start.17) | collective-permute-done | bytes 65568 | tf_op jit(solution)/shard_map/ppermute | solution.py:27
  58.7 9.8 %collective-permute-start.24 = (bf16[144,128]{1,0:T(8,128)(2,1)S(1)}, bf16[144,128]{1,0:T(8,128)(2,1)S(1)}, u32[]{:S(2)}, u32[]{:S(2)}) collective-permute-start(bf16[144,128]{1,0:T(8,128)(2,1)S(1)} %kept.1.refs_0_), channel_id=1, source_target_pairs={{0,28},{4,24},{8,20},{12,16},{16,12},{20,8},{24,4},{28,0},{1,29},{... | collective-permute-start | bytes 110600 | tf_op jit(solution)/shard_map/ppermute | solution.py:27
  68.7 2.5 %collective-permute-start.21 = (bf16[144,128]{1,0:T(8,128)(2,1)S(1)}, bf16[144,128]{1,0:T(8,128)(2,1)S(1)}, u32[]{:S(2)}, u32[]{:S(2)}) collective-permute-start(bf16[144,128]{1,0:T(8,128)(2,1)S(1)} %kept.1.refs_0_), channel_id=1, source_target_pairs={{0,16},{4,20},{8,24},{12,28},{16,0},{20,4},{24,8},{28,12},{1,17},{... | collective-permute-start | bytes 110600 | tf_op jit(solution)/shard_map/ppermute | solution.py:27
  71.2 1.1 %collective-permute-start.20 = (bf16[144,128]{1,0:T(8,128)(2,1)S(1)}, bf16[144,128]{1,0:T(8,128)(2,1)S(1)}, u32[]{:S(2)}, u32[]{:S(2)}) collective-permute-start(bf16[144,128]{1,0:T(8,128)(2,1)S(1)} %kept.1.refs_0_), channel_id=1, source_target_pairs={{0,12},{4,8},{8,4},{12,0},{16,28},{20,24},{24,20},{28,16},{1,13},{... | collective-permute-start | bytes 110600 | tf_op jit(solution)/shard_map/ppermute | solution.py:27
  72.3 0.8 collective-permute-start.19
  73.4 3.2 %residue.1 = bf16[2048,512]{1,0:T(8,128)(2,1)} custom-call(bf16[64,512]{1,0:T(8,128)(2,1)S(1)} %slope.2.refs_6_.refs_0_, bf16[64,512]{1,0:T(8,128)(2,1)S(1)} %collective-permute-done.6.refs_7_.refs_1_, bf16[64,512]{1,0:T(8,128)(2,1)S(1)} %collective-permute-done.7.refs_8_.refs_2_, bf16[64,512]{1,0:T(8,128)(2,1)S(1)} %collective-permute-done.8.refs_9_.refs_3_, ...), custom_call_target="tpu_custom_call" | custom-call | flops 1073741824 | bytes 8388608 | tf_op jit(solution)/shard_map/residue/pallas_call | solution.py:214
  76.8 4.4 %outer.1 = f32[2048,512]{1,0:T(8,128)} custom-call(bf16[144,128]{1,0:T(8,128)(2,1)S(1)} %kept.1.refs_0_, bf16[144,128]{1,0:T(8,128)(2,1)S(1)} %collective-permute-done.18.refs_1_, bf16[144,128]{1,0:T(8,128)(2,1)S(1)} %collective-permute-done.19.refs_2_, bf16[144,128]{1,0:T(8,128)(2,1)S(1)} %collective-permute-done.20.refs_3_, ...), custom_call_target="tpu_custom_call" | custom-call | flops 2147483648 | bytes 4194304 | tf_op jit(solution)/shard_map/outer/pallas_call | solution.py:257
  (50 shorter events, 8.1 us)
Async XLA Ops:
  0.6 18.7 %copy-start.1 = (bf16[1,2048,512]{2,1,0:T(8,128)(2,1)S(1)}, bf16[1,2048,512]{2,1,0:T(8,128)(2,1)}, u32[]{:S(2)}) copy-start(bf16[1,2048,512]{2,1,0:T(8,128)(2,1)} %param.8) | copy-start | bytes 6291460
  3.3 32.1 %copy-start.9 = (s32[1,1,128]{2,1,0:T(1,128)S(1)}, s32[1,1,128]{2,1,0:T(1,128)}, u32[]{:S(2)}) copy-start(s32[1,1,128]{2,1,0:T(1,128)} %param.11) | copy-start | bytes 1540
  3.3 9.1 %collective-permute-start.2 = (bf16[64,2048]{1,0:T(8,128)(2,1)S(1)}, bf16[64,2048]{1,0:T(8,128)(2,1)S(1)}, u32[]{:S(2)}, u32[]{:S(2)}) collective-permute-start(bf16[64,2048]{1,0:T(8,128)(2,1)S(1)} %get-tuple-element.37), channel_id=1, source_target_pairs={{0,3},{1,2},{2,1},{3,0},{4,7},{5,6},{6,5},{7,4},{8,11},{9,10},{10,... | collective-permute-start | bytes 786440 | tf_op jit(solution)/shard_map/ppermute | solution.py:27
  6.3 13.1 %collective-permute-start.1 = (bf16[64,2048]{1,0:T(8,128)(2,1)S(1)}, bf16[64,2048]{1,0:T(8,128)(2,1)S(1)}, u32[]{:S(2)}, u32[]{:S(2)}) collective-permute-start(bf16[64,2048]{1,0:T(8,128)(2,1)S(1)} %get-tuple-element.38), channel_id=1, source_target_pairs={{0,2},{1,3},{2,0},{3,1},{4,6},{5,7},{6,4},{7,5},{8,10},{9,11},{10,... | collective-permute-start | bytes 786440 | tf_op jit(solution)/shard_map/ppermute | solution.py:27
  6.5 12.8 %collective-permute-start = (bf16[64,2048]{1,0:T(8,128)(2,1)S(1)}, bf16[64,2048]{1,0:T(8,128)(2,1)S(1)}, u32[]{:S(2)}, u32[]{:S(2)}) collective-permute-start(bf16[64,2048]{1,0:T(8,128)(2,1)S(1)} %get-tuple-element.39), channel_id=1, source_target_pairs={{0,1},{1,0},{2,3},{3,2},{4,5},{5,4},{6,7},{7,6},{8,9},{9,8},{10,11... | collective-permute-start | bytes 786440 | tf_op jit(solution)/shard_map/ppermute | solution.py:27
  6.7 36.1 %collective-permute-start.11 = (bf16[64,2048]{1,0:T(8,128)(2,1)}, bf16[64,2048]{1,0:T(8,128)(2,1)}, u32[]{:S(2)}, u32[]{:S(2)}) collective-permute-start(bf16[64,2048]{1,0:T(8,128)(2,1)} %get-tuple-element.34), channel_id=1, source_target_pairs={{0,3},{1,2},{2,1},{3,0},{4,7},{5,6},{6,5},{7,4},{8,11},{9,10},{10,... | collective-permute-start | bytes 786440 | tf_op jit(solution)/shard_map/ppermute | solution.py:27
  9.0 35.1 %collective-permute-start.9 = (bf16[64,2048]{1,0:T(8,128)(2,1)}, bf16[64,2048]{1,0:T(8,128)(2,1)}, u32[]{:S(2)}, u32[]{:S(2)}) collective-permute-start(bf16[64,2048]{1,0:T(8,128)(2,1)} %get-tuple-element.35), channel_id=1, source_target_pairs={{0,1},{1,0},{2,3},{3,2},{4,5},{5,4},{6,7},{7,6},{8,9},{9,8},{10,11... | collective-permute-start | bytes 786440 | tf_op jit(solution)/shard_map/ppermute | solution.py:27
  12.4 31.7 %collective-permute-start.10 = (bf16[64,2048]{1,0:T(8,128)(2,1)}, bf16[64,2048]{1,0:T(8,128)(2,1)}, u32[]{:S(2)}, u32[]{:S(2)}) collective-permute-start(bf16[64,2048]{1,0:T(8,128)(2,1)} %get-tuple-element.41), channel_id=1, source_target_pairs={{0,2},{1,3},{2,0},{3,1},{4,6},{5,7},{6,4},{7,5},{8,10},{9,11},{10,... | collective-permute-start | bytes 786440 | tf_op jit(solution)/shard_map/ppermute | solution.py:27
  21.4 21.6 %copy-start = (bf16[1,2048,512]{2,1,0:T(8,128)(2,1)S(1)}, bf16[1,2048,512]{2,1,0:T(8,128)(2,1)}, u32[]{:S(2)}) copy-start(bf16[1,2048,512]{2,1,0:T(8,128)(2,1)} %param.9) | copy-start | bytes 6291460
  21.4 11.4 %collective-permute-start.4 = (bf16[64,512]{1,0:T(8,128)(2,1)S(1)}, bf16[64,512]{1,0:T(8,128)(2,1)S(1)}, u32[]{:S(2)}, u32[]{:S(2)}) collective-permute-start(bf16[64,512]{1,0:T(8,128)(2,1)S(1)} %get-tuple-element.20), channel_id=1, source_target_pairs={{0,2},{1,3},{2,0},{3,1},{4,6},{5,7},{6,4},{7,5},{8,10},{9,11},{10,... | collective-permute-start | bytes 196616 | tf_op jit(solution)/shard_map/ppermute | solution.py:27
  23.1 13.0 %collective-permute-start.5 = (bf16[64,512]{1,0:T(8,128)(2,1)}, bf16[64,512]{1,0:T(8,128)(2,1)}, u32[]{:S(2)}, u32[]{:S(2)}) collective-permute-start(bf16[64,512]{1,0:T(8,128)(2,1)} %get-tuple-element.21), channel_id=1, source_target_pairs={{0,3},{1,2},{2,1},{3,0},{4,7},{5,6},{6,5},{7,4},{8,11},{9,10},{10,... | collective-permute-start | bytes 196616 | tf_op jit(solution)/shard_map/ppermute | solution.py:27
  33.4 3.2 %collective-permute-start.3 = (bf16[64,512]{1,0:T(8,128)(2,1)S(1)}, bf16[64,512]{1,0:T(8,128)(2,1)}, u32[]{:S(2)}, u32[]{:S(2)}) collective-permute-start(bf16[64,512]{1,0:T(8,128)(2,1)S(1)} %get-tuple-element.19.after), channel_id=1, source_target_pairs={{0,1},{1,0},{2,3},{3,2},{4,5},{5,4},{6,7},{7,6},{8,9},{9,8},{10,11... | collective-permute-start | bytes 196616 | tf_op jit(solution)/shard_map/ppermute | solution.py:27
  36.1 10.2 %copy-start.2 = (bf16[1,2048,512]{2,1,0:T(8,128)(2,1)S(1)}, bf16[1,2048,512]{2,1,0:T(8,128)(2,1)}, u32[]{:S(2)}) copy-start(bf16[1,2048,512]{2,1,0:T(8,128)(2,1)} %param.8) | copy-start | bytes 6291460
  36.6 1.1 %copy-start.3 = (bf16[1,128,512]{2,1,0:T(8,128)(2,1)S(1)}, bf16[1,128,512]{2,1,0:T(8,128)(2,1)}, u32[]{:S(2)}) copy-start(bf16[1,128,512]{2,1,0:T(8,128)(2,1)} %param.7) | copy-start | bytes 393220
  37.6 0.9 %copy-start.6 = (f32[64,512]{1,0:T(8,128)S(1)}, f32[64,512]{1,0:T(8,128)}, u32[]{:S(2)}) copy-start(f32[64,512]{1,0:T(8,128)} %copy-done.5) | copy-start | bytes 393220
  40.3 4.1 %collective-permute-start.8 = (bf16[64,512]{1,0:T(8,128)(2,1)S(1)}, bf16[64,512]{1,0:T(8,128)(2,1)S(1)}, u32[]{:S(2)}, u32[]{:S(2)}) collective-permute-start(bf16[64,512]{1,0:T(8,128)(2,1)S(1)} %slope.2.refs_6_.refs_0_), channel_id=1, source_target_pairs={{0,3},{1,2},{2,1},{3,0},{4,7},{5,6},{6,5},{7,4},{8,11},{9,10},{10,... | collective-permute-start | bytes 196616 | tf_op jit(solution)/shard_map/ppermute | solution.py:27
  41.6 3.5 %collective-permute-start.7 = (bf16[64,512]{1,0:T(8,128)(2,1)S(1)}, bf16[64,512]{1,0:T(8,128)(2,1)S(1)}, u32[]{:S(2)}, u32[]{:S(2)}) collective-permute-start(bf16[64,512]{1,0:T(8,128)(2,1)S(1)} %slope.2.refs_6_.refs_0_), channel_id=1, source_target_pairs={{0,2},{1,3},{2,0},{3,1},{4,6},{5,7},{6,4},{7,5},{8,10},{9,11},{10,... | collective-permute-start | bytes 196616 | tf_op jit(solution)/shard_map/ppermute | solution.py:27
  42.8 3.5 %collective-permute-start.6 = (bf16[64,512]{1,0:T(8,128)(2,1)S(1)}, bf16[64,512]{1,0:T(8,128)(2,1)S(1)}, u32[]{:S(2)}, u32[]{:S(2)}) collective-permute-start(bf16[64,512]{1,0:T(8,128)(2,1)S(1)} %slope.2.refs_6_.refs_0_), channel_id=1, source_target_pairs={{0,1},{1,0},{2,3},{3,2},{4,5},{5,4},{6,7},{7,6},{8,9},{9,8},{10,11... | collective-permute-start | bytes 196616 | tf_op jit(solution)/shard_map/ppermute | solution.py:27
  46.3 6.9 %copy-start.4 = (bf16[1,128,512]{2,1,0:T(8,128)(2,1)S(1)}, bf16[1,128,512]{2,1,0:T(8,128)(2,1)}, u32[]{:S(2)}) copy-start(bf16[1,128,512]{2,1,0:T(8,128)(2,1)} %param.7) | copy-start | bytes 393220
  48.2 3.3 %collective-permute-start.13 = (bf16[64,512]{1,0:T(8,128)(2,1)S(1)}, bf16[64,512]{1,0:T(8,128)(2,1)S(1)}, u32[]{:S(2)}, u32[]{:S(2)}) collective-permute-start(bf16[64,512]{1,0:T(8,128)(2,1)S(1)} %get-tuple-element.27), channel_id=1, source_target_pairs={{0,2},{1,3},{2,0},{3,1},{4,6},{5,7},{6,4},{7,5},{8,10},{9,11},{10,... | collective-permute-start | bytes 196616 | tf_op jit(solution)/shard_map/ppermute | solution.py:27
  48.4 4.0 %collective-permute-start.14 = (bf16[64,512]{1,0:T(8,128)(2,1)S(1)}, bf16[64,512]{1,0:T(8,128)(2,1)S(1)}, u32[]{:S(2)}, u32[]{:S(2)}) collective-permute-start(bf16[64,512]{1,0:T(8,128)(2,1)S(1)} %get-tuple-element.28), channel_id=1, source_target_pairs={{0,3},{1,2},{2,1},{3,0},{4,7},{5,6},{6,5},{7,4},{8,11},{9,10},{10,... | collective-permute-start | bytes 196616 | tf_op jit(solution)/shard_map/ppermute | solution.py:27
  49.6 3.6 %collective-permute-start.12 = (bf16[64,512]{1,0:T(8,128)(2,1)S(1)}, bf16[64,512]{1,0:T(8,128)(2,1)S(1)}, u32[]{:S(2)}, u32[]{:S(2)}) collective-permute-start(bf16[64,512]{1,0:T(8,128)(2,1)S(1)} %get-tuple-element.26.after), channel_id=1, source_target_pairs={{0,1},{1,0},{2,3},{3,2},{4,5},{5,4},{6,7},{7,6},{8,9},{9,8},{10,11... | collective-permute-start | bytes 196616 | tf_op jit(solution)/shard_map/ppermute | solution.py:27
  53.3 4.5 %collective-permute-start.17 = (bf16[64,512]{1,0:T(8,128)(2,1)S(1)}, bf16[64,512]{1,0:T(8,128)(2,1)S(1)}, u32[]{:S(2)}, u32[]{:S(2)}) collective-permute-start(bf16[64,512]{1,0:T(8,128)(2,1)S(1)} %slope.3.refs_4_), channel_id=1, source_target_pairs={{0,3},{1,2},{2,1},{3,0},{4,7},{5,6},{6,5},{7,4},{8,11},{9,10},{10,... | collective-permute-start | bytes 196616 | tf_op jit(solution)/shard_map/ppermute | solution.py:27
  54.6 3.5 %collective-permute-start.16 = (bf16[64,512]{1,0:T(8,128)(2,1)S(1)}, bf16[64,512]{1,0:T(8,128)(2,1)S(1)}, u32[]{:S(2)}, u32[]{:S(2)}) collective-permute-start(bf16[64,512]{1,0:T(8,128)(2,1)S(1)} %slope.3.refs_4_), channel_id=1, source_target_pairs={{0,2},{1,3},{2,0},{3,1},{4,6},{5,7},{6,4},{7,5},{8,10},{9,11},{10,... | collective-permute-start | bytes 196616 | tf_op jit(solution)/shard_map/ppermute | solution.py:27
  55.3 3.1 %collective-permute-start.15 = (bf16[64,512]{1,0:T(8,128)(2,1)S(1)}, bf16[64,512]{1,0:T(8,128)(2,1)S(1)}, u32[]{:S(2)}, u32[]{:S(2)}) collective-permute-start(bf16[64,512]{1,0:T(8,128)(2,1)S(1)} %slope.3.refs_4_), channel_id=1, source_target_pairs={{0,1},{1,0},{2,3},{3,2},{4,5},{5,4},{6,7},{7,6},{8,9},{9,8},{10,11... | collective-permute-start | bytes 196616 | tf_op jit(solution)/shard_map/ppermute | solution.py:27
  58.7 13.7 %collective-permute-start.24 = (bf16[144,128]{1,0:T(8,128)(2,1)S(1)}, bf16[144,128]{1,0:T(8,128)(2,1)S(1)}, u32[]{:S(2)}, u32[]{:S(2)}) collective-permute-start(bf16[144,128]{1,0:T(8,128)(2,1)S(1)} %kept.1.refs_0_), channel_id=1, source_target_pairs={{0,28},{4,24},{8,20},{12,16},{16,12},{20,8},{24,4},{28,0},{1,29},{... | collective-permute-start | bytes 110600 | tf_op jit(solution)/shard_map/ppermute | solution.py:27
  68.5 4.7 %collective-permute-start.23 = (bf16[144,128]{1,0:T(8,128)(2,1)S(1)}, bf16[144,128]{1,0:T(8,128)(2,1)S(1)}, u32[]{:S(2)}, u32[]{:S(2)}) collective-permute-start(bf16[144,128]{1,0:T(8,128)(2,1)S(1)} %kept.1.refs_0_), channel_id=1, source_target_pairs={{0,24},{4,28},{8,16},{12,20},{16,8},{20,12},{24,0},{28,4},{1,25},{... | collective-permute-start | bytes 110600 | tf_op jit(solution)/shard_map/ppermute | solution.py:27
  68.7 7.8 %collective-permute-start.22 = (bf16[144,128]{1,0:T(8,128)(2,1)S(1)}, bf16[144,128]{1,0:T(8,128)(2,1)S(1)}, u32[]{:S(2)}, u32[]{:S(2)}) collective-permute-start(bf16[144,128]{1,0:T(8,128)(2,1)S(1)} %kept.1.refs_0_), channel_id=1, source_target_pairs={{0,20},{4,16},{8,28},{12,24},{16,4},{20,0},{24,12},{28,8},{1,21},{... | collective-permute-start | bytes 110600 | tf_op jit(solution)/shard_map/ppermute | solution.py:27
  68.7 7.8 %collective-permute-start.21 = (bf16[144,128]{1,0:T(8,128)(2,1)S(1)}, bf16[144,128]{1,0:T(8,128)(2,1)S(1)}, u32[]{:S(2)}, u32[]{:S(2)}) collective-permute-start(bf16[144,128]{1,0:T(8,128)(2,1)S(1)} %kept.1.refs_0_), channel_id=1, source_target_pairs={{0,16},{4,20},{8,24},{12,28},{16,0},{20,4},{24,8},{28,12},{1,17},{... | collective-permute-start | bytes 110600 | tf_op jit(solution)/shard_map/ppermute | solution.py:27
  71.2 5.3 %collective-permute-start.20 = (bf16[144,128]{1,0:T(8,128)(2,1)S(1)}, bf16[144,128]{1,0:T(8,128)(2,1)S(1)}, u32[]{:S(2)}, u32[]{:S(2)}) collective-permute-start(bf16[144,128]{1,0:T(8,128)(2,1)S(1)} %kept.1.refs_0_), channel_id=1, source_target_pairs={{0,12},{4,8},{8,4},{12,0},{16,28},{20,24},{24,20},{28,16},{1,13},{... | collective-permute-start | bytes 110600 | tf_op jit(solution)/shard_map/ppermute | solution.py:27
  72.3 4.5 %collective-permute-start.19 = (bf16[144,128]{1,0:T(8,128)(2,1)S(1)}, bf16[144,128]{1,0:T(8,128)(2,1)S(1)}, u32[]{:S(2)}, u32[]{:S(2)}) collective-permute-start(bf16[144,128]{1,0:T(8,128)(2,1)S(1)} %kept.1.refs_0_), channel_id=1, source_target_pairs={{0,8},{4,12},{8,0},{12,4},{16,24},{20,28},{24,16},{28,20},{1,9},{5... | collective-permute-start | bytes 110600 | tf_op jit(solution)/shard_map/ppermute | solution.py:27
  73.2 3.6 %collective-permute-start.18 = (bf16[144,128]{1,0:T(8,128)(2,1)S(1)}, bf16[144,128]{1,0:T(8,128)(2,1)S(1)}, u32[]{:S(2)}, u32[]{:S(2)}) collective-permute-start(bf16[144,128]{1,0:T(8,128)(2,1)S(1)} %kept.1.refs_0_), channel_id=1, source_target_pairs={{0,4},{4,0},{8,12},{12,8},{16,20},{20,16},{24,28},{28,24},{1,5},{5... | collective-permute-start | bytes 110600 | tf_op jit(solution)/shard_map/ppermute | solution.py:27
  (3 other events, 2.1 us)

commit v3 on v2

v3 whole, which is shorter than its diff:
```python
import functools

import jax
import jax.numpy as jnp
from jax import lax
from jax.experimental import pallas as pl
from jax.experimental.pallas import tpu as pltpu
from jax.sharding import PartitionSpec as P

LANES = 128
ANY = pl.BlockSpec(memory_space=pl.ANY)
VMEM = pl.BlockSpec(memory_space=pltpu.VMEM)
SMEM = pl.BlockSpec(memory_space=pltpu.SMEM)
MIB = 1024 * 1024


def params(mib):
    return pltpu.CompilerParams(vmem_limit_bytes=mib * MIB)


def cost(flops, nbytes):
    return pl.CostEstimate(flops=int(flops), bytes_accessed=int(nbytes), transcendentals=0)


def swap(x, axis, n, d):
    return lax.ppermute(x, axis, [(i, i ^ d) for i in range(n)])


def cut_kernel(cuts, tokens, *refs):
    outs, sems = refs[-len(cuts) - 1 : -1], refs[-1]
    me = lax.axis_index("shard")
    copies = []
    for k, (d, low, rows) in enumerate(cuts):
        depth = outs[k].shape[1]
        columns = pl.ds(pl.multiple_of((me ^ d) * depth, LANES), depth)
        copy = pltpu.make_async_copy(tokens.at[pl.ds(low, rows), columns], outs[k], sems.at[k])
        copy.start()
        copies.append(copy)
    for copy in copies:
        copy.wait()


def cut(tokens, depth, cuts, after):
    return pl.pallas_call(
        functools.partial(cut_kernel, cuts),
        out_shape=[jax.ShapeDtypeStruct((rows, depth), tokens.dtype) for _, _, rows in cuts],
        in_specs=[ANY] * (1 + len(after)),
        scratch_shapes=[pltpu.SemaphoreType.DMA((len(cuts),))],
        compiler_params=params(16),
        cost_estimate=cost(0, 4 * depth * sum(rows for _, _, rows in cuts)),
        name="cut",
    )(tokens, *after)


def project_kernel(n, *refs):
    pieces, w, outs, x = refs[:n], refs[n], refs[-n - 1 : -1], refs[-1]
    start = 0
    for piece in pieces:
        x[start : start + piece.shape[0], :] = piece[...]
        start += piece.shape[0]
    full = jnp.dot(x[...], w[...], preferred_element_type=jnp.float32)
    start = 0
    for out in outs:
        out[...] = full[start : start + out.shape[0], :].astype(out.dtype)
        start += out.shape[0]


def project(pieces, types, w, after):
    n = len(pieces)
    rows, depth = sum(p.shape[0] for p in pieces), pieces[0].shape[1]
    kw = w.shape[1]
    result = pl.pallas_call(
        functools.partial(project_kernel, n),
        out_shape=[jax.ShapeDtypeStruct((p.shape[0], kw), t) for p, t in zip(pieces, types)]
        + [jax.ShapeDtypeStruct((rows, depth), jnp.bfloat16)],
        in_specs=[VMEM] * (n + 1) + [ANY] * len(after),
        compiler_params=params(24),
        cost_estimate=cost(2 * rows * depth * kw, 2 * depth * (rows + kw)),
        name="project",
    )(*pieces, w, *after)
    return result[:n], result[n]


def slope_kernel(tok_dev, n, *refs):
    goal, mine, out = refs[0], refs[1], refs[-1]
    whole = refs[2 : 2 + n]
    halves = refs[2 + n : -2]
    half = out.shape[0] // 2
    for part in range(2):
        rows = slice(part * half, (part + 1) * half)
        key_proj = mine[rows, :]
        for product in whole:
            key_proj += product[rows, :].astype(jnp.float32)
        for product in halves[part::2]:
            key_proj += product[...].astype(jnp.float32)
        gap = key_proj - goal[rows, :].astype(jnp.float32)
        out[rows, :] = (gap / tok_dev).astype(jnp.bfloat16)


def slope(goal, mine, whole, halves, after):
    return pl.pallas_call(
        functools.partial(slope_kernel, goal.shape[0], len(whole)),
        out_shape=jax.ShapeDtypeStruct(mine.shape, jnp.bfloat16),
        in_specs=[VMEM] * (2 + len(whole) + len(halves)) + [ANY],
        compiler_params=params(8),
        cost_estimate=cost(4 * mine.size, 12 * mine.size),
        name="slope",
    )(goal, mine, *whole, *halves, after)


def pick_columns(wide, column):
    out = jnp.zeros((wide.shape[0], LANES), jnp.float32)
    for c in range(wide.shape[1] // LANES):
        out += jnp.where(column == c, wide[:, c * LANES : (c + 1) * LANES], 0.0)
    return out


def early_kernel(per_row, slots, slot_row, count, fb, after, fbk, keep):
    depth, kw = fb.shape
    cap = slots.shape[0]
    slot = slots[...]
    hot = slot // per_row == lax.broadcasted_iota(jnp.int32, (cap, depth), 1)
    hot = hot.astype(jnp.float32).astype(jnp.bfloat16)
    used = lax.broadcasted_iota(jnp.int32, (cap, 1), 0) < count[0, 0]
    wide = jnp.dot(hot, fb[...], preferred_element_type=jnp.float32)
    fbk[...] = jnp.where(used, pick_columns(wide, slot % per_row), 0.0)
    group = lax.broadcasted_iota(jnp.int32, (cap, kw), 1) // LANES
    mark = jnp.where(used & (slot % per_row == group), 1.0, 0.0).astype(jnp.bfloat16)
    tile = min(depth, 512)
    for t in range(depth // tile):
        line = lax.broadcasted_iota(jnp.int32, (tile, cap), 0) + t * tile
        hot = (slot_row[...] // per_row == line).astype(jnp.float32).astype(jnp.bfloat16)
        mask = jnp.dot(hot, mark, preferred_element_type=jnp.float32)
        keep[t * tile : (t + 1) * tile, :] = (1.0 - mask).astype(jnp.bfloat16)


def early(slots, slot_row, count, fb, after):
    depth, kw = fb.shape
    cap = slots.shape[0]
    return pl.pallas_call(
        functools.partial(early_kernel, kw // LANES),
        out_shape=[
            jax.ShapeDtypeStruct((cap, LANES), jnp.float32),
            jax.ShapeDtypeStruct((depth, kw), jnp.bfloat16),
        ],
        in_specs=[VMEM, VMEM, SMEM, VMEM, ANY],
        compiler_params=params(24),
        cost_estimate=cost(4 * cap * depth * kw, 4 * depth * kw),
        name="early",
    )(slots, slot_row, count, fb, after)


def prepare_kernel(per_row, n, *refs):
    xs, (slots, count), (xg, xt) = refs[:n], refs[n : n + 2], refs[-2:]
    depth = xs[0].shape[1]
    cap = slots.shape[0]
    used = lax.broadcasted_iota(jnp.int32, (cap, 1), 0) < count[0, 0]
    line = jnp.where(used, slots[...] // per_row, depth)
    hot = line == lax.broadcasted_iota(jnp.int32, (cap, depth), 1)
    hot = hot.astype(jnp.float32).astype(jnp.bfloat16)
    start = 0
    for x in xs:
        rows = x.shape[0]
        xg[:, start : start + rows] = lax.dot_general(
            hot, x[...], (((1,), (1,)), ((), ())), preferred_element_type=jnp.float32
        ).astype(jnp.bfloat16)
        xt[:, start : start + rows] = x[...].T
        start += rows


def prepare(xs, slots, count, per_row, after):
    rows, depth = sum(x.shape[0] for x in xs), xs[0].shape[1]
    cap = slots.shape[0]
    return pl.pallas_call(
        functools.partial(prepare_kernel, per_row, len(xs)),
        out_shape=[
            jax.ShapeDtypeStruct((cap, rows), jnp.bfloat16),
            jax.ShapeDtypeStruct((depth, rows), jnp.bfloat16),
        ],
        in_specs=[VMEM] * (len(xs) + 1) + [SMEM] + [ANY] * len(after),
        compiler_params=params(24),
        cost_estimate=cost(2 * cap * depth * rows, 4 * depth * rows),
        name="prepare",
    )(*xs, slots, count, *after)


def stack(slopes, order, s):
    start = 0
    for d, low, high in order:
        s[start : start + high - low, :] = slopes[d][low:high, :]
        start += high - low


def kept_kernel(per_row, order, *refs):
    n = len({d for d, _, _ in order})
    slopes, (fbk, slots, slot_row), out, s = refs[:n], refs[-5:-2], refs[-2], refs[-1]
    xgs = refs[n:-5]
    cap = slots.shape[0]
    stack(slopes, order, s)
    wide, start = 0.0, 0
    for xg in xgs:
        rows = xg.shape[1]
        wide += jnp.dot(xg[...], s[start : start + rows, :], preferred_element_type=jnp.float32)
        start += rows
    value = pick_columns(wide, slots[...] % per_row) + fbk[...]
    out[:cap, :] = value.astype(jnp.bfloat16)
    tail = out.shape[0] - cap
    number = jnp.broadcast_to(slot_row[...], (tail, cap))
    line = lax.broadcasted_iota(jnp.int32, (tail, cap), 0)
    number = jnp.where(line == 0, number // LANES, number % LANES)
    out[cap:, :] = number.astype(jnp.float32).astype(jnp.bfloat16)


def kept(slopes, order, xgs, fbk, slots, slot_row):
    cap = slots.shape[0]
    rows, kw = slopes[0].shape
    total = len(slopes) * rows
    return pl.pallas_call(
        functools.partial(kept_kernel, kw // LANES, order),
        out_shape=jax.ShapeDtypeStruct((cap + 16, LANES), jnp.bfloat16),
        scratch_shapes=[pltpu.VMEM((total, kw), jnp.bfloat16)],
        compiler_params=params(8),
        cost_estimate=cost(2 * cap * total * kw, 2 * total * kw),
        name="kept",
    )(*slopes, *xgs, fbk, slots, slot_row)


def residue_kernel(order, tile, *refs):
    n = len({d for d, _, _ in order})
    slopes, xts, (fb, keep, out, s, held, sems) = refs[:n], refs[n:-6], refs[-6:]
    stack(slopes, order, s)
    copies = []
    for t in range(out.shape[0] // tile):
        rows = slice(t * tile, (t + 1) * tile)
        pseudo, start = fb[rows, :].astype(jnp.float32), 0
        for xt in xts:
            part = s[start : start + xt.shape[1], :]
            pseudo += jnp.dot(xt[rows, :], part, preferred_element_type=jnp.float32)
            start += xt.shape[1]
        held[rows, :] = jnp.where(keep[rows, :] > 0, pseudo, 0.0).astype(jnp.bfloat16)
        copy = pltpu.make_async_copy(held.at[rows, :], out.at[rows, :], sems.at[t])
        copy.start()
        copies.append(copy)
    for copy in copies:
        copy.wait()


def residue(slopes, order, xts, fb, keep):
    depth, kw = fb.shape
    total = sum(xt.shape[1] for xt in xts)
    tile = min(depth, 512)
    return pl.pallas_call(
        functools.partial(residue_kernel, order, tile),
        out_shape=jax.ShapeDtypeStruct((depth, kw), jnp.bfloat16),
        in_specs=[VMEM] * (len(slopes) + len(xts) + 2),
        out_specs=ANY,
        scratch_shapes=[
            pltpu.VMEM((total, kw), jnp.bfloat16),
            pltpu.VMEM((depth, kw), jnp.bfloat16),
            pltpu.SemaphoreType.DMA((depth // tile,)),
        ],
        compiler_params=params(24),
        cost_estimate=cost(2 * total * depth * kw, 2 * depth * (total + 3 * kw)),
        name="residue",
    )(*slopes, *xts, fb, keep)


def outer_kernel(n, per_row, tile, *refs):
    messages, (out, wide, lines, held, sems) = refs[:n], refs[n:]
    cap = messages[0].shape[0] - 16
    for k in range(n):
        tail = messages[k][cap:, :].astype(jnp.float32)
        number = (tail[0:1, :] * LANES + tail[1:2, :]).astype(jnp.int32)
        lines[:, k * cap : (k + 1) * cap] = jnp.broadcast_to(number // per_row, (8, cap))
        column = jnp.broadcast_to((number % per_row).astype(jnp.float32), (LANES, cap)).T
        value = messages[k][:cap, :].astype(jnp.float32)
        for c in range(per_row):
            wide[k * cap : (k + 1) * cap, c * LANES : (c + 1) * LANES] = jnp.where(
                column == c, value, 0.0
            ).astype(jnp.bfloat16)
    copies = []
    for t in range(out.shape[0] // tile):
        rows = slice(t * tile, (t + 1) * tile)
        line = lax.broadcasted_iota(jnp.int32, (tile, n * cap), 0) + t * tile
        hot = (lines[0:1, :] == line).astype(jnp.float32).astype(jnp.bfloat16)
        held[rows, :] = jnp.dot(hot, wide[...], preferred_element_type=jnp.float32) / n
        copy = pltpu.make_async_copy(held.at[rows, :], out.at[rows, :], sems.at[t])
        copy.start()
        copies.append(copy)
    for copy in copies:
        copy.wait()


def outer(messages, depth, kw):
    n = len(messages)
    cap = messages[0].shape[0] - 16
    tile = min(depth, 512)
    return pl.pallas_call(
        functools.partial(outer_kernel, n, kw // LANES, tile),
        out_shape=jax.ShapeDtypeStruct((depth, kw), jnp.float32),
        out_specs=ANY,
        scratch_shapes=[
            pltpu.VMEM((n * cap, kw), jnp.bfloat16),
            pltpu.VMEM((8, n * cap), jnp.int32),
            pltpu.VMEM((depth, kw), jnp.float32),
            pltpu.SemaphoreType.DMA((depth // tile,)),
        ],
        compiler_params=params(24),
        cost_estimate=cost(2 * n * cap * depth * kw, 4 * depth * kw),
        name="outer",
    )(*messages)


def on_device(inputs, target, weights, feedback, counts, blocks):
    tokens, w, fb = inputs[0], weights[0], feedback[0]
    n_shard, n_rep = lax.axis_size("shard"), lax.axis_size("rep")
    tok_dev = tokens.shape[0]
    depth, kw = w.shape
    half = tok_dev // 2
    per_row = kw // LANES
    slot_row = blocks[0]
    slots = blocks.reshape(-1, 1)
    near = [d for d in range(1, n_shard) if d & (d - 1) == 0]
    far = [d for d in range(1, n_shard) if d & (d - 1) != 0]

    far_out = cut(tokens, depth, [(d, 0, tok_dev) for d in far], [])
    far_in = [swap(x, "shard", n_shard, d) for x, d in zip(far_out, far)]
    near_out, after = [], far_out[:1]
    for part in range(2):
        near_out.append(cut(tokens, depth, [(d, part * half, half) for d in near], after))
        if part == 0:
            fbk, keep = early(slots, slot_row, counts, fb, near_out[0][0])
            after = [fbk]
    near_in = [[swap(x, "shard", n_shard, d) for x, d in zip(out, near)] for out in near_out]
    (own,) = cut(tokens, depth, [(0, 0, tok_dev)], [near_out[1][0]])

    brief, wide = jnp.bfloat16, jnp.float32
    (mine, *products), x_far = project([own] + far_in, [wide] + [brief] * len(far), w, [])
    whole = [swap(p, "shard", n_shard, d) for p, d in zip(products, far)]
    xg_far, xt_far = prepare([x_far], slots, counts, per_row, [])
    after, halves, x_near = [xt_far, keep], [], []
    for part in range(2):
        products, x = project(near_in[part], [brief] * len(near), w, after)
        halves.append([swap(p, "shard", n_shard, d) for p, d in zip(products, near)])
        x_near.append(x)
        after = [products[0]]
    xg_near, xt_near = prepare(x_near, slots, counts, per_row, [products[0]])
    halves = [half_of[k] for k in range(len(near)) for half_of in halves]
    slopes = slope(target[0], mine, whole, halves, xt_near)
    slopes = [slopes] + [swap(slopes, "shard", n_shard, d) for d in range(1, n_shard)]

    order = [(d, 0, tok_dev) for d in [0] + far]
    order += [(d, part * half, (part + 1) * half) for part in range(2) for d in near]
    message = kept(slopes, order, [xg_far, xg_near], fbk, slots, slot_row)
    same_core = [message] + [swap(message, "rep", n_rep, d) for d in range(2, n_rep, 2)]
    messages = same_core + [swap(m, "rep", n_rep, 1) for m in same_core]
    new_feedback = residue(slopes, order, [xt_far, xt_near], fb, keep)
    return outer(messages, depth, kw), new_feedback[None]


def solution(mesh):
    placed = (
        P("rep", "shard", None),
        P("rep", "shard", None),
        P("rep", "shard", None),
        P("rep", "shard", None),
        P("rep", "shard"),
        P("rep", "shard", None),
    )
    return jax.shard_map(
        on_device,
        mesh=mesh,
        in_specs=placed,
        out_specs=(P("shard", None), P("rep", "shard", None)),
        check_vma=False,
    )
```

time: 81.9 us -> 60.7 us (0.74)
  waiting for transfers between devices: 24.7 us -> 16.1 us
  starting transfers between devices: 34.1 us -> 27.2 us
  local copies, waits for them, and re-layouts: 6.87 us -> 3.32 us
  Pallas kernels: 14.1 us -> 11.9 us
    ppermute x25 -> x20, waiting for transfers between devices: 24.7 us -> 16.1 us  [swap(): return lax.ppermute(x, axis, [(i, i ^ d) for i in range(n)])]
    ppermute x25 -> x20, starting transfers between devices: 34.1 us -> 27.2 us  [swap(): return lax.ppermute(x, axis, [(i, i ^ d) for i in range(n)])]
    dynamic_slice x1 -> x0, local copies, waits for them, and re-layouts: 2.66 us -> none  [on_device(): lax.dynamic_slice(tokens, (start, (me ^ d) * depth), (rows, depth))]
    pallas_call x7 -> x10, Pallas kernels: 9.89 us -> 8.28 us  [the longest x1 3.52 us: outer(): pl.pallas_call(functools.partial(outer_kernel, n, kw // LANES, tile), out...]
    unnamed x20 -> x14, local copies, waits for them, and re-layouts: 4.1 us -> 3.2 us
    pallas_call x2 -> x3, Pallas kernels: 3.19 us -> 2.54 us  [project(): pl.pallas_call(functools.partial(project_kernel, n), out_shape=[jax.Shape...]
  transfers between devices with their start and end apart: 25 -> 20, of which waited for: 14 -> 7; matrix products, arithmetic and copies ran while one was open for 0% -> 0% of each run, Pallas kernels for 9% -> 13%
where the time goes in v3:
time: 60.7 us; the launch traced here: 60 us
  starting transfers between devices  27.2 us (45%)
  waiting for transfers between devices  16.1 us (27%)
  Pallas kernels  11.9 us (20%)
  local copies, waits for them, and re-layouts  3.32 us (5%)
  between operations  1.51 us (2%)
    ppermute x20, starting transfers between devices, swap(): return lax.ppermute(x, axis, [(i, i ^ d) for i in range(n)])  27.2 us
    ppermute x20, waiting for transfers between devices, swap(): return lax.ppermute(x, axis, [(i, i ^ d) for i in range(n)])  16.1 us
    pallas_call x1, Pallas kernels, outer(): pl.pallas_call(functools.partial(outer_kernel, n, kw // LANES, tile), out...  3.52 us
    unnamed x14, local copies, waits for them, and re-layouts  3.2 us
    pallas_call x3, Pallas kernels, project(): pl.pallas_call(functools.partial(project_kernel, n), out_shape=[jax.Shape...  2.54 us
    pallas_call x1, Pallas kernels, residue(): pl.pallas_call(functools.partial(residue_kernel, order, tile), out_shape=...  2.34 us
  transfers between devices with their start and end apart: 20, of which 7 were waited for; matrix products, arithmetic and copies ran while one was open for 0% of the time, Pallas kernels for 13%

profile of v3, /device:TPU:1, one launch (start us, length us, event | category | flops | bytes accessed | tf_op | source)
XLA Modules:
  0.0 60.0 jit_solution(16391978191126277394)
XLA Ops:
  0.6 1.6 %copy-done = bf16[1,128,8192]{2,1,0:T(8,128)(2,1)S(1)} copy-done((bf16[1,128,8192]{2,1,0:T(8,128)(2,1)S(1)}, bf16[1,128,8192]{2,1,0:T(8,128)(2,1)}, u32[]{:S(2)}) %copy-start) | copy-done | bytes 2097176
  2.3 3.1 %collective-permute-start = (bf16[128,2048]{1,0:T(8,128)(2,1)S(1)}, bf16[128,2048]{1,0:T(8,128)(2,1)S(1)}, u32[]{:S(2)}, u32[]{:S(2)}) collective-permute-start(bf16[128,2048]{1,0:T(8,128)(2,1)S(1)} %cut.4.refs_0_), channel_id=1, source_target_pairs={{0,3},{1,2},{2,1},{3,0},{4,7},{5,6},{6,5},{7,4},{8,11},{9,10},{10,... | collective-permute-start | bytes 1572872 | tf_op jit(solution)/shard_map/ppermute | solution.py:26
  5.4 0.8 %cut.5 = (bf16[64,2048]{1,0:T(8,128)(2,1)}, bf16[64,2048]{1,0:T(8,128)(2,1)}) custom-call(bf16[128,8192]{1,0:T(8,128)(2,1)S(1)} %bitcast.8, bf16[128,2048]{1,0:T(8,128)(2,1)S(1)} %cut.4.refs_0_), custom_call_target="tpu_custom_call" | custom-call | bytes 1048576 | tf_op jit(solution)/shard_map/cut/pallas_call | solution.py:44
  7.4 1.6 %copy-done.3 = bf16[1,2048,512]{2,1,0:T(8,128)(2,1)S(1)} copy-done((bf16[1,2048,512]{2,1,0:T(8,128)(2,1)S(1)}, bf16[1,2048,512]{2,1,0:T(8,128)(2,1)}, u32[]{:S(2)}) %copy-start.3) | copy-done | bytes 2097176
  9.0 1.0 %early.1 = (f32[128,128]{1,0:T(8,128)S(1)}, bf16[2048,512]{1,0:T(8,128)(2,1)S(1)}) custom-call(s32[128,1]{1,0:T(8,128)S(1)} %copy.8.slots.refs_1_.refs_2_.refs_7_, s32[1,128]{1,0:T(1,128)S(1)} %bitcast.18, s32[1,1]{1,0:T(1,128)S(6)} %copy.12.count.refs_2_.refs_3_, bf16[2048,512]{1,0:T(8,128)(2,1)S(1)} %bitcast.14, bf16[64,2048]{1,0:T(8,128)(2,1)} %get-tuple-element.21.after), custom_call_target="tpu_custom_call" | custom-call | flops 536870912 | bytes 4194304 | tf_op jit(solution)/shard_map/early/pallas_call | solution.py:140
  10.1 1.5 %collective-permute-start.6 = (bf16[64,2048]{1,0:T(8,128)(2,1)S(1)}, bf16[64,2048]{1,0:T(8,128)(2,1)S(1)}, u32[]{:S(2)}, u32[]{:S(2)}) collective-permute-start(bf16[64,2048]{1,0:T(8,128)(2,1)S(1)} %get-tuple-element.31), channel_id=1, source_target_pairs={{0,2},{1,3},{2,0},{3,1},{4,6},{5,7},{6,4},{7,5},{8,10},{9,11},{10,... | collective-permute-start | bytes 786440 | tf_op jit(solution)/shard_map/ppermute | solution.py:26
  11.6 1.2 %collective-permute-start.5 = (bf16[64,2048]{1,0:T(8,128)(2,1)S(1)}, bf16[64,2048]{1,0:T(8,128)(2,1)S(1)}, u32[]{:S(2)}, u32[]{:S(2)}) collective-permute-start(bf16[64,2048]{1,0:T(8,128)(2,1)S(1)} %get-tuple-element.23.refs_0_), channel_id=1, source_target_pairs={{0,1},{1,0},{2,3},{3,2},{4,5},{5,4},{6,7},{7,6},{8,9},{9,8},{10,11... | collective-permute-start | bytes 786440 | tf_op jit(solution)/shard_map/ppermute | solution.py:26
  12.8 4.2 %collective-permute-done.refs_1_ = bf16[128,2048]{1,0:T(8,128)(2,1)S(1)} collective-permute-done((bf16[128,2048]{1,0:T(8,128)(2,1)S(1)}, bf16[128,2048]{1,0:T(8,128)(2,1)S(1)}, u32[]{:S(2)}, u32[]{:S(2)}) %collective-permute-start) | collective-permute-done | bytes 524320 | tf_op jit(solution)/shard_map/ppermute | solution.py:26
  17.0 0.7 %project.3 = (f32[128,512]{1,0:T(8,128)S(1)}, bf16[128,512]{1,0:T(8,128)(2,1)S(1)}, bf16[256,2048]{1,0:T(8,128)(2,1)S(1)}) custom-call(bf16[128,2048]{1,0:T(8,128)(2,1)S(1)} %cut.7.refs_0_, bf16[128,2048]{1,0:T(8,128)(2,1)S(1)} %collective-permute-done.refs_1_, bf16[2048,512]{1,0:T(8,128)(2,1)S(1)} %bitcast.11), custom_call_target="tpu_custom_call" | custom-call | flops 536870912 | bytes 3145728 | tf_op jit(solution)/shard_map/project/pallas_call | solution.py:72
  17.8 2.1 %collective-permute-start.1 = (bf16[128,512]{1,0:T(8,128)(2,1)S(1)}, bf16[128,512]{1,0:T(8,128)(2,1)S(1)}, u32[]{:S(2)}, u32[]{:S(2)}) collective-permute-start(bf16[128,512]{1,0:T(8,128)(2,1)S(1)} %get-tuple-element.25), channel_id=1, source_target_pairs={{0,3},{1,2},{2,1},{3,0},{4,7},{5,6},{6,5},{7,4},{8,11},{9,10},{10,... | collective-permute-start | bytes 393224 | tf_op jit(solution)/shard_map/ppermute | solution.py:26
  19.9 0.5 prepare.2
  20.4 3.0 %collective-permute-done.3.refs_1_ = bf16[64,2048]{1,0:T(8,128)(2,1)S(1)} collective-permute-done((bf16[64,2048]{1,0:T(8,128)(2,1)}, bf16[64,2048]{1,0:T(8,128)(2,1)S(1)}, u32[]{:S(2)}, u32[]{:S(2)}) %collective-permute-start.3) | collective-permute-done | bytes 262176 | tf_op jit(solution)/shard_map/ppermute | solution.py:26
  23.5 1.4 %project.4 = (bf16[64,512]{1,0:T(8,128)(2,1)S(1)}, bf16[64,512]{1,0:T(8,128)(2,1)S(1)}, bf16[128,2048]{1,0:T(8,128)(2,1)S(1)}) custom-call(bf16[64,2048]{1,0:T(8,128)(2,1)} %collective-permute-done.2.refs_0_, bf16[64,2048]{1,0:T(8,128)(2,1)S(1)} %collective-permute-done.3.refs_1_, bf16[2048,512]{1,0:T(8,128)(2,1)S(1)} %bitcast.12, ...), custom_call_target="tpu_custom_call" | custom-call | flops 268435456 | bytes 2621440 | tf_op jit(solution)/shard_map/project/pallas_call | solution.py:72
  24.9 1.4 %collective-permute-start.8 = (bf16[64,512]{1,0:T(8,128)(2,1)S(1)}, bf16[64,512]{1,0:T(8,128)(2,1)S(1)}, u32[]{:S(2)}, u32[]{:S(2)}) collective-permute-start(bf16[64,512]{1,0:T(8,128)(2,1)S(1)} %get-tuple-element.33), channel_id=1, source_target_pairs={{0,2},{1,3},{2,0},{3,1},{4,6},{5,7},{6,4},{7,5},{8,10},{9,11},{10,... | collective-permute-start | bytes 196616 | tf_op jit(solution)/shard_map/ppermute | solution.py:26
  26.3 1.3 %collective-permute-start.4 = (bf16[64,512]{1,0:T(8,128)(2,1)S(1)}, bf16[64,512]{1,0:T(8,128)(2,1)S(1)}, u32[]{:S(2)}, u32[]{:S(2)}) collective-permute-start(bf16[64,512]{1,0:T(8,128)(2,1)S(1)} %get-tuple-element.30.refs_3_), channel_id=1, source_target_pairs={{0,1},{1,0},{2,3},{3,2},{4,5},{5,4},{6,7},{7,6},{8,9},{9,8},{10,11... | collective-permute-start | bytes 196616 | tf_op jit(solution)/shard_map/ppermute | solution.py:26
  27.6 2.1 %collective-permute-done.6.refs_1_ = bf16[64,2048]{1,0:T(8,128)(2,1)S(1)} collective-permute-done((bf16[64,2048]{1,0:T(8,128)(2,1)S(1)}, bf16[64,2048]{1,0:T(8,128)(2,1)S(1)}, u32[]{:S(2)}, u32[]{:S(2)}) %collective-permute-start.6) | collective-permute-done | bytes 262176 | tf_op jit(solution)/shard_map/ppermute | solution.py:26
  29.7 0.4 project.5
  30.1 1.8 %collective-permute-start.9 = (bf16[64,512]{1,0:T(8,128)(2,1)S(1)}, bf16[64,512]{1,0:T(8,128)(2,1)S(1)}, u32[]{:S(2)}, u32[]{:S(2)}) collective-permute-start(bf16[64,512]{1,0:T(8,128)(2,1)S(1)} %get-tuple-element.34), channel_id=1, source_target_pairs={{0,2},{1,3},{2,0},{3,1},{4,6},{5,7},{6,4},{7,5},{8,10},{9,11},{10,... | collective-permute-start | bytes 196616 | tf_op jit(solution)/shard_map/ppermute | solution.py:26
  31.9 1.2 %collective-permute-start.7 = (bf16[64,512]{1,0:T(8,128)(2,1)S(1)}, bf16[64,512]{1,0:T(8,128)(2,1)S(1)}, u32[]{:S(2)}, u32[]{:S(2)}) collective-permute-start(bf16[64,512]{1,0:T(8,128)(2,1)S(1)} %get-tuple-element.32.refs_4_), channel_id=1, source_target_pairs={{0,1},{1,0},{2,3},{3,2},{4,5},{5,4},{6,7},{7,6},{8,9},{9,8},{10,11... | collective-permute-start | bytes 196616 | tf_op jit(solution)/shard_map/ppermute | solution.py:26
  33.2 0.5 prepare.3
  33.7 1.6 %collective-permute-done.7.refs_4_ = bf16[64,512]{1,0:T(8,128)(2,1)S(1)} collective-permute-done((bf16[64,512]{1,0:T(8,128)(2,1)S(1)}, bf16[64,512]{1,0:T(8,128)(2,1)S(1)}, u32[]{:S(2)}, u32[]{:S(2)}) %collective-permute-start.7) | collective-permute-done | bytes 65568 | tf_op jit(solution)/shard_map/ppermute | solution.py:26
  35.4 1.0 %collective-permute-start.12 = (bf16[128,512]{1,0:T(8,128)(2,1)S(1)}, bf16[128,512]{1,0:T(8,128)(2,1)S(1)}, u32[]{:S(2)}, u32[]{:S(2)}) collective-permute-start(bf16[128,512]{1,0:T(8,128)(2,1)S(1)} %slope.1.refs_0_), channel_id=1, source_target_pairs={{0,3},{1,2},{2,1},{3,0},{4,7},{5,6},{6,5},{7,4},{8,11},{9,10},{10,... | collective-permute-start | bytes 393224 | tf_op jit(solution)/shard_map/ppermute | solution.py:26
  36.4 1.5 %collective-permute-start.11 = (bf16[128,512]{1,0:T(8,128)(2,1)S(1)}, bf16[128,512]{1,0:T(8,128)(2,1)S(1)}, u32[]{:S(2)}, u32[]{:S(2)}) collective-permute-start(bf16[128,512]{1,0:T(8,128)(2,1)S(1)} %slope.1.refs_0_), channel_id=1, source_target_pairs={{0,2},{1,3},{2,0},{3,1},{4,6},{5,7},{6,4},{7,5},{8,10},{9,11},{10,... | collective-permute-start | bytes 393224 | tf_op jit(solution)/shard_map/ppermute | solution.py:26
  38.1 2.2 %collective-permute-done.12.refs_3_ = bf16[128,512]{1,0:T(8,128)(2,1)S(1)} collective-permute-done((bf16[128,512]{1,0:T(8,128)(2,1)S(1)}, bf16[128,512]{1,0:T(8,128)(2,1)S(1)}, u32[]{:S(2)}, u32[]{:S(2)}) %collective-permute-start.12) | collective-permute-done | bytes 131104 | tf_op jit(solution)/shard_map/ppermute | solution.py:26
  40.3 2.0 %collective-permute-done.11.refs_2_ = bf16[128,512]{1,0:T(8,128)(2,1)S(1)} collective-permute-done((bf16[128,512]{1,0:T(8,128)(2,1)S(1)}, bf16[128,512]{1,0:T(8,128)(2,1)S(1)}, u32[]{:S(2)}, u32[]{:S(2)}) %collective-permute-start.11) | collective-permute-done | bytes 131104 | tf_op jit(solution)/shard_map/ppermute | solution.py:26
  42.3 1.0 %collective-permute-done.10.refs_1_ = bf16[128,512]{1,0:T(8,128)(2,1)S(1)} collective-permute-done((bf16[128,512]{1,0:T(8,128)(2,1)S(1)}, bf16[128,512]{1,0:T(8,128)(2,1)S(1)}, u32[]{:S(2)}, u32[]{:S(2)}) %collective-permute-start.10) | collective-permute-done | bytes 131104 | tf_op jit(solution)/shard_map/ppermute | solution.py:26
  43.6 3.4 %collective-permute-start.15 = (bf16[144,128]{1,0:T(8,128)(2,1)S(1)}, bf16[144,128]{1,0:T(8,128)(2,1)S(1)}, u32[]{:S(2)}, u32[]{:S(2)}) collective-permute-start(bf16[144,128]{1,0:T(8,128)(2,1)S(1)} %kept.1.refs_0_), channel_id=1, source_target_pairs={{0,24},{4,28},{8,16},{12,20},{16,8},{20,12},{24,0},{28,4},{1,25},{... | collective-permute-start | bytes 110600 | tf_op jit(solution)/shard_map/ppermute | solution.py:26
  47.3 2.7 %collective-permute-start.16 = (bf16[144,128]{1,0:T(8,128)(2,1)S(1)}, bf16[144,128]{1,0:T(8,128)(2,1)S(1)}, u32[]{:S(2)}, u32[]{:S(2)}) collective-permute-start(bf16[144,128]{1,0:T(8,128)(2,1)S(1)} %kept.1.refs_0_), channel_id=1, source_target_pairs={{0,4},{4,0},{8,12},{12,8},{16,20},{20,16},{24,28},{28,24},{1,5},{5... | collective-permute-start | bytes 110600 | tf_op jit(solution)/shard_map/ppermute | solution.py:26
  50.0 1.5 %collective-permute-start.19 = (bf16[144,128]{1,0:T(8,128)(2,1)S(1)}, bf16[144,128]{1,0:T(8,128)(2,1)S(1)}, u32[]{:S(2)}, u32[]{:S(2)}) collective-permute-start(bf16[144,128]{1,0:T(8,128)(2,1)S(1)} %collective-permute-done.15.refs_3_), channel_id=1, source_target_pairs={{0,4},{4,0},{8,12},{12,8},{16,20},{20,16},{24,28},{28,24},{1,5},{5... | collective-permute-start | bytes 110600 | tf_op jit(solution)/shard_map/ppermute | solution.py:26
  51.5 2.6 %collective-permute-start.18 = (bf16[144,128]{1,0:T(8,128)(2,1)S(1)}, bf16[144,128]{1,0:T(8,128)(2,1)S(1)}, u32[]{:S(2)}, u32[]{:S(2)}) collective-permute-start(bf16[144,128]{1,0:T(8,128)(2,1)S(1)} %collective-permute-done.14.refs_2_), channel_id=1, source_target_pairs={{0,4},{4,0},{8,12},{12,8},{16,20},{20,16},{24,28},{28,24},{1,5},{5... | collective-permute-start | bytes 110600 | tf_op jit(solution)/shard_map/ppermute | solution.py:26
  54.1 2.3 %residue.1 = bf16[2048,512]{1,0:T(8,128)(2,1)} custom-call(bf16[128,512]{1,0:T(8,128)(2,1)S(1)} %slope.1.refs_0_, bf16[128,512]{1,0:T(8,128)(2,1)S(1)} %collective-permute-done.10.refs_1_, bf16[128,512]{1,0:T(8,128)(2,1)S(1)} %collective-permute-done.11.refs_2_, bf16[128,512]{1,0:T(8,128)(2,1)S(1)} %collective-permute-done.12.refs_3_, ...), custom_call_target="tpu_custom_call" | custom-call | flops 1073741824 | bytes 8388608 | tf_op jit(solution)/shard_map/residue/pallas_call | solution.py:252
  56.5 3.5 %outer.1 = f32[2048,512]{1,0:T(8,128)} custom-call(bf16[144,128]{1,0:T(8,128)(2,1)S(1)} %kept.1.refs_0_, bf16[144,128]{1,0:T(8,128)(2,1)S(1)} %collective-permute-done.13.refs_1_, bf16[144,128]{1,0:T(8,128)(2,1)S(1)} %collective-permute-done.14.refs_2_, bf16[144,128]{1,0:T(8,128)(2,1)S(1)} %collective-permute-done.15.refs_3_, ...), custom_call_target="tpu_custom_call" | custom-call | flops 2147483648 | bytes 4194304 | tf_op jit(solution)/shard_map/outer/pallas_call | solution.py:298
  (37 shorter events, 1.7 us)
Async XLA Ops:
  0.6 1.6 %copy-start = (bf16[1,128,8192]{2,1,0:T(8,128)(2,1)S(1)}, bf16[1,128,8192]{2,1,0:T(8,128)(2,1)}, u32[]{:S(2)}) copy-start(bf16[1,128,8192]{2,1,0:T(8,128)(2,1)} %param.6) | copy-start | bytes 6291460
  2.2 5.0 %copy-start.6 = (s32[1,1,128]{2,1,0:T(1,128)S(1)}, s32[1,1,128]{2,1,0:T(1,128)}, u32[]{:S(2)}) copy-start(s32[1,1,128]{2,1,0:T(1,128)} %param.11) | copy-start | bytes 1540
  2.3 7.7 %copy-start.1 = (bf16[1,128,8192]{2,1,0:T(8,128)(2,1)S(1)}, bf16[1,128,8192]{2,1,0:T(8,128)(2,1)}, u32[]{:S(2)}) copy-start(bf16[1,128,8192]{2,1,0:T(8,128)(2,1)} %param.6) | copy-start | bytes 6291460
  2.3 14.8 %collective-permute-start = (bf16[128,2048]{1,0:T(8,128)(2,1)S(1)}, bf16[128,2048]{1,0:T(8,128)(2,1)S(1)}, u32[]{:S(2)}, u32[]{:S(2)}) collective-permute-start(bf16[128,2048]{1,0:T(8,128)(2,1)S(1)} %cut.4.refs_0_), channel_id=1, source_target_pairs={{0,3},{1,2},{2,1},{3,0},{4,7},{5,6},{6,5},{7,4},{8,11},{9,10},{10,... | collective-permute-start | bytes 1572872 | tf_op jit(solution)/shard_map/ppermute | solution.py:26
  6.2 17.3 %collective-permute-start.3 = (bf16[64,2048]{1,0:T(8,128)(2,1)}, bf16[64,2048]{1,0:T(8,128)(2,1)S(1)}, u32[]{:S(2)}, u32[]{:S(2)}) collective-permute-start(bf16[64,2048]{1,0:T(8,128)(2,1)} %get-tuple-element.26), channel_id=1, source_target_pairs={{0,2},{1,3},{2,0},{3,1},{4,6},{5,7},{6,4},{7,5},{8,10},{9,11},{10,... | collective-permute-start | bytes 786440 | tf_op jit(solution)/shard_map/ppermute | solution.py:26
  6.5 17.0 %collective-permute-start.2 = (bf16[64,2048]{1,0:T(8,128)(2,1)}, bf16[64,2048]{1,0:T(8,128)(2,1)}, u32[]{:S(2)}, u32[]{:S(2)}) collective-permute-start(bf16[64,2048]{1,0:T(8,128)(2,1)} %get-tuple-element.21.after), channel_id=1, source_target_pairs={{0,1},{1,0},{2,3},{3,2},{4,5},{5,4},{6,7},{7,6},{8,9},{9,8},{10,11... | collective-permute-start | bytes 786440 | tf_op jit(solution)/shard_map/ppermute | solution.py:26
  7.4 1.6 %copy-start.3 = (bf16[1,2048,512]{2,1,0:T(8,128)(2,1)S(1)}, bf16[1,2048,512]{2,1,0:T(8,128)(2,1)}, u32[]{:S(2)}) copy-start(bf16[1,2048,512]{2,1,0:T(8,128)(2,1)} %param.9) | copy-start | bytes 6291460
  10.0 7.0 %copy-start.2 = (bf16[1,2048,512]{2,1,0:T(8,128)(2,1)S(1)}, bf16[1,2048,512]{2,1,0:T(8,128)(2,1)}, u32[]{:S(2)}) copy-start(bf16[1,2048,512]{2,1,0:T(8,128)(2,1)} %param.8) | copy-start | bytes 6291460
  10.1 19.5 %collective-permute-start.6 = (bf16[64,2048]{1,0:T(8,128)(2,1)S(1)}, bf16[64,2048]{1,0:T(8,128)(2,1)S(1)}, u32[]{:S(2)}, u32[]{:S(2)}) collective-permute-start(bf16[64,2048]{1,0:T(8,128)(2,1)S(1)} %get-tuple-element.31), channel_id=1, source_target_pairs={{0,2},{1,3},{2,0},{3,1},{4,6},{5,7},{6,4},{7,5},{8,10},{9,11},{10,... | collective-permute-start | bytes 786440 | tf_op jit(solution)/shard_map/ppermute | solution.py:26
  11.6 18.1 %collective-permute-start.5 = (bf16[64,2048]{1,0:T(8,128)(2,1)S(1)}, bf16[64,2048]{1,0:T(8,128)(2,1)S(1)}, u32[]{:S(2)}, u32[]{:S(2)}) collective-permute-start(bf16[64,2048]{1,0:T(8,128)(2,1)S(1)} %get-tuple-element.23.refs_0_), channel_id=1, source_target_pairs={{0,1},{1,0},{2,3},{3,2},{4,5},{5,4},{6,7},{7,6},{8,9},{9,8},{10,11... | collective-permute-start | bytes 786440 | tf_op jit(solution)/shard_map/ppermute | solution.py:26
  17.8 17.6 %collective-permute-start.1 = (bf16[128,512]{1,0:T(8,128)(2,1)S(1)}, bf16[128,512]{1,0:T(8,128)(2,1)S(1)}, u32[]{:S(2)}, u32[]{:S(2)}) collective-permute-start(bf16[128,512]{1,0:T(8,128)(2,1)S(1)} %get-tuple-element.25), channel_id=1, source_target_pairs={{0,3},{1,2},{2,1},{3,0},{4,7},{5,6},{6,5},{7,4},{8,11},{9,10},{10,... | collective-permute-start | bytes 393224 | tf_op jit(solution)/shard_map/ppermute | solution.py:26
  24.9 10.4 %copy-start.5 = (bf16[1,128,512]{2,1,0:T(8,128)(2,1)S(1)}, bf16[1,128,512]{2,1,0:T(8,128)(2,1)}, u32[]{:S(2)}) copy-start(bf16[1,128,512]{2,1,0:T(8,128)(2,1)} %param.7) | copy-start | bytes 393220
  24.9 8.8 %collective-permute-start.8 = (bf16[64,512]{1,0:T(8,128)(2,1)S(1)}, bf16[64,512]{1,0:T(8,128)(2,1)S(1)}, u32[]{:S(2)}, u32[]{:S(2)}) collective-permute-start(bf16[64,512]{1,0:T(8,128)(2,1)S(1)} %get-tuple-element.33), channel_id=1, source_target_pairs={{0,2},{1,3},{2,0},{3,1},{4,6},{5,7},{6,4},{7,5},{8,10},{9,11},{10,... | collective-permute-start | bytes 196616 | tf_op jit(solution)/shard_map/ppermute | solution.py:26
  26.3 7.4 %collective-permute-start.4 = (bf16[64,512]{1,0:T(8,128)(2,1)S(1)}, bf16[64,512]{1,0:T(8,128)(2,1)S(1)}, u32[]{:S(2)}, u32[]{:S(2)}) collective-permute-start(bf16[64,512]{1,0:T(8,128)(2,1)S(1)} %get-tuple-element.30.refs_3_), channel_id=1, source_target_pairs={{0,1},{1,0},{2,3},{3,2},{4,5},{5,4},{6,7},{7,6},{8,9},{9,8},{10,11... | collective-permute-start | bytes 196616 | tf_op jit(solution)/shard_map/ppermute | solution.py:26
  30.1 24.0 %copy-start.4 = (bf16[1,2048,512]{2,1,0:T(8,128)(2,1)S(1)}, bf16[1,2048,512]{2,1,0:T(8,128)(2,1)}, u32[]{:S(2)}) copy-start(bf16[1,2048,512]{2,1,0:T(8,128)(2,1)} %param.9) | copy-start | bytes 6291460
  30.1 3.6 %collective-permute-start.9 = (bf16[64,512]{1,0:T(8,128)(2,1)S(1)}, bf16[64,512]{1,0:T(8,128)(2,1)S(1)}, u32[]{:S(2)}, u32[]{:S(2)}) collective-permute-start(bf16[64,512]{1,0:T(8,128)(2,1)S(1)} %get-tuple-element.34), channel_id=1, source_target_pairs={{0,2},{1,3},{2,0},{3,1},{4,6},{5,7},{6,4},{7,5},{8,10},{9,11},{10,... | collective-permute-start | bytes 196616 | tf_op jit(solution)/shard_map/ppermute | solution.py:26
  31.9 3.4 %collective-permute-start.7 = (bf16[64,512]{1,0:T(8,128)(2,1)S(1)}, bf16[64,512]{1,0:T(8,128)(2,1)S(1)}, u32[]{:S(2)}, u32[]{:S(2)}) collective-permute-start(bf16[64,512]{1,0:T(8,128)(2,1)S(1)} %get-tuple-element.32.refs_4_), channel_id=1, source_target_pairs={{0,1},{1,0},{2,3},{3,2},{4,5},{5,4},{6,7},{7,6},{8,9},{9,8},{10,11... | collective-permute-start | bytes 196616 | tf_op jit(solution)/shard_map/ppermute | solution.py:26
  35.4 4.9 %collective-permute-start.12 = (bf16[128,512]{1,0:T(8,128)(2,1)S(1)}, bf16[128,512]{1,0:T(8,128)(2,1)S(1)}, u32[]{:S(2)}, u32[]{:S(2)}) collective-permute-start(bf16[128,512]{1,0:T(8,128)(2,1)S(1)} %slope.1.refs_0_), channel_id=1, source_target_pairs={{0,3},{1,2},{2,1},{3,0},{4,7},{5,6},{6,5},{7,4},{8,11},{9,10},{10,... | collective-permute-start | bytes 393224 | tf_op jit(solution)/shard_map/ppermute | solution.py:26
  36.4 5.9 %collective-permute-start.11 = (bf16[128,512]{1,0:T(8,128)(2,1)S(1)}, bf16[128,512]{1,0:T(8,128)(2,1)S(1)}, u32[]{:S(2)}, u32[]{:S(2)}) collective-permute-start(bf16[128,512]{1,0:T(8,128)(2,1)S(1)} %slope.1.refs_0_), channel_id=1, source_target_pairs={{0,2},{1,3},{2,0},{3,1},{4,6},{5,7},{6,4},{7,5},{8,10},{9,11},{10,... | collective-permute-start | bytes 393224 | tf_op jit(solution)/shard_map/ppermute | solution.py:26
  37.9 5.4 %collective-permute-start.10 = (bf16[128,512]{1,0:T(8,128)(2,1)S(1)}, bf16[128,512]{1,0:T(8,128)(2,1)S(1)}, u32[]{:S(2)}, u32[]{:S(2)}) collective-permute-start(bf16[128,512]{1,0:T(8,128)(2,1)S(1)} %slope.1.refs_0_), channel_id=1, source_target_pairs={{0,1},{1,0},{2,3},{3,2},{4,5},{5,4},{6,7},{7,6},{8,9},{9,8},{10,11... | collective-permute-start | bytes 393224 | tf_op jit(solution)/shard_map/ppermute | solution.py:26
  43.6 6.5 %collective-permute-start.15 = (bf16[144,128]{1,0:T(8,128)(2,1)S(1)}, bf16[144,128]{1,0:T(8,128)(2,1)S(1)}, u32[]{:S(2)}, u32[]{:S(2)}) collective-permute-start(bf16[144,128]{1,0:T(8,128)(2,1)S(1)} %kept.1.refs_0_), channel_id=1, source_target_pairs={{0,24},{4,28},{8,16},{12,20},{16,8},{20,12},{24,0},{28,4},{1,25},{... | collective-permute-start | bytes 110600 | tf_op jit(solution)/shard_map/ppermute | solution.py:26
  46.9 4.5 %collective-permute-start.14 = (bf16[144,128]{1,0:T(8,128)(2,1)S(1)}, bf16[144,128]{1,0:T(8,128)(2,1)S(1)}, u32[]{:S(2)}, u32[]{:S(2)}) collective-permute-start(bf16[144,128]{1,0:T(8,128)(2,1)S(1)} %kept.1.refs_0_), channel_id=1, source_target_pairs={{0,16},{4,20},{8,24},{12,28},{16,0},{20,4},{24,8},{28,12},{1,17},{... | collective-permute-start | bytes 110600 | tf_op jit(solution)/shard_map/ppermute | solution.py:26
  46.9 7.1 %collective-permute-start.13 = (bf16[144,128]{1,0:T(8,128)(2,1)S(1)}, bf16[144,128]{1,0:T(8,128)(2,1)S(1)}, u32[]{:S(2)}, u32[]{:S(2)}) collective-permute-start(bf16[144,128]{1,0:T(8,128)(2,1)S(1)} %kept.1.refs_0_), channel_id=1, source_target_pairs={{0,8},{4,12},{8,0},{12,4},{16,24},{20,28},{24,16},{28,20},{1,9},{5... | collective-permute-start | bytes 110600 | tf_op jit(solution)/shard_map/ppermute | solution.py:26
  47.3 9.1 %collective-permute-start.16 = (bf16[144,128]{1,0:T(8,128)(2,1)S(1)}, bf16[144,128]{1,0:T(8,128)(2,1)S(1)}, u32[]{:S(2)}, u32[]{:S(2)}) collective-permute-start(bf16[144,128]{1,0:T(8,128)(2,1)S(1)} %kept.1.refs_0_), channel_id=1, source_target_pairs={{0,4},{4,0},{8,12},{12,8},{16,20},{20,16},{24,28},{28,24},{1,5},{5... | collective-permute-start | bytes 110600 | tf_op jit(solution)/shard_map/ppermute | solution.py:26
  50.0 6.5 %collective-permute-start.19 = (bf16[144,128]{1,0:T(8,128)(2,1)S(1)}, bf16[144,128]{1,0:T(8,128)(2,1)S(1)}, u32[]{:S(2)}, u32[]{:S(2)}) collective-permute-start(bf16[144,128]{1,0:T(8,128)(2,1)S(1)} %collective-permute-done.15.refs_3_), channel_id=1, source_target_pairs={{0,4},{4,0},{8,12},{12,8},{16,20},{20,16},{24,28},{28,24},{1,5},{5... | collective-permute-start | bytes 110600 | tf_op jit(solution)/shard_map/ppermute | solution.py:26
  51.5 5.0 %collective-permute-start.18 = (bf16[144,128]{1,0:T(8,128)(2,1)S(1)}, bf16[144,128]{1,0:T(8,128)(2,1)S(1)}, u32[]{:S(2)}, u32[]{:S(2)}) collective-permute-start(bf16[144,128]{1,0:T(8,128)(2,1)S(1)} %collective-permute-done.14.refs_2_), channel_id=1, source_target_pairs={{0,4},{4,0},{8,12},{12,8},{16,20},{20,16},{24,28},{28,24},{1,5},{5... | collective-permute-start | bytes 110600 | tf_op jit(solution)/shard_map/ppermute | solution.py:26
  54.1 2.4 %collective-permute-start.17 = (bf16[144,128]{1,0:T(8,128)(2,1)S(1)}, bf16[144,128]{1,0:T(8,128)(2,1)S(1)}, u32[]{:S(2)}, u32[]{:S(2)}) collective-permute-start(bf16[144,128]{1,0:T(8,128)(2,1)S(1)} %collective-permute-done.13.refs_1_), channel_id=1, source_target_pairs={{0,4},{4,0},{8,12},{12,8},{16,20},{20,16},{24,28},{28,24},{1,5},{5... | collective-permute-start | bytes 110600 | tf_op jit(solution)/shard_map/ppermute | solution.py:26

commit v4 on v3

--- a/solution.py
+++ b/solution.py
@@ -10,6 +10,7 @@
 LANES = 128
 ANY = pl.BlockSpec(memory_space=pl.ANY)
 VMEM = pl.BlockSpec(memory_space=pltpu.VMEM)
+HBM = pl.BlockSpec(memory_space=pltpu.HBM)
 SMEM = pl.BlockSpec(memory_space=pltpu.SMEM)
 MIB = 1024 * 1024
 
@@ -44,7 +45,7 @@
     return pl.pallas_call(
         functools.partial(cut_kernel, cuts),
         out_shape=[jax.ShapeDtypeStruct((rows, depth), tokens.dtype) for _, _, rows in cuts],
-        in_specs=[ANY] * (1 + len(after)),
+        in_specs=[HBM] + [ANY] * len(after),
         scratch_shapes=[pltpu.SemaphoreType.DMA((len(cuts),))],
         compiler_params=params(16),
         cost_estimate=cost(0, 4 * depth * sum(rows for _, _, rows in cuts)),
@@ -81,31 +82,29 @@
     return result[:n], result[n]
 
 
-def slope_kernel(tok_dev, n, *refs):
+def slope_kernel(tok_dev, n, spans, *refs):
     goal, mine, out = refs[0], refs[1], refs[-1]
     whole = refs[2 : 2 + n]
-    halves = refs[2 + n : -2]
-    half = out.shape[0] // 2
-    for part in range(2):
-        rows = slice(part * half, (part + 1) * half)
-        key_proj = mine[rows, :]
+    shares = refs[2 + n : -2]
+    for part, (low, high) in enumerate(spans):
+        key_proj = mine[low:high, :]
         for product in whole:
-            key_proj += product[rows, :].astype(jnp.float32)
-        for product in halves[part::2]:
+            key_proj += product[low:high, :].astype(jnp.float32)
+        for product in shares[part :: len(spans)]:
             key_proj += product[...].astype(jnp.float32)
-        gap = key_proj - goal[rows, :].astype(jnp.float32)
-        out[rows, :] = (gap / tok_dev).astype(jnp.bfloat16)
-
-
-def slope(goal, mine, whole, halves, after):
-    return pl.pallas_call(
-        functools.partial(slope_kernel, goal.shape[0], len(whole)),
+        gap = key_proj - goal[low:high, :].astype(jnp.float32)
+        out[low:high, :] = (gap / tok_dev).astype(jnp.bfloat16)
+
+
+def slope(goal, mine, whole, shares, spans, after):
+    return pl.pallas_call(
+        functools.partial(slope_kernel, goal.shape[0], len(whole), spans),
         out_shape=jax.ShapeDtypeStruct(mine.shape, jnp.bfloat16),
-        in_specs=[VMEM] * (2 + len(whole) + len(halves)) + [ANY],
+        in_specs=[VMEM] * (2 + len(whole) + len(shares)) + [ANY],
         compiler_params=params(8),
         cost_estimate=cost(4 * mine.size, 12 * mine.size),
         name="slope",
-    )(goal, mine, *whole, *halves, after)
+    )(goal, mine, *whole, *shares, after)
 
 
 def pick_columns(wide, column):
@@ -225,30 +224,37 @@
     )(*slopes, *xgs, fbk, slots, slot_row)
 
 
+def send_out(held, out, sems, t, tile):
+    rows = pl.ds(pl.multiple_of(t * tile, tile), tile)
+    return pltpu.make_async_copy(held.at[rows, :], out.at[rows, :], sems.at[t])
+
+
 def residue_kernel(order, tile, *refs):
     n = len({d for d, _, _ in order})
     slopes, xts, (fb, keep, out, s, held, sems) = refs[:n], refs[n:-6], refs[-6:]
     stack(slopes, order, s)
-    copies = []
-    for t in range(out.shape[0] // tile):
-        rows = slice(t * tile, (t + 1) * tile)
+    tiles = out.shape[0] // tile
+
+    @pl.loop(0, tiles)
+    def _(t):
+        rows = pl.ds(pl.multiple_of(t * tile, tile), tile)
         pseudo, start = fb[rows, :].astype(jnp.float32), 0
         for xt in xts:
             part = s[start : start + xt.shape[1], :]
             pseudo += jnp.dot(xt[rows, :], part, preferred_element_type=jnp.float32)
             start += xt.shape[1]
         held[rows, :] = jnp.where(keep[rows, :] > 0, pseudo, 0.0).astype(jnp.bfloat16)
-        copy = pltpu.make_async_copy(held.at[rows, :], out.at[rows, :], sems.at[t])
-        copy.start()
-        copies.append(copy)
-    for copy in copies:
-        copy.wait()
+        send_out(held, out, sems, t, tile).start()
+
+    @pl.loop(0, tiles)
+    def _(t):
+        send_out(held, out, sems, t, tile).wait()
 
 
 def residue(slopes, order, xts, fb, keep):
     depth, kw = fb.shape
     total = sum(xt.shape[1] for xt in xts)
-    tile = min(depth, 512)
+    tile = min(depth, 256)
     return pl.pallas_call(
         functools.partial(residue_kernel, order, tile),
         out_shape=jax.ShapeDtypeStruct((depth, kw), jnp.bfloat16),
@@ -265,38 +271,62 @@
     )(*slopes, *xts, fb, keep)
 
 
-def outer_kernel(n, per_row, tile, *refs):
-    messages, (out, wide, lines, held, sems) = refs[:n], refs[n:]
-    cap = messages[0].shape[0] - 16
-    for k in range(n):
-        tail = messages[k][cap:, :].astype(jnp.float32)
-        number = (tail[0:1, :] * LANES + tail[1:2, :]).astype(jnp.int32)
-        lines[:, k * cap : (k + 1) * cap] = jnp.broadcast_to(number // per_row, (8, cap))
-        column = jnp.broadcast_to((number % per_row).astype(jnp.float32), (LANES, cap)).T
-        value = messages[k][:cap, :].astype(jnp.float32)
-        for c in range(per_row):
-            wide[k * cap : (k + 1) * cap, c * LANES : (c + 1) * LANES] = jnp.where(
-                column == c, value, 0.0
-            ).astype(jnp.bfloat16)
-    copies = []
-    for t in range(out.shape[0] // tile):
-        rows = slice(t * tile, (t + 1) * tile)
+def join_kernel(*refs):
+    out = refs[-1]
+    rows = refs[0].shape[0]
+    for k in range(len(refs) - 2):
+        out[k * rows : (k + 1) * rows, :] = refs[k][...]
+
+
+def join(messages, after):
+    rows, lanes = messages[0].shape
+    return pl.pallas_call(
+        join_kernel,
+        out_shape=jax.ShapeDtypeStruct((len(messages) * rows, lanes), jnp.bfloat16),
+        in_specs=[VMEM] * len(messages) + [ANY],
+        compiler_params=params(8),
+        cost_estimate=cost(0, 4 * len(messages) * rows * lanes),
+        name="join",
+    )(*messages, after)
+
+
+def outer_kernel(cap, per_row, tile, *refs):
+    groups, (out, wide, lines, held, sems) = refs[:-5], refs[-5:]
+    n = lines.shape[1] // cap
+    size = cap + 16
+    k = 0
+    for group in groups:
+        for start in range(0, group.shape[0], size):
+            tail = group[start + cap : start + size, :].astype(jnp.float32)
+            number = (tail[0:1, :] * LANES + tail[1:2, :]).astype(jnp.int32)
+            lines[:, k * cap : (k + 1) * cap] = jnp.broadcast_to(number // per_row, (8, cap))
+            column = jnp.broadcast_to((number % per_row).astype(jnp.float32), (LANES, cap)).T
+            value = group[start : start + cap, :].astype(jnp.float32)
+            for c in range(per_row):
+                wide[k * cap : (k + 1) * cap, c * LANES : (c + 1) * LANES] = jnp.where(
+                    column == c, value, 0.0
+                ).astype(jnp.bfloat16)
+            k += 1
+    tiles = out.shape[0] // tile
+
+    @pl.loop(0, tiles)
+    def _(t):
+        rows = pl.ds(pl.multiple_of(t * tile, tile), tile)
         line = lax.broadcasted_iota(jnp.int32, (tile, n * cap), 0) + t * tile
         hot = (lines[0:1, :] == line).astype(jnp.float32).astype(jnp.bfloat16)
         held[rows, :] = jnp.dot(hot, wide[...], preferred_element_type=jnp.float32) / n
-        copy = pltpu.make_async_copy(held.at[rows, :], out.at[rows, :], sems.at[t])
-        copy.start()
-        copies.append(copy)
-    for copy in copies:
-        copy.wait()
-
-
-def outer(messages, depth, kw):
-    n = len(messages)
-    cap = messages[0].shape[0] - 16
-    tile = min(depth, 512)
-    return pl.pallas_call(
-        functools.partial(outer_kernel, n, kw // LANES, tile),
+        send_out(held, out, sems, t, tile).start()
+
+    @pl.loop(0, tiles)
+    def _(t):
+        send_out(held, out, sems, t, tile).wait()
+
+
+def outer(groups, cap, depth, kw):
+    n = sum(group.shape[0] for group in groups) // (cap + 16)
+    tile = min(depth, 256)
+    return pl.pallas_call(
+        functools.partial(outer_kernel, cap, kw // LANES, tile),
         out_shape=jax.ShapeDtypeStruct((depth, kw), jnp.float32),
         out_specs=ANY,
         scratch_shapes=[
@@ -308,7 +338,7 @@
         compiler_params=params(24),
         cost_estimate=cost(2 * n * cap * depth * kw, 4 * depth * kw),
         name="outer",
-    )(*messages)
+    )(*groups)
 
 
 def on_device(inputs, target, weights, feedback, counts, blocks):
@@ -316,7 +346,8 @@
     n_shard, n_rep = lax.axis_size("shard"), lax.axis_size("rep")
     tok_dev = tokens.shape[0]
     depth, kw = w.shape
-    half = tok_dev // 2
+    early_rows = tok_dev * 3 // 4
+    spans = [(0, early_rows), (early_rows, tok_dev)]
     per_row = kw // LANES
     slot_row = blocks[0]
     slots = blocks.reshape(-1, 1)
@@ -326,9 +357,9 @@
     far_out = cut(tokens, depth, [(d, 0, tok_dev) for d in far], [])
     far_in = [swap(x, "shard", n_shard, d) for x, d in zip(far_out, far)]
     near_out, after = [], far_out[:1]
-    for part in range(2):
-        near_out.append(cut(tokens, depth, [(d, part * half, half) for d in near], after))
-        if part == 0:
+    for low, high in spans:
+        near_out.append(cut(tokens, depth, [(d, low, high - low) for d in near], after))
+        if low == 0:
             fbk, keep = early(slots, slot_row, counts, fb, near_out[0][0])
             after = [fbk]
     near_in = [[swap(x, "shard", n_shard, d) for x, d in zip(out, near)] for out in near_out]
@@ -338,24 +369,25 @@
     (mine, *products), x_far = project([own] + far_in, [wide] + [brief] * len(far), w, [])
     whole = [swap(p, "shard", n_shard, d) for p, d in zip(products, far)]
     xg_far, xt_far = prepare([x_far], slots, counts, per_row, [])
-    after, halves, x_near = [xt_far, keep], [], []
-    for part in range(2):
+    after, shares, x_near = [xt_far, keep], [], []
+    for part in range(len(spans)):
         products, x = project(near_in[part], [brief] * len(near), w, after)
-        halves.append([swap(p, "shard", n_shard, d) for p, d in zip(products, near)])
+        shares.append([swap(p, "shard", n_shard, d) for p, d in zip(products, near)])
         x_near.append(x)
         after = [products[0]]
     xg_near, xt_near = prepare(x_near, slots, counts, per_row, [products[0]])
-    halves = [half_of[k] for k in range(len(near)) for half_of in halves]
-    slopes = slope(target[0], mine, whole, halves, xt_near)
+    shares = [share[k] for k in range(len(near)) for share in shares]
+    slopes = slope(target[0], mine, whole, shares, spans, xt_near)
     slopes = [slopes] + [swap(slopes, "shard", n_shard, d) for d in range(1, n_shard)]
 
     order = [(d, 0, tok_dev) for d in [0] + far]
-    order += [(d, part * half, (part + 1) * half) for part in range(2) for d in near]
+    order += [(d, low, high) for low, high in spans for d in near]
     message = kept(slopes, order, [xg_far, xg_near], fbk, slots, slot_row)
     same_core = [message] + [swap(message, "rep", n_rep, d) for d in range(2, n_rep, 2)]
-    messages = same_core + [swap(m, "rep", n_rep, 1) for m in same_core]
     new_feedback = residue(slopes, order, [xt_far, xt_near], fb, keep)
-    return outer(messages, depth, kw), new_feedback[None]
+    joined = join(same_core, new_feedback)
+    groups = [joined, swap(joined, "rep", n_rep, 1)]
+    return outer(groups, message.shape[0] - 16, depth, kw), new_feedback[None]
 
 
 def solution(mesh):

time: 60.7 us -> 64.2 us (1.058)
  Pallas kernels: 11.9 us -> 15 us
  starting transfers between devices: 27.2 us -> 24.6 us
  waiting for transfers between devices: 16.1 us -> 17.7 us
  local copies, waits for them, and re-layouts: 3.32 us -> 4.9 us
    ppermute x20 -> x17, starting transfers between devices: 27.2 us -> 24.6 us  [swap(): return lax.ppermute(x, axis, [(i, i ^ d) for i in range(n)])]
    unnamed x14 -> x16, local copies, waits for them, and re-layouts: 3.2 us -> 4.79 us
    ppermute x20 -> x17, waiting for transfers between devices: 16.1 us -> 17.7 us  [swap(): return lax.ppermute(x, axis, [(i, i ^ d) for i in range(n)])]
    pallas_call x2 -> x3, Pallas kernels: 3.61 us -> 4.81 us  [the longest x1 4.71 us: outer(): pl.pallas_call(functools.partial(outer_kernel, cap, kw // LANES, tile), o...]
    pallas_call x1, Pallas kernels: 2.34 us -> 3.48 us  [residue(): pl.pallas_call(functools.partial(residue_kernel, order, tile), out_shape=...]
  transfers between devices with their start and end apart: 20 -> 17, of which waited for: 7 -> 10; matrix products, arithmetic and copies ran while one was open for 0% -> 0% of each run, Pallas kernels for 13% -> 16%
where the time goes in v4:
time: 64.2 us; the launch traced here: 63.7 us
  starting transfers between devices  24.6 us (38%)
  waiting for transfers between devices  17.7 us (28%)
  Pallas kernels  15 us (23%)
  local copies, waits for them, and re-layouts  4.9 us (8%)
  between operations  1.48 us (2%)
    ppermute x17, starting transfers between devices, swap(): return lax.ppermute(x, axis, [(i, i ^ d) for i in range(n)])  24.6 us
    ppermute x17, waiting for transfers between devices, swap(): return lax.ppermute(x, axis, [(i, i ^ d) for i in range(n)])  17.7 us
    unnamed x16, local copies, waits for them, and re-layouts  4.79 us
    pallas_call x1, Pallas kernels, outer(): pl.pallas_call(functools.partial(outer_kernel, cap, kw // LANES, tile), o...  4.71 us
    pallas_call x1, Pallas kernels, residue(): pl.pallas_call(functools.partial(residue_kernel, order, tile), out_shape=...  3.48 us
    pallas_call x3, Pallas kernels, project(): pl.pallas_call(functools.partial(project_kernel, n), out_shape=[jax.Shape...  2.87 us
    pallas_call x2, Pallas kernels, prepare(): pl.pallas_call(functools.partial(prepare_kernel, per_row, len(xs)), out_s...  1.43 us
  transfers between devices with their start and end apart: 17, of which 10 were waited for; matrix products, arithmetic and copies ran while one was open for 0% of the time, Pallas kernels for 16%

profile of v4, /device:TPU:1, one launch (start us, length us, event | category | flops | bytes accessed | tf_op | source)
XLA Modules:
  0.0 63.7 jit_solution(6175685014446214294)
XLA Ops:
  0.6 1.6 %copy-done = bf16[1,128,8192]{2,1,0:T(8,128)(2,1)S(1)} copy-done((bf16[1,128,8192]{2,1,0:T(8,128)(2,1)S(1)}, bf16[1,128,8192]{2,1,0:T(8,128)(2,1)}, u32[]{:S(2)}) %copy-start) | copy-done | bytes 2097176
  2.3 3.1 %collective-permute-start = (bf16[128,2048]{1,0:T(8,128)(2,1)S(1)}, bf16[128,2048]{1,0:T(8,128)(2,1)S(1)}, u32[]{:S(2)}, u32[]{:S(2)}) collective-permute-start(bf16[128,2048]{1,0:T(8,128)(2,1)S(1)} %cut.4.refs_0_), channel_id=1, source_target_pairs={{0,3},{1,2},{2,1},{3,0},{4,7},{5,6},{6,5},{7,4},{8,11},{9,10},{10,... | collective-permute-start | bytes 1572872 | tf_op jit(solution)/shard_map/ppermute | solution.py:27
  5.4 0.9 %cut.5 = (bf16[96,2048]{1,0:T(8,128)(2,1)}, bf16[96,2048]{1,0:T(8,128)(2,1)}) custom-call(bf16[128,8192]{1,0:T(8,128)(2,1)S(1)} %bitcast.8, bf16[128,2048]{1,0:T(8,128)(2,1)S(1)} %cut.4.refs_0_), custom_call_target="tpu_custom_call" | custom-call | bytes 1572864 | tf_op jit(solution)/shard_map/cut/pallas_call | solution.py:45
  7.5 1.6 %copy-done.3 = bf16[1,2048,512]{2,1,0:T(8,128)(2,1)S(1)} copy-done((bf16[1,2048,512]{2,1,0:T(8,128)(2,1)S(1)}, bf16[1,2048,512]{2,1,0:T(8,128)(2,1)}, u32[]{:S(2)}) %copy-start.3) | copy-done | bytes 2097176
  9.0 1.0 %early.1 = (f32[128,128]{1,0:T(8,128)S(1)}, bf16[2048,512]{1,0:T(8,128)(2,1)S(1)}) custom-call(s32[128,1]{1,0:T(8,128)S(1)} %copy.8.slots.refs_1_.refs_2_.refs_7_, s32[1,128]{1,0:T(1,128)S(1)} %bitcast.19, s32[1,1]{1,0:T(1,128)S(6)} %copy.12.count.refs_2_.refs_3_, bf16[2048,512]{1,0:T(8,128)(2,1)S(1)} %bitcast.14, bf16[96,2048]{1,0:T(8,128)(2,1)} %get-tuple-element.21.after), custom_call_target="tpu_custom_call" | custom-call | flops 536870912 | bytes 4194304 | tf_op jit(solution)/shard_map/early/pallas_call | solution.py:139
  10.2 1.4 %collective-permute-start.5 = (bf16[32,2048]{1,0:T(8,128)(2,1)S(1)}, bf16[32,2048]{1,0:T(8,128)(2,1)S(1)}, u32[]{:S(2)}, u32[]{:S(2)}) collective-permute-start(bf16[32,2048]{1,0:T(8,128)(2,1)S(1)} %get-tuple-element.23.refs_0_), channel_id=1, source_target_pairs={{0,1},{1,0},{2,3},{3,2},{4,5},{5,4},{6,7},{7,6},{8,9},{9,8},{10,11... | collective-permute-start | bytes 393224 | tf_op jit(solution)/shard_map/ppermute | solution.py:27
  11.7 1.2 %collective-permute-start.6 = (bf16[32,2048]{1,0:T(8,128)(2,1)S(1)}, bf16[32,2048]{1,0:T(8,128)(2,1)S(1)}, u32[]{:S(2)}, u32[]{:S(2)}) collective-permute-start(bf16[32,2048]{1,0:T(8,128)(2,1)S(1)} %get-tuple-element.31), channel_id=1, source_target_pairs={{0,2},{1,3},{2,0},{3,1},{4,6},{5,7},{6,4},{7,5},{8,10},{9,11},{10,... | collective-permute-start | bytes 393224 | tf_op jit(solution)/shard_map/ppermute | solution.py:27
  13.0 4.1 %collective-permute-done.refs_1_ = bf16[128,2048]{1,0:T(8,128)(2,1)S(1)} collective-permute-done((bf16[128,2048]{1,0:T(8,128)(2,1)S(1)}, bf16[128,2048]{1,0:T(8,128)(2,1)S(1)}, u32[]{:S(2)}, u32[]{:S(2)}) %collective-permute-start) | collective-permute-done | bytes 524320 | tf_op jit(solution)/shard_map/ppermute | solution.py:27
  17.8 2.1 %collective-permute-start.1 = (bf16[128,512]{1,0:T(8,128)(2,1)S(1)}, bf16[128,512]{1,0:T(8,128)(2,1)S(1)}, u32[]{:S(2)}, u32[]{:S(2)}) collective-permute-start(bf16[128,512]{1,0:T(8,128)(2,1)S(1)} %get-tuple-element.25), channel_id=1, source_target_pairs={{0,3},{1,2},{2,1},{3,0},{4,7},{5,6},{6,5},{7,4},{8,11},{9,10},{10,... | collective-permute-start | bytes 393224 | tf_op jit(solution)/shard_map/ppermute | solution.py:27
  20.4 5.1 %collective-permute-done.2.refs_0_ = bf16[96,2048]{1,0:T(8,128)(2,1)} collective-permute-done((bf16[96,2048]{1,0:T(8,128)(2,1)}, bf16[96,2048]{1,0:T(8,128)(2,1)}, u32[]{:S(2)}, u32[]{:S(2)}) %collective-permute-start.2) | collective-permute-done | bytes 393248 | tf_op jit(solution)/shard_map/ppermute | solution.py:27
  25.5 0.8 %collective-permute-done.3.refs_1_ = bf16[96,2048]{1,0:T(8,128)(2,1)} collective-permute-done((bf16[96,2048]{1,0:T(8,128)(2,1)}, bf16[96,2048]{1,0:T(8,128)(2,1)}, u32[]{:S(2)}, u32[]{:S(2)}) %collective-permute-start.3) | collective-permute-done | bytes 393248 | tf_op jit(solution)/shard_map/ppermute | solution.py:27
  26.3 1.7 %project.4 = (bf16[96,512]{1,0:T(8,128)(2,1)S(1)}, bf16[96,512]{1,0:T(8,128)(2,1)S(1)}, bf16[192,2048]{1,0:T(8,128)(2,1)S(1)}) custom-call(bf16[96,2048]{1,0:T(8,128)(2,1)} %collective-permute-done.2.refs_0_, bf16[96,2048]{1,0:T(8,128)(2,1)} %collective-permute-done.3.refs_1_, bf16[2048,512]{1,0:T(8,128)(2,1)S(1)} %bitcast.12, ...), custom_call_target="tpu_custom_call" | custom-call | flops 402653184 | bytes 2883584 | tf_op jit(solution)/shard_map/project/pallas_call | solution.py:73
  28.0 1.5 %collective-permute-start.4 = (bf16[96,512]{1,0:T(8,128)(2,1)S(1)}, bf16[96,512]{1,0:T(8,128)(2,1)S(1)}, u32[]{:S(2)}, u32[]{:S(2)}) collective-permute-start(bf16[96,512]{1,0:T(8,128)(2,1)S(1)} %get-tuple-element.30.refs_3_), channel_id=1, source_target_pairs={{0,1},{1,0},{2,3},{3,2},{4,5},{5,4},{6,7},{7,6},{8,9},{9,8},{10,11... | collective-permute-start | bytes 294920 | tf_op jit(solution)/shard_map/ppermute | solution.py:27
  29.5 1.2 %collective-permute-start.8 = (bf16[96,512]{1,0:T(8,128)(2,1)S(1)}, bf16[96,512]{1,0:T(8,128)(2,1)S(1)}, u32[]{:S(2)}, u32[]{:S(2)}) collective-permute-start(bf16[96,512]{1,0:T(8,128)(2,1)S(1)} %get-tuple-element.33), channel_id=1, source_target_pairs={{0,2},{1,3},{2,0},{3,1},{4,6},{5,7},{6,4},{7,5},{8,10},{9,11},{10,... | collective-permute-start | bytes 294920 | tf_op jit(solution)/shard_map/ppermute | solution.py:27
  31.2 0.7 %collective-permute-start.7 = (bf16[32,512]{1,0:T(8,128)(2,1)S(1)}, bf16[32,512]{1,0:T(8,128)(2,1)S(1)}, u32[]{:S(2)}, u32[]{:S(2)}) collective-permute-start(bf16[32,512]{1,0:T(8,128)(2,1)S(1)} %get-tuple-element.32.refs_4_), channel_id=1, source_target_pairs={{0,1},{1,0},{2,3},{3,2},{4,5},{5,4},{6,7},{7,6},{8,9},{9,8},{10,11... | collective-permute-start | bytes 98312 | tf_op jit(solution)/shard_map/ppermute | solution.py:27
  31.9 1.2 %collective-permute-start.9 = (bf16[32,512]{1,0:T(8,128)(2,1)S(1)}, bf16[32,512]{1,0:T(8,128)(2,1)S(1)}, u32[]{:S(2)}, u32[]{:S(2)}) collective-permute-start(bf16[32,512]{1,0:T(8,128)(2,1)S(1)} %get-tuple-element.34), channel_id=1, source_target_pairs={{0,2},{1,3},{2,0},{3,1},{4,6},{5,7},{6,4},{7,5},{8,10},{9,11},{10,... | collective-permute-start | bytes 98312 | tf_op jit(solution)/shard_map/ppermute | solution.py:27
  33.2 0.9 %prepare.3 = (bf16[128,256]{1,0:T(8,128)(2,1)S(1)}, bf16[2048,256]{1,0:T(8,128)(2,1)S(1)}) custom-call(bf16[192,2048]{1,0:T(8,128)(2,1)S(1)} %get-tuple-element.35.refs_0_, bf16[64,2048]{1,0:T(8,128)(2,1)S(1)} %get-tuple-element.36.refs_1_, s32[128,1]{1,0:T(8,128)S(1)} %copy.8.slots.refs_1_.refs_2_.refs_7_, s32[1,1]{1,0:T(1,128)S(6)} %copy.12.count.refs_2_.refs_3_, ...), custom_call_target="tpu_custom_call" | custom-call | flops 134217728 | bytes 2097152 | tf_op jit(solution)/shard_map/prepare/pallas_call | solution.py:173
  34.5 0.8 %collective-permute-done.9.refs_6_ = bf16[32,512]{1,0:T(8,128)(2,1)S(1)} collective-permute-done((bf16[32,512]{1,0:T(8,128)(2,1)S(1)}, bf16[32,512]{1,0:T(8,128)(2,1)S(1)}, u32[]{:S(2)}, u32[]{:S(2)}) %collective-permute-start.9) | collective-permute-done | bytes 32800 | tf_op jit(solution)/shard_map/ppermute | solution.py:27
  35.5 0.8 %collective-permute-start.10 = (bf16[128,512]{1,0:T(8,128)(2,1)S(1)}, bf16[128,512]{1,0:T(8,128)(2,1)S(1)}, u32[]{:S(2)}, u32[]{:S(2)}) collective-permute-start(bf16[128,512]{1,0:T(8,128)(2,1)S(1)} %slope.1.refs_0_), channel_id=1, source_target_pairs={{0,1},{1,0},{2,3},{3,2},{4,5},{5,4},{6,7},{7,6},{8,9},{9,8},{10,11... | collective-permute-start | bytes 393224 | tf_op jit(solution)/shard_map/ppermute | solution.py:27
  36.3 0.8 %collective-permute-start.11 = (bf16[128,512]{1,0:T(8,128)(2,1)S(1)}, bf16[128,512]{1,0:T(8,128)(2,1)S(1)}, u32[]{:S(2)}, u32[]{:S(2)}) collective-permute-start(bf16[128,512]{1,0:T(8,128)(2,1)S(1)} %slope.1.refs_0_), channel_id=1, source_target_pairs={{0,2},{1,3},{2,0},{3,1},{4,6},{5,7},{6,4},{7,5},{8,10},{9,11},{10,... | collective-permute-start | bytes 393224 | tf_op jit(solution)/shard_map/ppermute | solution.py:27
  37.0 1.1 %collective-permute-start.12 = (bf16[128,512]{1,0:T(8,128)(2,1)S(1)}, bf16[128,512]{1,0:T(8,128)(2,1)S(1)}, u32[]{:S(2)}, u32[]{:S(2)}) collective-permute-start(bf16[128,512]{1,0:T(8,128)(2,1)S(1)} %slope.1.refs_0_), channel_id=1, source_target_pairs={{0,3},{1,2},{2,1},{3,0},{4,7},{5,6},{6,5},{7,4},{8,11},{9,10},{10,... | collective-permute-start | bytes 393224 | tf_op jit(solution)/shard_map/ppermute | solution.py:27
  38.2 1.2 %collective-permute-done.10.refs_1_ = bf16[128,512]{1,0:T(8,128)(2,1)S(1)} collective-permute-done((bf16[128,512]{1,0:T(8,128)(2,1)S(1)}, bf16[128,512]{1,0:T(8,128)(2,1)S(1)}, u32[]{:S(2)}, u32[]{:S(2)}) %collective-permute-start.10) | collective-permute-done | bytes 131104 | tf_op jit(solution)/shard_map/ppermute | solution.py:27
  39.4 1.0 %collective-permute-done.11.refs_2_ = bf16[128,512]{1,0:T(8,128)(2,1)S(1)} collective-permute-done((bf16[128,512]{1,0:T(8,128)(2,1)S(1)}, bf16[128,512]{1,0:T(8,128)(2,1)S(1)}, u32[]{:S(2)}, u32[]{:S(2)}) %collective-permute-start.11) | collective-permute-done | bytes 131104 | tf_op jit(solution)/shard_map/ppermute | solution.py:27
  40.4 2.2 %collective-permute-done.12.refs_3_ = bf16[128,512]{1,0:T(8,128)(2,1)S(1)} collective-permute-done((bf16[128,512]{1,0:T(8,128)(2,1)S(1)}, bf16[128,512]{1,0:T(8,128)(2,1)S(1)}, u32[]{:S(2)}, u32[]{:S(2)}) %collective-permute-start.12) | collective-permute-done | bytes 131104 | tf_op jit(solution)/shard_map/ppermute | solution.py:27
  42.8 1.3 %collective-permute-start.13 = (bf16[144,128]{1,0:T(8,128)(2,1)S(1)}, bf16[144,128]{1,0:T(8,128)(2,1)S(1)}, u32[]{:S(2)}, u32[]{:S(2)}) collective-permute-start(bf16[144,128]{1,0:T(8,128)(2,1)S(1)} %kept.1.refs_0_), channel_id=1, source_target_pairs={{0,8},{4,12},{8,0},{12,4},{16,24},{20,28},{24,16},{28,20},{1,9},{5... | collective-permute-start | bytes 110600 | tf_op jit(solution)/shard_map/ppermute | solution.py:27
  44.1 2.3 %collective-permute-start.14 = (bf16[144,128]{1,0:T(8,128)(2,1)S(1)}, bf16[144,128]{1,0:T(8,128)(2,1)S(1)}, u32[]{:S(2)}, u32[]{:S(2)}) collective-permute-start(bf16[144,128]{1,0:T(8,128)(2,1)S(1)} %kept.1.refs_0_), channel_id=1, source_target_pairs={{0,16},{4,20},{8,24},{12,28},{16,0},{20,4},{24,8},{28,12},{1,17},{... | collective-permute-start | bytes 110600 | tf_op jit(solution)/shard_map/ppermute | solution.py:27
  46.5 3.5 %residue.1.refs_4_ = bf16[2048,512]{1,0:T(8,128)(2,1)} custom-call(bf16[128,512]{1,0:T(8,128)(2,1)S(1)} %slope.1.refs_0_, bf16[128,512]{1,0:T(8,128)(2,1)S(1)} %collective-permute-done.10.refs_1_, bf16[128,512]{1,0:T(8,128)(2,1)S(1)} %collective-permute-done.11.refs_2_, bf16[128,512]{1,0:T(8,128)(2,1)S(1)} %collective-permute-done.12.refs_3_, ...), custom_call_target="tpu_custom_call" | custom-call | flops 1073741824 | bytes 8388608 | tf_op jit(solution)/shard_map/residue/pallas_call | solution.py:258
  50.0 1.1 %collective-permute-done.15.refs_3_ = bf16[144,128]{1,0:T(8,128)(2,1)S(1)} collective-permute-done((bf16[144,128]{1,0:T(8,128)(2,1)S(1)}, bf16[144,128]{1,0:T(8,128)(2,1)S(1)}, u32[]{:S(2)}, u32[]{:S(2)}) %collective-permute-start.15) | collective-permute-done | bytes 36896 | tf_op jit(solution)/shard_map/ppermute | solution.py:27
  51.1 1.6 %copy-done.5 = bf16[2048,512]{1,0:T(8,128)(2,1)S(1)} copy-done((bf16[2048,512]{1,0:T(8,128)(2,1)S(1)}, bf16[2048,512]{1,0:T(8,128)(2,1)}, u32[]{:S(2)}) %copy-start.5) | copy-done | bytes 2097176
  52.7 5.3 %collective-permute-start.16 = (bf16[576,128]{1,0:T(8,128)(2,1)S(1)}, bf16[576,128]{1,0:T(8,128)(2,1)S(1)}, u32[]{:S(2)}, u32[]{:S(2)}) collective-permute-start(bf16[576,128]{1,0:T(8,128)(2,1)S(1)} %join.1.refs_0_), channel_id=1, source_target_pairs={{0,4},{4,0},{8,12},{12,8},{16,20},{20,16},{24,28},{28,24},{1,5},{5... | collective-permute-start | bytes 442376 | tf_op jit(solution)/shard_map/ppermute | solution.py:27
  58.0 1.0 %collective-permute-done.16.refs_1_ = bf16[576,128]{1,0:T(8,128)(2,1)S(1)} collective-permute-done((bf16[576,128]{1,0:T(8,128)(2,1)S(1)}, bf16[576,128]{1,0:T(8,128)(2,1)S(1)}, u32[]{:S(2)}, u32[]{:S(2)}) %collective-permute-start.16) | collective-permute-done | bytes 147488 | tf_op jit(solution)/shard_map/ppermute | solution.py:27
  59.0 4.7 %outer.1 = f32[2048,512]{1,0:T(8,128)} custom-call(bf16[576,128]{1,0:T(8,128)(2,1)S(1)} %join.1.refs_0_, bf16[576,128]{1,0:T(8,128)(2,1)S(1)} %collective-permute-done.16.refs_1_), custom_call_target="tpu_custom_call" | custom-call | flops 2147483648 | bytes 4194304 | tf_op jit(solution)/shard_map/outer/pallas_call | solution.py:328
  (34 shorter events, 3.3 us)
Async XLA Ops:
  0.6 1.6 %copy-start = (bf16[1,128,8192]{2,1,0:T(8,128)(2,1)S(1)}, bf16[1,128,8192]{2,1,0:T(8,128)(2,1)}, u32[]{:S(2)}) copy-start(bf16[1,128,8192]{2,1,0:T(8,128)(2,1)} %param.6) | copy-start | bytes 6291460
  2.2 4.5 %copy-start.7 = (s32[1,1,128]{2,1,0:T(1,128)S(1)}, s32[1,1,128]{2,1,0:T(1,128)}, u32[]{:S(2)}) copy-start(s32[1,1,128]{2,1,0:T(1,128)} %param.11) | copy-start | bytes 1540
  2.3 7.8 %copy-start.1 = (bf16[1,128,8192]{2,1,0:T(8,128)(2,1)S(1)}, bf16[1,128,8192]{2,1,0:T(8,128)(2,1)}, u32[]{:S(2)}) copy-start(bf16[1,128,8192]{2,1,0:T(8,128)(2,1)} %param.6) | copy-start | bytes 6291460
  2.3 14.8 %collective-permute-start = (bf16[128,2048]{1,0:T(8,128)(2,1)S(1)}, bf16[128,2048]{1,0:T(8,128)(2,1)S(1)}, u32[]{:S(2)}, u32[]{:S(2)}) collective-permute-start(bf16[128,2048]{1,0:T(8,128)(2,1)S(1)} %cut.4.refs_0_), channel_id=1, source_target_pairs={{0,3},{1,2},{2,1},{3,0},{4,7},{5,6},{6,5},{7,4},{8,11},{9,10},{10,... | collective-permute-start | bytes 1572872 | tf_op jit(solution)/shard_map/ppermute | solution.py:27
  6.3 19.2 %collective-permute-start.2 = (bf16[96,2048]{1,0:T(8,128)(2,1)}, bf16[96,2048]{1,0:T(8,128)(2,1)}, u32[]{:S(2)}, u32[]{:S(2)}) collective-permute-start(bf16[96,2048]{1,0:T(8,128)(2,1)} %get-tuple-element.21.after), channel_id=1, source_target_pairs={{0,1},{1,0},{2,3},{3,2},{4,5},{5,4},{6,7},{7,6},{8,9},{9,8},{10,11... | collective-permute-start | bytes 1179656 | tf_op jit(solution)/shard_map/ppermute | solution.py:27
  6.6 19.6 %collective-permute-start.3 = (bf16[96,2048]{1,0:T(8,128)(2,1)}, bf16[96,2048]{1,0:T(8,128)(2,1)}, u32[]{:S(2)}, u32[]{:S(2)}) collective-permute-start(bf16[96,2048]{1,0:T(8,128)(2,1)} %get-tuple-element.26), channel_id=1, source_target_pairs={{0,2},{1,3},{2,0},{3,1},{4,6},{5,7},{6,4},{7,5},{8,10},{9,11},{10,... | collective-permute-start | bytes 1179656 | tf_op jit(solution)/shard_map/ppermute | solution.py:27
  7.5 1.6 %copy-start.3 = (bf16[1,2048,512]{2,1,0:T(8,128)(2,1)S(1)}, bf16[1,2048,512]{2,1,0:T(8,128)(2,1)}, u32[]{:S(2)}) copy-start(bf16[1,2048,512]{2,1,0:T(8,128)(2,1)} %param.9) | copy-start | bytes 6291460
  10.1 6.9 %copy-start.2 = (bf16[1,2048,512]{2,1,0:T(8,128)(2,1)S(1)}, bf16[1,2048,512]{2,1,0:T(8,128)(2,1)}, u32[]{:S(2)}) copy-start(bf16[1,2048,512]{2,1,0:T(8,128)(2,1)} %param.8) | copy-start | bytes 6291460
  10.2 20.4 %collective-permute-start.5 = (bf16[32,2048]{1,0:T(8,128)(2,1)S(1)}, bf16[32,2048]{1,0:T(8,128)(2,1)S(1)}, u32[]{:S(2)}, u32[]{:S(2)}) collective-permute-start(bf16[32,2048]{1,0:T(8,128)(2,1)S(1)} %get-tuple-element.23.refs_0_), channel_id=1, source_target_pairs={{0,1},{1,0},{2,3},{3,2},{4,5},{5,4},{6,7},{7,6},{8,9},{9,8},{10,11... | collective-permute-start | bytes 393224 | tf_op jit(solution)/shard_map/ppermute | solution.py:27
  11.7 19.0 %collective-permute-start.6 = (bf16[32,2048]{1,0:T(8,128)(2,1)S(1)}, bf16[32,2048]{1,0:T(8,128)(2,1)S(1)}, u32[]{:S(2)}, u32[]{:S(2)}) collective-permute-start(bf16[32,2048]{1,0:T(8,128)(2,1)S(1)} %get-tuple-element.31), channel_id=1, source_target_pairs={{0,2},{1,3},{2,0},{3,1},{4,6},{5,7},{6,4},{7,5},{8,10},{9,11},{10,... | collective-permute-start | bytes 393224 | tf_op jit(solution)/shard_map/ppermute | solution.py:27
  17.8 17.6 %collective-permute-start.1 = (bf16[128,512]{1,0:T(8,128)(2,1)S(1)}, bf16[128,512]{1,0:T(8,128)(2,1)S(1)}, u32[]{:S(2)}, u32[]{:S(2)}) collective-permute-start(bf16[128,512]{1,0:T(8,128)(2,1)S(1)} %get-tuple-element.25), channel_id=1, source_target_pairs={{0,3},{1,2},{2,1},{3,0},{4,7},{5,6},{6,5},{7,4},{8,11},{9,10},{10,... | collective-permute-start | bytes 393224 | tf_op jit(solution)/shard_map/ppermute | solution.py:27
  28.0 7.4 %copy-start.6 = (bf16[1,128,512]{2,1,0:T(8,128)(2,1)S(1)}, bf16[1,128,512]{2,1,0:T(8,128)(2,1)}, u32[]{:S(2)}) copy-start(bf16[1,128,512]{2,1,0:T(8,128)(2,1)} %param.7) | copy-start | bytes 393220
  28.0 7.4 %collective-permute-start.4 = (bf16[96,512]{1,0:T(8,128)(2,1)S(1)}, bf16[96,512]{1,0:T(8,128)(2,1)S(1)}, u32[]{:S(2)}, u32[]{:S(2)}) collective-permute-start(bf16[96,512]{1,0:T(8,128)(2,1)S(1)} %get-tuple-element.30.refs_3_), channel_id=1, source_target_pairs={{0,1},{1,0},{2,3},{3,2},{4,5},{5,4},{6,7},{7,6},{8,9},{9,8},{10,11... | collective-permute-start | bytes 294920 | tf_op jit(solution)/shard_map/ppermute | solution.py:27
  29.5 5.9 %collective-permute-start.8 = (bf16[96,512]{1,0:T(8,128)(2,1)S(1)}, bf16[96,512]{1,0:T(8,128)(2,1)S(1)}, u32[]{:S(2)}, u32[]{:S(2)}) collective-permute-start(bf16[96,512]{1,0:T(8,128)(2,1)S(1)} %get-tuple-element.33), channel_id=1, source_target_pairs={{0,2},{1,3},{2,0},{3,1},{4,6},{5,7},{6,4},{7,5},{8,10},{9,11},{10,... | collective-permute-start | bytes 294920 | tf_op jit(solution)/shard_map/ppermute | solution.py:27
  31.2 15.3 %copy-start.4 = (bf16[1,2048,512]{2,1,0:T(8,128)(2,1)S(1)}, bf16[1,2048,512]{2,1,0:T(8,128)(2,1)}, u32[]{:S(2)}) copy-start(bf16[1,2048,512]{2,1,0:T(8,128)(2,1)} %param.9) | copy-start | bytes 6291460
  31.2 3.3 %collective-permute-start.7 = (bf16[32,512]{1,0:T(8,128)(2,1)S(1)}, bf16[32,512]{1,0:T(8,128)(2,1)S(1)}, u32[]{:S(2)}, u32[]{:S(2)}) collective-permute-start(bf16[32,512]{1,0:T(8,128)(2,1)S(1)} %get-tuple-element.32.refs_4_), channel_id=1, source_target_pairs={{0,1},{1,0},{2,3},{3,2},{4,5},{5,4},{6,7},{7,6},{8,9},{9,8},{10,11... | collective-permute-start | bytes 98312 | tf_op jit(solution)/shard_map/ppermute | solution.py:27
  31.9 3.4 %collective-permute-start.9 = (bf16[32,512]{1,0:T(8,128)(2,1)S(1)}, bf16[32,512]{1,0:T(8,128)(2,1)S(1)}, u32[]{:S(2)}, u32[]{:S(2)}) collective-permute-start(bf16[32,512]{1,0:T(8,128)(2,1)S(1)} %get-tuple-element.34), channel_id=1, source_target_pairs={{0,2},{1,3},{2,0},{3,1},{4,6},{5,7},{6,4},{7,5},{8,10},{9,11},{10,... | collective-permute-start | bytes 98312 | tf_op jit(solution)/shard_map/ppermute | solution.py:27
  35.5 3.9 %collective-permute-start.10 = (bf16[128,512]{1,0:T(8,128)(2,1)S(1)}, bf16[128,512]{1,0:T(8,128)(2,1)S(1)}, u32[]{:S(2)}, u32[]{:S(2)}) collective-permute-start(bf16[128,512]{1,0:T(8,128)(2,1)S(1)} %slope.1.refs_0_), channel_id=1, source_target_pairs={{0,1},{1,0},{2,3},{3,2},{4,5},{5,4},{6,7},{7,6},{8,9},{9,8},{10,11... | collective-permute-start | bytes 393224 | tf_op jit(solution)/shard_map/ppermute | solution.py:27
  36.3 4.1 %collective-permute-start.11 = (bf16[128,512]{1,0:T(8,128)(2,1)S(1)}, bf16[128,512]{1,0:T(8,128)(2,1)S(1)}, u32[]{:S(2)}, u32[]{:S(2)}) collective-permute-start(bf16[128,512]{1,0:T(8,128)(2,1)S(1)} %slope.1.refs_0_), channel_id=1, source_target_pairs={{0,2},{1,3},{2,0},{3,1},{4,6},{5,7},{6,4},{7,5},{8,10},{9,11},{10,... | collective-permute-start | bytes 393224 | tf_op jit(solution)/shard_map/ppermute | solution.py:27
  37.0 5.5 %collective-permute-start.12 = (bf16[128,512]{1,0:T(8,128)(2,1)S(1)}, bf16[128,512]{1,0:T(8,128)(2,1)S(1)}, u32[]{:S(2)}, u32[]{:S(2)}) collective-permute-start(bf16[128,512]{1,0:T(8,128)(2,1)S(1)} %slope.1.refs_0_), channel_id=1, source_target_pairs={{0,3},{1,2},{2,1},{3,0},{4,7},{5,6},{6,5},{7,4},{8,11},{9,10},{10,... | collective-permute-start | bytes 393224 | tf_op jit(solution)/shard_map/ppermute | solution.py:27
  42.8 7.1 %collective-permute-start.13 = (bf16[144,128]{1,0:T(8,128)(2,1)S(1)}, bf16[144,128]{1,0:T(8,128)(2,1)S(1)}, u32[]{:S(2)}, u32[]{:S(2)}) collective-permute-start(bf16[144,128]{1,0:T(8,128)(2,1)S(1)} %kept.1.refs_0_), channel_id=1, source_target_pairs={{0,8},{4,12},{8,0},{12,4},{16,24},{20,28},{24,16},{28,20},{1,9},{5... | collective-permute-start | bytes 110600 | tf_op jit(solution)/shard_map/ppermute | solution.py:27
  44.1 5.8 %collective-permute-start.14 = (bf16[144,128]{1,0:T(8,128)(2,1)S(1)}, bf16[144,128]{1,0:T(8,128)(2,1)S(1)}, u32[]{:S(2)}, u32[]{:S(2)}) collective-permute-start(bf16[144,128]{1,0:T(8,128)(2,1)S(1)} %kept.1.refs_0_), channel_id=1, source_target_pairs={{0,16},{4,20},{8,24},{12,28},{16,0},{20,4},{24,8},{28,12},{1,17},{... | collective-permute-start | bytes 110600 | tf_op jit(solution)/shard_map/ppermute | solution.py:27
  46.4 4.6 %collective-permute-start.15 = (bf16[144,128]{1,0:T(8,128)(2,1)S(1)}, bf16[144,128]{1,0:T(8,128)(2,1)S(1)}, u32[]{:S(2)}, u32[]{:S(2)}) collective-permute-start(bf16[144,128]{1,0:T(8,128)(2,1)S(1)} %kept.1.refs_0_), channel_id=1, source_target_pairs={{0,24},{4,28},{8,16},{12,20},{16,8},{20,12},{24,0},{28,4},{1,25},{... | collective-permute-start | bytes 110600 | tf_op jit(solution)/shard_map/ppermute | solution.py:27
  51.1 1.6 %copy-start.5 = (bf16[2048,512]{1,0:T(8,128)(2,1)S(1)}, bf16[2048,512]{1,0:T(8,128)(2,1)}, u32[]{:S(2)}) copy-start(bf16[2048,512]{1,0:T(8,128)(2,1)} %residue.1.refs_4_) | copy-start | bytes 6291460
  52.7 6.3 %collective-permute-start.16 = (bf16[576,128]{1,0:T(8,128)(2,1)S(1)}, bf16[576,128]{1,0:T(8,128)(2,1)S(1)}, u32[]{:S(2)}, u32[]{:S(2)}) collective-permute-start(bf16[576,128]{1,0:T(8,128)(2,1)S(1)} %join.1.refs_0_), channel_id=1, source_target_pairs={{0,4},{4,0},{8,12},{12,8},{16,20},{20,16},{24,28},{28,24},{1,5},{5... | collective-permute-start | bytes 442376 | tf_op jit(solution)/shard_map/ppermute | solution.py:27

commit v5 on v4

--- a/solution.py
+++ b/solution.py
@@ -9,26 +9,25 @@
 
 LANES = 128
 ANY = pl.BlockSpec(memory_space=pl.ANY)
+BRIEF = pl.CostEstimate(flops=1000, bytes_accessed=1000, transcendentals=0)
 VMEM = pl.BlockSpec(memory_space=pltpu.VMEM)
 HBM = pl.BlockSpec(memory_space=pltpu.HBM)
 SMEM = pl.BlockSpec(memory_space=pltpu.SMEM)
 MIB = 1024 * 1024
+TOKEN = jax.ShapeDtypeStruct((8, LANES), jnp.float32)
 
 
 def params(mib):
     return pltpu.CompilerParams(vmem_limit_bytes=mib * MIB)
 
 
-def cost(flops, nbytes):
-    return pl.CostEstimate(flops=int(flops), bytes_accessed=int(nbytes), transcendentals=0)
-
-
 def swap(x, axis, n, d):
     return lax.ppermute(x, axis, [(i, i ^ d) for i in range(n)])
 
 
 def cut_kernel(cuts, tokens, *refs):
-    outs, sems = refs[-len(cuts) - 1 : -1], refs[-1]
+    outs, (token, sems) = refs[-len(cuts) - 2 : -2], refs[-2:]
+    token[...] = jnp.zeros_like(token)
     me = lax.axis_index("shard")
     copies = []
     for k, (d, low, rows) in enumerate(cuts):
@@ -41,14 +40,15 @@
         copy.wait()
 
 
-def cut(tokens, depth, cuts, after):
+def cut(tokens, depth, cuts, after, mib=16):
     return pl.pallas_call(
         functools.partial(cut_kernel, cuts),
-        out_shape=[jax.ShapeDtypeStruct((rows, depth), tokens.dtype) for _, _, rows in cuts],
+        out_shape=[jax.ShapeDtypeStruct((rows, depth), tokens.dtype) for _, _, rows in cuts]
+        + [TOKEN],
         in_specs=[HBM] + [ANY] * len(after),
         scratch_shapes=[pltpu.SemaphoreType.DMA((len(cuts),))],
-        compiler_params=params(16),
-        cost_estimate=cost(0, 4 * depth * sum(rows for _, _, rows in cuts)),
+        compiler_params=params(mib),
+        cost_estimate=BRIEF,
         name="cut",
     )(tokens, *after)
 
@@ -76,7 +76,7 @@
         + [jax.ShapeDtypeStruct((rows, depth), jnp.bfloat16)],
         in_specs=[VMEM] * (n + 1) + [ANY] * len(after),
         compiler_params=params(24),
-        cost_estimate=cost(2 * rows * depth * kw, 2 * depth * (rows + kw)),
+        cost_estimate=BRIEF,
         name="project",
     )(*pieces, w, *after)
     return result[:n], result[n]
@@ -102,7 +102,7 @@
         out_shape=jax.ShapeDtypeStruct(mine.shape, jnp.bfloat16),
         in_specs=[VMEM] * (2 + len(whole) + len(shares)) + [ANY],
         compiler_params=params(8),
-        cost_estimate=cost(4 * mine.size, 12 * mine.size),
+        cost_estimate=BRIEF,
         name="slope",
     )(goal, mine, *whole, *shares, after)
 
@@ -114,7 +114,8 @@
     return out
 
 
-def early_kernel(per_row, slots, slot_row, count, fb, after, fbk, keep):
+def early_kernel(per_row, slots, slot_row, count, fb, after, fbk, keep, token):
+    token[...] = jnp.zeros_like(token)
     depth, kw = fb.shape
     cap = slots.shape[0]
     slot = slots[...]
@@ -141,16 +142,18 @@
         out_shape=[
             jax.ShapeDtypeStruct((cap, LANES), jnp.float32),
             jax.ShapeDtypeStruct((depth, kw), jnp.bfloat16),
+            TOKEN,
         ],
         in_specs=[VMEM, VMEM, SMEM, VMEM, ANY],
         compiler_params=params(24),
-        cost_estimate=cost(4 * cap * depth * kw, 4 * depth * kw),
+        cost_estimate=BRIEF,
         name="early",
     )(slots, slot_row, count, fb, after)
 
 
 def prepare_kernel(per_row, n, *refs):
-    xs, (slots, count), (xg, xt) = refs[:n], refs[n : n + 2], refs[-2:]
+    xs, (slots, count), (xg, xt, token) = refs[:n], refs[n : n + 2], refs[-3:]
+    token[...] = jnp.zeros_like(token)
     depth = xs[0].shape[1]
     cap = slots.shape[0]
     used = lax.broadcasted_iota(jnp.int32, (cap, 1), 0) < count[0, 0]
@@ -175,23 +178,24 @@
         out_shape=[
             jax.ShapeDtypeStruct((cap, rows), jnp.bfloat16),
             jax.ShapeDtypeStruct((depth, rows), jnp.bfloat16),
+            TOKEN,
         ],
         in_specs=[VMEM] * (len(xs) + 1) + [SMEM] + [ANY] * len(after),
         compiler_params=params(24),
-        cost_estimate=cost(2 * cap * depth * rows, 4 * depth * rows),
+        cost_estimate=BRIEF,
         name="prepare",
     )(*xs, slots, count, *after)
 
 
 def stack(slopes, order, s):
     start = 0
-    for d, low, high in order:
-        s[start : start + high - low, :] = slopes[d][low:high, :]
+    for k, low, high in order:
+        s[start : start + high - low, :] = slopes[k][low:high, :]
         start += high - low
 
 
 def kept_kernel(per_row, order, *refs):
-    n = len({d for d, _, _ in order})
+    n = len({k for k, _, _ in order})
     slopes, (fbk, slots, slot_row), out, s = refs[:n], refs[-5:-2], refs[-2], refs[-1]
     xgs = refs[n:-5]
     cap = slots.shape[0]
@@ -219,25 +223,24 @@
         out_shape=jax.ShapeDtypeStruct((cap + 16, LANES), jnp.bfloat16),
         scratch_shapes=[pltpu.VMEM((total, kw), jnp.bfloat16)],
         compiler_params=params(8),
-        cost_estimate=cost(2 * cap * total * kw, 2 * total * kw),
+        cost_estimate=BRIEF,
         name="kept",
     )(*slopes, *xgs, fbk, slots, slot_row)
 
 
 def send_out(held, out, sems, t, tile):
-    rows = pl.ds(pl.multiple_of(t * tile, tile), tile)
+    rows = pl.ds(t * tile, tile)
     return pltpu.make_async_copy(held.at[rows, :], out.at[rows, :], sems.at[t])
 
 
 def residue_kernel(order, tile, *refs):
-    n = len({d for d, _, _ in order})
-    slopes, xts, (fb, keep, out, s, held, sems) = refs[:n], refs[n:-6], refs[-6:]
+    n = len({k for k, _, _ in order})
+    slopes, xts, (fb, keep, out, token, s, held, sems) = refs[:n], refs[n:-7], refs[-7:]
+    token[...] = jnp.zeros_like(token)
     stack(slopes, order, s)
     tiles = out.shape[0] // tile
-
-    @pl.loop(0, tiles)
-    def _(t):
-        rows = pl.ds(pl.multiple_of(t * tile, tile), tile)
+    for t in range(tiles):
+        rows = slice(t * tile, (t + 1) * tile)
         pseudo, start = fb[rows, :].astype(jnp.float32), 0
         for xt in xts:
             part = s[start : start + xt.shape[1], :]
@@ -245,28 +248,29 @@
             start += xt.shape[1]
         held[rows, :] = jnp.where(keep[rows, :] > 0, pseudo, 0.0).astype(jnp.bfloat16)
         send_out(held, out, sems, t, tile).start()
-
-    @pl.loop(0, tiles)
-    def _(t):
+    for t in range(tiles):
         send_out(held, out, sems, t, tile).wait()
 
 
 def residue(slopes, order, xts, fb, keep):
     depth, kw = fb.shape
     total = sum(xt.shape[1] for xt in xts)
-    tile = min(depth, 256)
+    tile = min(depth, 512)
     return pl.pallas_call(
         functools.partial(residue_kernel, order, tile),
-        out_shape=jax.ShapeDtypeStruct((depth, kw), jnp.bfloat16),
+        out_shape=[
+            jax.ShapeDtypeStruct((depth, kw), jnp.bfloat16),
+            TOKEN,
+        ],
         in_specs=[VMEM] * (len(slopes) + len(xts) + 2),
-        out_specs=ANY,
+        out_specs=[ANY, VMEM],
         scratch_shapes=[
             pltpu.VMEM((total, kw), jnp.bfloat16),
             pltpu.VMEM((depth, kw), jnp.bfloat16),
             pltpu.SemaphoreType.DMA((depth // tile,)),
         ],
         compiler_params=params(24),
-        cost_estimate=cost(2 * total * depth * kw, 2 * depth * (total + 3 * kw)),
+        cost_estimate=BRIEF,
         name="residue",
     )(*slopes, *xts, fb, keep)
 
@@ -285,7 +289,7 @@
         out_shape=jax.ShapeDtypeStruct((len(messages) * rows, lanes), jnp.bfloat16),
         in_specs=[VMEM] * len(messages) + [ANY],
         compiler_params=params(8),
-        cost_estimate=cost(0, 4 * len(messages) * rows * lanes),
+        cost_estimate=BRIEF,
         name="join",
     )(*messages, after)
 
@@ -309,22 +313,19 @@
             k += 1
     tiles = out.shape[0] // tile
 
-    @pl.loop(0, tiles)
-    def _(t):
-        rows = pl.ds(pl.multiple_of(t * tile, tile), tile)
+    for t in range(tiles):
+        rows = slice(t * tile, (t + 1) * tile)
         line = lax.broadcasted_iota(jnp.int32, (tile, n * cap), 0) + t * tile
         hot = (lines[0:1, :] == line).astype(jnp.float32).astype(jnp.bfloat16)
         held[rows, :] = jnp.dot(hot, wide[...], preferred_element_type=jnp.float32) / n
         send_out(held, out, sems, t, tile).start()
-
-    @pl.loop(0, tiles)
-    def _(t):
+    for t in range(tiles):
         send_out(held, out, sems, t, tile).wait()
 
 
 def outer(groups, cap, depth, kw):
     n = sum(group.shape[0] for group in groups) // (cap + 16)
-    tile = min(depth, 256)
+    tile = min(depth, 512)
     return pl.pallas_call(
         functools.partial(outer_kernel, cap, kw // LANES, tile),
         out_shape=jax.ShapeDtypeStruct((depth, kw), jnp.float32),
@@ -336,7 +337,7 @@
             pltpu.SemaphoreType.DMA((depth // tile,)),
         ],
         compiler_params=params(24),
-        cost_estimate=cost(2 * n * cap * depth * kw, 4 * depth * kw),
+        cost_estimate=BRIEF,
         name="outer",
     )(*groups)
 
@@ -346,7 +347,7 @@
     n_shard, n_rep = lax.axis_size("shard"), lax.axis_size("rep")
     tok_dev = tokens.shape[0]
     depth, kw = w.shape
-    early_rows = tok_dev * 3 // 4
+    early_rows = tok_dev // 2
     spans = [(0, early_rows), (early_rows, tok_dev)]
     per_row = kw // LANES
     slot_row = blocks[0]
@@ -354,38 +355,38 @@
     near = [d for d in range(1, n_shard) if d & (d - 1) == 0]
     far = [d for d in range(1, n_shard) if d & (d - 1) != 0]
 
-    far_out = cut(tokens, depth, [(d, 0, tok_dev) for d in far], [])
+    *far_out, token = cut(tokens, depth, [(d, 0, tok_dev) for d in far], [], 60)
     far_in = [swap(x, "shard", n_shard, d) for x, d in zip(far_out, far)]
-    near_out, after = [], far_out[:1]
+    near_out = []
     for low, high in spans:
-        near_out.append(cut(tokens, depth, [(d, low, high - low) for d in near], after))
+        *out, token = cut(tokens, depth, [(d, low, high - low) for d in near], [token])
+        near_out.append(out)
         if low == 0:
-            fbk, keep = early(slots, slot_row, counts, fb, near_out[0][0])
-            after = [fbk]
+            fbk, keep, token = early(slots, slot_row, counts, fb, token)
     near_in = [[swap(x, "shard", n_shard, d) for x, d in zip(out, near)] for out in near_out]
-    (own,) = cut(tokens, depth, [(0, 0, tok_dev)], [near_out[1][0]])
+    own, _ = cut(tokens, depth, [(0, 0, tok_dev)], [token])
 
     brief, wide = jnp.bfloat16, jnp.float32
     (mine, *products), x_far = project([own] + far_in, [wide] + [brief] * len(far), w, [])
     whole = [swap(p, "shard", n_shard, d) for p, d in zip(products, far)]
-    xg_far, xt_far = prepare([x_far], slots, counts, per_row, [])
-    after, shares, x_near = [xt_far, keep], [], []
+    xg_far, xt_far, token = prepare([x_far], slots, counts, per_row, [])
+    after, shares, x_near = [token], [], []
     for part in range(len(spans)):
         products, x = project(near_in[part], [brief] * len(near), w, after)
         shares.append([swap(p, "shard", n_shard, d) for p, d in zip(products, near)])
         x_near.append(x)
-        after = [products[0]]
-    xg_near, xt_near = prepare(x_near, slots, counts, per_row, [products[0]])
+        after = products[-1:]
+    xg_near, xt_near, token = prepare(x_near, slots, counts, per_row, [products[0]])
     shares = [share[k] for k in range(len(near)) for share in shares]
-    slopes = slope(target[0], mine, whole, shares, spans, xt_near)
-    slopes = [slopes] + [swap(slopes, "shard", n_shard, d) for d in range(1, n_shard)]
-
-    order = [(d, 0, tok_dev) for d in [0] + far]
-    order += [(d, low, high) for low, high in spans for d in near]
+    slopes = slope(target[0], mine, whole, shares, spans, token)
+    slopes = [slopes] + [swap(slopes, "shard", n_shard, d) for d in far + near]
+
+    order = [(k, 0, tok_dev) for k in range(1 + len(far))]
+    order += [(k, low, high) for low, high in spans for k in range(1 + len(far), n_shard)]
     message = kept(slopes, order, [xg_far, xg_near], fbk, slots, slot_row)
     same_core = [message] + [swap(message, "rep", n_rep, d) for d in range(2, n_rep, 2)]
-    new_feedback = residue(slopes, order, [xt_far, xt_near], fb, keep)
-    joined = join(same_core, new_feedback)
+    new_feedback, token = residue(slopes, order, [xt_far, xt_near], fb, keep)
+    joined = join(same_core, token)
     groups = [joined, swap(joined, "rep", n_rep, 1)]
     return outer(groups, message.shape[0] - 16, depth, kw), new_feedback[None]
 

time: 64.2 us -> 61.2 us (0.953)
  local copies, waits for them, and re-layouts: 4.9 us -> 2.41 us
  waiting for transfers between devices: 17.7 us -> 19.4 us
  Pallas kernels: 15 us -> 13.4 us
    unnamed x16 -> x14, local copies, waits for them, and re-layouts: 4.79 us -> 2.3 us
    pallas_call x4, Pallas kernels: 1.16 us -> 3.46 us  [cut(): pl.pallas_call(functools.partial(cut_kernel, cuts), out_shape=[jax.ShapeD...]
    ppermute x17, waiting for transfers between devices: 17.7 us -> 19.4 us  [swap(): return lax.ppermute(x, axis, [(i, i ^ d) for i in range(n)])]
    pallas_call x3, Pallas kernels: 2.87 us -> 1.59 us  [project(): pl.pallas_call(functools.partial(project_kernel, n), out_shape=[jax.Shape...]
    pallas_call x1, Pallas kernels: 4.71 us -> 3.51 us  [outer(): pl.pallas_call(functools.partial(outer_kernel, cap, kw // LANES, tile), o...]
    pallas_call x1, Pallas kernels: 3.48 us -> 2.39 us  [residue(): pl.pallas_call(functools.partial(residue_kernel, order, tile), out_shape=...]
  transfers between devices with their start and end apart: 17 -> 17, of which waited for: 10 -> 12; matrix products, arithmetic and copies ran while one was open for 0% -> 0% of each run, Pallas kernels for 16% -> 12%
where the time goes in v5:
time: 61.2 us; the launch traced here: 60.7 us
  starting transfers between devices  24 us (39%)
  waiting for transfers between devices  19.4 us (32%)
  Pallas kernels  13.4 us (22%)
  local copies, waits for them, and re-layouts  2.41 us (4%)
  between operations  1.47 us (2%)
    ppermute x17, starting transfers between devices, swap(): return lax.ppermute(x, axis, [(i, i ^ d) for i in range(n)])  24 us
    ppermute x17, waiting for transfers between devices, swap(): return lax.ppermute(x, axis, [(i, i ^ d) for i in range(n)])  19.4 us
    pallas_call x1, Pallas kernels, outer(): pl.pallas_call(functools.partial(outer_kernel, cap, kw // LANES, tile), o...  3.51 us
    pallas_call x4, Pallas kernels, cut(): pl.pallas_call(functools.partial(cut_kernel, cuts), out_shape=[jax.ShapeD...  3.46 us
    pallas_call x1, Pallas kernels, residue(): pl.pallas_call(functools.partial(residue_kernel, order, tile), out_shape=...  2.39 us
    unnamed x14, local copies, waits for them, and re-layouts  2.3 us
    pallas_call x3, Pallas kernels, project(): pl.pallas_call(functools.partial(project_kernel, n), out_shape=[jax.Shape...  1.59 us
  transfers between devices with their start and end apart: 17, of which 12 were waited for; matrix products, arithmetic and copies ran while one was open for 0% of the time, Pallas kernels for 12%

profile of v5, /device:TPU:1, one launch (start us, length us, event | category | flops | bytes accessed | tf_op | source)
XLA Modules:
  0.0 60.7 jit_solution(15138859265955497471)
XLA Ops:
  0.6 2.0 %cut.4 = (bf16[128,2048]{1,0:T(8,128)(2,1)}, f32[8,128]{1,0:T(8,128)}) custom-call(bf16[128,8192]{1,0:T(8,128)(2,1)} %bitcast.7), custom_call_target="tpu_custom_call" | custom-call | flops 1000 | bytes 1000 | tf_op jit(solution)/shard_map/cut/pallas_call | solution.py:44
  2.7 3.1 %collective-permute-start = (bf16[128,2048]{1,0:T(8,128)(2,1)}, bf16[128,2048]{1,0:T(8,128)(2,1)S(1)}, u32[]{:S(2)}, u32[]{:S(2)}) collective-permute-start(bf16[128,2048]{1,0:T(8,128)(2,1)} %get-tuple-element.36), channel_id=1, source_target_pairs={{0,3},{1,2},{2,1},{3,0},{4,7},{5,6},{6,5},{7,4},{8,11},{9,10},{10,... | collective-permute-start | bytes 1572872 | tf_op jit(solution)/shard_map/ppermute | solution.py:25
  5.7 0.7 %copy-done.6 = f32[8,128]{1,0:T(8,128)S(1)} copy-done((f32[8,128]{1,0:T(8,128)S(1)}, f32[8,128]{1,0:T(8,128)}, u32[]{:S(2)}) %copy-start.6) | copy-done | bytes 4120
  6.4 0.8 %cut.5 = (bf16[64,2048]{1,0:T(8,128)(2,1)}, bf16[64,2048]{1,0:T(8,128)(2,1)S(1)}, f32[8,128]{1,0:T(8,128)S(1)}) custom-call(bf16[128,8192]{1,0:T(8,128)(2,1)S(1)} %bitcast.8, f32[8,128]{1,0:T(8,128)S(1)} %copy-done.6), custom_call_target="tpu_custom_call" | custom-call | flops 1000 | bytes 1000 | tf_op jit(solution)/shard_map/cut/pallas_call | solution.py:44
  8.3 1.6 %copy-done.2 = bf16[1,2048,512]{2,1,0:T(8,128)(2,1)S(1)} copy-done((bf16[1,2048,512]{2,1,0:T(8,128)(2,1)S(1)}, bf16[1,2048,512]{2,1,0:T(8,128)(2,1)}, u32[]{:S(2)}) %copy-start.2) | copy-done | bytes 2097176
  9.9 1.0 %early.1 = (f32[128,128]{1,0:T(8,128)S(1)}, bf16[2048,512]{1,0:T(8,128)(2,1)S(1)}, f32[8,128]{1,0:T(8,128)S(1)}) custom-call(s32[128,1]{1,0:T(8,128)S(1)} %copy.8.slots.refs_1_.refs_2_.refs_7_, s32[1,128]{1,0:T(1,128)S(1)} %bitcast.18, s32[1,1]{1,0:T(1,128)S(6)} %copy.12.count.refs_2_.refs_3_, bf16[2048,512]{1,0:T(8,128)(2,1)S(1)} %bitcast.14, ...), custom_call_target="tpu_custom_call" | custom-call | flops 1000 | bytes 1000 | tf_op jit(solution)/shard_map/early/pallas_call | solution.py:140
  11.0 1.5 %collective-permute-start.5 = (bf16[64,2048]{1,0:T(8,128)(2,1)S(1)}, bf16[64,2048]{1,0:T(8,128)(2,1)S(1)}, u32[]{:S(2)}, u32[]{:S(2)}) collective-permute-start(bf16[64,2048]{1,0:T(8,128)(2,1)S(1)} %get-tuple-element.44), channel_id=1, source_target_pairs={{0,1},{1,0},{2,3},{3,2},{4,5},{5,4},{6,7},{7,6},{8,9},{9,8},{10,11... | collective-permute-start | bytes 786440 | tf_op jit(solution)/shard_map/ppermute | solution.py:25
  12.5 1.2 %collective-permute-start.6 = (bf16[64,2048]{1,0:T(8,128)(2,1)S(1)}, bf16[64,2048]{1,0:T(8,128)(2,1)S(1)}, u32[]{:S(2)}, u32[]{:S(2)}) collective-permute-start(bf16[64,2048]{1,0:T(8,128)(2,1)S(1)} %get-tuple-element.45), channel_id=1, source_target_pairs={{0,2},{1,3},{2,0},{3,1},{4,6},{5,7},{6,4},{7,5},{8,10},{9,11},{10,... | collective-permute-start | bytes 786440 | tf_op jit(solution)/shard_map/ppermute | solution.py:25
  14.4 3.2 %collective-permute-done.refs_1_ = bf16[128,2048]{1,0:T(8,128)(2,1)S(1)} collective-permute-done((bf16[128,2048]{1,0:T(8,128)(2,1)}, bf16[128,2048]{1,0:T(8,128)(2,1)S(1)}, u32[]{:S(2)}, u32[]{:S(2)}) %collective-permute-start) | collective-permute-done | bytes 524320 | tf_op jit(solution)/shard_map/ppermute | solution.py:25
  17.6 0.7 %project.3 = (f32[128,512]{1,0:T(8,128)S(1)}, bf16[128,512]{1,0:T(8,128)(2,1)S(1)}, bf16[256,2048]{1,0:T(8,128)(2,1)S(1)}) custom-call(bf16[128,2048]{1,0:T(8,128)(2,1)S(1)} %get-tuple-element.35.refs_0_, bf16[128,2048]{1,0:T(8,128)(2,1)S(1)} %collective-permute-done.refs_1_, bf16[2048,512]{1,0:T(8,128)(2,1)S(1)} %bitcast.11), custom_call_target="tpu_custom_call" | custom-call | flops 1000 | bytes 1000 | tf_op jit(solution)/shard_map/project/pallas_call | solution.py:73
  18.3 2.1 %collective-permute-start.1 = (bf16[128,512]{1,0:T(8,128)(2,1)S(1)}, bf16[128,512]{1,0:T(8,128)(2,1)S(1)}, u32[]{:S(2)}, u32[]{:S(2)}) collective-permute-start(bf16[128,512]{1,0:T(8,128)(2,1)S(1)} %get-tuple-element.38), channel_id=1, source_target_pairs={{0,3},{1,2},{2,1},{3,0},{4,7},{5,6},{6,5},{7,4},{8,11},{9,10},{10,... | collective-permute-start | bytes 393224 | tf_op jit(solution)/shard_map/ppermute | solution.py:25
  21.0 2.2 %collective-permute-done.2.refs_0_ = bf16[64,2048]{1,0:T(8,128)(2,1)S(1)} collective-permute-done((bf16[64,2048]{1,0:T(8,128)(2,1)}, bf16[64,2048]{1,0:T(8,128)(2,1)S(1)}, u32[]{:S(2)}, u32[]{:S(2)}) %collective-permute-start.2) | collective-permute-done | bytes 262176 | tf_op jit(solution)/shard_map/ppermute | solution.py:25
  23.2 0.8 %collective-permute-done.3.refs_1_ = bf16[64,2048]{1,0:T(8,128)(2,1)S(1)} collective-permute-done((bf16[64,2048]{1,0:T(8,128)(2,1)S(1)}, bf16[64,2048]{1,0:T(8,128)(2,1)S(1)}, u32[]{:S(2)}, u32[]{:S(2)}) %collective-permute-start.3) | collective-permute-done | bytes 262176 | tf_op jit(solution)/shard_map/ppermute | solution.py:25
  24.4 1.5 %collective-permute-start.4 = (bf16[64,512]{1,0:T(8,128)(2,1)S(1)}, bf16[64,512]{1,0:T(8,128)(2,1)S(1)}, u32[]{:S(2)}, u32[]{:S(2)}) collective-permute-start(bf16[64,512]{1,0:T(8,128)(2,1)S(1)} %get-tuple-element.43), channel_id=1, source_target_pairs={{0,1},{1,0},{2,3},{3,2},{4,5},{5,4},{6,7},{7,6},{8,9},{9,8},{10,11... | collective-permute-start | bytes 196616 | tf_op jit(solution)/shard_map/ppermute | solution.py:25
  25.9 1.2 %collective-permute-start.8 = (bf16[64,512]{1,0:T(8,128)(2,1)S(1)}, bf16[64,512]{1,0:T(8,128)(2,1)S(1)}, u32[]{:S(2)}, u32[]{:S(2)}) collective-permute-start(bf16[64,512]{1,0:T(8,128)(2,1)S(1)} %get-tuple-element.46.refs_3_), channel_id=1, source_target_pairs={{0,2},{1,3},{2,0},{3,1},{4,6},{5,7},{6,4},{7,5},{8,10},{9,11},{10,... | collective-permute-start | bytes 196616 | tf_op jit(solution)/shard_map/ppermute | solution.py:25
  27.1 1.7 %collective-permute-done.5.refs_0_ = bf16[64,2048]{1,0:T(8,128)(2,1)S(1)} collective-permute-done((bf16[64,2048]{1,0:T(8,128)(2,1)S(1)}, bf16[64,2048]{1,0:T(8,128)(2,1)S(1)}, u32[]{:S(2)}, u32[]{:S(2)}) %collective-permute-start.5) | collective-permute-done | bytes 262176 | tf_op jit(solution)/shard_map/ppermute | solution.py:25
  28.8 1.4 %collective-permute-done.6.refs_1_ = bf16[64,2048]{1,0:T(8,128)(2,1)S(1)} collective-permute-done((bf16[64,2048]{1,0:T(8,128)(2,1)S(1)}, bf16[64,2048]{1,0:T(8,128)(2,1)S(1)}, u32[]{:S(2)}, u32[]{:S(2)}) %collective-permute-start.6) | collective-permute-done | bytes 262176 | tf_op jit(solution)/shard_map/ppermute | solution.py:25
  30.7 1.8 %collective-permute-start.7 = (bf16[64,512]{1,0:T(8,128)(2,1)S(1)}, bf16[64,512]{1,0:T(8,128)(2,1)S(1)}, u32[]{:S(2)}, u32[]{:S(2)}) collective-permute-start(bf16[64,512]{1,0:T(8,128)(2,1)S(1)} %get-tuple-element.47.refs_4_), channel_id=1, source_target_pairs={{0,1},{1,0},{2,3},{3,2},{4,5},{5,4},{6,7},{7,6},{8,9},{9,8},{10,11... | collective-permute-start | bytes 196616 | tf_op jit(solution)/shard_map/ppermute | solution.py:25
  32.5 1.2 %collective-permute-start.9 = (bf16[64,512]{1,0:T(8,128)(2,1)S(1)}, bf16[64,512]{1,0:T(8,128)(2,1)S(1)}, u32[]{:S(2)}, u32[]{:S(2)}) collective-permute-start(bf16[64,512]{1,0:T(8,128)(2,1)S(1)} %get-tuple-element.48), channel_id=1, source_target_pairs={{0,2},{1,3},{2,0},{3,1},{4,6},{5,7},{6,4},{7,5},{8,10},{9,11},{10,... | collective-permute-start | bytes 196616 | tf_op jit(solution)/shard_map/ppermute | solution.py:25
  34.6 1.3 %collective-permute-done.9.refs_6_ = bf16[64,512]{1,0:T(8,128)(2,1)S(1)} collective-permute-done((bf16[64,512]{1,0:T(8,128)(2,1)S(1)}, bf16[64,512]{1,0:T(8,128)(2,1)S(1)}, u32[]{:S(2)}, u32[]{:S(2)}) %collective-permute-start.9) | collective-permute-done | bytes 65568 | tf_op jit(solution)/shard_map/ppermute | solution.py:25
  36.0 1.0 %collective-permute-start.10 = (bf16[128,512]{1,0:T(8,128)(2,1)S(1)}, bf16[128,512]{1,0:T(8,128)(2,1)S(1)}, u32[]{:S(2)}, u32[]{:S(2)}) collective-permute-start(bf16[128,512]{1,0:T(8,128)(2,1)S(1)} %slope.1.refs_0_), channel_id=1, source_target_pairs={{0,3},{1,2},{2,1},{3,0},{4,7},{5,6},{6,5},{7,4},{8,11},{9,10},{10,... | collective-permute-start | bytes 393224 | tf_op jit(solution)/shard_map/ppermute | solution.py:25
  37.0 1.5 %collective-permute-start.11 = (bf16[128,512]{1,0:T(8,128)(2,1)S(1)}, bf16[128,512]{1,0:T(8,128)(2,1)S(1)}, u32[]{:S(2)}, u32[]{:S(2)}) collective-permute-start(bf16[128,512]{1,0:T(8,128)(2,1)S(1)} %slope.1.refs_0_), channel_id=1, source_target_pairs={{0,1},{1,0},{2,3},{3,2},{4,5},{5,4},{6,7},{7,6},{8,9},{9,8},{10,11... | collective-permute-start | bytes 393224 | tf_op jit(solution)/shard_map/ppermute | solution.py:25
  38.7 2.1 %collective-permute-done.10.refs_1_ = bf16[128,512]{1,0:T(8,128)(2,1)S(1)} collective-permute-done((bf16[128,512]{1,0:T(8,128)(2,1)S(1)}, bf16[128,512]{1,0:T(8,128)(2,1)S(1)}, u32[]{:S(2)}, u32[]{:S(2)}) %collective-permute-start.10) | collective-permute-done | bytes 131104 | tf_op jit(solution)/shard_map/ppermute | solution.py:25
  40.8 2.1 %collective-permute-done.11.refs_2_ = bf16[128,512]{1,0:T(8,128)(2,1)S(1)} collective-permute-done((bf16[128,512]{1,0:T(8,128)(2,1)S(1)}, bf16[128,512]{1,0:T(8,128)(2,1)S(1)}, u32[]{:S(2)}, u32[]{:S(2)}) %collective-permute-start.11) | collective-permute-done | bytes 131104 | tf_op jit(solution)/shard_map/ppermute | solution.py:25
  42.9 1.1 %collective-permute-done.12.refs_3_ = bf16[128,512]{1,0:T(8,128)(2,1)S(1)} collective-permute-done((bf16[128,512]{1,0:T(8,128)(2,1)S(1)}, bf16[128,512]{1,0:T(8,128)(2,1)S(1)}, u32[]{:S(2)}, u32[]{:S(2)}) %collective-permute-start.12) | collective-permute-done | bytes 131104 | tf_op jit(solution)/shard_map/ppermute | solution.py:25
  44.2 1.4 %collective-permute-start.13 = (bf16[144,128]{1,0:T(8,128)(2,1)S(1)}, bf16[144,128]{1,0:T(8,128)(2,1)S(1)}, u32[]{:S(2)}, u32[]{:S(2)}) collective-permute-start(bf16[144,128]{1,0:T(8,128)(2,1)S(1)} %kept.1.refs_0_), channel_id=1, source_target_pairs={{0,8},{4,12},{8,0},{12,4},{16,24},{20,28},{24,16},{28,20},{1,9},{5... | collective-permute-start | bytes 110600 | tf_op jit(solution)/shard_map/ppermute | solution.py:25
  45.6 2.3 %collective-permute-start.14 = (bf16[144,128]{1,0:T(8,128)(2,1)S(1)}, bf16[144,128]{1,0:T(8,128)(2,1)S(1)}, u32[]{:S(2)}, u32[]{:S(2)}) collective-permute-start(bf16[144,128]{1,0:T(8,128)(2,1)S(1)} %kept.1.refs_0_), channel_id=1, source_target_pairs={{0,16},{4,20},{8,24},{12,28},{16,0},{20,4},{24,8},{28,12},{1,17},{... | collective-permute-start | bytes 110600 | tf_op jit(solution)/shard_map/ppermute | solution.py:25
  47.9 2.4 %residue.1 = (bf16[2048,512]{1,0:T(8,128)(2,1)}, f32[8,128]{1,0:T(8,128)S(1)}) custom-call(bf16[128,512]{1,0:T(8,128)(2,1)S(1)} %slope.1.refs_0_, bf16[128,512]{1,0:T(8,128)(2,1)S(1)} %collective-permute-done.10.refs_1_, bf16[128,512]{1,0:T(8,128)(2,1)S(1)} %collective-permute-done.11.refs_2_, bf16[128,512]{1,0:T(8,128)(2,1)S(1)} %collective-permute-done.12.refs_3_, ...), custom_call_target="tpu_custom_call" | custom-call | flops 1000 | bytes 1000 | tf_op jit(solution)/shard_map/residue/pallas_call | solution.py:259
  50.3 2.2 %collective-permute-done.15.refs_3_ = bf16[144,128]{1,0:T(8,128)(2,1)S(1)} collective-permute-done((bf16[144,128]{1,0:T(8,128)(2,1)S(1)}, bf16[144,128]{1,0:T(8,128)(2,1)S(1)}, u32[]{:S(2)}, u32[]{:S(2)}) %collective-permute-start.15) | collective-permute-done | bytes 36896 | tf_op jit(solution)/shard_map/ppermute | solution.py:25
  52.5 3.7 %collective-permute-start.16 = (bf16[576,128]{1,0:T(8,128)(2,1)S(1)}, bf16[576,128]{1,0:T(8,128)(2,1)S(1)}, u32[]{:S(2)}, u32[]{:S(2)}) collective-permute-start(bf16[576,128]{1,0:T(8,128)(2,1)S(1)} %join.1.refs_0_), channel_id=1, source_target_pairs={{0,4},{4,0},{8,12},{12,8},{16,20},{20,16},{24,28},{28,24},{1,5},{5... | collective-permute-start | bytes 442376 | tf_op jit(solution)/shard_map/ppermute | solution.py:25
  56.2 1.0 %collective-permute-done.16.refs_1_ = bf16[576,128]{1,0:T(8,128)(2,1)S(1)} collective-permute-done((bf16[576,128]{1,0:T(8,128)(2,1)S(1)}, bf16[576,128]{1,0:T(8,128)(2,1)S(1)}, u32[]{:S(2)}, u32[]{:S(2)}) %collective-permute-start.16) | collective-permute-done | bytes 147488 | tf_op jit(solution)/shard_map/ppermute | solution.py:25
  57.2 3.5 %outer.1 = f32[2048,512]{1,0:T(8,128)} custom-call(bf16[576,128]{1,0:T(8,128)(2,1)S(1)} %join.1.refs_0_, bf16[576,128]{1,0:T(8,128)(2,1)S(1)} %collective-permute-done.16.refs_1_), custom_call_target="tpu_custom_call" | custom-call | flops 1000 | bytes 1000 | tf_op jit(solution)/shard_map/outer/pallas_call | solution.py:329
  (32 shorter events, 4.1 us)
Async XLA Ops:
  0.6 5.1 %copy-start = (bf16[1,128,8192]{2,1,0:T(8,128)(2,1)S(1)}, bf16[1,128,8192]{2,1,0:T(8,128)(2,1)}, u32[]{:S(2)}) copy-start(bf16[1,128,8192]{2,1,0:T(8,128)(2,1)} %param.6) | copy-start | bytes 6291460
  0.6 6.9 %copy-start.5 = (s32[1,1,128]{2,1,0:T(1,128)S(1)}, s32[1,1,128]{2,1,0:T(1,128)}, u32[]{:S(2)}) copy-start(s32[1,1,128]{2,1,0:T(1,128)} %param.11) | copy-start | bytes 1540
  2.7 15.0 %collective-permute-start = (bf16[128,2048]{1,0:T(8,128)(2,1)}, bf16[128,2048]{1,0:T(8,128)(2,1)S(1)}, u32[]{:S(2)}, u32[]{:S(2)}) collective-permute-start(bf16[128,2048]{1,0:T(8,128)(2,1)} %get-tuple-element.36), channel_id=1, source_target_pairs={{0,3},{1,2},{2,1},{3,0},{4,7},{5,6},{6,5},{7,4},{8,11},{9,10},{10,... | collective-permute-start | bytes 1572872 | tf_op jit(solution)/shard_map/ppermute | solution.py:25
  5.7 0.7 %copy-start.6 = (f32[8,128]{1,0:T(8,128)S(1)}, f32[8,128]{1,0:T(8,128)}, u32[]{:S(2)}) copy-start(f32[8,128]{1,0:T(8,128)} %get-tuple-element.31.refs_0_) | copy-start | bytes 12292
  7.2 16.0 %collective-permute-start.2 = (bf16[64,2048]{1,0:T(8,128)(2,1)}, bf16[64,2048]{1,0:T(8,128)(2,1)S(1)}, u32[]{:S(2)}, u32[]{:S(2)}) collective-permute-start(bf16[64,2048]{1,0:T(8,128)(2,1)} %get-tuple-element.39), channel_id=1, source_target_pairs={{0,1},{1,0},{2,3},{3,2},{4,5},{5,4},{6,7},{7,6},{8,9},{9,8},{10,11... | collective-permute-start | bytes 786440 | tf_op jit(solution)/shard_map/ppermute | solution.py:25
  7.5 16.4 %collective-permute-start.3 = (bf16[64,2048]{1,0:T(8,128)(2,1)S(1)}, bf16[64,2048]{1,0:T(8,128)(2,1)S(1)}, u32[]{:S(2)}, u32[]{:S(2)}) collective-permute-start(bf16[64,2048]{1,0:T(8,128)(2,1)S(1)} %get-tuple-element.40), channel_id=1, source_target_pairs={{0,2},{1,3},{2,0},{3,1},{4,6},{5,7},{6,4},{7,5},{8,10},{9,11},{10,... | collective-permute-start | bytes 786440 | tf_op jit(solution)/shard_map/ppermute | solution.py:25
  8.3 1.6 %copy-start.2 = (bf16[1,2048,512]{2,1,0:T(8,128)(2,1)S(1)}, bf16[1,2048,512]{2,1,0:T(8,128)(2,1)}, u32[]{:S(2)}) copy-start(bf16[1,2048,512]{2,1,0:T(8,128)(2,1)} %param.9) | copy-start | bytes 6291460
  11.0 6.7 %copy-start.1 = (bf16[1,2048,512]{2,1,0:T(8,128)(2,1)S(1)}, bf16[1,2048,512]{2,1,0:T(8,128)(2,1)}, u32[]{:S(2)}) copy-start(bf16[1,2048,512]{2,1,0:T(8,128)(2,1)} %param.8) | copy-start | bytes 6291460
  11.0 17.7 %collective-permute-start.5 = (bf16[64,2048]{1,0:T(8,128)(2,1)S(1)}, bf16[64,2048]{1,0:T(8,128)(2,1)S(1)}, u32[]{:S(2)}, u32[]{:S(2)}) collective-permute-start(bf16[64,2048]{1,0:T(8,128)(2,1)S(1)} %get-tuple-element.44), channel_id=1, source_target_pairs={{0,1},{1,0},{2,3},{3,2},{4,5},{5,4},{6,7},{7,6},{8,9},{9,8},{10,11... | collective-permute-start | bytes 786440 | tf_op jit(solution)/shard_map/ppermute | solution.py:25
  12.5 17.7 %collective-permute-start.6 = (bf16[64,2048]{1,0:T(8,128)(2,1)S(1)}, bf16[64,2048]{1,0:T(8,128)(2,1)S(1)}, u32[]{:S(2)}, u32[]{:S(2)}) collective-permute-start(bf16[64,2048]{1,0:T(8,128)(2,1)S(1)} %get-tuple-element.45), channel_id=1, source_target_pairs={{0,2},{1,3},{2,0},{3,1},{4,6},{5,7},{6,4},{7,5},{8,10},{9,11},{10,... | collective-permute-start | bytes 786440 | tf_op jit(solution)/shard_map/ppermute | solution.py:25
  18.3 17.6 %collective-permute-start.1 = (bf16[128,512]{1,0:T(8,128)(2,1)S(1)}, bf16[128,512]{1,0:T(8,128)(2,1)S(1)}, u32[]{:S(2)}, u32[]{:S(2)}) collective-permute-start(bf16[128,512]{1,0:T(8,128)(2,1)S(1)} %get-tuple-element.38), channel_id=1, source_target_pairs={{0,3},{1,2},{2,1},{3,0},{4,7},{5,6},{6,5},{7,4},{8,11},{9,10},{10,... | collective-permute-start | bytes 393224 | tf_op jit(solution)/shard_map/ppermute | solution.py:25
  24.4 11.5 %copy-start.4 = (bf16[1,128,512]{2,1,0:T(8,128)(2,1)S(1)}, bf16[1,128,512]{2,1,0:T(8,128)(2,1)}, u32[]{:S(2)}) copy-start(bf16[1,128,512]{2,1,0:T(8,128)(2,1)} %param.7) | copy-start | bytes 393220
  24.4 9.9 %collective-permute-start.4 = (bf16[64,512]{1,0:T(8,128)(2,1)S(1)}, bf16[64,512]{1,0:T(8,128)(2,1)S(1)}, u32[]{:S(2)}, u32[]{:S(2)}) collective-permute-start(bf16[64,512]{1,0:T(8,128)(2,1)S(1)} %get-tuple-element.43), channel_id=1, source_target_pairs={{0,1},{1,0},{2,3},{3,2},{4,5},{5,4},{6,7},{7,6},{8,9},{9,8},{10,11... | collective-permute-start | bytes 196616 | tf_op jit(solution)/shard_map/ppermute | solution.py:25
  25.9 8.7 %collective-permute-start.8 = (bf16[64,512]{1,0:T(8,128)(2,1)S(1)}, bf16[64,512]{1,0:T(8,128)(2,1)S(1)}, u32[]{:S(2)}, u32[]{:S(2)}) collective-permute-start(bf16[64,512]{1,0:T(8,128)(2,1)S(1)} %get-tuple-element.46.refs_3_), channel_id=1, source_target_pairs={{0,2},{1,3},{2,0},{3,1},{4,6},{5,7},{6,4},{7,5},{8,10},{9,11},{10,... | collective-permute-start | bytes 196616 | tf_op jit(solution)/shard_map/ppermute | solution.py:25
  30.7 17.2 %copy-start.3 = (bf16[1,2048,512]{2,1,0:T(8,128)(2,1)S(1)}, bf16[1,2048,512]{2,1,0:T(8,128)(2,1)}, u32[]{:S(2)}) copy-start(bf16[1,2048,512]{2,1,0:T(8,128)(2,1)} %param.9) | copy-start | bytes 6291460
  30.7 3.9 %collective-permute-start.7 = (bf16[64,512]{1,0:T(8,128)(2,1)S(1)}, bf16[64,512]{1,0:T(8,128)(2,1)S(1)}, u32[]{:S(2)}, u32[]{:S(2)}) collective-permute-start(bf16[64,512]{1,0:T(8,128)(2,1)S(1)} %get-tuple-element.47.refs_4_), channel_id=1, source_target_pairs={{0,1},{1,0},{2,3},{3,2},{4,5},{5,4},{6,7},{7,6},{8,9},{9,8},{10,11... | collective-permute-start | bytes 196616 | tf_op jit(solution)/shard_map/ppermute | solution.py:25
  32.5 3.4 %collective-permute-start.9 = (bf16[64,512]{1,0:T(8,128)(2,1)S(1)}, bf16[64,512]{1,0:T(8,128)(2,1)S(1)}, u32[]{:S(2)}, u32[]{:S(2)}) collective-permute-start(bf16[64,512]{1,0:T(8,128)(2,1)S(1)} %get-tuple-element.48), channel_id=1, source_target_pairs={{0,2},{1,3},{2,0},{3,1},{4,6},{5,7},{6,4},{7,5},{8,10},{9,11},{10,... | collective-permute-start | bytes 196616 | tf_op jit(solution)/shard_map/ppermute | solution.py:25
  36.0 4.8 %collective-permute-start.10 = (bf16[128,512]{1,0:T(8,128)(2,1)S(1)}, bf16[128,512]{1,0:T(8,128)(2,1)S(1)}, u32[]{:S(2)}, u32[]{:S(2)}) collective-permute-start(bf16[128,512]{1,0:T(8,128)(2,1)S(1)} %slope.1.refs_0_), channel_id=1, source_target_pairs={{0,3},{1,2},{2,1},{3,0},{4,7},{5,6},{6,5},{7,4},{8,11},{9,10},{10,... | collective-permute-start | bytes 393224 | tf_op jit(solution)/shard_map/ppermute | solution.py:25
  37.0 5.9 %collective-permute-start.11 = (bf16[128,512]{1,0:T(8,128)(2,1)S(1)}, bf16[128,512]{1,0:T(8,128)(2,1)S(1)}, u32[]{:S(2)}, u32[]{:S(2)}) collective-permute-start(bf16[128,512]{1,0:T(8,128)(2,1)S(1)} %slope.1.refs_0_), channel_id=1, source_target_pairs={{0,1},{1,0},{2,3},{3,2},{4,5},{5,4},{6,7},{7,6},{8,9},{9,8},{10,11... | collective-permute-start | bytes 393224 | tf_op jit(solution)/shard_map/ppermute | solution.py:25
  38.5 5.5 %collective-permute-start.12 = (bf16[128,512]{1,0:T(8,128)(2,1)S(1)}, bf16[128,512]{1,0:T(8,128)(2,1)S(1)}, u32[]{:S(2)}, u32[]{:S(2)}) collective-permute-start(bf16[128,512]{1,0:T(8,128)(2,1)S(1)} %slope.1.refs_0_), channel_id=1, source_target_pairs={{0,2},{1,3},{2,0},{3,1},{4,6},{5,7},{6,4},{7,5},{8,10},{9,11},{10,... | collective-permute-start | bytes 393224 | tf_op jit(solution)/shard_map/ppermute | solution.py:25
  44.2 6.1 %collective-permute-start.13 = (bf16[144,128]{1,0:T(8,128)(2,1)S(1)}, bf16[144,128]{1,0:T(8,128)(2,1)S(1)}, u32[]{:S(2)}, u32[]{:S(2)}) collective-permute-start(bf16[144,128]{1,0:T(8,128)(2,1)S(1)} %kept.1.refs_0_), channel_id=1, source_target_pairs={{0,8},{4,12},{8,0},{12,4},{16,24},{20,28},{24,16},{28,20},{1,9},{5... | collective-permute-start | bytes 110600 | tf_op jit(solution)/shard_map/ppermute | solution.py:25
  45.6 4.7 %collective-permute-start.14 = (bf16[144,128]{1,0:T(8,128)(2,1)S(1)}, bf16[144,128]{1,0:T(8,128)(2,1)S(1)}, u32[]{:S(2)}, u32[]{:S(2)}) collective-permute-start(bf16[144,128]{1,0:T(8,128)(2,1)S(1)} %kept.1.refs_0_), channel_id=1, source_target_pairs={{0,16},{4,20},{8,24},{12,28},{16,0},{20,4},{24,8},{28,12},{1,17},{... | collective-permute-start | bytes 110600 | tf_op jit(solution)/shard_map/ppermute | solution.py:25
  47.9 4.6 %collective-permute-start.15 = (bf16[144,128]{1,0:T(8,128)(2,1)S(1)}, bf16[144,128]{1,0:T(8,128)(2,1)S(1)}, u32[]{:S(2)}, u32[]{:S(2)}) collective-permute-start(bf16[144,128]{1,0:T(8,128)(2,1)S(1)} %kept.1.refs_0_), channel_id=1, source_target_pairs={{0,24},{4,28},{8,16},{12,20},{16,8},{20,12},{24,0},{28,4},{1,25},{... | collective-permute-start | bytes 110600 | tf_op jit(solution)/shard_map/ppermute | solution.py:25
  52.5 4.7 %collective-permute-start.16 = (bf16[576,128]{1,0:T(8,128)(2,1)S(1)}, bf16[576,128]{1,0:T(8,128)(2,1)S(1)}, u32[]{:S(2)}, u32[]{:S(2)}) collective-permute-start(bf16[576,128]{1,0:T(8,128)(2,1)S(1)} %join.1.refs_0_), channel_id=1, source_target_pairs={{0,4},{4,0},{8,12},{12,8},{16,20},{20,16},{24,28},{28,24},{1,5},{5... | collective-permute-start | bytes 442376 | tf_op jit(solution)/shard_map/ppermute | solution.py:25

commit v6 on v5

--- a/solution.py
+++ b/solution.py
@@ -11,7 +11,6 @@
 ANY = pl.BlockSpec(memory_space=pl.ANY)
 BRIEF = pl.CostEstimate(flops=1000, bytes_accessed=1000, transcendentals=0)
 VMEM = pl.BlockSpec(memory_space=pltpu.VMEM)
-HBM = pl.BlockSpec(memory_space=pltpu.HBM)
 SMEM = pl.BlockSpec(memory_space=pltpu.SMEM)
 MIB = 1024 * 1024
 TOKEN = jax.ShapeDtypeStruct((8, LANES), jnp.float32)
@@ -45,7 +44,8 @@
         functools.partial(cut_kernel, cuts),
         out_shape=[jax.ShapeDtypeStruct((rows, depth), tokens.dtype) for _, _, rows in cuts]
         + [TOKEN],
-        in_specs=[HBM] + [ANY] * len(after),
+        in_specs=[ANY] * (1 + len(after)),
+        out_specs=[ANY] * len(cuts) + [VMEM],
         scratch_shapes=[pltpu.SemaphoreType.DMA((len(cuts),))],
         compiler_params=params(mib),
         cost_estimate=BRIEF,
@@ -294,52 +294,68 @@
     )(*messages, after)
 
 
-def outer_kernel(cap, per_row, tile, *refs):
-    groups, (out, wide, lines, held, sems) = refs[:-5], refs[-5:]
-    n = lines.shape[1] // cap
+def spread(group, wide, lines, cap, per_row):
     size = cap + 16
-    k = 0
-    for group in groups:
-        for start in range(0, group.shape[0], size):
-            tail = group[start + cap : start + size, :].astype(jnp.float32)
-            number = (tail[0:1, :] * LANES + tail[1:2, :]).astype(jnp.int32)
-            lines[:, k * cap : (k + 1) * cap] = jnp.broadcast_to(number // per_row, (8, cap))
-            column = jnp.broadcast_to((number % per_row).astype(jnp.float32), (LANES, cap)).T
-            value = group[start : start + cap, :].astype(jnp.float32)
-            for c in range(per_row):
-                wide[k * cap : (k + 1) * cap, c * LANES : (c + 1) * LANES] = jnp.where(
-                    column == c, value, 0.0
-                ).astype(jnp.bfloat16)
-            k += 1
+    for k in range(group.shape[0] // size):
+        start = k * size
+        tail = group[start + cap : start + size, :].astype(jnp.float32)
+        number = (tail[0:1, :] * LANES + tail[1:2, :]).astype(jnp.int32)
+        lines[:, k * cap : (k + 1) * cap] = jnp.broadcast_to(number // per_row, (8, cap))
+        column = jnp.broadcast_to((number % per_row).astype(jnp.float32), (LANES, cap)).T
+        value = group[start : start + cap, :].astype(jnp.float32)
+        for c in range(per_row):
+            wide[k * cap : (k + 1) * cap, c * LANES : (c + 1) * LANES] = jnp.where(
+                column == c, value, 0.0
+            ).astype(jnp.bfloat16)
+
+
+def place(lines, wide, t, tile):
+    line = lax.broadcasted_iota(jnp.int32, (tile, lines.shape[1]), 0) + t * tile
+    hot = (lines[0:1, :] == line).astype(jnp.float32).astype(jnp.bfloat16)
+    return jnp.dot(hot, wide[...], preferred_element_type=jnp.float32)
+
+
+def half_kernel(cap, per_row, tile, group, out, wide, lines):
+    spread(group, wide, lines, cap, per_row)
+    for t in range(out.shape[0] // tile):
+        out[t * tile : (t + 1) * tile, :] = place(lines, wide, t, tile)
+
+
+def outer_kernel(cap, per_row, tile, n, group, half, out, wide, lines, held, sems):
+    spread(group, wide, lines, cap, per_row)
     tiles = out.shape[0] // tile
-
     for t in range(tiles):
         rows = slice(t * tile, (t + 1) * tile)
-        line = lax.broadcasted_iota(jnp.int32, (tile, n * cap), 0) + t * tile
-        hot = (lines[0:1, :] == line).astype(jnp.float32).astype(jnp.bfloat16)
-        held[rows, :] = jnp.dot(hot, wide[...], preferred_element_type=jnp.float32) / n
+        held[rows, :] = (half[rows, :] + place(lines, wide, t, tile)) / n
         send_out(held, out, sems, t, tile).start()
     for t in range(tiles):
         send_out(held, out, sems, t, tile).wait()
 
 
 def outer(groups, cap, depth, kw):
-    n = sum(group.shape[0] for group in groups) // (cap + 16)
+    slots = groups[0].shape[0] // (cap + 16) * cap
+    n = 2 * slots // cap
     tile = min(depth, 512)
-    return pl.pallas_call(
-        functools.partial(outer_kernel, cap, kw // LANES, tile),
-        out_shape=jax.ShapeDtypeStruct((depth, kw), jnp.float32),
+    shape = jax.ShapeDtypeStruct((depth, kw), jnp.float32)
+    scratch = [pltpu.VMEM((slots, kw), jnp.bfloat16), pltpu.VMEM((8, slots), jnp.int32)]
+    half = pl.pallas_call(
+        functools.partial(half_kernel, cap, kw // LANES, tile),
+        out_shape=shape,
+        scratch_shapes=scratch,
+        compiler_params=params(24),
+        cost_estimate=BRIEF,
+        name="half",
+    )(groups[0])
+    return pl.pallas_call(
+        functools.partial(outer_kernel, cap, kw // LANES, tile, n),
+        out_shape=shape,
         out_specs=ANY,
-        scratch_shapes=[
-            pltpu.VMEM((n * cap, kw), jnp.bfloat16),
-            pltpu.VMEM((8, n * cap), jnp.int32),
-            pltpu.VMEM((depth, kw), jnp.float32),
-            pltpu.SemaphoreType.DMA((depth // tile,)),
-        ],
+        scratch_shapes=scratch
+        + [pltpu.VMEM((depth, kw), jnp.float32), pltpu.SemaphoreType.DMA((depth // tile,))],
         compiler_params=params(24),
         cost_estimate=BRIEF,
         name="outer",
-    )(*groups)
+    )(groups[1], half)
 
 
 def on_device(inputs, target, weights, feedback, counts, blocks):
@@ -347,7 +363,7 @@
     n_shard, n_rep = lax.axis_size("shard"), lax.axis_size("rep")
     tok_dev = tokens.shape[0]
     depth, kw = w.shape
-    early_rows = tok_dev // 2
+    early_rows = tok_dev * 3 // 4
     spans = [(0, early_rows), (early_rows, tok_dev)]
     per_row = kw // LANES
     slot_row = blocks[0]
@@ -364,6 +380,7 @@
         if low == 0:
             fbk, keep, token = early(slots, slot_row, counts, fb, token)
     near_in = [[swap(x, "shard", n_shard, d) for x, d in zip(out, near)] for out in near_out]
+
     own, _ = cut(tokens, depth, [(0, 0, tok_dev)], [token])
 
     brief, wide = jnp.bfloat16, jnp.float32
@@ -384,7 +401,7 @@
     order = [(k, 0, tok_dev) for k in range(1 + len(far))]
     order += [(k, low, high) for low, high in spans for k in range(1 + len(far), n_shard)]
     message = kept(slopes, order, [xg_far, xg_near], fbk, slots, slot_row)
-    same_core = [message] + [swap(message, "rep", n_rep, d) for d in range(2, n_rep, 2)]
+    same_core = [message] + [swap(message, "rep", n_rep, d) for d in range(n_rep - 2, 0, -2)]
     new_feedback, token = residue(slopes, order, [xt_far, xt_near], fb, keep)
     joined = join(same_core, token)
     groups = [joined, swap(joined, "rep", n_rep, 1)]

time: 61.2 us -> 76.2 us (1.25)
  Pallas kernels: 13.4 us -> 30.3 us
  waiting for transfers between devices: 19.4 us -> 17.2 us
    pallas_call x4, Pallas kernels: 3.46 us -> 19.2 us  [cut(): pl.pallas_call(functools.partial(cut_kernel, cuts), out_shape=[jax.ShapeD...]
    ppermute x17, waiting for transfers between devices: 19.4 us -> 17.2 us  [swap(): return lax.ppermute(x, axis, [(i, i ^ d) for i in range(n)])]
    pallas_call x1 -> x2, Pallas kernels: 3.51 us -> 4.07 us  [the longest x1 2.65 us: outer(): pl.pallas_call(functools.partial(outer_kernel, cap, kw // LANES, tile, n)...]
  transfers between devices with their start and end apart: 17 -> 17, of which waited for: 12 -> 9; matrix products, arithmetic and copies ran while one was open for 0% -> 0% of each run, Pallas kernels for 12% -> 13%
where the time goes in v6:
time: 76.2 us; the launch traced here: 76 us
  Pallas kernels  30.3 us (40%)
  starting transfers between devices  24.6 us (32%)
  waiting for transfers between devices  17.2 us (23%)
  local copies, waits for them, and re-layouts  2.41 us (3%)
  between operations  1.48 us (2%)
    ppermute x17, starting transfers between devices, swap(): return lax.ppermute(x, axis, [(i, i ^ d) for i in range(n)])  24.6 us
    pallas_call x4, Pallas kernels, cut(): pl.pallas_call(functools.partial(cut_kernel, cuts), out_shape=[jax.ShapeD...  19.2 us
    ppermute x17, waiting for transfers between devices, swap(): return lax.ppermute(x, axis, [(i, i ^ d) for i in range(n)])  17.2 us
    pallas_call x1, Pallas kernels, outer(): pl.pallas_call(functools.partial(outer_kernel, cap, kw // LANES, tile, n)...  2.65 us
    pallas_call x1, Pallas kernels, residue(): pl.pallas_call(functools.partial(residue_kernel, order, tile), out_shape=...  2.39 us
    unnamed x14, local copies, waits for them, and re-layouts  2.3 us
    pallas_call x3, Pallas kernels, project(): pl.pallas_call(functools.partial(project_kernel, n), out_shape=[jax.Shape...  1.75 us
  transfers between devices with their start and end apart: 17, of which 9 were waited for; matrix products, arithmetic and copies ran while one was open for 0% of the time, Pallas kernels for 13%

profile of v6, /device:TPU:1, one launch (start us, length us, event | category | flops | bytes accessed | tf_op | source)
XLA Modules:
  0.0 76.0 jit_solution(14295670841856850706)
XLA Ops:
  0.6 17.6 %cut.4 = (bf16[128,2048]{1,0:T(8,128)(2,1)}, f32[8,128]{1,0:T(8,128)}) custom-call(bf16[128,8192]{1,0:T(8,128)(2,1)} %bitcast.7), custom_call_target="tpu_custom_call" | custom-call | flops 1000 | bytes 1000 | tf_op jit(solution)/shard_map/cut/pallas_call | solution.py:43
  18.2 3.1 %collective-permute-start = (bf16[128,2048]{1,0:T(8,128)(2,1)}, bf16[128,2048]{1,0:T(8,128)(2,1)S(1)}, u32[]{:S(2)}, u32[]{:S(2)}) collective-permute-start(bf16[128,2048]{1,0:T(8,128)(2,1)} %get-tuple-element.36), channel_id=1, source_target_pairs={{0,3},{1,2},{2,1},{3,0},{4,7},{5,6},{6,5},{7,4},{8,11},{9,10},{10,... | collective-permute-start | bytes 1572872 | tf_op jit(solution)/shard_map/ppermute | solution.py:24
  21.3 0.7 copy-done.6
  22.0 0.9 %cut.5 = (bf16[96,2048]{1,0:T(8,128)(2,1)}, bf16[96,2048]{1,0:T(8,128)(2,1)}, f32[8,128]{1,0:T(8,128)S(1)}) custom-call(bf16[128,8192]{1,0:T(8,128)(2,1)S(1)} %bitcast.8, f32[8,128]{1,0:T(8,128)S(1)} %copy-done.6), custom_call_target="tpu_custom_call" | custom-call | flops 1000 | bytes 1000 | tf_op jit(solution)/shard_map/cut/pallas_call | solution.py:43
  24.0 1.6 %copy-done.2 = bf16[1,2048,512]{2,1,0:T(8,128)(2,1)S(1)} copy-done((bf16[1,2048,512]{2,1,0:T(8,128)(2,1)S(1)}, bf16[1,2048,512]{2,1,0:T(8,128)(2,1)}, u32[]{:S(2)}) %copy-start.2) | copy-done | bytes 2097176
  25.6 1.0 %early.1 = (f32[128,128]{1,0:T(8,128)S(1)}, bf16[2048,512]{1,0:T(8,128)(2,1)S(1)}, f32[8,128]{1,0:T(8,128)S(1)}) custom-call(s32[128,1]{1,0:T(8,128)S(1)} %copy.8.slots.refs_1_.refs_2_.refs_7_, s32[1,128]{1,0:T(1,128)S(1)} %bitcast.18, s32[1,1]{1,0:T(1,128)S(6)} %copy.12.count.refs_2_.refs_3_, bf16[2048,512]{1,0:T(8,128)(2,1)S(1)} %bitcast.14, ...), custom_call_target="tpu_custom_call" | custom-call | flops 1000 | bytes 1000 | tf_op jit(solution)/shard_map/early/pallas_call | solution.py:140
  26.8 1.5 %collective-permute-start.5 = (bf16[32,2048]{1,0:T(8,128)(2,1)S(1)}, bf16[32,2048]{1,0:T(8,128)(2,1)S(1)}, u32[]{:S(2)}, u32[]{:S(2)}) collective-permute-start(bf16[32,2048]{1,0:T(8,128)(2,1)S(1)} %get-tuple-element.44), channel_id=1, source_target_pairs={{0,1},{1,0},{2,3},{3,2},{4,5},{5,4},{6,7},{7,6},{8,9},{9,8},{10,11... | collective-permute-start | bytes 393224 | tf_op jit(solution)/shard_map/ppermute | solution.py:24
  28.3 1.2 %collective-permute-start.6 = (bf16[32,2048]{1,0:T(8,128)(2,1)S(1)}, bf16[32,2048]{1,0:T(8,128)(2,1)S(1)}, u32[]{:S(2)}, u32[]{:S(2)}) collective-permute-start(bf16[32,2048]{1,0:T(8,128)(2,1)S(1)} %get-tuple-element.45), channel_id=1, source_target_pairs={{0,2},{1,3},{2,0},{3,1},{4,6},{5,7},{6,4},{7,5},{8,10},{9,11},{10,... | collective-permute-start | bytes 393224 | tf_op jit(solution)/shard_map/ppermute | solution.py:24
  29.5 0.6 cut.7
  30.1 3.1 %collective-permute-done.refs_1_ = bf16[128,2048]{1,0:T(8,128)(2,1)S(1)} collective-permute-done((bf16[128,2048]{1,0:T(8,128)(2,1)}, bf16[128,2048]{1,0:T(8,128)(2,1)S(1)}, u32[]{:S(2)}, u32[]{:S(2)}) %collective-permute-start) | collective-permute-done | bytes 524320 | tf_op jit(solution)/shard_map/ppermute | solution.py:24
  33.2 0.7 project.3
  33.9 2.1 %collective-permute-start.1 = (bf16[128,512]{1,0:T(8,128)(2,1)S(1)}, bf16[128,512]{1,0:T(8,128)(2,1)S(1)}, u32[]{:S(2)}, u32[]{:S(2)}) collective-permute-start(bf16[128,512]{1,0:T(8,128)(2,1)S(1)} %get-tuple-element.38), channel_id=1, source_target_pairs={{0,3},{1,2},{2,1},{3,0},{4,7},{5,6},{6,5},{7,4},{8,11},{9,10},{10,... | collective-permute-start | bytes 393224 | tf_op jit(solution)/shard_map/ppermute | solution.py:24
  36.6 5.0 %collective-permute-done.2.refs_0_ = bf16[96,2048]{1,0:T(8,128)(2,1)S(1)} collective-permute-done((bf16[96,2048]{1,0:T(8,128)(2,1)}, bf16[96,2048]{1,0:T(8,128)(2,1)S(1)}, u32[]{:S(2)}, u32[]{:S(2)}) %collective-permute-start.2) | collective-permute-done | bytes 393248 | tf_op jit(solution)/shard_map/ppermute | solution.py:24
  41.6 0.8 %collective-permute-done.3.refs_1_ = bf16[96,2048]{1,0:T(8,128)(2,1)S(1)} collective-permute-done((bf16[96,2048]{1,0:T(8,128)(2,1)}, bf16[96,2048]{1,0:T(8,128)(2,1)S(1)}, u32[]{:S(2)}, u32[]{:S(2)}) %collective-permute-start.3) | collective-permute-done | bytes 393248 | tf_op jit(solution)/shard_map/ppermute | solution.py:24
  42.3 0.6 project.4
  42.9 1.5 %collective-permute-start.4 = (bf16[96,512]{1,0:T(8,128)(2,1)S(1)}, bf16[96,512]{1,0:T(8,128)(2,1)S(1)}, u32[]{:S(2)}, u32[]{:S(2)}) collective-permute-start(bf16[96,512]{1,0:T(8,128)(2,1)S(1)} %get-tuple-element.43), channel_id=1, source_target_pairs={{0,1},{1,0},{2,3},{3,2},{4,5},{5,4},{6,7},{7,6},{8,9},{9,8},{10,11... | collective-permute-start | bytes 294920 | tf_op jit(solution)/shard_map/ppermute | solution.py:24
  44.4 1.2 %collective-permute-start.8 = (bf16[96,512]{1,0:T(8,128)(2,1)S(1)}, bf16[96,512]{1,0:T(8,128)(2,1)S(1)}, u32[]{:S(2)}, u32[]{:S(2)}) collective-permute-start(bf16[96,512]{1,0:T(8,128)(2,1)S(1)} %get-tuple-element.46.refs_3_), channel_id=1, source_target_pairs={{0,2},{1,3},{2,0},{3,1},{4,6},{5,7},{6,4},{7,5},{8,10},{9,11},{10,... | collective-permute-start | bytes 294920 | tf_op jit(solution)/shard_map/ppermute | solution.py:24
  46.3 1.8 %collective-permute-start.9 = (bf16[32,512]{1,0:T(8,128)(2,1)S(1)}, bf16[32,512]{1,0:T(8,128)(2,1)S(1)}, u32[]{:S(2)}, u32[]{:S(2)}) collective-permute-start(bf16[32,512]{1,0:T(8,128)(2,1)S(1)} %get-tuple-element.48), channel_id=1, source_target_pairs={{0,2},{1,3},{2,0},{3,1},{4,6},{5,7},{6,4},{7,5},{8,10},{9,11},{10,... | collective-permute-start | bytes 98312 | tf_op jit(solution)/shard_map/ppermute | solution.py:24
  48.1 1.2 %collective-permute-start.7 = (bf16[32,512]{1,0:T(8,128)(2,1)S(1)}, bf16[32,512]{1,0:T(8,128)(2,1)S(1)}, u32[]{:S(2)}, u32[]{:S(2)}) collective-permute-start(bf16[32,512]{1,0:T(8,128)(2,1)S(1)} %get-tuple-element.47.refs_4_), channel_id=1, source_target_pairs={{0,1},{1,0},{2,3},{3,2},{4,5},{5,4},{6,7},{7,6},{8,9},{9,8},{10,11... | collective-permute-start | bytes 98312 | tf_op jit(solution)/shard_map/ppermute | solution.py:24
  49.3 0.9 %prepare.3 = (bf16[128,256]{1,0:T(8,128)(2,1)S(1)}, bf16[2048,256]{1,0:T(8,128)(2,1)S(1)}, f32[8,128]{1,0:T(8,128)S(1)}) custom-call(bf16[192,2048]{1,0:T(8,128)(2,1)S(1)} %get-tuple-element.49.refs_0_, bf16[64,2048]{1,0:T(8,128)(2,1)S(1)} %get-tuple-element.50.refs_1_, s32[128,1]{1,0:T(8,128)S(1)} %copy.8.slots.refs_1_.refs_2_.refs_7_, ...), custom_call_target="tpu_custom_call" | custom-call | flops 1000 | bytes 1000 | tf_op jit(solution)/shard_map/prepare/pallas_call | solution.py:176
  50.2 0.9 %collective-permute-done.7.refs_4_ = bf16[32,512]{1,0:T(8,128)(2,1)S(1)} collective-permute-done((bf16[32,512]{1,0:T(8,128)(2,1)S(1)}, bf16[32,512]{1,0:T(8,128)(2,1)S(1)}, u32[]{:S(2)}, u32[]{:S(2)}) %collective-permute-start.7) | collective-permute-done | bytes 32800 | tf_op jit(solution)/shard_map/ppermute | solution.py:24
  51.7 1.5 %collective-permute-start.11 = (bf16[128,512]{1,0:T(8,128)(2,1)S(1)}, bf16[128,512]{1,0:T(8,128)(2,1)S(1)}, u32[]{:S(2)}, u32[]{:S(2)}) collective-permute-start(bf16[128,512]{1,0:T(8,128)(2,1)S(1)} %slope.1.refs_0_), channel_id=1, source_target_pairs={{0,1},{1,0},{2,3},{3,2},{4,5},{5,4},{6,7},{7,6},{8,9},{9,8},{10,11... | collective-permute-start | bytes 393224 | tf_op jit(solution)/shard_map/ppermute | solution.py:24
  53.3 0.7 collective-permute-start.10
  54.0 1.2 %collective-permute-done.12.refs_3_ = bf16[128,512]{1,0:T(8,128)(2,1)S(1)} collective-permute-done((bf16[128,512]{1,0:T(8,128)(2,1)S(1)}, bf16[128,512]{1,0:T(8,128)(2,1)S(1)}, u32[]{:S(2)}, u32[]{:S(2)}) %collective-permute-start.12) | collective-permute-done | bytes 131104 | tf_op jit(solution)/shard_map/ppermute | solution.py:24
  55.6 2.9 %collective-permute-done.10.refs_1_ = bf16[128,512]{1,0:T(8,128)(2,1)S(1)} collective-permute-done((bf16[128,512]{1,0:T(8,128)(2,1)S(1)}, bf16[128,512]{1,0:T(8,128)(2,1)S(1)}, u32[]{:S(2)}, u32[]{:S(2)}) %collective-permute-start.10) | collective-permute-done | bytes 131104 | tf_op jit(solution)/shard_map/ppermute | solution.py:24
  58.8 1.5 %collective-permute-start.15 = (bf16[144,128]{1,0:T(8,128)(2,1)S(1)}, bf16[144,128]{1,0:T(8,128)(2,1)S(1)}, u32[]{:S(2)}, u32[]{:S(2)}) collective-permute-start(bf16[144,128]{1,0:T(8,128)(2,1)S(1)} %kept.1.refs_0_), channel_id=1, source_target_pairs={{0,8},{4,12},{8,0},{12,4},{16,24},{20,28},{24,16},{28,20},{1,9},{5... | collective-permute-start | bytes 110600 | tf_op jit(solution)/shard_map/ppermute | solution.py:24
  60.3 2.3 %collective-permute-start.14 = (bf16[144,128]{1,0:T(8,128)(2,1)S(1)}, bf16[144,128]{1,0:T(8,128)(2,1)S(1)}, u32[]{:S(2)}, u32[]{:S(2)}) collective-permute-start(bf16[144,128]{1,0:T(8,128)(2,1)S(1)} %kept.1.refs_0_), channel_id=1, source_target_pairs={{0,16},{4,20},{8,24},{12,28},{16,0},{20,4},{24,8},{28,12},{1,17},{... | collective-permute-start | bytes 110600 | tf_op jit(solution)/shard_map/ppermute | solution.py:24
  62.6 2.4 %residue.1 = (bf16[2048,512]{1,0:T(8,128)(2,1)}, f32[8,128]{1,0:T(8,128)S(1)}) custom-call(bf16[128,512]{1,0:T(8,128)(2,1)S(1)} %slope.1.refs_0_, bf16[128,512]{1,0:T(8,128)(2,1)S(1)} %collective-permute-done.10.refs_1_, bf16[128,512]{1,0:T(8,128)(2,1)S(1)} %collective-permute-done.11.refs_2_, bf16[128,512]{1,0:T(8,128)(2,1)S(1)} %collective-permute-done.12.refs_3_, ...), custom_call_target="tpu_custom_call" | custom-call | flops 1000 | bytes 1000 | tf_op jit(solution)/shard_map/residue/pallas_call | solution.py:259
  65.0 2.7 %collective-permute-done.13.refs_1_ = bf16[144,128]{1,0:T(8,128)(2,1)S(1)} collective-permute-done((bf16[144,128]{1,0:T(8,128)(2,1)S(1)}, bf16[144,128]{1,0:T(8,128)(2,1)S(1)}, u32[]{:S(2)}, u32[]{:S(2)}) %collective-permute-start.13) | collective-permute-done | bytes 36896 | tf_op jit(solution)/shard_map/ppermute | solution.py:24
  67.7 4.1 %collective-permute-start.16 = (bf16[576,128]{1,0:T(8,128)(2,1)S(1)}, bf16[576,128]{1,0:T(8,128)(2,1)S(1)}, u32[]{:S(2)}, u32[]{:S(2)}) collective-permute-start(bf16[576,128]{1,0:T(8,128)(2,1)S(1)} %join.1.group), channel_id=1, source_target_pairs={{0,4},{4,0},{8,12},{12,8},{16,20},{20,16},{24,28},{28,24},{1,5},{5... | collective-permute-start | bytes 442376 | tf_op jit(solution)/shard_map/ppermute | solution.py:24
  71.9 1.4 %half.1 = f32[2048,512]{1,0:T(8,128)S(1)} custom-call(bf16[576,128]{1,0:T(8,128)(2,1)S(1)} %join.1.group), custom_call_target="tpu_custom_call" | custom-call | flops 1000 | bytes 1000 | tf_op jit(solution)/shard_map/half/pallas_call | solution.py:341
  73.3 2.7 %outer.1 = f32[2048,512]{1,0:T(8,128)} custom-call(bf16[576,128]{1,0:T(8,128)(2,1)S(1)} %collective-permute-done.16.group, f32[2048,512]{1,0:T(8,128)S(1)} %half.1), custom_call_target="tpu_custom_call" | custom-call | flops 1000 | bytes 1000 | tf_op jit(solution)/shard_map/outer/pallas_call | solution.py:349
  (33 shorter events, 3.2 us)
Async XLA Ops:
  0.6 20.7 %copy-start = (bf16[1,128,8192]{2,1,0:T(8,128)(2,1)S(1)}, bf16[1,128,8192]{2,1,0:T(8,128)(2,1)}, u32[]{:S(2)}) copy-start(bf16[1,128,8192]{2,1,0:T(8,128)(2,1)} %param.6) | copy-start | bytes 6291460
  0.6 23.3 %copy-start.5 = (s32[1,1,128]{2,1,0:T(1,128)S(1)}, s32[1,1,128]{2,1,0:T(1,128)}, u32[]{:S(2)}) copy-start(s32[1,1,128]{2,1,0:T(1,128)} %param.11) | copy-start | bytes 1540
  18.2 15.0 %collective-permute-start = (bf16[128,2048]{1,0:T(8,128)(2,1)}, bf16[128,2048]{1,0:T(8,128)(2,1)S(1)}, u32[]{:S(2)}, u32[]{:S(2)}) collective-permute-start(bf16[128,2048]{1,0:T(8,128)(2,1)} %get-tuple-element.36), channel_id=1, source_target_pairs={{0,3},{1,2},{2,1},{3,0},{4,7},{5,6},{6,5},{7,4},{8,11},{9,10},{10,... | collective-permute-start | bytes 1572872 | tf_op jit(solution)/shard_map/ppermute | solution.py:24
  21.3 0.7 copy-start.6
  22.9 18.7 %collective-permute-start.2 = (bf16[96,2048]{1,0:T(8,128)(2,1)}, bf16[96,2048]{1,0:T(8,128)(2,1)S(1)}, u32[]{:S(2)}, u32[]{:S(2)}) collective-permute-start(bf16[96,2048]{1,0:T(8,128)(2,1)} %get-tuple-element.39), channel_id=1, source_target_pairs={{0,1},{1,0},{2,3},{3,2},{4,5},{5,4},{6,7},{7,6},{8,9},{9,8},{10,11... | collective-permute-start | bytes 1179656 | tf_op jit(solution)/shard_map/ppermute | solution.py:24
  23.2 19.1 %collective-permute-start.3 = (bf16[96,2048]{1,0:T(8,128)(2,1)}, bf16[96,2048]{1,0:T(8,128)(2,1)S(1)}, u32[]{:S(2)}, u32[]{:S(2)}) collective-permute-start(bf16[96,2048]{1,0:T(8,128)(2,1)} %get-tuple-element.40), channel_id=1, source_target_pairs={{0,2},{1,3},{2,0},{3,1},{4,6},{5,7},{6,4},{7,5},{8,10},{9,11},{10,... | collective-permute-start | bytes 1179656 | tf_op jit(solution)/shard_map/ppermute | solution.py:24
  24.0 1.6 %copy-start.2 = (bf16[1,2048,512]{2,1,0:T(8,128)(2,1)S(1)}, bf16[1,2048,512]{2,1,0:T(8,128)(2,1)}, u32[]{:S(2)}) copy-start(bf16[1,2048,512]{2,1,0:T(8,128)(2,1)} %param.9) | copy-start | bytes 6291460
  26.7 6.5 %copy-start.1 = (bf16[1,2048,512]{2,1,0:T(8,128)(2,1)S(1)}, bf16[1,2048,512]{2,1,0:T(8,128)(2,1)}, u32[]{:S(2)}) copy-start(bf16[1,2048,512]{2,1,0:T(8,128)(2,1)} %param.8) | copy-start | bytes 6291460
  26.8 18.8 %collective-permute-start.5 = (bf16[32,2048]{1,0:T(8,128)(2,1)S(1)}, bf16[32,2048]{1,0:T(8,128)(2,1)S(1)}, u32[]{:S(2)}, u32[]{:S(2)}) collective-permute-start(bf16[32,2048]{1,0:T(8,128)(2,1)S(1)} %get-tuple-element.44), channel_id=1, source_target_pairs={{0,1},{1,0},{2,3},{3,2},{4,5},{5,4},{6,7},{7,6},{8,9},{9,8},{10,11... | collective-permute-start | bytes 393224 | tf_op jit(solution)/shard_map/ppermute | solution.py:24
  28.3 17.6 %collective-permute-start.6 = (bf16[32,2048]{1,0:T(8,128)(2,1)S(1)}, bf16[32,2048]{1,0:T(8,128)(2,1)S(1)}, u32[]{:S(2)}, u32[]{:S(2)}) collective-permute-start(bf16[32,2048]{1,0:T(8,128)(2,1)S(1)} %get-tuple-element.45), channel_id=1, source_target_pairs={{0,2},{1,3},{2,0},{3,1},{4,6},{5,7},{6,4},{7,5},{8,10},{9,11},{10,... | collective-permute-start | bytes 393224 | tf_op jit(solution)/shard_map/ppermute | solution.py:24
  33.9 17.2 %collective-permute-start.1 = (bf16[128,512]{1,0:T(8,128)(2,1)S(1)}, bf16[128,512]{1,0:T(8,128)(2,1)S(1)}, u32[]{:S(2)}, u32[]{:S(2)}) collective-permute-start(bf16[128,512]{1,0:T(8,128)(2,1)S(1)} %get-tuple-element.38), channel_id=1, source_target_pairs={{0,3},{1,2},{2,1},{3,0},{4,7},{5,6},{6,5},{7,4},{8,11},{9,10},{10,... | collective-permute-start | bytes 393224 | tf_op jit(solution)/shard_map/ppermute | solution.py:24
  42.9 8.2 %copy-start.4 = (bf16[1,128,512]{2,1,0:T(8,128)(2,1)S(1)}, bf16[1,128,512]{2,1,0:T(8,128)(2,1)}, u32[]{:S(2)}) copy-start(bf16[1,128,512]{2,1,0:T(8,128)(2,1)} %param.7) | copy-start | bytes 393220
  42.9 8.2 %collective-permute-start.4 = (bf16[96,512]{1,0:T(8,128)(2,1)S(1)}, bf16[96,512]{1,0:T(8,128)(2,1)S(1)}, u32[]{:S(2)}, u32[]{:S(2)}) collective-permute-start(bf16[96,512]{1,0:T(8,128)(2,1)S(1)} %get-tuple-element.43), channel_id=1, source_target_pairs={{0,1},{1,0},{2,3},{3,2},{4,5},{5,4},{6,7},{7,6},{8,9},{9,8},{10,11... | collective-permute-start | bytes 294920 | tf_op jit(solution)/shard_map/ppermute | solution.py:24
  44.4 18.2 %copy-start.3 = (bf16[1,2048,512]{2,1,0:T(8,128)(2,1)S(1)}, bf16[1,2048,512]{2,1,0:T(8,128)(2,1)}, u32[]{:S(2)}) copy-start(bf16[1,2048,512]{2,1,0:T(8,128)(2,1)} %param.9) | copy-start | bytes 6291460
  44.4 6.8 %collective-permute-start.8 = (bf16[96,512]{1,0:T(8,128)(2,1)S(1)}, bf16[96,512]{1,0:T(8,128)(2,1)S(1)}, u32[]{:S(2)}, u32[]{:S(2)}) collective-permute-start(bf16[96,512]{1,0:T(8,128)(2,1)S(1)} %get-tuple-element.46.refs_3_), channel_id=1, source_target_pairs={{0,2},{1,3},{2,0},{3,1},{4,6},{5,7},{6,4},{7,5},{8,10},{9,11},{10,... | collective-permute-start | bytes 294920 | tf_op jit(solution)/shard_map/ppermute | solution.py:24
  46.3 3.9 %collective-permute-start.9 = (bf16[32,512]{1,0:T(8,128)(2,1)S(1)}, bf16[32,512]{1,0:T(8,128)(2,1)S(1)}, u32[]{:S(2)}, u32[]{:S(2)}) collective-permute-start(bf16[32,512]{1,0:T(8,128)(2,1)S(1)} %get-tuple-element.48), channel_id=1, source_target_pairs={{0,2},{1,3},{2,0},{3,1},{4,6},{5,7},{6,4},{7,5},{8,10},{9,11},{10,... | collective-permute-start | bytes 98312 | tf_op jit(solution)/shard_map/ppermute | solution.py:24
  48.1 3.0 %collective-permute-start.7 = (bf16[32,512]{1,0:T(8,128)(2,1)S(1)}, bf16[32,512]{1,0:T(8,128)(2,1)S(1)}, u32[]{:S(2)}, u32[]{:S(2)}) collective-permute-start(bf16[32,512]{1,0:T(8,128)(2,1)S(1)} %get-tuple-element.47.refs_4_), channel_id=1, source_target_pairs={{0,1},{1,0},{2,3},{3,2},{4,5},{5,4},{6,7},{7,6},{8,9},{9,8},{10,11... | collective-permute-start | bytes 98312 | tf_op jit(solution)/shard_map/ppermute | solution.py:24
  51.3 3.9 %collective-permute-start.12 = (bf16[128,512]{1,0:T(8,128)(2,1)S(1)}, bf16[128,512]{1,0:T(8,128)(2,1)S(1)}, u32[]{:S(2)}, u32[]{:S(2)}) collective-permute-start(bf16[128,512]{1,0:T(8,128)(2,1)S(1)} %slope.1.refs_0_), channel_id=1, source_target_pairs={{0,2},{1,3},{2,0},{3,1},{4,6},{5,7},{6,4},{7,5},{8,10},{9,11},{10,... | collective-permute-start | bytes 393224 | tf_op jit(solution)/shard_map/ppermute | solution.py:24
  51.7 3.9 %collective-permute-start.11 = (bf16[128,512]{1,0:T(8,128)(2,1)S(1)}, bf16[128,512]{1,0:T(8,128)(2,1)S(1)}, u32[]{:S(2)}, u32[]{:S(2)}) collective-permute-start(bf16[128,512]{1,0:T(8,128)(2,1)S(1)} %slope.1.refs_0_), channel_id=1, source_target_pairs={{0,1},{1,0},{2,3},{3,2},{4,5},{5,4},{6,7},{7,6},{8,9},{9,8},{10,11... | collective-permute-start | bytes 393224 | tf_op jit(solution)/shard_map/ppermute | solution.py:24
  53.3 5.3 %collective-permute-start.10 = (bf16[128,512]{1,0:T(8,128)(2,1)S(1)}, bf16[128,512]{1,0:T(8,128)(2,1)S(1)}, u32[]{:S(2)}, u32[]{:S(2)}) collective-permute-start(bf16[128,512]{1,0:T(8,128)(2,1)S(1)} %slope.1.refs_0_), channel_id=1, source_target_pairs={{0,3},{1,2},{2,1},{3,0},{4,7},{5,6},{6,5},{7,4},{8,11},{9,10},{10,... | collective-permute-start | bytes 393224 | tf_op jit(solution)/shard_map/ppermute | solution.py:24
  58.8 6.2 %collective-permute-start.15 = (bf16[144,128]{1,0:T(8,128)(2,1)S(1)}, bf16[144,128]{1,0:T(8,128)(2,1)S(1)}, u32[]{:S(2)}, u32[]{:S(2)}) collective-permute-start(bf16[144,128]{1,0:T(8,128)(2,1)S(1)} %kept.1.refs_0_), channel_id=1, source_target_pairs={{0,8},{4,12},{8,0},{12,4},{16,24},{20,28},{24,16},{28,20},{1,9},{5... | collective-permute-start | bytes 110600 | tf_op jit(solution)/shard_map/ppermute | solution.py:24
  60.3 4.7 %collective-permute-start.14 = (bf16[144,128]{1,0:T(8,128)(2,1)S(1)}, bf16[144,128]{1,0:T(8,128)(2,1)S(1)}, u32[]{:S(2)}, u32[]{:S(2)}) collective-permute-start(bf16[144,128]{1,0:T(8,128)(2,1)S(1)} %kept.1.refs_0_), channel_id=1, source_target_pairs={{0,16},{4,20},{8,24},{12,28},{16,0},{20,4},{24,8},{28,12},{1,17},{... | collective-permute-start | bytes 110600 | tf_op jit(solution)/shard_map/ppermute | solution.py:24
  62.6 5.1 %collective-permute-start.13 = (bf16[144,128]{1,0:T(8,128)(2,1)S(1)}, bf16[144,128]{1,0:T(8,128)(2,1)S(1)}, u32[]{:S(2)}, u32[]{:S(2)}) collective-permute-start(bf16[144,128]{1,0:T(8,128)(2,1)S(1)} %kept.1.refs_0_), channel_id=1, source_target_pairs={{0,24},{4,28},{8,16},{12,20},{16,8},{20,12},{24,0},{28,4},{1,25},{... | collective-permute-start | bytes 110600 | tf_op jit(solution)/shard_map/ppermute | solution.py:24
  67.7 5.6 %collective-permute-start.16 = (bf16[576,128]{1,0:T(8,128)(2,1)S(1)}, bf16[576,128]{1,0:T(8,128)(2,1)S(1)}, u32[]{:S(2)}, u32[]{:S(2)}) collective-permute-start(bf16[576,128]{1,0:T(8,128)(2,1)S(1)} %join.1.group), channel_id=1, source_target_pairs={{0,4},{4,0},{8,12},{12,8},{16,20},{20,16},{24,28},{28,24},{1,5},{5... | collective-permute-start | bytes 442376 | tf_op jit(solution)/shard_map/ppermute | solution.py:24

commit v7 on v6

--- a/solution.py
+++ b/solution.py
@@ -39,7 +39,7 @@
         copy.wait()
 
 
-def cut(tokens, depth, cuts, after, mib=16):
+def cut(tokens, depth, cuts, after):
     return pl.pallas_call(
         functools.partial(cut_kernel, cuts),
         out_shape=[jax.ShapeDtypeStruct((rows, depth), tokens.dtype) for _, _, rows in cuts]
@@ -47,7 +47,7 @@
         in_specs=[ANY] * (1 + len(after)),
         out_specs=[ANY] * len(cuts) + [VMEM],
         scratch_shapes=[pltpu.SemaphoreType.DMA((len(cuts),))],
-        compiler_params=params(mib),
+        compiler_params=params(16),
         cost_estimate=BRIEF,
         name="cut",
     )(tokens, *after)
@@ -194,18 +194,30 @@
         start += high - low
 
 
+def gather_kernel(order, *refs):
+    slopes, (xg, out, s) = refs[:-3], refs[-3:]
+    stack(slopes, order, s)
+    out[...] = jnp.dot(xg[...], s[...], preferred_element_type=jnp.float32)
+
+
+def gather(slopes, order, xg):
+    kw = slopes[0].shape[1]
+    return pl.pallas_call(
+        functools.partial(gather_kernel, order),
+        out_shape=jax.ShapeDtypeStruct((xg.shape[0], kw), jnp.float32),
+        scratch_shapes=[pltpu.VMEM((xg.shape[1], kw), jnp.bfloat16)],
+        compiler_params=params(8),
+        cost_estimate=BRIEF,
+        name="gather",
+    )(*slopes, xg)
+
+
 def kept_kernel(per_row, order, *refs):
-    n = len({k for k, _, _ in order})
-    slopes, (fbk, slots, slot_row), out, s = refs[:n], refs[-5:-2], refs[-2], refs[-1]
-    xgs = refs[n:-5]
+    slopes, (wide, xg, fbk, slots, slot_row, out, s) = refs[:-7], refs[-7:]
     cap = slots.shape[0]
     stack(slopes, order, s)
-    wide, start = 0.0, 0
-    for xg in xgs:
-        rows = xg.shape[1]
-        wide += jnp.dot(xg[...], s[start : start + rows, :], preferred_element_type=jnp.float32)
-        start += rows
-    value = pick_columns(wide, slots[...] % per_row) + fbk[...]
+    total = wide[...] + jnp.dot(xg[...], s[...], preferred_element_type=jnp.float32)
+    value = pick_columns(total, slots[...] % per_row) + fbk[...]
     out[:cap, :] = value.astype(jnp.bfloat16)
     tail = out.shape[0] - cap
     number = jnp.broadcast_to(slot_row[...], (tail, cap))
@@ -214,18 +226,16 @@
     out[cap:, :] = number.astype(jnp.float32).astype(jnp.bfloat16)
 
 
-def kept(slopes, order, xgs, fbk, slots, slot_row):
-    cap = slots.shape[0]
-    rows, kw = slopes[0].shape
-    total = len(slopes) * rows
+def kept(slopes, order, wide, xg, fbk, slots, slot_row):
+    cap, kw = wide.shape
     return pl.pallas_call(
         functools.partial(kept_kernel, kw // LANES, order),
         out_shape=jax.ShapeDtypeStruct((cap + 16, LANES), jnp.bfloat16),
-        scratch_shapes=[pltpu.VMEM((total, kw), jnp.bfloat16)],
+        scratch_shapes=[pltpu.VMEM((xg.shape[1], kw), jnp.bfloat16)],
         compiler_params=params(8),
         cost_estimate=BRIEF,
         name="kept",
-    )(*slopes, *xgs, fbk, slots, slot_row)
+    )(*slopes, wide, xg, fbk, slots, slot_row)
 
 
 def send_out(held, out, sems, t, tile):
@@ -275,23 +285,23 @@
     )(*slopes, *xts, fb, keep)
 
 
-def join_kernel(*refs):
-    out = refs[-1]
-    rows = refs[0].shape[0]
-    for k in range(len(refs) - 2):
-        out[k * rows : (k + 1) * rows, :] = refs[k][...]
-
-
-def join(messages, after):
-    rows, lanes = messages[0].shape
-    return pl.pallas_call(
-        join_kernel,
-        out_shape=jax.ShapeDtypeStruct((len(messages) * rows, lanes), jnp.bfloat16),
-        in_specs=[VMEM] * len(messages) + [ANY],
+def join_kernel(n, *refs):
+    out, start = refs[-1], 0
+    for part in refs[:n]:
+        out[start : start + part.shape[0], :] = part[...]
+        start += part.shape[0]
+
+
+def join(parts, after):
+    rows, lanes = sum(part.shape[0] for part in parts), parts[0].shape[1]
+    return pl.pallas_call(
+        functools.partial(join_kernel, len(parts)),
+        out_shape=jax.ShapeDtypeStruct((rows, lanes), jnp.bfloat16),
+        in_specs=[VMEM] * len(parts) + [ANY] * len(after),
         compiler_params=params(8),
         cost_estimate=BRIEF,
         name="join",
-    )(*messages, after)
+    )(*parts, *after)
 
 
 def spread(group, wide, lines, cap, per_row):
@@ -371,9 +381,10 @@
     near = [d for d in range(1, n_shard) if d & (d - 1) == 0]
     far = [d for d in range(1, n_shard) if d & (d - 1) != 0]
 
-    *far_out, token = cut(tokens, depth, [(d, 0, tok_dev) for d in far], [], 60)
+    me = lax.axis_index("shard")
+    far_out = [lax.dynamic_slice(tokens, (0, (me ^ d) * depth), (tok_dev, depth)) for d in far]
     far_in = [swap(x, "shard", n_shard, d) for x, d in zip(far_out, far)]
-    near_out = []
+    near_out, token = [], far_out[0]
     for low, high in spans:
         *out, token = cut(tokens, depth, [(d, low, high - low) for d in near], [token])
         near_out.append(out)
@@ -398,12 +409,17 @@
     slopes = slope(target[0], mine, whole, shares, spans, token)
     slopes = [slopes] + [swap(slopes, "shard", n_shard, d) for d in far + near]
 
-    order = [(k, 0, tok_dev) for k in range(1 + len(far))]
-    order += [(k, low, high) for low, high in spans for k in range(1 + len(far), n_shard)]
-    message = kept(slopes, order, [xg_far, xg_near], fbk, slots, slot_row)
-    same_core = [message] + [swap(message, "rep", n_rep, d) for d in range(n_rep - 2, 0, -2)]
+    n_far = 1 + len(far)
+    order_far = [(k, 0, tok_dev) for k in range(n_far)]
+    order_near = [(k, low, high) for low, high in spans for k in range(len(near))]
+    wide = gather(slopes[:n_far], order_far, xg_far)
+    message = kept(slopes[n_far:], order_near, wide, xg_near, fbk, slots, slot_row)
+    same_core = [swap(message, "rep", n_rep, d) for d in range(n_rep - 2, 0, -2)]
+    order = order_far + [(n_far + k, low, high) for k, low, high in order_near]
     new_feedback, token = residue(slopes, order, [xt_far, xt_near], fb, keep)
-    joined = join(same_core, token)
+    joined, after = message, [token]
+    for received in same_core:
+        joined, after = join([joined, received], after), []
     groups = [joined, swap(joined, "rep", n_rep, 1)]
     return outer(groups, message.shape[0] - 16, depth, kw), new_feedback[None]
 

time: 76.2 us -> 57.7 us (0.76)
  Pallas kernels: 30.3 us -> 13.9 us
  waiting for transfers between devices: 17.2 us -> 13.9 us
  local copies, waits for them, and re-layouts: 2.41 us -> 4.4 us
  starting transfers between devices: 24.6 us -> 23.7 us
    pallas_call x4 -> x3, Pallas kernels: 19.2 us -> 1.64 us  [cut(): pl.pallas_call(functools.partial(cut_kernel, cuts), out_shape=[jax.ShapeD...]
    ppermute x17, waiting for transfers between devices: 17.2 us -> 13.9 us  [swap(): return lax.ppermute(x, axis, [(i, i ^ d) for i in range(n)])]
    pallas_call x3, Pallas kernels: 1.75 us -> 2.87 us  [project(): pl.pallas_call(functools.partial(project_kernel, n), out_shape=[jax.Shape...]
    dynamic_slice x0 -> x1, local copies, waits for them, and re-layouts: none -> 1.08 us  [on_device(): lax.dynamic_slice(tokens, (0, (me ^ d) * depth), (tok_dev, depth))]
    ppermute x17, starting transfers between devices: 24.6 us -> 23.7 us  [swap(): return lax.ppermute(x, axis, [(i, i ^ d) for i in range(n)])]
    unnamed x14, local copies, waits for them, and re-layouts: 2.3 us -> 3.2 us
  transfers between devices with their start and end apart: 17 -> 17, of which waited for: 9 -> 9; matrix products, arithmetic and copies ran while one was open for 0% -> 0% of each run, Pallas kernels for 13% -> 19%
where the time goes in v7:
time: 57.7 us; the launch traced here: 57.5 us
  starting transfers between devices  23.7 us (41%)
  Pallas kernels  13.9 us (24%)
  waiting for transfers between devices  13.9 us (24%)
  local copies, waits for them, and re-layouts  4.4 us (8%)
  between operations  1.51 us (3%)
    ppermute x17, starting transfers between devices, swap(): return lax.ppermute(x, axis, [(i, i ^ d) for i in range(n)])  23.7 us
    ppermute x17, waiting for transfers between devices, swap(): return lax.ppermute(x, axis, [(i, i ^ d) for i in range(n)])  13.9 us
    unnamed x14, local copies, waits for them, and re-layouts  3.2 us
    pallas_call x3, Pallas kernels, project(): pl.pallas_call(functools.partial(project_kernel, n), out_shape=[jax.Shape...  2.87 us
    pallas_call x1, Pallas kernels, outer(): pl.pallas_call(functools.partial(outer_kernel, cap, kw // LANES, tile, n)...  2.65 us
    pallas_call x1, Pallas kernels, residue(): pl.pallas_call(functools.partial(residue_kernel, order, tile), out_shape=...  2.39 us
    pallas_call x3, Pallas kernels, cut(): pl.pallas_call(functools.partial(cut_kernel, cuts), out_shape=[jax.ShapeD...  1.64 us
    pallas_call x2, Pallas kernels, prepare(): pl.pallas_call(functools.partial(prepare_kernel, per_row, len(xs)), out_s...  1.43 us
  transfers between devices with their start and end apart: 17, of which 9 were waited for; matrix products, arithmetic and copies ran while one was open for 0% of the time, Pallas kernels for 19%

profile of v7, /device:TPU:1, one launch (start us, length us, event | category | flops | bytes accessed | tf_op | source)
XLA Modules:
  0.0 57.5 jit_solution(2752857949478097111)
XLA Ops:
  0.6 1.1 %dynamic-slice_bitcast_fusion.refs_0_ = bf16[128,2048]{1,0:T(8,128)(2,1)S(1)} fusion(bf16[1,128,8192]{2,1,0:T(8,128)(2,1)} %param.6, s32[]{:T(128)S(6)} %select_n.3), kind=kLoop, calls=%fused_computation | loop fusion | bytes 1048580 | tf_op jit(solution)/shard_map/dynamic_slice | solution.py:385
  1.7 3.1 %collective-permute-start = (bf16[128,2048]{1,0:T(8,128)(2,1)S(1)}, bf16[128,2048]{1,0:T(8,128)(2,1)S(1)}, u32[]{:S(2)}, u32[]{:S(2)}) collective-permute-start(bf16[128,2048]{1,0:T(8,128)(2,1)S(1)} %dynamic-slice_bitcast_fusion.refs_0_), channel_id=1, source_target_pairs={{0,3},{1,2},{2,1},{3,0},{4,7},{5,6},{6,5},{7,4},{8,11},{9,10},{10,... | collective-permute-start | bytes 1572872 | tf_op jit(solution)/shard_map/ppermute | solution.py:24
  4.8 1.6 %copy-done = bf16[1,128,8192]{2,1,0:T(8,128)(2,1)S(1)} copy-done((bf16[1,128,8192]{2,1,0:T(8,128)(2,1)S(1)}, bf16[1,128,8192]{2,1,0:T(8,128)(2,1)}, u32[]{:S(2)}) %copy-start) | copy-done | bytes 2097176
  6.4 0.9 %cut.3 = (bf16[96,2048]{1,0:T(8,128)(2,1)}, bf16[96,2048]{1,0:T(8,128)(2,1)}, f32[8,128]{1,0:T(8,128)S(1)}) custom-call(bf16[128,8192]{1,0:T(8,128)(2,1)S(1)} %bitcast.9, bf16[128,2048]{1,0:T(8,128)(2,1)S(1)} %dynamic-slice_bitcast_fusion.refs_0_), custom_call_target="tpu_custom_call" | custom-call | flops 1000 | bytes 1000 | tf_op jit(solution)/shard_map/cut/pallas_call | solution.py:43
  8.4 1.6 %copy-done.3 = bf16[1,2048,512]{2,1,0:T(8,128)(2,1)S(1)} copy-done((bf16[1,2048,512]{2,1,0:T(8,128)(2,1)S(1)}, bf16[1,2048,512]{2,1,0:T(8,128)(2,1)}, u32[]{:S(2)}) %copy-start.3) | copy-done | bytes 2097176
  10.0 1.0 %early.1 = (f32[128,128]{1,0:T(8,128)S(1)}, bf16[2048,512]{1,0:T(8,128)(2,1)S(1)}, f32[8,128]{1,0:T(8,128)S(1)}) custom-call(s32[128,1]{1,0:T(8,128)S(1)} %copy.8.slots.refs_1_.refs_2_.refs_5_, s32[1,128]{1,0:T(1,128)S(1)} %bitcast.19, s32[1,1]{1,0:T(1,128)S(6)} %copy.12.count.refs_2_.refs_3_, bf16[2048,512]{1,0:T(8,128)(2,1)S(1)} %bitcast.15, ...), custom_call_target="tpu_custom_call" | custom-call | flops 1000 | bytes 1000 | tf_op jit(solution)/shard_map/early/pallas_call | solution.py:140
  11.2 1.5 %collective-permute-start.5 = (bf16[32,2048]{1,0:T(8,128)(2,1)S(1)}, bf16[32,2048]{1,0:T(8,128)(2,1)S(1)}, u32[]{:S(2)}, u32[]{:S(2)}) collective-permute-start(bf16[32,2048]{1,0:T(8,128)(2,1)S(1)} %get-tuple-element.40), channel_id=1, source_target_pairs={{0,1},{1,0},{2,3},{3,2},{4,5},{5,4},{6,7},{7,6},{8,9},{9,8},{10,11... | collective-permute-start | bytes 393224 | tf_op jit(solution)/shard_map/ppermute | solution.py:24
  12.7 1.2 %collective-permute-start.6 = (bf16[32,2048]{1,0:T(8,128)(2,1)S(1)}, bf16[32,2048]{1,0:T(8,128)(2,1)S(1)}, u32[]{:S(2)}, u32[]{:S(2)}) collective-permute-start(bf16[32,2048]{1,0:T(8,128)(2,1)S(1)} %get-tuple-element.41), channel_id=1, source_target_pairs={{0,2},{1,3},{2,0},{3,1},{4,6},{5,7},{6,4},{7,5},{8,10},{9,11},{10,... | collective-permute-start | bytes 393224 | tf_op jit(solution)/shard_map/ppermute | solution.py:24
  13.9 0.6 %cut.5 = (bf16[128,2048]{1,0:T(8,128)(2,1)S(1)}, f32[8,128]{1,0:T(8,128)}) custom-call(bf16[128,8192]{1,0:T(8,128)(2,1)S(1)} %bitcast.11, f32[8,128]{1,0:T(8,128)S(1)} %get-tuple-element.31.refs_0_), custom_call_target="tpu_custom_call" | custom-call | flops 1000 | bytes 1000 | tf_op jit(solution)/shard_map/cut/pallas_call | solution.py:43
  14.6 1.9 %collective-permute-done.refs_1_ = bf16[128,2048]{1,0:T(8,128)(2,1)S(1)} collective-permute-done((bf16[128,2048]{1,0:T(8,128)(2,1)S(1)}, bf16[128,2048]{1,0:T(8,128)(2,1)S(1)}, u32[]{:S(2)}, u32[]{:S(2)}) %collective-permute-start) | collective-permute-done | bytes 524320 | tf_op jit(solution)/shard_map/ppermute | solution.py:24
  16.5 0.7 %project.3 = (f32[128,512]{1,0:T(8,128)S(1)}, bf16[128,512]{1,0:T(8,128)(2,1)S(1)}, bf16[256,2048]{1,0:T(8,128)(2,1)S(1)}) custom-call(bf16[128,2048]{1,0:T(8,128)(2,1)S(1)} %get-tuple-element.32.refs_0_, bf16[128,2048]{1,0:T(8,128)(2,1)S(1)} %collective-permute-done.refs_1_, bf16[2048,512]{1,0:T(8,128)(2,1)S(1)} %bitcast.12), custom_call_target="tpu_custom_call" | custom-call | flops 1000 | bytes 1000 | tf_op jit(solution)/shard_map/project/pallas_call | solution.py:73
  17.2 2.1 %collective-permute-start.1 = (bf16[128,512]{1,0:T(8,128)(2,1)S(1)}, bf16[128,512]{1,0:T(8,128)(2,1)S(1)}, u32[]{:S(2)}, u32[]{:S(2)}) collective-permute-start(bf16[128,512]{1,0:T(8,128)(2,1)S(1)} %get-tuple-element.34), channel_id=1, source_target_pairs={{0,3},{1,2},{2,1},{3,0},{4,7},{5,6},{6,5},{7,4},{8,11},{9,10},{10,... | collective-permute-start | bytes 393224 | tf_op jit(solution)/shard_map/ppermute | solution.py:24
  19.9 5.1 %collective-permute-done.2.refs_0_ = bf16[96,2048]{1,0:T(8,128)(2,1)} collective-permute-done((bf16[96,2048]{1,0:T(8,128)(2,1)}, bf16[96,2048]{1,0:T(8,128)(2,1)}, u32[]{:S(2)}, u32[]{:S(2)}) %collective-permute-start.2) | collective-permute-done | bytes 393248 | tf_op jit(solution)/shard_map/ppermute | solution.py:24
  25.0 0.8 %collective-permute-done.3.refs_1_ = bf16[96,2048]{1,0:T(8,128)(2,1)} collective-permute-done((bf16[96,2048]{1,0:T(8,128)(2,1)}, bf16[96,2048]{1,0:T(8,128)(2,1)}, u32[]{:S(2)}, u32[]{:S(2)}) %collective-permute-start.3) | collective-permute-done | bytes 393248 | tf_op jit(solution)/shard_map/ppermute | solution.py:24
  25.7 1.7 %project.4 = (bf16[96,512]{1,0:T(8,128)(2,1)S(1)}, bf16[96,512]{1,0:T(8,128)(2,1)S(1)}, bf16[192,2048]{1,0:T(8,128)(2,1)S(1)}) custom-call(bf16[96,2048]{1,0:T(8,128)(2,1)} %collective-permute-done.2.refs_0_, bf16[96,2048]{1,0:T(8,128)(2,1)} %collective-permute-done.3.refs_1_, bf16[2048,512]{1,0:T(8,128)(2,1)S(1)} %bitcast.13, ...), custom_call_target="tpu_custom_call" | custom-call | flops 1000 | bytes 1000 | tf_op jit(solution)/shard_map/project/pallas_call | solution.py:73
  27.4 1.5 %collective-permute-start.4 = (bf16[96,512]{1,0:T(8,128)(2,1)S(1)}, bf16[96,512]{1,0:T(8,128)(2,1)S(1)}, u32[]{:S(2)}, u32[]{:S(2)}) collective-permute-start(bf16[96,512]{1,0:T(8,128)(2,1)S(1)} %get-tuple-element.39), channel_id=1, source_target_pairs={{0,1},{1,0},{2,3},{3,2},{4,5},{5,4},{6,7},{7,6},{8,9},{9,8},{10,11... | collective-permute-start | bytes 294920 | tf_op jit(solution)/shard_map/ppermute | solution.py:24
  28.9 1.2 %collective-permute-start.8 = (bf16[96,512]{1,0:T(8,128)(2,1)S(1)}, bf16[96,512]{1,0:T(8,128)(2,1)S(1)}, u32[]{:S(2)}, u32[]{:S(2)}) collective-permute-start(bf16[96,512]{1,0:T(8,128)(2,1)S(1)} %get-tuple-element.42.refs_3_), channel_id=1, source_target_pairs={{0,2},{1,3},{2,0},{3,1},{4,6},{5,7},{6,4},{7,5},{8,10},{9,11},{10,... | collective-permute-start | bytes 294920 | tf_op jit(solution)/shard_map/ppermute | solution.py:24
  30.6 0.8 %collective-permute-start.9 = (bf16[32,512]{1,0:T(8,128)(2,1)S(1)}, bf16[32,512]{1,0:T(8,128)(2,1)S(1)}, u32[]{:S(2)}, u32[]{:S(2)}) collective-permute-start(bf16[32,512]{1,0:T(8,128)(2,1)S(1)} %get-tuple-element.44), channel_id=1, source_target_pairs={{0,2},{1,3},{2,0},{3,1},{4,6},{5,7},{6,4},{7,5},{8,10},{9,11},{10,... | collective-permute-start | bytes 98312 | tf_op jit(solution)/shard_map/ppermute | solution.py:24
  31.4 1.2 %collective-permute-start.7 = (bf16[32,512]{1,0:T(8,128)(2,1)S(1)}, bf16[32,512]{1,0:T(8,128)(2,1)S(1)}, u32[]{:S(2)}, u32[]{:S(2)}) collective-permute-start(bf16[32,512]{1,0:T(8,128)(2,1)S(1)} %get-tuple-element.43.refs_4_), channel_id=1, source_target_pairs={{0,1},{1,0},{2,3},{3,2},{4,5},{5,4},{6,7},{7,6},{8,9},{9,8},{10,11... | collective-permute-start | bytes 98312 | tf_op jit(solution)/shard_map/ppermute | solution.py:24
  32.6 0.9 %prepare.3 = (bf16[128,256]{1,0:T(8,128)(2,1)S(1)}, bf16[2048,256]{1,0:T(8,128)(2,1)S(1)}, f32[8,128]{1,0:T(8,128)S(1)}) custom-call(bf16[192,2048]{1,0:T(8,128)(2,1)S(1)} %get-tuple-element.45.refs_0_, bf16[64,2048]{1,0:T(8,128)(2,1)S(1)} %get-tuple-element.46.refs_1_, s32[128,1]{1,0:T(8,128)S(1)} %copy.8.slots.refs_1_.refs_2_.refs_5_, ...), custom_call_target="tpu_custom_call" | custom-call | flops 1000 | bytes 1000 | tf_op jit(solution)/shard_map/prepare/pallas_call | solution.py:176
  33.7 0.7 %collective-permute-done.7.refs_4_ = bf16[32,512]{1,0:T(8,128)(2,1)S(1)} collective-permute-done((bf16[32,512]{1,0:T(8,128)(2,1)S(1)}, bf16[32,512]{1,0:T(8,128)(2,1)S(1)}, u32[]{:S(2)}, u32[]{:S(2)}) %collective-permute-start.7) | collective-permute-done | bytes 32800 | tf_op jit(solution)/shard_map/ppermute | solution.py:24
  34.6 1.6 %collective-permute-start.12 = (bf16[128,512]{1,0:T(8,128)(2,1)S(1)}, bf16[128,512]{1,0:T(8,128)(2,1)S(1)}, u32[]{:S(2)}, u32[]{:S(2)}) collective-permute-start(bf16[128,512]{1,0:T(8,128)(2,1)S(1)} %slope.1.refs_0_), channel_id=1, source_target_pairs={{0,3},{1,2},{2,1},{3,0},{4,7},{5,6},{6,5},{7,4},{8,11},{9,10},{10,... | collective-permute-start | bytes 393224 | tf_op jit(solution)/shard_map/ppermute | solution.py:24
  36.1 0.9 %collective-permute-start.11 = (bf16[128,512]{1,0:T(8,128)(2,1)S(1)}, bf16[128,512]{1,0:T(8,128)(2,1)S(1)}, u32[]{:S(2)}, u32[]{:S(2)}) collective-permute-start(bf16[128,512]{1,0:T(8,128)(2,1)S(1)} %slope.1.refs_0_), channel_id=1, source_target_pairs={{0,2},{1,3},{2,0},{3,1},{4,6},{5,7},{6,4},{7,5},{8,10},{9,11},{10,... | collective-permute-start | bytes 393224 | tf_op jit(solution)/shard_map/ppermute | solution.py:24
  37.3 2.2 %collective-permute-done.12.refs_1_ = bf16[128,512]{1,0:T(8,128)(2,1)S(1)} collective-permute-done((bf16[128,512]{1,0:T(8,128)(2,1)S(1)}, bf16[128,512]{1,0:T(8,128)(2,1)S(1)}, u32[]{:S(2)}, u32[]{:S(2)}) %collective-permute-start.12) | collective-permute-done | bytes 131104 | tf_op jit(solution)/shard_map/ppermute | solution.py:24
  39.6 1.1 %collective-permute-done.11.refs_1_.refs_3_ = bf16[128,512]{1,0:T(8,128)(2,1)S(1)} collective-permute-done((bf16[128,512]{1,0:T(8,128)(2,1)S(1)}, bf16[128,512]{1,0:T(8,128)(2,1)S(1)}, u32[]{:S(2)}, u32[]{:S(2)}) %collective-permute-start.11) | collective-permute-done | bytes 131104 | tf_op jit(solution)/shard_map/ppermute | solution.py:24
  40.8 0.8 %collective-permute-done.10.refs_0_.refs_2_ = bf16[128,512]{1,0:T(8,128)(2,1)S(1)} collective-permute-done((bf16[128,512]{1,0:T(8,128)(2,1)S(1)}, bf16[128,512]{1,0:T(8,128)(2,1)S(1)}, u32[]{:S(2)}, u32[]{:S(2)}) %collective-permute-start.10) | collective-permute-done | bytes 131104 | tf_op jit(solution)/shard_map/ppermute | solution.py:24
  41.8 3.4 %collective-permute-start.13 = (bf16[144,128]{1,0:T(8,128)(2,1)S(1)}, bf16[144,128]{1,0:T(8,128)(2,1)S(1)}, u32[]{:S(2)}, u32[]{:S(2)}) collective-permute-start(bf16[144,128]{1,0:T(8,128)(2,1)S(1)} %kept.1.refs_0_), channel_id=1, source_target_pairs={{0,24},{4,28},{8,16},{12,20},{16,8},{20,12},{24,0},{28,4},{1,25},{... | collective-permute-start | bytes 110600 | tf_op jit(solution)/shard_map/ppermute | solution.py:24
  45.6 2.4 %residue.1 = (bf16[2048,512]{1,0:T(8,128)(2,1)}, f32[8,128]{1,0:T(8,128)S(1)}) custom-call(bf16[128,512]{1,0:T(8,128)(2,1)S(1)} %slope.1.refs_0_, bf16[128,512]{1,0:T(8,128)(2,1)S(1)} %collective-permute-done.12.refs_1_, bf16[128,512]{1,0:T(8,128)(2,1)S(1)} %collective-permute-done.10.refs_0_.refs_2_, ...), custom_call_target="tpu_custom_call" | custom-call | flops 1000 | bytes 1000 | tf_op jit(solution)/shard_map/residue/pallas_call | solution.py:269
  48.0 1.1 %collective-permute-done.14.refs_1_ = bf16[144,128]{1,0:T(8,128)(2,1)S(1)} collective-permute-done((bf16[144,128]{1,0:T(8,128)(2,1)S(1)}, bf16[144,128]{1,0:T(8,128)(2,1)S(1)}, u32[]{:S(2)}, u32[]{:S(2)}) %collective-permute-start.14) | collective-permute-done | bytes 36896 | tf_op jit(solution)/shard_map/ppermute | solution.py:24
  49.1 4.3 %collective-permute-start.16 = (bf16[576,128]{1,0:T(8,128)(2,1)S(1)}, bf16[576,128]{1,0:T(8,128)(2,1)S(1)}, u32[]{:S(2)}, u32[]{:S(2)}) collective-permute-start(bf16[576,128]{1,0:T(8,128)(2,1)S(1)} %join.5.group), channel_id=1, source_target_pairs={{0,4},{4,0},{8,12},{12,8},{16,20},{20,16},{24,28},{28,24},{1,5},{5... | collective-permute-start | bytes 442376 | tf_op jit(solution)/shard_map/ppermute | solution.py:24
  53.4 1.4 %half.1 = f32[2048,512]{1,0:T(8,128)S(1)} custom-call(bf16[576,128]{1,0:T(8,128)(2,1)S(1)} %join.5.group), custom_call_target="tpu_custom_call" | custom-call | flops 1000 | bytes 1000 | tf_op jit(solution)/shard_map/half/pallas_call | solution.py:351
  54.8 2.6 %outer.1 = f32[2048,512]{1,0:T(8,128)} custom-call(bf16[576,128]{1,0:T(8,128)(2,1)S(1)} %collective-permute-done.16.group, f32[2048,512]{1,0:T(8,128)S(1)} %half.1), custom_call_target="tpu_custom_call" | custom-call | flops 1000 | bytes 1000 | tf_op jit(solution)/shard_map/outer/pallas_call | solution.py:359
  (36 shorter events, 3.0 us)
Async XLA Ops:
  0.6 7.7 %copy-start.6 = (s32[1,1,128]{2,1,0:T(1,128)S(1)}, s32[1,1,128]{2,1,0:T(1,128)}, u32[]{:S(2)}) copy-start(s32[1,1,128]{2,1,0:T(1,128)} %param.11) | copy-start | bytes 1540
  1.7 14.8 %collective-permute-start = (bf16[128,2048]{1,0:T(8,128)(2,1)S(1)}, bf16[128,2048]{1,0:T(8,128)(2,1)S(1)}, u32[]{:S(2)}, u32[]{:S(2)}) collective-permute-start(bf16[128,2048]{1,0:T(8,128)(2,1)S(1)} %dynamic-slice_bitcast_fusion.refs_0_), channel_id=1, source_target_pairs={{0,3},{1,2},{2,1},{3,0},{4,7},{5,6},{6,5},{7,4},{8,11},{9,10},{10,... | collective-permute-start | bytes 1572872 | tf_op jit(solution)/shard_map/ppermute | solution.py:24
  4.8 1.6 %copy-start = (bf16[1,128,8192]{2,1,0:T(8,128)(2,1)S(1)}, bf16[1,128,8192]{2,1,0:T(8,128)(2,1)}, u32[]{:S(2)}) copy-start(bf16[1,128,8192]{2,1,0:T(8,128)(2,1)} %param.6) | copy-start | bytes 6291460
  6.4 4.7 %copy-start.1 = (bf16[1,128,8192]{2,1,0:T(8,128)(2,1)S(1)}, bf16[1,128,8192]{2,1,0:T(8,128)(2,1)}, u32[]{:S(2)}) copy-start(bf16[1,128,8192]{2,1,0:T(8,128)(2,1)} %param.6) | copy-start | bytes 6291460
  7.3 17.7 %collective-permute-start.2 = (bf16[96,2048]{1,0:T(8,128)(2,1)}, bf16[96,2048]{1,0:T(8,128)(2,1)}, u32[]{:S(2)}, u32[]{:S(2)}) collective-permute-start(bf16[96,2048]{1,0:T(8,128)(2,1)} %get-tuple-element.35), channel_id=1, source_target_pairs={{0,1},{1,0},{2,3},{3,2},{4,5},{5,4},{6,7},{7,6},{8,9},{9,8},{10,11... | collective-permute-start | bytes 1179656 | tf_op jit(solution)/shard_map/ppermute | solution.py:24
  7.6 18.1 %collective-permute-start.3 = (bf16[96,2048]{1,0:T(8,128)(2,1)}, bf16[96,2048]{1,0:T(8,128)(2,1)}, u32[]{:S(2)}, u32[]{:S(2)}) collective-permute-start(bf16[96,2048]{1,0:T(8,128)(2,1)} %get-tuple-element.36), channel_id=1, source_target_pairs={{0,2},{1,3},{2,0},{3,1},{4,6},{5,7},{6,4},{7,5},{8,10},{9,11},{10,... | collective-permute-start | bytes 1179656 | tf_op jit(solution)/shard_map/ppermute | solution.py:24
  8.4 1.6 %copy-start.3 = (bf16[1,2048,512]{2,1,0:T(8,128)(2,1)S(1)}, bf16[1,2048,512]{2,1,0:T(8,128)(2,1)}, u32[]{:S(2)}) copy-start(bf16[1,2048,512]{2,1,0:T(8,128)(2,1)} %param.9) | copy-start | bytes 6291460
  11.1 5.4 %copy-start.2 = (bf16[1,2048,512]{2,1,0:T(8,128)(2,1)S(1)}, bf16[1,2048,512]{2,1,0:T(8,128)(2,1)}, u32[]{:S(2)}) copy-start(bf16[1,2048,512]{2,1,0:T(8,128)(2,1)} %param.8) | copy-start | bytes 6291460
  11.2 18.9 %collective-permute-start.5 = (bf16[32,2048]{1,0:T(8,128)(2,1)S(1)}, bf16[32,2048]{1,0:T(8,128)(2,1)S(1)}, u32[]{:S(2)}, u32[]{:S(2)}) collective-permute-start(bf16[32,2048]{1,0:T(8,128)(2,1)S(1)} %get-tuple-element.40), channel_id=1, source_target_pairs={{0,1},{1,0},{2,3},{3,2},{4,5},{5,4},{6,7},{7,6},{8,9},{9,8},{10,11... | collective-permute-start | bytes 393224 | tf_op jit(solution)/shard_map/ppermute | solution.py:24
  12.7 17.5 %collective-permute-start.6 = (bf16[32,2048]{1,0:T(8,128)(2,1)S(1)}, bf16[32,2048]{1,0:T(8,128)(2,1)S(1)}, u32[]{:S(2)}, u32[]{:S(2)}) collective-permute-start(bf16[32,2048]{1,0:T(8,128)(2,1)S(1)} %get-tuple-element.41), channel_id=1, source_target_pairs={{0,2},{1,3},{2,0},{3,1},{4,6},{5,7},{6,4},{7,5},{8,10},{9,11},{10,... | collective-permute-start | bytes 393224 | tf_op jit(solution)/shard_map/ppermute | solution.py:24
  17.2 17.3 %collective-permute-start.1 = (bf16[128,512]{1,0:T(8,128)(2,1)S(1)}, bf16[128,512]{1,0:T(8,128)(2,1)S(1)}, u32[]{:S(2)}, u32[]{:S(2)}) collective-permute-start(bf16[128,512]{1,0:T(8,128)(2,1)S(1)} %get-tuple-element.34), channel_id=1, source_target_pairs={{0,3},{1,2},{2,1},{3,0},{4,7},{5,6},{6,5},{7,4},{8,11},{9,10},{10,... | collective-permute-start | bytes 393224 | tf_op jit(solution)/shard_map/ppermute | solution.py:24
  27.4 7.1 %copy-start.5 = (bf16[1,128,512]{2,1,0:T(8,128)(2,1)S(1)}, bf16[1,128,512]{2,1,0:T(8,128)(2,1)}, u32[]{:S(2)}) copy-start(bf16[1,128,512]{2,1,0:T(8,128)(2,1)} %param.7) | copy-start | bytes 393220
  27.4 7.0 %collective-permute-start.4 = (bf16[96,512]{1,0:T(8,128)(2,1)S(1)}, bf16[96,512]{1,0:T(8,128)(2,1)S(1)}, u32[]{:S(2)}, u32[]{:S(2)}) collective-permute-start(bf16[96,512]{1,0:T(8,128)(2,1)S(1)} %get-tuple-element.39), channel_id=1, source_target_pairs={{0,1},{1,0},{2,3},{3,2},{4,5},{5,4},{6,7},{7,6},{8,9},{9,8},{10,11... | collective-permute-start | bytes 294920 | tf_op jit(solution)/shard_map/ppermute | solution.py:24
  28.9 5.6 %collective-permute-start.8 = (bf16[96,512]{1,0:T(8,128)(2,1)S(1)}, bf16[96,512]{1,0:T(8,128)(2,1)S(1)}, u32[]{:S(2)}, u32[]{:S(2)}) collective-permute-start(bf16[96,512]{1,0:T(8,128)(2,1)S(1)} %get-tuple-element.42.refs_3_), channel_id=1, source_target_pairs={{0,2},{1,3},{2,0},{3,1},{4,6},{5,7},{6,4},{7,5},{8,10},{9,11},{10,... | collective-permute-start | bytes 294920 | tf_op jit(solution)/shard_map/ppermute | solution.py:24
  30.6 14.9 %copy-start.4 = (bf16[1,2048,512]{2,1,0:T(8,128)(2,1)S(1)}, bf16[1,2048,512]{2,1,0:T(8,128)(2,1)}, u32[]{:S(2)}) copy-start(bf16[1,2048,512]{2,1,0:T(8,128)(2,1)} %param.9) | copy-start | bytes 6291460
  30.6 3.1 %collective-permute-start.9 = (bf16[32,512]{1,0:T(8,128)(2,1)S(1)}, bf16[32,512]{1,0:T(8,128)(2,1)S(1)}, u32[]{:S(2)}, u32[]{:S(2)}) collective-permute-start(bf16[32,512]{1,0:T(8,128)(2,1)S(1)} %get-tuple-element.44), channel_id=1, source_target_pairs={{0,2},{1,3},{2,0},{3,1},{4,6},{5,7},{6,4},{7,5},{8,10},{9,11},{10,... | collective-permute-start | bytes 98312 | tf_op jit(solution)/shard_map/ppermute | solution.py:24
  31.4 3.1 %collective-permute-start.7 = (bf16[32,512]{1,0:T(8,128)(2,1)S(1)}, bf16[32,512]{1,0:T(8,128)(2,1)S(1)}, u32[]{:S(2)}, u32[]{:S(2)}) collective-permute-start(bf16[32,512]{1,0:T(8,128)(2,1)S(1)} %get-tuple-element.43.refs_4_), channel_id=1, source_target_pairs={{0,1},{1,0},{2,3},{3,2},{4,5},{5,4},{6,7},{7,6},{8,9},{9,8},{10,11... | collective-permute-start | bytes 98312 | tf_op jit(solution)/shard_map/ppermute | solution.py:24
  34.6 4.9 %collective-permute-start.12 = (bf16[128,512]{1,0:T(8,128)(2,1)S(1)}, bf16[128,512]{1,0:T(8,128)(2,1)S(1)}, u32[]{:S(2)}, u32[]{:S(2)}) collective-permute-start(bf16[128,512]{1,0:T(8,128)(2,1)S(1)} %slope.1.refs_0_), channel_id=1, source_target_pairs={{0,3},{1,2},{2,1},{3,0},{4,7},{5,6},{6,5},{7,4},{8,11},{9,10},{10,... | collective-permute-start | bytes 393224 | tf_op jit(solution)/shard_map/ppermute | solution.py:24
  36.1 4.6 %collective-permute-start.11 = (bf16[128,512]{1,0:T(8,128)(2,1)S(1)}, bf16[128,512]{1,0:T(8,128)(2,1)S(1)}, u32[]{:S(2)}, u32[]{:S(2)}) collective-permute-start(bf16[128,512]{1,0:T(8,128)(2,1)S(1)} %slope.1.refs_0_), channel_id=1, source_target_pairs={{0,2},{1,3},{2,0},{3,1},{4,6},{5,7},{6,4},{7,5},{8,10},{9,11},{10,... | collective-permute-start | bytes 393224 | tf_op jit(solution)/shard_map/ppermute | solution.py:24
  37.0 4.6 %collective-permute-start.10 = (bf16[128,512]{1,0:T(8,128)(2,1)S(1)}, bf16[128,512]{1,0:T(8,128)(2,1)S(1)}, u32[]{:S(2)}, u32[]{:S(2)}) collective-permute-start(bf16[128,512]{1,0:T(8,128)(2,1)S(1)} %slope.1.refs_0_), channel_id=1, source_target_pairs={{0,1},{1,0},{2,3},{3,2},{4,5},{5,4},{6,7},{7,6},{8,9},{9,8},{10,11... | collective-permute-start | bytes 393224 | tf_op jit(solution)/shard_map/ppermute | solution.py:24
  41.8 6.1 %collective-permute-start.13 = (bf16[144,128]{1,0:T(8,128)(2,1)S(1)}, bf16[144,128]{1,0:T(8,128)(2,1)S(1)}, u32[]{:S(2)}, u32[]{:S(2)}) collective-permute-start(bf16[144,128]{1,0:T(8,128)(2,1)S(1)} %kept.1.refs_0_), channel_id=1, source_target_pairs={{0,24},{4,28},{8,16},{12,20},{16,8},{20,12},{24,0},{28,4},{1,25},{... | collective-permute-start | bytes 110600 | tf_op jit(solution)/shard_map/ppermute | solution.py:24
  45.2 3.9 %collective-permute-start.14 = (bf16[144,128]{1,0:T(8,128)(2,1)S(1)}, bf16[144,128]{1,0:T(8,128)(2,1)S(1)}, u32[]{:S(2)}, u32[]{:S(2)}) collective-permute-start(bf16[144,128]{1,0:T(8,128)(2,1)S(1)} %kept.1.refs_0_), channel_id=1, source_target_pairs={{0,16},{4,20},{8,24},{12,28},{16,0},{20,4},{24,8},{28,12},{1,17},{... | collective-permute-start | bytes 110600 | tf_op jit(solution)/shard_map/ppermute | solution.py:24
  45.2 3.9 %collective-permute-start.15 = (bf16[144,128]{1,0:T(8,128)(2,1)S(1)}, bf16[144,128]{1,0:T(8,128)(2,1)S(1)}, u32[]{:S(2)}, u32[]{:S(2)}) collective-permute-start(bf16[144,128]{1,0:T(8,128)(2,1)S(1)} %kept.1.refs_0_), channel_id=1, source_target_pairs={{0,8},{4,12},{8,0},{12,4},{16,24},{20,28},{24,16},{28,20},{1,9},{5... | collective-permute-start | bytes 110600 | tf_op jit(solution)/shard_map/ppermute | solution.py:24
  49.1 5.7 %collective-permute-start.16 = (bf16[576,128]{1,0:T(8,128)(2,1)S(1)}, bf16[576,128]{1,0:T(8,128)(2,1)S(1)}, u32[]{:S(2)}, u32[]{:S(2)}) collective-permute-start(bf16[576,128]{1,0:T(8,128)(2,1)S(1)} %join.5.group), channel_id=1, source_target_pairs={{0,4},{4,0},{8,12},{12,8},{16,20},{20,16},{24,28},{28,24},{1,5},{5... | collective-permute-start | bytes 442376 | tf_op jit(solution)/shard_map/ppermute | solution.py:24

commit v8 on v7

--- a/solution.py
+++ b/solution.py
@@ -47,7 +47,7 @@
         in_specs=[ANY] * (1 + len(after)),
         out_specs=[ANY] * len(cuts) + [VMEM],
         scratch_shapes=[pltpu.SemaphoreType.DMA((len(cuts),))],
-        compiler_params=params(16),
+        compiler_params=params(6),
         cost_estimate=BRIEF,
         name="cut",
     )(tokens, *after)
@@ -75,7 +75,7 @@
         out_shape=[jax.ShapeDtypeStruct((p.shape[0], kw), t) for p, t in zip(pieces, types)]
         + [jax.ShapeDtypeStruct((rows, depth), jnp.bfloat16)],
         in_specs=[VMEM] * (n + 1) + [ANY] * len(after),
-        compiler_params=params(24),
+        compiler_params=params(14),
         cost_estimate=BRIEF,
         name="project",
     )(*pieces, w, *after)
@@ -107,6 +107,11 @@
     )(goal, mine, *whole, *shares, after)
 
 
+def as_column(row):
+    size = row.shape[1]
+    return jnp.broadcast_to(row.astype(jnp.float32), (size, size)).T.astype(jnp.int32)
+
+
 def pick_columns(wide, column):
     out = jnp.zeros((wide.shape[0], LANES), jnp.float32)
     for c in range(wide.shape[1] // LANES):
@@ -114,11 +119,11 @@
     return out
 
 
-def early_kernel(per_row, slots, slot_row, count, fb, after, fbk, keep, token):
+def early_kernel(per_row, slot_row, count, fb, after, fbk, keep, token):
     token[...] = jnp.zeros_like(token)
     depth, kw = fb.shape
-    cap = slots.shape[0]
-    slot = slots[...]
+    cap = slot_row.shape[1]
+    slot = as_column(slot_row[...])[:, 0:1]
     hot = slot // per_row == lax.broadcasted_iota(jnp.int32, (cap, depth), 1)
     hot = hot.astype(jnp.float32).astype(jnp.bfloat16)
     used = lax.broadcasted_iota(jnp.int32, (cap, 1), 0) < count[0, 0]
@@ -134,9 +139,9 @@
         keep[t * tile : (t + 1) * tile, :] = (1.0 - mask).astype(jnp.bfloat16)
 
 
-def early(slots, slot_row, count, fb, after):
+def early(slot_row, count, fb, after):
     depth, kw = fb.shape
-    cap = slots.shape[0]
+    cap = slot_row.shape[1]
     return pl.pallas_call(
         functools.partial(early_kernel, kw // LANES),
         out_shape=[
@@ -144,20 +149,20 @@
             jax.ShapeDtypeStruct((depth, kw), jnp.bfloat16),
             TOKEN,
         ],
-        in_specs=[VMEM, VMEM, SMEM, VMEM, ANY],
-        compiler_params=params(24),
+        in_specs=[VMEM, SMEM, VMEM, ANY],
+        compiler_params=params(14),
         cost_estimate=BRIEF,
         name="early",
-    )(slots, slot_row, count, fb, after)
+    )(slot_row, count, fb, after)
 
 
 def prepare_kernel(per_row, n, *refs):
-    xs, (slots, count), (xg, xt, token) = refs[:n], refs[n : n + 2], refs[-3:]
+    xs, (slot_row, count), (xg, xt, token) = refs[:n], refs[n : n + 2], refs[-3:]
     token[...] = jnp.zeros_like(token)
     depth = xs[0].shape[1]
-    cap = slots.shape[0]
+    cap = slot_row.shape[1]
     used = lax.broadcasted_iota(jnp.int32, (cap, 1), 0) < count[0, 0]
-    line = jnp.where(used, slots[...] // per_row, depth)
+    line = jnp.where(used, as_column(slot_row[...])[:, 0:1] // per_row, depth)
     hot = line == lax.broadcasted_iota(jnp.int32, (cap, depth), 1)
     hot = hot.astype(jnp.float32).astype(jnp.bfloat16)
     start = 0
@@ -170,9 +175,9 @@
         start += rows
 
 
-def prepare(xs, slots, count, per_row, after):
+def prepare(xs, slot_row, count, per_row, after):
     rows, depth = sum(x.shape[0] for x in xs), xs[0].shape[1]
-    cap = slots.shape[0]
+    cap = slot_row.shape[1]
     return pl.pallas_call(
         functools.partial(prepare_kernel, per_row, len(xs)),
         out_shape=[
@@ -181,10 +186,10 @@
             TOKEN,
         ],
         in_specs=[VMEM] * (len(xs) + 1) + [SMEM] + [ANY] * len(after),
-        compiler_params=params(24),
+        compiler_params=params(14),
         cost_estimate=BRIEF,
         name="prepare",
-    )(*xs, slots, count, *after)
+    )(*xs, slot_row, count, *after)
 
 
 def stack(slopes, order, s):
@@ -213,11 +218,11 @@
 
 
 def kept_kernel(per_row, order, *refs):
-    slopes, (wide, xg, fbk, slots, slot_row, out, s) = refs[:-7], refs[-7:]
-    cap = slots.shape[0]
+    slopes, (wide, xg, fbk, slot_row, out, s) = refs[:-6], refs[-6:]
+    cap = slot_row.shape[1]
     stack(slopes, order, s)
     total = wide[...] + jnp.dot(xg[...], s[...], preferred_element_type=jnp.float32)
-    value = pick_columns(total, slots[...] % per_row) + fbk[...]
+    value = pick_columns(total, as_column(slot_row[...])[:, 0:1] % per_row) + fbk[...]
     out[:cap, :] = value.astype(jnp.bfloat16)
     tail = out.shape[0] - cap
     number = jnp.broadcast_to(slot_row[...], (tail, cap))
@@ -226,7 +231,7 @@
     out[cap:, :] = number.astype(jnp.float32).astype(jnp.bfloat16)
 
 
-def kept(slopes, order, wide, xg, fbk, slots, slot_row):
+def kept(slopes, order, wide, xg, fbk, slot_row):
     cap, kw = wide.shape
     return pl.pallas_call(
         functools.partial(kept_kernel, kw // LANES, order),
@@ -235,7 +240,7 @@
         compiler_params=params(8),
         cost_estimate=BRIEF,
         name="kept",
-    )(*slopes, wide, xg, fbk, slots, slot_row)
+    )(*slopes, wide, xg, fbk, slot_row)
 
 
 def send_out(held, out, sems, t, tile):
@@ -279,7 +284,7 @@
             pltpu.VMEM((depth, kw), jnp.bfloat16),
             pltpu.SemaphoreType.DMA((depth // tile,)),
         ],
-        compiler_params=params(24),
+        compiler_params=params(14),
         cost_estimate=BRIEF,
         name="residue",
     )(*slopes, *xts, fb, keep)
@@ -352,7 +357,7 @@
         functools.partial(half_kernel, cap, kw // LANES, tile),
         out_shape=shape,
         scratch_shapes=scratch,
-        compiler_params=params(24),
+        compiler_params=params(14),
         cost_estimate=BRIEF,
         name="half",
     )(groups[0])
@@ -362,7 +367,7 @@
         out_specs=ANY,
         scratch_shapes=scratch
         + [pltpu.VMEM((depth, kw), jnp.float32), pltpu.SemaphoreType.DMA((depth // tile,))],
-        compiler_params=params(24),
+        compiler_params=params(14),
         cost_estimate=BRIEF,
         name="outer",
     )(groups[1], half)
@@ -377,7 +382,6 @@
     spans = [(0, early_rows), (early_rows, tok_dev)]
     per_row = kw // LANES
     slot_row = blocks[0]
-    slots = blocks.reshape(-1, 1)
     near = [d for d in range(1, n_shard) if d & (d - 1) == 0]
     far = [d for d in range(1, n_shard) if d & (d - 1) != 0]
 
@@ -389,7 +393,7 @@
         *out, token = cut(tokens, depth, [(d, low, high - low) for d in near], [token])
         near_out.append(out)
         if low == 0:
-            fbk, keep, token = early(slots, slot_row, counts, fb, token)
+            fbk, keep, token = early(slot_row, counts, fb, token)
     near_in = [[swap(x, "shard", n_shard, d) for x, d in zip(out, near)] for out in near_out]
 
     own, _ = cut(tokens, depth, [(0, 0, tok_dev)], [token])
@@ -397,14 +401,14 @@
     brief, wide = jnp.bfloat16, jnp.float32
     (mine, *products), x_far = project([own] + far_in, [wide] + [brief] * len(far), w, [])
     whole = [swap(p, "shard", n_shard, d) for p, d in zip(products, far)]
-    xg_far, xt_far, token = prepare([x_far], slots, counts, per_row, [])
+    xg_far, xt_far, token = prepare([x_far], slot_row, counts, per_row, [])
     after, shares, x_near = [token], [], []
     for part in range(len(spans)):
         products, x = project(near_in[part], [brief] * len(near), w, after)
         shares.append([swap(p, "shard", n_shard, d) for p, d in zip(products, near)])
         x_near.append(x)
         after = products[-1:]
-    xg_near, xt_near, token = prepare(x_near, slots, counts, per_row, [products[0]])
+    xg_near, xt_near, token = prepare(x_near, slot_row, counts, per_row, [products[0]])
     shares = [share[k] for k in range(len(near)) for share in shares]
     slopes = slope(target[0], mine, whole, shares, spans, token)
     slopes = [slopes] + [swap(slopes, "shard", n_shard, d) for d in far + near]
@@ -413,7 +417,7 @@
     order_far = [(k, 0, tok_dev) for k in range(n_far)]
     order_near = [(k, low, high) for low, high in spans for k in range(len(near))]
     wide = gather(slopes[:n_far], order_far, xg_far)
-    message = kept(slopes[n_far:], order_near, wide, xg_near, fbk, slots, slot_row)
+    message = kept(slopes[n_far:], order_near, wide, xg_near, fbk, slot_row)
     same_core = [swap(message, "rep", n_rep, d) for d in range(n_rep - 2, 0, -2)]
     order = order_far + [(n_far + k, low, high) for k, low, high in order_near]
     new_feedback, token = residue(slopes, order, [xt_far, xt_near], fb, keep)

time: 57.7 us -> 57.6 us (level)
  waiting for transfers between devices: 13.9 us -> 15.8 us
  Pallas kernels: 13.9 us -> 12.3 us
    ppermute x17, waiting for transfers between devices: 13.9 us -> 15.8 us  [swap(): return lax.ppermute(x, axis, [(i, i ^ d) for i in range(n)])]
    pallas_call x3, Pallas kernels: 2.87 us -> 1.76 us  [project(): pl.pallas_call(functools.partial(project_kernel, n), out_shape=[jax.Shape...]
    pallas_call x3, Pallas kernels: 1.64 us -> 0.83 us  [cut(): pl.pallas_call(functools.partial(cut_kernel, cuts), out_shape=[jax.ShapeD...]
  transfers between devices with their start and end apart: 17 -> 17, of which waited for: 9 -> 9; matrix products, arithmetic and copies ran while one was open for 0% -> 0% of each run, Pallas kernels for 19% -> 16%
where the time goes in v8:
time: 57.6 us; the launch traced here: 57.4 us
  starting transfers between devices  23.4 us (41%)
  waiting for transfers between devices  15.8 us (27%)
  Pallas kernels  12.3 us (21%)
  local copies, waits for them, and re-layouts  4.29 us (7%)
  between operations  1.69 us (3%)
    ppermute x17, starting transfers between devices, swap(): return lax.ppermute(x, axis, [(i, i ^ d) for i in range(n)])  23.4 us
    ppermute x17, waiting for transfers between devices, swap(): return lax.ppermute(x, axis, [(i, i ^ d) for i in range(n)])  15.8 us
    unnamed x14, local copies, waits for them, and re-layouts  3.2 us
    pallas_call x1, Pallas kernels, outer(): pl.pallas_call(functools.partial(outer_kernel, cap, kw // LANES, tile, n)...  2.65 us
    pallas_call x1, Pallas kernels, residue(): pl.pallas_call(functools.partial(residue_kernel, order, tile), out_shape=...  2.4 us
    pallas_call x3, Pallas kernels, project(): pl.pallas_call(functools.partial(project_kernel, n), out_shape=[jax.Shape...  1.76 us
    pallas_call x2, Pallas kernels, prepare(): pl.pallas_call(functools.partial(prepare_kernel, per_row, len(xs)), out_s...  1.55 us
    pallas_call x1, Pallas kernels, outer(): pl.pallas_call(functools.partial(half_kernel, cap, kw // LANES, tile), ou...  1.42 us
  transfers between devices with their start and end apart: 17, of which 9 were waited for; matrix products, arithmetic and copies ran while one was open for 0% of the time, Pallas kernels for 16%

profile of v8, /device:TPU:1, one launch (start us, length us, event | category | flops | bytes accessed | tf_op | source)
XLA Modules:
  0.0 57.4 jit_solution(5277821571915621425)
XLA Ops:
  0.6 1.1 %dynamic-slice_bitcast_fusion.refs_0_ = bf16[128,2048]{1,0:T(8,128)(2,1)S(1)} fusion(bf16[1,128,8192]{2,1,0:T(8,128)(2,1)} %param.6, s32[]{:T(128)S(6)} %select_n.3), kind=kLoop, calls=%fused_computation | loop fusion | bytes 1048580 | tf_op jit(solution)/shard_map/dynamic_slice | solution.py:389
  1.7 3.1 %collective-permute-start = (bf16[128,2048]{1,0:T(8,128)(2,1)S(1)}, bf16[128,2048]{1,0:T(8,128)(2,1)S(1)}, u32[]{:S(2)}, u32[]{:S(2)}) collective-permute-start(bf16[128,2048]{1,0:T(8,128)(2,1)S(1)} %dynamic-slice_bitcast_fusion.refs_0_), channel_id=1, source_target_pairs={{0,3},{1,2},{2,1},{3,0},{4,7},{5,6},{6,5},{7,4},{8,11},{9,10},{10,... | collective-permute-start | bytes 1572872 | tf_op jit(solution)/shard_map/ppermute | solution.py:24
  4.8 1.6 %copy-done = bf16[1,128,8192]{2,1,0:T(8,128)(2,1)S(1)} copy-done((bf16[1,128,8192]{2,1,0:T(8,128)(2,1)S(1)}, bf16[1,128,8192]{2,1,0:T(8,128)(2,1)}, u32[]{:S(2)}) %copy-start) | copy-done | bytes 2097176
  7.7 1.6 %copy-done.3 = bf16[1,2048,512]{2,1,0:T(8,128)(2,1)S(1)} copy-done((bf16[1,2048,512]{2,1,0:T(8,128)(2,1)S(1)}, bf16[1,2048,512]{2,1,0:T(8,128)(2,1)}, u32[]{:S(2)}) %copy-start.3) | copy-done | bytes 2097176
  9.3 1.1 %early.1 = (f32[128,128]{1,0:T(8,128)S(1)}, bf16[2048,512]{1,0:T(8,128)(2,1)S(1)}, f32[8,128]{1,0:T(8,128)S(1)}) custom-call(s32[1,128]{1,0:T(1,128)S(1)} %bitcast.17, s32[1,1]{1,0:T(1,128)S(6)} %copy.8.count.refs_2_.refs_3_, bf16[2048,512]{1,0:T(8,128)(2,1)S(1)} %bitcast.14, f32[8,128]{1,0:T(8,128)S(1)} %get-tuple-element.29.after), custom_call_target="tpu_custom_call" | custom-call | flops 1000 | bytes 1000 | tf_op jit(solution)/shard_map/early/pallas_call | solution.py:145
  10.5 1.3 %collective-permute-start.5 = (bf16[32,2048]{1,0:T(8,128)(2,1)S(1)}, bf16[32,2048]{1,0:T(8,128)(2,1)S(1)}, u32[]{:S(2)}, u32[]{:S(2)}) collective-permute-start(bf16[32,2048]{1,0:T(8,128)(2,1)S(1)} %get-tuple-element.40), channel_id=1, source_target_pairs={{0,1},{1,0},{2,3},{3,2},{4,5},{5,4},{6,7},{7,6},{8,9},{9,8},{10,11... | collective-permute-start | bytes 393224 | tf_op jit(solution)/shard_map/ppermute | solution.py:24
  11.8 1.2 %collective-permute-start.6 = (bf16[32,2048]{1,0:T(8,128)(2,1)S(1)}, bf16[32,2048]{1,0:T(8,128)(2,1)S(1)}, u32[]{:S(2)}, u32[]{:S(2)}) collective-permute-start(bf16[32,2048]{1,0:T(8,128)(2,1)S(1)} %get-tuple-element.41), channel_id=1, source_target_pairs={{0,2},{1,3},{2,0},{3,1},{4,6},{5,7},{6,4},{7,5},{8,10},{9,11},{10,... | collective-permute-start | bytes 393224 | tf_op jit(solution)/shard_map/ppermute | solution.py:24
  13.1 0.6 %cut.5 = (bf16[128,2048]{1,0:T(8,128)(2,1)S(1)}, f32[8,128]{1,0:T(8,128)}) custom-call(bf16[128,8192]{1,0:T(8,128)(2,1)S(1)} %bitcast.10, f32[8,128]{1,0:T(8,128)S(1)} %get-tuple-element.31.refs_0_), custom_call_target="tpu_custom_call" | custom-call | flops 1000 | bytes 1000 | tf_op jit(solution)/shard_map/cut/pallas_call | solution.py:43
  13.7 2.8 %collective-permute-done.refs_1_ = bf16[128,2048]{1,0:T(8,128)(2,1)S(1)} collective-permute-done((bf16[128,2048]{1,0:T(8,128)(2,1)S(1)}, bf16[128,2048]{1,0:T(8,128)(2,1)S(1)}, u32[]{:S(2)}, u32[]{:S(2)}) %collective-permute-start) | collective-permute-done | bytes 524320 | tf_op jit(solution)/shard_map/ppermute | solution.py:24
  16.5 0.7 %project.3 = (f32[128,512]{1,0:T(8,128)S(1)}, bf16[128,512]{1,0:T(8,128)(2,1)S(1)}, bf16[256,2048]{1,0:T(8,128)(2,1)S(1)}) custom-call(bf16[128,2048]{1,0:T(8,128)(2,1)S(1)} %get-tuple-element.32.refs_0_, bf16[128,2048]{1,0:T(8,128)(2,1)S(1)} %collective-permute-done.refs_1_, bf16[2048,512]{1,0:T(8,128)(2,1)S(1)} %bitcast.11), custom_call_target="tpu_custom_call" | custom-call | flops 1000 | bytes 1000 | tf_op jit(solution)/shard_map/project/pallas_call | solution.py:73
  17.2 2.1 %collective-permute-start.1 = (bf16[128,512]{1,0:T(8,128)(2,1)S(1)}, bf16[128,512]{1,0:T(8,128)(2,1)S(1)}, u32[]{:S(2)}, u32[]{:S(2)}) collective-permute-start(bf16[128,512]{1,0:T(8,128)(2,1)S(1)} %get-tuple-element.34), channel_id=1, source_target_pairs={{0,3},{1,2},{2,1},{3,0},{4,7},{5,6},{6,5},{7,4},{8,11},{9,10},{10,... | collective-permute-start | bytes 393224 | tf_op jit(solution)/shard_map/ppermute | solution.py:24
  19.3 0.6 %prepare.2 = (bf16[128,256]{1,0:T(8,128)(2,1)S(1)}, bf16[2048,256]{1,0:T(8,128)(2,1)S(1)}, f32[8,128]{1,0:T(8,128)S(1)}) custom-call(bf16[256,2048]{1,0:T(8,128)(2,1)S(1)} %get-tuple-element.37.refs_0_, s32[1,128]{1,0:T(1,128)S(1)} %bitcast.18, s32[1,1]{1,0:T(1,128)S(6)} %copy.8.count.refs_2_.refs_3_), custom_call_target="tpu_custom_call" | custom-call | flops 1000 | bytes 1000 | tf_op jit(solution)/shard_map/prepare/pallas_call | solution.py:181
  19.9 4.9 %collective-permute-done.2.refs_0_ = bf16[96,2048]{1,0:T(8,128)(2,1)S(1)} collective-permute-done((bf16[96,2048]{1,0:T(8,128)(2,1)S(1)}, bf16[96,2048]{1,0:T(8,128)(2,1)S(1)}, u32[]{:S(2)}, u32[]{:S(2)}) %collective-permute-start.2) | collective-permute-done | bytes 393248 | tf_op jit(solution)/shard_map/ppermute | solution.py:24
  24.8 0.8 %collective-permute-done.3.refs_1_ = bf16[96,2048]{1,0:T(8,128)(2,1)S(1)} collective-permute-done((bf16[96,2048]{1,0:T(8,128)(2,1)S(1)}, bf16[96,2048]{1,0:T(8,128)(2,1)S(1)}, u32[]{:S(2)}, u32[]{:S(2)}) %collective-permute-start.3) | collective-permute-done | bytes 393248 | tf_op jit(solution)/shard_map/ppermute | solution.py:24
  25.6 0.6 %project.4 = (bf16[96,512]{1,0:T(8,128)(2,1)S(1)}, bf16[96,512]{1,0:T(8,128)(2,1)S(1)}, bf16[192,2048]{1,0:T(8,128)(2,1)S(1)}) custom-call(bf16[96,2048]{1,0:T(8,128)(2,1)S(1)} %collective-permute-done.2.refs_0_, bf16[96,2048]{1,0:T(8,128)(2,1)S(1)} %collective-permute-done.3.refs_1_, bf16[2048,512]{1,0:T(8,128)(2,1)S(1)} %bitcast.12, ...), custom_call_target="tpu_custom_call" | custom-call | flops 1000 | bytes 1000 | tf_op jit(solution)/shard_map/project/pallas_call | solution.py:73
  26.2 1.5 %collective-permute-start.4 = (bf16[96,512]{1,0:T(8,128)(2,1)S(1)}, bf16[96,512]{1,0:T(8,128)(2,1)S(1)}, u32[]{:S(2)}, u32[]{:S(2)}) collective-permute-start(bf16[96,512]{1,0:T(8,128)(2,1)S(1)} %get-tuple-element.39), channel_id=1, source_target_pairs={{0,1},{1,0},{2,3},{3,2},{4,5},{5,4},{6,7},{7,6},{8,9},{9,8},{10,11... | collective-permute-start | bytes 294920 | tf_op jit(solution)/shard_map/ppermute | solution.py:24
  27.7 1.2 %collective-permute-start.8 = (bf16[96,512]{1,0:T(8,128)(2,1)S(1)}, bf16[96,512]{1,0:T(8,128)(2,1)S(1)}, u32[]{:S(2)}, u32[]{:S(2)}) collective-permute-start(bf16[96,512]{1,0:T(8,128)(2,1)S(1)} %get-tuple-element.42.refs_3_), channel_id=1, source_target_pairs={{0,2},{1,3},{2,0},{3,1},{4,6},{5,7},{6,4},{7,5},{8,10},{9,11},{10,... | collective-permute-start | bytes 294920 | tf_op jit(solution)/shard_map/ppermute | solution.py:24
  29.6 1.8 %collective-permute-start.9 = (bf16[32,512]{1,0:T(8,128)(2,1)S(1)}, bf16[32,512]{1,0:T(8,128)(2,1)S(1)}, u32[]{:S(2)}, u32[]{:S(2)}) collective-permute-start(bf16[32,512]{1,0:T(8,128)(2,1)S(1)} %get-tuple-element.44), channel_id=1, source_target_pairs={{0,2},{1,3},{2,0},{3,1},{4,6},{5,7},{6,4},{7,5},{8,10},{9,11},{10,... | collective-permute-start | bytes 98312 | tf_op jit(solution)/shard_map/ppermute | solution.py:24
  31.4 1.2 %collective-permute-start.7 = (bf16[32,512]{1,0:T(8,128)(2,1)S(1)}, bf16[32,512]{1,0:T(8,128)(2,1)S(1)}, u32[]{:S(2)}, u32[]{:S(2)}) collective-permute-start(bf16[32,512]{1,0:T(8,128)(2,1)S(1)} %get-tuple-element.43.refs_4_), channel_id=1, source_target_pairs={{0,1},{1,0},{2,3},{3,2},{4,5},{5,4},{6,7},{7,6},{8,9},{9,8},{10,11... | collective-permute-start | bytes 98312 | tf_op jit(solution)/shard_map/ppermute | solution.py:24
  32.6 0.9 %prepare.3 = (bf16[128,256]{1,0:T(8,128)(2,1)S(1)}, bf16[2048,256]{1,0:T(8,128)(2,1)S(1)}, f32[8,128]{1,0:T(8,128)S(1)}) custom-call(bf16[192,2048]{1,0:T(8,128)(2,1)S(1)} %get-tuple-element.45.refs_0_, bf16[64,2048]{1,0:T(8,128)(2,1)S(1)} %get-tuple-element.46.refs_1_, s32[1,128]{1,0:T(1,128)S(1)} %bitcast.19, s32[1,1]{1,0:T(1,128)S(6)} %copy.8.count.refs_2_.refs_3_, ...), custom_call_target="tpu_custom_call" | custom-call | flops 1000 | bytes 1000 | tf_op jit(solution)/shard_map/prepare/pallas_call | solution.py:181
  33.6 0.9 %collective-permute-done.7.refs_4_ = bf16[32,512]{1,0:T(8,128)(2,1)S(1)} collective-permute-done((bf16[32,512]{1,0:T(8,128)(2,1)S(1)}, bf16[32,512]{1,0:T(8,128)(2,1)S(1)}, u32[]{:S(2)}, u32[]{:S(2)}) %collective-permute-start.7) | collective-permute-done | bytes 32800 | tf_op jit(solution)/shard_map/ppermute | solution.py:24
  34.6 1.7 %collective-permute-start.12 = (bf16[128,512]{1,0:T(8,128)(2,1)S(1)}, bf16[128,512]{1,0:T(8,128)(2,1)S(1)}, u32[]{:S(2)}, u32[]{:S(2)}) collective-permute-start(bf16[128,512]{1,0:T(8,128)(2,1)S(1)} %slope.1.refs_0_), channel_id=1, source_target_pairs={{0,3},{1,2},{2,1},{3,0},{4,7},{5,6},{6,5},{7,4},{8,11},{9,10},{10,... | collective-permute-start | bytes 393224 | tf_op jit(solution)/shard_map/ppermute | solution.py:24
  36.3 0.8 %collective-permute-start.11 = (bf16[128,512]{1,0:T(8,128)(2,1)S(1)}, bf16[128,512]{1,0:T(8,128)(2,1)S(1)}, u32[]{:S(2)}, u32[]{:S(2)}) collective-permute-start(bf16[128,512]{1,0:T(8,128)(2,1)S(1)} %slope.1.refs_0_), channel_id=1, source_target_pairs={{0,2},{1,3},{2,0},{3,1},{4,6},{5,7},{6,4},{7,5},{8,10},{9,11},{10,... | collective-permute-start | bytes 393224 | tf_op jit(solution)/shard_map/ppermute | solution.py:24
  37.3 2.1 %collective-permute-done.12.refs_1_ = bf16[128,512]{1,0:T(8,128)(2,1)S(1)} collective-permute-done((bf16[128,512]{1,0:T(8,128)(2,1)S(1)}, bf16[128,512]{1,0:T(8,128)(2,1)S(1)}, u32[]{:S(2)}, u32[]{:S(2)}) %collective-permute-start.12) | collective-permute-done | bytes 131104 | tf_op jit(solution)/shard_map/ppermute | solution.py:24
  39.6 2.4 %collective-permute-done.11.refs_1_.refs_3_ = bf16[128,512]{1,0:T(8,128)(2,1)S(1)} collective-permute-done((bf16[128,512]{1,0:T(8,128)(2,1)S(1)}, bf16[128,512]{1,0:T(8,128)(2,1)S(1)}, u32[]{:S(2)}, u32[]{:S(2)}) %collective-permute-start.11) | collective-permute-done | bytes 131104 | tf_op jit(solution)/shard_map/ppermute | solution.py:24
  41.9 0.5 collective-permute-done.10.refs_0_.refs_2_
  42.7 3.4 %collective-permute-start.13 = (bf16[144,128]{1,0:T(8,128)(2,1)S(1)}, bf16[144,128]{1,0:T(8,128)(2,1)S(1)}, u32[]{:S(2)}, u32[]{:S(2)}) collective-permute-start(bf16[144,128]{1,0:T(8,128)(2,1)S(1)} %kept.1.refs_0_), channel_id=1, source_target_pairs={{0,24},{4,28},{8,16},{12,20},{16,8},{20,12},{24,0},{28,4},{1,25},{... | collective-permute-start | bytes 110600 | tf_op jit(solution)/shard_map/ppermute | solution.py:24
  46.5 2.4 %residue.1 = (bf16[2048,512]{1,0:T(8,128)(2,1)}, f32[8,128]{1,0:T(8,128)S(1)}) custom-call(bf16[128,512]{1,0:T(8,128)(2,1)S(1)} %slope.1.refs_0_, bf16[128,512]{1,0:T(8,128)(2,1)S(1)} %collective-permute-done.12.refs_1_, bf16[128,512]{1,0:T(8,128)(2,1)S(1)} %collective-permute-done.10.refs_0_.refs_2_, ...), custom_call_target="tpu_custom_call" | custom-call | flops 1000 | bytes 1000 | tf_op jit(solution)/shard_map/residue/pallas_call | solution.py:274
  48.9 1.3 %collective-permute-done.14.refs_1_ = bf16[144,128]{1,0:T(8,128)(2,1)S(1)} collective-permute-done((bf16[144,128]{1,0:T(8,128)(2,1)S(1)}, bf16[144,128]{1,0:T(8,128)(2,1)S(1)}, u32[]{:S(2)}, u32[]{:S(2)}) %collective-permute-start.14) | collective-permute-done | bytes 36896 | tf_op jit(solution)/shard_map/ppermute | solution.py:24
  50.3 3.1 %collective-permute-start.16 = (bf16[576,128]{1,0:T(8,128)(2,1)S(1)}, bf16[576,128]{1,0:T(8,128)(2,1)S(1)}, u32[]{:S(2)}, u32[]{:S(2)}) collective-permute-start(bf16[576,128]{1,0:T(8,128)(2,1)S(1)} %join.5.group), channel_id=1, source_target_pairs={{0,4},{4,0},{8,12},{12,8},{16,20},{20,16},{24,28},{28,24},{1,5},{5... | collective-permute-start | bytes 442376 | tf_op jit(solution)/shard_map/ppermute | solution.py:24
  53.4 1.4 %half.1 = f32[2048,512]{1,0:T(8,128)S(1)} custom-call(bf16[576,128]{1,0:T(8,128)(2,1)S(1)} %join.5.group), custom_call_target="tpu_custom_call" | custom-call | flops 1000 | bytes 1000 | tf_op jit(solution)/shard_map/half/pallas_call | solution.py:356
  54.8 2.7 %outer.1 = f32[2048,512]{1,0:T(8,128)} custom-call(bf16[576,128]{1,0:T(8,128)(2,1)S(1)} %collective-permute-done.16.group, f32[2048,512]{1,0:T(8,128)S(1)} %half.1), custom_call_target="tpu_custom_call" | custom-call | flops 1000 | bytes 1000 | tf_op jit(solution)/shard_map/outer/pallas_call | solution.py:364
  (35 shorter events, 2.5 us)
Async XLA Ops:
  0.6 7.0 %copy-start.6 = (s32[1,1,128]{2,1,0:T(1,128)S(1)}, s32[1,1,128]{2,1,0:T(1,128)}, u32[]{:S(2)}) copy-start(s32[1,1,128]{2,1,0:T(1,128)} %param.11) | copy-start | bytes 1540
  1.7 14.8 %collective-permute-start = (bf16[128,2048]{1,0:T(8,128)(2,1)S(1)}, bf16[128,2048]{1,0:T(8,128)(2,1)S(1)}, u32[]{:S(2)}, u32[]{:S(2)}) collective-permute-start(bf16[128,2048]{1,0:T(8,128)(2,1)S(1)} %dynamic-slice_bitcast_fusion.refs_0_), channel_id=1, source_target_pairs={{0,3},{1,2},{2,1},{3,0},{4,7},{5,6},{6,5},{7,4},{8,11},{9,10},{10,... | collective-permute-start | bytes 1572872 | tf_op jit(solution)/shard_map/ppermute | solution.py:24
  4.8 1.6 %copy-start = (bf16[1,128,8192]{2,1,0:T(8,128)(2,1)S(1)}, bf16[1,128,8192]{2,1,0:T(8,128)(2,1)}, u32[]{:S(2)}) copy-start(bf16[1,128,8192]{2,1,0:T(8,128)(2,1)} %param.6) | copy-start | bytes 6291460
  6.4 4.0 %copy-start.1 = (bf16[1,128,8192]{2,1,0:T(8,128)(2,1)S(1)}, bf16[1,128,8192]{2,1,0:T(8,128)(2,1)}, u32[]{:S(2)}) copy-start(bf16[1,128,8192]{2,1,0:T(8,128)(2,1)} %param.6) | copy-start | bytes 6291460
  6.5 18.4 %collective-permute-start.2 = (bf16[96,2048]{1,0:T(8,128)(2,1)S(1)}, bf16[96,2048]{1,0:T(8,128)(2,1)S(1)}, u32[]{:S(2)}, u32[]{:S(2)}) collective-permute-start(bf16[96,2048]{1,0:T(8,128)(2,1)S(1)} %get-tuple-element.35), channel_id=1, source_target_pairs={{0,1},{1,0},{2,3},{3,2},{4,5},{5,4},{6,7},{7,6},{8,9},{9,8},{10,11... | collective-permute-start | bytes 1179656 | tf_op jit(solution)/shard_map/ppermute | solution.py:24
  6.8 18.8 %collective-permute-start.3 = (bf16[96,2048]{1,0:T(8,128)(2,1)S(1)}, bf16[96,2048]{1,0:T(8,128)(2,1)S(1)}, u32[]{:S(2)}, u32[]{:S(2)}) collective-permute-start(bf16[96,2048]{1,0:T(8,128)(2,1)S(1)} %get-tuple-element.36), channel_id=1, source_target_pairs={{0,2},{1,3},{2,0},{3,1},{4,6},{5,7},{6,4},{7,5},{8,10},{9,11},{10,... | collective-permute-start | bytes 1179656 | tf_op jit(solution)/shard_map/ppermute | solution.py:24
  7.7 1.6 %copy-start.3 = (bf16[1,2048,512]{2,1,0:T(8,128)(2,1)S(1)}, bf16[1,2048,512]{2,1,0:T(8,128)(2,1)}, u32[]{:S(2)}) copy-start(bf16[1,2048,512]{2,1,0:T(8,128)(2,1)} %param.9) | copy-start | bytes 6291460
  10.4 6.1 %copy-start.2 = (bf16[1,2048,512]{2,1,0:T(8,128)(2,1)S(1)}, bf16[1,2048,512]{2,1,0:T(8,128)(2,1)}, u32[]{:S(2)}) copy-start(bf16[1,2048,512]{2,1,0:T(8,128)(2,1)} %param.8) | copy-start | bytes 6291460
  10.5 18.4 %collective-permute-start.5 = (bf16[32,2048]{1,0:T(8,128)(2,1)S(1)}, bf16[32,2048]{1,0:T(8,128)(2,1)S(1)}, u32[]{:S(2)}, u32[]{:S(2)}) collective-permute-start(bf16[32,2048]{1,0:T(8,128)(2,1)S(1)} %get-tuple-element.40), channel_id=1, source_target_pairs={{0,1},{1,0},{2,3},{3,2},{4,5},{5,4},{6,7},{7,6},{8,9},{9,8},{10,11... | collective-permute-start | bytes 393224 | tf_op jit(solution)/shard_map/ppermute | solution.py:24
  11.8 17.3 %collective-permute-start.6 = (bf16[32,2048]{1,0:T(8,128)(2,1)S(1)}, bf16[32,2048]{1,0:T(8,128)(2,1)S(1)}, u32[]{:S(2)}, u32[]{:S(2)}) collective-permute-start(bf16[32,2048]{1,0:T(8,128)(2,1)S(1)} %get-tuple-element.41), channel_id=1, source_target_pairs={{0,2},{1,3},{2,0},{3,1},{4,6},{5,7},{6,4},{7,5},{8,10},{9,11},{10,... | collective-permute-start | bytes 393224 | tf_op jit(solution)/shard_map/ppermute | solution.py:24
  17.2 17.2 %collective-permute-start.1 = (bf16[128,512]{1,0:T(8,128)(2,1)S(1)}, bf16[128,512]{1,0:T(8,128)(2,1)S(1)}, u32[]{:S(2)}, u32[]{:S(2)}) collective-permute-start(bf16[128,512]{1,0:T(8,128)(2,1)S(1)} %get-tuple-element.34), channel_id=1, source_target_pairs={{0,3},{1,2},{2,1},{3,0},{4,7},{5,6},{6,5},{7,4},{8,11},{9,10},{10,... | collective-permute-start | bytes 393224 | tf_op jit(solution)/shard_map/ppermute | solution.py:24
  26.2 8.3 %copy-start.5 = (bf16[1,128,512]{2,1,0:T(8,128)(2,1)S(1)}, bf16[1,128,512]{2,1,0:T(8,128)(2,1)}, u32[]{:S(2)}) copy-start(bf16[1,128,512]{2,1,0:T(8,128)(2,1)} %param.7) | copy-start | bytes 393220
  26.2 8.2 %collective-permute-start.4 = (bf16[96,512]{1,0:T(8,128)(2,1)S(1)}, bf16[96,512]{1,0:T(8,128)(2,1)S(1)}, u32[]{:S(2)}, u32[]{:S(2)}) collective-permute-start(bf16[96,512]{1,0:T(8,128)(2,1)S(1)} %get-tuple-element.39), channel_id=1, source_target_pairs={{0,1},{1,0},{2,3},{3,2},{4,5},{5,4},{6,7},{7,6},{8,9},{9,8},{10,11... | collective-permute-start | bytes 294920 | tf_op jit(solution)/shard_map/ppermute | solution.py:24
  27.7 6.8 %collective-permute-start.8 = (bf16[96,512]{1,0:T(8,128)(2,1)S(1)}, bf16[96,512]{1,0:T(8,128)(2,1)S(1)}, u32[]{:S(2)}, u32[]{:S(2)}) collective-permute-start(bf16[96,512]{1,0:T(8,128)(2,1)S(1)} %get-tuple-element.42.refs_3_), channel_id=1, source_target_pairs={{0,2},{1,3},{2,0},{3,1},{4,6},{5,7},{6,4},{7,5},{8,10},{9,11},{10,... | collective-permute-start | bytes 294920 | tf_op jit(solution)/shard_map/ppermute | solution.py:24
  29.6 16.9 %copy-start.4 = (bf16[1,2048,512]{2,1,0:T(8,128)(2,1)S(1)}, bf16[1,2048,512]{2,1,0:T(8,128)(2,1)}, u32[]{:S(2)}) copy-start(bf16[1,2048,512]{2,1,0:T(8,128)(2,1)} %param.9) | copy-start | bytes 6291460
  29.6 4.0 %collective-permute-start.9 = (bf16[32,512]{1,0:T(8,128)(2,1)S(1)}, bf16[32,512]{1,0:T(8,128)(2,1)S(1)}, u32[]{:S(2)}, u32[]{:S(2)}) collective-permute-start(bf16[32,512]{1,0:T(8,128)(2,1)S(1)} %get-tuple-element.44), channel_id=1, source_target_pairs={{0,2},{1,3},{2,0},{3,1},{4,6},{5,7},{6,4},{7,5},{8,10},{9,11},{10,... | collective-permute-start | bytes 98312 | tf_op jit(solution)/shard_map/ppermute | solution.py:24
  31.4 3.0 %collective-permute-start.7 = (bf16[32,512]{1,0:T(8,128)(2,1)S(1)}, bf16[32,512]{1,0:T(8,128)(2,1)S(1)}, u32[]{:S(2)}, u32[]{:S(2)}) collective-permute-start(bf16[32,512]{1,0:T(8,128)(2,1)S(1)} %get-tuple-element.43.refs_4_), channel_id=1, source_target_pairs={{0,1},{1,0},{2,3},{3,2},{4,5},{5,4},{6,7},{7,6},{8,9},{9,8},{10,11... | collective-permute-start | bytes 98312 | tf_op jit(solution)/shard_map/ppermute | solution.py:24
  34.6 4.9 %collective-permute-start.12 = (bf16[128,512]{1,0:T(8,128)(2,1)S(1)}, bf16[128,512]{1,0:T(8,128)(2,1)S(1)}, u32[]{:S(2)}, u32[]{:S(2)}) collective-permute-start(bf16[128,512]{1,0:T(8,128)(2,1)S(1)} %slope.1.refs_0_), channel_id=1, source_target_pairs={{0,3},{1,2},{2,1},{3,0},{4,7},{5,6},{6,5},{7,4},{8,11},{9,10},{10,... | collective-permute-start | bytes 393224 | tf_op jit(solution)/shard_map/ppermute | solution.py:24
  36.3 5.7 %collective-permute-start.11 = (bf16[128,512]{1,0:T(8,128)(2,1)S(1)}, bf16[128,512]{1,0:T(8,128)(2,1)S(1)}, u32[]{:S(2)}, u32[]{:S(2)}) collective-permute-start(bf16[128,512]{1,0:T(8,128)(2,1)S(1)} %slope.1.refs_0_), channel_id=1, source_target_pairs={{0,2},{1,3},{2,0},{3,1},{4,6},{5,7},{6,4},{7,5},{8,10},{9,11},{10,... | collective-permute-start | bytes 393224 | tf_op jit(solution)/shard_map/ppermute | solution.py:24
  37.0 5.4 %collective-permute-start.10 = (bf16[128,512]{1,0:T(8,128)(2,1)S(1)}, bf16[128,512]{1,0:T(8,128)(2,1)S(1)}, u32[]{:S(2)}, u32[]{:S(2)}) collective-permute-start(bf16[128,512]{1,0:T(8,128)(2,1)S(1)} %slope.1.refs_0_), channel_id=1, source_target_pairs={{0,1},{1,0},{2,3},{3,2},{4,5},{5,4},{6,7},{7,6},{8,9},{9,8},{10,11... | collective-permute-start | bytes 393224 | tf_op jit(solution)/shard_map/ppermute | solution.py:24
  42.7 6.2 %collective-permute-start.13 = (bf16[144,128]{1,0:T(8,128)(2,1)S(1)}, bf16[144,128]{1,0:T(8,128)(2,1)S(1)}, u32[]{:S(2)}, u32[]{:S(2)}) collective-permute-start(bf16[144,128]{1,0:T(8,128)(2,1)S(1)} %kept.1.refs_0_), channel_id=1, source_target_pairs={{0,24},{4,28},{8,16},{12,20},{16,8},{20,12},{24,0},{28,4},{1,25},{... | collective-permute-start | bytes 110600 | tf_op jit(solution)/shard_map/ppermute | solution.py:24
  46.1 4.1 %collective-permute-start.14 = (bf16[144,128]{1,0:T(8,128)(2,1)S(1)}, bf16[144,128]{1,0:T(8,128)(2,1)S(1)}, u32[]{:S(2)}, u32[]{:S(2)}) collective-permute-start(bf16[144,128]{1,0:T(8,128)(2,1)S(1)} %kept.1.refs_0_), channel_id=1, source_target_pairs={{0,16},{4,20},{8,24},{12,28},{16,0},{20,4},{24,8},{28,12},{1,17},{... | collective-permute-start | bytes 110600 | tf_op jit(solution)/shard_map/ppermute | solution.py:24
  46.1 4.1 %collective-permute-start.15 = (bf16[144,128]{1,0:T(8,128)(2,1)S(1)}, bf16[144,128]{1,0:T(8,128)(2,1)S(1)}, u32[]{:S(2)}, u32[]{:S(2)}) collective-permute-start(bf16[144,128]{1,0:T(8,128)(2,1)S(1)} %kept.1.refs_0_), channel_id=1, source_target_pairs={{0,8},{4,12},{8,0},{12,4},{16,24},{20,28},{24,16},{28,20},{1,9},{5... | collective-permute-start | bytes 110600 | tf_op jit(solution)/shard_map/ppermute | solution.py:24
  50.3 4.5 %collective-permute-start.16 = (bf16[576,128]{1,0:T(8,128)(2,1)S(1)}, bf16[576,128]{1,0:T(8,128)(2,1)S(1)}, u32[]{:S(2)}, u32[]{:S(2)}) collective-permute-start(bf16[576,128]{1,0:T(8,128)(2,1)S(1)} %join.5.group), channel_id=1, source_target_pairs={{0,4},{4,0},{8,12},{12,8},{16,20},{20,16},{24,28},{28,24},{1,5},{5... | collective-permute-start | bytes 442376 | tf_op jit(solution)/shard_map/ppermute | solution.py:24

commit v9 on v8

--- a/solution.py
+++ b/solution.py
@@ -192,36 +192,21 @@
     )(*xs, slot_row, count, *after)
 
 
-def stack(slopes, order, s):
+def kept_kernel(per_row, order, slopes, *refs):
+    xgs, (fbk, slot_row, out, s) = refs[:-4], refs[-4:]
+    cap = slot_row.shape[1]
+    me = lax.axis_index("shard")
+    tok_dev = slopes.shape[0] // lax.axis_size("shard")
     start = 0
-    for k, low, high in order:
-        s[start : start + high - low, :] = slopes[k][low:high, :]
+    for d, low, high in order:
+        rows = pl.ds(pl.multiple_of((me ^ d) * tok_dev + low, 16), high - low)
+        s[start : start + high - low, :] = slopes[rows, :]
         start += high - low
-
-
-def gather_kernel(order, *refs):
-    slopes, (xg, out, s) = refs[:-3], refs[-3:]
-    stack(slopes, order, s)
-    out[...] = jnp.dot(xg[...], s[...], preferred_element_type=jnp.float32)
-
-
-def gather(slopes, order, xg):
-    kw = slopes[0].shape[1]
-    return pl.pallas_call(
-        functools.partial(gather_kernel, order),
-        out_shape=jax.ShapeDtypeStruct((xg.shape[0], kw), jnp.float32),
-        scratch_shapes=[pltpu.VMEM((xg.shape[1], kw), jnp.bfloat16)],
-        compiler_params=params(8),
-        cost_estimate=BRIEF,
-        name="gather",
-    )(*slopes, xg)
-
-
-def kept_kernel(per_row, order, *refs):
-    slopes, (wide, xg, fbk, slot_row, out, s) = refs[:-6], refs[-6:]
-    cap = slot_row.shape[1]
-    stack(slopes, order, s)
-    total = wide[...] + jnp.dot(xg[...], s[...], preferred_element_type=jnp.float32)
+    total, start = 0.0, 0
+    for xg in xgs:
+        part = s[start : start + xg.shape[1], :]
+        total += jnp.dot(xg[...], part, preferred_element_type=jnp.float32)
+        start += xg.shape[1]
     value = pick_columns(total, as_column(slot_row[...])[:, 0:1] % per_row) + fbk[...]
     out[:cap, :] = value.astype(jnp.bfloat16)
     tail = out.shape[0] - cap
@@ -231,16 +216,18 @@
     out[cap:, :] = number.astype(jnp.float32).astype(jnp.bfloat16)
 
 
-def kept(slopes, order, wide, xg, fbk, slot_row):
-    cap, kw = wide.shape
-    return pl.pallas_call(
-        functools.partial(kept_kernel, kw // LANES, order),
-        out_shape=jax.ShapeDtypeStruct((cap + 16, LANES), jnp.bfloat16),
-        scratch_shapes=[pltpu.VMEM((xg.shape[1], kw), jnp.bfloat16)],
+def kept(slopes, order, xgs, fbk, slot_row):
+    cap = slot_row.shape[1]
+    return pl.pallas_call(
+        functools.partial(kept_kernel, slopes.shape[1] // LANES, order),
+        out_shape=[
+            jax.ShapeDtypeStruct((cap + 16, LANES), jnp.bfloat16),
+            jax.ShapeDtypeStruct(slopes.shape, jnp.bfloat16),
+        ],
         compiler_params=params(8),
         cost_estimate=BRIEF,
         name="kept",
-    )(*slopes, wide, xg, fbk, slot_row)
+    )(slopes, *xgs, fbk, slot_row)
 
 
 def send_out(held, out, sems, t, tile):
@@ -248,11 +235,9 @@
     return pltpu.make_async_copy(held.at[rows, :], out.at[rows, :], sems.at[t])
 
 
-def residue_kernel(order, tile, *refs):
-    n = len({k for k, _, _ in order})
-    slopes, xts, (fb, keep, out, token, s, held, sems) = refs[:n], refs[n:-7], refs[-7:]
+def residue_kernel(tile, s, *refs):
+    xts, (fb, keep, out, token, held, sems) = refs[:-6], refs[-6:]
     token[...] = jnp.zeros_like(token)
-    stack(slopes, order, s)
     tiles = out.shape[0] // tile
     for t in range(tiles):
         rows = slice(t * tile, (t + 1) * tile)
@@ -267,27 +252,22 @@
         send_out(held, out, sems, t, tile).wait()
 
 
-def residue(slopes, order, xts, fb, keep):
+def residue(s, xts, fb, keep):
     depth, kw = fb.shape
-    total = sum(xt.shape[1] for xt in xts)
     tile = min(depth, 512)
     return pl.pallas_call(
-        functools.partial(residue_kernel, order, tile),
-        out_shape=[
-            jax.ShapeDtypeStruct((depth, kw), jnp.bfloat16),
-            TOKEN,
-        ],
-        in_specs=[VMEM] * (len(slopes) + len(xts) + 2),
+        functools.partial(residue_kernel, tile),
+        out_shape=[jax.ShapeDtypeStruct((depth, kw), jnp.bfloat16), TOKEN],
+        in_specs=[VMEM] * (len(xts) + 3),
         out_specs=[ANY, VMEM],
         scratch_shapes=[
-            pltpu.VMEM((total, kw), jnp.bfloat16),
             pltpu.VMEM((depth, kw), jnp.bfloat16),
             pltpu.SemaphoreType.DMA((depth // tile,)),
         ],
         compiler_params=params(14),
         cost_estimate=BRIEF,
         name="residue",
-    )(*slopes, *xts, fb, keep)
+    )(s, *xts, fb, keep)
 
 
 def join_kernel(n, *refs):
@@ -411,16 +391,13 @@
     xg_near, xt_near, token = prepare(x_near, slot_row, counts, per_row, [products[0]])
     shares = [share[k] for k in range(len(near)) for share in shares]
     slopes = slope(target[0], mine, whole, shares, spans, token)
-    slopes = [slopes] + [swap(slopes, "shard", n_shard, d) for d in far + near]
-
-    n_far = 1 + len(far)
-    order_far = [(k, 0, tok_dev) for k in range(n_far)]
-    order_near = [(k, low, high) for low, high in spans for k in range(len(near))]
-    wide = gather(slopes[:n_far], order_far, xg_far)
-    message = kept(slopes[n_far:], order_near, wide, xg_near, fbk, slot_row)
+    slopes = lax.all_gather(slopes, "shard", axis=0, tiled=True)
+
+    order = [(d, 0, tok_dev) for d in [0] + far]
+    order += [(d, low, high) for low, high in spans for d in near]
+    message, slopes = kept(slopes, order, [xg_far, xg_near], fbk, slot_row)
     same_core = [swap(message, "rep", n_rep, d) for d in range(n_rep - 2, 0, -2)]
-    order = order_far + [(n_far + k, low, high) for k, low, high in order_near]
-    new_feedback, token = residue(slopes, order, [xt_far, xt_near], fb, keep)
+    new_feedback, token = residue(slopes, [xt_far, xt_near], fb, keep)
     joined, after = message, [token]
     for received in same_core:
         joined, after = join([joined, received], after), []

time: 57.6 us -> 60.4 us (1.049)
  blocking collectives: 0 us -> 8.19 us
  waiting for transfers between devices: 15.8 us -> 10.4 us
    all_gather x0 -> x1, blocking collectives: none -> 8.19 us  [on_device(): slopes = lax.all_gather(slopes, 'shard', axis=0, tiled=True)]
    ppermute x17 -> x14, waiting for transfers between devices: 15.8 us -> 10.4 us  [swap(): return lax.ppermute(x, axis, [(i, i ^ d) for i in range(n)])]
    pallas_call x3 -> x2, Pallas kernels: 2.84 us -> 2.67 us  [the longest x1 2.38 us: residue(): pl.pallas_call(functools.partial(residue_kernel, tile), out_shape=[jax.Sh...]
    ppermute x17 -> x14, starting transfers between devices: 23.4 us -> 23.4 us  [swap(): return lax.ppermute(x, axis, [(i, i ^ d) for i in range(n)])]
  transfers between devices with their start and end apart: 17 -> 14, of which waited for: 9 -> 6; matrix products, arithmetic and copies ran while one was open for 0% -> 0% of each run, Pallas kernels for 16% -> 15%
where the time goes in v9:
time: 60.4 us; the launch traced here: 60.1 us
  starting transfers between devices  23.4 us (39%)
  Pallas kernels  12.1 us (20%)
  waiting for transfers between devices  10.4 us (17%)
  blocking collectives  8.19 us (14%)
  local copies, waits for them, and re-layouts  4.29 us (7%)
  between operations  1.68 us (3%)
    ppermute x14, starting transfers between devices, swap(): return lax.ppermute(x, axis, [(i, i ^ d) for i in range(n)])  23.4 us
    ppermute x14, waiting for transfers between devices, swap(): return lax.ppermute(x, axis, [(i, i ^ d) for i in range(n)])  10.4 us
    all_gather x1, blocking collectives, on_device(): slopes = lax.all_gather(slopes, 'shard', axis=0, tiled=True)  8.19 us
    unnamed x14, local copies, waits for them, and re-layouts  3.2 us
    pallas_call x1, Pallas kernels, outer(): pl.pallas_call(functools.partial(outer_kernel, cap, kw // LANES, tile, n)...  2.65 us
    pallas_call x1, Pallas kernels, residue(): pl.pallas_call(functools.partial(residue_kernel, tile), out_shape=[jax.Sh...  2.38 us
    pallas_call x3, Pallas kernels, project(): pl.pallas_call(functools.partial(project_kernel, n), out_shape=[jax.Shape...  1.76 us
    pallas_call x2, Pallas kernels, prepare(): pl.pallas_call(functools.partial(prepare_kernel, per_row, len(xs)), out_s...  1.55 us
  transfers between devices with their start and end apart: 14, of which 6 were waited for; matrix products, arithmetic and copies ran while one was open for 0% of the time, Pallas kernels for 15%

profile of v9, /device:TPU:1, one launch (start us, length us, event | category | flops | bytes accessed | tf_op | source)
XLA Modules:
  0.0 60.1 jit_solution(911544113025705508)
XLA Ops:
  0.6 1.1 %dynamic-slice_bitcast_fusion.refs_0_ = bf16[128,2048]{1,0:T(8,128)(2,1)S(1)} fusion(bf16[1,128,8192]{2,1,0:T(8,128)(2,1)} %param.6, s32[]{:T(128)S(6)} %select_n.3), kind=kLoop, calls=%fused_computation | loop fusion | bytes 1048580 | tf_op jit(solution)/shard_map/dynamic_slice | solution.py:369
  1.7 3.1 %collective-permute-start = (bf16[128,2048]{1,0:T(8,128)(2,1)S(1)}, bf16[128,2048]{1,0:T(8,128)(2,1)S(1)}, u32[]{:S(2)}, u32[]{:S(2)}) collective-permute-start(bf16[128,2048]{1,0:T(8,128)(2,1)S(1)} %dynamic-slice_bitcast_fusion.refs_0_), channel_id=1, source_target_pairs={{0,3},{1,2},{2,1},{3,0},{4,7},{5,6},{6,5},{7,4},{8,11},{9,10},{10,... | collective-permute-start | bytes 1572872 | tf_op jit(solution)/shard_map/ppermute | solution.py:24
  4.8 1.6 %copy-done = bf16[1,128,8192]{2,1,0:T(8,128)(2,1)S(1)} copy-done((bf16[1,128,8192]{2,1,0:T(8,128)(2,1)S(1)}, bf16[1,128,8192]{2,1,0:T(8,128)(2,1)}, u32[]{:S(2)}) %copy-start) | copy-done | bytes 2097176
  6.5 0.3 collective-permute-start.2
  7.7 1.6 %copy-done.3 = bf16[1,2048,512]{2,1,0:T(8,128)(2,1)S(1)} copy-done((bf16[1,2048,512]{2,1,0:T(8,128)(2,1)S(1)}, bf16[1,2048,512]{2,1,0:T(8,128)(2,1)}, u32[]{:S(2)}) %copy-start.3) | copy-done | bytes 2097176
  9.3 1.1 %early.1 = (f32[128,128]{1,0:T(8,128)S(1)}, bf16[2048,512]{1,0:T(8,128)(2,1)S(1)}, f32[8,128]{1,0:T(8,128)S(1)}) custom-call(s32[1,128]{1,0:T(1,128)S(1)} %bitcast.17, s32[1,1]{1,0:T(1,128)S(6)} %copy.8.count.refs_2_.refs_3_, bf16[2048,512]{1,0:T(8,128)(2,1)S(1)} %bitcast.14, f32[8,128]{1,0:T(8,128)S(1)} %get-tuple-element.31.after), custom_call_target="tpu_custom_call" | custom-call | flops 1000 | bytes 1000 | tf_op jit(solution)/shard_map/early/pallas_call | solution.py:145
  10.5 1.3 %collective-permute-start.5 = (bf16[32,2048]{1,0:T(8,128)(2,1)S(1)}, bf16[32,2048]{1,0:T(8,128)(2,1)S(1)}, u32[]{:S(2)}, u32[]{:S(2)}) collective-permute-start(bf16[32,2048]{1,0:T(8,128)(2,1)S(1)} %get-tuple-element.42), channel_id=1, source_target_pairs={{0,1},{1,0},{2,3},{3,2},{4,5},{5,4},{6,7},{7,6},{8,9},{9,8},{10,11... | collective-permute-start | bytes 393224 | tf_op jit(solution)/shard_map/ppermute | solution.py:24
  11.8 1.2 %collective-permute-start.6 = (bf16[32,2048]{1,0:T(8,128)(2,1)S(1)}, bf16[32,2048]{1,0:T(8,128)(2,1)S(1)}, u32[]{:S(2)}, u32[]{:S(2)}) collective-permute-start(bf16[32,2048]{1,0:T(8,128)(2,1)S(1)} %get-tuple-element.43), channel_id=1, source_target_pairs={{0,2},{1,3},{2,0},{3,1},{4,6},{5,7},{6,4},{7,5},{8,10},{9,11},{10,... | collective-permute-start | bytes 393224 | tf_op jit(solution)/shard_map/ppermute | solution.py:24
  13.1 0.6 %cut.5 = (bf16[128,2048]{1,0:T(8,128)(2,1)S(1)}, f32[8,128]{1,0:T(8,128)}) custom-call(bf16[128,8192]{1,0:T(8,128)(2,1)S(1)} %bitcast.10, f32[8,128]{1,0:T(8,128)S(1)} %get-tuple-element.33.refs_0_), custom_call_target="tpu_custom_call" | custom-call | flops 1000 | bytes 1000 | tf_op jit(solution)/shard_map/cut/pallas_call | solution.py:43
  13.7 2.8 %collective-permute-done.refs_1_ = bf16[128,2048]{1,0:T(8,128)(2,1)S(1)} collective-permute-done((bf16[128,2048]{1,0:T(8,128)(2,1)S(1)}, bf16[128,2048]{1,0:T(8,128)(2,1)S(1)}, u32[]{:S(2)}, u32[]{:S(2)}) %collective-permute-start) | collective-permute-done | bytes 524320 | tf_op jit(solution)/shard_map/ppermute | solution.py:24
  16.5 0.7 %project.3 = (f32[128,512]{1,0:T(8,128)S(1)}, bf16[128,512]{1,0:T(8,128)(2,1)S(1)}, bf16[256,2048]{1,0:T(8,128)(2,1)S(1)}) custom-call(bf16[128,2048]{1,0:T(8,128)(2,1)S(1)} %get-tuple-element.34.refs_0_, bf16[128,2048]{1,0:T(8,128)(2,1)S(1)} %collective-permute-done.refs_1_, bf16[2048,512]{1,0:T(8,128)(2,1)S(1)} %bitcast.11), custom_call_target="tpu_custom_call" | custom-call | flops 1000 | bytes 1000 | tf_op jit(solution)/shard_map/project/pallas_call | solution.py:73
  17.2 2.1 %collective-permute-start.1 = (bf16[128,512]{1,0:T(8,128)(2,1)S(1)}, bf16[128,512]{1,0:T(8,128)(2,1)S(1)}, u32[]{:S(2)}, u32[]{:S(2)}) collective-permute-start(bf16[128,512]{1,0:T(8,128)(2,1)S(1)} %get-tuple-element.36), channel_id=1, source_target_pairs={{0,3},{1,2},{2,1},{3,0},{4,7},{5,6},{6,5},{7,4},{8,11},{9,10},{10,... | collective-permute-start | bytes 393224 | tf_op jit(solution)/shard_map/ppermute | solution.py:24
  19.3 0.6 %prepare.2 = (bf16[128,256]{1,0:T(8,128)(2,1)S(1)}, bf16[2048,256]{1,0:T(8,128)(2,1)S(1)}, f32[8,128]{1,0:T(8,128)S(1)}) custom-call(bf16[256,2048]{1,0:T(8,128)(2,1)S(1)} %get-tuple-element.39.refs_0_, s32[1,128]{1,0:T(1,128)S(1)} %bitcast.18, s32[1,1]{1,0:T(1,128)S(6)} %copy.8.count.refs_2_.refs_3_), custom_call_target="tpu_custom_call" | custom-call | flops 1000 | bytes 1000 | tf_op jit(solution)/shard_map/prepare/pallas_call | solution.py:181
  19.9 4.9 %collective-permute-done.2.refs_0_ = bf16[96,2048]{1,0:T(8,128)(2,1)S(1)} collective-permute-done((bf16[96,2048]{1,0:T(8,128)(2,1)S(1)}, bf16[96,2048]{1,0:T(8,128)(2,1)S(1)}, u32[]{:S(2)}, u32[]{:S(2)}) %collective-permute-start.2) | collective-permute-done | bytes 393248 | tf_op jit(solution)/shard_map/ppermute | solution.py:24
  24.8 0.8 %collective-permute-done.3.refs_1_ = bf16[96,2048]{1,0:T(8,128)(2,1)S(1)} collective-permute-done((bf16[96,2048]{1,0:T(8,128)(2,1)S(1)}, bf16[96,2048]{1,0:T(8,128)(2,1)S(1)}, u32[]{:S(2)}, u32[]{:S(2)}) %collective-permute-start.3) | collective-permute-done | bytes 393248 | tf_op jit(solution)/shard_map/ppermute | solution.py:24
  25.6 0.6 project.4
  26.2 1.5 %collective-permute-start.4 = (bf16[96,512]{1,0:T(8,128)(2,1)S(1)}, bf16[96,512]{1,0:T(8,128)(2,1)S(1)}, u32[]{:S(2)}, u32[]{:S(2)}) collective-permute-start(bf16[96,512]{1,0:T(8,128)(2,1)S(1)} %get-tuple-element.41), channel_id=1, source_target_pairs={{0,1},{1,0},{2,3},{3,2},{4,5},{5,4},{6,7},{7,6},{8,9},{9,8},{10,11... | collective-permute-start | bytes 294920 | tf_op jit(solution)/shard_map/ppermute | solution.py:24
  27.7 1.2 %collective-permute-start.8 = (bf16[96,512]{1,0:T(8,128)(2,1)S(1)}, bf16[96,512]{1,0:T(8,128)(2,1)S(1)}, u32[]{:S(2)}, u32[]{:S(2)}) collective-permute-start(bf16[96,512]{1,0:T(8,128)(2,1)S(1)} %get-tuple-element.44.refs_3_), channel_id=1, source_target_pairs={{0,2},{1,3},{2,0},{3,1},{4,6},{5,7},{6,4},{7,5},{8,10},{9,11},{10,... | collective-permute-start | bytes 294920 | tf_op jit(solution)/shard_map/ppermute | solution.py:24
  29.1 0.5 project.5
  29.6 1.8 %collective-permute-start.9 = (bf16[32,512]{1,0:T(8,128)(2,1)S(1)}, bf16[32,512]{1,0:T(8,128)(2,1)S(1)}, u32[]{:S(2)}, u32[]{:S(2)}) collective-permute-start(bf16[32,512]{1,0:T(8,128)(2,1)S(1)} %get-tuple-element.46), channel_id=1, source_target_pairs={{0,2},{1,3},{2,0},{3,1},{4,6},{5,7},{6,4},{7,5},{8,10},{9,11},{10,... | collective-permute-start | bytes 98312 | tf_op jit(solution)/shard_map/ppermute | solution.py:24
  31.4 1.2 %collective-permute-start.7 = (bf16[32,512]{1,0:T(8,128)(2,1)S(1)}, bf16[32,512]{1,0:T(8,128)(2,1)S(1)}, u32[]{:S(2)}, u32[]{:S(2)}) collective-permute-start(bf16[32,512]{1,0:T(8,128)(2,1)S(1)} %get-tuple-element.45.refs_4_), channel_id=1, source_target_pairs={{0,1},{1,0},{2,3},{3,2},{4,5},{5,4},{6,7},{7,6},{8,9},{9,8},{10,11... | collective-permute-start | bytes 98312 | tf_op jit(solution)/shard_map/ppermute | solution.py:24
  32.6 0.9 %prepare.3 = (bf16[128,256]{1,0:T(8,128)(2,1)S(1)}, bf16[2048,256]{1,0:T(8,128)(2,1)S(1)}, f32[8,128]{1,0:T(8,128)S(1)}) custom-call(bf16[192,2048]{1,0:T(8,128)(2,1)S(1)} %get-tuple-element.47.refs_0_, bf16[64,2048]{1,0:T(8,128)(2,1)S(1)} %get-tuple-element.48.refs_1_, s32[1,128]{1,0:T(1,128)S(1)} %bitcast.19, s32[1,1]{1,0:T(1,128)S(6)} %copy.8.count.refs_2_.refs_3_, ...), custom_call_target="tpu_custom_call" | custom-call | flops 1000 | bytes 1000 | tf_op jit(solution)/shard_map/prepare/pallas_call | solution.py:181
  33.6 0.9 %collective-permute-done.7.refs_4_ = bf16[32,512]{1,0:T(8,128)(2,1)S(1)} collective-permute-done((bf16[32,512]{1,0:T(8,128)(2,1)S(1)}, bf16[32,512]{1,0:T(8,128)(2,1)S(1)}, u32[]{:S(2)}, u32[]{:S(2)}) %collective-permute-start.7) | collective-permute-done | bytes 32800 | tf_op jit(solution)/shard_map/ppermute | solution.py:24
  34.6 8.2 %all_gather.3.slopes = bf16[512,512]{1,0:T(8,128)(2,1)S(1)} all-gather(bf16[128,512]{1,0:T(8,128)(2,1)S(1)} %slope.1), channel_id=1, replica_groups=mesh['rep'=8,'shard'=4] {'shard'}, dimensions={0}, use_global_device_ids=true | all-gather | bytes 655360 | tf_op jit(solution)/shard_map/all_gather | solution.py:394
  42.7 0.3 kept.1
  43.0 3.4 %collective-permute-start.10 = (bf16[144,128]{1,0:T(8,128)(2,1)S(1)}, bf16[144,128]{1,0:T(8,128)(2,1)S(1)}, u32[]{:S(2)}, u32[]{:S(2)}) collective-permute-start(bf16[144,128]{1,0:T(8,128)(2,1)S(1)} %get-tuple-element.53.refs_0_), channel_id=1, source_target_pairs={{0,24},{4,28},{8,16},{12,20},{16,8},{20,12},{24,0},{28,4},{1,25},{... | collective-permute-start | bytes 110600 | tf_op jit(solution)/shard_map/ppermute | solution.py:24
  46.4 0.4 collective-permute-start.12
  46.8 2.4 %residue.1 = (bf16[2048,512]{1,0:T(8,128)(2,1)}, f32[8,128]{1,0:T(8,128)S(1)}) custom-call(bf16[512,512]{1,0:T(8,128)(2,1)S(1)} %get-tuple-element.54.s, bf16[2048,256]{1,0:T(8,128)(2,1)S(1)} %get-tuple-element.55.refs_0_, bf16[2048,256]{1,0:T(8,128)(2,1)S(1)} %get-tuple-element.56.refs_1_, bf16[2048,512]{1,0:T(8,128)(2,1)S(1)} %bitcast.15, ...), custom_call_target="tpu_custom_call" | custom-call | flops 1000 | bytes 1000 | tf_op jit(solution)/shard_map/residue/pallas_call | solution.py:258
  49.2 0.9 %collective-permute-done.11.refs_1_ = bf16[144,128]{1,0:T(8,128)(2,1)S(1)} collective-permute-done((bf16[144,128]{1,0:T(8,128)(2,1)S(1)}, bf16[144,128]{1,0:T(8,128)(2,1)S(1)}, u32[]{:S(2)}, u32[]{:S(2)}) %collective-permute-start.11) | collective-permute-done | bytes 36896 | tf_op jit(solution)/shard_map/ppermute | solution.py:24
  50.2 5.9 %collective-permute-start.13 = (bf16[576,128]{1,0:T(8,128)(2,1)S(1)}, bf16[576,128]{1,0:T(8,128)(2,1)S(1)}, u32[]{:S(2)}, u32[]{:S(2)}) collective-permute-start(bf16[576,128]{1,0:T(8,128)(2,1)S(1)} %join.5.group), channel_id=1, source_target_pairs={{0,4},{4,0},{8,12},{12,8},{16,20},{20,16},{24,28},{28,24},{1,5},{5... | collective-permute-start | bytes 442376 | tf_op jit(solution)/shard_map/ppermute | solution.py:24
  56.1 1.4 %half.1 = f32[2048,512]{1,0:T(8,128)S(1)} custom-call(bf16[576,128]{1,0:T(8,128)(2,1)S(1)} %join.5.group), custom_call_target="tpu_custom_call" | custom-call | flops 1000 | bytes 1000 | tf_op jit(solution)/shard_map/half/pallas_call | solution.py:336
  57.5 2.7 %outer.1 = f32[2048,512]{1,0:T(8,128)} custom-call(bf16[576,128]{1,0:T(8,128)(2,1)S(1)} %collective-permute-done.13.group, f32[2048,512]{1,0:T(8,128)S(1)} %half.1), custom_call_target="tpu_custom_call" | custom-call | flops 1000 | bytes 1000 | tf_op jit(solution)/shard_map/outer/pallas_call | solution.py:344
  (29 shorter events, 0.6 us)
Async XLA Ops:
  0.6 7.0 %copy-start.6 = (s32[1,1,128]{2,1,0:T(1,128)S(1)}, s32[1,1,128]{2,1,0:T(1,128)}, u32[]{:S(2)}) copy-start(s32[1,1,128]{2,1,0:T(1,128)} %param.11) | copy-start | bytes 1540
  1.7 14.8 %collective-permute-start = (bf16[128,2048]{1,0:T(8,128)(2,1)S(1)}, bf16[128,2048]{1,0:T(8,128)(2,1)S(1)}, u32[]{:S(2)}, u32[]{:S(2)}) collective-permute-start(bf16[128,2048]{1,0:T(8,128)(2,1)S(1)} %dynamic-slice_bitcast_fusion.refs_0_), channel_id=1, source_target_pairs={{0,3},{1,2},{2,1},{3,0},{4,7},{5,6},{6,5},{7,4},{8,11},{9,10},{10,... | collective-permute-start | bytes 1572872 | tf_op jit(solution)/shard_map/ppermute | solution.py:24
  4.8 1.6 %copy-start = (bf16[1,128,8192]{2,1,0:T(8,128)(2,1)S(1)}, bf16[1,128,8192]{2,1,0:T(8,128)(2,1)}, u32[]{:S(2)}) copy-start(bf16[1,128,8192]{2,1,0:T(8,128)(2,1)} %param.6) | copy-start | bytes 6291460
  6.4 4.0 %copy-start.1 = (bf16[1,128,8192]{2,1,0:T(8,128)(2,1)S(1)}, bf16[1,128,8192]{2,1,0:T(8,128)(2,1)}, u32[]{:S(2)}) copy-start(bf16[1,128,8192]{2,1,0:T(8,128)(2,1)} %param.6) | copy-start | bytes 6291460
  6.5 18.4 %collective-permute-start.2 = (bf16[96,2048]{1,0:T(8,128)(2,1)S(1)}, bf16[96,2048]{1,0:T(8,128)(2,1)S(1)}, u32[]{:S(2)}, u32[]{:S(2)}) collective-permute-start(bf16[96,2048]{1,0:T(8,128)(2,1)S(1)} %get-tuple-element.37), channel_id=1, source_target_pairs={{0,1},{1,0},{2,3},{3,2},{4,5},{5,4},{6,7},{7,6},{8,9},{9,8},{10,11... | collective-permute-start | bytes 1179656 | tf_op jit(solution)/shard_map/ppermute | solution.py:24
  6.8 18.8 %collective-permute-start.3 = (bf16[96,2048]{1,0:T(8,128)(2,1)S(1)}, bf16[96,2048]{1,0:T(8,128)(2,1)S(1)}, u32[]{:S(2)}, u32[]{:S(2)}) collective-permute-start(bf16[96,2048]{1,0:T(8,128)(2,1)S(1)} %get-tuple-element.38), channel_id=1, source_target_pairs={{0,2},{1,3},{2,0},{3,1},{4,6},{5,7},{6,4},{7,5},{8,10},{9,11},{10,... | collective-permute-start | bytes 1179656 | tf_op jit(solution)/shard_map/ppermute | solution.py:24
  7.7 1.6 %copy-start.3 = (bf16[1,2048,512]{2,1,0:T(8,128)(2,1)S(1)}, bf16[1,2048,512]{2,1,0:T(8,128)(2,1)}, u32[]{:S(2)}) copy-start(bf16[1,2048,512]{2,1,0:T(8,128)(2,1)} %param.9) | copy-start | bytes 6291460
  10.4 6.1 %copy-start.2 = (bf16[1,2048,512]{2,1,0:T(8,128)(2,1)S(1)}, bf16[1,2048,512]{2,1,0:T(8,128)(2,1)}, u32[]{:S(2)}) copy-start(bf16[1,2048,512]{2,1,0:T(8,128)(2,1)} %param.8) | copy-start | bytes 6291460
  10.5 18.4 %collective-permute-start.5 = (bf16[32,2048]{1,0:T(8,128)(2,1)S(1)}, bf16[32,2048]{1,0:T(8,128)(2,1)S(1)}, u32[]{:S(2)}, u32[]{:S(2)}) collective-permute-start(bf16[32,2048]{1,0:T(8,128)(2,1)S(1)} %get-tuple-element.42), channel_id=1, source_target_pairs={{0,1},{1,0},{2,3},{3,2},{4,5},{5,4},{6,7},{7,6},{8,9},{9,8},{10,11... | collective-permute-start | bytes 393224 | tf_op jit(solution)/shard_map/ppermute | solution.py:24
  11.8 17.3 %collective-permute-start.6 = (bf16[32,2048]{1,0:T(8,128)(2,1)S(1)}, bf16[32,2048]{1,0:T(8,128)(2,1)S(1)}, u32[]{:S(2)}, u32[]{:S(2)}) collective-permute-start(bf16[32,2048]{1,0:T(8,128)(2,1)S(1)} %get-tuple-element.43), channel_id=1, source_target_pairs={{0,2},{1,3},{2,0},{3,1},{4,6},{5,7},{6,4},{7,5},{8,10},{9,11},{10,... | collective-permute-start | bytes 393224 | tf_op jit(solution)/shard_map/ppermute | solution.py:24
  17.2 17.2 %collective-permute-start.1 = (bf16[128,512]{1,0:T(8,128)(2,1)S(1)}, bf16[128,512]{1,0:T(8,128)(2,1)S(1)}, u32[]{:S(2)}, u32[]{:S(2)}) collective-permute-start(bf16[128,512]{1,0:T(8,128)(2,1)S(1)} %get-tuple-element.36), channel_id=1, source_target_pairs={{0,3},{1,2},{2,1},{3,0},{4,7},{5,6},{6,5},{7,4},{8,11},{9,10},{10,... | collective-permute-start | bytes 393224 | tf_op jit(solution)/shard_map/ppermute | solution.py:24
  26.2 8.3 %copy-start.5 = (bf16[1,128,512]{2,1,0:T(8,128)(2,1)S(1)}, bf16[1,128,512]{2,1,0:T(8,128)(2,1)}, u32[]{:S(2)}) copy-start(bf16[1,128,512]{2,1,0:T(8,128)(2,1)} %param.7) | copy-start | bytes 393220
  26.2 8.2 %collective-permute-start.4 = (bf16[96,512]{1,0:T(8,128)(2,1)S(1)}, bf16[96,512]{1,0:T(8,128)(2,1)S(1)}, u32[]{:S(2)}, u32[]{:S(2)}) collective-permute-start(bf16[96,512]{1,0:T(8,128)(2,1)S(1)} %get-tuple-element.41), channel_id=1, source_target_pairs={{0,1},{1,0},{2,3},{3,2},{4,5},{5,4},{6,7},{7,6},{8,9},{9,8},{10,11... | collective-permute-start | bytes 294920 | tf_op jit(solution)/shard_map/ppermute | solution.py:24
  27.7 6.8 %collective-permute-start.8 = (bf16[96,512]{1,0:T(8,128)(2,1)S(1)}, bf16[96,512]{1,0:T(8,128)(2,1)S(1)}, u32[]{:S(2)}, u32[]{:S(2)}) collective-permute-start(bf16[96,512]{1,0:T(8,128)(2,1)S(1)} %get-tuple-element.44.refs_3_), channel_id=1, source_target_pairs={{0,2},{1,3},{2,0},{3,1},{4,6},{5,7},{6,4},{7,5},{8,10},{9,11},{10,... | collective-permute-start | bytes 294920 | tf_op jit(solution)/shard_map/ppermute | solution.py:24
  29.6 17.2 %copy-start.4 = (bf16[1,2048,512]{2,1,0:T(8,128)(2,1)S(1)}, bf16[1,2048,512]{2,1,0:T(8,128)(2,1)}, u32[]{:S(2)}) copy-start(bf16[1,2048,512]{2,1,0:T(8,128)(2,1)} %param.9) | copy-start | bytes 6291460
  29.6 4.0 %collective-permute-start.9 = (bf16[32,512]{1,0:T(8,128)(2,1)S(1)}, bf16[32,512]{1,0:T(8,128)(2,1)S(1)}, u32[]{:S(2)}, u32[]{:S(2)}) collective-permute-start(bf16[32,512]{1,0:T(8,128)(2,1)S(1)} %get-tuple-element.46), channel_id=1, source_target_pairs={{0,2},{1,3},{2,0},{3,1},{4,6},{5,7},{6,4},{7,5},{8,10},{9,11},{10,... | collective-permute-start | bytes 98312 | tf_op jit(solution)/shard_map/ppermute | solution.py:24
  31.4 3.0 %collective-permute-start.7 = (bf16[32,512]{1,0:T(8,128)(2,1)S(1)}, bf16[32,512]{1,0:T(8,128)(2,1)S(1)}, u32[]{:S(2)}, u32[]{:S(2)}) collective-permute-start(bf16[32,512]{1,0:T(8,128)(2,1)S(1)} %get-tuple-element.45.refs_4_), channel_id=1, source_target_pairs={{0,1},{1,0},{2,3},{3,2},{4,5},{5,4},{6,7},{7,6},{8,9},{9,8},{10,11... | collective-permute-start | bytes 98312 | tf_op jit(solution)/shard_map/ppermute | solution.py:24
  43.0 6.1 %collective-permute-start.10 = (bf16[144,128]{1,0:T(8,128)(2,1)S(1)}, bf16[144,128]{1,0:T(8,128)(2,1)S(1)}, u32[]{:S(2)}, u32[]{:S(2)}) collective-permute-start(bf16[144,128]{1,0:T(8,128)(2,1)S(1)} %get-tuple-element.53.refs_0_), channel_id=1, source_target_pairs={{0,24},{4,28},{8,16},{12,20},{16,8},{20,12},{24,0},{28,4},{1,25},{... | collective-permute-start | bytes 110600 | tf_op jit(solution)/shard_map/ppermute | solution.py:24
  46.4 3.7 %collective-permute-start.11 = (bf16[144,128]{1,0:T(8,128)(2,1)S(1)}, bf16[144,128]{1,0:T(8,128)(2,1)S(1)}, u32[]{:S(2)}, u32[]{:S(2)}) collective-permute-start(bf16[144,128]{1,0:T(8,128)(2,1)S(1)} %get-tuple-element.53.refs_0_), channel_id=1, source_target_pairs={{0,16},{4,20},{8,24},{12,28},{16,0},{20,4},{24,8},{28,12},{1,17},{... | collective-permute-start | bytes 110600 | tf_op jit(solution)/shard_map/ppermute | solution.py:24
  46.4 3.7 %collective-permute-start.12 = (bf16[144,128]{1,0:T(8,128)(2,1)S(1)}, bf16[144,128]{1,0:T(8,128)(2,1)S(1)}, u32[]{:S(2)}, u32[]{:S(2)}) collective-permute-start(bf16[144,128]{1,0:T(8,128)(2,1)S(1)} %get-tuple-element.53.refs_0_), channel_id=1, source_target_pairs={{0,8},{4,12},{8,0},{12,4},{16,24},{20,28},{24,16},{28,20},{1,9},{5... | collective-permute-start | bytes 110600 | tf_op jit(solution)/shard_map/ppermute | solution.py:24
  50.2 7.3 %collective-permute-start.13 = (bf16[576,128]{1,0:T(8,128)(2,1)S(1)}, bf16[576,128]{1,0:T(8,128)(2,1)S(1)}, u32[]{:S(2)}, u32[]{:S(2)}) collective-permute-start(bf16[576,128]{1,0:T(8,128)(2,1)S(1)} %join.5.group), channel_id=1, source_target_pairs={{0,4},{4,0},{8,12},{12,8},{16,20},{20,16},{24,28},{28,24},{1,5},{5... | collective-permute-start | bytes 442376 | tf_op jit(solution)/shard_map/ppermute | solution.py:24

commit v10 on v8

--- a/solution.py
+++ b/solution.py
@@ -53,8 +53,8 @@
     )(tokens, *after)
 
 
-def project_kernel(n, *refs):
-    pieces, w, outs, x = refs[:n], refs[n], refs[-n - 1 : -1], refs[-1]
+def project_kernel(n, m, *refs):
+    pieces, w, outs, x = refs[:n], refs[n], refs[-m - 1 : -1], refs[-1]
     start = 0
     for piece in pieces:
         x[start : start + piece.shape[0], :] = piece[...]
@@ -66,20 +66,20 @@
         start += out.shape[0]
 
 
-def project(pieces, types, w, after):
+def project(pieces, outs, w, after):
     n = len(pieces)
     rows, depth = sum(p.shape[0] for p in pieces), pieces[0].shape[1]
     kw = w.shape[1]
     result = pl.pallas_call(
-        functools.partial(project_kernel, n),
-        out_shape=[jax.ShapeDtypeStruct((p.shape[0], kw), t) for p, t in zip(pieces, types)]
+        functools.partial(project_kernel, n, len(outs)),
+        out_shape=[jax.ShapeDtypeStruct((r, kw), t) for r, t in outs]
         + [jax.ShapeDtypeStruct((rows, depth), jnp.bfloat16)],
         in_specs=[VMEM] * (n + 1) + [ANY] * len(after),
         compiler_params=params(14),
         cost_estimate=BRIEF,
         name="project",
     )(*pieces, w, *after)
-    return result[:n], result[n]
+    return result[:-1], result[-1]
 
 
 def slope_kernel(tok_dev, n, spans, *refs):
@@ -378,7 +378,7 @@
     n_shard, n_rep = lax.axis_size("shard"), lax.axis_size("rep")
     tok_dev = tokens.shape[0]
     depth, kw = w.shape
-    early_rows = tok_dev * 3 // 4
+    early_rows = tok_dev // 2
     spans = [(0, early_rows), (early_rows, tok_dev)]
     per_row = kw // LANES
     slot_row = blocks[0]
@@ -386,29 +386,47 @@
     far = [d for d in range(1, n_shard) if d & (d - 1) != 0]
 
     me = lax.axis_index("shard")
-    far_out = [lax.dynamic_slice(tokens, (0, (me ^ d) * depth), (tok_dev, depth)) for d in far]
-    far_in = [swap(x, "shard", n_shard, d) for x, d in zip(far_out, far)]
-    near_out, token = [], far_out[0]
+    rows = tok_dev // 2 if n_shard == 4 else tok_dev
+    far_out = [
+        [
+            lax.dynamic_slice(tokens, (low, (me ^ d) * depth), (rows, depth))
+            for low in range(0, tok_dev, rows)
+        ]
+        for d in far
+    ]
+    if n_shard == 4:
+        ((by_x, by_y),) = far_out
+        by_x, by_y = swap(by_x, "shard", n_shard, 1), swap(by_y, "shard", n_shard, 2)
+        hops = [by_x, by_y]
+        far_in = [swap(by_x, "shard", n_shard, 2), swap(by_y, "shard", n_shard, 1)]
+    else:
+        hops = []
+        far_in = [swap(x, "shard", n_shard, d) for (x,), d in zip(far_out, far)]
+    near_out, after = [], [far_out[0][0]]
     for low, high in spans:
-        *out, token = cut(tokens, depth, [(d, low, high - low) for d in near], [token])
+        *out, token = cut(tokens, depth, [(d, low, high - low) for d in near], after)
         near_out.append(out)
         if low == 0:
             fbk, keep, token = early(slot_row, counts, fb, token)
+            after = [token] + hops
     near_in = [[swap(x, "shard", n_shard, d) for x, d in zip(out, near)] for out in near_out]
 
     own, _ = cut(tokens, depth, [(0, 0, tok_dev)], [token])
 
     brief, wide = jnp.bfloat16, jnp.float32
-    (mine, *products), x_far = project([own] + far_in, [wide] + [brief] * len(far), w, [])
+    near_outs = [[(high - low, brief)] * len(near) for low, high in spans]
+    early_near, x_early = project(near_in[0], near_outs[0], w, [])
+    outs = [(tok_dev, wide)] + [(tok_dev, brief)] * len(far)
+    (mine, *products), x_far = project([own] + far_in, outs, w, early_near[-1:])
     whole = [swap(p, "shard", n_shard, d) for p, d in zip(products, far)]
-    xg_far, xt_far, token = prepare([x_far], slot_row, counts, per_row, [])
-    after, shares, x_near = [token], [], []
-    for part in range(len(spans)):
-        products, x = project(near_in[part], [brief] * len(near), w, after)
-        shares.append([swap(p, "shard", n_shard, d) for p, d in zip(products, near)])
-        x_near.append(x)
-        after = products[-1:]
-    xg_near, xt_near, token = prepare(x_near, slot_row, counts, per_row, [products[0]])
+    xg_far, xt_far, token = prepare([x_far], slot_row, counts, per_row, products)
+    late_near, x_late = project(near_in[1], near_outs[1], w, [token])
+    shares = [
+        [swap(p, "shard", n_shard, d) for p, d in zip(part, near)]
+        for part in (early_near, late_near)
+    ]
+    x_near = [x_early, x_late]
+    xg_near, xt_near, token = prepare(x_near, slot_row, counts, per_row, late_near[:1])
     shares = [share[k] for k in range(len(near)) for share in shares]
     slopes = slope(target[0], mine, whole, shares, spans, token)
     slopes = [slopes] + [swap(slopes, "shard", n_shard, d) for d in far + near]

time: 57.6 us -> 57.5 us (level)
  starting transfers between devices: 23.4 us -> 24.1 us
  Pallas kernels: 12.3 us -> 11.7 us
    ppermute x17 -> x20, starting transfers between devices: 23.4 us -> 24.1 us  [swap(): return lax.ppermute(x, axis, [(i, i ^ d) for i in range(n)])]
    ppermute x17 -> x20, waiting for transfers between devices: 15.8 us -> 15.7 us  [swap(): return lax.ppermute(x, axis, [(i, i ^ d) for i in range(n)])]
  transfers between devices with their start and end apart: 17 -> 20, of which waited for: 9 -> 9; matrix products, arithmetic and copies ran while one was open for 0% -> 0% of each run, Pallas kernels for 16% -> 15%
where the time goes in v10:
time: 57.5 us; the launch traced here: 57.3 us
  starting transfers between devices  24.1 us (42%)
  waiting for transfers between devices  15.7 us (27%)
  Pallas kernels  11.7 us (20%)
  local copies, waits for them, and re-layouts  4.28 us (7%)
  between operations  1.53 us (3%)
    ppermute x20, starting transfers between devices, swap(): return lax.ppermute(x, axis, [(i, i ^ d) for i in range(n)])  24.1 us
    ppermute x20, waiting for transfers between devices, swap(): return lax.ppermute(x, axis, [(i, i ^ d) for i in range(n)])  15.7 us
    unnamed x14, local copies, waits for them, and re-layouts  3.2 us
    pallas_call x1, Pallas kernels, outer(): pl.pallas_call(functools.partial(outer_kernel, cap, kw // LANES, tile, n)...  2.65 us
    pallas_call x1, Pallas kernels, residue(): pl.pallas_call(functools.partial(residue_kernel, order, tile), out_shape=...  2.37 us
    pallas_call x3, Pallas kernels, project(): pl.pallas_call(functools.partial(project_kernel, n, len(outs)), out_shape...  1.62 us
    pallas_call x1, Pallas kernels, outer(): pl.pallas_call(functools.partial(half_kernel, cap, kw // LANES, tile), ou...  1.42 us
    pallas_call x2, Pallas kernels, prepare(): pl.pallas_call(functools.partial(prepare_kernel, per_row, len(xs)), out_s...  1.2 us
  transfers between devices with their start and end apart: 20, of which 9 were waited for; matrix products, arithmetic and copies ran while one was open for 0% of the time, Pallas kernels for 15%

profile of v10, /device:TPU:1, one launch (start us, length us, event | category | flops | bytes accessed | tf_op | source)
XLA Modules:
  0.0 57.3 jit_solution(16831288266375048834)
XLA Ops:
  0.6 1.1 %dynamic-slice_bitcast_fusion = (bf16[64,2048]{1,0:T(8,128)(2,1)S(1)}, bf16[64,2048]{1,0:T(8,128)(2,1)S(1)}) fusion(bf16[1,128,8192]{2,1,0:T(8,128)(2,1)} %param.6, s32[]{:T(128)S(6)} %select_n.4), kind=kLoop, calls=%fused_computation | loop fusion | bytes 1048580 | tf_op jit(solution)/shard_map/dynamic_slice | solution.py:392
  1.7 2.1 %collective-permute-start.1 = (bf16[64,2048]{1,0:T(8,128)(2,1)S(1)}, bf16[64,2048]{1,0:T(8,128)(2,1)S(1)}, u32[]{:S(2)}, u32[]{:S(2)}) collective-permute-start(bf16[64,2048]{1,0:T(8,128)(2,1)S(1)} %get-tuple-element.56), channel_id=1, source_target_pairs={{0,2},{1,3},{2,0},{3,1},{4,6},{5,7},{6,4},{7,5},{8,10},{9,11},{10,... | collective-permute-start | bytes 786440 | tf_op jit(solution)/shard_map/ppermute | solution.py:24
  3.9 1.2 %collective-permute-start = (bf16[64,2048]{1,0:T(8,128)(2,1)S(1)}, bf16[64,2048]{1,0:T(8,128)(2,1)S(1)}, u32[]{:S(2)}, u32[]{:S(2)}) collective-permute-start(bf16[64,2048]{1,0:T(8,128)(2,1)S(1)} %get-tuple-element.57.refs_0_), channel_id=1, source_target_pairs={{0,1},{1,0},{2,3},{3,2},{4,5},{5,4},{6,7},{7,6},{8,9},{9,8},{10,11... | collective-permute-start | bytes 786440 | tf_op jit(solution)/shard_map/ppermute | solution.py:24
  5.1 1.6 %copy-done = bf16[1,128,8192]{2,1,0:T(8,128)(2,1)S(1)} copy-done((bf16[1,128,8192]{2,1,0:T(8,128)(2,1)S(1)}, bf16[1,128,8192]{2,1,0:T(8,128)(2,1)}, u32[]{:S(2)}) %copy-start) | copy-done | bytes 2097176
  7.1 2.8 %collective-permute-done.1.refs_2_ = bf16[64,2048]{1,0:T(8,128)(2,1)S(1)} collective-permute-done((bf16[64,2048]{1,0:T(8,128)(2,1)S(1)}, bf16[64,2048]{1,0:T(8,128)(2,1)S(1)}, u32[]{:S(2)}, u32[]{:S(2)}) %collective-permute-start.1) | collective-permute-done | bytes 262176 | tf_op jit(solution)/shard_map/ppermute | solution.py:24
  9.9 1.1 %collective-permute-start.3 = (bf16[64,2048]{1,0:T(8,128)(2,1)S(1)}, bf16[64,2048]{1,0:T(8,128)(2,1)S(1)}, u32[]{:S(2)}, u32[]{:S(2)}) collective-permute-start(bf16[64,2048]{1,0:T(8,128)(2,1)S(1)} %collective-permute-done.1.refs_2_), channel_id=1, source_target_pairs={{0,1},{1,0},{2,3},{3,2},{4,5},{5,4},{6,7},{7,6},{8,9},{9,8},{10,11... | collective-permute-start | bytes 786440 | tf_op jit(solution)/shard_map/ppermute | solution.py:24
  11.0 1.2 %collective-permute-start.2 = (bf16[64,2048]{1,0:T(8,128)(2,1)S(1)}, bf16[64,2048]{1,0:T(8,128)(2,1)S(1)}, u32[]{:S(2)}, u32[]{:S(2)}) collective-permute-start(bf16[64,2048]{1,0:T(8,128)(2,1)S(1)} %collective-permute-done.refs_1_), channel_id=1, source_target_pairs={{0,2},{1,3},{2,0},{3,1},{4,6},{5,7},{6,4},{7,5},{8,10},{9,11},{10,... | collective-permute-start | bytes 786440 | tf_op jit(solution)/shard_map/ppermute | solution.py:24
  12.9 1.6 %copy-done.3 = bf16[1,2048,512]{2,1,0:T(8,128)(2,1)S(1)} copy-done((bf16[1,2048,512]{2,1,0:T(8,128)(2,1)S(1)}, bf16[1,2048,512]{2,1,0:T(8,128)(2,1)}, u32[]{:S(2)}) %copy-start.3) | copy-done | bytes 2097176
  14.5 1.1 %early.1 = (f32[128,128]{1,0:T(8,128)S(1)}, bf16[2048,512]{1,0:T(8,128)(2,1)S(1)}, f32[8,128]{1,0:T(8,128)S(1)}) custom-call(s32[1,128]{1,0:T(1,128)S(1)} %bitcast.19, s32[1,1]{1,0:T(1,128)S(6)} %copy.8.count.refs_2_.refs_3_, bf16[2048,512]{1,0:T(8,128)(2,1)S(1)} %bitcast.16, f32[8,128]{1,0:T(8,128)S(1)} %get-tuple-element.29.after), custom_call_target="tpu_custom_call" | custom-call | flops 1000 | bytes 1000 | tf_op jit(solution)/shard_map/early/pallas_call | solution.py:145
  16.3 0.6 %collective-permute-start.9 = (bf16[64,2048]{1,0:T(8,128)(2,1)S(1)}, bf16[64,2048]{1,0:T(8,128)(2,1)S(1)}, u32[]{:S(2)}, u32[]{:S(2)}) collective-permute-start(bf16[64,2048]{1,0:T(8,128)(2,1)S(1)} %get-tuple-element.40), channel_id=1, source_target_pairs={{0,2},{1,3},{2,0},{3,1},{4,6},{5,7},{6,4},{7,5},{8,10},{9,11},{10,... | collective-permute-start | bytes 786440 | tf_op jit(solution)/shard_map/ppermute | solution.py:24
  16.9 0.6 %cut.5 = (bf16[128,2048]{1,0:T(8,128)(2,1)S(1)}, f32[8,128]{1,0:T(8,128)}) custom-call(bf16[128,8192]{1,0:T(8,128)(2,1)S(1)} %bitcast.12, f32[8,128]{1,0:T(8,128)S(1)} %get-tuple-element.31.refs_0_), custom_call_target="tpu_custom_call" | custom-call | flops 1000 | bytes 1000 | tf_op jit(solution)/shard_map/cut/pallas_call | solution.py:43
  18.1 3.9 %collective-permute-done.3.refs_2_ = bf16[64,2048]{1,0:T(8,128)(2,1)S(1)} collective-permute-done((bf16[64,2048]{1,0:T(8,128)(2,1)S(1)}, bf16[64,2048]{1,0:T(8,128)(2,1)S(1)}, u32[]{:S(2)}, u32[]{:S(2)}) %collective-permute-start.3) | collective-permute-done | bytes 262176 | tf_op jit(solution)/shard_map/ppermute | solution.py:24
  22.0 0.7 %project.4 = (f32[128,512]{1,0:T(8,128)S(1)}, bf16[128,512]{1,0:T(8,128)(2,1)S(1)}, bf16[256,2048]{1,0:T(8,128)(2,1)S(1)}) custom-call(bf16[128,2048]{1,0:T(8,128)(2,1)S(1)} %get-tuple-element.32.refs_0_, bf16[64,2048]{1,0:T(8,128)(2,1)S(1)} %collective-permute-done.2.refs_1_, bf16[64,2048]{1,0:T(8,128)(2,1)S(1)} %collective-permute-done.3.refs_2_, ...), custom_call_target="tpu_custom_call" | custom-call | flops 1000 | bytes 1000 | tf_op jit(solution)/shard_map/project/pallas_call | solution.py:73
  22.7 1.3 %collective-permute-start.6 = (bf16[128,512]{1,0:T(8,128)(2,1)S(1)}, bf16[128,512]{1,0:T(8,128)(2,1)S(1)}, u32[]{:S(2)}, u32[]{:S(2)}) collective-permute-start(bf16[128,512]{1,0:T(8,128)(2,1)S(1)} %get-tuple-element.37.refs_3_), channel_id=1, source_target_pairs={{0,3},{1,2},{2,1},{3,0},{4,7},{5,6},{6,5},{7,4},{8,11},{9,10},{10,... | collective-permute-start | bytes 393224 | tf_op jit(solution)/shard_map/ppermute | solution.py:24
  24.0 1.2 %collective-permute-start.11 = (bf16[64,512]{1,0:T(8,128)(2,1)S(1)}, bf16[64,512]{1,0:T(8,128)(2,1)S(1)}, u32[]{:S(2)}, u32[]{:S(2)}) collective-permute-start(bf16[64,512]{1,0:T(8,128)(2,1)S(1)} %get-tuple-element.35.refs_4_), channel_id=1, source_target_pairs={{0,2},{1,3},{2,0},{3,1},{4,6},{5,7},{6,4},{7,5},{8,10},{9,11},{10,... | collective-permute-start | bytes 196616 | tf_op jit(solution)/shard_map/ppermute | solution.py:24
  25.4 0.6 %prepare.2 = (bf16[128,256]{1,0:T(8,128)(2,1)S(1)}, bf16[2048,256]{1,0:T(8,128)(2,1)S(1)}, f32[8,128]{1,0:T(8,128)S(1)}) custom-call(bf16[256,2048]{1,0:T(8,128)(2,1)S(1)} %get-tuple-element.41.refs_0_, s32[1,128]{1,0:T(1,128)S(1)} %bitcast.20, s32[1,1]{1,0:T(1,128)S(6)} %copy.8.count.refs_2_.refs_3_, bf16[128,512]{1,0:T(8,128)(2,1)S(1)} %get-tuple-element.37.refs_3_), custom_call_target="tpu_custom_call" | custom-call | flops 1000 | bytes 1000 | tf_op jit(solution)/shard_map/prepare/pallas_call | solution.py:181
  26.0 1.6 %collective-permute-done.8.refs_0_ = bf16[64,2048]{1,0:T(8,128)(2,1)S(1)} collective-permute-done((bf16[64,2048]{1,0:T(8,128)(2,1)S(1)}, bf16[64,2048]{1,0:T(8,128)(2,1)S(1)}, u32[]{:S(2)}, u32[]{:S(2)}) %collective-permute-start.8) | collective-permute-done | bytes 262176 | tf_op jit(solution)/shard_map/ppermute | solution.py:24
  28.5 1.1 %collective-permute-start.10 = (bf16[64,512]{1,0:T(8,128)(2,1)S(1)}, bf16[64,512]{1,0:T(8,128)(2,1)S(1)}, u32[]{:S(2)}, u32[]{:S(2)}) collective-permute-start(bf16[64,512]{1,0:T(8,128)(2,1)S(1)} %get-tuple-element.43.refs_4_), channel_id=1, source_target_pairs={{0,1},{1,0},{2,3},{3,2},{4,5},{5,4},{6,7},{7,6},{8,9},{9,8},{10,11... | collective-permute-start | bytes 196616 | tf_op jit(solution)/shard_map/ppermute | solution.py:24
  29.6 0.6 %prepare.3 = (bf16[128,256]{1,0:T(8,128)(2,1)S(1)}, bf16[2048,256]{1,0:T(8,128)(2,1)S(1)}, f32[8,128]{1,0:T(8,128)S(1)}) custom-call(bf16[128,2048]{1,0:T(8,128)(2,1)S(1)} %get-tuple-element.45.refs_0_, bf16[128,2048]{1,0:T(8,128)(2,1)S(1)} %get-tuple-element.46.refs_1_, s32[1,128]{1,0:T(1,128)S(1)} %bitcast.21, s32[1,1]{1,0:T(1,128)S(6)} %copy.8.count.refs_2_.refs_3_, ...), custom_call_target="tpu_custom_call" | custom-call | flops 1000 | bytes 1000 | tf_op jit(solution)/shard_map/prepare/pallas_call | solution.py:181
  30.2 1.5 %collective-permute-done.7.refs_3_ = bf16[64,512]{1,0:T(8,128)(2,1)S(1)} collective-permute-done((bf16[64,512]{1,0:T(8,128)(2,1)S(1)}, bf16[64,512]{1,0:T(8,128)(2,1)S(1)}, u32[]{:S(2)}, u32[]{:S(2)}) %collective-permute-start.7) | collective-permute-done | bytes 65568 | tf_op jit(solution)/shard_map/ppermute | solution.py:24
  31.8 1.4 %collective-permute-done.12.refs_6_ = bf16[64,512]{1,0:T(8,128)(2,1)S(1)} collective-permute-done((bf16[64,512]{1,0:T(8,128)(2,1)S(1)}, bf16[64,512]{1,0:T(8,128)(2,1)S(1)}, u32[]{:S(2)}, u32[]{:S(2)}) %collective-permute-start.12) | collective-permute-done | bytes 65568 | tf_op jit(solution)/shard_map/ppermute | solution.py:24
  33.3 1.6 %collective-permute-start.15 = (bf16[128,512]{1,0:T(8,128)(2,1)S(1)}, bf16[128,512]{1,0:T(8,128)(2,1)S(1)}, u32[]{:S(2)}, u32[]{:S(2)}) collective-permute-start(bf16[128,512]{1,0:T(8,128)(2,1)S(1)} %slope.1.refs_0_), channel_id=1, source_target_pairs={{0,3},{1,2},{2,1},{3,0},{4,7},{5,6},{6,5},{7,4},{8,11},{9,10},{10,... | collective-permute-start | bytes 393224 | tf_op jit(solution)/shard_map/ppermute | solution.py:24
  34.8 0.6 %collective-permute-start.14 = (bf16[128,512]{1,0:T(8,128)(2,1)S(1)}, bf16[128,512]{1,0:T(8,128)(2,1)S(1)}, u32[]{:S(2)}, u32[]{:S(2)}) collective-permute-start(bf16[128,512]{1,0:T(8,128)(2,1)S(1)} %slope.1.refs_0_), channel_id=1, source_target_pairs={{0,2},{1,3},{2,0},{3,1},{4,6},{5,7},{6,4},{7,5},{8,10},{9,11},{10,... | collective-permute-start | bytes 393224 | tf_op jit(solution)/shard_map/ppermute | solution.py:24
  35.5 0.5 collective-permute-start.13
  36.0 2.2 %collective-permute-done.15.refs_1_ = bf16[128,512]{1,0:T(8,128)(2,1)S(1)} collective-permute-done((bf16[128,512]{1,0:T(8,128)(2,1)S(1)}, bf16[128,512]{1,0:T(8,128)(2,1)S(1)}, u32[]{:S(2)}, u32[]{:S(2)}) %collective-permute-start.15) | collective-permute-done | bytes 131104 | tf_op jit(solution)/shard_map/ppermute | solution.py:24
  38.3 1.1 %collective-permute-done.14.refs_1_.refs_3_ = bf16[128,512]{1,0:T(8,128)(2,1)S(1)} collective-permute-done((bf16[128,512]{1,0:T(8,128)(2,1)S(1)}, bf16[128,512]{1,0:T(8,128)(2,1)S(1)}, u32[]{:S(2)}, u32[]{:S(2)}) %collective-permute-start.14) | collective-permute-done | bytes 131104 | tf_op jit(solution)/shard_map/ppermute | solution.py:24
  39.7 3.6 %collective-permute-start.16 = (bf16[144,128]{1,0:T(8,128)(2,1)S(1)}, bf16[144,128]{1,0:T(8,128)(2,1)S(1)}, u32[]{:S(2)}, u32[]{:S(2)}) collective-permute-start(bf16[144,128]{1,0:T(8,128)(2,1)S(1)} %kept.1.refs_0_), channel_id=1, source_target_pairs={{0,24},{4,28},{8,16},{12,20},{16,8},{20,12},{24,0},{28,4},{1,25},{... | collective-permute-start | bytes 110600 | tf_op jit(solution)/shard_map/ppermute | solution.py:24
  43.7 2.4 %residue.1 = (bf16[2048,512]{1,0:T(8,128)(2,1)}, f32[8,128]{1,0:T(8,128)S(1)}) custom-call(bf16[128,512]{1,0:T(8,128)(2,1)S(1)} %slope.1.refs_0_, bf16[128,512]{1,0:T(8,128)(2,1)S(1)} %collective-permute-done.15.refs_1_, bf16[128,512]{1,0:T(8,128)(2,1)S(1)} %collective-permute-done.13.refs_0_.refs_2_, ...), custom_call_target="tpu_custom_call" | custom-call | flops 1000 | bytes 1000 | tf_op jit(solution)/shard_map/residue/pallas_call | solution.py:274
  46.1 0.9 %collective-permute-done.17.refs_1_ = bf16[144,128]{1,0:T(8,128)(2,1)S(1)} collective-permute-done((bf16[144,128]{1,0:T(8,128)(2,1)S(1)}, bf16[144,128]{1,0:T(8,128)(2,1)S(1)}, u32[]{:S(2)}, u32[]{:S(2)}) %collective-permute-start.17) | collective-permute-done | bytes 36896 | tf_op jit(solution)/shard_map/ppermute | solution.py:24
  47.1 6.1 %collective-permute-start.19 = (bf16[576,128]{1,0:T(8,128)(2,1)S(1)}, bf16[576,128]{1,0:T(8,128)(2,1)S(1)}, u32[]{:S(2)}, u32[]{:S(2)}) collective-permute-start(bf16[576,128]{1,0:T(8,128)(2,1)S(1)} %join.5.group), channel_id=1, source_target_pairs={{0,4},{4,0},{8,12},{12,8},{16,20},{20,16},{24,28},{28,24},{1,5},{5... | collective-permute-start | bytes 442376 | tf_op jit(solution)/shard_map/ppermute | solution.py:24
  53.2 1.4 %half.1 = f32[2048,512]{1,0:T(8,128)S(1)} custom-call(bf16[576,128]{1,0:T(8,128)(2,1)S(1)} %join.5.group), custom_call_target="tpu_custom_call" | custom-call | flops 1000 | bytes 1000 | tf_op jit(solution)/shard_map/half/pallas_call | solution.py:356
  54.6 2.6 %outer.1 = f32[2048,512]{1,0:T(8,128)} custom-call(bf16[576,128]{1,0:T(8,128)(2,1)S(1)} %collective-permute-done.19.group, f32[2048,512]{1,0:T(8,128)S(1)} %half.1), custom_call_target="tpu_custom_call" | custom-call | flops 1000 | bytes 1000 | tf_op jit(solution)/shard_map/outer/pallas_call | solution.py:364
  (41 shorter events, 3.7 us)
Async XLA Ops:
  0.6 12.3 %copy-start.6 = (s32[1,1,128]{2,1,0:T(1,128)S(1)}, s32[1,1,128]{2,1,0:T(1,128)}, u32[]{:S(2)}) copy-start(s32[1,1,128]{2,1,0:T(1,128)} %param.11) | copy-start | bytes 1540
  1.7 8.2 %collective-permute-start.1 = (bf16[64,2048]{1,0:T(8,128)(2,1)S(1)}, bf16[64,2048]{1,0:T(8,128)(2,1)S(1)}, u32[]{:S(2)}, u32[]{:S(2)}) collective-permute-start(bf16[64,2048]{1,0:T(8,128)(2,1)S(1)} %get-tuple-element.56), channel_id=1, source_target_pairs={{0,2},{1,3},{2,0},{3,1},{4,6},{5,7},{6,4},{7,5},{8,10},{9,11},{10,... | collective-permute-start | bytes 786440 | tf_op jit(solution)/shard_map/ppermute | solution.py:24
  3.9 7.1 %collective-permute-start = (bf16[64,2048]{1,0:T(8,128)(2,1)S(1)}, bf16[64,2048]{1,0:T(8,128)(2,1)S(1)}, u32[]{:S(2)}, u32[]{:S(2)}) collective-permute-start(bf16[64,2048]{1,0:T(8,128)(2,1)S(1)} %get-tuple-element.57.refs_0_), channel_id=1, source_target_pairs={{0,1},{1,0},{2,3},{3,2},{4,5},{5,4},{6,7},{7,6},{8,9},{9,8},{10,11... | collective-permute-start | bytes 786440 | tf_op jit(solution)/shard_map/ppermute | solution.py:24
  5.1 1.6 %copy-start = (bf16[1,128,8192]{2,1,0:T(8,128)(2,1)S(1)}, bf16[1,128,8192]{2,1,0:T(8,128)(2,1)}, u32[]{:S(2)}) copy-start(bf16[1,128,8192]{2,1,0:T(8,128)(2,1)} %param.6) | copy-start | bytes 6291460
  6.7 9.0 %copy-start.1 = (bf16[1,128,8192]{2,1,0:T(8,128)(2,1)S(1)}, bf16[1,128,8192]{2,1,0:T(8,128)(2,1)}, u32[]{:S(2)}) copy-start(bf16[1,128,8192]{2,1,0:T(8,128)(2,1)} %param.6) | copy-start | bytes 6291460
  6.7 9.6 %collective-permute-start.4 = (bf16[64,2048]{1,0:T(8,128)(2,1)S(1)}, bf16[64,2048]{1,0:T(8,128)(2,1)S(1)}, u32[]{:S(2)}, u32[]{:S(2)}) collective-permute-start(bf16[64,2048]{1,0:T(8,128)(2,1)S(1)} %get-tuple-element.33), channel_id=1, source_target_pairs={{0,1},{1,0},{2,3},{3,2},{4,5},{5,4},{6,7},{7,6},{8,9},{9,8},{10,11... | collective-permute-start | bytes 786440 | tf_op jit(solution)/shard_map/ppermute | solution.py:24
  7.1 10.5 %collective-permute-start.5 = (bf16[64,2048]{1,0:T(8,128)(2,1)S(1)}, bf16[64,2048]{1,0:T(8,128)(2,1)S(1)}, u32[]{:S(2)}, u32[]{:S(2)}) collective-permute-start(bf16[64,2048]{1,0:T(8,128)(2,1)S(1)} %get-tuple-element.34), channel_id=1, source_target_pairs={{0,2},{1,3},{2,0},{3,1},{4,6},{5,7},{6,4},{7,5},{8,10},{9,11},{10,... | collective-permute-start | bytes 786440 | tf_op jit(solution)/shard_map/ppermute | solution.py:24
  9.9 12.1 %collective-permute-start.3 = (bf16[64,2048]{1,0:T(8,128)(2,1)S(1)}, bf16[64,2048]{1,0:T(8,128)(2,1)S(1)}, u32[]{:S(2)}, u32[]{:S(2)}) collective-permute-start(bf16[64,2048]{1,0:T(8,128)(2,1)S(1)} %collective-permute-done.1.refs_2_), channel_id=1, source_target_pairs={{0,1},{1,0},{2,3},{3,2},{4,5},{5,4},{6,7},{7,6},{8,9},{9,8},{10,11... | collective-permute-start | bytes 786440 | tf_op jit(solution)/shard_map/ppermute | solution.py:24
  11.0 10.9 %collective-permute-start.2 = (bf16[64,2048]{1,0:T(8,128)(2,1)S(1)}, bf16[64,2048]{1,0:T(8,128)(2,1)S(1)}, u32[]{:S(2)}, u32[]{:S(2)}) collective-permute-start(bf16[64,2048]{1,0:T(8,128)(2,1)S(1)} %collective-permute-done.refs_1_), channel_id=1, source_target_pairs={{0,2},{1,3},{2,0},{3,1},{4,6},{5,7},{6,4},{7,5},{8,10},{9,11},{10,... | collective-permute-start | bytes 786440 | tf_op jit(solution)/shard_map/ppermute | solution.py:24
  12.9 1.6 %copy-start.3 = (bf16[1,2048,512]{2,1,0:T(8,128)(2,1)S(1)}, bf16[1,2048,512]{2,1,0:T(8,128)(2,1)}, u32[]{:S(2)}) copy-start(bf16[1,2048,512]{2,1,0:T(8,128)(2,1)} %param.9) | copy-start | bytes 6291460
  15.6 2.0 %copy-start.2 = (bf16[1,2048,512]{2,1,0:T(8,128)(2,1)S(1)}, bf16[1,2048,512]{2,1,0:T(8,128)(2,1)}, u32[]{:S(2)}) copy-start(bf16[1,2048,512]{2,1,0:T(8,128)(2,1)} %param.8) | copy-start | bytes 6291460
  15.7 11.8 %collective-permute-start.8 = (bf16[64,2048]{1,0:T(8,128)(2,1)S(1)}, bf16[64,2048]{1,0:T(8,128)(2,1)S(1)}, u32[]{:S(2)}, u32[]{:S(2)}) collective-permute-start(bf16[64,2048]{1,0:T(8,128)(2,1)S(1)} %get-tuple-element.39), channel_id=1, source_target_pairs={{0,1},{1,0},{2,3},{3,2},{4,5},{5,4},{6,7},{7,6},{8,9},{9,8},{10,11... | collective-permute-start | bytes 786440 | tf_op jit(solution)/shard_map/ppermute | solution.py:24
  16.3 11.2 %collective-permute-start.9 = (bf16[64,2048]{1,0:T(8,128)(2,1)S(1)}, bf16[64,2048]{1,0:T(8,128)(2,1)S(1)}, u32[]{:S(2)}, u32[]{:S(2)}) collective-permute-start(bf16[64,2048]{1,0:T(8,128)(2,1)S(1)} %get-tuple-element.40), channel_id=1, source_target_pairs={{0,2},{1,3},{2,0},{3,1},{4,6},{5,7},{6,4},{7,5},{8,10},{9,11},{10,... | collective-permute-start | bytes 786440 | tf_op jit(solution)/shard_map/ppermute | solution.py:24
  22.7 10.5 %collective-permute-start.6 = (bf16[128,512]{1,0:T(8,128)(2,1)S(1)}, bf16[128,512]{1,0:T(8,128)(2,1)S(1)}, u32[]{:S(2)}, u32[]{:S(2)}) collective-permute-start(bf16[128,512]{1,0:T(8,128)(2,1)S(1)} %get-tuple-element.37.refs_3_), channel_id=1, source_target_pairs={{0,3},{1,2},{2,1},{3,0},{4,7},{5,6},{6,5},{7,4},{8,11},{9,10},{10,... | collective-permute-start | bytes 393224 | tf_op jit(solution)/shard_map/ppermute | solution.py:24
  24.0 7.8 %collective-permute-start.11 = (bf16[64,512]{1,0:T(8,128)(2,1)S(1)}, bf16[64,512]{1,0:T(8,128)(2,1)S(1)}, u32[]{:S(2)}, u32[]{:S(2)}) collective-permute-start(bf16[64,512]{1,0:T(8,128)(2,1)S(1)} %get-tuple-element.35.refs_4_), channel_id=1, source_target_pairs={{0,2},{1,3},{2,0},{3,1},{4,6},{5,7},{6,4},{7,5},{8,10},{9,11},{10,... | collective-permute-start | bytes 196616 | tf_op jit(solution)/shard_map/ppermute | solution.py:24
  25.1 6.6 %collective-permute-start.7 = (bf16[64,512]{1,0:T(8,128)(2,1)S(1)}, bf16[64,512]{1,0:T(8,128)(2,1)S(1)}, u32[]{:S(2)}, u32[]{:S(2)}) collective-permute-start(bf16[64,512]{1,0:T(8,128)(2,1)S(1)} %get-tuple-element.38), channel_id=1, source_target_pairs={{0,1},{1,0},{2,3},{3,2},{4,5},{5,4},{6,7},{7,6},{8,9},{9,8},{10,11... | collective-permute-start | bytes 196616 | tf_op jit(solution)/shard_map/ppermute | solution.py:24
  26.0 7.2 %copy-start.5 = (bf16[1,128,512]{2,1,0:T(8,128)(2,1)S(1)}, bf16[1,128,512]{2,1,0:T(8,128)(2,1)}, u32[]{:S(2)}) copy-start(bf16[1,128,512]{2,1,0:T(8,128)(2,1)} %param.7) | copy-start | bytes 393220
  28.0 15.7 %copy-start.4 = (bf16[1,2048,512]{2,1,0:T(8,128)(2,1)S(1)}, bf16[1,2048,512]{2,1,0:T(8,128)(2,1)}, u32[]{:S(2)}) copy-start(bf16[1,2048,512]{2,1,0:T(8,128)(2,1)} %param.9) | copy-start | bytes 6291460
  28.0 5.1 %collective-permute-start.12 = (bf16[64,512]{1,0:T(8,128)(2,1)S(1)}, bf16[64,512]{1,0:T(8,128)(2,1)S(1)}, u32[]{:S(2)}, u32[]{:S(2)}) collective-permute-start(bf16[64,512]{1,0:T(8,128)(2,1)S(1)} %get-tuple-element.44), channel_id=1, source_target_pairs={{0,2},{1,3},{2,0},{3,1},{4,6},{5,7},{6,4},{7,5},{8,10},{9,11},{10,... | collective-permute-start | bytes 196616 | tf_op jit(solution)/shard_map/ppermute | solution.py:24
  28.5 4.7 %collective-permute-start.10 = (bf16[64,512]{1,0:T(8,128)(2,1)S(1)}, bf16[64,512]{1,0:T(8,128)(2,1)S(1)}, u32[]{:S(2)}, u32[]{:S(2)}) collective-permute-start(bf16[64,512]{1,0:T(8,128)(2,1)S(1)} %get-tuple-element.43.refs_4_), channel_id=1, source_target_pairs={{0,1},{1,0},{2,3},{3,2},{4,5},{5,4},{6,7},{7,6},{8,9},{9,8},{10,11... | collective-permute-start | bytes 196616 | tf_op jit(solution)/shard_map/ppermute | solution.py:24
  33.3 4.9 %collective-permute-start.15 = (bf16[128,512]{1,0:T(8,128)(2,1)S(1)}, bf16[128,512]{1,0:T(8,128)(2,1)S(1)}, u32[]{:S(2)}, u32[]{:S(2)}) collective-permute-start(bf16[128,512]{1,0:T(8,128)(2,1)S(1)} %slope.1.refs_0_), channel_id=1, source_target_pairs={{0,3},{1,2},{2,1},{3,0},{4,7},{5,6},{6,5},{7,4},{8,11},{9,10},{10,... | collective-permute-start | bytes 393224 | tf_op jit(solution)/shard_map/ppermute | solution.py:24
  34.8 4.6 %collective-permute-start.14 = (bf16[128,512]{1,0:T(8,128)(2,1)S(1)}, bf16[128,512]{1,0:T(8,128)(2,1)S(1)}, u32[]{:S(2)}, u32[]{:S(2)}) collective-permute-start(bf16[128,512]{1,0:T(8,128)(2,1)S(1)} %slope.1.refs_0_), channel_id=1, source_target_pairs={{0,2},{1,3},{2,0},{3,1},{4,6},{5,7},{6,4},{7,5},{8,10},{9,11},{10,... | collective-permute-start | bytes 393224 | tf_op jit(solution)/shard_map/ppermute | solution.py:24
  35.5 4.0 %collective-permute-start.13 = (bf16[128,512]{1,0:T(8,128)(2,1)S(1)}, bf16[128,512]{1,0:T(8,128)(2,1)S(1)}, u32[]{:S(2)}, u32[]{:S(2)}) collective-permute-start(bf16[128,512]{1,0:T(8,128)(2,1)S(1)} %slope.1.refs_0_), channel_id=1, source_target_pairs={{0,1},{1,0},{2,3},{3,2},{4,5},{5,4},{6,7},{7,6},{8,9},{9,8},{10,11... | collective-permute-start | bytes 393224 | tf_op jit(solution)/shard_map/ppermute | solution.py:24
  39.7 6.3 %collective-permute-start.16 = (bf16[144,128]{1,0:T(8,128)(2,1)S(1)}, bf16[144,128]{1,0:T(8,128)(2,1)S(1)}, u32[]{:S(2)}, u32[]{:S(2)}) collective-permute-start(bf16[144,128]{1,0:T(8,128)(2,1)S(1)} %kept.1.refs_0_), channel_id=1, source_target_pairs={{0,24},{4,28},{8,16},{12,20},{16,8},{20,12},{24,0},{28,4},{1,25},{... | collective-permute-start | bytes 110600 | tf_op jit(solution)/shard_map/ppermute | solution.py:24
  43.3 3.7 %collective-permute-start.17 = (bf16[144,128]{1,0:T(8,128)(2,1)S(1)}, bf16[144,128]{1,0:T(8,128)(2,1)S(1)}, u32[]{:S(2)}, u32[]{:S(2)}) collective-permute-start(bf16[144,128]{1,0:T(8,128)(2,1)S(1)} %kept.1.refs_0_), channel_id=1, source_target_pairs={{0,16},{4,20},{8,24},{12,28},{16,0},{20,4},{24,8},{28,12},{1,17},{... | collective-permute-start | bytes 110600 | tf_op jit(solution)/shard_map/ppermute | solution.py:24
  43.3 3.7 %collective-permute-start.18 = (bf16[144,128]{1,0:T(8,128)(2,1)S(1)}, bf16[144,128]{1,0:T(8,128)(2,1)S(1)}, u32[]{:S(2)}, u32[]{:S(2)}) collective-permute-start(bf16[144,128]{1,0:T(8,128)(2,1)S(1)} %kept.1.refs_0_), channel_id=1, source_target_pairs={{0,8},{4,12},{8,0},{12,4},{16,24},{20,28},{24,16},{28,20},{1,9},{5... | collective-permute-start | bytes 110600 | tf_op jit(solution)/shard_map/ppermute | solution.py:24
  47.1 7.5 %collective-permute-start.19 = (bf16[576,128]{1,0:T(8,128)(2,1)S(1)}, bf16[576,128]{1,0:T(8,128)(2,1)S(1)}, u32[]{:S(2)}, u32[]{:S(2)}) collective-permute-start(bf16[576,128]{1,0:T(8,128)(2,1)S(1)} %join.5.group), channel_id=1, source_target_pairs={{0,4},{4,0},{8,12},{12,8},{16,20},{20,16},{24,28},{28,24},{1,5},{5... | collective-permute-start | bytes 442376 | tf_op jit(solution)/shard_map/ppermute | solution.py:24

commit v11 on v8

--- a/solution.py
+++ b/solution.py
@@ -244,8 +244,12 @@
 
 
 def send_out(held, out, sems, t, tile):
-    rows = pl.ds(t * tile, tile)
-    return pltpu.make_async_copy(held.at[rows, :], out.at[rows, :], sems.at[t])
+    share = tile // sems.shape[1]
+    spans = [pl.ds(t * tile + k * share, share) for k in range(sems.shape[1])]
+    return [
+        pltpu.make_async_copy(held.at[rows, :], out.at[rows, :], sems.at[t, k])
+        for k, rows in enumerate(spans)
+    ]
 
 
 def residue_kernel(order, tile, *refs):
@@ -262,9 +266,11 @@
             pseudo += jnp.dot(xt[rows, :], part, preferred_element_type=jnp.float32)
             start += xt.shape[1]
         held[rows, :] = jnp.where(keep[rows, :] > 0, pseudo, 0.0).astype(jnp.bfloat16)
-        send_out(held, out, sems, t, tile).start()
+        for copy in send_out(held, out, sems, t, tile):
+            copy.start()
     for t in range(tiles):
-        send_out(held, out, sems, t, tile).wait()
+        for copy in send_out(held, out, sems, t, tile):
+            copy.wait()
 
 
 def residue(slopes, order, xts, fb, keep):
@@ -282,7 +288,7 @@
         scratch_shapes=[
             pltpu.VMEM((total, kw), jnp.bfloat16),
             pltpu.VMEM((depth, kw), jnp.bfloat16),
-            pltpu.SemaphoreType.DMA((depth // tile,)),
+            pltpu.SemaphoreType.DMA((depth // tile, 4)),
         ],
         compiler_params=params(14),
         cost_estimate=BRIEF,
@@ -342,9 +348,11 @@
     for t in range(tiles):
         rows = slice(t * tile, (t + 1) * tile)
         held[rows, :] = (half[rows, :] + place(lines, wide, t, tile)) / n
-        send_out(held, out, sems, t, tile).start()
+        for copy in send_out(held, out, sems, t, tile):
+            copy.start()
     for t in range(tiles):
-        send_out(held, out, sems, t, tile).wait()
+        for copy in send_out(held, out, sems, t, tile):
+            copy.wait()
 
 
 def outer(groups, cap, depth, kw):
@@ -366,7 +374,7 @@
         out_shape=shape,
         out_specs=ANY,
         scratch_shapes=scratch
-        + [pltpu.VMEM((depth, kw), jnp.float32), pltpu.SemaphoreType.DMA((depth // tile,))],
+        + [pltpu.VMEM((depth, kw), jnp.float32), pltpu.SemaphoreType.DMA((depth // tile, 4))],
         compiler_params=params(14),
         cost_estimate=BRIEF,
         name="outer",
@@ -418,7 +426,7 @@
     order_near = [(k, low, high) for low, high in spans for k in range(len(near))]
     wide = gather(slopes[:n_far], order_far, xg_far)
     message = kept(slopes[n_far:], order_near, wide, xg_near, fbk, slot_row)
-    same_core = [swap(message, "rep", n_rep, d) for d in range(n_rep - 2, 0, -2)]
+    same_core = [swap(message, "rep", n_rep, d) for d in [2, *range(n_rep - 2, 2, -2)]]
     order = order_far + [(n_far + k, low, high) for k, low, high in order_near]
     new_feedback, token = residue(slopes, order, [xt_far, xt_near], fb, keep)
     joined, after = message, [token]

time: 57.6 us -> 58.6 us (1.017)
  no operation moved by 1% of the time
where the time goes in v11:
time: 58.6 us; the launch traced here: 58.3 us
  starting transfers between devices  23.7 us (40%)
  waiting for transfers between devices  16.2 us (28%)
  Pallas kernels  12.5 us (21%)
  local copies, waits for them, and re-layouts  4.29 us (7%)
  between operations  1.69 us (3%)
    ppermute x17, starting transfers between devices, swap(): return lax.ppermute(x, axis, [(i, i ^ d) for i in range(n)])  23.7 us
    ppermute x17, waiting for transfers between devices, swap(): return lax.ppermute(x, axis, [(i, i ^ d) for i in range(n)])  16.2 us
    unnamed x14, local copies, waits for them, and re-layouts  3.2 us
    pallas_call x1, Pallas kernels, outer(): pl.pallas_call(functools.partial(outer_kernel, cap, kw // LANES, tile, n)...  2.74 us
    pallas_call x1, Pallas kernels, residue(): pl.pallas_call(functools.partial(residue_kernel, order, tile), out_shape=...  2.5 us
    pallas_call x3, Pallas kernels, project(): pl.pallas_call(functools.partial(project_kernel, n), out_shape=[jax.Shape...  1.76 us
    pallas_call x2, Pallas kernels, prepare(): pl.pallas_call(functools.partial(prepare_kernel, per_row, len(xs)), out_s...  1.55 us
    pallas_call x1, Pallas kernels, outer(): pl.pallas_call(functools.partial(half_kernel, cap, kw // LANES, tile), ou...  1.42 us
  transfers between devices with their start and end apart: 17, of which 9 were waited for; matrix products, arithmetic and copies ran while one was open for 0% of the time, Pallas kernels for 16%

profile of v11, /device:TPU:1, one launch (start us, length us, event | category | flops | bytes accessed | tf_op | source)
XLA Modules:
  0.0 58.3 jit_solution(15137114429774683084)
XLA Ops:
  0.6 1.1 %dynamic-slice_bitcast_fusion.refs_0_ = bf16[128,2048]{1,0:T(8,128)(2,1)S(1)} fusion(bf16[1,128,8192]{2,1,0:T(8,128)(2,1)} %param.6, s32[]{:T(128)S(6)} %select_n.3), kind=kLoop, calls=%fused_computation | loop fusion | bytes 1048580 | tf_op jit(solution)/shard_map/dynamic_slice | solution.py:397
  1.7 3.1 %collective-permute-start = (bf16[128,2048]{1,0:T(8,128)(2,1)S(1)}, bf16[128,2048]{1,0:T(8,128)(2,1)S(1)}, u32[]{:S(2)}, u32[]{:S(2)}) collective-permute-start(bf16[128,2048]{1,0:T(8,128)(2,1)S(1)} %dynamic-slice_bitcast_fusion.refs_0_), channel_id=1, source_target_pairs={{0,3},{1,2},{2,1},{3,0},{4,7},{5,6},{6,5},{7,4},{8,11},{9,10},{10,... | collective-permute-start | bytes 1572872 | tf_op jit(solution)/shard_map/ppermute | solution.py:24
  4.8 1.6 %copy-done = bf16[1,128,8192]{2,1,0:T(8,128)(2,1)S(1)} copy-done((bf16[1,128,8192]{2,1,0:T(8,128)(2,1)S(1)}, bf16[1,128,8192]{2,1,0:T(8,128)(2,1)}, u32[]{:S(2)}) %copy-start) | copy-done | bytes 2097176
  7.7 1.6 %copy-done.3 = bf16[1,2048,512]{2,1,0:T(8,128)(2,1)S(1)} copy-done((bf16[1,2048,512]{2,1,0:T(8,128)(2,1)S(1)}, bf16[1,2048,512]{2,1,0:T(8,128)(2,1)}, u32[]{:S(2)}) %copy-start.3) | copy-done | bytes 2097176
  9.3 1.1 %early.1 = (f32[128,128]{1,0:T(8,128)S(1)}, bf16[2048,512]{1,0:T(8,128)(2,1)S(1)}, f32[8,128]{1,0:T(8,128)S(1)}) custom-call(s32[1,128]{1,0:T(1,128)S(1)} %bitcast.17, s32[1,1]{1,0:T(1,128)S(6)} %copy.8.count.refs_2_.refs_3_, bf16[2048,512]{1,0:T(8,128)(2,1)S(1)} %bitcast.14, f32[8,128]{1,0:T(8,128)S(1)} %get-tuple-element.29.after), custom_call_target="tpu_custom_call" | custom-call | flops 1000 | bytes 1000 | tf_op jit(solution)/shard_map/early/pallas_call | solution.py:145
  10.5 1.3 %collective-permute-start.5 = (bf16[32,2048]{1,0:T(8,128)(2,1)S(1)}, bf16[32,2048]{1,0:T(8,128)(2,1)S(1)}, u32[]{:S(2)}, u32[]{:S(2)}) collective-permute-start(bf16[32,2048]{1,0:T(8,128)(2,1)S(1)} %get-tuple-element.40), channel_id=1, source_target_pairs={{0,1},{1,0},{2,3},{3,2},{4,5},{5,4},{6,7},{7,6},{8,9},{9,8},{10,11... | collective-permute-start | bytes 393224 | tf_op jit(solution)/shard_map/ppermute | solution.py:24
  11.8 1.2 %collective-permute-start.6 = (bf16[32,2048]{1,0:T(8,128)(2,1)S(1)}, bf16[32,2048]{1,0:T(8,128)(2,1)S(1)}, u32[]{:S(2)}, u32[]{:S(2)}) collective-permute-start(bf16[32,2048]{1,0:T(8,128)(2,1)S(1)} %get-tuple-element.41), channel_id=1, source_target_pairs={{0,2},{1,3},{2,0},{3,1},{4,6},{5,7},{6,4},{7,5},{8,10},{9,11},{10,... | collective-permute-start | bytes 393224 | tf_op jit(solution)/shard_map/ppermute | solution.py:24
  13.1 0.6 %cut.5 = (bf16[128,2048]{1,0:T(8,128)(2,1)S(1)}, f32[8,128]{1,0:T(8,128)}) custom-call(bf16[128,8192]{1,0:T(8,128)(2,1)S(1)} %bitcast.10, f32[8,128]{1,0:T(8,128)S(1)} %get-tuple-element.31.refs_0_), custom_call_target="tpu_custom_call" | custom-call | flops 1000 | bytes 1000 | tf_op jit(solution)/shard_map/cut/pallas_call | solution.py:43
  13.7 2.8 %collective-permute-done.refs_1_ = bf16[128,2048]{1,0:T(8,128)(2,1)S(1)} collective-permute-done((bf16[128,2048]{1,0:T(8,128)(2,1)S(1)}, bf16[128,2048]{1,0:T(8,128)(2,1)S(1)}, u32[]{:S(2)}, u32[]{:S(2)}) %collective-permute-start) | collective-permute-done | bytes 524320 | tf_op jit(solution)/shard_map/ppermute | solution.py:24
  16.5 0.7 %project.3 = (f32[128,512]{1,0:T(8,128)S(1)}, bf16[128,512]{1,0:T(8,128)(2,1)S(1)}, bf16[256,2048]{1,0:T(8,128)(2,1)S(1)}) custom-call(bf16[128,2048]{1,0:T(8,128)(2,1)S(1)} %get-tuple-element.32.refs_0_, bf16[128,2048]{1,0:T(8,128)(2,1)S(1)} %collective-permute-done.refs_1_, bf16[2048,512]{1,0:T(8,128)(2,1)S(1)} %bitcast.11), custom_call_target="tpu_custom_call" | custom-call | flops 1000 | bytes 1000 | tf_op jit(solution)/shard_map/project/pallas_call | solution.py:73
  17.2 2.1 %collective-permute-start.1 = (bf16[128,512]{1,0:T(8,128)(2,1)S(1)}, bf16[128,512]{1,0:T(8,128)(2,1)S(1)}, u32[]{:S(2)}, u32[]{:S(2)}) collective-permute-start(bf16[128,512]{1,0:T(8,128)(2,1)S(1)} %get-tuple-element.34), channel_id=1, source_target_pairs={{0,3},{1,2},{2,1},{3,0},{4,7},{5,6},{6,5},{7,4},{8,11},{9,10},{10,... | collective-permute-start | bytes 393224 | tf_op jit(solution)/shard_map/ppermute | solution.py:24
  19.3 0.6 %prepare.2 = (bf16[128,256]{1,0:T(8,128)(2,1)S(1)}, bf16[2048,256]{1,0:T(8,128)(2,1)S(1)}, f32[8,128]{1,0:T(8,128)S(1)}) custom-call(bf16[256,2048]{1,0:T(8,128)(2,1)S(1)} %get-tuple-element.37.refs_0_, s32[1,128]{1,0:T(1,128)S(1)} %bitcast.18, s32[1,1]{1,0:T(1,128)S(6)} %copy.8.count.refs_2_.refs_3_), custom_call_target="tpu_custom_call" | custom-call | flops 1000 | bytes 1000 | tf_op jit(solution)/shard_map/prepare/pallas_call | solution.py:181
  19.9 4.9 %collective-permute-done.2.refs_0_ = bf16[96,2048]{1,0:T(8,128)(2,1)S(1)} collective-permute-done((bf16[96,2048]{1,0:T(8,128)(2,1)S(1)}, bf16[96,2048]{1,0:T(8,128)(2,1)S(1)}, u32[]{:S(2)}, u32[]{:S(2)}) %collective-permute-start.2) | collective-permute-done | bytes 393248 | tf_op jit(solution)/shard_map/ppermute | solution.py:24
  24.8 0.8 %collective-permute-done.3.refs_1_ = bf16[96,2048]{1,0:T(8,128)(2,1)S(1)} collective-permute-done((bf16[96,2048]{1,0:T(8,128)(2,1)S(1)}, bf16[96,2048]{1,0:T(8,128)(2,1)S(1)}, u32[]{:S(2)}, u32[]{:S(2)}) %collective-permute-start.3) | collective-permute-done | bytes 393248 | tf_op jit(solution)/shard_map/ppermute | solution.py:24
  25.6 0.6 project.4
  26.2 1.5 %collective-permute-start.4 = (bf16[96,512]{1,0:T(8,128)(2,1)S(1)}, bf16[96,512]{1,0:T(8,128)(2,1)S(1)}, u32[]{:S(2)}, u32[]{:S(2)}) collective-permute-start(bf16[96,512]{1,0:T(8,128)(2,1)S(1)} %get-tuple-element.39), channel_id=1, source_target_pairs={{0,1},{1,0},{2,3},{3,2},{4,5},{5,4},{6,7},{7,6},{8,9},{9,8},{10,11... | collective-permute-start | bytes 294920 | tf_op jit(solution)/shard_map/ppermute | solution.py:24
  27.7 1.2 %collective-permute-start.8 = (bf16[96,512]{1,0:T(8,128)(2,1)S(1)}, bf16[96,512]{1,0:T(8,128)(2,1)S(1)}, u32[]{:S(2)}, u32[]{:S(2)}) collective-permute-start(bf16[96,512]{1,0:T(8,128)(2,1)S(1)} %get-tuple-element.42.refs_3_), channel_id=1, source_target_pairs={{0,2},{1,3},{2,0},{3,1},{4,6},{5,7},{6,4},{7,5},{8,10},{9,11},{10,... | collective-permute-start | bytes 294920 | tf_op jit(solution)/shard_map/ppermute | solution.py:24
  29.6 1.8 %collective-permute-start.9 = (bf16[32,512]{1,0:T(8,128)(2,1)S(1)}, bf16[32,512]{1,0:T(8,128)(2,1)S(1)}, u32[]{:S(2)}, u32[]{:S(2)}) collective-permute-start(bf16[32,512]{1,0:T(8,128)(2,1)S(1)} %get-tuple-element.44), channel_id=1, source_target_pairs={{0,2},{1,3},{2,0},{3,1},{4,6},{5,7},{6,4},{7,5},{8,10},{9,11},{10,... | collective-permute-start | bytes 98312 | tf_op jit(solution)/shard_map/ppermute | solution.py:24
  31.4 1.2 %collective-permute-start.7 = (bf16[32,512]{1,0:T(8,128)(2,1)S(1)}, bf16[32,512]{1,0:T(8,128)(2,1)S(1)}, u32[]{:S(2)}, u32[]{:S(2)}) collective-permute-start(bf16[32,512]{1,0:T(8,128)(2,1)S(1)} %get-tuple-element.43.refs_4_), channel_id=1, source_target_pairs={{0,1},{1,0},{2,3},{3,2},{4,5},{5,4},{6,7},{7,6},{8,9},{9,8},{10,11... | collective-permute-start | bytes 98312 | tf_op jit(solution)/shard_map/ppermute | solution.py:24
  32.6 0.9 %prepare.3 = (bf16[128,256]{1,0:T(8,128)(2,1)S(1)}, bf16[2048,256]{1,0:T(8,128)(2,1)S(1)}, f32[8,128]{1,0:T(8,128)S(1)}) custom-call(bf16[192,2048]{1,0:T(8,128)(2,1)S(1)} %get-tuple-element.45.refs_0_, bf16[64,2048]{1,0:T(8,128)(2,1)S(1)} %get-tuple-element.46.refs_1_, s32[1,128]{1,0:T(1,128)S(1)} %bitcast.19, s32[1,1]{1,0:T(1,128)S(6)} %copy.8.count.refs_2_.refs_3_, ...), custom_call_target="tpu_custom_call" | custom-call | flops 1000 | bytes 1000 | tf_op jit(solution)/shard_map/prepare/pallas_call | solution.py:181
  33.6 0.9 %collective-permute-done.7.refs_4_ = bf16[32,512]{1,0:T(8,128)(2,1)S(1)} collective-permute-done((bf16[32,512]{1,0:T(8,128)(2,1)S(1)}, bf16[32,512]{1,0:T(8,128)(2,1)S(1)}, u32[]{:S(2)}, u32[]{:S(2)}) %collective-permute-start.7) | collective-permute-done | bytes 32800 | tf_op jit(solution)/shard_map/ppermute | solution.py:24
  34.6 1.7 %collective-permute-start.12 = (bf16[128,512]{1,0:T(8,128)(2,1)S(1)}, bf16[128,512]{1,0:T(8,128)(2,1)S(1)}, u32[]{:S(2)}, u32[]{:S(2)}) collective-permute-start(bf16[128,512]{1,0:T(8,128)(2,1)S(1)} %slope.1.refs_0_), channel_id=1, source_target_pairs={{0,3},{1,2},{2,1},{3,0},{4,7},{5,6},{6,5},{7,4},{8,11},{9,10},{10,... | collective-permute-start | bytes 393224 | tf_op jit(solution)/shard_map/ppermute | solution.py:24
  36.3 0.8 %collective-permute-start.11 = (bf16[128,512]{1,0:T(8,128)(2,1)S(1)}, bf16[128,512]{1,0:T(8,128)(2,1)S(1)}, u32[]{:S(2)}, u32[]{:S(2)}) collective-permute-start(bf16[128,512]{1,0:T(8,128)(2,1)S(1)} %slope.1.refs_0_), channel_id=1, source_target_pairs={{0,2},{1,3},{2,0},{3,1},{4,6},{5,7},{6,4},{7,5},{8,10},{9,11},{10,... | collective-permute-start | bytes 393224 | tf_op jit(solution)/shard_map/ppermute | solution.py:24
  37.3 2.1 %collective-permute-done.12.refs_1_ = bf16[128,512]{1,0:T(8,128)(2,1)S(1)} collective-permute-done((bf16[128,512]{1,0:T(8,128)(2,1)S(1)}, bf16[128,512]{1,0:T(8,128)(2,1)S(1)}, u32[]{:S(2)}, u32[]{:S(2)}) %collective-permute-start.12) | collective-permute-done | bytes 131104 | tf_op jit(solution)/shard_map/ppermute | solution.py:24
  39.6 2.4 %collective-permute-done.11.refs_1_.refs_3_ = bf16[128,512]{1,0:T(8,128)(2,1)S(1)} collective-permute-done((bf16[128,512]{1,0:T(8,128)(2,1)S(1)}, bf16[128,512]{1,0:T(8,128)(2,1)S(1)}, u32[]{:S(2)}, u32[]{:S(2)}) %collective-permute-start.11) | collective-permute-done | bytes 131104 | tf_op jit(solution)/shard_map/ppermute | solution.py:24
  42.7 1.4 %collective-permute-start.13 = (bf16[144,128]{1,0:T(8,128)(2,1)S(1)}, bf16[144,128]{1,0:T(8,128)(2,1)S(1)}, u32[]{:S(2)}, u32[]{:S(2)}) collective-permute-start(bf16[144,128]{1,0:T(8,128)(2,1)S(1)} %kept.1.refs_0_), channel_id=1, source_target_pairs={{0,8},{4,12},{8,0},{12,4},{16,24},{20,28},{24,16},{28,20},{1,9},{5... | collective-permute-start | bytes 110600 | tf_op jit(solution)/shard_map/ppermute | solution.py:24
  44.1 2.2 %collective-permute-start.14 = (bf16[144,128]{1,0:T(8,128)(2,1)S(1)}, bf16[144,128]{1,0:T(8,128)(2,1)S(1)}, u32[]{:S(2)}, u32[]{:S(2)}) collective-permute-start(bf16[144,128]{1,0:T(8,128)(2,1)S(1)} %kept.1.refs_0_), channel_id=1, source_target_pairs={{0,24},{4,28},{8,16},{12,20},{16,8},{20,12},{24,0},{28,4},{1,25},{... | collective-permute-start | bytes 110600 | tf_op jit(solution)/shard_map/ppermute | solution.py:24
  46.4 2.5 %residue.1 = (bf16[2048,512]{1,0:T(8,128)(2,1)}, f32[8,128]{1,0:T(8,128)S(1)}) custom-call(bf16[128,512]{1,0:T(8,128)(2,1)S(1)} %slope.1.refs_0_, bf16[128,512]{1,0:T(8,128)(2,1)S(1)} %collective-permute-done.12.refs_1_, bf16[128,512]{1,0:T(8,128)(2,1)S(1)} %collective-permute-done.10.refs_0_.refs_2_, ...), custom_call_target="tpu_custom_call" | custom-call | flops 1000 | bytes 1000 | tf_op jit(solution)/shard_map/residue/pallas_call | solution.py:280
  49.0 1.6 %collective-permute-done.15.refs_1_ = bf16[144,128]{1,0:T(8,128)(2,1)S(1)} collective-permute-done((bf16[144,128]{1,0:T(8,128)(2,1)S(1)}, bf16[144,128]{1,0:T(8,128)(2,1)S(1)}, u32[]{:S(2)}, u32[]{:S(2)}) %collective-permute-start.15) | collective-permute-done | bytes 36896 | tf_op jit(solution)/shard_map/ppermute | solution.py:24
  50.6 3.6 %collective-permute-start.16 = (bf16[576,128]{1,0:T(8,128)(2,1)S(1)}, bf16[576,128]{1,0:T(8,128)(2,1)S(1)}, u32[]{:S(2)}, u32[]{:S(2)}) collective-permute-start(bf16[576,128]{1,0:T(8,128)(2,1)S(1)} %join.5.group), channel_id=1, source_target_pairs={{0,4},{4,0},{8,12},{12,8},{16,20},{20,16},{24,28},{28,24},{1,5},{5... | collective-permute-start | bytes 442376 | tf_op jit(solution)/shard_map/ppermute | solution.py:24
  54.2 1.4 %half.1 = f32[2048,512]{1,0:T(8,128)S(1)} custom-call(bf16[576,128]{1,0:T(8,128)(2,1)S(1)} %join.5.group), custom_call_target="tpu_custom_call" | custom-call | flops 1000 | bytes 1000 | tf_op jit(solution)/shard_map/half/pallas_call | solution.py:364
  55.6 2.7 %outer.1 = f32[2048,512]{1,0:T(8,128)} custom-call(bf16[576,128]{1,0:T(8,128)(2,1)S(1)} %collective-permute-done.16.group, f32[2048,512]{1,0:T(8,128)S(1)} %half.1), custom_call_target="tpu_custom_call" | custom-call | flops 1000 | bytes 1000 | tf_op jit(solution)/shard_map/outer/pallas_call | solution.py:372
  (35 shorter events, 2.7 us)
Async XLA Ops:
  0.6 7.0 %copy-start.6 = (s32[1,1,128]{2,1,0:T(1,128)S(1)}, s32[1,1,128]{2,1,0:T(1,128)}, u32[]{:S(2)}) copy-start(s32[1,1,128]{2,1,0:T(1,128)} %param.11) | copy-start | bytes 1540
  1.7 14.8 %collective-permute-start = (bf16[128,2048]{1,0:T(8,128)(2,1)S(1)}, bf16[128,2048]{1,0:T(8,128)(2,1)S(1)}, u32[]{:S(2)}, u32[]{:S(2)}) collective-permute-start(bf16[128,2048]{1,0:T(8,128)(2,1)S(1)} %dynamic-slice_bitcast_fusion.refs_0_), channel_id=1, source_target_pairs={{0,3},{1,2},{2,1},{3,0},{4,7},{5,6},{6,5},{7,4},{8,11},{9,10},{10,... | collective-permute-start | bytes 1572872 | tf_op jit(solution)/shard_map/ppermute | solution.py:24
  4.8 1.6 %copy-start = (bf16[1,128,8192]{2,1,0:T(8,128)(2,1)S(1)}, bf16[1,128,8192]{2,1,0:T(8,128)(2,1)}, u32[]{:S(2)}) copy-start(bf16[1,128,8192]{2,1,0:T(8,128)(2,1)} %param.6) | copy-start | bytes 6291460
  6.4 4.0 %copy-start.1 = (bf16[1,128,8192]{2,1,0:T(8,128)(2,1)S(1)}, bf16[1,128,8192]{2,1,0:T(8,128)(2,1)}, u32[]{:S(2)}) copy-start(bf16[1,128,8192]{2,1,0:T(8,128)(2,1)} %param.6) | copy-start | bytes 6291460
  6.5 18.4 %collective-permute-start.2 = (bf16[96,2048]{1,0:T(8,128)(2,1)S(1)}, bf16[96,2048]{1,0:T(8,128)(2,1)S(1)}, u32[]{:S(2)}, u32[]{:S(2)}) collective-permute-start(bf16[96,2048]{1,0:T(8,128)(2,1)S(1)} %get-tuple-element.35), channel_id=1, source_target_pairs={{0,1},{1,0},{2,3},{3,2},{4,5},{5,4},{6,7},{7,6},{8,9},{9,8},{10,11... | collective-permute-start | bytes 1179656 | tf_op jit(solution)/shard_map/ppermute | solution.py:24
  6.8 18.8 %collective-permute-start.3 = (bf16[96,2048]{1,0:T(8,128)(2,1)S(1)}, bf16[96,2048]{1,0:T(8,128)(2,1)S(1)}, u32[]{:S(2)}, u32[]{:S(2)}) collective-permute-start(bf16[96,2048]{1,0:T(8,128)(2,1)S(1)} %get-tuple-element.36), channel_id=1, source_target_pairs={{0,2},{1,3},{2,0},{3,1},{4,6},{5,7},{6,4},{7,5},{8,10},{9,11},{10,... | collective-permute-start | bytes 1179656 | tf_op jit(solution)/shard_map/ppermute | solution.py:24
  7.7 1.6 %copy-start.3 = (bf16[1,2048,512]{2,1,0:T(8,128)(2,1)S(1)}, bf16[1,2048,512]{2,1,0:T(8,128)(2,1)}, u32[]{:S(2)}) copy-start(bf16[1,2048,512]{2,1,0:T(8,128)(2,1)} %param.9) | copy-start | bytes 6291460
  10.4 6.1 %copy-start.2 = (bf16[1,2048,512]{2,1,0:T(8,128)(2,1)S(1)}, bf16[1,2048,512]{2,1,0:T(8,128)(2,1)}, u32[]{:S(2)}) copy-start(bf16[1,2048,512]{2,1,0:T(8,128)(2,1)} %param.8) | copy-start | bytes 6291460
  10.5 18.4 %collective-permute-start.5 = (bf16[32,2048]{1,0:T(8,128)(2,1)S(1)}, bf16[32,2048]{1,0:T(8,128)(2,1)S(1)}, u32[]{:S(2)}, u32[]{:S(2)}) collective-permute-start(bf16[32,2048]{1,0:T(8,128)(2,1)S(1)} %get-tuple-element.40), channel_id=1, source_target_pairs={{0,1},{1,0},{2,3},{3,2},{4,5},{5,4},{6,7},{7,6},{8,9},{9,8},{10,11... | collective-permute-start | bytes 393224 | tf_op jit(solution)/shard_map/ppermute | solution.py:24
  11.8 17.3 %collective-permute-start.6 = (bf16[32,2048]{1,0:T(8,128)(2,1)S(1)}, bf16[32,2048]{1,0:T(8,128)(2,1)S(1)}, u32[]{:S(2)}, u32[]{:S(2)}) collective-permute-start(bf16[32,2048]{1,0:T(8,128)(2,1)S(1)} %get-tuple-element.41), channel_id=1, source_target_pairs={{0,2},{1,3},{2,0},{3,1},{4,6},{5,7},{6,4},{7,5},{8,10},{9,11},{10,... | collective-permute-start | bytes 393224 | tf_op jit(solution)/shard_map/ppermute | solution.py:24
  17.2 17.2 %collective-permute-start.1 = (bf16[128,512]{1,0:T(8,128)(2,1)S(1)}, bf16[128,512]{1,0:T(8,128)(2,1)S(1)}, u32[]{:S(2)}, u32[]{:S(2)}) collective-permute-start(bf16[128,512]{1,0:T(8,128)(2,1)S(1)} %get-tuple-element.34), channel_id=1, source_target_pairs={{0,3},{1,2},{2,1},{3,0},{4,7},{5,6},{6,5},{7,4},{8,11},{9,10},{10,... | collective-permute-start | bytes 393224 | tf_op jit(solution)/shard_map/ppermute | solution.py:24
  26.2 8.3 %copy-start.5 = (bf16[1,128,512]{2,1,0:T(8,128)(2,1)S(1)}, bf16[1,128,512]{2,1,0:T(8,128)(2,1)}, u32[]{:S(2)}) copy-start(bf16[1,128,512]{2,1,0:T(8,128)(2,1)} %param.7) | copy-start | bytes 393220
  26.2 8.2 %collective-permute-start.4 = (bf16[96,512]{1,0:T(8,128)(2,1)S(1)}, bf16[96,512]{1,0:T(8,128)(2,1)S(1)}, u32[]{:S(2)}, u32[]{:S(2)}) collective-permute-start(bf16[96,512]{1,0:T(8,128)(2,1)S(1)} %get-tuple-element.39), channel_id=1, source_target_pairs={{0,1},{1,0},{2,3},{3,2},{4,5},{5,4},{6,7},{7,6},{8,9},{9,8},{10,11... | collective-permute-start | bytes 294920 | tf_op jit(solution)/shard_map/ppermute | solution.py:24
  27.7 6.8 %collective-permute-start.8 = (bf16[96,512]{1,0:T(8,128)(2,1)S(1)}, bf16[96,512]{1,0:T(8,128)(2,1)S(1)}, u32[]{:S(2)}, u32[]{:S(2)}) collective-permute-start(bf16[96,512]{1,0:T(8,128)(2,1)S(1)} %get-tuple-element.42.refs_3_), channel_id=1, source_target_pairs={{0,2},{1,3},{2,0},{3,1},{4,6},{5,7},{6,4},{7,5},{8,10},{9,11},{10,... | collective-permute-start | bytes 294920 | tf_op jit(solution)/shard_map/ppermute | solution.py:24
  29.6 16.8 %copy-start.4 = (bf16[1,2048,512]{2,1,0:T(8,128)(2,1)S(1)}, bf16[1,2048,512]{2,1,0:T(8,128)(2,1)}, u32[]{:S(2)}) copy-start(bf16[1,2048,512]{2,1,0:T(8,128)(2,1)} %param.9) | copy-start | bytes 6291460
  29.6 4.0 %collective-permute-start.9 = (bf16[32,512]{1,0:T(8,128)(2,1)S(1)}, bf16[32,512]{1,0:T(8,128)(2,1)S(1)}, u32[]{:S(2)}, u32[]{:S(2)}) collective-permute-start(bf16[32,512]{1,0:T(8,128)(2,1)S(1)} %get-tuple-element.44), channel_id=1, source_target_pairs={{0,2},{1,3},{2,0},{3,1},{4,6},{5,7},{6,4},{7,5},{8,10},{9,11},{10,... | collective-permute-start | bytes 98312 | tf_op jit(solution)/shard_map/ppermute | solution.py:24
  31.4 3.0 %collective-permute-start.7 = (bf16[32,512]{1,0:T(8,128)(2,1)S(1)}, bf16[32,512]{1,0:T(8,128)(2,1)S(1)}, u32[]{:S(2)}, u32[]{:S(2)}) collective-permute-start(bf16[32,512]{1,0:T(8,128)(2,1)S(1)} %get-tuple-element.43.refs_4_), channel_id=1, source_target_pairs={{0,1},{1,0},{2,3},{3,2},{4,5},{5,4},{6,7},{7,6},{8,9},{9,8},{10,11... | collective-permute-start | bytes 98312 | tf_op jit(solution)/shard_map/ppermute | solution.py:24
  34.6 4.9 %collective-permute-start.12 = (bf16[128,512]{1,0:T(8,128)(2,1)S(1)}, bf16[128,512]{1,0:T(8,128)(2,1)S(1)}, u32[]{:S(2)}, u32[]{:S(2)}) collective-permute-start(bf16[128,512]{1,0:T(8,128)(2,1)S(1)} %slope.1.refs_0_), channel_id=1, source_target_pairs={{0,3},{1,2},{2,1},{3,0},{4,7},{5,6},{6,5},{7,4},{8,11},{9,10},{10,... | collective-permute-start | bytes 393224 | tf_op jit(solution)/shard_map/ppermute | solution.py:24
  36.3 5.7 %collective-permute-start.11 = (bf16[128,512]{1,0:T(8,128)(2,1)S(1)}, bf16[128,512]{1,0:T(8,128)(2,1)S(1)}, u32[]{:S(2)}, u32[]{:S(2)}) collective-permute-start(bf16[128,512]{1,0:T(8,128)(2,1)S(1)} %slope.1.refs_0_), channel_id=1, source_target_pairs={{0,2},{1,3},{2,0},{3,1},{4,6},{5,7},{6,4},{7,5},{8,10},{9,11},{10,... | collective-permute-start | bytes 393224 | tf_op jit(solution)/shard_map/ppermute | solution.py:24
  37.0 5.4 %collective-permute-start.10 = (bf16[128,512]{1,0:T(8,128)(2,1)S(1)}, bf16[128,512]{1,0:T(8,128)(2,1)S(1)}, u32[]{:S(2)}, u32[]{:S(2)}) collective-permute-start(bf16[128,512]{1,0:T(8,128)(2,1)S(1)} %slope.1.refs_0_), channel_id=1, source_target_pairs={{0,1},{1,0},{2,3},{3,2},{4,5},{5,4},{6,7},{7,6},{8,9},{9,8},{10,11... | collective-permute-start | bytes 393224 | tf_op jit(solution)/shard_map/ppermute | solution.py:24
  42.7 6.2 %collective-permute-start.13 = (bf16[144,128]{1,0:T(8,128)(2,1)S(1)}, bf16[144,128]{1,0:T(8,128)(2,1)S(1)}, u32[]{:S(2)}, u32[]{:S(2)}) collective-permute-start(bf16[144,128]{1,0:T(8,128)(2,1)S(1)} %kept.1.refs_0_), channel_id=1, source_target_pairs={{0,8},{4,12},{8,0},{12,4},{16,24},{20,28},{24,16},{28,20},{1,9},{5... | collective-permute-start | bytes 110600 | tf_op jit(solution)/shard_map/ppermute | solution.py:24
  44.1 4.9 %collective-permute-start.14 = (bf16[144,128]{1,0:T(8,128)(2,1)S(1)}, bf16[144,128]{1,0:T(8,128)(2,1)S(1)}, u32[]{:S(2)}, u32[]{:S(2)}) collective-permute-start(bf16[144,128]{1,0:T(8,128)(2,1)S(1)} %kept.1.refs_0_), channel_id=1, source_target_pairs={{0,24},{4,28},{8,16},{12,20},{16,8},{20,12},{24,0},{28,4},{1,25},{... | collective-permute-start | bytes 110600 | tf_op jit(solution)/shard_map/ppermute | solution.py:24
  46.3 4.3 %collective-permute-start.15 = (bf16[144,128]{1,0:T(8,128)(2,1)S(1)}, bf16[144,128]{1,0:T(8,128)(2,1)S(1)}, u32[]{:S(2)}, u32[]{:S(2)}) collective-permute-start(bf16[144,128]{1,0:T(8,128)(2,1)S(1)} %kept.1.refs_0_), channel_id=1, source_target_pairs={{0,16},{4,20},{8,24},{12,28},{16,0},{20,4},{24,8},{28,12},{1,17},{... | collective-permute-start | bytes 110600 | tf_op jit(solution)/shard_map/ppermute | solution.py:24
  50.6 5.0 %collective-permute-start.16 = (bf16[576,128]{1,0:T(8,128)(2,1)S(1)}, bf16[576,128]{1,0:T(8,128)(2,1)S(1)}, u32[]{:S(2)}, u32[]{:S(2)}) collective-permute-start(bf16[576,128]{1,0:T(8,128)(2,1)S(1)} %join.5.group), channel_id=1, source_target_pairs={{0,4},{4,0},{8,12},{12,8},{16,20},{20,16},{24,28},{28,24},{1,5},{5... | collective-permute-start | bytes 442376 | tf_op jit(solution)/shard_map/ppermute | solution.py:24

commit v12 on v8

--- a/solution.py
+++ b/solution.py
@@ -53,8 +53,8 @@
     )(tokens, *after)
 
 
-def project_kernel(n, *refs):
-    pieces, w, outs, x = refs[:n], refs[n], refs[-n - 1 : -1], refs[-1]
+def project_kernel(n, m, *refs):
+    pieces, w, outs, x = refs[:n], refs[n], refs[-m - 1 : -1], refs[-1]
     start = 0
     for piece in pieces:
         x[start : start + piece.shape[0], :] = piece[...]
@@ -66,20 +66,20 @@
         start += out.shape[0]
 
 
-def project(pieces, types, w, after):
+def project(pieces, outs, w, after):
     n = len(pieces)
     rows, depth = sum(p.shape[0] for p in pieces), pieces[0].shape[1]
     kw = w.shape[1]
     result = pl.pallas_call(
-        functools.partial(project_kernel, n),
-        out_shape=[jax.ShapeDtypeStruct((p.shape[0], kw), t) for p, t in zip(pieces, types)]
+        functools.partial(project_kernel, n, len(outs)),
+        out_shape=[jax.ShapeDtypeStruct((r, kw), t) for r, t in outs]
         + [jax.ShapeDtypeStruct((rows, depth), jnp.bfloat16)],
         in_specs=[VMEM] * (n + 1) + [ANY] * len(after),
         compiler_params=params(14),
         cost_estimate=BRIEF,
         name="project",
     )(*pieces, w, *after)
-    return result[:n], result[n]
+    return result[:-1], result[-1]
 
 
 def slope_kernel(tok_dev, n, spans, *refs):
@@ -341,7 +341,7 @@
     tiles = out.shape[0] // tile
     for t in range(tiles):
         rows = slice(t * tile, (t + 1) * tile)
-        held[rows, :] = (half[rows, :] + place(lines, wide, t, tile)) / n
+        held[rows, :] = (half[rows, :] + place(lines, wide, t, tile)) * (1.0 / n)
         send_out(held, out, sems, t, tile).start()
     for t in range(tiles):
         send_out(held, out, sems, t, tile).wait()
@@ -386,9 +386,14 @@
     far = [d for d in range(1, n_shard) if d & (d - 1) != 0]
 
     me = lax.axis_index("shard")
-    far_out = [lax.dynamic_slice(tokens, (0, (me ^ d) * depth), (tok_dev, depth)) for d in far]
-    far_in = [swap(x, "shard", n_shard, d) for x, d in zip(far_out, far)]
-    near_out, token = [], far_out[0]
+    first = tok_dev // 4
+    far_out, rest = [], tokens
+    for low, high in [(0, first), (first, tok_dev)]:
+        out = [lax.dynamic_slice(rest, (low, (me ^ d) * depth), (high - low, depth)) for d in far]
+        rest, *out = lax.optimization_barrier((rest, *out))
+        far_out.append(out)
+    far_in = [[swap(x, "shard", n_shard, d) for x in xs] for d, xs in zip(far, zip(*far_out))]
+    near_out, token = [], far_out[1][0]
     for low, high in spans:
         *out, token = cut(tokens, depth, [(d, low, high - low) for d in near], [token])
         near_out.append(out)
@@ -399,12 +404,14 @@
     own, _ = cut(tokens, depth, [(0, 0, tok_dev)], [token])
 
     brief, wide = jnp.bfloat16, jnp.float32
-    (mine, *products), x_far = project([own] + far_in, [wide] + [brief] * len(far), w, [])
+    outs = [(tok_dev, wide)] + [(tok_dev, brief)] * len(far)
+    (mine, *products), x_far = project([own] + sum(far_in, []), outs, w, [])
     whole = [swap(p, "shard", n_shard, d) for p, d in zip(products, far)]
     xg_far, xt_far, token = prepare([x_far], slot_row, counts, per_row, [])
     after, shares, x_near = [token], [], []
-    for part in range(len(spans)):
-        products, x = project(near_in[part], [brief] * len(near), w, after)
+    for part, (low, high) in enumerate(spans):
+        outs = [(high - low, brief)] * len(near)
+        products, x = project(near_in[part], outs, w, after)
         shares.append([swap(p, "shard", n_shard, d) for p, d in zip(products, near)])
         x_near.append(x)
         after = products[-1:]

time: 57.6 us -> 62.7 us (1.089)
  waiting for transfers between devices: 15.8 us -> 18.3 us
  starting transfers between devices: 23.4 us -> 25.2 us
  local copies, waits for them, and re-layouts: 4.29 us -> 5.15 us
    ppermute x17 -> x18, waiting for transfers between devices: 15.8 us -> 18.3 us  [swap(): return lax.ppermute(x, axis, [(i, i ^ d) for i in range(n)])]
    ppermute x17 -> x18, starting transfers between devices: 23.4 us -> 25.2 us  [swap(): return lax.ppermute(x, axis, [(i, i ^ d) for i in range(n)])]
    dynamic_slice x1 -> x2, local copies, waits for them, and re-layouts: 1.08 us -> 1.95 us  [on_device(): lax.dynamic_slice(rest, (low, (me ^ d) * depth), (high - low, depth))]
  transfers between devices with their start and end apart: 17 -> 18, of which waited for: 9 -> 5; matrix products, arithmetic and copies ran while one was open for 0% -> 0% of each run, Pallas kernels for 16% -> 15%
where the time goes in v12:
time: 62.7 us; the launch traced here: 62.5 us
  starting transfers between devices  25.2 us (40%)
  waiting for transfers between devices  18.3 us (29%)
  Pallas kernels  12.3 us (20%)
  local copies, waits for them, and re-layouts  5.15 us (8%)
  between operations  1.55 us (2%)
    ppermute x18, starting transfers between devices, swap(): return lax.ppermute(x, axis, [(i, i ^ d) for i in range(n)])  25.2 us
    ppermute x18, waiting for transfers between devices, swap(): return lax.ppermute(x, axis, [(i, i ^ d) for i in range(n)])  18.3 us
    unnamed x14, local copies, waits for them, and re-layouts  3.2 us
    pallas_call x1, Pallas kernels, outer(): pl.pallas_call(functools.partial(outer_kernel, cap, kw // LANES, tile, n)...  2.65 us
    pallas_call x1, Pallas kernels, residue(): pl.pallas_call(functools.partial(residue_kernel, order, tile), out_shape=...  2.37 us
    dynamic_slice x2, local copies, waits for them, and re-layouts, on_device(): lax.dynamic_slice(rest, (low, (me ^ d) * depth), (high - low, depth))  1.95 us
    pallas_call x3, Pallas kernels, project(): pl.pallas_call(functools.partial(project_kernel, n, len(outs)), out_shape...  1.78 us
    pallas_call x2, Pallas kernels, prepare(): pl.pallas_call(functools.partial(prepare_kernel, per_row, len(xs)), out_s...  1.55 us
  transfers between devices with their start and end apart: 18, of which 5 were waited for; matrix products, arithmetic and copies ran while one was open for 0% of the time, Pallas kernels for 15%

profile of v12, /device:TPU:1, one launch (start us, length us, event | category | flops | bytes accessed | tf_op | source)
XLA Modules:
  0.0 62.5 jit_solution(13120719193144604996)
XLA Ops:
  0.6 0.9 %dynamic-slice_bitcast_fusion = bf16[32,2048]{1,0:T(8,128)(2,1)S(1)} fusion(bf16[1,128,8192]{2,1,0:T(8,128)(2,1)} %param.6, s32[]{:T(128)S(6)} %select_n.4), kind=kLoop, calls=%fused_computation | loop fusion | bytes 262148 | tf_op jit(solution)/shard_map/dynamic_slice | solution.py:392
  1.6 1.0 %constant_dynamic-slice_fusion.refs_0_ = bf16[96,2048]{1,0:T(8,128)(2,1)S(1)} fusion(bf16[128,8192]{1,0:T(8,128)(2,1)} %bitcast.8, s32[]{:T(128)S(6)} %select_n.4), kind=kLoop, calls=%fused_computation.1 | loop fusion | bytes 786436 | tf_op jit(solution)/shard_map/dynamic_slice | solution.py:392
  2.6 3.1 %collective-permute-start.1 = (bf16[96,2048]{1,0:T(8,128)(2,1)S(1)}, bf16[96,2048]{1,0:T(8,128)(2,1)S(1)}, u32[]{:S(2)}, u32[]{:S(2)}) collective-permute-start(bf16[96,2048]{1,0:T(8,128)(2,1)S(1)} %constant_dynamic-slice_fusion.refs_0_), channel_id=1, source_target_pairs={{0,3},{1,2},{2,1},{3,0},{4,7},{5,6},{6,5},{7,4},{8,11},{9,10},{10,... | collective-permute-start | bytes 1179656 | tf_op jit(solution)/shard_map/ppermute | solution.py:24
  5.7 1.6 %copy-done = bf16[1,128,8192]{2,1,0:T(8,128)(2,1)S(1)} copy-done((bf16[1,128,8192]{2,1,0:T(8,128)(2,1)S(1)}, bf16[1,128,8192]{2,1,0:T(8,128)(2,1)}, u32[]{:S(2)}) %copy-start) | copy-done | bytes 2097176
  7.7 2.3 %collective-permute-start = (bf16[32,2048]{1,0:T(8,128)(2,1)S(1)}, bf16[32,2048]{1,0:T(8,128)(2,1)S(1)}, u32[]{:S(2)}, u32[]{:S(2)}) collective-permute-start(bf16[32,2048]{1,0:T(8,128)(2,1)S(1)} %dynamic-slice_bitcast_fusion), channel_id=1, source_target_pairs={{0,3},{1,2},{2,1},{3,0},{4,7},{5,6},{6,5},{7,4},{8,11},{9,10},{10,... | collective-permute-start | bytes 393224 | tf_op jit(solution)/shard_map/ppermute | solution.py:24
  10.7 1.6 %copy-done.3 = bf16[1,2048,512]{2,1,0:T(8,128)(2,1)S(1)} copy-done((bf16[1,2048,512]{2,1,0:T(8,128)(2,1)S(1)}, bf16[1,2048,512]{2,1,0:T(8,128)(2,1)}, u32[]{:S(2)}) %copy-start.3) | copy-done | bytes 2097176
  12.3 1.1 %early.1 = (f32[128,128]{1,0:T(8,128)S(1)}, bf16[2048,512]{1,0:T(8,128)(2,1)S(1)}, f32[8,128]{1,0:T(8,128)S(1)}) custom-call(s32[1,128]{1,0:T(1,128)S(1)} %bitcast.18, s32[1,1]{1,0:T(1,128)S(6)} %copy.8.count.refs_2_.refs_3_, bf16[2048,512]{1,0:T(8,128)(2,1)S(1)} %bitcast.15, f32[8,128]{1,0:T(8,128)S(1)} %get-tuple-element.34.after), custom_call_target="tpu_custom_call" | custom-call | flops 1000 | bytes 1000 | tf_op jit(solution)/shard_map/early/pallas_call | solution.py:145
  13.9 11.9 %collective-permute-done.refs_1_ = bf16[32,2048]{1,0:T(8,128)(2,1)S(1)} collective-permute-done((bf16[32,2048]{1,0:T(8,128)(2,1)S(1)}, bf16[32,2048]{1,0:T(8,128)(2,1)S(1)}, u32[]{:S(2)}, u32[]{:S(2)}) %collective-permute-start) | collective-permute-done | bytes 131104 | tf_op jit(solution)/shard_map/ppermute | solution.py:24
  25.8 1.1 %collective-permute-start.7 = (bf16[32,2048]{1,0:T(8,128)(2,1)S(1)}, bf16[32,2048]{1,0:T(8,128)(2,1)S(1)}, u32[]{:S(2)}, u32[]{:S(2)}) collective-permute-start(bf16[32,2048]{1,0:T(8,128)(2,1)S(1)} %get-tuple-element.47), channel_id=1, source_target_pairs={{0,2},{1,3},{2,0},{3,1},{4,6},{5,7},{6,4},{7,5},{8,10},{9,11},{10,... | collective-permute-start | bytes 393224 | tf_op jit(solution)/shard_map/ppermute | solution.py:24
  26.9 0.6 %cut.5 = (bf16[128,2048]{1,0:T(8,128)(2,1)S(1)}, f32[8,128]{1,0:T(8,128)}) custom-call(bf16[128,8192]{1,0:T(8,128)(2,1)S(1)} %bitcast.11, f32[8,128]{1,0:T(8,128)S(1)} %get-tuple-element.36.refs_0_), custom_call_target="tpu_custom_call" | custom-call | flops 1000 | bytes 1000 | tf_op jit(solution)/shard_map/cut/pallas_call | solution.py:43
  27.6 0.7 %project.3 = (f32[128,512]{1,0:T(8,128)S(1)}, bf16[128,512]{1,0:T(8,128)(2,1)S(1)}, bf16[256,2048]{1,0:T(8,128)(2,1)S(1)}) custom-call(bf16[128,2048]{1,0:T(8,128)(2,1)S(1)} %get-tuple-element.37.refs_0_, bf16[32,2048]{1,0:T(8,128)(2,1)S(1)} %collective-permute-done.refs_1_, bf16[96,2048]{1,0:T(8,128)(2,1)S(1)} %collective-permute-done.1.refs_2_, ...), custom_call_target="tpu_custom_call" | custom-call | flops 1000 | bytes 1000 | tf_op jit(solution)/shard_map/project/pallas_call | solution.py:73
  28.3 1.2 %collective-permute-start.2 = (bf16[128,512]{1,0:T(8,128)(2,1)S(1)}, bf16[128,512]{1,0:T(8,128)(2,1)S(1)}, u32[]{:S(2)}, u32[]{:S(2)}) collective-permute-start(bf16[128,512]{1,0:T(8,128)(2,1)S(1)} %get-tuple-element.40), channel_id=1, source_target_pairs={{0,3},{1,2},{2,1},{3,0},{4,7},{5,6},{6,5},{7,4},{8,11},{9,10},{10,... | collective-permute-start | bytes 393224 | tf_op jit(solution)/shard_map/ppermute | solution.py:24
  29.5 0.6 prepare.2
  30.1 0.6 project.4
  30.7 0.4 collective-permute-start.5
  31.2 1.1 %collective-permute-start.9 = (bf16[96,512]{1,0:T(8,128)(2,1)S(1)}, bf16[96,512]{1,0:T(8,128)(2,1)S(1)}, u32[]{:S(2)}, u32[]{:S(2)}) collective-permute-start(bf16[96,512]{1,0:T(8,128)(2,1)S(1)} %get-tuple-element.48.refs_3_), channel_id=1, source_target_pairs={{0,2},{1,3},{2,0},{3,1},{4,6},{5,7},{6,4},{7,5},{8,10},{9,11},{10,... | collective-permute-start | bytes 294920 | tf_op jit(solution)/shard_map/ppermute | solution.py:24
  32.3 0.5 project.5
  32.8 0.4 collective-permute-start.10
  33.2 1.1 %collective-permute-start.8 = (bf16[32,512]{1,0:T(8,128)(2,1)S(1)}, bf16[32,512]{1,0:T(8,128)(2,1)S(1)}, u32[]{:S(2)}, u32[]{:S(2)}) collective-permute-start(bf16[32,512]{1,0:T(8,128)(2,1)S(1)} %get-tuple-element.49.refs_4_), channel_id=1, source_target_pairs={{0,1},{1,0},{2,3},{3,2},{4,5},{5,4},{6,7},{7,6},{8,9},{9,8},{10,11... | collective-permute-start | bytes 98312 | tf_op jit(solution)/shard_map/ppermute | solution.py:24
  34.3 0.9 %prepare.3 = (bf16[128,256]{1,0:T(8,128)(2,1)S(1)}, bf16[2048,256]{1,0:T(8,128)(2,1)S(1)}, f32[8,128]{1,0:T(8,128)S(1)}) custom-call(bf16[192,2048]{1,0:T(8,128)(2,1)S(1)} %get-tuple-element.51.refs_0_, bf16[64,2048]{1,0:T(8,128)(2,1)S(1)} %get-tuple-element.52.refs_1_, s32[1,128]{1,0:T(1,128)S(1)} %bitcast.20, s32[1,1]{1,0:T(1,128)S(6)} %copy.8.count.refs_2_.refs_3_, ...), custom_call_target="tpu_custom_call" | custom-call | flops 1000 | bytes 1000 | tf_op jit(solution)/shard_map/prepare/pallas_call | solution.py:181
  35.3 2.0 %collective-permute-done.10.refs_6_ = bf16[32,512]{1,0:T(8,128)(2,1)S(1)} collective-permute-done((bf16[32,512]{1,0:T(8,128)(2,1)S(1)}, bf16[32,512]{1,0:T(8,128)(2,1)S(1)}, u32[]{:S(2)}, u32[]{:S(2)}) %collective-permute-start.10) | collective-permute-done | bytes 32800 | tf_op jit(solution)/shard_map/ppermute | solution.py:24
  37.4 1.6 %collective-permute-start.13 = (bf16[128,512]{1,0:T(8,128)(2,1)S(1)}, bf16[128,512]{1,0:T(8,128)(2,1)S(1)}, u32[]{:S(2)}, u32[]{:S(2)}) collective-permute-start(bf16[128,512]{1,0:T(8,128)(2,1)S(1)} %slope.1.refs_0_), channel_id=1, source_target_pairs={{0,3},{1,2},{2,1},{3,0},{4,7},{5,6},{6,5},{7,4},{8,11},{9,10},{10,... | collective-permute-start | bytes 393224 | tf_op jit(solution)/shard_map/ppermute | solution.py:24
  38.9 0.8 %collective-permute-start.12 = (bf16[128,512]{1,0:T(8,128)(2,1)S(1)}, bf16[128,512]{1,0:T(8,128)(2,1)S(1)}, u32[]{:S(2)}, u32[]{:S(2)}) collective-permute-start(bf16[128,512]{1,0:T(8,128)(2,1)S(1)} %slope.1.refs_0_), channel_id=1, source_target_pairs={{0,2},{1,3},{2,0},{3,1},{4,6},{5,7},{6,4},{7,5},{8,10},{9,11},{10,... | collective-permute-start | bytes 393224 | tf_op jit(solution)/shard_map/ppermute | solution.py:24
  40.1 2.5 %collective-permute-done.13.refs_1_ = bf16[128,512]{1,0:T(8,128)(2,1)S(1)} collective-permute-done((bf16[128,512]{1,0:T(8,128)(2,1)S(1)}, bf16[128,512]{1,0:T(8,128)(2,1)S(1)}, u32[]{:S(2)}, u32[]{:S(2)}) %collective-permute-start.13) | collective-permute-done | bytes 131104 | tf_op jit(solution)/shard_map/ppermute | solution.py:24
  42.8 0.9 %collective-permute-done.12.refs_1_.refs_3_ = bf16[128,512]{1,0:T(8,128)(2,1)S(1)} collective-permute-done((bf16[128,512]{1,0:T(8,128)(2,1)S(1)}, bf16[128,512]{1,0:T(8,128)(2,1)S(1)}, u32[]{:S(2)}, u32[]{:S(2)}) %collective-permute-start.12) | collective-permute-done | bytes 131104 | tf_op jit(solution)/shard_map/ppermute | solution.py:24
  44.0 3.3 %collective-permute-start.14 = (bf16[144,128]{1,0:T(8,128)(2,1)S(1)}, bf16[144,128]{1,0:T(8,128)(2,1)S(1)}, u32[]{:S(2)}, u32[]{:S(2)}) collective-permute-start(bf16[144,128]{1,0:T(8,128)(2,1)S(1)} %kept.1.refs_0_), channel_id=1, source_target_pairs={{0,24},{4,28},{8,16},{12,20},{16,8},{20,12},{24,0},{28,4},{1,25},{... | collective-permute-start | bytes 110600 | tf_op jit(solution)/shard_map/ppermute | solution.py:24
  47.3 0.4 collective-permute-start.16
  47.7 2.4 %residue.1 = (bf16[2048,512]{1,0:T(8,128)(2,1)}, f32[8,128]{1,0:T(8,128)S(1)}) custom-call(bf16[128,512]{1,0:T(8,128)(2,1)S(1)} %slope.1.refs_0_, bf16[128,512]{1,0:T(8,128)(2,1)S(1)} %collective-permute-done.13.refs_1_, bf16[128,512]{1,0:T(8,128)(2,1)S(1)} %collective-permute-done.11.refs_0_.refs_2_, ...), custom_call_target="tpu_custom_call" | custom-call | flops 1000 | bytes 1000 | tf_op jit(solution)/shard_map/residue/pallas_call | solution.py:274
  50.1 0.9 %collective-permute-done.15.refs_1_ = bf16[144,128]{1,0:T(8,128)(2,1)S(1)} collective-permute-done((bf16[144,128]{1,0:T(8,128)(2,1)S(1)}, bf16[144,128]{1,0:T(8,128)(2,1)S(1)}, u32[]{:S(2)}, u32[]{:S(2)}) %collective-permute-start.15) | collective-permute-done | bytes 36896 | tf_op jit(solution)/shard_map/ppermute | solution.py:24
  51.1 7.3 %collective-permute-start.17 = (bf16[576,128]{1,0:T(8,128)(2,1)S(1)}, bf16[576,128]{1,0:T(8,128)(2,1)S(1)}, u32[]{:S(2)}, u32[]{:S(2)}) collective-permute-start(bf16[576,128]{1,0:T(8,128)(2,1)S(1)} %join.5.group), channel_id=1, source_target_pairs={{0,4},{4,0},{8,12},{12,8},{16,20},{20,16},{24,28},{28,24},{1,5},{5... | collective-permute-start | bytes 442376 | tf_op jit(solution)/shard_map/ppermute | solution.py:24
  58.4 1.4 %half.1 = f32[2048,512]{1,0:T(8,128)S(1)} custom-call(bf16[576,128]{1,0:T(8,128)(2,1)S(1)} %join.5.group), custom_call_target="tpu_custom_call" | custom-call | flops 1000 | bytes 1000 | tf_op jit(solution)/shard_map/half/pallas_call | solution.py:356
  59.8 2.7 %outer.1 = f32[2048,512]{1,0:T(8,128)} custom-call(bf16[576,128]{1,0:T(8,128)(2,1)S(1)} %collective-permute-done.17.group, f32[2048,512]{1,0:T(8,128)S(1)} %half.1), custom_call_target="tpu_custom_call" | custom-call | flops 1000 | bytes 1000 | tf_op jit(solution)/shard_map/outer/pallas_call | solution.py:364
  (38 shorter events, 1.9 us)
Async XLA Ops:
  0.6 10.1 %copy-start.6 = (s32[1,1,128]{2,1,0:T(1,128)S(1)}, s32[1,1,128]{2,1,0:T(1,128)}, u32[]{:S(2)}) copy-start(s32[1,1,128]{2,1,0:T(1,128)} %param.11) | copy-start | bytes 1540
  2.6 24.9 %collective-permute-start.1 = (bf16[96,2048]{1,0:T(8,128)(2,1)S(1)}, bf16[96,2048]{1,0:T(8,128)(2,1)S(1)}, u32[]{:S(2)}, u32[]{:S(2)}) collective-permute-start(bf16[96,2048]{1,0:T(8,128)(2,1)S(1)} %constant_dynamic-slice_fusion.refs_0_), channel_id=1, source_target_pairs={{0,3},{1,2},{2,1},{3,0},{4,7},{5,6},{6,5},{7,4},{8,11},{9,10},{10,... | collective-permute-start | bytes 1179656 | tf_op jit(solution)/shard_map/ppermute | solution.py:24
  5.7 1.6 %copy-start = (bf16[1,128,8192]{2,1,0:T(8,128)(2,1)S(1)}, bf16[1,128,8192]{2,1,0:T(8,128)(2,1)}, u32[]{:S(2)}) copy-start(bf16[1,128,8192]{2,1,0:T(8,128)(2,1)} %param.6) | copy-start | bytes 6291460
  7.3 6.2 %copy-start.1 = (bf16[1,128,8192]{2,1,0:T(8,128)(2,1)S(1)}, bf16[1,128,8192]{2,1,0:T(8,128)(2,1)}, u32[]{:S(2)}) copy-start(bf16[1,128,8192]{2,1,0:T(8,128)(2,1)} %param.6) | copy-start | bytes 6291460
  7.3 22.8 %collective-permute-start.3 = (bf16[96,2048]{1,0:T(8,128)(2,1)S(1)}, bf16[96,2048]{1,0:T(8,128)(2,1)S(1)}, u32[]{:S(2)}, u32[]{:S(2)}) collective-permute-start(bf16[96,2048]{1,0:T(8,128)(2,1)S(1)} %get-tuple-element.41), channel_id=1, source_target_pairs={{0,1},{1,0},{2,3},{3,2},{4,5},{5,4},{6,7},{7,6},{8,9},{9,8},{10,11... | collective-permute-start | bytes 1179656 | tf_op jit(solution)/shard_map/ppermute | solution.py:24
  7.7 22.5 %collective-permute-start.4 = (bf16[96,2048]{1,0:T(8,128)(2,1)S(1)}, bf16[96,2048]{1,0:T(8,128)(2,1)S(1)}, u32[]{:S(2)}, u32[]{:S(2)}) collective-permute-start(bf16[96,2048]{1,0:T(8,128)(2,1)S(1)} %get-tuple-element.42), channel_id=1, source_target_pairs={{0,2},{1,3},{2,0},{3,1},{4,6},{5,7},{6,4},{7,5},{8,10},{9,11},{10,... | collective-permute-start | bytes 1179656 | tf_op jit(solution)/shard_map/ppermute | solution.py:24
  7.7 18.1 %collective-permute-start = (bf16[32,2048]{1,0:T(8,128)(2,1)S(1)}, bf16[32,2048]{1,0:T(8,128)(2,1)S(1)}, u32[]{:S(2)}, u32[]{:S(2)}) collective-permute-start(bf16[32,2048]{1,0:T(8,128)(2,1)S(1)} %dynamic-slice_bitcast_fusion), channel_id=1, source_target_pairs={{0,3},{1,2},{2,1},{3,0},{4,7},{5,6},{6,5},{7,4},{8,11},{9,10},{10,... | collective-permute-start | bytes 393224 | tf_op jit(solution)/shard_map/ppermute | solution.py:24
  10.7 1.6 %copy-start.3 = (bf16[1,2048,512]{2,1,0:T(8,128)(2,1)S(1)}, bf16[1,2048,512]{2,1,0:T(8,128)(2,1)}, u32[]{:S(2)}) copy-start(bf16[1,2048,512]{2,1,0:T(8,128)(2,1)} %param.9) | copy-start | bytes 6291460
  13.4 14.1 %copy-start.2 = (bf16[1,2048,512]{2,1,0:T(8,128)(2,1)S(1)}, bf16[1,2048,512]{2,1,0:T(8,128)(2,1)}, u32[]{:S(2)}) copy-start(bf16[1,2048,512]{2,1,0:T(8,128)(2,1)} %param.8) | copy-start | bytes 6291460
  13.6 18.7 %collective-permute-start.6 = (bf16[32,2048]{1,0:T(8,128)(2,1)S(1)}, bf16[32,2048]{1,0:T(8,128)(2,1)S(1)}, u32[]{:S(2)}, u32[]{:S(2)}) collective-permute-start(bf16[32,2048]{1,0:T(8,128)(2,1)S(1)} %get-tuple-element.46), channel_id=1, source_target_pairs={{0,1},{1,0},{2,3},{3,2},{4,5},{5,4},{6,7},{7,6},{8,9},{9,8},{10,11... | collective-permute-start | bytes 393224 | tf_op jit(solution)/shard_map/ppermute | solution.py:24
  25.8 6.5 %collective-permute-start.7 = (bf16[32,2048]{1,0:T(8,128)(2,1)S(1)}, bf16[32,2048]{1,0:T(8,128)(2,1)S(1)}, u32[]{:S(2)}, u32[]{:S(2)}) collective-permute-start(bf16[32,2048]{1,0:T(8,128)(2,1)S(1)} %get-tuple-element.47), channel_id=1, source_target_pairs={{0,2},{1,3},{2,0},{3,1},{4,6},{5,7},{6,4},{7,5},{8,10},{9,11},{10,... | collective-permute-start | bytes 393224 | tf_op jit(solution)/shard_map/ppermute | solution.py:24
  28.3 9.0 %collective-permute-start.2 = (bf16[128,512]{1,0:T(8,128)(2,1)S(1)}, bf16[128,512]{1,0:T(8,128)(2,1)S(1)}, u32[]{:S(2)}, u32[]{:S(2)}) collective-permute-start(bf16[128,512]{1,0:T(8,128)(2,1)S(1)} %get-tuple-element.40), channel_id=1, source_target_pairs={{0,3},{1,2},{2,1},{3,0},{4,7},{5,6},{6,5},{7,4},{8,11},{9,10},{10,... | collective-permute-start | bytes 393224 | tf_op jit(solution)/shard_map/ppermute | solution.py:24
  30.7 6.5 %copy-start.5 = (bf16[1,128,512]{2,1,0:T(8,128)(2,1)S(1)}, bf16[1,128,512]{2,1,0:T(8,128)(2,1)}, u32[]{:S(2)}) copy-start(bf16[1,128,512]{2,1,0:T(8,128)(2,1)} %param.7) | copy-start | bytes 393220
  30.7 6.5 %collective-permute-start.5 = (bf16[96,512]{1,0:T(8,128)(2,1)S(1)}, bf16[96,512]{1,0:T(8,128)(2,1)S(1)}, u32[]{:S(2)}, u32[]{:S(2)}) collective-permute-start(bf16[96,512]{1,0:T(8,128)(2,1)S(1)} %get-tuple-element.45), channel_id=1, source_target_pairs={{0,1},{1,0},{2,3},{3,2},{4,5},{5,4},{6,7},{7,6},{8,9},{9,8},{10,11... | collective-permute-start | bytes 294920 | tf_op jit(solution)/shard_map/ppermute | solution.py:24
  31.2 6.1 %collective-permute-start.9 = (bf16[96,512]{1,0:T(8,128)(2,1)S(1)}, bf16[96,512]{1,0:T(8,128)(2,1)S(1)}, u32[]{:S(2)}, u32[]{:S(2)}) collective-permute-start(bf16[96,512]{1,0:T(8,128)(2,1)S(1)} %get-tuple-element.48.refs_3_), channel_id=1, source_target_pairs={{0,2},{1,3},{2,0},{3,1},{4,6},{5,7},{6,4},{7,5},{8,10},{9,11},{10,... | collective-permute-start | bytes 294920 | tf_op jit(solution)/shard_map/ppermute | solution.py:24
  32.8 14.9 %copy-start.4 = (bf16[1,2048,512]{2,1,0:T(8,128)(2,1)S(1)}, bf16[1,2048,512]{2,1,0:T(8,128)(2,1)}, u32[]{:S(2)}) copy-start(bf16[1,2048,512]{2,1,0:T(8,128)(2,1)} %param.9) | copy-start | bytes 6291460
  32.8 4.4 %collective-permute-start.10 = (bf16[32,512]{1,0:T(8,128)(2,1)S(1)}, bf16[32,512]{1,0:T(8,128)(2,1)S(1)}, u32[]{:S(2)}, u32[]{:S(2)}) collective-permute-start(bf16[32,512]{1,0:T(8,128)(2,1)S(1)} %get-tuple-element.50), channel_id=1, source_target_pairs={{0,2},{1,3},{2,0},{3,1},{4,6},{5,7},{6,4},{7,5},{8,10},{9,11},{10,... | collective-permute-start | bytes 98312 | tf_op jit(solution)/shard_map/ppermute | solution.py:24
  33.2 4.0 %collective-permute-start.8 = (bf16[32,512]{1,0:T(8,128)(2,1)S(1)}, bf16[32,512]{1,0:T(8,128)(2,1)S(1)}, u32[]{:S(2)}, u32[]{:S(2)}) collective-permute-start(bf16[32,512]{1,0:T(8,128)(2,1)S(1)} %get-tuple-element.49.refs_4_), channel_id=1, source_target_pairs={{0,1},{1,0},{2,3},{3,2},{4,5},{5,4},{6,7},{7,6},{8,9},{9,8},{10,11... | collective-permute-start | bytes 98312 | tf_op jit(solution)/shard_map/ppermute | solution.py:24
  37.4 5.2 %collective-permute-start.13 = (bf16[128,512]{1,0:T(8,128)(2,1)S(1)}, bf16[128,512]{1,0:T(8,128)(2,1)S(1)}, u32[]{:S(2)}, u32[]{:S(2)}) collective-permute-start(bf16[128,512]{1,0:T(8,128)(2,1)S(1)} %slope.1.refs_0_), channel_id=1, source_target_pairs={{0,3},{1,2},{2,1},{3,0},{4,7},{5,6},{6,5},{7,4},{8,11},{9,10},{10,... | collective-permute-start | bytes 393224 | tf_op jit(solution)/shard_map/ppermute | solution.py:24
  38.9 4.8 %collective-permute-start.12 = (bf16[128,512]{1,0:T(8,128)(2,1)S(1)}, bf16[128,512]{1,0:T(8,128)(2,1)S(1)}, u32[]{:S(2)}, u32[]{:S(2)}) collective-permute-start(bf16[128,512]{1,0:T(8,128)(2,1)S(1)} %slope.1.refs_0_), channel_id=1, source_target_pairs={{0,2},{1,3},{2,0},{3,1},{4,6},{5,7},{6,4},{7,5},{8,10},{9,11},{10,... | collective-permute-start | bytes 393224 | tf_op jit(solution)/shard_map/ppermute | solution.py:24
  39.7 4.0 %collective-permute-start.11 = (bf16[128,512]{1,0:T(8,128)(2,1)S(1)}, bf16[128,512]{1,0:T(8,128)(2,1)S(1)}, u32[]{:S(2)}, u32[]{:S(2)}) collective-permute-start(bf16[128,512]{1,0:T(8,128)(2,1)S(1)} %slope.1.refs_0_), channel_id=1, source_target_pairs={{0,1},{1,0},{2,3},{3,2},{4,5},{5,4},{6,7},{7,6},{8,9},{9,8},{10,11... | collective-permute-start | bytes 393224 | tf_op jit(solution)/shard_map/ppermute | solution.py:24
  44.0 6.1 %collective-permute-start.14 = (bf16[144,128]{1,0:T(8,128)(2,1)S(1)}, bf16[144,128]{1,0:T(8,128)(2,1)S(1)}, u32[]{:S(2)}, u32[]{:S(2)}) collective-permute-start(bf16[144,128]{1,0:T(8,128)(2,1)S(1)} %kept.1.refs_0_), channel_id=1, source_target_pairs={{0,24},{4,28},{8,16},{12,20},{16,8},{20,12},{24,0},{28,4},{1,25},{... | collective-permute-start | bytes 110600 | tf_op jit(solution)/shard_map/ppermute | solution.py:24
  47.3 3.7 %collective-permute-start.15 = (bf16[144,128]{1,0:T(8,128)(2,1)S(1)}, bf16[144,128]{1,0:T(8,128)(2,1)S(1)}, u32[]{:S(2)}, u32[]{:S(2)}) collective-permute-start(bf16[144,128]{1,0:T(8,128)(2,1)S(1)} %kept.1.refs_0_), channel_id=1, source_target_pairs={{0,16},{4,20},{8,24},{12,28},{16,0},{20,4},{24,8},{28,12},{1,17},{... | collective-permute-start | bytes 110600 | tf_op jit(solution)/shard_map/ppermute | solution.py:24
  47.3 3.7 %collective-permute-start.16 = (bf16[144,128]{1,0:T(8,128)(2,1)S(1)}, bf16[144,128]{1,0:T(8,128)(2,1)S(1)}, u32[]{:S(2)}, u32[]{:S(2)}) collective-permute-start(bf16[144,128]{1,0:T(8,128)(2,1)S(1)} %kept.1.refs_0_), channel_id=1, source_target_pairs={{0,8},{4,12},{8,0},{12,4},{16,24},{20,28},{24,16},{28,20},{1,9},{5... | collective-permute-start | bytes 110600 | tf_op jit(solution)/shard_map/ppermute | solution.py:24
  51.1 8.8 %collective-permute-start.17 = (bf16[576,128]{1,0:T(8,128)(2,1)S(1)}, bf16[576,128]{1,0:T(8,128)(2,1)S(1)}, u32[]{:S(2)}, u32[]{:S(2)}) collective-permute-start(bf16[576,128]{1,0:T(8,128)(2,1)S(1)} %join.5.group), channel_id=1, source_target_pairs={{0,4},{4,0},{8,12},{12,8},{16,20},{20,16},{24,28},{28,24},{1,5},{5... | collective-permute-start | bytes 442376 | tf_op jit(solution)/shard_map/ppermute | solution.py:24

commit v13 on v8

--- a/solution.py
+++ b/solution.py
@@ -341,7 +341,7 @@
     tiles = out.shape[0] // tile
     for t in range(tiles):
         rows = slice(t * tile, (t + 1) * tile)
-        held[rows, :] = (half[rows, :] + place(lines, wide, t, tile)) / n
+        held[rows, :] = (half[rows, :] + place(lines, wide, t, tile)) * (1.0 / n)
         send_out(held, out, sems, t, tile).start()
     for t in range(tiles):
         send_out(held, out, sems, t, tile).wait()
@@ -350,7 +350,7 @@
 def outer(groups, cap, depth, kw):
     slots = groups[0].shape[0] // (cap + 16) * cap
     n = 2 * slots // cap
-    tile = min(depth, 512)
+    tile = min(depth, 256)
     shape = jax.ShapeDtypeStruct((depth, kw), jnp.float32)
     scratch = [pltpu.VMEM((slots, kw), jnp.bfloat16), pltpu.VMEM((8, slots), jnp.int32)]
     half = pl.pallas_call(
@@ -418,7 +418,8 @@
     order_near = [(k, low, high) for low, high in spans for k in range(len(near))]
     wide = gather(slopes[:n_far], order_far, xg_far)
     message = kept(slopes[n_far:], order_near, wide, xg_near, fbk, slot_row)
-    same_core = [swap(message, "rep", n_rep, d) for d in range(n_rep - 2, 0, -2)]
+    chips = [4, *range(n_rep - 2, 4, -2), 2] if n_rep > 4 else list(range(2, n_rep, 2))
+    same_core = [swap(message, "rep", n_rep, d) for d in chips]
     order = order_far + [(n_far + k, low, high) for k, low, high in order_near]
     new_feedback, token = residue(slopes, order, [xt_far, xt_near], fb, keep)
     joined, after = message, [token]

time: 57.6 us -> 57.4 us (level)
  no operation moved by 1% of the time
where the time goes in v13:
time: 57.4 us; the launch traced here: 57.2 us
  starting transfers between devices  23.6 us (41%)
  waiting for transfers between devices  15.5 us (27%)
  Pallas kernels  12.2 us (21%)
  local copies, waits for them, and re-layouts  4.29 us (7%)
  between operations  1.69 us (3%)
    ppermute x17, starting transfers between devices, swap(): return lax.ppermute(x, axis, [(i, i ^ d) for i in range(n)])  23.6 us
    ppermute x17, waiting for transfers between devices, swap(): return lax.ppermute(x, axis, [(i, i ^ d) for i in range(n)])  15.5 us
    unnamed x14, local copies, waits for them, and re-layouts  3.2 us
    pallas_call x1, Pallas kernels, outer(): pl.pallas_call(functools.partial(outer_kernel, cap, kw // LANES, tile, n)...  2.54 us
    pallas_call x1, Pallas kernels, residue(): pl.pallas_call(functools.partial(residue_kernel, order, tile), out_shape=...  2.4 us
    pallas_call x3, Pallas kernels, project(): pl.pallas_call(functools.partial(project_kernel, n), out_shape=[jax.Shape...  1.76 us
    pallas_call x2, Pallas kernels, prepare(): pl.pallas_call(functools.partial(prepare_kernel, per_row, len(xs)), out_s...  1.55 us
    pallas_call x1, Pallas kernels, outer(): pl.pallas_call(functools.partial(half_kernel, cap, kw // LANES, tile), ou...  1.41 us
  transfers between devices with their start and end apart: 17, of which 9 were waited for; matrix products, arithmetic and copies ran while one was open for 0% of the time, Pallas kernels for 16%

profile of v13, /device:TPU:1, one launch (start us, length us, event | category | flops | bytes accessed | tf_op | source)
XLA Modules:
  0.0 57.2 jit_solution(15767938084208597349)
XLA Ops:
  0.6 1.1 %dynamic-slice_bitcast_fusion.refs_0_ = bf16[128,2048]{1,0:T(8,128)(2,1)S(1)} fusion(bf16[1,128,8192]{2,1,0:T(8,128)(2,1)} %param.6, s32[]{:T(128)S(6)} %select_n.3), kind=kLoop, calls=%fused_computation | loop fusion | bytes 1048580 | tf_op jit(solution)/shard_map/dynamic_slice | solution.py:389
  1.7 3.1 %collective-permute-start = (bf16[128,2048]{1,0:T(8,128)(2,1)S(1)}, bf16[128,2048]{1,0:T(8,128)(2,1)S(1)}, u32[]{:S(2)}, u32[]{:S(2)}) collective-permute-start(bf16[128,2048]{1,0:T(8,128)(2,1)S(1)} %dynamic-slice_bitcast_fusion.refs_0_), channel_id=1, source_target_pairs={{0,3},{1,2},{2,1},{3,0},{4,7},{5,6},{6,5},{7,4},{8,11},{9,10},{10,... | collective-permute-start | bytes 1572872 | tf_op jit(solution)/shard_map/ppermute | solution.py:24
  4.8 1.6 %copy-done = bf16[1,128,8192]{2,1,0:T(8,128)(2,1)S(1)} copy-done((bf16[1,128,8192]{2,1,0:T(8,128)(2,1)S(1)}, bf16[1,128,8192]{2,1,0:T(8,128)(2,1)}, u32[]{:S(2)}) %copy-start) | copy-done | bytes 2097176
  7.7 1.6 %copy-done.3 = bf16[1,2048,512]{2,1,0:T(8,128)(2,1)S(1)} copy-done((bf16[1,2048,512]{2,1,0:T(8,128)(2,1)S(1)}, bf16[1,2048,512]{2,1,0:T(8,128)(2,1)}, u32[]{:S(2)}) %copy-start.3) | copy-done | bytes 2097176
  9.3 1.1 %early.1 = (f32[128,128]{1,0:T(8,128)S(1)}, bf16[2048,512]{1,0:T(8,128)(2,1)S(1)}, f32[8,128]{1,0:T(8,128)S(1)}) custom-call(s32[1,128]{1,0:T(1,128)S(1)} %bitcast.17, s32[1,1]{1,0:T(1,128)S(6)} %copy.8.count.refs_2_.refs_3_, bf16[2048,512]{1,0:T(8,128)(2,1)S(1)} %bitcast.14, f32[8,128]{1,0:T(8,128)S(1)} %get-tuple-element.29.after), custom_call_target="tpu_custom_call" | custom-call | flops 1000 | bytes 1000 | tf_op jit(solution)/shard_map/early/pallas_call | solution.py:145
  10.5 1.3 %collective-permute-start.5 = (bf16[32,2048]{1,0:T(8,128)(2,1)S(1)}, bf16[32,2048]{1,0:T(8,128)(2,1)S(1)}, u32[]{:S(2)}, u32[]{:S(2)}) collective-permute-start(bf16[32,2048]{1,0:T(8,128)(2,1)S(1)} %get-tuple-element.40), channel_id=1, source_target_pairs={{0,1},{1,0},{2,3},{3,2},{4,5},{5,4},{6,7},{7,6},{8,9},{9,8},{10,11... | collective-permute-start | bytes 393224 | tf_op jit(solution)/shard_map/ppermute | solution.py:24
  11.8 1.2 %collective-permute-start.6 = (bf16[32,2048]{1,0:T(8,128)(2,1)S(1)}, bf16[32,2048]{1,0:T(8,128)(2,1)S(1)}, u32[]{:S(2)}, u32[]{:S(2)}) collective-permute-start(bf16[32,2048]{1,0:T(8,128)(2,1)S(1)} %get-tuple-element.41), channel_id=1, source_target_pairs={{0,2},{1,3},{2,0},{3,1},{4,6},{5,7},{6,4},{7,5},{8,10},{9,11},{10,... | collective-permute-start | bytes 393224 | tf_op jit(solution)/shard_map/ppermute | solution.py:24
  13.1 0.6 %cut.5 = (bf16[128,2048]{1,0:T(8,128)(2,1)S(1)}, f32[8,128]{1,0:T(8,128)}) custom-call(bf16[128,8192]{1,0:T(8,128)(2,1)S(1)} %bitcast.10, f32[8,128]{1,0:T(8,128)S(1)} %get-tuple-element.31.refs_0_), custom_call_target="tpu_custom_call" | custom-call | flops 1000 | bytes 1000 | tf_op jit(solution)/shard_map/cut/pallas_call | solution.py:43
  13.7 2.8 %collective-permute-done.refs_1_ = bf16[128,2048]{1,0:T(8,128)(2,1)S(1)} collective-permute-done((bf16[128,2048]{1,0:T(8,128)(2,1)S(1)}, bf16[128,2048]{1,0:T(8,128)(2,1)S(1)}, u32[]{:S(2)}, u32[]{:S(2)}) %collective-permute-start) | collective-permute-done | bytes 524320 | tf_op jit(solution)/shard_map/ppermute | solution.py:24
  16.5 0.7 %project.3 = (f32[128,512]{1,0:T(8,128)S(1)}, bf16[128,512]{1,0:T(8,128)(2,1)S(1)}, bf16[256,2048]{1,0:T(8,128)(2,1)S(1)}) custom-call(bf16[128,2048]{1,0:T(8,128)(2,1)S(1)} %get-tuple-element.32.refs_0_, bf16[128,2048]{1,0:T(8,128)(2,1)S(1)} %collective-permute-done.refs_1_, bf16[2048,512]{1,0:T(8,128)(2,1)S(1)} %bitcast.11), custom_call_target="tpu_custom_call" | custom-call | flops 1000 | bytes 1000 | tf_op jit(solution)/shard_map/project/pallas_call | solution.py:73
  17.2 2.1 %collective-permute-start.1 = (bf16[128,512]{1,0:T(8,128)(2,1)S(1)}, bf16[128,512]{1,0:T(8,128)(2,1)S(1)}, u32[]{:S(2)}, u32[]{:S(2)}) collective-permute-start(bf16[128,512]{1,0:T(8,128)(2,1)S(1)} %get-tuple-element.34), channel_id=1, source_target_pairs={{0,3},{1,2},{2,1},{3,0},{4,7},{5,6},{6,5},{7,4},{8,11},{9,10},{10,... | collective-permute-start | bytes 393224 | tf_op jit(solution)/shard_map/ppermute | solution.py:24
  19.3 0.6 %prepare.2 = (bf16[128,256]{1,0:T(8,128)(2,1)S(1)}, bf16[2048,256]{1,0:T(8,128)(2,1)S(1)}, f32[8,128]{1,0:T(8,128)S(1)}) custom-call(bf16[256,2048]{1,0:T(8,128)(2,1)S(1)} %get-tuple-element.37.refs_0_, s32[1,128]{1,0:T(1,128)S(1)} %bitcast.18, s32[1,1]{1,0:T(1,128)S(6)} %copy.8.count.refs_2_.refs_3_), custom_call_target="tpu_custom_call" | custom-call | flops 1000 | bytes 1000 | tf_op jit(solution)/shard_map/prepare/pallas_call | solution.py:181
  19.9 4.9 %collective-permute-done.2.refs_0_ = bf16[96,2048]{1,0:T(8,128)(2,1)S(1)} collective-permute-done((bf16[96,2048]{1,0:T(8,128)(2,1)S(1)}, bf16[96,2048]{1,0:T(8,128)(2,1)S(1)}, u32[]{:S(2)}, u32[]{:S(2)}) %collective-permute-start.2) | collective-permute-done | bytes 393248 | tf_op jit(solution)/shard_map/ppermute | solution.py:24
  24.8 0.8 %collective-permute-done.3.refs_1_ = bf16[96,2048]{1,0:T(8,128)(2,1)S(1)} collective-permute-done((bf16[96,2048]{1,0:T(8,128)(2,1)S(1)}, bf16[96,2048]{1,0:T(8,128)(2,1)S(1)}, u32[]{:S(2)}, u32[]{:S(2)}) %collective-permute-start.3) | collective-permute-done | bytes 393248 | tf_op jit(solution)/shard_map/ppermute | solution.py:24
  25.6 0.6 %project.4 = (bf16[96,512]{1,0:T(8,128)(2,1)S(1)}, bf16[96,512]{1,0:T(8,128)(2,1)S(1)}, bf16[192,2048]{1,0:T(8,128)(2,1)S(1)}) custom-call(bf16[96,2048]{1,0:T(8,128)(2,1)S(1)} %collective-permute-done.2.refs_0_, bf16[96,2048]{1,0:T(8,128)(2,1)S(1)} %collective-permute-done.3.refs_1_, bf16[2048,512]{1,0:T(8,128)(2,1)S(1)} %bitcast.12, ...), custom_call_target="tpu_custom_call" | custom-call | flops 1000 | bytes 1000 | tf_op jit(solution)/shard_map/project/pallas_call | solution.py:73
  26.2 1.5 %collective-permute-start.4 = (bf16[96,512]{1,0:T(8,128)(2,1)S(1)}, bf16[96,512]{1,0:T(8,128)(2,1)S(1)}, u32[]{:S(2)}, u32[]{:S(2)}) collective-permute-start(bf16[96,512]{1,0:T(8,128)(2,1)S(1)} %get-tuple-element.39), channel_id=1, source_target_pairs={{0,1},{1,0},{2,3},{3,2},{4,5},{5,4},{6,7},{7,6},{8,9},{9,8},{10,11... | collective-permute-start | bytes 294920 | tf_op jit(solution)/shard_map/ppermute | solution.py:24
  27.7 1.2 %collective-permute-start.8 = (bf16[96,512]{1,0:T(8,128)(2,1)S(1)}, bf16[96,512]{1,0:T(8,128)(2,1)S(1)}, u32[]{:S(2)}, u32[]{:S(2)}) collective-permute-start(bf16[96,512]{1,0:T(8,128)(2,1)S(1)} %get-tuple-element.42.refs_3_), channel_id=1, source_target_pairs={{0,2},{1,3},{2,0},{3,1},{4,6},{5,7},{6,4},{7,5},{8,10},{9,11},{10,... | collective-permute-start | bytes 294920 | tf_op jit(solution)/shard_map/ppermute | solution.py:24
  29.6 1.8 %collective-permute-start.9 = (bf16[32,512]{1,0:T(8,128)(2,1)S(1)}, bf16[32,512]{1,0:T(8,128)(2,1)S(1)}, u32[]{:S(2)}, u32[]{:S(2)}) collective-permute-start(bf16[32,512]{1,0:T(8,128)(2,1)S(1)} %get-tuple-element.44), channel_id=1, source_target_pairs={{0,2},{1,3},{2,0},{3,1},{4,6},{5,7},{6,4},{7,5},{8,10},{9,11},{10,... | collective-permute-start | bytes 98312 | tf_op jit(solution)/shard_map/ppermute | solution.py:24
  31.4 1.2 %collective-permute-start.7 = (bf16[32,512]{1,0:T(8,128)(2,1)S(1)}, bf16[32,512]{1,0:T(8,128)(2,1)S(1)}, u32[]{:S(2)}, u32[]{:S(2)}) collective-permute-start(bf16[32,512]{1,0:T(8,128)(2,1)S(1)} %get-tuple-element.43.refs_4_), channel_id=1, source_target_pairs={{0,1},{1,0},{2,3},{3,2},{4,5},{5,4},{6,7},{7,6},{8,9},{9,8},{10,11... | collective-permute-start | bytes 98312 | tf_op jit(solution)/shard_map/ppermute | solution.py:24
  32.6 0.9 %prepare.3 = (bf16[128,256]{1,0:T(8,128)(2,1)S(1)}, bf16[2048,256]{1,0:T(8,128)(2,1)S(1)}, f32[8,128]{1,0:T(8,128)S(1)}) custom-call(bf16[192,2048]{1,0:T(8,128)(2,1)S(1)} %get-tuple-element.45.refs_0_, bf16[64,2048]{1,0:T(8,128)(2,1)S(1)} %get-tuple-element.46.refs_1_, s32[1,128]{1,0:T(1,128)S(1)} %bitcast.19, s32[1,1]{1,0:T(1,128)S(6)} %copy.8.count.refs_2_.refs_3_, ...), custom_call_target="tpu_custom_call" | custom-call | flops 1000 | bytes 1000 | tf_op jit(solution)/shard_map/prepare/pallas_call | solution.py:181
  33.6 0.9 %collective-permute-done.7.refs_4_ = bf16[32,512]{1,0:T(8,128)(2,1)S(1)} collective-permute-done((bf16[32,512]{1,0:T(8,128)(2,1)S(1)}, bf16[32,512]{1,0:T(8,128)(2,1)S(1)}, u32[]{:S(2)}, u32[]{:S(2)}) %collective-permute-start.7) | collective-permute-done | bytes 32800 | tf_op jit(solution)/shard_map/ppermute | solution.py:24
  34.6 1.7 %collective-permute-start.12 = (bf16[128,512]{1,0:T(8,128)(2,1)S(1)}, bf16[128,512]{1,0:T(8,128)(2,1)S(1)}, u32[]{:S(2)}, u32[]{:S(2)}) collective-permute-start(bf16[128,512]{1,0:T(8,128)(2,1)S(1)} %slope.1.refs_0_), channel_id=1, source_target_pairs={{0,3},{1,2},{2,1},{3,0},{4,7},{5,6},{6,5},{7,4},{8,11},{9,10},{10,... | collective-permute-start | bytes 393224 | tf_op jit(solution)/shard_map/ppermute | solution.py:24
  36.3 0.8 %collective-permute-start.11 = (bf16[128,512]{1,0:T(8,128)(2,1)S(1)}, bf16[128,512]{1,0:T(8,128)(2,1)S(1)}, u32[]{:S(2)}, u32[]{:S(2)}) collective-permute-start(bf16[128,512]{1,0:T(8,128)(2,1)S(1)} %slope.1.refs_0_), channel_id=1, source_target_pairs={{0,2},{1,3},{2,0},{3,1},{4,6},{5,7},{6,4},{7,5},{8,10},{9,11},{10,... | collective-permute-start | bytes 393224 | tf_op jit(solution)/shard_map/ppermute | solution.py:24
  37.3 2.1 %collective-permute-done.12.refs_1_ = bf16[128,512]{1,0:T(8,128)(2,1)S(1)} collective-permute-done((bf16[128,512]{1,0:T(8,128)(2,1)S(1)}, bf16[128,512]{1,0:T(8,128)(2,1)S(1)}, u32[]{:S(2)}, u32[]{:S(2)}) %collective-permute-start.12) | collective-permute-done | bytes 131104 | tf_op jit(solution)/shard_map/ppermute | solution.py:24
  39.6 2.4 %collective-permute-done.11.refs_1_.refs_3_ = bf16[128,512]{1,0:T(8,128)(2,1)S(1)} collective-permute-done((bf16[128,512]{1,0:T(8,128)(2,1)S(1)}, bf16[128,512]{1,0:T(8,128)(2,1)S(1)}, u32[]{:S(2)}, u32[]{:S(2)}) %collective-permute-start.11) | collective-permute-done | bytes 131104 | tf_op jit(solution)/shard_map/ppermute | solution.py:24
  42.7 2.4 %collective-permute-start.13 = (bf16[144,128]{1,0:T(8,128)(2,1)S(1)}, bf16[144,128]{1,0:T(8,128)(2,1)S(1)}, u32[]{:S(2)}, u32[]{:S(2)}) collective-permute-start(bf16[144,128]{1,0:T(8,128)(2,1)S(1)} %kept.1.refs_0_), channel_id=1, source_target_pairs={{0,16},{4,20},{8,24},{12,28},{16,0},{20,4},{24,8},{28,12},{1,17},{... | collective-permute-start | bytes 110600 | tf_op jit(solution)/shard_map/ppermute | solution.py:24
  45.1 1.1 %collective-permute-start.14 = (bf16[144,128]{1,0:T(8,128)(2,1)S(1)}, bf16[144,128]{1,0:T(8,128)(2,1)S(1)}, u32[]{:S(2)}, u32[]{:S(2)}) collective-permute-start(bf16[144,128]{1,0:T(8,128)(2,1)S(1)} %kept.1.refs_0_), channel_id=1, source_target_pairs={{0,24},{4,28},{8,16},{12,20},{16,8},{20,12},{24,0},{28,4},{1,25},{... | collective-permute-start | bytes 110600 | tf_op jit(solution)/shard_map/ppermute | solution.py:24
  46.4 2.4 %residue.1 = (bf16[2048,512]{1,0:T(8,128)(2,1)}, f32[8,128]{1,0:T(8,128)S(1)}) custom-call(bf16[128,512]{1,0:T(8,128)(2,1)S(1)} %slope.1.refs_0_, bf16[128,512]{1,0:T(8,128)(2,1)S(1)} %collective-permute-done.12.refs_1_, bf16[128,512]{1,0:T(8,128)(2,1)S(1)} %collective-permute-done.10.refs_0_.refs_2_, ...), custom_call_target="tpu_custom_call" | custom-call | flops 1000 | bytes 1000 | tf_op jit(solution)/shard_map/residue/pallas_call | solution.py:274
  48.8 1.0 %collective-permute-done.14.refs_1_ = bf16[144,128]{1,0:T(8,128)(2,1)S(1)} collective-permute-done((bf16[144,128]{1,0:T(8,128)(2,1)S(1)}, bf16[144,128]{1,0:T(8,128)(2,1)S(1)}, u32[]{:S(2)}, u32[]{:S(2)}) %collective-permute-start.14) | collective-permute-done | bytes 36896 | tf_op jit(solution)/shard_map/ppermute | solution.py:24
  49.9 3.4 %collective-permute-start.16 = (bf16[576,128]{1,0:T(8,128)(2,1)S(1)}, bf16[576,128]{1,0:T(8,128)(2,1)S(1)}, u32[]{:S(2)}, u32[]{:S(2)}) collective-permute-start(bf16[576,128]{1,0:T(8,128)(2,1)S(1)} %join.5.group), channel_id=1, source_target_pairs={{0,4},{4,0},{8,12},{12,8},{16,20},{20,16},{24,28},{28,24},{1,5},{5... | collective-permute-start | bytes 442376 | tf_op jit(solution)/shard_map/ppermute | solution.py:24
  53.2 1.4 %half.1 = f32[2048,512]{1,0:T(8,128)S(1)} custom-call(bf16[576,128]{1,0:T(8,128)(2,1)S(1)} %join.5.group), custom_call_target="tpu_custom_call" | custom-call | flops 1000 | bytes 1000 | tf_op jit(solution)/shard_map/half/pallas_call | solution.py:356
  54.7 2.5 %outer.1 = f32[2048,512]{1,0:T(8,128)} custom-call(bf16[576,128]{1,0:T(8,128)(2,1)S(1)} %collective-permute-done.16.group, f32[2048,512]{1,0:T(8,128)S(1)} %half.1), custom_call_target="tpu_custom_call" | custom-call | flops 1000 | bytes 1000 | tf_op jit(solution)/shard_map/outer/pallas_call | solution.py:364
  (35 shorter events, 2.8 us)
Async XLA Ops:
  0.6 7.0 %copy-start.6 = (s32[1,1,128]{2,1,0:T(1,128)S(1)}, s32[1,1,128]{2,1,0:T(1,128)}, u32[]{:S(2)}) copy-start(s32[1,1,128]{2,1,0:T(1,128)} %param.11) | copy-start | bytes 1540
  1.7 14.8 %collective-permute-start = (bf16[128,2048]{1,0:T(8,128)(2,1)S(1)}, bf16[128,2048]{1,0:T(8,128)(2,1)S(1)}, u32[]{:S(2)}, u32[]{:S(2)}) collective-permute-start(bf16[128,2048]{1,0:T(8,128)(2,1)S(1)} %dynamic-slice_bitcast_fusion.refs_0_), channel_id=1, source_target_pairs={{0,3},{1,2},{2,1},{3,0},{4,7},{5,6},{6,5},{7,4},{8,11},{9,10},{10,... | collective-permute-start | bytes 1572872 | tf_op jit(solution)/shard_map/ppermute | solution.py:24
  4.8 1.6 %copy-start = (bf16[1,128,8192]{2,1,0:T(8,128)(2,1)S(1)}, bf16[1,128,8192]{2,1,0:T(8,128)(2,1)}, u32[]{:S(2)}) copy-start(bf16[1,128,8192]{2,1,0:T(8,128)(2,1)} %param.6) | copy-start | bytes 6291460
  6.4 4.0 %copy-start.1 = (bf16[1,128,8192]{2,1,0:T(8,128)(2,1)S(1)}, bf16[1,128,8192]{2,1,0:T(8,128)(2,1)}, u32[]{:S(2)}) copy-start(bf16[1,128,8192]{2,1,0:T(8,128)(2,1)} %param.6) | copy-start | bytes 6291460
  6.5 18.4 %collective-permute-start.2 = (bf16[96,2048]{1,0:T(8,128)(2,1)S(1)}, bf16[96,2048]{1,0:T(8,128)(2,1)S(1)}, u32[]{:S(2)}, u32[]{:S(2)}) collective-permute-start(bf16[96,2048]{1,0:T(8,128)(2,1)S(1)} %get-tuple-element.35), channel_id=1, source_target_pairs={{0,1},{1,0},{2,3},{3,2},{4,5},{5,4},{6,7},{7,6},{8,9},{9,8},{10,11... | collective-permute-start | bytes 1179656 | tf_op jit(solution)/shard_map/ppermute | solution.py:24
  6.8 18.8 %collective-permute-start.3 = (bf16[96,2048]{1,0:T(8,128)(2,1)S(1)}, bf16[96,2048]{1,0:T(8,128)(2,1)S(1)}, u32[]{:S(2)}, u32[]{:S(2)}) collective-permute-start(bf16[96,2048]{1,0:T(8,128)(2,1)S(1)} %get-tuple-element.36), channel_id=1, source_target_pairs={{0,2},{1,3},{2,0},{3,1},{4,6},{5,7},{6,4},{7,5},{8,10},{9,11},{10,... | collective-permute-start | bytes 1179656 | tf_op jit(solution)/shard_map/ppermute | solution.py:24
  7.7 1.6 %copy-start.3 = (bf16[1,2048,512]{2,1,0:T(8,128)(2,1)S(1)}, bf16[1,2048,512]{2,1,0:T(8,128)(2,1)}, u32[]{:S(2)}) copy-start(bf16[1,2048,512]{2,1,0:T(8,128)(2,1)} %param.9) | copy-start | bytes 6291460
  10.4 6.1 %copy-start.2 = (bf16[1,2048,512]{2,1,0:T(8,128)(2,1)S(1)}, bf16[1,2048,512]{2,1,0:T(8,128)(2,1)}, u32[]{:S(2)}) copy-start(bf16[1,2048,512]{2,1,0:T(8,128)(2,1)} %param.8) | copy-start | bytes 6291460
  10.5 18.4 %collective-permute-start.5 = (bf16[32,2048]{1,0:T(8,128)(2,1)S(1)}, bf16[32,2048]{1,0:T(8,128)(2,1)S(1)}, u32[]{:S(2)}, u32[]{:S(2)}) collective-permute-start(bf16[32,2048]{1,0:T(8,128)(2,1)S(1)} %get-tuple-element.40), channel_id=1, source_target_pairs={{0,1},{1,0},{2,3},{3,2},{4,5},{5,4},{6,7},{7,6},{8,9},{9,8},{10,11... | collective-permute-start | bytes 393224 | tf_op jit(solution)/shard_map/ppermute | solution.py:24
  11.8 17.3 %collective-permute-start.6 = (bf16[32,2048]{1,0:T(8,128)(2,1)S(1)}, bf16[32,2048]{1,0:T(8,128)(2,1)S(1)}, u32[]{:S(2)}, u32[]{:S(2)}) collective-permute-start(bf16[32,2048]{1,0:T(8,128)(2,1)S(1)} %get-tuple-element.41), channel_id=1, source_target_pairs={{0,2},{1,3},{2,0},{3,1},{4,6},{5,7},{6,4},{7,5},{8,10},{9,11},{10,... | collective-permute-start | bytes 393224 | tf_op jit(solution)/shard_map/ppermute | solution.py:24
  17.2 17.2 %collective-permute-start.1 = (bf16[128,512]{1,0:T(8,128)(2,1)S(1)}, bf16[128,512]{1,0:T(8,128)(2,1)S(1)}, u32[]{:S(2)}, u32[]{:S(2)}) collective-permute-start(bf16[128,512]{1,0:T(8,128)(2,1)S(1)} %get-tuple-element.34), channel_id=1, source_target_pairs={{0,3},{1,2},{2,1},{3,0},{4,7},{5,6},{6,5},{7,4},{8,11},{9,10},{10,... | collective-permute-start | bytes 393224 | tf_op jit(solution)/shard_map/ppermute | solution.py:24
  26.2 8.3 %copy-start.5 = (bf16[1,128,512]{2,1,0:T(8,128)(2,1)S(1)}, bf16[1,128,512]{2,1,0:T(8,128)(2,1)}, u32[]{:S(2)}) copy-start(bf16[1,128,512]{2,1,0:T(8,128)(2,1)} %param.7) | copy-start | bytes 393220
  26.2 8.2 %collective-permute-start.4 = (bf16[96,512]{1,0:T(8,128)(2,1)S(1)}, bf16[96,512]{1,0:T(8,128)(2,1)S(1)}, u32[]{:S(2)}, u32[]{:S(2)}) collective-permute-start(bf16[96,512]{1,0:T(8,128)(2,1)S(1)} %get-tuple-element.39), channel_id=1, source_target_pairs={{0,1},{1,0},{2,3},{3,2},{4,5},{5,4},{6,7},{7,6},{8,9},{9,8},{10,11... | collective-permute-start | bytes 294920 | tf_op jit(solution)/shard_map/ppermute | solution.py:24
  27.7 6.8 %collective-permute-start.8 = (bf16[96,512]{1,0:T(8,128)(2,1)S(1)}, bf16[96,512]{1,0:T(8,128)(2,1)S(1)}, u32[]{:S(2)}, u32[]{:S(2)}) collective-permute-start(bf16[96,512]{1,0:T(8,128)(2,1)S(1)} %get-tuple-element.42.refs_3_), channel_id=1, source_target_pairs={{0,2},{1,3},{2,0},{3,1},{4,6},{5,7},{6,4},{7,5},{8,10},{9,11},{10,... | collective-permute-start | bytes 294920 | tf_op jit(solution)/shard_map/ppermute | solution.py:24
  29.6 16.8 %copy-start.4 = (bf16[1,2048,512]{2,1,0:T(8,128)(2,1)S(1)}, bf16[1,2048,512]{2,1,0:T(8,128)(2,1)}, u32[]{:S(2)}) copy-start(bf16[1,2048,512]{2,1,0:T(8,128)(2,1)} %param.9) | copy-start | bytes 6291460
  29.6 4.0 %collective-permute-start.9 = (bf16[32,512]{1,0:T(8,128)(2,1)S(1)}, bf16[32,512]{1,0:T(8,128)(2,1)S(1)}, u32[]{:S(2)}, u32[]{:S(2)}) collective-permute-start(bf16[32,512]{1,0:T(8,128)(2,1)S(1)} %get-tuple-element.44), channel_id=1, source_target_pairs={{0,2},{1,3},{2,0},{3,1},{4,6},{5,7},{6,4},{7,5},{8,10},{9,11},{10,... | collective-permute-start | bytes 98312 | tf_op jit(solution)/shard_map/ppermute | solution.py:24
  31.4 3.0 %collective-permute-start.7 = (bf16[32,512]{1,0:T(8,128)(2,1)S(1)}, bf16[32,512]{1,0:T(8,128)(2,1)S(1)}, u32[]{:S(2)}, u32[]{:S(2)}) collective-permute-start(bf16[32,512]{1,0:T(8,128)(2,1)S(1)} %get-tuple-element.43.refs_4_), channel_id=1, source_target_pairs={{0,1},{1,0},{2,3},{3,2},{4,5},{5,4},{6,7},{7,6},{8,9},{9,8},{10,11... | collective-permute-start | bytes 98312 | tf_op jit(solution)/shard_map/ppermute | solution.py:24
  34.6 4.9 %collective-permute-start.12 = (bf16[128,512]{1,0:T(8,128)(2,1)S(1)}, bf16[128,512]{1,0:T(8,128)(2,1)S(1)}, u32[]{:S(2)}, u32[]{:S(2)}) collective-permute-start(bf16[128,512]{1,0:T(8,128)(2,1)S(1)} %slope.1.refs_0_), channel_id=1, source_target_pairs={{0,3},{1,2},{2,1},{3,0},{4,7},{5,6},{6,5},{7,4},{8,11},{9,10},{10,... | collective-permute-start | bytes 393224 | tf_op jit(solution)/shard_map/ppermute | solution.py:24
  36.3 5.7 %collective-permute-start.11 = (bf16[128,512]{1,0:T(8,128)(2,1)S(1)}, bf16[128,512]{1,0:T(8,128)(2,1)S(1)}, u32[]{:S(2)}, u32[]{:S(2)}) collective-permute-start(bf16[128,512]{1,0:T(8,128)(2,1)S(1)} %slope.1.refs_0_), channel_id=1, source_target_pairs={{0,2},{1,3},{2,0},{3,1},{4,6},{5,7},{6,4},{7,5},{8,10},{9,11},{10,... | collective-permute-start | bytes 393224 | tf_op jit(solution)/shard_map/ppermute | solution.py:24
  37.0 5.4 %collective-permute-start.10 = (bf16[128,512]{1,0:T(8,128)(2,1)S(1)}, bf16[128,512]{1,0:T(8,128)(2,1)S(1)}, u32[]{:S(2)}, u32[]{:S(2)}) collective-permute-start(bf16[128,512]{1,0:T(8,128)(2,1)S(1)} %slope.1.refs_0_), channel_id=1, source_target_pairs={{0,1},{1,0},{2,3},{3,2},{4,5},{5,4},{6,7},{7,6},{8,9},{9,8},{10,11... | collective-permute-start | bytes 393224 | tf_op jit(solution)/shard_map/ppermute | solution.py:24
  42.7 6.1 %collective-permute-start.13 = (bf16[144,128]{1,0:T(8,128)(2,1)S(1)}, bf16[144,128]{1,0:T(8,128)(2,1)S(1)}, u32[]{:S(2)}, u32[]{:S(2)}) collective-permute-start(bf16[144,128]{1,0:T(8,128)(2,1)S(1)} %kept.1.refs_0_), channel_id=1, source_target_pairs={{0,16},{4,20},{8,24},{12,28},{16,0},{20,4},{24,8},{28,12},{1,17},{... | collective-permute-start | bytes 110600 | tf_op jit(solution)/shard_map/ppermute | solution.py:24
  45.1 4.7 %collective-permute-start.14 = (bf16[144,128]{1,0:T(8,128)(2,1)S(1)}, bf16[144,128]{1,0:T(8,128)(2,1)S(1)}, u32[]{:S(2)}, u32[]{:S(2)}) collective-permute-start(bf16[144,128]{1,0:T(8,128)(2,1)S(1)} %kept.1.refs_0_), channel_id=1, source_target_pairs={{0,24},{4,28},{8,16},{12,20},{16,8},{20,12},{24,0},{28,4},{1,25},{... | collective-permute-start | bytes 110600 | tf_op jit(solution)/shard_map/ppermute | solution.py:24
  46.2 3.7 %collective-permute-start.15 = (bf16[144,128]{1,0:T(8,128)(2,1)S(1)}, bf16[144,128]{1,0:T(8,128)(2,1)S(1)}, u32[]{:S(2)}, u32[]{:S(2)}) collective-permute-start(bf16[144,128]{1,0:T(8,128)(2,1)S(1)} %kept.1.refs_0_), channel_id=1, source_target_pairs={{0,8},{4,12},{8,0},{12,4},{16,24},{20,28},{24,16},{28,20},{1,9},{5... | collective-permute-start | bytes 110600 | tf_op jit(solution)/shard_map/ppermute | solution.py:24
  49.9 4.8 %collective-permute-start.16 = (bf16[576,128]{1,0:T(8,128)(2,1)S(1)}, bf16[576,128]{1,0:T(8,128)(2,1)S(1)}, u32[]{:S(2)}, u32[]{:S(2)}) collective-permute-start(bf16[576,128]{1,0:T(8,128)(2,1)S(1)} %join.5.group), channel_id=1, source_target_pairs={{0,4},{4,0},{8,12},{12,8},{16,20},{20,16},{24,28},{28,24},{1,5},{5... | collective-permute-start | bytes 442376 | tf_op jit(solution)/shard_map/ppermute | solution.py:24

commit v14 on v13

--- a/solution.py
+++ b/solution.py
@@ -270,7 +270,7 @@
 def residue(slopes, order, xts, fb, keep):
     depth, kw = fb.shape
     total = sum(xt.shape[1] for xt in xts)
-    tile = min(depth, 512)
+    tile = min(depth, 256)
     return pl.pallas_call(
         functools.partial(residue_kernel, order, tile),
         out_shape=[
@@ -418,8 +418,7 @@
     order_near = [(k, low, high) for low, high in spans for k in range(len(near))]
     wide = gather(slopes[:n_far], order_far, xg_far)
     message = kept(slopes[n_far:], order_near, wide, xg_near, fbk, slot_row)
-    chips = [4, *range(n_rep - 2, 4, -2), 2] if n_rep > 4 else list(range(2, n_rep, 2))
-    same_core = [swap(message, "rep", n_rep, d) for d in chips]
+    same_core = [swap(message, "rep", n_rep, d) for d in range(n_rep - 2, 0, -2)]
     order = order_far + [(n_far + k, low, high) for k, low, high in order_near]
     new_feedback, token = residue(slopes, order, [xt_far, xt_near], fb, keep)
     joined, after = message, [token]

time: 57.4 us -> 57.5 us (level)
  no operation moved by 1% of the time
where the time goes in v14:
time: 57.5 us; the launch traced here: 57.3 us
  starting transfers between devices  23.4 us (41%)
  waiting for transfers between devices  15.8 us (27%)
  Pallas kernels  12.1 us (21%)
  local copies, waits for them, and re-layouts  4.29 us (7%)
  between operations  1.69 us (3%)
    ppermute x17, starting transfers between devices, swap(): return lax.ppermute(x, axis, [(i, i ^ d) for i in range(n)])  23.4 us
    ppermute x17, waiting for transfers between devices, swap(): return lax.ppermute(x, axis, [(i, i ^ d) for i in range(n)])  15.8 us
    unnamed x14, local copies, waits for them, and re-layouts  3.2 us
    pallas_call x1, Pallas kernels, outer(): pl.pallas_call(functools.partial(outer_kernel, cap, kw // LANES, tile, n)...  2.54 us
    pallas_call x1, Pallas kernels, residue(): pl.pallas_call(functools.partial(residue_kernel, order, tile), out_shape=...  2.38 us
    pallas_call x3, Pallas kernels, project(): pl.pallas_call(functools.partial(project_kernel, n), out_shape=[jax.Shape...  1.76 us
    pallas_call x2, Pallas kernels, prepare(): pl.pallas_call(functools.partial(prepare_kernel, per_row, len(xs)), out_s...  1.55 us
    pallas_call x1, Pallas kernels, outer(): pl.pallas_call(functools.partial(half_kernel, cap, kw // LANES, tile), ou...  1.41 us
  transfers between devices with their start and end apart: 17, of which 9 were waited for; matrix products, arithmetic and copies ran while one was open for 0% of the time, Pallas kernels for 16%

profile of v14, /device:TPU:1, one launch (start us, length us, event | category | flops | bytes accessed | tf_op | source)
XLA Modules:
  0.0 57.3 jit_solution(8629864649611227696)
XLA Ops:
  0.6 1.1 %dynamic-slice_bitcast_fusion.refs_0_ = bf16[128,2048]{1,0:T(8,128)(2,1)S(1)} fusion(bf16[1,128,8192]{2,1,0:T(8,128)(2,1)} %param.6, s32[]{:T(128)S(6)} %select_n.3), kind=kLoop, calls=%fused_computation | loop fusion | bytes 1048580 | tf_op jit(solution)/shard_map/dynamic_slice | solution.py:389
  1.7 3.1 %collective-permute-start = (bf16[128,2048]{1,0:T(8,128)(2,1)S(1)}, bf16[128,2048]{1,0:T(8,128)(2,1)S(1)}, u32[]{:S(2)}, u32[]{:S(2)}) collective-permute-start(bf16[128,2048]{1,0:T(8,128)(2,1)S(1)} %dynamic-slice_bitcast_fusion.refs_0_), channel_id=1, source_target_pairs={{0,3},{1,2},{2,1},{3,0},{4,7},{5,6},{6,5},{7,4},{8,11},{9,10},{10,... | collective-permute-start | bytes 1572872 | tf_op jit(solution)/shard_map/ppermute | solution.py:24
  4.8 1.6 %copy-done = bf16[1,128,8192]{2,1,0:T(8,128)(2,1)S(1)} copy-done((bf16[1,128,8192]{2,1,0:T(8,128)(2,1)S(1)}, bf16[1,128,8192]{2,1,0:T(8,128)(2,1)}, u32[]{:S(2)}) %copy-start) | copy-done | bytes 2097176
  7.7 1.6 %copy-done.3 = bf16[1,2048,512]{2,1,0:T(8,128)(2,1)S(1)} copy-done((bf16[1,2048,512]{2,1,0:T(8,128)(2,1)S(1)}, bf16[1,2048,512]{2,1,0:T(8,128)(2,1)}, u32[]{:S(2)}) %copy-start.3) | copy-done | bytes 2097176
  9.3 1.1 %early.1 = (f32[128,128]{1,0:T(8,128)S(1)}, bf16[2048,512]{1,0:T(8,128)(2,1)S(1)}, f32[8,128]{1,0:T(8,128)S(1)}) custom-call(s32[1,128]{1,0:T(1,128)S(1)} %bitcast.17, s32[1,1]{1,0:T(1,128)S(6)} %copy.8.count.refs_2_.refs_3_, bf16[2048,512]{1,0:T(8,128)(2,1)S(1)} %bitcast.14, f32[8,128]{1,0:T(8,128)S(1)} %get-tuple-element.29.after), custom_call_target="tpu_custom_call" | custom-call | flops 1000 | bytes 1000 | tf_op jit(solution)/shard_map/early/pallas_call | solution.py:145
  10.5 1.3 %collective-permute-start.5 = (bf16[32,2048]{1,0:T(8,128)(2,1)S(1)}, bf16[32,2048]{1,0:T(8,128)(2,1)S(1)}, u32[]{:S(2)}, u32[]{:S(2)}) collective-permute-start(bf16[32,2048]{1,0:T(8,128)(2,1)S(1)} %get-tuple-element.40), channel_id=1, source_target_pairs={{0,1},{1,0},{2,3},{3,2},{4,5},{5,4},{6,7},{7,6},{8,9},{9,8},{10,11... | collective-permute-start | bytes 393224 | tf_op jit(solution)/shard_map/ppermute | solution.py:24
  11.8 1.2 %collective-permute-start.6 = (bf16[32,2048]{1,0:T(8,128)(2,1)S(1)}, bf16[32,2048]{1,0:T(8,128)(2,1)S(1)}, u32[]{:S(2)}, u32[]{:S(2)}) collective-permute-start(bf16[32,2048]{1,0:T(8,128)(2,1)S(1)} %get-tuple-element.41), channel_id=1, source_target_pairs={{0,2},{1,3},{2,0},{3,1},{4,6},{5,7},{6,4},{7,5},{8,10},{9,11},{10,... | collective-permute-start | bytes 393224 | tf_op jit(solution)/shard_map/ppermute | solution.py:24
  13.1 0.6 %cut.5 = (bf16[128,2048]{1,0:T(8,128)(2,1)S(1)}, f32[8,128]{1,0:T(8,128)}) custom-call(bf16[128,8192]{1,0:T(8,128)(2,1)S(1)} %bitcast.10, f32[8,128]{1,0:T(8,128)S(1)} %get-tuple-element.31.refs_0_), custom_call_target="tpu_custom_call" | custom-call | flops 1000 | bytes 1000 | tf_op jit(solution)/shard_map/cut/pallas_call | solution.py:43
  13.7 2.8 %collective-permute-done.refs_1_ = bf16[128,2048]{1,0:T(8,128)(2,1)S(1)} collective-permute-done((bf16[128,2048]{1,0:T(8,128)(2,1)S(1)}, bf16[128,2048]{1,0:T(8,128)(2,1)S(1)}, u32[]{:S(2)}, u32[]{:S(2)}) %collective-permute-start) | collective-permute-done | bytes 524320 | tf_op jit(solution)/shard_map/ppermute | solution.py:24
  16.5 0.7 %project.3 = (f32[128,512]{1,0:T(8,128)S(1)}, bf16[128,512]{1,0:T(8,128)(2,1)S(1)}, bf16[256,2048]{1,0:T(8,128)(2,1)S(1)}) custom-call(bf16[128,2048]{1,0:T(8,128)(2,1)S(1)} %get-tuple-element.32.refs_0_, bf16[128,2048]{1,0:T(8,128)(2,1)S(1)} %collective-permute-done.refs_1_, bf16[2048,512]{1,0:T(8,128)(2,1)S(1)} %bitcast.11), custom_call_target="tpu_custom_call" | custom-call | flops 1000 | bytes 1000 | tf_op jit(solution)/shard_map/project/pallas_call | solution.py:73
  17.2 2.1 %collective-permute-start.1 = (bf16[128,512]{1,0:T(8,128)(2,1)S(1)}, bf16[128,512]{1,0:T(8,128)(2,1)S(1)}, u32[]{:S(2)}, u32[]{:S(2)}) collective-permute-start(bf16[128,512]{1,0:T(8,128)(2,1)S(1)} %get-tuple-element.34), channel_id=1, source_target_pairs={{0,3},{1,2},{2,1},{3,0},{4,7},{5,6},{6,5},{7,4},{8,11},{9,10},{10,... | collective-permute-start | bytes 393224 | tf_op jit(solution)/shard_map/ppermute | solution.py:24
  19.3 0.6 %prepare.2 = (bf16[128,256]{1,0:T(8,128)(2,1)S(1)}, bf16[2048,256]{1,0:T(8,128)(2,1)S(1)}, f32[8,128]{1,0:T(8,128)S(1)}) custom-call(bf16[256,2048]{1,0:T(8,128)(2,1)S(1)} %get-tuple-element.37.refs_0_, s32[1,128]{1,0:T(1,128)S(1)} %bitcast.18, s32[1,1]{1,0:T(1,128)S(6)} %copy.8.count.refs_2_.refs_3_), custom_call_target="tpu_custom_call" | custom-call | flops 1000 | bytes 1000 | tf_op jit(solution)/shard_map/prepare/pallas_call | solution.py:181
  19.9 4.9 %collective-permute-done.2.refs_0_ = bf16[96,2048]{1,0:T(8,128)(2,1)S(1)} collective-permute-done((bf16[96,2048]{1,0:T(8,128)(2,1)S(1)}, bf16[96,2048]{1,0:T(8,128)(2,1)S(1)}, u32[]{:S(2)}, u32[]{:S(2)}) %collective-permute-start.2) | collective-permute-done | bytes 393248 | tf_op jit(solution)/shard_map/ppermute | solution.py:24
  24.8 0.8 %collective-permute-done.3.refs_1_ = bf16[96,2048]{1,0:T(8,128)(2,1)S(1)} collective-permute-done((bf16[96,2048]{1,0:T(8,128)(2,1)S(1)}, bf16[96,2048]{1,0:T(8,128)(2,1)S(1)}, u32[]{:S(2)}, u32[]{:S(2)}) %collective-permute-start.3) | collective-permute-done | bytes 393248 | tf_op jit(solution)/shard_map/ppermute | solution.py:24
  25.6 0.6 %project.4 = (bf16[96,512]{1,0:T(8,128)(2,1)S(1)}, bf16[96,512]{1,0:T(8,128)(2,1)S(1)}, bf16[192,2048]{1,0:T(8,128)(2,1)S(1)}) custom-call(bf16[96,2048]{1,0:T(8,128)(2,1)S(1)} %collective-permute-done.2.refs_0_, bf16[96,2048]{1,0:T(8,128)(2,1)S(1)} %collective-permute-done.3.refs_1_, bf16[2048,512]{1,0:T(8,128)(2,1)S(1)} %bitcast.12, ...), custom_call_target="tpu_custom_call" | custom-call | flops 1000 | bytes 1000 | tf_op jit(solution)/shard_map/project/pallas_call | solution.py:73
  26.2 1.5 %collective-permute-start.4 = (bf16[96,512]{1,0:T(8,128)(2,1)S(1)}, bf16[96,512]{1,0:T(8,128)(2,1)S(1)}, u32[]{:S(2)}, u32[]{:S(2)}) collective-permute-start(bf16[96,512]{1,0:T(8,128)(2,1)S(1)} %get-tuple-element.39), channel_id=1, source_target_pairs={{0,1},{1,0},{2,3},{3,2},{4,5},{5,4},{6,7},{7,6},{8,9},{9,8},{10,11... | collective-permute-start | bytes 294920 | tf_op jit(solution)/shard_map/ppermute | solution.py:24
  27.7 1.2 %collective-permute-start.8 = (bf16[96,512]{1,0:T(8,128)(2,1)S(1)}, bf16[96,512]{1,0:T(8,128)(2,1)S(1)}, u32[]{:S(2)}, u32[]{:S(2)}) collective-permute-start(bf16[96,512]{1,0:T(8,128)(2,1)S(1)} %get-tuple-element.42.refs_3_), channel_id=1, source_target_pairs={{0,2},{1,3},{2,0},{3,1},{4,6},{5,7},{6,4},{7,5},{8,10},{9,11},{10,... | collective-permute-start | bytes 294920 | tf_op jit(solution)/shard_map/ppermute | solution.py:24
  29.6 1.8 %collective-permute-start.9 = (bf16[32,512]{1,0:T(8,128)(2,1)S(1)}, bf16[32,512]{1,0:T(8,128)(2,1)S(1)}, u32[]{:S(2)}, u32[]{:S(2)}) collective-permute-start(bf16[32,512]{1,0:T(8,128)(2,1)S(1)} %get-tuple-element.44), channel_id=1, source_target_pairs={{0,2},{1,3},{2,0},{3,1},{4,6},{5,7},{6,4},{7,5},{8,10},{9,11},{10,... | collective-permute-start | bytes 98312 | tf_op jit(solution)/shard_map/ppermute | solution.py:24
  31.4 1.2 %collective-permute-start.7 = (bf16[32,512]{1,0:T(8,128)(2,1)S(1)}, bf16[32,512]{1,0:T(8,128)(2,1)S(1)}, u32[]{:S(2)}, u32[]{:S(2)}) collective-permute-start(bf16[32,512]{1,0:T(8,128)(2,1)S(1)} %get-tuple-element.43.refs_4_), channel_id=1, source_target_pairs={{0,1},{1,0},{2,3},{3,2},{4,5},{5,4},{6,7},{7,6},{8,9},{9,8},{10,11... | collective-permute-start | bytes 98312 | tf_op jit(solution)/shard_map/ppermute | solution.py:24
  32.6 0.9 %prepare.3 = (bf16[128,256]{1,0:T(8,128)(2,1)S(1)}, bf16[2048,256]{1,0:T(8,128)(2,1)S(1)}, f32[8,128]{1,0:T(8,128)S(1)}) custom-call(bf16[192,2048]{1,0:T(8,128)(2,1)S(1)} %get-tuple-element.45.refs_0_, bf16[64,2048]{1,0:T(8,128)(2,1)S(1)} %get-tuple-element.46.refs_1_, s32[1,128]{1,0:T(1,128)S(1)} %bitcast.19, s32[1,1]{1,0:T(1,128)S(6)} %copy.8.count.refs_2_.refs_3_, ...), custom_call_target="tpu_custom_call" | custom-call | flops 1000 | bytes 1000 | tf_op jit(solution)/shard_map/prepare/pallas_call | solution.py:181
  33.6 0.9 %collective-permute-done.7.refs_4_ = bf16[32,512]{1,0:T(8,128)(2,1)S(1)} collective-permute-done((bf16[32,512]{1,0:T(8,128)(2,1)S(1)}, bf16[32,512]{1,0:T(8,128)(2,1)S(1)}, u32[]{:S(2)}, u32[]{:S(2)}) %collective-permute-start.7) | collective-permute-done | bytes 32800 | tf_op jit(solution)/shard_map/ppermute | solution.py:24
  34.6 1.7 %collective-permute-start.12 = (bf16[128,512]{1,0:T(8,128)(2,1)S(1)}, bf16[128,512]{1,0:T(8,128)(2,1)S(1)}, u32[]{:S(2)}, u32[]{:S(2)}) collective-permute-start(bf16[128,512]{1,0:T(8,128)(2,1)S(1)} %slope.1.refs_0_), channel_id=1, source_target_pairs={{0,3},{1,2},{2,1},{3,0},{4,7},{5,6},{6,5},{7,4},{8,11},{9,10},{10,... | collective-permute-start | bytes 393224 | tf_op jit(solution)/shard_map/ppermute | solution.py:24
  36.3 0.8 %collective-permute-start.11 = (bf16[128,512]{1,0:T(8,128)(2,1)S(1)}, bf16[128,512]{1,0:T(8,128)(2,1)S(1)}, u32[]{:S(2)}, u32[]{:S(2)}) collective-permute-start(bf16[128,512]{1,0:T(8,128)(2,1)S(1)} %slope.1.refs_0_), channel_id=1, source_target_pairs={{0,2},{1,3},{2,0},{3,1},{4,6},{5,7},{6,4},{7,5},{8,10},{9,11},{10,... | collective-permute-start | bytes 393224 | tf_op jit(solution)/shard_map/ppermute | solution.py:24
  37.3 2.1 %collective-permute-done.12.refs_1_ = bf16[128,512]{1,0:T(8,128)(2,1)S(1)} collective-permute-done((bf16[128,512]{1,0:T(8,128)(2,1)S(1)}, bf16[128,512]{1,0:T(8,128)(2,1)S(1)}, u32[]{:S(2)}, u32[]{:S(2)}) %collective-permute-start.12) | collective-permute-done | bytes 131104 | tf_op jit(solution)/shard_map/ppermute | solution.py:24
  39.6 2.4 %collective-permute-done.11.refs_1_.refs_3_ = bf16[128,512]{1,0:T(8,128)(2,1)S(1)} collective-permute-done((bf16[128,512]{1,0:T(8,128)(2,1)S(1)}, bf16[128,512]{1,0:T(8,128)(2,1)S(1)}, u32[]{:S(2)}, u32[]{:S(2)}) %collective-permute-start.11) | collective-permute-done | bytes 131104 | tf_op jit(solution)/shard_map/ppermute | solution.py:24
  41.9 0.5 collective-permute-done.10.refs_0_.refs_2_
  42.7 3.4 %collective-permute-start.13 = (bf16[144,128]{1,0:T(8,128)(2,1)S(1)}, bf16[144,128]{1,0:T(8,128)(2,1)S(1)}, u32[]{:S(2)}, u32[]{:S(2)}) collective-permute-start(bf16[144,128]{1,0:T(8,128)(2,1)S(1)} %kept.1.refs_0_), channel_id=1, source_target_pairs={{0,24},{4,28},{8,16},{12,20},{16,8},{20,12},{24,0},{28,4},{1,25},{... | collective-permute-start | bytes 110600 | tf_op jit(solution)/shard_map/ppermute | solution.py:24
  46.5 2.4 %residue.1 = (bf16[2048,512]{1,0:T(8,128)(2,1)}, f32[8,128]{1,0:T(8,128)S(1)}) custom-call(bf16[128,512]{1,0:T(8,128)(2,1)S(1)} %slope.1.refs_0_, bf16[128,512]{1,0:T(8,128)(2,1)S(1)} %collective-permute-done.12.refs_1_, bf16[128,512]{1,0:T(8,128)(2,1)S(1)} %collective-permute-done.10.refs_0_.refs_2_, ...), custom_call_target="tpu_custom_call" | custom-call | flops 1000 | bytes 1000 | tf_op jit(solution)/shard_map/residue/pallas_call | solution.py:274
  48.9 1.3 %collective-permute-done.14.refs_1_ = bf16[144,128]{1,0:T(8,128)(2,1)S(1)} collective-permute-done((bf16[144,128]{1,0:T(8,128)(2,1)S(1)}, bf16[144,128]{1,0:T(8,128)(2,1)S(1)}, u32[]{:S(2)}, u32[]{:S(2)}) %collective-permute-start.14) | collective-permute-done | bytes 36896 | tf_op jit(solution)/shard_map/ppermute | solution.py:24
  50.3 3.1 %collective-permute-start.16 = (bf16[576,128]{1,0:T(8,128)(2,1)S(1)}, bf16[576,128]{1,0:T(8,128)(2,1)S(1)}, u32[]{:S(2)}, u32[]{:S(2)}) collective-permute-start(bf16[576,128]{1,0:T(8,128)(2,1)S(1)} %join.5.group), channel_id=1, source_target_pairs={{0,4},{4,0},{8,12},{12,8},{16,20},{20,16},{24,28},{28,24},{1,5},{5... | collective-permute-start | bytes 442376 | tf_op jit(solution)/shard_map/ppermute | solution.py:24
  53.4 1.4 %half.1 = f32[2048,512]{1,0:T(8,128)S(1)} custom-call(bf16[576,128]{1,0:T(8,128)(2,1)S(1)} %join.5.group), custom_call_target="tpu_custom_call" | custom-call | flops 1000 | bytes 1000 | tf_op jit(solution)/shard_map/half/pallas_call | solution.py:356
  54.8 2.5 %outer.1 = f32[2048,512]{1,0:T(8,128)} custom-call(bf16[576,128]{1,0:T(8,128)(2,1)S(1)} %collective-permute-done.16.group, f32[2048,512]{1,0:T(8,128)S(1)} %half.1), custom_call_target="tpu_custom_call" | custom-call | flops 1000 | bytes 1000 | tf_op jit(solution)/shard_map/outer/pallas_call | solution.py:364
  (35 shorter events, 2.5 us)
Async XLA Ops:
  0.6 7.0 %copy-start.6 = (s32[1,1,128]{2,1,0:T(1,128)S(1)}, s32[1,1,128]{2,1,0:T(1,128)}, u32[]{:S(2)}) copy-start(s32[1,1,128]{2,1,0:T(1,128)} %param.11) | copy-start | bytes 1540
  1.7 14.8 %collective-permute-start = (bf16[128,2048]{1,0:T(8,128)(2,1)S(1)}, bf16[128,2048]{1,0:T(8,128)(2,1)S(1)}, u32[]{:S(2)}, u32[]{:S(2)}) collective-permute-start(bf16[128,2048]{1,0:T(8,128)(2,1)S(1)} %dynamic-slice_bitcast_fusion.refs_0_), channel_id=1, source_target_pairs={{0,3},{1,2},{2,1},{3,0},{4,7},{5,6},{6,5},{7,4},{8,11},{9,10},{10,... | collective-permute-start | bytes 1572872 | tf_op jit(solution)/shard_map/ppermute | solution.py:24
  4.8 1.6 %copy-start = (bf16[1,128,8192]{2,1,0:T(8,128)(2,1)S(1)}, bf16[1,128,8192]{2,1,0:T(8,128)(2,1)}, u32[]{:S(2)}) copy-start(bf16[1,128,8192]{2,1,0:T(8,128)(2,1)} %param.6) | copy-start | bytes 6291460
  6.4 4.0 %copy-start.1 = (bf16[1,128,8192]{2,1,0:T(8,128)(2,1)S(1)}, bf16[1,128,8192]{2,1,0:T(8,128)(2,1)}, u32[]{:S(2)}) copy-start(bf16[1,128,8192]{2,1,0:T(8,128)(2,1)} %param.6) | copy-start | bytes 6291460
  6.5 18.4 %collective-permute-start.2 = (bf16[96,2048]{1,0:T(8,128)(2,1)S(1)}, bf16[96,2048]{1,0:T(8,128)(2,1)S(1)}, u32[]{:S(2)}, u32[]{:S(2)}) collective-permute-start(bf16[96,2048]{1,0:T(8,128)(2,1)S(1)} %get-tuple-element.35), channel_id=1, source_target_pairs={{0,1},{1,0},{2,3},{3,2},{4,5},{5,4},{6,7},{7,6},{8,9},{9,8},{10,11... | collective-permute-start | bytes 1179656 | tf_op jit(solution)/shard_map/ppermute | solution.py:24
  6.8 18.8 %collective-permute-start.3 = (bf16[96,2048]{1,0:T(8,128)(2,1)S(1)}, bf16[96,2048]{1,0:T(8,128)(2,1)S(1)}, u32[]{:S(2)}, u32[]{:S(2)}) collective-permute-start(bf16[96,2048]{1,0:T(8,128)(2,1)S(1)} %get-tuple-element.36), channel_id=1, source_target_pairs={{0,2},{1,3},{2,0},{3,1},{4,6},{5,7},{6,4},{7,5},{8,10},{9,11},{10,... | collective-permute-start | bytes 1179656 | tf_op jit(solution)/shard_map/ppermute | solution.py:24
  7.7 1.6 %copy-start.3 = (bf16[1,2048,512]{2,1,0:T(8,128)(2,1)S(1)}, bf16[1,2048,512]{2,1,0:T(8,128)(2,1)}, u32[]{:S(2)}) copy-start(bf16[1,2048,512]{2,1,0:T(8,128)(2,1)} %param.9) | copy-start | bytes 6291460
  10.4 6.1 %copy-start.2 = (bf16[1,2048,512]{2,1,0:T(8,128)(2,1)S(1)}, bf16[1,2048,512]{2,1,0:T(8,128)(2,1)}, u32[]{:S(2)}) copy-start(bf16[1,2048,512]{2,1,0:T(8,128)(2,1)} %param.8) | copy-start | bytes 6291460
  10.5 18.4 %collective-permute-start.5 = (bf16[32,2048]{1,0:T(8,128)(2,1)S(1)}, bf16[32,2048]{1,0:T(8,128)(2,1)S(1)}, u32[]{:S(2)}, u32[]{:S(2)}) collective-permute-start(bf16[32,2048]{1,0:T(8,128)(2,1)S(1)} %get-tuple-element.40), channel_id=1, source_target_pairs={{0,1},{1,0},{2,3},{3,2},{4,5},{5,4},{6,7},{7,6},{8,9},{9,8},{10,11... | collective-permute-start | bytes 393224 | tf_op jit(solution)/shard_map/ppermute | solution.py:24
  11.8 17.3 %collective-permute-start.6 = (bf16[32,2048]{1,0:T(8,128)(2,1)S(1)}, bf16[32,2048]{1,0:T(8,128)(2,1)S(1)}, u32[]{:S(2)}, u32[]{:S(2)}) collective-permute-start(bf16[32,2048]{1,0:T(8,128)(2,1)S(1)} %get-tuple-element.41), channel_id=1, source_target_pairs={{0,2},{1,3},{2,0},{3,1},{4,6},{5,7},{6,4},{7,5},{8,10},{9,11},{10,... | collective-permute-start | bytes 393224 | tf_op jit(solution)/shard_map/ppermute | solution.py:24
  17.2 17.2 %collective-permute-start.1 = (bf16[128,512]{1,0:T(8,128)(2,1)S(1)}, bf16[128,512]{1,0:T(8,128)(2,1)S(1)}, u32[]{:S(2)}, u32[]{:S(2)}) collective-permute-start(bf16[128,512]{1,0:T(8,128)(2,1)S(1)} %get-tuple-element.34), channel_id=1, source_target_pairs={{0,3},{1,2},{2,1},{3,0},{4,7},{5,6},{6,5},{7,4},{8,11},{9,10},{10,... | collective-permute-start | bytes 393224 | tf_op jit(solution)/shard_map/ppermute | solution.py:24
  26.2 8.3 %copy-start.5 = (bf16[1,128,512]{2,1,0:T(8,128)(2,1)S(1)}, bf16[1,128,512]{2,1,0:T(8,128)(2,1)}, u32[]{:S(2)}) copy-start(bf16[1,128,512]{2,1,0:T(8,128)(2,1)} %param.7) | copy-start | bytes 393220
  26.2 8.2 %collective-permute-start.4 = (bf16[96,512]{1,0:T(8,128)(2,1)S(1)}, bf16[96,512]{1,0:T(8,128)(2,1)S(1)}, u32[]{:S(2)}, u32[]{:S(2)}) collective-permute-start(bf16[96,512]{1,0:T(8,128)(2,1)S(1)} %get-tuple-element.39), channel_id=1, source_target_pairs={{0,1},{1,0},{2,3},{3,2},{4,5},{5,4},{6,7},{7,6},{8,9},{9,8},{10,11... | collective-permute-start | bytes 294920 | tf_op jit(solution)/shard_map/ppermute | solution.py:24
  27.7 6.8 %collective-permute-start.8 = (bf16[96,512]{1,0:T(8,128)(2,1)S(1)}, bf16[96,512]{1,0:T(8,128)(2,1)S(1)}, u32[]{:S(2)}, u32[]{:S(2)}) collective-permute-start(bf16[96,512]{1,0:T(8,128)(2,1)S(1)} %get-tuple-element.42.refs_3_), channel_id=1, source_target_pairs={{0,2},{1,3},{2,0},{3,1},{4,6},{5,7},{6,4},{7,5},{8,10},{9,11},{10,... | collective-permute-start | bytes 294920 | tf_op jit(solution)/shard_map/ppermute | solution.py:24
  29.6 16.9 %copy-start.4 = (bf16[1,2048,512]{2,1,0:T(8,128)(2,1)S(1)}, bf16[1,2048,512]{2,1,0:T(8,128)(2,1)}, u32[]{:S(2)}) copy-start(bf16[1,2048,512]{2,1,0:T(8,128)(2,1)} %param.9) | copy-start | bytes 6291460
  29.6 4.0 %collective-permute-start.9 = (bf16[32,512]{1,0:T(8,128)(2,1)S(1)}, bf16[32,512]{1,0:T(8,128)(2,1)S(1)}, u32[]{:S(2)}, u32[]{:S(2)}) collective-permute-start(bf16[32,512]{1,0:T(8,128)(2,1)S(1)} %get-tuple-element.44), channel_id=1, source_target_pairs={{0,2},{1,3},{2,0},{3,1},{4,6},{5,7},{6,4},{7,5},{8,10},{9,11},{10,... | collective-permute-start | bytes 98312 | tf_op jit(solution)/shard_map/ppermute | solution.py:24
  31.4 3.0 %collective-permute-start.7 = (bf16[32,512]{1,0:T(8,128)(2,1)S(1)}, bf16[32,512]{1,0:T(8,128)(2,1)S(1)}, u32[]{:S(2)}, u32[]{:S(2)}) collective-permute-start(bf16[32,512]{1,0:T(8,128)(2,1)S(1)} %get-tuple-element.43.refs_4_), channel_id=1, source_target_pairs={{0,1},{1,0},{2,3},{3,2},{4,5},{5,4},{6,7},{7,6},{8,9},{9,8},{10,11... | collective-permute-start | bytes 98312 | tf_op jit(solution)/shard_map/ppermute | solution.py:24
  34.6 4.9 %collective-permute-start.12 = (bf16[128,512]{1,0:T(8,128)(2,1)S(1)}, bf16[128,512]{1,0:T(8,128)(2,1)S(1)}, u32[]{:S(2)}, u32[]{:S(2)}) collective-permute-start(bf16[128,512]{1,0:T(8,128)(2,1)S(1)} %slope.1.refs_0_), channel_id=1, source_target_pairs={{0,3},{1,2},{2,1},{3,0},{4,7},{5,6},{6,5},{7,4},{8,11},{9,10},{10,... | collective-permute-start | bytes 393224 | tf_op jit(solution)/shard_map/ppermute | solution.py:24
  36.3 5.7 %collective-permute-start.11 = (bf16[128,512]{1,0:T(8,128)(2,1)S(1)}, bf16[128,512]{1,0:T(8,128)(2,1)S(1)}, u32[]{:S(2)}, u32[]{:S(2)}) collective-permute-start(bf16[128,512]{1,0:T(8,128)(2,1)S(1)} %slope.1.refs_0_), channel_id=1, source_target_pairs={{0,2},{1,3},{2,0},{3,1},{4,6},{5,7},{6,4},{7,5},{8,10},{9,11},{10,... | collective-permute-start | bytes 393224 | tf_op jit(solution)/shard_map/ppermute | solution.py:24
  37.0 5.4 %collective-permute-start.10 = (bf16[128,512]{1,0:T(8,128)(2,1)S(1)}, bf16[128,512]{1,0:T(8,128)(2,1)S(1)}, u32[]{:S(2)}, u32[]{:S(2)}) collective-permute-start(bf16[128,512]{1,0:T(8,128)(2,1)S(1)} %slope.1.refs_0_), channel_id=1, source_target_pairs={{0,1},{1,0},{2,3},{3,2},{4,5},{5,4},{6,7},{7,6},{8,9},{9,8},{10,11... | collective-permute-start | bytes 393224 | tf_op jit(solution)/shard_map/ppermute | solution.py:24
  42.7 6.1 %collective-permute-start.13 = (bf16[144,128]{1,0:T(8,128)(2,1)S(1)}, bf16[144,128]{1,0:T(8,128)(2,1)S(1)}, u32[]{:S(2)}, u32[]{:S(2)}) collective-permute-start(bf16[144,128]{1,0:T(8,128)(2,1)S(1)} %kept.1.refs_0_), channel_id=1, source_target_pairs={{0,24},{4,28},{8,16},{12,20},{16,8},{20,12},{24,0},{28,4},{1,25},{... | collective-permute-start | bytes 110600 | tf_op jit(solution)/shard_map/ppermute | solution.py:24
  46.1 4.1 %collective-permute-start.14 = (bf16[144,128]{1,0:T(8,128)(2,1)S(1)}, bf16[144,128]{1,0:T(8,128)(2,1)S(1)}, u32[]{:S(2)}, u32[]{:S(2)}) collective-permute-start(bf16[144,128]{1,0:T(8,128)(2,1)S(1)} %kept.1.refs_0_), channel_id=1, source_target_pairs={{0,16},{4,20},{8,24},{12,28},{16,0},{20,4},{24,8},{28,12},{1,17},{... | collective-permute-start | bytes 110600 | tf_op jit(solution)/shard_map/ppermute | solution.py:24
  46.1 4.1 %collective-permute-start.15 = (bf16[144,128]{1,0:T(8,128)(2,1)S(1)}, bf16[144,128]{1,0:T(8,128)(2,1)S(1)}, u32[]{:S(2)}, u32[]{:S(2)}) collective-permute-start(bf16[144,128]{1,0:T(8,128)(2,1)S(1)} %kept.1.refs_0_), channel_id=1, source_target_pairs={{0,8},{4,12},{8,0},{12,4},{16,24},{20,28},{24,16},{28,20},{1,9},{5... | collective-permute-start | bytes 110600 | tf_op jit(solution)/shard_map/ppermute | solution.py:24
  50.3 4.5 %collective-permute-start.16 = (bf16[576,128]{1,0:T(8,128)(2,1)S(1)}, bf16[576,128]{1,0:T(8,128)(2,1)S(1)}, u32[]{:S(2)}, u32[]{:S(2)}) collective-permute-start(bf16[576,128]{1,0:T(8,128)(2,1)S(1)} %join.5.group), channel_id=1, source_target_pairs={{0,4},{4,0},{8,12},{12,8},{16,20},{20,16},{24,28},{28,24},{1,5},{5... | collective-permute-start | bytes 442376 | tf_op jit(solution)/shard_map/ppermute | solution.py:24

commit v15 on v14

--- a/solution.py
+++ b/solution.py
@@ -218,29 +218,24 @@
 
 
 def kept_kernel(per_row, order, *refs):
-    slopes, (wide, xg, fbk, slot_row, out, s) = refs[:-6], refs[-6:]
-    cap = slot_row.shape[1]
+    slopes, (wide, xg, fbk, slot_row, after, out, s) = refs[:-7], refs[-7:]
     stack(slopes, order, s)
     total = wide[...] + jnp.dot(xg[...], s[...], preferred_element_type=jnp.float32)
     value = pick_columns(total, as_column(slot_row[...])[:, 0:1] % per_row) + fbk[...]
-    out[:cap, :] = value.astype(jnp.bfloat16)
-    tail = out.shape[0] - cap
-    number = jnp.broadcast_to(slot_row[...], (tail, cap))
-    line = lax.broadcasted_iota(jnp.int32, (tail, cap), 0)
-    number = jnp.where(line == 0, number // LANES, number % LANES)
-    out[cap:, :] = number.astype(jnp.float32).astype(jnp.bfloat16)
-
-
-def kept(slopes, order, wide, xg, fbk, slot_row):
+    out[...] = value.astype(jnp.bfloat16)
+
+
+def kept(slopes, order, wide, xg, fbk, slot_row, after):
     cap, kw = wide.shape
     return pl.pallas_call(
         functools.partial(kept_kernel, kw // LANES, order),
-        out_shape=jax.ShapeDtypeStruct((cap + 16, LANES), jnp.bfloat16),
+        out_shape=jax.ShapeDtypeStruct((cap, LANES), jnp.bfloat16),
+        in_specs=[VMEM] * (len(slopes) + 4) + [ANY],
         scratch_shapes=[pltpu.VMEM((xg.shape[1], kw), jnp.bfloat16)],
         compiler_params=params(8),
         cost_estimate=BRIEF,
         name="kept",
-    )(*slopes, wide, xg, fbk, slot_row)
+    )(*slopes, wide, xg, fbk, slot_row, after)
 
 
 def send_out(held, out, sems, t, tile):
@@ -309,68 +304,108 @@
     )(*parts, *after)
 
 
-def spread(group, wide, lines, cap, per_row):
-    size = cap + 16
-    for k in range(group.shape[0] // size):
-        start = k * size
-        tail = group[start + cap : start + size, :].astype(jnp.float32)
-        number = (tail[0:1, :] * LANES + tail[1:2, :]).astype(jnp.int32)
-        lines[:, k * cap : (k + 1) * cap] = jnp.broadcast_to(number // per_row, (8, cap))
-        column = jnp.broadcast_to((number % per_row).astype(jnp.float32), (LANES, cap)).T
-        value = group[start : start + cap, :].astype(jnp.float32)
-        for c in range(per_row):
-            wide[k * cap : (k + 1) * cap, c * LANES : (c + 1) * LANES] = jnp.where(
-                column == c, value, 0.0
-            ).astype(jnp.bfloat16)
-
-
-def place(lines, wide, t, tile):
-    line = lax.broadcasted_iota(jnp.int32, (tile, lines.shape[1]), 0) + t * tile
-    hot = (lines[0:1, :] == line).astype(jnp.float32).astype(jnp.bfloat16)
-    return jnp.dot(hot, wide[...], preferred_element_type=jnp.float32)
-
-
-def half_kernel(cap, per_row, tile, group, out, wide, lines):
-    spread(group, wide, lines, cap, per_row)
+def number_kernel(row, after, out):
+    out[...] = row[...]
+
+
+def number(row, after):
+    return pl.pallas_call(
+        number_kernel,
+        out_shape=jax.ShapeDtypeStruct(row.shape, row.dtype),
+        in_specs=[VMEM, ANY],
+        compiler_params=params(4),
+        cost_estimate=BRIEF,
+        name="number",
+    )(row, after)
+
+
+def places_kernel(per_row, tile, order, numbers, after, *refs):
+    hots, columns, (token, lines) = refs[:2], refs[2:4], refs[4:]
+    token[...] = jnp.zeros_like(token)
+    cap = numbers.shape[1]
+    rep = lax.axis_index("rep")
+    for core in range(2):
+        for k, d in enumerate(order):
+            row = numbers[pl.ds(rep ^ d ^ core, 1), :]
+            lines[:, k * cap : (k + 1) * cap] = jnp.broadcast_to(row // per_row, (8, cap))
+            column = as_column(row % per_row).astype(jnp.float32)
+            columns[core][k * cap : (k + 1) * cap, :] = column.astype(jnp.bfloat16)
+        for t in range(hots[core].shape[0] // tile):
+            line = lax.broadcasted_iota(jnp.int32, (tile, lines.shape[1]), 0) + t * tile
+            hot = (lines[0:1, :] == line).astype(jnp.float32).astype(jnp.bfloat16)
+            hots[core][t * tile : (t + 1) * tile, :] = hot
+
+
+def places(numbers, order, depth, per_row, after):
+    cap = numbers.shape[1]
+    slots = len(order) * cap
+    return pl.pallas_call(
+        functools.partial(places_kernel, per_row, min(depth, 256), order),
+        out_shape=[jax.ShapeDtypeStruct((depth, slots), jnp.bfloat16)] * 2
+        + [jax.ShapeDtypeStruct((slots, LANES), jnp.bfloat16)] * 2
+        + [TOKEN],
+        in_specs=[VMEM, ANY],
+        scratch_shapes=[pltpu.VMEM((8, slots), jnp.int32)],
+        compiler_params=params(14),
+        cost_estimate=BRIEF,
+        name="places",
+    )(numbers, after)
+
+
+def spread(group, columns, wide):
+    column, value = columns[...].astype(jnp.float32), group[...].astype(jnp.float32)
+    for c in range(wide.shape[1] // LANES):
+        wide[:, c * LANES : (c + 1) * LANES] = jnp.where(column == c, value, 0.0).astype(
+            jnp.bfloat16
+        )
+
+
+def half_kernel(tile, group, hot, columns, out, wide):
+    spread(group, columns, wide)
     for t in range(out.shape[0] // tile):
-        out[t * tile : (t + 1) * tile, :] = place(lines, wide, t, tile)
-
-
-def outer_kernel(cap, per_row, tile, n, group, half, out, wide, lines, held, sems):
-    spread(group, wide, lines, cap, per_row)
+        rows = slice(t * tile, (t + 1) * tile)
+        out[rows, :] = jnp.dot(hot[rows, :], wide[...], preferred_element_type=jnp.float32)
+
+
+def outer_kernel(tile, n, group, hot, columns, half, out, wide, held, sems):
+    spread(group, columns, wide)
     tiles = out.shape[0] // tile
     for t in range(tiles):
         rows = slice(t * tile, (t + 1) * tile)
-        held[rows, :] = (half[rows, :] + place(lines, wide, t, tile)) * (1.0 / n)
+        rest = jnp.dot(hot[rows, :], wide[...], preferred_element_type=jnp.float32)
+        held[rows, :] = (half[rows, :] + rest) * (1.0 / n)
         send_out(held, out, sems, t, tile).start()
     for t in range(tiles):
         send_out(held, out, sems, t, tile).wait()
 
 
-def outer(groups, cap, depth, kw):
-    slots = groups[0].shape[0] // (cap + 16) * cap
-    n = 2 * slots // cap
+def outer(groups, hots, columns, kw, n):
+    depth, slots = hots[0].shape
     tile = min(depth, 256)
     shape = jax.ShapeDtypeStruct((depth, kw), jnp.float32)
-    scratch = [pltpu.VMEM((slots, kw), jnp.bfloat16), pltpu.VMEM((8, slots), jnp.int32)]
+    wide = pltpu.VMEM((slots, kw), jnp.bfloat16)
     half = pl.pallas_call(
-        functools.partial(half_kernel, cap, kw // LANES, tile),
+        functools.partial(half_kernel, min(depth, 512)),
         out_shape=shape,
-        scratch_shapes=scratch,
+        scratch_shapes=[wide],
         compiler_params=params(14),
         cost_estimate=BRIEF,
         name="half",
-    )(groups[0])
-    return pl.pallas_call(
-        functools.partial(outer_kernel, cap, kw // LANES, tile, n),
+    )(groups[0], hots[0], columns[0])
+    return pl.pallas_call(
+        functools.partial(outer_kernel, tile, n),
         out_shape=shape,
+        in_specs=[VMEM] * 4,
         out_specs=ANY,
-        scratch_shapes=scratch
-        + [pltpu.VMEM((depth, kw), jnp.float32), pltpu.SemaphoreType.DMA((depth // tile,))],
-        compiler_params=params(14),
+        scratch_shapes=[
+            wide,
+            pltpu.VMEM((depth, kw), jnp.float32),
+            pltpu.SemaphoreType.DMA((depth // tile,)),
+        ],
+        compiler_params=params(16),
         cost_estimate=BRIEF,
         name="outer",
-    )(groups[1], half)
+    )(groups[1], hots[1], columns[1], half)
 
 
 def on_device(inputs, target, weights, feedback, counts, blocks):
@@ -393,7 +428,8 @@
         *out, token = cut(tokens, depth, [(d, low, high - low) for d in near], [token])
         near_out.append(out)
         if low == 0:
-            fbk, keep, token = early(slot_row, counts, fb, token)
+            numbers = lax.all_gather(number(slot_row, token), "rep", axis=0, tiled=True)
+            fbk, keep, token = early(slot_row, counts, fb, numbers)
     near_in = [[swap(x, "shard", n_shard, d) for x, d in zip(out, near)] for out in near_out]
 
     own, _ = cut(tokens, depth, [(0, 0, tok_dev)], [token])
@@ -411,21 +447,23 @@
     xg_near, xt_near, token = prepare(x_near, slot_row, counts, per_row, [products[0]])
     shares = [share[k] for k in range(len(near)) for share in shares]
     slopes = slope(target[0], mine, whole, shares, spans, token)
+    chips = [0, *range(n_rep - 2, 0, -2)]
+    *where, token = places(numbers, chips, depth, per_row, slopes)
     slopes = [slopes] + [swap(slopes, "shard", n_shard, d) for d in far + near]
 
     n_far = 1 + len(far)
     order_far = [(k, 0, tok_dev) for k in range(n_far)]
     order_near = [(k, low, high) for low, high in spans for k in range(len(near))]
     wide = gather(slopes[:n_far], order_far, xg_far)
-    message = kept(slopes[n_far:], order_near, wide, xg_near, fbk, slot_row)
-    same_core = [swap(message, "rep", n_rep, d) for d in range(n_rep - 2, 0, -2)]
+    message = kept(slopes[n_far:], order_near, wide, xg_near, fbk, slot_row, token)
+    same_core = [swap(message, "rep", n_rep, d) for d in chips[1:]]
     order = order_far + [(n_far + k, low, high) for k, low, high in order_near]
     new_feedback, token = residue(slopes, order, [xt_far, xt_near], fb, keep)
     joined, after = message, [token]
     for received in same_core:
         joined, after = join([joined, received], after), []
     groups = [joined, swap(joined, "rep", n_rep, 1)]
-    return outer(groups, message.shape[0] - 16, depth, kw), new_feedback[None]
+    return outer(groups, where[:2], where[2:], kw, n_rep), new_feedback[None]
 
 
 def solution(mesh):

time: 57.5 us -> 57.5 us (level)
  blocking collectives: 0 us -> 13.2 us
  waiting for transfers between devices: 15.8 us -> 5.21 us
  starting transfers between devices: 23.4 us -> 19.7 us
  Pallas kernels: 12.1 us -> 13.2 us
    all_gather x0 -> x1, blocking collectives: none -> 13.2 us  [on_device(): numbers = lax.all_gather(number(slot_row, token), 'rep', axis=0, tiled=True)]
    ppermute x17, waiting for transfers between devices: 15.8 us -> 5.21 us  [swap(): return lax.ppermute(x, axis, [(i, i ^ d) for i in range(n)])]
    ppermute x17, starting transfers between devices: 23.4 us -> 19.7 us  [swap(): return lax.ppermute(x, axis, [(i, i ^ d) for i in range(n)])]
    pallas_call x2 -> x4, Pallas kernels: 3.95 us -> 5.01 us  [the longest x1 2.46 us: outer(): pl.pallas_call(functools.partial(outer_kernel, tile, n), out_shape=shape,...]
  transfers between devices with their start and end apart: 17 -> 17, of which waited for: 9 -> 4; matrix products, arithmetic and copies ran while one was open for 0% -> 0% of each run, Pallas kernels for 16% -> 18%
where the time goes in v15:
time: 57.5 us; the launch traced here: 57.3 us
  starting transfers between devices  19.7 us (34%)
  Pallas kernels  13.2 us (23%)
  blocking collectives  13.2 us (23%)
  waiting for transfers between devices  5.21 us (9%)
  local copies, waits for them, and re-layouts  4.29 us (7%)
  between operations  1.71 us (3%)
    ppermute x17, starting transfers between devices, swap(): return lax.ppermute(x, axis, [(i, i ^ d) for i in range(n)])  19.7 us
    all_gather x1, blocking collectives, on_device(): numbers = lax.all_gather(number(slot_row, token), 'rep', axis=0, tiled=True)  13.2 us
    ppermute x17, waiting for transfers between devices, swap(): return lax.ppermute(x, axis, [(i, i ^ d) for i in range(n)])  5.21 us
    unnamed x14, local copies, waits for them, and re-layouts  3.21 us
    pallas_call x1, Pallas kernels, outer(): pl.pallas_call(functools.partial(outer_kernel, tile, n), out_shape=shape,...  2.46 us
    pallas_call x1, Pallas kernels, residue(): pl.pallas_call(functools.partial(residue_kernel, order, tile), out_shape=...  2.34 us
    pallas_call x3, Pallas kernels, project(): pl.pallas_call(functools.partial(project_kernel, n), out_shape=[jax.Shape...  1.76 us
    pallas_call x2, Pallas kernels, prepare(): pl.pallas_call(functools.partial(prepare_kernel, per_row, len(xs)), out_s...  1.57 us
  transfers between devices with their start and end apart: 17, of which 4 were waited for; matrix products, arithmetic and copies ran while one was open for 0% of the time, Pallas kernels for 18%

profile of v15, /device:TPU:1, one launch (start us, length us, event | category | flops | bytes accessed | tf_op | source)
XLA Modules:
  0.0 57.3 jit_solution(13715732526131725980)
XLA Ops:
  0.6 1.1 %dynamic-slice_bitcast_fusion.refs_0_ = bf16[128,2048]{1,0:T(8,128)(2,1)S(1)} fusion(bf16[1,128,8192]{2,1,0:T(8,128)(2,1)} %param.6, s32[]{:T(128)S(6)} %select_n.3), kind=kLoop, calls=%fused_computation | loop fusion | bytes 1048580 | tf_op jit(solution)/shard_map/dynamic_slice | solution.py:424
  1.7 3.1 %collective-permute-start = (bf16[128,2048]{1,0:T(8,128)(2,1)S(1)}, bf16[128,2048]{1,0:T(8,128)(2,1)S(1)}, u32[]{:S(2)}, u32[]{:S(2)}) collective-permute-start(bf16[128,2048]{1,0:T(8,128)(2,1)S(1)} %dynamic-slice_bitcast_fusion.refs_0_), channel_id=1, source_target_pairs={{0,3},{1,2},{2,1},{3,0},{4,7},{5,6},{6,5},{7,4},{8,11},{9,10},{10,... | collective-permute-start | bytes 1572872 | tf_op jit(solution)/shard_map/ppermute | solution.py:24
  4.8 1.6 %copy-done = bf16[1,128,8192]{2,1,0:T(8,128)(2,1)S(1)} copy-done((bf16[1,128,8192]{2,1,0:T(8,128)(2,1)S(1)}, bf16[1,128,8192]{2,1,0:T(8,128)(2,1)}, u32[]{:S(2)}) %copy-start) | copy-done | bytes 2097176
  7.7 13.2 %all-gather = s32[8,1,128]{2,1,0:T(1,128)S(1)} all-gather(s32[1,1,128]{2,1,0:T(1,128)S(1)} %bitcast.26), channel_id=1, replica_groups=mesh['rep'=8,'shard'=4] {'rep'}, dimensions={0}, use_global_device_ids=true | all-gather | bytes 4608 | tf_op jit(solution)/shard_map/all_gather | solution.py:431
  20.9 1.6 %copy-done.3 = bf16[1,2048,512]{2,1,0:T(8,128)(2,1)S(1)} copy-done((bf16[1,2048,512]{2,1,0:T(8,128)(2,1)S(1)}, bf16[1,2048,512]{2,1,0:T(8,128)(2,1)}, u32[]{:S(2)}) %copy-start.3) | copy-done | bytes 2097176
  22.5 1.1 %early.1 = (f32[128,128]{1,0:T(8,128)S(1)}, bf16[2048,512]{1,0:T(8,128)(2,1)S(1)}, f32[8,128]{1,0:T(8,128)S(1)}) custom-call(s32[1,128]{1,0:T(1,128)S(1)} %bitcast.22, s32[1,1]{1,0:T(1,128)S(6)} %copy.9.count.refs_2_.refs_3_, bf16[2048,512]{1,0:T(8,128)(2,1)S(1)} %bitcast.16, s32[8,128]{1,0:T(8,128)S(1)} %bitcast.19), custom_call_target="tpu_custom_call" | custom-call | flops 1000 | bytes 1000 | tf_op jit(solution)/shard_map/early/pallas_call | solution.py:145
  23.8 1.3 %collective-permute-start.5 = (bf16[32,2048]{1,0:T(8,128)(2,1)S(1)}, bf16[32,2048]{1,0:T(8,128)(2,1)S(1)}, u32[]{:S(2)}, u32[]{:S(2)}) collective-permute-start(bf16[32,2048]{1,0:T(8,128)(2,1)S(1)} %get-tuple-element.45), channel_id=1, source_target_pairs={{0,1},{1,0},{2,3},{3,2},{4,5},{5,4},{6,7},{7,6},{8,9},{9,8},{10,11... | collective-permute-start | bytes 393224 | tf_op jit(solution)/shard_map/ppermute | solution.py:24
  25.1 1.2 %collective-permute-start.6 = (bf16[32,2048]{1,0:T(8,128)(2,1)S(1)}, bf16[32,2048]{1,0:T(8,128)(2,1)S(1)}, u32[]{:S(2)}, u32[]{:S(2)}) collective-permute-start(bf16[32,2048]{1,0:T(8,128)(2,1)S(1)} %get-tuple-element.46), channel_id=1, source_target_pairs={{0,2},{1,3},{2,0},{3,1},{4,6},{5,7},{6,4},{7,5},{8,10},{9,11},{10,... | collective-permute-start | bytes 393224 | tf_op jit(solution)/shard_map/ppermute | solution.py:24
  26.3 0.6 %cut.5 = (bf16[128,2048]{1,0:T(8,128)(2,1)S(1)}, f32[8,128]{1,0:T(8,128)}) custom-call(bf16[128,8192]{1,0:T(8,128)(2,1)S(1)} %bitcast.12, f32[8,128]{1,0:T(8,128)S(1)} %get-tuple-element.36.refs_0_), custom_call_target="tpu_custom_call" | custom-call | flops 1000 | bytes 1000 | tf_op jit(solution)/shard_map/cut/pallas_call | solution.py:43
  27.0 0.7 %project.3 = (f32[128,512]{1,0:T(8,128)S(1)}, bf16[128,512]{1,0:T(8,128)(2,1)S(1)}, bf16[256,2048]{1,0:T(8,128)(2,1)S(1)}) custom-call(bf16[128,2048]{1,0:T(8,128)(2,1)S(1)} %get-tuple-element.37.refs_0_, bf16[128,2048]{1,0:T(8,128)(2,1)S(1)} %collective-permute-done.refs_1_, bf16[2048,512]{1,0:T(8,128)(2,1)S(1)} %bitcast.13), custom_call_target="tpu_custom_call" | custom-call | flops 1000 | bytes 1000 | tf_op jit(solution)/shard_map/project/pallas_call | solution.py:73
  27.7 0.5 collective-permute-start.1
  28.2 0.6 %prepare.2 = (bf16[128,256]{1,0:T(8,128)(2,1)S(1)}, bf16[2048,256]{1,0:T(8,128)(2,1)S(1)}, f32[8,128]{1,0:T(8,128)S(1)}) custom-call(bf16[256,2048]{1,0:T(8,128)(2,1)S(1)} %get-tuple-element.42.refs_0_, s32[1,128]{1,0:T(1,128)S(1)} %bitcast.23, s32[1,1]{1,0:T(1,128)S(6)} %copy.9.count.refs_2_.refs_3_), custom_call_target="tpu_custom_call" | custom-call | flops 1000 | bytes 1000 | tf_op jit(solution)/shard_map/prepare/pallas_call | solution.py:181
  28.8 0.6 %project.4 = (bf16[96,512]{1,0:T(8,128)(2,1)S(1)}, bf16[96,512]{1,0:T(8,128)(2,1)S(1)}, bf16[192,2048]{1,0:T(8,128)(2,1)S(1)}) custom-call(bf16[96,2048]{1,0:T(8,128)(2,1)S(1)} %collective-permute-done.2.refs_0_, bf16[96,2048]{1,0:T(8,128)(2,1)S(1)} %collective-permute-done.3.refs_1_, bf16[2048,512]{1,0:T(8,128)(2,1)S(1)} %bitcast.14, ...), custom_call_target="tpu_custom_call" | custom-call | flops 1000 | bytes 1000 | tf_op jit(solution)/shard_map/project/pallas_call | solution.py:73
  29.4 1.0 %collective-permute-start.4 = (bf16[96,512]{1,0:T(8,128)(2,1)S(1)}, bf16[96,512]{1,0:T(8,128)(2,1)S(1)}, u32[]{:S(2)}, u32[]{:S(2)}) collective-permute-start(bf16[96,512]{1,0:T(8,128)(2,1)S(1)} %get-tuple-element.44), channel_id=1, source_target_pairs={{0,1},{1,0},{2,3},{3,2},{4,5},{5,4},{6,7},{7,6},{8,9},{9,8},{10,11... | collective-permute-start | bytes 294920 | tf_op jit(solution)/shard_map/ppermute | solution.py:24
  30.5 1.2 %collective-permute-start.8 = (bf16[96,512]{1,0:T(8,128)(2,1)S(1)}, bf16[96,512]{1,0:T(8,128)(2,1)S(1)}, u32[]{:S(2)}, u32[]{:S(2)}) collective-permute-start(bf16[96,512]{1,0:T(8,128)(2,1)S(1)} %get-tuple-element.47.refs_3_), channel_id=1, source_target_pairs={{0,2},{1,3},{2,0},{3,1},{4,6},{5,7},{6,4},{7,5},{8,10},{9,11},{10,... | collective-permute-start | bytes 294920 | tf_op jit(solution)/shard_map/ppermute | solution.py:24
  31.7 0.5 project.5
  32.5 0.5 collective-permute-start.7
  33.0 0.9 %prepare.3 = (bf16[128,256]{1,0:T(8,128)(2,1)S(1)}, bf16[2048,256]{1,0:T(8,128)(2,1)S(1)}, f32[8,128]{1,0:T(8,128)S(1)}) custom-call(bf16[192,2048]{1,0:T(8,128)(2,1)S(1)} %get-tuple-element.50.refs_0_, bf16[64,2048]{1,0:T(8,128)(2,1)S(1)} %get-tuple-element.51.refs_1_, s32[1,128]{1,0:T(1,128)S(1)} %bitcast.24, s32[1,1]{1,0:T(1,128)S(6)} %copy.9.count.refs_2_.refs_3_, ...), custom_call_target="tpu_custom_call" | custom-call | flops 1000 | bytes 1000 | tf_op jit(solution)/shard_map/prepare/pallas_call | solution.py:181
  33.9 2.2 %collective-permute-done.9.refs_6_ = bf16[32,512]{1,0:T(8,128)(2,1)S(1)} collective-permute-done((bf16[32,512]{1,0:T(8,128)(2,1)S(1)}, bf16[32,512]{1,0:T(8,128)(2,1)S(1)}, u32[]{:S(2)}, u32[]{:S(2)}) %collective-permute-start.9) | collective-permute-done | bytes 32800 | tf_op jit(solution)/shard_map/ppermute | solution.py:24
  36.2 1.0 %collective-permute-start.12 = (bf16[128,512]{1,0:T(8,128)(2,1)S(1)}, bf16[128,512]{1,0:T(8,128)(2,1)S(1)}, u32[]{:S(2)}, u32[]{:S(2)}) collective-permute-start(bf16[128,512]{1,0:T(8,128)(2,1)S(1)} %slope.1.refs_0_.after), channel_id=1, source_target_pairs={{0,3},{1,2},{2,1},{3,0},{4,7},{5,6},{6,5},{7,4},{8,11},{9,10},{10,... | collective-permute-start | bytes 393224 | tf_op jit(solution)/shard_map/ppermute | solution.py:24
  37.2 0.5 collective-permute-start.11
  37.7 1.2 %collective-permute-start.10 = (bf16[128,512]{1,0:T(8,128)(2,1)S(1)}, bf16[128,512]{1,0:T(8,128)(2,1)S(1)}, u32[]{:S(2)}, u32[]{:S(2)}) collective-permute-start(bf16[128,512]{1,0:T(8,128)(2,1)S(1)} %slope.1.refs_0_.after), channel_id=1, source_target_pairs={{0,1},{1,0},{2,3},{3,2},{4,5},{5,4},{6,7},{7,6},{8,9},{9,8},{10,11... | collective-permute-start | bytes 393224 | tf_op jit(solution)/shard_map/ppermute | solution.py:24
  39.0 1.2 %places.1 = (bf16[2048,512]{1,0:T(8,128)(2,1)S(1)}, bf16[2048,512]{1,0:T(8,128)(2,1)S(1)}, bf16[512,128]{1,0:T(8,128)(2,1)S(1)}, bf16[512,128]{1,0:T(8,128)(2,1)S(1)}, f32[8,128]{1,0:T(8,128)S(1)}) custom-call(s32[8,128]{1,0:T(8,128)S(1)} %bitcast.20, bf16[128,512]{1,0:T(8,128)(2,1)S(1)} %slope.1.refs_0_.after), custom_call_target="tpu_custom_call" | custom-call | flops 1000 | bytes 1000 | tf_op jit(solution)/shard_map/places/pallas_call | solution.py:342
  40.2 0.9 %collective-permute-done.12.refs_1_ = bf16[128,512]{1,0:T(8,128)(2,1)S(1)} collective-permute-done((bf16[128,512]{1,0:T(8,128)(2,1)S(1)}, bf16[128,512]{1,0:T(8,128)(2,1)S(1)}, u32[]{:S(2)}, u32[]{:S(2)}) %collective-permute-start.12) | collective-permute-done | bytes 131104 | tf_op jit(solution)/shard_map/ppermute | solution.py:24
  41.3 1.1 %collective-permute-done.11.refs_1_.refs_3_ = bf16[128,512]{1,0:T(8,128)(2,1)S(1)} collective-permute-done((bf16[128,512]{1,0:T(8,128)(2,1)S(1)}, bf16[128,512]{1,0:T(8,128)(2,1)S(1)}, u32[]{:S(2)}, u32[]{:S(2)}) %collective-permute-start.11) | collective-permute-done | bytes 131104 | tf_op jit(solution)/shard_map/ppermute | solution.py:24
  42.7 3.4 %collective-permute-start.13 = (bf16[128,128]{1,0:T(8,128)(2,1)S(1)}, bf16[128,128]{1,0:T(8,128)(2,1)S(1)}, u32[]{:S(2)}, u32[]{:S(2)}) collective-permute-start(bf16[128,128]{1,0:T(8,128)(2,1)S(1)} %kept.1.refs_0_), channel_id=1, source_target_pairs={{0,24},{4,28},{8,16},{12,20},{16,8},{20,12},{24,0},{28,4},{1,25},{... | collective-permute-start | bytes 98312 | tf_op jit(solution)/shard_map/ppermute | solution.py:24
  46.1 0.4 collective-permute-start.15
  46.5 2.3 %residue.1 = (bf16[2048,512]{1,0:T(8,128)(2,1)}, f32[8,128]{1,0:T(8,128)S(1)}) custom-call(bf16[128,512]{1,0:T(8,128)(2,1)S(1)} %slope.1.refs_0_.after, bf16[128,512]{1,0:T(8,128)(2,1)S(1)} %collective-permute-done.12.refs_1_, bf16[128,512]{1,0:T(8,128)(2,1)S(1)} %collective-permute-done.10.refs_0_.refs_2_, ...), custom_call_target="tpu_custom_call" | custom-call | flops 1000 | bytes 1000 | tf_op jit(solution)/shard_map/residue/pallas_call | solution.py:269
  48.9 0.9 %collective-permute-done.14.refs_1_ = bf16[128,128]{1,0:T(8,128)(2,1)S(1)} collective-permute-done((bf16[128,128]{1,0:T(8,128)(2,1)S(1)}, bf16[128,128]{1,0:T(8,128)(2,1)S(1)}, u32[]{:S(2)}, u32[]{:S(2)}) %collective-permute-start.14) | collective-permute-done | bytes 32800 | tf_op jit(solution)/shard_map/ppermute | solution.py:24
  49.8 3.7 %collective-permute-start.16 = (bf16[512,128]{1,0:T(8,128)(2,1)S(1)}, bf16[512,128]{1,0:T(8,128)(2,1)S(1)}, u32[]{:S(2)}, u32[]{:S(2)}) collective-permute-start(bf16[512,128]{1,0:T(8,128)(2,1)S(1)} %join.5.group), channel_id=1, source_target_pairs={{0,4},{4,0},{8,12},{12,8},{16,20},{20,16},{24,28},{28,24},{1,5},{5... | collective-permute-start | bytes 393224 | tf_op jit(solution)/shard_map/ppermute | solution.py:24
  53.5 1.3 %half.1 = f32[2048,512]{1,0:T(8,128)S(1)} custom-call(bf16[512,128]{1,0:T(8,128)(2,1)S(1)} %join.5.group, bf16[2048,512]{1,0:T(8,128)(2,1)S(1)} %get-tuple-element.63.hot, bf16[512,128]{1,0:T(8,128)(2,1)S(1)} %get-tuple-element.64.columns), custom_call_target="tpu_custom_call" | custom-call | flops 1000 | bytes 1000 | tf_op jit(solution)/shard_map/half/pallas_call | solution.py:387
  54.8 2.5 %outer.1 = f32[2048,512]{1,0:T(8,128)} custom-call(bf16[512,128]{1,0:T(8,128)(2,1)S(1)} %collective-permute-done.16.group, bf16[2048,512]{1,0:T(8,128)(2,1)S(1)} %get-tuple-element.61.hot, bf16[512,128]{1,0:T(8,128)(2,1)S(1)} %get-tuple-element.62.columns, f32[2048,512]{1,0:T(8,128)S(1)} %half.1), custom_call_target="tpu_custom_call" | custom-call | flops 1000 | bytes 1000 | tf_op jit(solution)/shard_map/outer/pallas_call | solution.py:395
  (38 shorter events, 1.5 us)
Async XLA Ops:
  0.6 6.2 %copy-start.6 = (s32[1,1,128]{2,1,0:T(1,128)S(1)}, s32[1,1,128]{2,1,0:T(1,128)}, u32[]{:S(2)}) copy-start(s32[1,1,128]{2,1,0:T(1,128)} %param.11) | copy-start | bytes 1540
  1.7 25.2 %collective-permute-start = (bf16[128,2048]{1,0:T(8,128)(2,1)S(1)}, bf16[128,2048]{1,0:T(8,128)(2,1)S(1)}, u32[]{:S(2)}, u32[]{:S(2)}) collective-permute-start(bf16[128,2048]{1,0:T(8,128)(2,1)S(1)} %dynamic-slice_bitcast_fusion.refs_0_), channel_id=1, source_target_pairs={{0,3},{1,2},{2,1},{3,0},{4,7},{5,6},{6,5},{7,4},{8,11},{9,10},{10,... | collective-permute-start | bytes 1572872 | tf_op jit(solution)/shard_map/ppermute | solution.py:24
  4.8 1.6 %copy-start = (bf16[1,128,8192]{2,1,0:T(8,128)(2,1)S(1)}, bf16[1,128,8192]{2,1,0:T(8,128)(2,1)}, u32[]{:S(2)}) copy-start(bf16[1,128,8192]{2,1,0:T(8,128)(2,1)} %param.6) | copy-start | bytes 6291460
  6.4 17.2 %copy-start.1 = (bf16[1,128,8192]{2,1,0:T(8,128)(2,1)S(1)}, bf16[1,128,8192]{2,1,0:T(8,128)(2,1)}, u32[]{:S(2)}) copy-start(bf16[1,128,8192]{2,1,0:T(8,128)(2,1)} %param.6) | copy-start | bytes 6291460
  6.5 22.3 %collective-permute-start.2 = (bf16[96,2048]{1,0:T(8,128)(2,1)S(1)}, bf16[96,2048]{1,0:T(8,128)(2,1)S(1)}, u32[]{:S(2)}, u32[]{:S(2)}) collective-permute-start(bf16[96,2048]{1,0:T(8,128)(2,1)S(1)} %get-tuple-element.40), channel_id=1, source_target_pairs={{0,1},{1,0},{2,3},{3,2},{4,5},{5,4},{6,7},{7,6},{8,9},{9,8},{10,11... | collective-permute-start | bytes 1179656 | tf_op jit(solution)/shard_map/ppermute | solution.py:24
  6.8 22.0 %collective-permute-start.3 = (bf16[96,2048]{1,0:T(8,128)(2,1)S(1)}, bf16[96,2048]{1,0:T(8,128)(2,1)S(1)}, u32[]{:S(2)}, u32[]{:S(2)}) collective-permute-start(bf16[96,2048]{1,0:T(8,128)(2,1)S(1)} %get-tuple-element.41), channel_id=1, source_target_pairs={{0,2},{1,3},{2,0},{3,1},{4,6},{5,7},{6,4},{7,5},{8,10},{9,11},{10,... | collective-permute-start | bytes 1179656 | tf_op jit(solution)/shard_map/ppermute | solution.py:24
  20.9 1.6 %copy-start.3 = (bf16[1,2048,512]{2,1,0:T(8,128)(2,1)S(1)}, bf16[1,2048,512]{2,1,0:T(8,128)(2,1)}, u32[]{:S(2)}) copy-start(bf16[1,2048,512]{2,1,0:T(8,128)(2,1)} %param.9) | copy-start | bytes 6291460
  23.6 3.3 %copy-start.2 = (bf16[1,2048,512]{2,1,0:T(8,128)(2,1)S(1)}, bf16[1,2048,512]{2,1,0:T(8,128)(2,1)}, u32[]{:S(2)}) copy-start(bf16[1,2048,512]{2,1,0:T(8,128)(2,1)} %param.8) | copy-start | bytes 6291460
  23.8 7.9 %collective-permute-start.5 = (bf16[32,2048]{1,0:T(8,128)(2,1)S(1)}, bf16[32,2048]{1,0:T(8,128)(2,1)S(1)}, u32[]{:S(2)}, u32[]{:S(2)}) collective-permute-start(bf16[32,2048]{1,0:T(8,128)(2,1)S(1)} %get-tuple-element.45), channel_id=1, source_target_pairs={{0,1},{1,0},{2,3},{3,2},{4,5},{5,4},{6,7},{7,6},{8,9},{9,8},{10,11... | collective-permute-start | bytes 393224 | tf_op jit(solution)/shard_map/ppermute | solution.py:24
  25.1 6.6 %collective-permute-start.6 = (bf16[32,2048]{1,0:T(8,128)(2,1)S(1)}, bf16[32,2048]{1,0:T(8,128)(2,1)S(1)}, u32[]{:S(2)}, u32[]{:S(2)}) collective-permute-start(bf16[32,2048]{1,0:T(8,128)(2,1)S(1)} %get-tuple-element.46), channel_id=1, source_target_pairs={{0,2},{1,3},{2,0},{3,1},{4,6},{5,7},{6,4},{7,5},{8,10},{9,11},{10,... | collective-permute-start | bytes 393224 | tf_op jit(solution)/shard_map/ppermute | solution.py:24
  27.7 8.5 %collective-permute-start.1 = (bf16[128,512]{1,0:T(8,128)(2,1)S(1)}, bf16[128,512]{1,0:T(8,128)(2,1)S(1)}, u32[]{:S(2)}, u32[]{:S(2)}) collective-permute-start(bf16[128,512]{1,0:T(8,128)(2,1)S(1)} %get-tuple-element.39), channel_id=1, source_target_pairs={{0,3},{1,2},{2,1},{3,0},{4,7},{5,6},{6,5},{7,4},{8,11},{9,10},{10,... | collective-permute-start | bytes 393224 | tf_op jit(solution)/shard_map/ppermute | solution.py:24
  29.4 6.7 %copy-start.5 = (bf16[1,128,512]{2,1,0:T(8,128)(2,1)S(1)}, bf16[1,128,512]{2,1,0:T(8,128)(2,1)}, u32[]{:S(2)}) copy-start(bf16[1,128,512]{2,1,0:T(8,128)(2,1)} %param.7) | copy-start | bytes 393220
  29.4 6.7 %collective-permute-start.4 = (bf16[96,512]{1,0:T(8,128)(2,1)S(1)}, bf16[96,512]{1,0:T(8,128)(2,1)S(1)}, u32[]{:S(2)}, u32[]{:S(2)}) collective-permute-start(bf16[96,512]{1,0:T(8,128)(2,1)S(1)} %get-tuple-element.44), channel_id=1, source_target_pairs={{0,1},{1,0},{2,3},{3,2},{4,5},{5,4},{6,7},{7,6},{8,9},{9,8},{10,11... | collective-permute-start | bytes 294920 | tf_op jit(solution)/shard_map/ppermute | solution.py:24
  30.5 5.7 %collective-permute-start.8 = (bf16[96,512]{1,0:T(8,128)(2,1)S(1)}, bf16[96,512]{1,0:T(8,128)(2,1)S(1)}, u32[]{:S(2)}, u32[]{:S(2)}) collective-permute-start(bf16[96,512]{1,0:T(8,128)(2,1)S(1)} %get-tuple-element.47.refs_3_), channel_id=1, source_target_pairs={{0,2},{1,3},{2,0},{3,1},{4,6},{5,7},{6,4},{7,5},{8,10},{9,11},{10,... | collective-permute-start | bytes 294920 | tf_op jit(solution)/shard_map/ppermute | solution.py:24
  32.2 14.3 %copy-start.4 = (bf16[1,2048,512]{2,1,0:T(8,128)(2,1)S(1)}, bf16[1,2048,512]{2,1,0:T(8,128)(2,1)}, u32[]{:S(2)}) copy-start(bf16[1,2048,512]{2,1,0:T(8,128)(2,1)} %param.9) | copy-start | bytes 6291460
  32.2 3.9 %collective-permute-start.9 = (bf16[32,512]{1,0:T(8,128)(2,1)S(1)}, bf16[32,512]{1,0:T(8,128)(2,1)S(1)}, u32[]{:S(2)}, u32[]{:S(2)}) collective-permute-start(bf16[32,512]{1,0:T(8,128)(2,1)S(1)} %get-tuple-element.49), channel_id=1, source_target_pairs={{0,2},{1,3},{2,0},{3,1},{4,6},{5,7},{6,4},{7,5},{8,10},{9,11},{10,... | collective-permute-start | bytes 98312 | tf_op jit(solution)/shard_map/ppermute | solution.py:24
  32.5 3.6 %collective-permute-start.7 = (bf16[32,512]{1,0:T(8,128)(2,1)S(1)}, bf16[32,512]{1,0:T(8,128)(2,1)S(1)}, u32[]{:S(2)}, u32[]{:S(2)}) collective-permute-start(bf16[32,512]{1,0:T(8,128)(2,1)S(1)} %get-tuple-element.48.refs_4_), channel_id=1, source_target_pairs={{0,1},{1,0},{2,3},{3,2},{4,5},{5,4},{6,7},{7,6},{8,9},{9,8},{10,11... | collective-permute-start | bytes 98312 | tf_op jit(solution)/shard_map/ppermute | solution.py:24
  36.2 4.9 %collective-permute-start.12 = (bf16[128,512]{1,0:T(8,128)(2,1)S(1)}, bf16[128,512]{1,0:T(8,128)(2,1)S(1)}, u32[]{:S(2)}, u32[]{:S(2)}) collective-permute-start(bf16[128,512]{1,0:T(8,128)(2,1)S(1)} %slope.1.refs_0_.after), channel_id=1, source_target_pairs={{0,3},{1,2},{2,1},{3,0},{4,7},{5,6},{6,5},{7,4},{8,11},{9,10},{10,... | collective-permute-start | bytes 393224 | tf_op jit(solution)/shard_map/ppermute | solution.py:24
  37.2 5.2 %collective-permute-start.11 = (bf16[128,512]{1,0:T(8,128)(2,1)S(1)}, bf16[128,512]{1,0:T(8,128)(2,1)S(1)}, u32[]{:S(2)}, u32[]{:S(2)}) collective-permute-start(bf16[128,512]{1,0:T(8,128)(2,1)S(1)} %slope.1.refs_0_.after), channel_id=1, source_target_pairs={{0,2},{1,3},{2,0},{3,1},{4,6},{5,7},{6,4},{7,5},{8,10},{9,11},{10,... | collective-permute-start | bytes 393224 | tf_op jit(solution)/shard_map/ppermute | solution.py:24
  37.7 4.7 %collective-permute-start.10 = (bf16[128,512]{1,0:T(8,128)(2,1)S(1)}, bf16[128,512]{1,0:T(8,128)(2,1)S(1)}, u32[]{:S(2)}, u32[]{:S(2)}) collective-permute-start(bf16[128,512]{1,0:T(8,128)(2,1)S(1)} %slope.1.refs_0_.after), channel_id=1, source_target_pairs={{0,1},{1,0},{2,3},{3,2},{4,5},{5,4},{6,7},{7,6},{8,9},{9,8},{10,11... | collective-permute-start | bytes 393224 | tf_op jit(solution)/shard_map/ppermute | solution.py:24
  42.7 6.1 %collective-permute-start.13 = (bf16[128,128]{1,0:T(8,128)(2,1)S(1)}, bf16[128,128]{1,0:T(8,128)(2,1)S(1)}, u32[]{:S(2)}, u32[]{:S(2)}) collective-permute-start(bf16[128,128]{1,0:T(8,128)(2,1)S(1)} %kept.1.refs_0_), channel_id=1, source_target_pairs={{0,24},{4,28},{8,16},{12,20},{16,8},{20,12},{24,0},{28,4},{1,25},{... | collective-permute-start | bytes 98312 | tf_op jit(solution)/shard_map/ppermute | solution.py:24
  46.1 3.7 %collective-permute-start.14 = (bf16[128,128]{1,0:T(8,128)(2,1)S(1)}, bf16[128,128]{1,0:T(8,128)(2,1)S(1)}, u32[]{:S(2)}, u32[]{:S(2)}) collective-permute-start(bf16[128,128]{1,0:T(8,128)(2,1)S(1)} %kept.1.refs_0_), channel_id=1, source_target_pairs={{0,16},{4,20},{8,24},{12,28},{16,0},{20,4},{24,8},{28,12},{1,17},{... | collective-permute-start | bytes 98312 | tf_op jit(solution)/shard_map/ppermute | solution.py:24
  46.1 3.7 %collective-permute-start.15 = (bf16[128,128]{1,0:T(8,128)(2,1)S(1)}, bf16[128,128]{1,0:T(8,128)(2,1)S(1)}, u32[]{:S(2)}, u32[]{:S(2)}) collective-permute-start(bf16[128,128]{1,0:T(8,128)(2,1)S(1)} %kept.1.refs_0_), channel_id=1, source_target_pairs={{0,8},{4,12},{8,0},{12,4},{16,24},{20,28},{24,16},{28,20},{1,9},{5... | collective-permute-start | bytes 98312 | tf_op jit(solution)/shard_map/ppermute | solution.py:24
  49.8 5.0 %collective-permute-start.16 = (bf16[512,128]{1,0:T(8,128)(2,1)S(1)}, bf16[512,128]{1,0:T(8,128)(2,1)S(1)}, u32[]{:S(2)}, u32[]{:S(2)}) collective-permute-start(bf16[512,128]{1,0:T(8,128)(2,1)S(1)} %join.5.group), channel_id=1, source_target_pairs={{0,4},{4,0},{8,12},{12,8},{16,20},{20,16},{24,28},{28,24},{1,5},{5... | collective-permute-start | bytes 393224 | tf_op jit(solution)/shard_map/ppermute | solution.py:24

commit v16 on v9

--- a/solution.py
+++ b/solution.py
@@ -93,13 +93,14 @@
         for product in shares[part :: len(spans)]:
             key_proj += product[...].astype(jnp.float32)
         gap = key_proj - goal[low:high, :].astype(jnp.float32)
-        out[low:high, :] = (gap / tok_dev).astype(jnp.bfloat16)
-
-
-def slope(goal, mine, whole, shares, spans, after):
+        for k in range(out.shape[0]):
+            out[k, low:high, :] = (gap / tok_dev).astype(jnp.bfloat16)
+
+
+def slope(goal, mine, whole, shares, spans, after, copies):
     return pl.pallas_call(
         functools.partial(slope_kernel, goal.shape[0], len(whole), spans),
-        out_shape=jax.ShapeDtypeStruct(mine.shape, jnp.bfloat16),
+        out_shape=jax.ShapeDtypeStruct((copies, *mine.shape), jnp.bfloat16),
         in_specs=[VMEM] * (2 + len(whole) + len(shares)) + [ANY],
         compiler_params=params(8),
         cost_estimate=BRIEF,
@@ -254,7 +255,7 @@
 
 def residue(s, xts, fb, keep):
     depth, kw = fb.shape
-    tile = min(depth, 512)
+    tile = min(depth, 256)
     return pl.pallas_call(
         functools.partial(residue_kernel, tile),
         out_shape=[jax.ShapeDtypeStruct((depth, kw), jnp.bfloat16), TOKEN],
@@ -321,7 +322,7 @@
     tiles = out.shape[0] // tile
     for t in range(tiles):
         rows = slice(t * tile, (t + 1) * tile)
-        held[rows, :] = (half[rows, :] + place(lines, wide, t, tile)) / n
+        held[rows, :] = (half[rows, :] + place(lines, wide, t, tile)) * (1.0 / n)
         send_out(held, out, sems, t, tile).start()
     for t in range(tiles):
         send_out(held, out, sems, t, tile).wait()
@@ -330,7 +331,7 @@
 def outer(groups, cap, depth, kw):
     slots = groups[0].shape[0] // (cap + 16) * cap
     n = 2 * slots // cap
-    tile = min(depth, 512)
+    tile = min(depth, 256)
     shape = jax.ShapeDtypeStruct((depth, kw), jnp.float32)
     scratch = [pltpu.VMEM((slots, kw), jnp.bfloat16), pltpu.VMEM((8, slots), jnp.int32)]
     half = pl.pallas_call(
@@ -390,8 +391,8 @@
         after = products[-1:]
     xg_near, xt_near, token = prepare(x_near, slot_row, counts, per_row, [products[0]])
     shares = [share[k] for k in range(len(near)) for share in shares]
-    slopes = slope(target[0], mine, whole, shares, spans, token)
-    slopes = lax.all_gather(slopes, "shard", axis=0, tiled=True)
+    slopes = slope(target[0], mine, whole, shares, spans, token, n_shard)
+    slopes = lax.all_to_all(slopes, "shard", 0, 0).reshape(-1, kw)
 
     order = [(d, 0, tok_dev) for d in [0] + far]
     order += [(d, low, high) for low, high in spans for d in near]

time: 60.4 us -> 60 us (level)
  starting transfers between devices: 23.4 us -> 22 us
  blocking collectives: 8.19 us -> 9.17 us
    all_to_all x0 -> x1, blocking collectives: none -> 9.17 us  [on_device(): slopes = lax.all_to_all(slopes, 'shard', 0, 0).reshape(-1, kw)]
    all_gather x1 -> x0, blocking collectives: 8.19 us -> none  [on_device(): slopes = lax.all_gather(slopes, 'shard', axis=0, tiled=True)]
    ppermute x14, starting transfers between devices: 23.4 us -> 22 us  [swap(): return lax.ppermute(x, axis, [(i, i ^ d) for i in range(n)])]
where the time goes in v16:
time: 60 us; the launch traced here: 59.7 us
  starting transfers between devices  22 us (37%)
  Pallas kernels  12 us (20%)
  waiting for transfers between devices  10.6 us (18%)
  blocking collectives  9.17 us (15%)
  local copies, waits for them, and re-layouts  4.28 us (7%)
  between operations  1.68 us (3%)
    ppermute x14, starting transfers between devices, swap(): return lax.ppermute(x, axis, [(i, i ^ d) for i in range(n)])  22 us
    ppermute x14, waiting for transfers between devices, swap(): return lax.ppermute(x, axis, [(i, i ^ d) for i in range(n)])  10.6 us
    all_to_all x1, blocking collectives, on_device(): slopes = lax.all_to_all(slopes, 'shard', 0, 0).reshape(-1, kw)  9.17 us
    unnamed x14, local copies, waits for them, and re-layouts  3.2 us
    pallas_call x1, Pallas kernels, outer(): pl.pallas_call(functools.partial(outer_kernel, cap, kw // LANES, tile, n)...  2.54 us
    pallas_call x1, Pallas kernels, residue(): pl.pallas_call(functools.partial(residue_kernel, tile), out_shape=[jax.Sh...  2.38 us
    pallas_call x3, Pallas kernels, project(): pl.pallas_call(functools.partial(project_kernel, n), out_shape=[jax.Shape...  1.76 us
    pallas_call x2, Pallas kernels, prepare(): pl.pallas_call(functools.partial(prepare_kernel, per_row, len(xs)), out_s...  1.55 us
  transfers between devices with their start and end apart: 14, of which 6 were waited for; matrix products, arithmetic and copies ran while one was open for 0% of the time, Pallas kernels for 15%

profile of v16, /device:TPU:1, one launch (start us, length us, event | category | flops | bytes accessed | tf_op | source)
XLA Modules:
  0.0 59.7 jit_solution(15416378558147628881)
XLA Ops:
  0.6 1.1 %dynamic-slice_bitcast_fusion.refs_0_ = bf16[128,2048]{1,0:T(8,128)(2,1)S(1)} fusion(bf16[1,128,8192]{2,1,0:T(8,128)(2,1)} %param.6, s32[]{:T(128)S(6)} %select_n.3), kind=kLoop, calls=%fused_computation | loop fusion | bytes 1048580 | tf_op jit(solution)/shard_map/dynamic_slice | solution.py:370
  1.7 3.1 %collective-permute-start = (bf16[128,2048]{1,0:T(8,128)(2,1)S(1)}, bf16[128,2048]{1,0:T(8,128)(2,1)S(1)}, u32[]{:S(2)}, u32[]{:S(2)}) collective-permute-start(bf16[128,2048]{1,0:T(8,128)(2,1)S(1)} %dynamic-slice_bitcast_fusion.refs_0_), channel_id=1, source_target_pairs={{0,3},{1,2},{2,1},{3,0},{4,7},{5,6},{6,5},{7,4},{8,11},{9,10},{10,... | collective-permute-start | bytes 1572872 | tf_op jit(solution)/shard_map/ppermute | solution.py:24
  4.8 1.6 %copy-done = bf16[1,128,8192]{2,1,0:T(8,128)(2,1)S(1)} copy-done((bf16[1,128,8192]{2,1,0:T(8,128)(2,1)S(1)}, bf16[1,128,8192]{2,1,0:T(8,128)(2,1)}, u32[]{:S(2)}) %copy-start) | copy-done | bytes 2097176
  6.5 0.3 collective-permute-start.2
  7.7 1.6 %copy-done.3 = bf16[1,2048,512]{2,1,0:T(8,128)(2,1)S(1)} copy-done((bf16[1,2048,512]{2,1,0:T(8,128)(2,1)S(1)}, bf16[1,2048,512]{2,1,0:T(8,128)(2,1)}, u32[]{:S(2)}) %copy-start.3) | copy-done | bytes 2097176
  9.3 1.1 %early.1 = (f32[128,128]{1,0:T(8,128)S(1)}, bf16[2048,512]{1,0:T(8,128)(2,1)S(1)}, f32[8,128]{1,0:T(8,128)S(1)}) custom-call(s32[1,128]{1,0:T(1,128)S(1)} %bitcast.19, s32[1,1]{1,0:T(1,128)S(6)} %copy.8.count.refs_2_.refs_3_, bf16[2048,512]{1,0:T(8,128)(2,1)S(1)} %bitcast.15, f32[8,128]{1,0:T(8,128)S(1)} %get-tuple-element.31.after), custom_call_target="tpu_custom_call" | custom-call | flops 1000 | bytes 1000 | tf_op jit(solution)/shard_map/early/pallas_call | solution.py:146
  10.5 1.3 %collective-permute-start.5 = (bf16[32,2048]{1,0:T(8,128)(2,1)S(1)}, bf16[32,2048]{1,0:T(8,128)(2,1)S(1)}, u32[]{:S(2)}, u32[]{:S(2)}) collective-permute-start(bf16[32,2048]{1,0:T(8,128)(2,1)S(1)} %get-tuple-element.42), channel_id=1, source_target_pairs={{0,1},{1,0},{2,3},{3,2},{4,5},{5,4},{6,7},{7,6},{8,9},{9,8},{10,11... | collective-permute-start | bytes 393224 | tf_op jit(solution)/shard_map/ppermute | solution.py:24
  11.8 1.2 %collective-permute-start.6 = (bf16[32,2048]{1,0:T(8,128)(2,1)S(1)}, bf16[32,2048]{1,0:T(8,128)(2,1)S(1)}, u32[]{:S(2)}, u32[]{:S(2)}) collective-permute-start(bf16[32,2048]{1,0:T(8,128)(2,1)S(1)} %get-tuple-element.43), channel_id=1, source_target_pairs={{0,2},{1,3},{2,0},{3,1},{4,6},{5,7},{6,4},{7,5},{8,10},{9,11},{10,... | collective-permute-start | bytes 393224 | tf_op jit(solution)/shard_map/ppermute | solution.py:24
  13.1 0.6 %cut.5 = (bf16[128,2048]{1,0:T(8,128)(2,1)S(1)}, f32[8,128]{1,0:T(8,128)}) custom-call(bf16[128,8192]{1,0:T(8,128)(2,1)S(1)} %bitcast.11, f32[8,128]{1,0:T(8,128)S(1)} %get-tuple-element.33.refs_0_), custom_call_target="tpu_custom_call" | custom-call | flops 1000 | bytes 1000 | tf_op jit(solution)/shard_map/cut/pallas_call | solution.py:43
  13.7 2.8 %collective-permute-done.refs_1_ = bf16[128,2048]{1,0:T(8,128)(2,1)S(1)} collective-permute-done((bf16[128,2048]{1,0:T(8,128)(2,1)S(1)}, bf16[128,2048]{1,0:T(8,128)(2,1)S(1)}, u32[]{:S(2)}, u32[]{:S(2)}) %collective-permute-start) | collective-permute-done | bytes 524320 | tf_op jit(solution)/shard_map/ppermute | solution.py:24
  16.5 0.7 %project.3 = (f32[128,512]{1,0:T(8,128)S(1)}, bf16[128,512]{1,0:T(8,128)(2,1)S(1)}, bf16[256,2048]{1,0:T(8,128)(2,1)S(1)}) custom-call(bf16[128,2048]{1,0:T(8,128)(2,1)S(1)} %get-tuple-element.34.refs_0_, bf16[128,2048]{1,0:T(8,128)(2,1)S(1)} %collective-permute-done.refs_1_, bf16[2048,512]{1,0:T(8,128)(2,1)S(1)} %bitcast.12), custom_call_target="tpu_custom_call" | custom-call | flops 1000 | bytes 1000 | tf_op jit(solution)/shard_map/project/pallas_call | solution.py:73
  17.2 2.1 %collective-permute-start.1 = (bf16[128,512]{1,0:T(8,128)(2,1)S(1)}, bf16[128,512]{1,0:T(8,128)(2,1)S(1)}, u32[]{:S(2)}, u32[]{:S(2)}) collective-permute-start(bf16[128,512]{1,0:T(8,128)(2,1)S(1)} %get-tuple-element.36), channel_id=1, source_target_pairs={{0,3},{1,2},{2,1},{3,0},{4,7},{5,6},{6,5},{7,4},{8,11},{9,10},{10,... | collective-permute-start | bytes 393224 | tf_op jit(solution)/shard_map/ppermute | solution.py:24
  19.3 0.6 %prepare.2 = (bf16[128,256]{1,0:T(8,128)(2,1)S(1)}, bf16[2048,256]{1,0:T(8,128)(2,1)S(1)}, f32[8,128]{1,0:T(8,128)S(1)}) custom-call(bf16[256,2048]{1,0:T(8,128)(2,1)S(1)} %get-tuple-element.39.refs_0_, s32[1,128]{1,0:T(1,128)S(1)} %bitcast.20, s32[1,1]{1,0:T(1,128)S(6)} %copy.8.count.refs_2_.refs_3_), custom_call_target="tpu_custom_call" | custom-call | flops 1000 | bytes 1000 | tf_op jit(solution)/shard_map/prepare/pallas_call | solution.py:182
  19.9 4.9 %collective-permute-done.2.refs_0_ = bf16[96,2048]{1,0:T(8,128)(2,1)S(1)} collective-permute-done((bf16[96,2048]{1,0:T(8,128)(2,1)S(1)}, bf16[96,2048]{1,0:T(8,128)(2,1)S(1)}, u32[]{:S(2)}, u32[]{:S(2)}) %collective-permute-start.2) | collective-permute-done | bytes 393248 | tf_op jit(solution)/shard_map/ppermute | solution.py:24
  24.8 0.8 %collective-permute-done.3.refs_1_ = bf16[96,2048]{1,0:T(8,128)(2,1)S(1)} collective-permute-done((bf16[96,2048]{1,0:T(8,128)(2,1)S(1)}, bf16[96,2048]{1,0:T(8,128)(2,1)S(1)}, u32[]{:S(2)}, u32[]{:S(2)}) %collective-permute-start.3) | collective-permute-done | bytes 393248 | tf_op jit(solution)/shard_map/ppermute | solution.py:24
  25.6 0.6 project.4
  26.2 1.5 %collective-permute-start.4 = (bf16[96,512]{1,0:T(8,128)(2,1)S(1)}, bf16[96,512]{1,0:T(8,128)(2,1)S(1)}, u32[]{:S(2)}, u32[]{:S(2)}) collective-permute-start(bf16[96,512]{1,0:T(8,128)(2,1)S(1)} %get-tuple-element.41), channel_id=1, source_target_pairs={{0,1},{1,0},{2,3},{3,2},{4,5},{5,4},{6,7},{7,6},{8,9},{9,8},{10,11... | collective-permute-start | bytes 294920 | tf_op jit(solution)/shard_map/ppermute | solution.py:24
  27.7 1.2 %collective-permute-start.8 = (bf16[96,512]{1,0:T(8,128)(2,1)S(1)}, bf16[96,512]{1,0:T(8,128)(2,1)S(1)}, u32[]{:S(2)}, u32[]{:S(2)}) collective-permute-start(bf16[96,512]{1,0:T(8,128)(2,1)S(1)} %get-tuple-element.44.refs_3_), channel_id=1, source_target_pairs={{0,2},{1,3},{2,0},{3,1},{4,6},{5,7},{6,4},{7,5},{8,10},{9,11},{10,... | collective-permute-start | bytes 294920 | tf_op jit(solution)/shard_map/ppermute | solution.py:24
  29.1 0.5 project.5
  29.6 1.8 %collective-permute-start.9 = (bf16[32,512]{1,0:T(8,128)(2,1)S(1)}, bf16[32,512]{1,0:T(8,128)(2,1)S(1)}, u32[]{:S(2)}, u32[]{:S(2)}) collective-permute-start(bf16[32,512]{1,0:T(8,128)(2,1)S(1)} %get-tuple-element.46), channel_id=1, source_target_pairs={{0,2},{1,3},{2,0},{3,1},{4,6},{5,7},{6,4},{7,5},{8,10},{9,11},{10,... | collective-permute-start | bytes 98312 | tf_op jit(solution)/shard_map/ppermute | solution.py:24
  31.4 1.2 %collective-permute-start.7 = (bf16[32,512]{1,0:T(8,128)(2,1)S(1)}, bf16[32,512]{1,0:T(8,128)(2,1)S(1)}, u32[]{:S(2)}, u32[]{:S(2)}) collective-permute-start(bf16[32,512]{1,0:T(8,128)(2,1)S(1)} %get-tuple-element.45.refs_4_), channel_id=1, source_target_pairs={{0,1},{1,0},{2,3},{3,2},{4,5},{5,4},{6,7},{7,6},{8,9},{9,8},{10,11... | collective-permute-start | bytes 98312 | tf_op jit(solution)/shard_map/ppermute | solution.py:24
  32.6 0.9 %prepare.3 = (bf16[128,256]{1,0:T(8,128)(2,1)S(1)}, bf16[2048,256]{1,0:T(8,128)(2,1)S(1)}, f32[8,128]{1,0:T(8,128)S(1)}) custom-call(bf16[192,2048]{1,0:T(8,128)(2,1)S(1)} %get-tuple-element.47.refs_0_, bf16[64,2048]{1,0:T(8,128)(2,1)S(1)} %get-tuple-element.48.refs_1_, s32[1,128]{1,0:T(1,128)S(1)} %bitcast.21, s32[1,1]{1,0:T(1,128)S(6)} %copy.8.count.refs_2_.refs_3_, ...), custom_call_target="tpu_custom_call" | custom-call | flops 1000 | bytes 1000 | tf_op jit(solution)/shard_map/prepare/pallas_call | solution.py:182
  33.6 0.9 %collective-permute-done.7.refs_4_ = bf16[32,512]{1,0:T(8,128)(2,1)S(1)} collective-permute-done((bf16[32,512]{1,0:T(8,128)(2,1)S(1)}, bf16[32,512]{1,0:T(8,128)(2,1)S(1)}, u32[]{:S(2)}, u32[]{:S(2)}) %collective-permute-start.7) | collective-permute-done | bytes 32800 | tf_op jit(solution)/shard_map/ppermute | solution.py:24
  34.5 9.2 %all_to_all.5 = bf16[4,128,512]{2,1,0:T(8,128)(2,1)S(1)} all-to-all(bf16[4,128,512]{2,1,0:T(8,128)(2,1)S(1)} %slope.1), channel_id=1, replica_groups=mesh['rep'=8,'shard'=4] {'shard'}, dimensions={0} | all-to-all | bytes 1048576 | tf_op jit(solution)/shard_map/all_to_all | solution.py:395
  43.7 0.3 kept.1
  44.0 3.5 %collective-permute-start.10 = (bf16[144,128]{1,0:T(8,128)(2,1)S(1)}, bf16[144,128]{1,0:T(8,128)(2,1)S(1)}, u32[]{:S(2)}, u32[]{:S(2)}) collective-permute-start(bf16[144,128]{1,0:T(8,128)(2,1)S(1)} %get-tuple-element.53.refs_0_), channel_id=1, source_target_pairs={{0,24},{4,28},{8,16},{12,20},{16,8},{20,12},{24,0},{28,4},{1,25},{... | collective-permute-start | bytes 110600 | tf_op jit(solution)/shard_map/ppermute | solution.py:24
  47.5 0.4 collective-permute-start.12
  47.9 2.4 %residue.1 = (bf16[2048,512]{1,0:T(8,128)(2,1)}, f32[8,128]{1,0:T(8,128)S(1)}) custom-call(bf16[512,512]{1,0:T(8,128)(2,1)S(1)} %get-tuple-element.54.s, bf16[2048,256]{1,0:T(8,128)(2,1)S(1)} %get-tuple-element.55.refs_0_, bf16[2048,256]{1,0:T(8,128)(2,1)S(1)} %get-tuple-element.56.refs_1_, bf16[2048,512]{1,0:T(8,128)(2,1)S(1)} %bitcast.16, ...), custom_call_target="tpu_custom_call" | custom-call | flops 1000 | bytes 1000 | tf_op jit(solution)/shard_map/residue/pallas_call | solution.py:259
  50.3 1.1 %collective-permute-done.11.refs_1_ = bf16[144,128]{1,0:T(8,128)(2,1)S(1)} collective-permute-done((bf16[144,128]{1,0:T(8,128)(2,1)S(1)}, bf16[144,128]{1,0:T(8,128)(2,1)S(1)}, u32[]{:S(2)}, u32[]{:S(2)}) %collective-permute-start.11) | collective-permute-done | bytes 36896 | tf_op jit(solution)/shard_map/ppermute | solution.py:24
  51.5 4.3 %collective-permute-start.13 = (bf16[576,128]{1,0:T(8,128)(2,1)S(1)}, bf16[576,128]{1,0:T(8,128)(2,1)S(1)}, u32[]{:S(2)}, u32[]{:S(2)}) collective-permute-start(bf16[576,128]{1,0:T(8,128)(2,1)S(1)} %join.5.group), channel_id=1, source_target_pairs={{0,4},{4,0},{8,12},{12,8},{16,20},{20,16},{24,28},{28,24},{1,5},{5... | collective-permute-start | bytes 442376 | tf_op jit(solution)/shard_map/ppermute | solution.py:24
  55.7 1.4 %half.1 = f32[2048,512]{1,0:T(8,128)S(1)} custom-call(bf16[576,128]{1,0:T(8,128)(2,1)S(1)} %join.5.group), custom_call_target="tpu_custom_call" | custom-call | flops 1000 | bytes 1000 | tf_op jit(solution)/shard_map/half/pallas_call | solution.py:337
  57.2 2.5 %outer.1 = f32[2048,512]{1,0:T(8,128)} custom-call(bf16[576,128]{1,0:T(8,128)(2,1)S(1)} %collective-permute-done.13.group, f32[2048,512]{1,0:T(8,128)S(1)} %half.1), custom_call_target="tpu_custom_call" | custom-call | flops 1000 | bytes 1000 | tf_op jit(solution)/shard_map/outer/pallas_call | solution.py:345
  (29 shorter events, 0.6 us)
Async XLA Ops:
  0.6 7.0 %copy-start.6 = (s32[1,1,128]{2,1,0:T(1,128)S(1)}, s32[1,1,128]{2,1,0:T(1,128)}, u32[]{:S(2)}) copy-start(s32[1,1,128]{2,1,0:T(1,128)} %param.11) | copy-start | bytes 1540
  1.7 14.8 %collective-permute-start = (bf16[128,2048]{1,0:T(8,128)(2,1)S(1)}, bf16[128,2048]{1,0:T(8,128)(2,1)S(1)}, u32[]{:S(2)}, u32[]{:S(2)}) collective-permute-start(bf16[128,2048]{1,0:T(8,128)(2,1)S(1)} %dynamic-slice_bitcast_fusion.refs_0_), channel_id=1, source_target_pairs={{0,3},{1,2},{2,1},{3,0},{4,7},{5,6},{6,5},{7,4},{8,11},{9,10},{10,... | collective-permute-start | bytes 1572872 | tf_op jit(solution)/shard_map/ppermute | solution.py:24
  4.8 1.6 %copy-start = (bf16[1,128,8192]{2,1,0:T(8,128)(2,1)S(1)}, bf16[1,128,8192]{2,1,0:T(8,128)(2,1)}, u32[]{:S(2)}) copy-start(bf16[1,128,8192]{2,1,0:T(8,128)(2,1)} %param.6) | copy-start | bytes 6291460
  6.4 4.0 %copy-start.1 = (bf16[1,128,8192]{2,1,0:T(8,128)(2,1)S(1)}, bf16[1,128,8192]{2,1,0:T(8,128)(2,1)}, u32[]{:S(2)}) copy-start(bf16[1,128,8192]{2,1,0:T(8,128)(2,1)} %param.6) | copy-start | bytes 6291460
  6.5 18.4 %collective-permute-start.2 = (bf16[96,2048]{1,0:T(8,128)(2,1)S(1)}, bf16[96,2048]{1,0:T(8,128)(2,1)S(1)}, u32[]{:S(2)}, u32[]{:S(2)}) collective-permute-start(bf16[96,2048]{1,0:T(8,128)(2,1)S(1)} %get-tuple-element.37), channel_id=1, source_target_pairs={{0,1},{1,0},{2,3},{3,2},{4,5},{5,4},{6,7},{7,6},{8,9},{9,8},{10,11... | collective-permute-start | bytes 1179656 | tf_op jit(solution)/shard_map/ppermute | solution.py:24
  6.8 18.8 %collective-permute-start.3 = (bf16[96,2048]{1,0:T(8,128)(2,1)S(1)}, bf16[96,2048]{1,0:T(8,128)(2,1)S(1)}, u32[]{:S(2)}, u32[]{:S(2)}) collective-permute-start(bf16[96,2048]{1,0:T(8,128)(2,1)S(1)} %get-tuple-element.38), channel_id=1, source_target_pairs={{0,2},{1,3},{2,0},{3,1},{4,6},{5,7},{6,4},{7,5},{8,10},{9,11},{10,... | collective-permute-start | bytes 1179656 | tf_op jit(solution)/shard_map/ppermute | solution.py:24
  7.7 1.6 %copy-start.3 = (bf16[1,2048,512]{2,1,0:T(8,128)(2,1)S(1)}, bf16[1,2048,512]{2,1,0:T(8,128)(2,1)}, u32[]{:S(2)}) copy-start(bf16[1,2048,512]{2,1,0:T(8,128)(2,1)} %param.9) | copy-start | bytes 6291460
  10.4 6.1 %copy-start.2 = (bf16[1,2048,512]{2,1,0:T(8,128)(2,1)S(1)}, bf16[1,2048,512]{2,1,0:T(8,128)(2,1)}, u32[]{:S(2)}) copy-start(bf16[1,2048,512]{2,1,0:T(8,128)(2,1)} %param.8) | copy-start | bytes 6291460
  10.5 18.4 %collective-permute-start.5 = (bf16[32,2048]{1,0:T(8,128)(2,1)S(1)}, bf16[32,2048]{1,0:T(8,128)(2,1)S(1)}, u32[]{:S(2)}, u32[]{:S(2)}) collective-permute-start(bf16[32,2048]{1,0:T(8,128)(2,1)S(1)} %get-tuple-element.42), channel_id=1, source_target_pairs={{0,1},{1,0},{2,3},{3,2},{4,5},{5,4},{6,7},{7,6},{8,9},{9,8},{10,11... | collective-permute-start | bytes 393224 | tf_op jit(solution)/shard_map/ppermute | solution.py:24
  11.8 17.3 %collective-permute-start.6 = (bf16[32,2048]{1,0:T(8,128)(2,1)S(1)}, bf16[32,2048]{1,0:T(8,128)(2,1)S(1)}, u32[]{:S(2)}, u32[]{:S(2)}) collective-permute-start(bf16[32,2048]{1,0:T(8,128)(2,1)S(1)} %get-tuple-element.43), channel_id=1, source_target_pairs={{0,2},{1,3},{2,0},{3,1},{4,6},{5,7},{6,4},{7,5},{8,10},{9,11},{10,... | collective-permute-start | bytes 393224 | tf_op jit(solution)/shard_map/ppermute | solution.py:24
  17.2 17.2 %collective-permute-start.1 = (bf16[128,512]{1,0:T(8,128)(2,1)S(1)}, bf16[128,512]{1,0:T(8,128)(2,1)S(1)}, u32[]{:S(2)}, u32[]{:S(2)}) collective-permute-start(bf16[128,512]{1,0:T(8,128)(2,1)S(1)} %get-tuple-element.36), channel_id=1, source_target_pairs={{0,3},{1,2},{2,1},{3,0},{4,7},{5,6},{6,5},{7,4},{8,11},{9,10},{10,... | collective-permute-start | bytes 393224 | tf_op jit(solution)/shard_map/ppermute | solution.py:24
  26.2 8.2 %copy-start.5 = (bf16[1,128,512]{2,1,0:T(8,128)(2,1)S(1)}, bf16[1,128,512]{2,1,0:T(8,128)(2,1)}, u32[]{:S(2)}) copy-start(bf16[1,128,512]{2,1,0:T(8,128)(2,1)} %param.7) | copy-start | bytes 393220
  26.2 8.2 %collective-permute-start.4 = (bf16[96,512]{1,0:T(8,128)(2,1)S(1)}, bf16[96,512]{1,0:T(8,128)(2,1)S(1)}, u32[]{:S(2)}, u32[]{:S(2)}) collective-permute-start(bf16[96,512]{1,0:T(8,128)(2,1)S(1)} %get-tuple-element.41), channel_id=1, source_target_pairs={{0,1},{1,0},{2,3},{3,2},{4,5},{5,4},{6,7},{7,6},{8,9},{9,8},{10,11... | collective-permute-start | bytes 294920 | tf_op jit(solution)/shard_map/ppermute | solution.py:24
  27.7 6.8 %collective-permute-start.8 = (bf16[96,512]{1,0:T(8,128)(2,1)S(1)}, bf16[96,512]{1,0:T(8,128)(2,1)S(1)}, u32[]{:S(2)}, u32[]{:S(2)}) collective-permute-start(bf16[96,512]{1,0:T(8,128)(2,1)S(1)} %get-tuple-element.44.refs_3_), channel_id=1, source_target_pairs={{0,2},{1,3},{2,0},{3,1},{4,6},{5,7},{6,4},{7,5},{8,10},{9,11},{10,... | collective-permute-start | bytes 294920 | tf_op jit(solution)/shard_map/ppermute | solution.py:24
  29.6 4.0 %collective-permute-start.9 = (bf16[32,512]{1,0:T(8,128)(2,1)S(1)}, bf16[32,512]{1,0:T(8,128)(2,1)S(1)}, u32[]{:S(2)}, u32[]{:S(2)}) collective-permute-start(bf16[32,512]{1,0:T(8,128)(2,1)S(1)} %get-tuple-element.46), channel_id=1, source_target_pairs={{0,2},{1,3},{2,0},{3,1},{4,6},{5,7},{6,4},{7,5},{8,10},{9,11},{10,... | collective-permute-start | bytes 98312 | tf_op jit(solution)/shard_map/ppermute | solution.py:24
  31.4 16.5 %copy-start.4 = (bf16[1,2048,512]{2,1,0:T(8,128)(2,1)S(1)}, bf16[1,2048,512]{2,1,0:T(8,128)(2,1)}, u32[]{:S(2)}) copy-start(bf16[1,2048,512]{2,1,0:T(8,128)(2,1)} %param.9) | copy-start | bytes 6291460
  31.4 3.0 %collective-permute-start.7 = (bf16[32,512]{1,0:T(8,128)(2,1)S(1)}, bf16[32,512]{1,0:T(8,128)(2,1)S(1)}, u32[]{:S(2)}, u32[]{:S(2)}) collective-permute-start(bf16[32,512]{1,0:T(8,128)(2,1)S(1)} %get-tuple-element.45.refs_4_), channel_id=1, source_target_pairs={{0,1},{1,0},{2,3},{3,2},{4,5},{5,4},{6,7},{7,6},{8,9},{9,8},{10,11... | collective-permute-start | bytes 98312 | tf_op jit(solution)/shard_map/ppermute | solution.py:24
  44.0 6.3 %collective-permute-start.10 = (bf16[144,128]{1,0:T(8,128)(2,1)S(1)}, bf16[144,128]{1,0:T(8,128)(2,1)S(1)}, u32[]{:S(2)}, u32[]{:S(2)}) collective-permute-start(bf16[144,128]{1,0:T(8,128)(2,1)S(1)} %get-tuple-element.53.refs_0_), channel_id=1, source_target_pairs={{0,24},{4,28},{8,16},{12,20},{16,8},{20,12},{24,0},{28,4},{1,25},{... | collective-permute-start | bytes 110600 | tf_op jit(solution)/shard_map/ppermute | solution.py:24
  47.5 3.9 %collective-permute-start.11 = (bf16[144,128]{1,0:T(8,128)(2,1)S(1)}, bf16[144,128]{1,0:T(8,128)(2,1)S(1)}, u32[]{:S(2)}, u32[]{:S(2)}) collective-permute-start(bf16[144,128]{1,0:T(8,128)(2,1)S(1)} %get-tuple-element.53.refs_0_), channel_id=1, source_target_pairs={{0,16},{4,20},{8,24},{12,28},{16,0},{20,4},{24,8},{28,12},{1,17},{... | collective-permute-start | bytes 110600 | tf_op jit(solution)/shard_map/ppermute | solution.py:24
  47.5 3.9 %collective-permute-start.12 = (bf16[144,128]{1,0:T(8,128)(2,1)S(1)}, bf16[144,128]{1,0:T(8,128)(2,1)S(1)}, u32[]{:S(2)}, u32[]{:S(2)}) collective-permute-start(bf16[144,128]{1,0:T(8,128)(2,1)S(1)} %get-tuple-element.53.refs_0_), channel_id=1, source_target_pairs={{0,8},{4,12},{8,0},{12,4},{16,24},{20,28},{24,16},{28,20},{1,9},{5... | collective-permute-start | bytes 110600 | tf_op jit(solution)/shard_map/ppermute | solution.py:24
  51.5 5.7 %collective-permute-start.13 = (bf16[576,128]{1,0:T(8,128)(2,1)S(1)}, bf16[576,128]{1,0:T(8,128)(2,1)S(1)}, u32[]{:S(2)}, u32[]{:S(2)}) collective-permute-start(bf16[576,128]{1,0:T(8,128)(2,1)S(1)} %join.5.group), channel_id=1, source_target_pairs={{0,4},{4,0},{8,12},{12,8},{16,20},{20,16},{24,28},{28,24},{1,5},{5... | collective-permute-start | bytes 442376 | tf_op jit(solution)/shard_map/ppermute | solution.py:24

commit v17 on v10

--- a/solution.py
+++ b/solution.py
@@ -270,7 +270,7 @@
 def residue(slopes, order, xts, fb, keep):
     depth, kw = fb.shape
     total = sum(xt.shape[1] for xt in xts)
-    tile = min(depth, 512)
+    tile = min(depth, 256)
     return pl.pallas_call(
         functools.partial(residue_kernel, order, tile),
         out_shape=[
@@ -341,7 +341,7 @@
     tiles = out.shape[0] // tile
     for t in range(tiles):
         rows = slice(t * tile, (t + 1) * tile)
-        held[rows, :] = (half[rows, :] + place(lines, wide, t, tile)) / n
+        held[rows, :] = (half[rows, :] + place(lines, wide, t, tile)) * (1.0 / n)
         send_out(held, out, sems, t, tile).start()
     for t in range(tiles):
         send_out(held, out, sems, t, tile).wait()
@@ -350,7 +350,7 @@
 def outer(groups, cap, depth, kw):
     slots = groups[0].shape[0] // (cap + 16) * cap
     n = 2 * slots // cap
-    tile = min(depth, 512)
+    tile = min(depth, 256)
     shape = jax.ShapeDtypeStruct((depth, kw), jnp.float32)
     scratch = [pltpu.VMEM((slots, kw), jnp.bfloat16), pltpu.VMEM((8, slots), jnp.int32)]
     half = pl.pallas_call(

time: 57.5 us -> 57.4 us (level)
  no operation moved by 1% of the time
where the time goes in v17:
time: 57.4 us; the launch traced here: 57.2 us
  starting transfers between devices  24.1 us (42%)
  waiting for transfers between devices  15.7 us (27%)
  Pallas kernels  11.6 us (20%)
  local copies, waits for them, and re-layouts  4.28 us (7%)
  between operations  1.53 us (3%)
    ppermute x20, starting transfers between devices, swap(): return lax.ppermute(x, axis, [(i, i ^ d) for i in range(n)])  24.1 us
    ppermute x20, waiting for transfers between devices, swap(): return lax.ppermute(x, axis, [(i, i ^ d) for i in range(n)])  15.7 us
    unnamed x14, local copies, waits for them, and re-layouts  3.2 us
    pallas_call x1, Pallas kernels, outer(): pl.pallas_call(functools.partial(outer_kernel, cap, kw // LANES, tile, n)...  2.54 us
    pallas_call x1, Pallas kernels, residue(): pl.pallas_call(functools.partial(residue_kernel, order, tile), out_shape=...  2.38 us
    pallas_call x3, Pallas kernels, project(): pl.pallas_call(functools.partial(project_kernel, n, len(outs)), out_shape...  1.62 us
    pallas_call x1, Pallas kernels, outer(): pl.pallas_call(functools.partial(half_kernel, cap, kw // LANES, tile), ou...  1.41 us
    pallas_call x2, Pallas kernels, prepare(): pl.pallas_call(functools.partial(prepare_kernel, per_row, len(xs)), out_s...  1.2 us
  transfers between devices with their start and end apart: 20, of which 9 were waited for; matrix products, arithmetic and copies ran while one was open for 0% of the time, Pallas kernels for 15%

profile of v17, /device:TPU:1, one launch (start us, length us, event | category | flops | bytes accessed | tf_op | source)
XLA Modules:
  0.0 57.2 jit_solution(2499087110693830841)
XLA Ops:
  0.6 1.1 %dynamic-slice_bitcast_fusion = (bf16[64,2048]{1,0:T(8,128)(2,1)S(1)}, bf16[64,2048]{1,0:T(8,128)(2,1)S(1)}) fusion(bf16[1,128,8192]{2,1,0:T(8,128)(2,1)} %param.6, s32[]{:T(128)S(6)} %select_n.4), kind=kLoop, calls=%fused_computation | loop fusion | bytes 1048580 | tf_op jit(solution)/shard_map/dynamic_slice | solution.py:392
  1.7 2.1 %collective-permute-start.1 = (bf16[64,2048]{1,0:T(8,128)(2,1)S(1)}, bf16[64,2048]{1,0:T(8,128)(2,1)S(1)}, u32[]{:S(2)}, u32[]{:S(2)}) collective-permute-start(bf16[64,2048]{1,0:T(8,128)(2,1)S(1)} %get-tuple-element.56), channel_id=1, source_target_pairs={{0,2},{1,3},{2,0},{3,1},{4,6},{5,7},{6,4},{7,5},{8,10},{9,11},{10,... | collective-permute-start | bytes 786440 | tf_op jit(solution)/shard_map/ppermute | solution.py:24
  3.9 1.2 %collective-permute-start = (bf16[64,2048]{1,0:T(8,128)(2,1)S(1)}, bf16[64,2048]{1,0:T(8,128)(2,1)S(1)}, u32[]{:S(2)}, u32[]{:S(2)}) collective-permute-start(bf16[64,2048]{1,0:T(8,128)(2,1)S(1)} %get-tuple-element.57.refs_0_), channel_id=1, source_target_pairs={{0,1},{1,0},{2,3},{3,2},{4,5},{5,4},{6,7},{7,6},{8,9},{9,8},{10,11... | collective-permute-start | bytes 786440 | tf_op jit(solution)/shard_map/ppermute | solution.py:24
  5.1 1.6 %copy-done = bf16[1,128,8192]{2,1,0:T(8,128)(2,1)S(1)} copy-done((bf16[1,128,8192]{2,1,0:T(8,128)(2,1)S(1)}, bf16[1,128,8192]{2,1,0:T(8,128)(2,1)}, u32[]{:S(2)}) %copy-start) | copy-done | bytes 2097176
  7.1 2.8 %collective-permute-done.1.refs_2_ = bf16[64,2048]{1,0:T(8,128)(2,1)S(1)} collective-permute-done((bf16[64,2048]{1,0:T(8,128)(2,1)S(1)}, bf16[64,2048]{1,0:T(8,128)(2,1)S(1)}, u32[]{:S(2)}, u32[]{:S(2)}) %collective-permute-start.1) | collective-permute-done | bytes 262176 | tf_op jit(solution)/shard_map/ppermute | solution.py:24
  9.9 1.1 %collective-permute-start.3 = (bf16[64,2048]{1,0:T(8,128)(2,1)S(1)}, bf16[64,2048]{1,0:T(8,128)(2,1)S(1)}, u32[]{:S(2)}, u32[]{:S(2)}) collective-permute-start(bf16[64,2048]{1,0:T(8,128)(2,1)S(1)} %collective-permute-done.1.refs_2_), channel_id=1, source_target_pairs={{0,1},{1,0},{2,3},{3,2},{4,5},{5,4},{6,7},{7,6},{8,9},{9,8},{10,11... | collective-permute-start | bytes 786440 | tf_op jit(solution)/shard_map/ppermute | solution.py:24
  11.0 1.2 %collective-permute-start.2 = (bf16[64,2048]{1,0:T(8,128)(2,1)S(1)}, bf16[64,2048]{1,0:T(8,128)(2,1)S(1)}, u32[]{:S(2)}, u32[]{:S(2)}) collective-permute-start(bf16[64,2048]{1,0:T(8,128)(2,1)S(1)} %collective-permute-done.refs_1_), channel_id=1, source_target_pairs={{0,2},{1,3},{2,0},{3,1},{4,6},{5,7},{6,4},{7,5},{8,10},{9,11},{10,... | collective-permute-start | bytes 786440 | tf_op jit(solution)/shard_map/ppermute | solution.py:24
  12.9 1.6 %copy-done.3 = bf16[1,2048,512]{2,1,0:T(8,128)(2,1)S(1)} copy-done((bf16[1,2048,512]{2,1,0:T(8,128)(2,1)S(1)}, bf16[1,2048,512]{2,1,0:T(8,128)(2,1)}, u32[]{:S(2)}) %copy-start.3) | copy-done | bytes 2097176
  14.5 1.1 %early.1 = (f32[128,128]{1,0:T(8,128)S(1)}, bf16[2048,512]{1,0:T(8,128)(2,1)S(1)}, f32[8,128]{1,0:T(8,128)S(1)}) custom-call(s32[1,128]{1,0:T(1,128)S(1)} %bitcast.19, s32[1,1]{1,0:T(1,128)S(6)} %copy.8.count.refs_2_.refs_3_, bf16[2048,512]{1,0:T(8,128)(2,1)S(1)} %bitcast.16, f32[8,128]{1,0:T(8,128)S(1)} %get-tuple-element.29.after), custom_call_target="tpu_custom_call" | custom-call | flops 1000 | bytes 1000 | tf_op jit(solution)/shard_map/early/pallas_call | solution.py:145
  16.3 0.6 %collective-permute-start.9 = (bf16[64,2048]{1,0:T(8,128)(2,1)S(1)}, bf16[64,2048]{1,0:T(8,128)(2,1)S(1)}, u32[]{:S(2)}, u32[]{:S(2)}) collective-permute-start(bf16[64,2048]{1,0:T(8,128)(2,1)S(1)} %get-tuple-element.40), channel_id=1, source_target_pairs={{0,2},{1,3},{2,0},{3,1},{4,6},{5,7},{6,4},{7,5},{8,10},{9,11},{10,... | collective-permute-start | bytes 786440 | tf_op jit(solution)/shard_map/ppermute | solution.py:24
  16.9 0.6 %cut.5 = (bf16[128,2048]{1,0:T(8,128)(2,1)S(1)}, f32[8,128]{1,0:T(8,128)}) custom-call(bf16[128,8192]{1,0:T(8,128)(2,1)S(1)} %bitcast.12, f32[8,128]{1,0:T(8,128)S(1)} %get-tuple-element.31.refs_0_), custom_call_target="tpu_custom_call" | custom-call | flops 1000 | bytes 1000 | tf_op jit(solution)/shard_map/cut/pallas_call | solution.py:43
  18.1 3.9 %collective-permute-done.3.refs_2_ = bf16[64,2048]{1,0:T(8,128)(2,1)S(1)} collective-permute-done((bf16[64,2048]{1,0:T(8,128)(2,1)S(1)}, bf16[64,2048]{1,0:T(8,128)(2,1)S(1)}, u32[]{:S(2)}, u32[]{:S(2)}) %collective-permute-start.3) | collective-permute-done | bytes 262176 | tf_op jit(solution)/shard_map/ppermute | solution.py:24
  22.0 0.7 %project.4 = (f32[128,512]{1,0:T(8,128)S(1)}, bf16[128,512]{1,0:T(8,128)(2,1)S(1)}, bf16[256,2048]{1,0:T(8,128)(2,1)S(1)}) custom-call(bf16[128,2048]{1,0:T(8,128)(2,1)S(1)} %get-tuple-element.32.refs_0_, bf16[64,2048]{1,0:T(8,128)(2,1)S(1)} %collective-permute-done.2.refs_1_, bf16[64,2048]{1,0:T(8,128)(2,1)S(1)} %collective-permute-done.3.refs_2_, ...), custom_call_target="tpu_custom_call" | custom-call | flops 1000 | bytes 1000 | tf_op jit(solution)/shard_map/project/pallas_call | solution.py:73
  22.7 1.3 %collective-permute-start.6 = (bf16[128,512]{1,0:T(8,128)(2,1)S(1)}, bf16[128,512]{1,0:T(8,128)(2,1)S(1)}, u32[]{:S(2)}, u32[]{:S(2)}) collective-permute-start(bf16[128,512]{1,0:T(8,128)(2,1)S(1)} %get-tuple-element.37.refs_3_), channel_id=1, source_target_pairs={{0,3},{1,2},{2,1},{3,0},{4,7},{5,6},{6,5},{7,4},{8,11},{9,10},{10,... | collective-permute-start | bytes 393224 | tf_op jit(solution)/shard_map/ppermute | solution.py:24
  24.0 1.2 %collective-permute-start.11 = (bf16[64,512]{1,0:T(8,128)(2,1)S(1)}, bf16[64,512]{1,0:T(8,128)(2,1)S(1)}, u32[]{:S(2)}, u32[]{:S(2)}) collective-permute-start(bf16[64,512]{1,0:T(8,128)(2,1)S(1)} %get-tuple-element.35.refs_4_), channel_id=1, source_target_pairs={{0,2},{1,3},{2,0},{3,1},{4,6},{5,7},{6,4},{7,5},{8,10},{9,11},{10,... | collective-permute-start | bytes 196616 | tf_op jit(solution)/shard_map/ppermute | solution.py:24
  25.4 0.6 %prepare.2 = (bf16[128,256]{1,0:T(8,128)(2,1)S(1)}, bf16[2048,256]{1,0:T(8,128)(2,1)S(1)}, f32[8,128]{1,0:T(8,128)S(1)}) custom-call(bf16[256,2048]{1,0:T(8,128)(2,1)S(1)} %get-tuple-element.41.refs_0_, s32[1,128]{1,0:T(1,128)S(1)} %bitcast.20, s32[1,1]{1,0:T(1,128)S(6)} %copy.8.count.refs_2_.refs_3_, bf16[128,512]{1,0:T(8,128)(2,1)S(1)} %get-tuple-element.37.refs_3_), custom_call_target="tpu_custom_call" | custom-call | flops 1000 | bytes 1000 | tf_op jit(solution)/shard_map/prepare/pallas_call | solution.py:181
  26.0 1.6 %collective-permute-done.8.refs_0_ = bf16[64,2048]{1,0:T(8,128)(2,1)S(1)} collective-permute-done((bf16[64,2048]{1,0:T(8,128)(2,1)S(1)}, bf16[64,2048]{1,0:T(8,128)(2,1)S(1)}, u32[]{:S(2)}, u32[]{:S(2)}) %collective-permute-start.8) | collective-permute-done | bytes 262176 | tf_op jit(solution)/shard_map/ppermute | solution.py:24
  28.5 1.1 %collective-permute-start.10 = (bf16[64,512]{1,0:T(8,128)(2,1)S(1)}, bf16[64,512]{1,0:T(8,128)(2,1)S(1)}, u32[]{:S(2)}, u32[]{:S(2)}) collective-permute-start(bf16[64,512]{1,0:T(8,128)(2,1)S(1)} %get-tuple-element.43.refs_4_), channel_id=1, source_target_pairs={{0,1},{1,0},{2,3},{3,2},{4,5},{5,4},{6,7},{7,6},{8,9},{9,8},{10,11... | collective-permute-start | bytes 196616 | tf_op jit(solution)/shard_map/ppermute | solution.py:24
  29.6 0.6 %prepare.3 = (bf16[128,256]{1,0:T(8,128)(2,1)S(1)}, bf16[2048,256]{1,0:T(8,128)(2,1)S(1)}, f32[8,128]{1,0:T(8,128)S(1)}) custom-call(bf16[128,2048]{1,0:T(8,128)(2,1)S(1)} %get-tuple-element.45.refs_0_, bf16[128,2048]{1,0:T(8,128)(2,1)S(1)} %get-tuple-element.46.refs_1_, s32[1,128]{1,0:T(1,128)S(1)} %bitcast.21, s32[1,1]{1,0:T(1,128)S(6)} %copy.8.count.refs_2_.refs_3_, ...), custom_call_target="tpu_custom_call" | custom-call | flops 1000 | bytes 1000 | tf_op jit(solution)/shard_map/prepare/pallas_call | solution.py:181
  30.2 1.5 %collective-permute-done.7.refs_3_ = bf16[64,512]{1,0:T(8,128)(2,1)S(1)} collective-permute-done((bf16[64,512]{1,0:T(8,128)(2,1)S(1)}, bf16[64,512]{1,0:T(8,128)(2,1)S(1)}, u32[]{:S(2)}, u32[]{:S(2)}) %collective-permute-start.7) | collective-permute-done | bytes 65568 | tf_op jit(solution)/shard_map/ppermute | solution.py:24
  31.8 1.4 %collective-permute-done.12.refs_6_ = bf16[64,512]{1,0:T(8,128)(2,1)S(1)} collective-permute-done((bf16[64,512]{1,0:T(8,128)(2,1)S(1)}, bf16[64,512]{1,0:T(8,128)(2,1)S(1)}, u32[]{:S(2)}, u32[]{:S(2)}) %collective-permute-start.12) | collective-permute-done | bytes 65568 | tf_op jit(solution)/shard_map/ppermute | solution.py:24
  33.3 1.6 %collective-permute-start.15 = (bf16[128,512]{1,0:T(8,128)(2,1)S(1)}, bf16[128,512]{1,0:T(8,128)(2,1)S(1)}, u32[]{:S(2)}, u32[]{:S(2)}) collective-permute-start(bf16[128,512]{1,0:T(8,128)(2,1)S(1)} %slope.1.refs_0_), channel_id=1, source_target_pairs={{0,3},{1,2},{2,1},{3,0},{4,7},{5,6},{6,5},{7,4},{8,11},{9,10},{10,... | collective-permute-start | bytes 393224 | tf_op jit(solution)/shard_map/ppermute | solution.py:24
  34.8 0.6 %collective-permute-start.14 = (bf16[128,512]{1,0:T(8,128)(2,1)S(1)}, bf16[128,512]{1,0:T(8,128)(2,1)S(1)}, u32[]{:S(2)}, u32[]{:S(2)}) collective-permute-start(bf16[128,512]{1,0:T(8,128)(2,1)S(1)} %slope.1.refs_0_), channel_id=1, source_target_pairs={{0,2},{1,3},{2,0},{3,1},{4,6},{5,7},{6,4},{7,5},{8,10},{9,11},{10,... | collective-permute-start | bytes 393224 | tf_op jit(solution)/shard_map/ppermute | solution.py:24
  35.5 0.5 collective-permute-start.13
  36.0 2.2 %collective-permute-done.15.refs_1_ = bf16[128,512]{1,0:T(8,128)(2,1)S(1)} collective-permute-done((bf16[128,512]{1,0:T(8,128)(2,1)S(1)}, bf16[128,512]{1,0:T(8,128)(2,1)S(1)}, u32[]{:S(2)}, u32[]{:S(2)}) %collective-permute-start.15) | collective-permute-done | bytes 131104 | tf_op jit(solution)/shard_map/ppermute | solution.py:24
  38.3 1.1 %collective-permute-done.14.refs_1_.refs_3_ = bf16[128,512]{1,0:T(8,128)(2,1)S(1)} collective-permute-done((bf16[128,512]{1,0:T(8,128)(2,1)S(1)}, bf16[128,512]{1,0:T(8,128)(2,1)S(1)}, u32[]{:S(2)}, u32[]{:S(2)}) %collective-permute-start.14) | collective-permute-done | bytes 131104 | tf_op jit(solution)/shard_map/ppermute | solution.py:24
  39.7 3.6 %collective-permute-start.16 = (bf16[144,128]{1,0:T(8,128)(2,1)S(1)}, bf16[144,128]{1,0:T(8,128)(2,1)S(1)}, u32[]{:S(2)}, u32[]{:S(2)}) collective-permute-start(bf16[144,128]{1,0:T(8,128)(2,1)S(1)} %kept.1.refs_0_), channel_id=1, source_target_pairs={{0,24},{4,28},{8,16},{12,20},{16,8},{20,12},{24,0},{28,4},{1,25},{... | collective-permute-start | bytes 110600 | tf_op jit(solution)/shard_map/ppermute | solution.py:24
  43.7 2.4 %residue.1 = (bf16[2048,512]{1,0:T(8,128)(2,1)}, f32[8,128]{1,0:T(8,128)S(1)}) custom-call(bf16[128,512]{1,0:T(8,128)(2,1)S(1)} %slope.1.refs_0_, bf16[128,512]{1,0:T(8,128)(2,1)S(1)} %collective-permute-done.15.refs_1_, bf16[128,512]{1,0:T(8,128)(2,1)S(1)} %collective-permute-done.13.refs_0_.refs_2_, ...), custom_call_target="tpu_custom_call" | custom-call | flops 1000 | bytes 1000 | tf_op jit(solution)/shard_map/residue/pallas_call | solution.py:274
  46.1 0.9 %collective-permute-done.17.refs_1_ = bf16[144,128]{1,0:T(8,128)(2,1)S(1)} collective-permute-done((bf16[144,128]{1,0:T(8,128)(2,1)S(1)}, bf16[144,128]{1,0:T(8,128)(2,1)S(1)}, u32[]{:S(2)}, u32[]{:S(2)}) %collective-permute-start.17) | collective-permute-done | bytes 36896 | tf_op jit(solution)/shard_map/ppermute | solution.py:24
  47.1 6.1 %collective-permute-start.19 = (bf16[576,128]{1,0:T(8,128)(2,1)S(1)}, bf16[576,128]{1,0:T(8,128)(2,1)S(1)}, u32[]{:S(2)}, u32[]{:S(2)}) collective-permute-start(bf16[576,128]{1,0:T(8,128)(2,1)S(1)} %join.5.group), channel_id=1, source_target_pairs={{0,4},{4,0},{8,12},{12,8},{16,20},{20,16},{24,28},{28,24},{1,5},{5... | collective-permute-start | bytes 442376 | tf_op jit(solution)/shard_map/ppermute | solution.py:24
  53.2 1.4 %half.1 = f32[2048,512]{1,0:T(8,128)S(1)} custom-call(bf16[576,128]{1,0:T(8,128)(2,1)S(1)} %join.5.group), custom_call_target="tpu_custom_call" | custom-call | flops 1000 | bytes 1000 | tf_op jit(solution)/shard_map/half/pallas_call | solution.py:356
  54.6 2.5 %outer.1 = f32[2048,512]{1,0:T(8,128)} custom-call(bf16[576,128]{1,0:T(8,128)(2,1)S(1)} %collective-permute-done.19.group, f32[2048,512]{1,0:T(8,128)S(1)} %half.1), custom_call_target="tpu_custom_call" | custom-call | flops 1000 | bytes 1000 | tf_op jit(solution)/shard_map/outer/pallas_call | solution.py:364
  (41 shorter events, 3.7 us)
Async XLA Ops:
  0.6 12.3 %copy-start.6 = (s32[1,1,128]{2,1,0:T(1,128)S(1)}, s32[1,1,128]{2,1,0:T(1,128)}, u32[]{:S(2)}) copy-start(s32[1,1,128]{2,1,0:T(1,128)} %param.11) | copy-start | bytes 1540
  1.7 8.2 %collective-permute-start.1 = (bf16[64,2048]{1,0:T(8,128)(2,1)S(1)}, bf16[64,2048]{1,0:T(8,128)(2,1)S(1)}, u32[]{:S(2)}, u32[]{:S(2)}) collective-permute-start(bf16[64,2048]{1,0:T(8,128)(2,1)S(1)} %get-tuple-element.56), channel_id=1, source_target_pairs={{0,2},{1,3},{2,0},{3,1},{4,6},{5,7},{6,4},{7,5},{8,10},{9,11},{10,... | collective-permute-start | bytes 786440 | tf_op jit(solution)/shard_map/ppermute | solution.py:24
  3.9 7.1 %collective-permute-start = (bf16[64,2048]{1,0:T(8,128)(2,1)S(1)}, bf16[64,2048]{1,0:T(8,128)(2,1)S(1)}, u32[]{:S(2)}, u32[]{:S(2)}) collective-permute-start(bf16[64,2048]{1,0:T(8,128)(2,1)S(1)} %get-tuple-element.57.refs_0_), channel_id=1, source_target_pairs={{0,1},{1,0},{2,3},{3,2},{4,5},{5,4},{6,7},{7,6},{8,9},{9,8},{10,11... | collective-permute-start | bytes 786440 | tf_op jit(solution)/shard_map/ppermute | solution.py:24
  5.1 1.6 %copy-start = (bf16[1,128,8192]{2,1,0:T(8,128)(2,1)S(1)}, bf16[1,128,8192]{2,1,0:T(8,128)(2,1)}, u32[]{:S(2)}) copy-start(bf16[1,128,8192]{2,1,0:T(8,128)(2,1)} %param.6) | copy-start | bytes 6291460
  6.7 9.0 %copy-start.1 = (bf16[1,128,8192]{2,1,0:T(8,128)(2,1)S(1)}, bf16[1,128,8192]{2,1,0:T(8,128)(2,1)}, u32[]{:S(2)}) copy-start(bf16[1,128,8192]{2,1,0:T(8,128)(2,1)} %param.6) | copy-start | bytes 6291460
  6.7 9.6 %collective-permute-start.4 = (bf16[64,2048]{1,0:T(8,128)(2,1)S(1)}, bf16[64,2048]{1,0:T(8,128)(2,1)S(1)}, u32[]{:S(2)}, u32[]{:S(2)}) collective-permute-start(bf16[64,2048]{1,0:T(8,128)(2,1)S(1)} %get-tuple-element.33), channel_id=1, source_target_pairs={{0,1},{1,0},{2,3},{3,2},{4,5},{5,4},{6,7},{7,6},{8,9},{9,8},{10,11... | collective-permute-start | bytes 786440 | tf_op jit(solution)/shard_map/ppermute | solution.py:24
  7.1 10.5 %collective-permute-start.5 = (bf16[64,2048]{1,0:T(8,128)(2,1)S(1)}, bf16[64,2048]{1,0:T(8,128)(2,1)S(1)}, u32[]{:S(2)}, u32[]{:S(2)}) collective-permute-start(bf16[64,2048]{1,0:T(8,128)(2,1)S(1)} %get-tuple-element.34), channel_id=1, source_target_pairs={{0,2},{1,3},{2,0},{3,1},{4,6},{5,7},{6,4},{7,5},{8,10},{9,11},{10,... | collective-permute-start | bytes 786440 | tf_op jit(solution)/shard_map/ppermute | solution.py:24
  9.9 12.1 %collective-permute-start.3 = (bf16[64,2048]{1,0:T(8,128)(2,1)S(1)}, bf16[64,2048]{1,0:T(8,128)(2,1)S(1)}, u32[]{:S(2)}, u32[]{:S(2)}) collective-permute-start(bf16[64,2048]{1,0:T(8,128)(2,1)S(1)} %collective-permute-done.1.refs_2_), channel_id=1, source_target_pairs={{0,1},{1,0},{2,3},{3,2},{4,5},{5,4},{6,7},{7,6},{8,9},{9,8},{10,11... | collective-permute-start | bytes 786440 | tf_op jit(solution)/shard_map/ppermute | solution.py:24
  11.0 10.9 %collective-permute-start.2 = (bf16[64,2048]{1,0:T(8,128)(2,1)S(1)}, bf16[64,2048]{1,0:T(8,128)(2,1)S(1)}, u32[]{:S(2)}, u32[]{:S(2)}) collective-permute-start(bf16[64,2048]{1,0:T(8,128)(2,1)S(1)} %collective-permute-done.refs_1_), channel_id=1, source_target_pairs={{0,2},{1,3},{2,0},{3,1},{4,6},{5,7},{6,4},{7,5},{8,10},{9,11},{10,... | collective-permute-start | bytes 786440 | tf_op jit(solution)/shard_map/ppermute | solution.py:24
  12.9 1.6 %copy-start.3 = (bf16[1,2048,512]{2,1,0:T(8,128)(2,1)S(1)}, bf16[1,2048,512]{2,1,0:T(8,128)(2,1)}, u32[]{:S(2)}) copy-start(bf16[1,2048,512]{2,1,0:T(8,128)(2,1)} %param.9) | copy-start | bytes 6291460
  15.6 2.0 %copy-start.2 = (bf16[1,2048,512]{2,1,0:T(8,128)(2,1)S(1)}, bf16[1,2048,512]{2,1,0:T(8,128)(2,1)}, u32[]{:S(2)}) copy-start(bf16[1,2048,512]{2,1,0:T(8,128)(2,1)} %param.8) | copy-start | bytes 6291460
  15.7 11.8 %collective-permute-start.8 = (bf16[64,2048]{1,0:T(8,128)(2,1)S(1)}, bf16[64,2048]{1,0:T(8,128)(2,1)S(1)}, u32[]{:S(2)}, u32[]{:S(2)}) collective-permute-start(bf16[64,2048]{1,0:T(8,128)(2,1)S(1)} %get-tuple-element.39), channel_id=1, source_target_pairs={{0,1},{1,0},{2,3},{3,2},{4,5},{5,4},{6,7},{7,6},{8,9},{9,8},{10,11... | collective-permute-start | bytes 786440 | tf_op jit(solution)/shard_map/ppermute | solution.py:24
  16.3 11.2 %collective-permute-start.9 = (bf16[64,2048]{1,0:T(8,128)(2,1)S(1)}, bf16[64,2048]{1,0:T(8,128)(2,1)S(1)}, u32[]{:S(2)}, u32[]{:S(2)}) collective-permute-start(bf16[64,2048]{1,0:T(8,128)(2,1)S(1)} %get-tuple-element.40), channel_id=1, source_target_pairs={{0,2},{1,3},{2,0},{3,1},{4,6},{5,7},{6,4},{7,5},{8,10},{9,11},{10,... | collective-permute-start | bytes 786440 | tf_op jit(solution)/shard_map/ppermute | solution.py:24
  22.7 10.5 %collective-permute-start.6 = (bf16[128,512]{1,0:T(8,128)(2,1)S(1)}, bf16[128,512]{1,0:T(8,128)(2,1)S(1)}, u32[]{:S(2)}, u32[]{:S(2)}) collective-permute-start(bf16[128,512]{1,0:T(8,128)(2,1)S(1)} %get-tuple-element.37.refs_3_), channel_id=1, source_target_pairs={{0,3},{1,2},{2,1},{3,0},{4,7},{5,6},{6,5},{7,4},{8,11},{9,10},{10,... | collective-permute-start | bytes 393224 | tf_op jit(solution)/shard_map/ppermute | solution.py:24
  24.0 7.8 %collective-permute-start.11 = (bf16[64,512]{1,0:T(8,128)(2,1)S(1)}, bf16[64,512]{1,0:T(8,128)(2,1)S(1)}, u32[]{:S(2)}, u32[]{:S(2)}) collective-permute-start(bf16[64,512]{1,0:T(8,128)(2,1)S(1)} %get-tuple-element.35.refs_4_), channel_id=1, source_target_pairs={{0,2},{1,3},{2,0},{3,1},{4,6},{5,7},{6,4},{7,5},{8,10},{9,11},{10,... | collective-permute-start | bytes 196616 | tf_op jit(solution)/shard_map/ppermute | solution.py:24
  25.1 6.6 %collective-permute-start.7 = (bf16[64,512]{1,0:T(8,128)(2,1)S(1)}, bf16[64,512]{1,0:T(8,128)(2,1)S(1)}, u32[]{:S(2)}, u32[]{:S(2)}) collective-permute-start(bf16[64,512]{1,0:T(8,128)(2,1)S(1)} %get-tuple-element.38), channel_id=1, source_target_pairs={{0,1},{1,0},{2,3},{3,2},{4,5},{5,4},{6,7},{7,6},{8,9},{9,8},{10,11... | collective-permute-start | bytes 196616 | tf_op jit(solution)/shard_map/ppermute | solution.py:24
  26.0 7.2 %copy-start.5 = (bf16[1,128,512]{2,1,0:T(8,128)(2,1)S(1)}, bf16[1,128,512]{2,1,0:T(8,128)(2,1)}, u32[]{:S(2)}) copy-start(bf16[1,128,512]{2,1,0:T(8,128)(2,1)} %param.7) | copy-start | bytes 393220
  28.0 15.7 %copy-start.4 = (bf16[1,2048,512]{2,1,0:T(8,128)(2,1)S(1)}, bf16[1,2048,512]{2,1,0:T(8,128)(2,1)}, u32[]{:S(2)}) copy-start(bf16[1,2048,512]{2,1,0:T(8,128)(2,1)} %param.9) | copy-start | bytes 6291460
  28.0 5.1 %collective-permute-start.12 = (bf16[64,512]{1,0:T(8,128)(2,1)S(1)}, bf16[64,512]{1,0:T(8,128)(2,1)S(1)}, u32[]{:S(2)}, u32[]{:S(2)}) collective-permute-start(bf16[64,512]{1,0:T(8,128)(2,1)S(1)} %get-tuple-element.44), channel_id=1, source_target_pairs={{0,2},{1,3},{2,0},{3,1},{4,6},{5,7},{6,4},{7,5},{8,10},{9,11},{10,... | collective-permute-start | bytes 196616 | tf_op jit(solution)/shard_map/ppermute | solution.py:24
  28.5 4.7 %collective-permute-start.10 = (bf16[64,512]{1,0:T(8,128)(2,1)S(1)}, bf16[64,512]{1,0:T(8,128)(2,1)S(1)}, u32[]{:S(2)}, u32[]{:S(2)}) collective-permute-start(bf16[64,512]{1,0:T(8,128)(2,1)S(1)} %get-tuple-element.43.refs_4_), channel_id=1, source_target_pairs={{0,1},{1,0},{2,3},{3,2},{4,5},{5,4},{6,7},{7,6},{8,9},{9,8},{10,11... | collective-permute-start | bytes 196616 | tf_op jit(solution)/shard_map/ppermute | solution.py:24
  33.3 4.9 %collective-permute-start.15 = (bf16[128,512]{1,0:T(8,128)(2,1)S(1)}, bf16[128,512]{1,0:T(8,128)(2,1)S(1)}, u32[]{:S(2)}, u32[]{:S(2)}) collective-permute-start(bf16[128,512]{1,0:T(8,128)(2,1)S(1)} %slope.1.refs_0_), channel_id=1, source_target_pairs={{0,3},{1,2},{2,1},{3,0},{4,7},{5,6},{6,5},{7,4},{8,11},{9,10},{10,... | collective-permute-start | bytes 393224 | tf_op jit(solution)/shard_map/ppermute | solution.py:24
  34.8 4.6 %collective-permute-start.14 = (bf16[128,512]{1,0:T(8,128)(2,1)S(1)}, bf16[128,512]{1,0:T(8,128)(2,1)S(1)}, u32[]{:S(2)}, u32[]{:S(2)}) collective-permute-start(bf16[128,512]{1,0:T(8,128)(2,1)S(1)} %slope.1.refs_0_), channel_id=1, source_target_pairs={{0,2},{1,3},{2,0},{3,1},{4,6},{5,7},{6,4},{7,5},{8,10},{9,11},{10,... | collective-permute-start | bytes 393224 | tf_op jit(solution)/shard_map/ppermute | solution.py:24
  35.5 4.0 %collective-permute-start.13 = (bf16[128,512]{1,0:T(8,128)(2,1)S(1)}, bf16[128,512]{1,0:T(8,128)(2,1)S(1)}, u32[]{:S(2)}, u32[]{:S(2)}) collective-permute-start(bf16[128,512]{1,0:T(8,128)(2,1)S(1)} %slope.1.refs_0_), channel_id=1, source_target_pairs={{0,1},{1,0},{2,3},{3,2},{4,5},{5,4},{6,7},{7,6},{8,9},{9,8},{10,11... | collective-permute-start | bytes 393224 | tf_op jit(solution)/shard_map/ppermute | solution.py:24
  39.7 6.3 %collective-permute-start.16 = (bf16[144,128]{1,0:T(8,128)(2,1)S(1)}, bf16[144,128]{1,0:T(8,128)(2,1)S(1)}, u32[]{:S(2)}, u32[]{:S(2)}) collective-permute-start(bf16[144,128]{1,0:T(8,128)(2,1)S(1)} %kept.1.refs_0_), channel_id=1, source_target_pairs={{0,24},{4,28},{8,16},{12,20},{16,8},{20,12},{24,0},{28,4},{1,25},{... | collective-permute-start | bytes 110600 | tf_op jit(solution)/shard_map/ppermute | solution.py:24
  43.3 3.7 %collective-permute-start.17 = (bf16[144,128]{1,0:T(8,128)(2,1)S(1)}, bf16[144,128]{1,0:T(8,128)(2,1)S(1)}, u32[]{:S(2)}, u32[]{:S(2)}) collective-permute-start(bf16[144,128]{1,0:T(8,128)(2,1)S(1)} %kept.1.refs_0_), channel_id=1, source_target_pairs={{0,16},{4,20},{8,24},{12,28},{16,0},{20,4},{24,8},{28,12},{1,17},{... | collective-permute-start | bytes 110600 | tf_op jit(solution)/shard_map/ppermute | solution.py:24
  43.3 3.7 %collective-permute-start.18 = (bf16[144,128]{1,0:T(8,128)(2,1)S(1)}, bf16[144,128]{1,0:T(8,128)(2,1)S(1)}, u32[]{:S(2)}, u32[]{:S(2)}) collective-permute-start(bf16[144,128]{1,0:T(8,128)(2,1)S(1)} %kept.1.refs_0_), channel_id=1, source_target_pairs={{0,8},{4,12},{8,0},{12,4},{16,24},{20,28},{24,16},{28,20},{1,9},{5... | collective-permute-start | bytes 110600 | tf_op jit(solution)/shard_map/ppermute | solution.py:24
  47.1 7.5 %collective-permute-start.19 = (bf16[576,128]{1,0:T(8,128)(2,1)S(1)}, bf16[576,128]{1,0:T(8,128)(2,1)S(1)}, u32[]{:S(2)}, u32[]{:S(2)}) collective-permute-start(bf16[576,128]{1,0:T(8,128)(2,1)S(1)} %join.5.group), channel_id=1, source_target_pairs={{0,4},{4,0},{8,12},{12,8},{16,20},{20,16},{24,28},{28,24},{1,5},{5... | collective-permute-start | bytes 442376 | tf_op jit(solution)/shard_map/ppermute | solution.py:24

commit v18 on v17

--- a/solution.py
+++ b/solution.py
@@ -378,7 +378,7 @@
     n_shard, n_rep = lax.axis_size("shard"), lax.axis_size("rep")
     tok_dev = tokens.shape[0]
     depth, kw = w.shape
-    early_rows = tok_dev // 2
+    early_rows = tok_dev * 5 // 8
     spans = [(0, early_rows), (early_rows, tok_dev)]
     per_row = kw // LANES
     slot_row = blocks[0]

time: 57.4 us -> 58.4 us (1.017)
  starting transfers between devices: 24.1 us -> 24.9 us
    ppermute x20, starting transfers between devices: 24.1 us -> 24.9 us  [swap(): return lax.ppermute(x, axis, [(i, i ^ d) for i in range(n)])]
  transfers between devices with their start and end apart: 20 -> 20, of which waited for: 9 -> 9; matrix products, arithmetic and copies ran while one was open for 0% -> 0% of each run, Pallas kernels for 15% -> 16%
where the time goes in v18:
time: 58.4 us; the launch traced here: 58.2 us
  starting transfers between devices  24.9 us (43%)
  waiting for transfers between devices  15.5 us (27%)
  Pallas kernels  12 us (21%)
  local copies, waits for them, and re-layouts  4.28 us (7%)
  between operations  1.52 us (3%)
    ppermute x20, starting transfers between devices, swap(): return lax.ppermute(x, axis, [(i, i ^ d) for i in range(n)])  24.9 us
    ppermute x20, waiting for transfers between devices, swap(): return lax.ppermute(x, axis, [(i, i ^ d) for i in range(n)])  15.5 us
    unnamed x14, local copies, waits for them, and re-layouts  3.2 us
    pallas_call x1, Pallas kernels, outer(): pl.pallas_call(functools.partial(outer_kernel, cap, kw // LANES, tile, n)...  2.54 us
    pallas_call x1, Pallas kernels, residue(): pl.pallas_call(functools.partial(residue_kernel, order, tile), out_shape=...  2.38 us
    pallas_call x3, Pallas kernels, project(): pl.pallas_call(functools.partial(project_kernel, n, len(outs)), out_shape...  1.69 us
    pallas_call x2, Pallas kernels, prepare(): pl.pallas_call(functools.partial(prepare_kernel, per_row, len(xs)), out_s...  1.53 us
    pallas_call x1, Pallas kernels, outer(): pl.pallas_call(functools.partial(half_kernel, cap, kw // LANES, tile), ou...  1.41 us
  transfers between devices with their start and end apart: 20, of which 9 were waited for; matrix products, arithmetic and copies ran while one was open for 0% of the time, Pallas kernels for 16%

profile of v18, /device:TPU:1, one launch (start us, length us, event | category | flops | bytes accessed | tf_op | source)
XLA Modules:
  0.0 58.2 jit_solution(2968260485060931930)
XLA Ops:
  0.6 1.1 %dynamic-slice_bitcast_fusion = (bf16[64,2048]{1,0:T(8,128)(2,1)S(1)}, bf16[64,2048]{1,0:T(8,128)(2,1)S(1)}) fusion(bf16[1,128,8192]{2,1,0:T(8,128)(2,1)} %param.6, s32[]{:T(128)S(6)} %select_n.4), kind=kLoop, calls=%fused_computation | loop fusion | bytes 1048580 | tf_op jit(solution)/shard_map/dynamic_slice | solution.py:392
  1.7 2.1 %collective-permute-start.1 = (bf16[64,2048]{1,0:T(8,128)(2,1)S(1)}, bf16[64,2048]{1,0:T(8,128)(2,1)S(1)}, u32[]{:S(2)}, u32[]{:S(2)}) collective-permute-start(bf16[64,2048]{1,0:T(8,128)(2,1)S(1)} %get-tuple-element.56), channel_id=1, source_target_pairs={{0,2},{1,3},{2,0},{3,1},{4,6},{5,7},{6,4},{7,5},{8,10},{9,11},{10,... | collective-permute-start | bytes 786440 | tf_op jit(solution)/shard_map/ppermute | solution.py:24
  3.9 1.2 %collective-permute-start = (bf16[64,2048]{1,0:T(8,128)(2,1)S(1)}, bf16[64,2048]{1,0:T(8,128)(2,1)S(1)}, u32[]{:S(2)}, u32[]{:S(2)}) collective-permute-start(bf16[64,2048]{1,0:T(8,128)(2,1)S(1)} %get-tuple-element.57.refs_0_), channel_id=1, source_target_pairs={{0,1},{1,0},{2,3},{3,2},{4,5},{5,4},{6,7},{7,6},{8,9},{9,8},{10,11... | collective-permute-start | bytes 786440 | tf_op jit(solution)/shard_map/ppermute | solution.py:24
  5.1 1.6 %copy-done = bf16[1,128,8192]{2,1,0:T(8,128)(2,1)S(1)} copy-done((bf16[1,128,8192]{2,1,0:T(8,128)(2,1)S(1)}, bf16[1,128,8192]{2,1,0:T(8,128)(2,1)}, u32[]{:S(2)}) %copy-start) | copy-done | bytes 2097176
  7.1 2.8 %collective-permute-done.1.refs_2_ = bf16[64,2048]{1,0:T(8,128)(2,1)S(1)} collective-permute-done((bf16[64,2048]{1,0:T(8,128)(2,1)S(1)}, bf16[64,2048]{1,0:T(8,128)(2,1)S(1)}, u32[]{:S(2)}, u32[]{:S(2)}) %collective-permute-start.1) | collective-permute-done | bytes 262176 | tf_op jit(solution)/shard_map/ppermute | solution.py:24
  9.9 1.1 %collective-permute-start.3 = (bf16[64,2048]{1,0:T(8,128)(2,1)S(1)}, bf16[64,2048]{1,0:T(8,128)(2,1)S(1)}, u32[]{:S(2)}, u32[]{:S(2)}) collective-permute-start(bf16[64,2048]{1,0:T(8,128)(2,1)S(1)} %collective-permute-done.1.refs_2_), channel_id=1, source_target_pairs={{0,1},{1,0},{2,3},{3,2},{4,5},{5,4},{6,7},{7,6},{8,9},{9,8},{10,11... | collective-permute-start | bytes 786440 | tf_op jit(solution)/shard_map/ppermute | solution.py:24
  11.0 1.2 %collective-permute-start.2 = (bf16[64,2048]{1,0:T(8,128)(2,1)S(1)}, bf16[64,2048]{1,0:T(8,128)(2,1)S(1)}, u32[]{:S(2)}, u32[]{:S(2)}) collective-permute-start(bf16[64,2048]{1,0:T(8,128)(2,1)S(1)} %collective-permute-done.refs_1_), channel_id=1, source_target_pairs={{0,2},{1,3},{2,0},{3,1},{4,6},{5,7},{6,4},{7,5},{8,10},{9,11},{10,... | collective-permute-start | bytes 786440 | tf_op jit(solution)/shard_map/ppermute | solution.py:24
  12.9 1.6 %copy-done.3 = bf16[1,2048,512]{2,1,0:T(8,128)(2,1)S(1)} copy-done((bf16[1,2048,512]{2,1,0:T(8,128)(2,1)S(1)}, bf16[1,2048,512]{2,1,0:T(8,128)(2,1)}, u32[]{:S(2)}) %copy-start.3) | copy-done | bytes 2097176
  14.5 1.1 %early.1 = (f32[128,128]{1,0:T(8,128)S(1)}, bf16[2048,512]{1,0:T(8,128)(2,1)S(1)}, f32[8,128]{1,0:T(8,128)S(1)}) custom-call(s32[1,128]{1,0:T(1,128)S(1)} %bitcast.19, s32[1,1]{1,0:T(1,128)S(6)} %copy.8.count.refs_2_.refs_3_, bf16[2048,512]{1,0:T(8,128)(2,1)S(1)} %bitcast.16, f32[8,128]{1,0:T(8,128)S(1)} %get-tuple-element.29.after), custom_call_target="tpu_custom_call" | custom-call | flops 1000 | bytes 1000 | tf_op jit(solution)/shard_map/early/pallas_call | solution.py:145
  16.1 1.6 %collective-permute-done.4.refs_0_ = bf16[80,2048]{1,0:T(8,128)(2,1)S(1)} collective-permute-done((bf16[80,2048]{1,0:T(8,128)(2,1)S(1)}, bf16[80,2048]{1,0:T(8,128)(2,1)S(1)}, u32[]{:S(2)}, u32[]{:S(2)}) %collective-permute-start.4) | collective-permute-done | bytes 327712 | tf_op jit(solution)/shard_map/ppermute | solution.py:24
  18.1 0.6 %cut.5 = (bf16[128,2048]{1,0:T(8,128)(2,1)S(1)}, f32[8,128]{1,0:T(8,128)}) custom-call(bf16[128,8192]{1,0:T(8,128)(2,1)S(1)} %bitcast.12, f32[8,128]{1,0:T(8,128)S(1)} %get-tuple-element.31.refs_0_), custom_call_target="tpu_custom_call" | custom-call | flops 1000 | bytes 1000 | tf_op jit(solution)/shard_map/cut/pallas_call | solution.py:43
  18.8 0.5 project.3
  19.3 4.0 %collective-permute-done.3.refs_2_ = bf16[64,2048]{1,0:T(8,128)(2,1)S(1)} collective-permute-done((bf16[64,2048]{1,0:T(8,128)(2,1)S(1)}, bf16[64,2048]{1,0:T(8,128)(2,1)S(1)}, u32[]{:S(2)}, u32[]{:S(2)}) %collective-permute-start.3) | collective-permute-done | bytes 262176 | tf_op jit(solution)/shard_map/ppermute | solution.py:24
  23.4 0.7 %project.4 = (f32[128,512]{1,0:T(8,128)S(1)}, bf16[128,512]{1,0:T(8,128)(2,1)S(1)}, bf16[256,2048]{1,0:T(8,128)(2,1)S(1)}) custom-call(bf16[128,2048]{1,0:T(8,128)(2,1)S(1)} %get-tuple-element.32.refs_0_, bf16[64,2048]{1,0:T(8,128)(2,1)S(1)} %collective-permute-done.2.refs_1_, bf16[64,2048]{1,0:T(8,128)(2,1)S(1)} %collective-permute-done.3.refs_2_, ...), custom_call_target="tpu_custom_call" | custom-call | flops 1000 | bytes 1000 | tf_op jit(solution)/shard_map/project/pallas_call | solution.py:73
  24.1 1.3 %collective-permute-start.6 = (bf16[128,512]{1,0:T(8,128)(2,1)S(1)}, bf16[128,512]{1,0:T(8,128)(2,1)S(1)}, u32[]{:S(2)}, u32[]{:S(2)}) collective-permute-start(bf16[128,512]{1,0:T(8,128)(2,1)S(1)} %get-tuple-element.37.refs_3_), channel_id=1, source_target_pairs={{0,3},{1,2},{2,1},{3,0},{4,7},{5,6},{6,5},{7,4},{8,11},{9,10},{10,... | collective-permute-start | bytes 393224 | tf_op jit(solution)/shard_map/ppermute | solution.py:24
  25.7 1.1 %collective-permute-start.11 = (bf16[80,512]{1,0:T(8,128)(2,1)S(1)}, bf16[80,512]{1,0:T(8,128)(2,1)S(1)}, u32[]{:S(2)}, u32[]{:S(2)}) collective-permute-start(bf16[80,512]{1,0:T(8,128)(2,1)S(1)} %get-tuple-element.35.refs_4_), channel_id=1, source_target_pairs={{0,2},{1,3},{2,0},{3,1},{4,6},{5,7},{6,4},{7,5},{8,10},{9,11},{10,... | collective-permute-start | bytes 245768 | tf_op jit(solution)/shard_map/ppermute | solution.py:24
  26.8 0.6 %prepare.2 = (bf16[128,256]{1,0:T(8,128)(2,1)S(1)}, bf16[2048,256]{1,0:T(8,128)(2,1)S(1)}, f32[8,128]{1,0:T(8,128)S(1)}) custom-call(bf16[256,2048]{1,0:T(8,128)(2,1)S(1)} %get-tuple-element.41.refs_0_, s32[1,128]{1,0:T(1,128)S(1)} %bitcast.20, s32[1,1]{1,0:T(1,128)S(6)} %copy.8.count.refs_2_.refs_3_, bf16[128,512]{1,0:T(8,128)(2,1)S(1)} %get-tuple-element.37.refs_3_), custom_call_target="tpu_custom_call" | custom-call | flops 1000 | bytes 1000 | tf_op jit(solution)/shard_map/prepare/pallas_call | solution.py:181
  27.6 0.5 project.5
  28.5 1.1 %collective-permute-start.10 = (bf16[48,512]{1,0:T(8,128)(2,1)S(1)}, bf16[48,512]{1,0:T(8,128)(2,1)S(1)}, u32[]{:S(2)}, u32[]{:S(2)}) collective-permute-start(bf16[48,512]{1,0:T(8,128)(2,1)S(1)} %get-tuple-element.43.refs_4_), channel_id=1, source_target_pairs={{0,1},{1,0},{2,3},{3,2},{4,5},{5,4},{6,7},{7,6},{8,9},{9,8},{10,11... | collective-permute-start | bytes 147464 | tf_op jit(solution)/shard_map/ppermute | solution.py:24
  29.6 0.9 %prepare.3 = (bf16[128,256]{1,0:T(8,128)(2,1)S(1)}, bf16[2048,256]{1,0:T(8,128)(2,1)S(1)}, f32[8,128]{1,0:T(8,128)S(1)}) custom-call(bf16[160,2048]{1,0:T(8,128)(2,1)S(1)} %get-tuple-element.45.refs_0_, bf16[96,2048]{1,0:T(8,128)(2,1)S(1)} %get-tuple-element.46.refs_1_, s32[1,128]{1,0:T(1,128)S(1)} %bitcast.21, s32[1,1]{1,0:T(1,128)S(6)} %copy.8.count.refs_2_.refs_3_, ...), custom_call_target="tpu_custom_call" | custom-call | flops 1000 | bytes 1000 | tf_op jit(solution)/shard_map/prepare/pallas_call | solution.py:181
  30.6 1.6 %collective-permute-done.7.refs_3_ = bf16[80,512]{1,0:T(8,128)(2,1)S(1)} collective-permute-done((bf16[80,512]{1,0:T(8,128)(2,1)S(1)}, bf16[80,512]{1,0:T(8,128)(2,1)S(1)}, u32[]{:S(2)}, u32[]{:S(2)}) %collective-permute-start.7) | collective-permute-done | bytes 81952 | tf_op jit(solution)/shard_map/ppermute | solution.py:24
  32.1 1.0 %collective-permute-done.10.refs_4_ = bf16[48,512]{1,0:T(8,128)(2,1)S(1)} collective-permute-done((bf16[48,512]{1,0:T(8,128)(2,1)S(1)}, bf16[48,512]{1,0:T(8,128)(2,1)S(1)}, u32[]{:S(2)}, u32[]{:S(2)}) %collective-permute-start.10) | collective-permute-done | bytes 49184 | tf_op jit(solution)/shard_map/ppermute | solution.py:24
  33.3 1.1 %collective-permute-start.15 = (bf16[128,512]{1,0:T(8,128)(2,1)S(1)}, bf16[128,512]{1,0:T(8,128)(2,1)S(1)}, u32[]{:S(2)}, u32[]{:S(2)}) collective-permute-start(bf16[128,512]{1,0:T(8,128)(2,1)S(1)} %slope.1.refs_0_), channel_id=1, source_target_pairs={{0,3},{1,2},{2,1},{3,0},{4,7},{5,6},{6,5},{7,4},{8,11},{9,10},{10,... | collective-permute-start | bytes 393224 | tf_op jit(solution)/shard_map/ppermute | solution.py:24
  34.4 1.2 %collective-permute-start.14 = (bf16[128,512]{1,0:T(8,128)(2,1)S(1)}, bf16[128,512]{1,0:T(8,128)(2,1)S(1)}, u32[]{:S(2)}, u32[]{:S(2)}) collective-permute-start(bf16[128,512]{1,0:T(8,128)(2,1)S(1)} %slope.1.refs_0_), channel_id=1, source_target_pairs={{0,2},{1,3},{2,0},{3,1},{4,6},{5,7},{6,4},{7,5},{8,10},{9,11},{10,... | collective-permute-start | bytes 393224 | tf_op jit(solution)/shard_map/ppermute | solution.py:24
  36.0 2.5 %collective-permute-done.15.refs_1_ = bf16[128,512]{1,0:T(8,128)(2,1)S(1)} collective-permute-done((bf16[128,512]{1,0:T(8,128)(2,1)S(1)}, bf16[128,512]{1,0:T(8,128)(2,1)S(1)}, u32[]{:S(2)}, u32[]{:S(2)}) %collective-permute-start.15) | collective-permute-done | bytes 131104 | tf_op jit(solution)/shard_map/ppermute | solution.py:24
  38.7 0.8 %collective-permute-done.14.refs_1_.refs_3_ = bf16[128,512]{1,0:T(8,128)(2,1)S(1)} collective-permute-done((bf16[128,512]{1,0:T(8,128)(2,1)S(1)}, bf16[128,512]{1,0:T(8,128)(2,1)S(1)}, u32[]{:S(2)}, u32[]{:S(2)}) %collective-permute-start.14) | collective-permute-done | bytes 131104 | tf_op jit(solution)/shard_map/ppermute | solution.py:24
  39.8 3.3 %collective-permute-start.16 = (bf16[144,128]{1,0:T(8,128)(2,1)S(1)}, bf16[144,128]{1,0:T(8,128)(2,1)S(1)}, u32[]{:S(2)}, u32[]{:S(2)}) collective-permute-start(bf16[144,128]{1,0:T(8,128)(2,1)S(1)} %kept.1.refs_0_), channel_id=1, source_target_pairs={{0,24},{4,28},{8,16},{12,20},{16,8},{20,12},{24,0},{28,4},{1,25},{... | collective-permute-start | bytes 110600 | tf_op jit(solution)/shard_map/ppermute | solution.py:24
  43.5 2.4 %residue.1 = (bf16[2048,512]{1,0:T(8,128)(2,1)}, f32[8,128]{1,0:T(8,128)S(1)}) custom-call(bf16[128,512]{1,0:T(8,128)(2,1)S(1)} %slope.1.refs_0_, bf16[128,512]{1,0:T(8,128)(2,1)S(1)} %collective-permute-done.15.refs_1_, bf16[128,512]{1,0:T(8,128)(2,1)S(1)} %collective-permute-done.13.refs_0_.refs_2_, ...), custom_call_target="tpu_custom_call" | custom-call | flops 1000 | bytes 1000 | tf_op jit(solution)/shard_map/residue/pallas_call | solution.py:274
  45.9 0.9 %collective-permute-done.17.refs_1_ = bf16[144,128]{1,0:T(8,128)(2,1)S(1)} collective-permute-done((bf16[144,128]{1,0:T(8,128)(2,1)S(1)}, bf16[144,128]{1,0:T(8,128)(2,1)S(1)}, u32[]{:S(2)}, u32[]{:S(2)}) %collective-permute-start.17) | collective-permute-done | bytes 36896 | tf_op jit(solution)/shard_map/ppermute | solution.py:24
  46.9 7.4 %collective-permute-start.19 = (bf16[576,128]{1,0:T(8,128)(2,1)S(1)}, bf16[576,128]{1,0:T(8,128)(2,1)S(1)}, u32[]{:S(2)}, u32[]{:S(2)}) collective-permute-start(bf16[576,128]{1,0:T(8,128)(2,1)S(1)} %join.5.group), channel_id=1, source_target_pairs={{0,4},{4,0},{8,12},{12,8},{16,20},{20,16},{24,28},{28,24},{1,5},{5... | collective-permute-start | bytes 442376 | tf_op jit(solution)/shard_map/ppermute | solution.py:24
  54.2 1.4 %half.1 = f32[2048,512]{1,0:T(8,128)S(1)} custom-call(bf16[576,128]{1,0:T(8,128)(2,1)S(1)} %join.5.group), custom_call_target="tpu_custom_call" | custom-call | flops 1000 | bytes 1000 | tf_op jit(solution)/shard_map/half/pallas_call | solution.py:356
  55.7 2.5 %outer.1 = f32[2048,512]{1,0:T(8,128)} custom-call(bf16[576,128]{1,0:T(8,128)(2,1)S(1)} %collective-permute-done.19.group, f32[2048,512]{1,0:T(8,128)S(1)} %half.1), custom_call_target="tpu_custom_call" | custom-call | flops 1000 | bytes 1000 | tf_op jit(solution)/shard_map/outer/pallas_call | solution.py:364
  (41 shorter events, 3.6 us)
Async XLA Ops:
  0.6 12.3 %copy-start.6 = (s32[1,1,128]{2,1,0:T(1,128)S(1)}, s32[1,1,128]{2,1,0:T(1,128)}, u32[]{:S(2)}) copy-start(s32[1,1,128]{2,1,0:T(1,128)} %param.11) | copy-start | bytes 1540
  1.7 8.2 %collective-permute-start.1 = (bf16[64,2048]{1,0:T(8,128)(2,1)S(1)}, bf16[64,2048]{1,0:T(8,128)(2,1)S(1)}, u32[]{:S(2)}, u32[]{:S(2)}) collective-permute-start(bf16[64,2048]{1,0:T(8,128)(2,1)S(1)} %get-tuple-element.56), channel_id=1, source_target_pairs={{0,2},{1,3},{2,0},{3,1},{4,6},{5,7},{6,4},{7,5},{8,10},{9,11},{10,... | collective-permute-start | bytes 786440 | tf_op jit(solution)/shard_map/ppermute | solution.py:24
  3.9 7.1 %collective-permute-start = (bf16[64,2048]{1,0:T(8,128)(2,1)S(1)}, bf16[64,2048]{1,0:T(8,128)(2,1)S(1)}, u32[]{:S(2)}, u32[]{:S(2)}) collective-permute-start(bf16[64,2048]{1,0:T(8,128)(2,1)S(1)} %get-tuple-element.57.refs_0_), channel_id=1, source_target_pairs={{0,1},{1,0},{2,3},{3,2},{4,5},{5,4},{6,7},{7,6},{8,9},{9,8},{10,11... | collective-permute-start | bytes 786440 | tf_op jit(solution)/shard_map/ppermute | solution.py:24
  5.1 1.6 %copy-start = (bf16[1,128,8192]{2,1,0:T(8,128)(2,1)S(1)}, bf16[1,128,8192]{2,1,0:T(8,128)(2,1)}, u32[]{:S(2)}) copy-start(bf16[1,128,8192]{2,1,0:T(8,128)(2,1)} %param.6) | copy-start | bytes 6291460
  6.7 9.0 %copy-start.1 = (bf16[1,128,8192]{2,1,0:T(8,128)(2,1)S(1)}, bf16[1,128,8192]{2,1,0:T(8,128)(2,1)}, u32[]{:S(2)}) copy-start(bf16[1,128,8192]{2,1,0:T(8,128)(2,1)} %param.6) | copy-start | bytes 6291460
  6.7 11.0 %collective-permute-start.4 = (bf16[80,2048]{1,0:T(8,128)(2,1)S(1)}, bf16[80,2048]{1,0:T(8,128)(2,1)S(1)}, u32[]{:S(2)}, u32[]{:S(2)}) collective-permute-start(bf16[80,2048]{1,0:T(8,128)(2,1)S(1)} %get-tuple-element.33), channel_id=1, source_target_pairs={{0,1},{1,0},{2,3},{3,2},{4,5},{5,4},{6,7},{7,6},{8,9},{9,8},{10,11... | collective-permute-start | bytes 983048 | tf_op jit(solution)/shard_map/ppermute | solution.py:24
  7.1 11.7 %collective-permute-start.5 = (bf16[80,2048]{1,0:T(8,128)(2,1)S(1)}, bf16[80,2048]{1,0:T(8,128)(2,1)S(1)}, u32[]{:S(2)}, u32[]{:S(2)}) collective-permute-start(bf16[80,2048]{1,0:T(8,128)(2,1)S(1)} %get-tuple-element.34), channel_id=1, source_target_pairs={{0,2},{1,3},{2,0},{3,1},{4,6},{5,7},{6,4},{7,5},{8,10},{9,11},{10,... | collective-permute-start | bytes 983048 | tf_op jit(solution)/shard_map/ppermute | solution.py:24
  9.9 13.5 %collective-permute-start.3 = (bf16[64,2048]{1,0:T(8,128)(2,1)S(1)}, bf16[64,2048]{1,0:T(8,128)(2,1)S(1)}, u32[]{:S(2)}, u32[]{:S(2)}) collective-permute-start(bf16[64,2048]{1,0:T(8,128)(2,1)S(1)} %collective-permute-done.1.refs_2_), channel_id=1, source_target_pairs={{0,1},{1,0},{2,3},{3,2},{4,5},{5,4},{6,7},{7,6},{8,9},{9,8},{10,11... | collective-permute-start | bytes 786440 | tf_op jit(solution)/shard_map/ppermute | solution.py:24
  11.0 12.3 %collective-permute-start.2 = (bf16[64,2048]{1,0:T(8,128)(2,1)S(1)}, bf16[64,2048]{1,0:T(8,128)(2,1)S(1)}, u32[]{:S(2)}, u32[]{:S(2)}) collective-permute-start(bf16[64,2048]{1,0:T(8,128)(2,1)S(1)} %collective-permute-done.refs_1_), channel_id=1, source_target_pairs={{0,2},{1,3},{2,0},{3,1},{4,6},{5,7},{6,4},{7,5},{8,10},{9,11},{10,... | collective-permute-start | bytes 786440 | tf_op jit(solution)/shard_map/ppermute | solution.py:24
  12.9 1.6 %copy-start.3 = (bf16[1,2048,512]{2,1,0:T(8,128)(2,1)S(1)}, bf16[1,2048,512]{2,1,0:T(8,128)(2,1)}, u32[]{:S(2)}) copy-start(bf16[1,2048,512]{2,1,0:T(8,128)(2,1)} %param.9) | copy-start | bytes 6291460
  15.6 3.2 %copy-start.2 = (bf16[1,2048,512]{2,1,0:T(8,128)(2,1)S(1)}, bf16[1,2048,512]{2,1,0:T(8,128)(2,1)}, u32[]{:S(2)}) copy-start(bf16[1,2048,512]{2,1,0:T(8,128)(2,1)} %param.8) | copy-start | bytes 6291460
  15.8 11.8 %collective-permute-start.8 = (bf16[48,2048]{1,0:T(8,128)(2,1)S(1)}, bf16[48,2048]{1,0:T(8,128)(2,1)S(1)}, u32[]{:S(2)}, u32[]{:S(2)}) collective-permute-start(bf16[48,2048]{1,0:T(8,128)(2,1)S(1)} %get-tuple-element.39), channel_id=1, source_target_pairs={{0,1},{1,0},{2,3},{3,2},{4,5},{5,4},{6,7},{7,6},{8,9},{9,8},{10,11... | collective-permute-start | bytes 589832 | tf_op jit(solution)/shard_map/ppermute | solution.py:24
  17.7 9.8 %collective-permute-start.9 = (bf16[48,2048]{1,0:T(8,128)(2,1)S(1)}, bf16[48,2048]{1,0:T(8,128)(2,1)S(1)}, u32[]{:S(2)}, u32[]{:S(2)}) collective-permute-start(bf16[48,2048]{1,0:T(8,128)(2,1)S(1)} %get-tuple-element.40), channel_id=1, source_target_pairs={{0,2},{1,3},{2,0},{3,1},{4,6},{5,7},{6,4},{7,5},{8,10},{9,11},{10,... | collective-permute-start | bytes 589832 | tf_op jit(solution)/shard_map/ppermute | solution.py:24
  24.1 9.1 %collective-permute-start.6 = (bf16[128,512]{1,0:T(8,128)(2,1)S(1)}, bf16[128,512]{1,0:T(8,128)(2,1)S(1)}, u32[]{:S(2)}, u32[]{:S(2)}) collective-permute-start(bf16[128,512]{1,0:T(8,128)(2,1)S(1)} %get-tuple-element.37.refs_3_), channel_id=1, source_target_pairs={{0,3},{1,2},{2,1},{3,0},{4,7},{5,6},{6,5},{7,4},{8,11},{9,10},{10,... | collective-permute-start | bytes 393224 | tf_op jit(solution)/shard_map/ppermute | solution.py:24
  25.4 6.7 %collective-permute-start.7 = (bf16[80,512]{1,0:T(8,128)(2,1)S(1)}, bf16[80,512]{1,0:T(8,128)(2,1)S(1)}, u32[]{:S(2)}, u32[]{:S(2)}) collective-permute-start(bf16[80,512]{1,0:T(8,128)(2,1)S(1)} %get-tuple-element.38), channel_id=1, source_target_pairs={{0,1},{1,0},{2,3},{3,2},{4,5},{5,4},{6,7},{7,6},{8,9},{9,8},{10,11... | collective-permute-start | bytes 245768 | tf_op jit(solution)/shard_map/ppermute | solution.py:24
  25.7 6.4 %collective-permute-start.11 = (bf16[80,512]{1,0:T(8,128)(2,1)S(1)}, bf16[80,512]{1,0:T(8,128)(2,1)S(1)}, u32[]{:S(2)}, u32[]{:S(2)}) collective-permute-start(bf16[80,512]{1,0:T(8,128)(2,1)S(1)} %get-tuple-element.35.refs_4_), channel_id=1, source_target_pairs={{0,2},{1,3},{2,0},{3,1},{4,6},{5,7},{6,4},{7,5},{8,10},{9,11},{10,... | collective-permute-start | bytes 245768 | tf_op jit(solution)/shard_map/ppermute | solution.py:24
  27.4 5.8 %copy-start.5 = (bf16[1,128,512]{2,1,0:T(8,128)(2,1)S(1)}, bf16[1,128,512]{2,1,0:T(8,128)(2,1)}, u32[]{:S(2)}) copy-start(bf16[1,128,512]{2,1,0:T(8,128)(2,1)} %param.7) | copy-start | bytes 393220
  28.0 15.4 %copy-start.4 = (bf16[1,2048,512]{2,1,0:T(8,128)(2,1)S(1)}, bf16[1,2048,512]{2,1,0:T(8,128)(2,1)}, u32[]{:S(2)}) copy-start(bf16[1,2048,512]{2,1,0:T(8,128)(2,1)} %param.9) | copy-start | bytes 6291460
  28.1 4.1 %collective-permute-start.12 = (bf16[48,512]{1,0:T(8,128)(2,1)S(1)}, bf16[48,512]{1,0:T(8,128)(2,1)S(1)}, u32[]{:S(2)}, u32[]{:S(2)}) collective-permute-start(bf16[48,512]{1,0:T(8,128)(2,1)S(1)} %get-tuple-element.44), channel_id=1, source_target_pairs={{0,2},{1,3},{2,0},{3,1},{4,6},{5,7},{6,4},{7,5},{8,10},{9,11},{10,... | collective-permute-start | bytes 147464 | tf_op jit(solution)/shard_map/ppermute | solution.py:24
  28.5 4.7 %collective-permute-start.10 = (bf16[48,512]{1,0:T(8,128)(2,1)S(1)}, bf16[48,512]{1,0:T(8,128)(2,1)S(1)}, u32[]{:S(2)}, u32[]{:S(2)}) collective-permute-start(bf16[48,512]{1,0:T(8,128)(2,1)S(1)} %get-tuple-element.43.refs_4_), channel_id=1, source_target_pairs={{0,1},{1,0},{2,3},{3,2},{4,5},{5,4},{6,7},{7,6},{8,9},{9,8},{10,11... | collective-permute-start | bytes 147464 | tf_op jit(solution)/shard_map/ppermute | solution.py:24
  33.3 5.2 %collective-permute-start.15 = (bf16[128,512]{1,0:T(8,128)(2,1)S(1)}, bf16[128,512]{1,0:T(8,128)(2,1)S(1)}, u32[]{:S(2)}, u32[]{:S(2)}) collective-permute-start(bf16[128,512]{1,0:T(8,128)(2,1)S(1)} %slope.1.refs_0_), channel_id=1, source_target_pairs={{0,3},{1,2},{2,1},{3,0},{4,7},{5,6},{6,5},{7,4},{8,11},{9,10},{10,... | collective-permute-start | bytes 393224 | tf_op jit(solution)/shard_map/ppermute | solution.py:24
  34.4 5.2 %collective-permute-start.14 = (bf16[128,512]{1,0:T(8,128)(2,1)S(1)}, bf16[128,512]{1,0:T(8,128)(2,1)S(1)}, u32[]{:S(2)}, u32[]{:S(2)}) collective-permute-start(bf16[128,512]{1,0:T(8,128)(2,1)S(1)} %slope.1.refs_0_), channel_id=1, source_target_pairs={{0,2},{1,3},{2,0},{3,1},{4,6},{5,7},{6,4},{7,5},{8,10},{9,11},{10,... | collective-permute-start | bytes 393224 | tf_op jit(solution)/shard_map/ppermute | solution.py:24
  35.6 3.9 %collective-permute-start.13 = (bf16[128,512]{1,0:T(8,128)(2,1)S(1)}, bf16[128,512]{1,0:T(8,128)(2,1)S(1)}, u32[]{:S(2)}, u32[]{:S(2)}) collective-permute-start(bf16[128,512]{1,0:T(8,128)(2,1)S(1)} %slope.1.refs_0_), channel_id=1, source_target_pairs={{0,1},{1,0},{2,3},{3,2},{4,5},{5,4},{6,7},{7,6},{8,9},{9,8},{10,11... | collective-permute-start | bytes 393224 | tf_op jit(solution)/shard_map/ppermute | solution.py:24
  39.8 6.1 %collective-permute-start.16 = (bf16[144,128]{1,0:T(8,128)(2,1)S(1)}, bf16[144,128]{1,0:T(8,128)(2,1)S(1)}, u32[]{:S(2)}, u32[]{:S(2)}) collective-permute-start(bf16[144,128]{1,0:T(8,128)(2,1)S(1)} %kept.1.refs_0_), channel_id=1, source_target_pairs={{0,24},{4,28},{8,16},{12,20},{16,8},{20,12},{24,0},{28,4},{1,25},{... | collective-permute-start | bytes 110600 | tf_op jit(solution)/shard_map/ppermute | solution.py:24
  43.1 3.7 %collective-permute-start.17 = (bf16[144,128]{1,0:T(8,128)(2,1)S(1)}, bf16[144,128]{1,0:T(8,128)(2,1)S(1)}, u32[]{:S(2)}, u32[]{:S(2)}) collective-permute-start(bf16[144,128]{1,0:T(8,128)(2,1)S(1)} %kept.1.refs_0_), channel_id=1, source_target_pairs={{0,16},{4,20},{8,24},{12,28},{16,0},{20,4},{24,8},{28,12},{1,17},{... | collective-permute-start | bytes 110600 | tf_op jit(solution)/shard_map/ppermute | solution.py:24
  43.1 3.7 %collective-permute-start.18 = (bf16[144,128]{1,0:T(8,128)(2,1)S(1)}, bf16[144,128]{1,0:T(8,128)(2,1)S(1)}, u32[]{:S(2)}, u32[]{:S(2)}) collective-permute-start(bf16[144,128]{1,0:T(8,128)(2,1)S(1)} %kept.1.refs_0_), channel_id=1, source_target_pairs={{0,8},{4,12},{8,0},{12,4},{16,24},{20,28},{24,16},{28,20},{1,9},{5... | collective-permute-start | bytes 110600 | tf_op jit(solution)/shard_map/ppermute | solution.py:24
  46.9 8.8 %collective-permute-start.19 = (bf16[576,128]{1,0:T(8,128)(2,1)S(1)}, bf16[576,128]{1,0:T(8,128)(2,1)S(1)}, u32[]{:S(2)}, u32[]{:S(2)}) collective-permute-start(bf16[576,128]{1,0:T(8,128)(2,1)S(1)} %join.5.group), channel_id=1, source_target_pairs={{0,4},{4,0},{8,12},{12,8},{16,20},{20,16},{24,28},{28,24},{1,5},{5... | collective-permute-start | bytes 442376 | tf_op jit(solution)/shard_map/ppermute | solution.py:24

commit v19 on v18

--- a/solution.py
+++ b/solution.py
@@ -378,7 +378,7 @@
     n_shard, n_rep = lax.axis_size("shard"), lax.axis_size("rep")
     tok_dev = tokens.shape[0]
     depth, kw = w.shape
-    early_rows = tok_dev * 5 // 8
+    early_rows = tok_dev * 3 // 8
     spans = [(0, early_rows), (early_rows, tok_dev)]
     per_row = kw // LANES
     slot_row = blocks[0]

time: 58.4 us -> 64.8 us (1.11)
  waiting for transfers between devices: 15.5 us -> 19.6 us
  starting transfers between devices: 24.9 us -> 26.9 us
    ppermute x20, waiting for transfers between devices: 15.5 us -> 19.6 us  [swap(): return lax.ppermute(x, axis, [(i, i ^ d) for i in range(n)])]
    ppermute x20, starting transfers between devices: 24.9 us -> 26.9 us  [swap(): return lax.ppermute(x, axis, [(i, i ^ d) for i in range(n)])]
  transfers between devices with their start and end apart: 20 -> 20, of which waited for: 9 -> 8; matrix products, arithmetic and copies ran while one was open for 0% -> 0% of each run, Pallas kernels for 16% -> 14%
where the time goes in v19:
time: 64.8 us; the launch traced here: 64.6 us
  starting transfers between devices  26.9 us (42%)
  waiting for transfers between devices  19.6 us (30%)
  Pallas kernels  12.1 us (19%)
  local copies, waits for them, and re-layouts  4.27 us (7%)
  between operations  1.74 us (3%)
    ppermute x20, starting transfers between devices, swap(): return lax.ppermute(x, axis, [(i, i ^ d) for i in range(n)])  26.9 us
    ppermute x20, waiting for transfers between devices, swap(): return lax.ppermute(x, axis, [(i, i ^ d) for i in range(n)])  19.6 us
    unnamed x14, local copies, waits for them, and re-layouts  3.2 us
    pallas_call x1, Pallas kernels, outer(): pl.pallas_call(functools.partial(outer_kernel, cap, kw // LANES, tile, n)...  2.54 us
    pallas_call x1, Pallas kernels, residue(): pl.pallas_call(functools.partial(residue_kernel, order, tile), out_shape=...  2.39 us
    pallas_call x3, Pallas kernels, project(): pl.pallas_call(functools.partial(project_kernel, n, len(outs)), out_shape...  1.7 us
    pallas_call x2, Pallas kernels, prepare(): pl.pallas_call(functools.partial(prepare_kernel, per_row, len(xs)), out_s...  1.56 us
    pallas_call x1, Pallas kernels, outer(): pl.pallas_call(functools.partial(half_kernel, cap, kw // LANES, tile), ou...  1.41 us
  transfers between devices with their start and end apart: 20, of which 8 were waited for; matrix products, arithmetic and copies ran while one was open for 0% of the time, Pallas kernels for 14%

profile of v19, /device:TPU:1, one launch (start us, length us, event | category | flops | bytes accessed | tf_op | source)
XLA Modules:
  0.0 64.6 jit_solution(10819563483199298548)
XLA Ops:
  0.6 1.1 %dynamic-slice_bitcast_fusion = (bf16[64,2048]{1,0:T(8,128)(2,1)S(1)}, bf16[64,2048]{1,0:T(8,128)(2,1)S(1)}) fusion(bf16[1,128,8192]{2,1,0:T(8,128)(2,1)} %param.6, s32[]{:T(128)S(6)} %select_n.4), kind=kLoop, calls=%fused_computation | loop fusion | bytes 1048580 | tf_op jit(solution)/shard_map/dynamic_slice | solution.py:392
  1.7 2.1 %collective-permute-start.1 = (bf16[64,2048]{1,0:T(8,128)(2,1)S(1)}, bf16[64,2048]{1,0:T(8,128)(2,1)S(1)}, u32[]{:S(2)}, u32[]{:S(2)}) collective-permute-start(bf16[64,2048]{1,0:T(8,128)(2,1)S(1)} %get-tuple-element.56), channel_id=1, source_target_pairs={{0,2},{1,3},{2,0},{3,1},{4,6},{5,7},{6,4},{7,5},{8,10},{9,11},{10,... | collective-permute-start | bytes 786440 | tf_op jit(solution)/shard_map/ppermute | solution.py:24
  3.9 1.2 %collective-permute-start = (bf16[64,2048]{1,0:T(8,128)(2,1)S(1)}, bf16[64,2048]{1,0:T(8,128)(2,1)S(1)}, u32[]{:S(2)}, u32[]{:S(2)}) collective-permute-start(bf16[64,2048]{1,0:T(8,128)(2,1)S(1)} %get-tuple-element.57.refs_0_), channel_id=1, source_target_pairs={{0,1},{1,0},{2,3},{3,2},{4,5},{5,4},{6,7},{7,6},{8,9},{9,8},{10,11... | collective-permute-start | bytes 786440 | tf_op jit(solution)/shard_map/ppermute | solution.py:24
  5.1 1.6 %copy-done = bf16[1,128,8192]{2,1,0:T(8,128)(2,1)S(1)} copy-done((bf16[1,128,8192]{2,1,0:T(8,128)(2,1)S(1)}, bf16[1,128,8192]{2,1,0:T(8,128)(2,1)}, u32[]{:S(2)}) %copy-start) | copy-done | bytes 2097176
  8.0 1.6 %copy-done.3 = bf16[1,2048,512]{2,1,0:T(8,128)(2,1)S(1)} copy-done((bf16[1,2048,512]{2,1,0:T(8,128)(2,1)S(1)}, bf16[1,2048,512]{2,1,0:T(8,128)(2,1)}, u32[]{:S(2)}) %copy-start.3) | copy-done | bytes 2097176
  9.6 1.1 %early.1 = (f32[128,128]{1,0:T(8,128)S(1)}, bf16[2048,512]{1,0:T(8,128)(2,1)S(1)}, f32[8,128]{1,0:T(8,128)S(1)}) custom-call(s32[1,128]{1,0:T(1,128)S(1)} %bitcast.19, s32[1,1]{1,0:T(1,128)S(6)} %copy.8.count.refs_2_.refs_3_, bf16[2048,512]{1,0:T(8,128)(2,1)S(1)} %bitcast.16, f32[8,128]{1,0:T(8,128)S(1)} %get-tuple-element.29.after), custom_call_target="tpu_custom_call" | custom-call | flops 1000 | bytes 1000 | tf_op jit(solution)/shard_map/early/pallas_call | solution.py:145
  10.8 1.3 %collective-permute-start.8 = (bf16[80,2048]{1,0:T(8,128)(2,1)S(1)}, bf16[80,2048]{1,0:T(8,128)(2,1)S(1)}, u32[]{:S(2)}, u32[]{:S(2)}) collective-permute-start(bf16[80,2048]{1,0:T(8,128)(2,1)S(1)} %get-tuple-element.39), channel_id=1, source_target_pairs={{0,1},{1,0},{2,3},{3,2},{4,5},{5,4},{6,7},{7,6},{8,9},{9,8},{10,11... | collective-permute-start | bytes 983048 | tf_op jit(solution)/shard_map/ppermute | solution.py:24
  12.7 1.1 %collective-permute-start.2 = (bf16[64,2048]{1,0:T(8,128)(2,1)S(1)}, bf16[64,2048]{1,0:T(8,128)(2,1)S(1)}, u32[]{:S(2)}, u32[]{:S(2)}) collective-permute-start(bf16[64,2048]{1,0:T(8,128)(2,1)S(1)} %collective-permute-done.refs_1_), channel_id=1, source_target_pairs={{0,2},{1,3},{2,0},{3,1},{4,6},{5,7},{6,4},{7,5},{8,10},{9,11},{10,... | collective-permute-start | bytes 786440 | tf_op jit(solution)/shard_map/ppermute | solution.py:24
  13.8 1.1 %collective-permute-done.4.refs_0_ = bf16[48,2048]{1,0:T(8,128)(2,1)S(1)} collective-permute-done((bf16[48,2048]{1,0:T(8,128)(2,1)S(1)}, bf16[48,2048]{1,0:T(8,128)(2,1)S(1)}, u32[]{:S(2)}, u32[]{:S(2)}) %collective-permute-start.4) | collective-permute-done | bytes 196640 | tf_op jit(solution)/shard_map/ppermute | solution.py:24
  15.3 12.2 %collective-permute-done.5.refs_1_ = bf16[48,2048]{1,0:T(8,128)(2,1)S(1)} collective-permute-done((bf16[48,2048]{1,0:T(8,128)(2,1)S(1)}, bf16[48,2048]{1,0:T(8,128)(2,1)S(1)}, u32[]{:S(2)}, u32[]{:S(2)}) %collective-permute-start.5) | collective-permute-done | bytes 196640 | tf_op jit(solution)/shard_map/ppermute | solution.py:24
  27.5 0.5 project.3
  28.0 0.6 %cut.5 = (bf16[128,2048]{1,0:T(8,128)(2,1)S(1)}, f32[8,128]{1,0:T(8,128)}) custom-call(bf16[128,8192]{1,0:T(8,128)(2,1)S(1)} %bitcast.12, f32[8,128]{1,0:T(8,128)S(1)} %get-tuple-element.31.refs_0_), custom_call_target="tpu_custom_call" | custom-call | flops 1000 | bytes 1000 | tf_op jit(solution)/shard_map/cut/pallas_call | solution.py:43
  28.7 0.7 %project.4 = (f32[128,512]{1,0:T(8,128)S(1)}, bf16[128,512]{1,0:T(8,128)(2,1)S(1)}, bf16[256,2048]{1,0:T(8,128)(2,1)S(1)}) custom-call(bf16[128,2048]{1,0:T(8,128)(2,1)S(1)} %get-tuple-element.32.refs_0_, bf16[64,2048]{1,0:T(8,128)(2,1)S(1)} %collective-permute-done.2.refs_1_, bf16[64,2048]{1,0:T(8,128)(2,1)S(1)} %collective-permute-done.3.refs_2_, ...), custom_call_target="tpu_custom_call" | custom-call | flops 1000 | bytes 1000 | tf_op jit(solution)/shard_map/project/pallas_call | solution.py:73
  29.4 1.1 %collective-permute-start.6 = (bf16[128,512]{1,0:T(8,128)(2,1)S(1)}, bf16[128,512]{1,0:T(8,128)(2,1)S(1)}, u32[]{:S(2)}, u32[]{:S(2)}) collective-permute-start(bf16[128,512]{1,0:T(8,128)(2,1)S(1)} %get-tuple-element.37.refs_3_), channel_id=1, source_target_pairs={{0,3},{1,2},{2,1},{3,0},{4,7},{5,6},{6,5},{7,4},{8,11},{9,10},{10,... | collective-permute-start | bytes 393224 | tf_op jit(solution)/shard_map/ppermute | solution.py:24
  30.4 0.6 prepare.2
  31.1 0.5 project.5
  31.6 0.5 collective-permute-start.12
  32.1 1.2 %collective-permute-start.10 = (bf16[80,512]{1,0:T(8,128)(2,1)S(1)}, bf16[80,512]{1,0:T(8,128)(2,1)S(1)}, u32[]{:S(2)}, u32[]{:S(2)}) collective-permute-start(bf16[80,512]{1,0:T(8,128)(2,1)S(1)} %get-tuple-element.43.refs_4_), channel_id=1, source_target_pairs={{0,1},{1,0},{2,3},{3,2},{4,5},{5,4},{6,7},{7,6},{8,9},{9,8},{10,11... | collective-permute-start | bytes 245768 | tf_op jit(solution)/shard_map/ppermute | solution.py:24
  33.6 1.0 %collective-permute-start.11 = (bf16[48,512]{1,0:T(8,128)(2,1)S(1)}, bf16[48,512]{1,0:T(8,128)(2,1)S(1)}, u32[]{:S(2)}, u32[]{:S(2)}) collective-permute-start(bf16[48,512]{1,0:T(8,128)(2,1)S(1)} %get-tuple-element.35.refs_4_), channel_id=1, source_target_pairs={{0,2},{1,3},{2,0},{3,1},{4,6},{5,7},{6,4},{7,5},{8,10},{9,11},{10,... | collective-permute-start | bytes 147464 | tf_op jit(solution)/shard_map/ppermute | solution.py:24
  34.6 1.0 %prepare.3 = (bf16[128,256]{1,0:T(8,128)(2,1)S(1)}, bf16[2048,256]{1,0:T(8,128)(2,1)S(1)}, f32[8,128]{1,0:T(8,128)S(1)}) custom-call(bf16[96,2048]{1,0:T(8,128)(2,1)S(1)} %get-tuple-element.45.refs_0_, bf16[160,2048]{1,0:T(8,128)(2,1)S(1)} %get-tuple-element.46.refs_1_, s32[1,128]{1,0:T(1,128)S(1)} %bitcast.21, s32[1,1]{1,0:T(1,128)S(6)} %copy.8.count.refs_2_.refs_3_, ...), custom_call_target="tpu_custom_call" | custom-call | flops 1000 | bytes 1000 | tf_op jit(solution)/shard_map/prepare/pallas_call | solution.py:181
  35.6 0.7 %collective-permute-done.7.refs_3_ = bf16[48,512]{1,0:T(8,128)(2,1)S(1)} collective-permute-done((bf16[48,512]{1,0:T(8,128)(2,1)S(1)}, bf16[48,512]{1,0:T(8,128)(2,1)S(1)}, u32[]{:S(2)}, u32[]{:S(2)}) %collective-permute-start.7) | collective-permute-done | bytes 49184 | tf_op jit(solution)/shard_map/ppermute | solution.py:24
  36.6 1.4 %collective-permute-start.15 = (bf16[128,512]{1,0:T(8,128)(2,1)S(1)}, bf16[128,512]{1,0:T(8,128)(2,1)S(1)}, u32[]{:S(2)}, u32[]{:S(2)}) collective-permute-start(bf16[128,512]{1,0:T(8,128)(2,1)S(1)} %slope.1.refs_0_), channel_id=1, source_target_pairs={{0,3},{1,2},{2,1},{3,0},{4,7},{5,6},{6,5},{7,4},{8,11},{9,10},{10,... | collective-permute-start | bytes 393224 | tf_op jit(solution)/shard_map/ppermute | solution.py:24
  38.1 1.1 %collective-permute-start.14 = (bf16[128,512]{1,0:T(8,128)(2,1)S(1)}, bf16[128,512]{1,0:T(8,128)(2,1)S(1)}, u32[]{:S(2)}, u32[]{:S(2)}) collective-permute-start(bf16[128,512]{1,0:T(8,128)(2,1)S(1)} %slope.1.refs_0_), channel_id=1, source_target_pairs={{0,2},{1,3},{2,0},{3,1},{4,6},{5,7},{6,4},{7,5},{8,10},{9,11},{10,... | collective-permute-start | bytes 393224 | tf_op jit(solution)/shard_map/ppermute | solution.py:24
  39.4 3.3 %collective-permute-done.15.refs_1_ = bf16[128,512]{1,0:T(8,128)(2,1)S(1)} collective-permute-done((bf16[128,512]{1,0:T(8,128)(2,1)S(1)}, bf16[128,512]{1,0:T(8,128)(2,1)S(1)}, u32[]{:S(2)}, u32[]{:S(2)}) %collective-permute-start.15) | collective-permute-done | bytes 131104 | tf_op jit(solution)/shard_map/ppermute | solution.py:24
  42.8 0.9 %collective-permute-done.14.refs_1_.refs_3_ = bf16[128,512]{1,0:T(8,128)(2,1)S(1)} collective-permute-done((bf16[128,512]{1,0:T(8,128)(2,1)S(1)}, bf16[128,512]{1,0:T(8,128)(2,1)S(1)}, u32[]{:S(2)}, u32[]{:S(2)}) %collective-permute-start.14) | collective-permute-done | bytes 131104 | tf_op jit(solution)/shard_map/ppermute | solution.py:24
  44.3 3.1 %collective-permute-start.16 = (bf16[144,128]{1,0:T(8,128)(2,1)S(1)}, bf16[144,128]{1,0:T(8,128)(2,1)S(1)}, u32[]{:S(2)}, u32[]{:S(2)}) collective-permute-start(bf16[144,128]{1,0:T(8,128)(2,1)S(1)} %kept.1.refs_0_), channel_id=1, source_target_pairs={{0,24},{4,28},{8,16},{12,20},{16,8},{20,12},{24,0},{28,4},{1,25},{... | collective-permute-start | bytes 110600 | tf_op jit(solution)/shard_map/ppermute | solution.py:24
  47.5 0.5 collective-permute-start.18
  48.0 2.4 %residue.1 = (bf16[2048,512]{1,0:T(8,128)(2,1)}, f32[8,128]{1,0:T(8,128)S(1)}) custom-call(bf16[128,512]{1,0:T(8,128)(2,1)S(1)} %slope.1.refs_0_, bf16[128,512]{1,0:T(8,128)(2,1)S(1)} %collective-permute-done.15.refs_1_, bf16[128,512]{1,0:T(8,128)(2,1)S(1)} %collective-permute-done.13.refs_0_.refs_2_, ...), custom_call_target="tpu_custom_call" | custom-call | flops 1000 | bytes 1000 | tf_op jit(solution)/shard_map/residue/pallas_call | solution.py:274
  50.4 0.8 %collective-permute-done.17.refs_1_ = bf16[144,128]{1,0:T(8,128)(2,1)S(1)} collective-permute-done((bf16[144,128]{1,0:T(8,128)(2,1)S(1)}, bf16[144,128]{1,0:T(8,128)(2,1)S(1)}, u32[]{:S(2)}, u32[]{:S(2)}) %collective-permute-start.17) | collective-permute-done | bytes 36896 | tf_op jit(solution)/shard_map/ppermute | solution.py:24
  51.2 9.4 %collective-permute-start.19 = (bf16[576,128]{1,0:T(8,128)(2,1)S(1)}, bf16[576,128]{1,0:T(8,128)(2,1)S(1)}, u32[]{:S(2)}, u32[]{:S(2)}) collective-permute-start(bf16[576,128]{1,0:T(8,128)(2,1)S(1)} %join.5.group), channel_id=1, source_target_pairs={{0,4},{4,0},{8,12},{12,8},{16,20},{20,16},{24,28},{28,24},{1,5},{5... | collective-permute-start | bytes 442376 | tf_op jit(solution)/shard_map/ppermute | solution.py:24
  60.6 1.4 %half.1 = f32[2048,512]{1,0:T(8,128)S(1)} custom-call(bf16[576,128]{1,0:T(8,128)(2,1)S(1)} %join.5.group), custom_call_target="tpu_custom_call" | custom-call | flops 1000 | bytes 1000 | tf_op jit(solution)/shard_map/half/pallas_call | solution.py:356
  62.1 2.5 %outer.1 = f32[2048,512]{1,0:T(8,128)} custom-call(bf16[576,128]{1,0:T(8,128)(2,1)S(1)} %collective-permute-done.19.group, f32[2048,512]{1,0:T(8,128)S(1)} %half.1), custom_call_target="tpu_custom_call" | custom-call | flops 1000 | bytes 1000 | tf_op jit(solution)/shard_map/outer/pallas_call | solution.py:364
  (41 shorter events, 3.3 us)
Async XLA Ops:
  0.6 7.3 %copy-start.6 = (s32[1,1,128]{2,1,0:T(1,128)S(1)}, s32[1,1,128]{2,1,0:T(1,128)}, u32[]{:S(2)}) copy-start(s32[1,1,128]{2,1,0:T(1,128)} %param.11) | copy-start | bytes 1540
  1.7 8.9 %collective-permute-start.1 = (bf16[64,2048]{1,0:T(8,128)(2,1)S(1)}, bf16[64,2048]{1,0:T(8,128)(2,1)S(1)}, u32[]{:S(2)}, u32[]{:S(2)}) collective-permute-start(bf16[64,2048]{1,0:T(8,128)(2,1)S(1)} %get-tuple-element.56), channel_id=1, source_target_pairs={{0,2},{1,3},{2,0},{3,1},{4,6},{5,7},{6,4},{7,5},{8,10},{9,11},{10,... | collective-permute-start | bytes 786440 | tf_op jit(solution)/shard_map/ppermute | solution.py:24
  3.9 6.9 %collective-permute-start = (bf16[64,2048]{1,0:T(8,128)(2,1)S(1)}, bf16[64,2048]{1,0:T(8,128)(2,1)S(1)}, u32[]{:S(2)}, u32[]{:S(2)}) collective-permute-start(bf16[64,2048]{1,0:T(8,128)(2,1)S(1)} %get-tuple-element.57.refs_0_), channel_id=1, source_target_pairs={{0,1},{1,0},{2,3},{3,2},{4,5},{5,4},{6,7},{7,6},{8,9},{9,8},{10,11... | collective-permute-start | bytes 786440 | tf_op jit(solution)/shard_map/ppermute | solution.py:24
  5.1 1.6 %copy-start = (bf16[1,128,8192]{2,1,0:T(8,128)(2,1)S(1)}, bf16[1,128,8192]{2,1,0:T(8,128)(2,1)}, u32[]{:S(2)}) copy-start(bf16[1,128,8192]{2,1,0:T(8,128)(2,1)} %param.6) | copy-start | bytes 6291460
  6.7 4.1 %copy-start.1 = (bf16[1,128,8192]{2,1,0:T(8,128)(2,1)S(1)}, bf16[1,128,8192]{2,1,0:T(8,128)(2,1)}, u32[]{:S(2)}) copy-start(bf16[1,128,8192]{2,1,0:T(8,128)(2,1)} %param.6) | copy-start | bytes 6291460
  6.8 8.2 %collective-permute-start.4 = (bf16[48,2048]{1,0:T(8,128)(2,1)S(1)}, bf16[48,2048]{1,0:T(8,128)(2,1)S(1)}, u32[]{:S(2)}, u32[]{:S(2)}) collective-permute-start(bf16[48,2048]{1,0:T(8,128)(2,1)S(1)} %get-tuple-element.33), channel_id=1, source_target_pairs={{0,1},{1,0},{2,3},{3,2},{4,5},{5,4},{6,7},{7,6},{8,9},{9,8},{10,11... | collective-permute-start | bytes 589832 | tf_op jit(solution)/shard_map/ppermute | solution.py:24
  8.0 1.6 %copy-start.3 = (bf16[1,2048,512]{2,1,0:T(8,128)(2,1)S(1)}, bf16[1,2048,512]{2,1,0:T(8,128)(2,1)}, u32[]{:S(2)}) copy-start(bf16[1,2048,512]{2,1,0:T(8,128)(2,1)} %param.9) | copy-start | bytes 6291460
  9.6 17.9 %copy-start.2 = (bf16[1,2048,512]{2,1,0:T(8,128)(2,1)S(1)}, bf16[1,2048,512]{2,1,0:T(8,128)(2,1)}, u32[]{:S(2)}) copy-start(bf16[1,2048,512]{2,1,0:T(8,128)(2,1)} %param.8) | copy-start | bytes 6291460
  10.8 20.3 %collective-permute-start.8 = (bf16[80,2048]{1,0:T(8,128)(2,1)S(1)}, bf16[80,2048]{1,0:T(8,128)(2,1)S(1)}, u32[]{:S(2)}, u32[]{:S(2)}) collective-permute-start(bf16[80,2048]{1,0:T(8,128)(2,1)S(1)} %get-tuple-element.39), channel_id=1, source_target_pairs={{0,1},{1,0},{2,3},{3,2},{4,5},{5,4},{6,7},{7,6},{8,9},{9,8},{10,11... | collective-permute-start | bytes 983048 | tf_op jit(solution)/shard_map/ppermute | solution.py:24
  12.1 19.0 %collective-permute-start.9 = (bf16[80,2048]{1,0:T(8,128)(2,1)S(1)}, bf16[80,2048]{1,0:T(8,128)(2,1)S(1)}, u32[]{:S(2)}, u32[]{:S(2)}) collective-permute-start(bf16[80,2048]{1,0:T(8,128)(2,1)S(1)} %get-tuple-element.40), channel_id=1, source_target_pairs={{0,2},{1,3},{2,0},{3,1},{4,6},{5,7},{6,4},{7,5},{8,10},{9,11},{10,... | collective-permute-start | bytes 983048 | tf_op jit(solution)/shard_map/ppermute | solution.py:24
  12.4 16.2 %collective-permute-start.3 = (bf16[64,2048]{1,0:T(8,128)(2,1)S(1)}, bf16[64,2048]{1,0:T(8,128)(2,1)S(1)}, u32[]{:S(2)}, u32[]{:S(2)}) collective-permute-start(bf16[64,2048]{1,0:T(8,128)(2,1)S(1)} %collective-permute-done.1.refs_2_), channel_id=1, source_target_pairs={{0,1},{1,0},{2,3},{3,2},{4,5},{5,4},{6,7},{7,6},{8,9},{9,8},{10,11... | collective-permute-start | bytes 786440 | tf_op jit(solution)/shard_map/ppermute | solution.py:24
  12.7 15.9 %collective-permute-start.2 = (bf16[64,2048]{1,0:T(8,128)(2,1)S(1)}, bf16[64,2048]{1,0:T(8,128)(2,1)S(1)}, u32[]{:S(2)}, u32[]{:S(2)}) collective-permute-start(bf16[64,2048]{1,0:T(8,128)(2,1)S(1)} %collective-permute-done.refs_1_), channel_id=1, source_target_pairs={{0,2},{1,3},{2,0},{3,1},{4,6},{5,7},{6,4},{7,5},{8,10},{9,11},{10,... | collective-permute-start | bytes 786440 | tf_op jit(solution)/shard_map/ppermute | solution.py:24
  14.9 12.6 %collective-permute-start.5 = (bf16[48,2048]{1,0:T(8,128)(2,1)S(1)}, bf16[48,2048]{1,0:T(8,128)(2,1)S(1)}, u32[]{:S(2)}, u32[]{:S(2)}) collective-permute-start(bf16[48,2048]{1,0:T(8,128)(2,1)S(1)} %get-tuple-element.34), channel_id=1, source_target_pairs={{0,2},{1,3},{2,0},{3,1},{4,6},{5,7},{6,4},{7,5},{8,10},{9,11},{10,... | collective-permute-start | bytes 589832 | tf_op jit(solution)/shard_map/ppermute | solution.py:24
  29.4 7.2 %collective-permute-start.6 = (bf16[128,512]{1,0:T(8,128)(2,1)S(1)}, bf16[128,512]{1,0:T(8,128)(2,1)S(1)}, u32[]{:S(2)}, u32[]{:S(2)}) collective-permute-start(bf16[128,512]{1,0:T(8,128)(2,1)S(1)} %get-tuple-element.37.refs_3_), channel_id=1, source_target_pairs={{0,3},{1,2},{2,1},{3,0},{4,7},{5,6},{6,5},{7,4},{8,11},{9,10},{10,... | collective-permute-start | bytes 393224 | tf_op jit(solution)/shard_map/ppermute | solution.py:24
  31.0 5.5 %copy-start.5 = (bf16[1,128,512]{2,1,0:T(8,128)(2,1)S(1)}, bf16[1,128,512]{2,1,0:T(8,128)(2,1)}, u32[]{:S(2)}) copy-start(bf16[1,128,512]{2,1,0:T(8,128)(2,1)} %param.7) | copy-start | bytes 393220
  31.6 16.4 %copy-start.4 = (bf16[1,2048,512]{2,1,0:T(8,128)(2,1)S(1)}, bf16[1,2048,512]{2,1,0:T(8,128)(2,1)}, u32[]{:S(2)}) copy-start(bf16[1,2048,512]{2,1,0:T(8,128)(2,1)} %param.9) | copy-start | bytes 6291460
  31.6 4.9 %collective-permute-start.12 = (bf16[80,512]{1,0:T(8,128)(2,1)S(1)}, bf16[80,512]{1,0:T(8,128)(2,1)S(1)}, u32[]{:S(2)}, u32[]{:S(2)}) collective-permute-start(bf16[80,512]{1,0:T(8,128)(2,1)S(1)} %get-tuple-element.44), channel_id=1, source_target_pairs={{0,2},{1,3},{2,0},{3,1},{4,6},{5,7},{6,4},{7,5},{8,10},{9,11},{10,... | collective-permute-start | bytes 245768 | tf_op jit(solution)/shard_map/ppermute | solution.py:24
  32.1 4.4 %collective-permute-start.10 = (bf16[80,512]{1,0:T(8,128)(2,1)S(1)}, bf16[80,512]{1,0:T(8,128)(2,1)S(1)}, u32[]{:S(2)}, u32[]{:S(2)}) collective-permute-start(bf16[80,512]{1,0:T(8,128)(2,1)S(1)} %get-tuple-element.43.refs_4_), channel_id=1, source_target_pairs={{0,1},{1,0},{2,3},{3,2},{4,5},{5,4},{6,7},{7,6},{8,9},{9,8},{10,11... | collective-permute-start | bytes 245768 | tf_op jit(solution)/shard_map/ppermute | solution.py:24
  33.3 2.9 %collective-permute-start.7 = (bf16[48,512]{1,0:T(8,128)(2,1)S(1)}, bf16[48,512]{1,0:T(8,128)(2,1)S(1)}, u32[]{:S(2)}, u32[]{:S(2)}) collective-permute-start(bf16[48,512]{1,0:T(8,128)(2,1)S(1)} %get-tuple-element.38), channel_id=1, source_target_pairs={{0,1},{1,0},{2,3},{3,2},{4,5},{5,4},{6,7},{7,6},{8,9},{9,8},{10,11... | collective-permute-start | bytes 147464 | tf_op jit(solution)/shard_map/ppermute | solution.py:24
  33.6 2.9 %collective-permute-start.11 = (bf16[48,512]{1,0:T(8,128)(2,1)S(1)}, bf16[48,512]{1,0:T(8,128)(2,1)S(1)}, u32[]{:S(2)}, u32[]{:S(2)}) collective-permute-start(bf16[48,512]{1,0:T(8,128)(2,1)S(1)} %get-tuple-element.35.refs_4_), channel_id=1, source_target_pairs={{0,2},{1,3},{2,0},{3,1},{4,6},{5,7},{6,4},{7,5},{8,10},{9,11},{10,... | collective-permute-start | bytes 147464 | tf_op jit(solution)/shard_map/ppermute | solution.py:24
  36.6 6.0 %collective-permute-start.15 = (bf16[128,512]{1,0:T(8,128)(2,1)S(1)}, bf16[128,512]{1,0:T(8,128)(2,1)S(1)}, u32[]{:S(2)}, u32[]{:S(2)}) collective-permute-start(bf16[128,512]{1,0:T(8,128)(2,1)S(1)} %slope.1.refs_0_), channel_id=1, source_target_pairs={{0,3},{1,2},{2,1},{3,0},{4,7},{5,6},{6,5},{7,4},{8,11},{9,10},{10,... | collective-permute-start | bytes 393224 | tf_op jit(solution)/shard_map/ppermute | solution.py:24
  38.1 5.7 %collective-permute-start.14 = (bf16[128,512]{1,0:T(8,128)(2,1)S(1)}, bf16[128,512]{1,0:T(8,128)(2,1)S(1)}, u32[]{:S(2)}, u32[]{:S(2)}) collective-permute-start(bf16[128,512]{1,0:T(8,128)(2,1)S(1)} %slope.1.refs_0_), channel_id=1, source_target_pairs={{0,2},{1,3},{2,0},{3,1},{4,6},{5,7},{6,4},{7,5},{8,10},{9,11},{10,... | collective-permute-start | bytes 393224 | tf_op jit(solution)/shard_map/ppermute | solution.py:24
  39.1 5.0 %collective-permute-start.13 = (bf16[128,512]{1,0:T(8,128)(2,1)S(1)}, bf16[128,512]{1,0:T(8,128)(2,1)S(1)}, u32[]{:S(2)}, u32[]{:S(2)}) collective-permute-start(bf16[128,512]{1,0:T(8,128)(2,1)S(1)} %slope.1.refs_0_), channel_id=1, source_target_pairs={{0,1},{1,0},{2,3},{3,2},{4,5},{5,4},{6,7},{7,6},{8,9},{9,8},{10,11... | collective-permute-start | bytes 393224 | tf_op jit(solution)/shard_map/ppermute | solution.py:24
  44.3 6.0 %collective-permute-start.16 = (bf16[144,128]{1,0:T(8,128)(2,1)S(1)}, bf16[144,128]{1,0:T(8,128)(2,1)S(1)}, u32[]{:S(2)}, u32[]{:S(2)}) collective-permute-start(bf16[144,128]{1,0:T(8,128)(2,1)S(1)} %kept.1.refs_0_), channel_id=1, source_target_pairs={{0,24},{4,28},{8,16},{12,20},{16,8},{20,12},{24,0},{28,4},{1,25},{... | collective-permute-start | bytes 110600 | tf_op jit(solution)/shard_map/ppermute | solution.py:24
  47.5 3.7 %collective-permute-start.17 = (bf16[144,128]{1,0:T(8,128)(2,1)S(1)}, bf16[144,128]{1,0:T(8,128)(2,1)S(1)}, u32[]{:S(2)}, u32[]{:S(2)}) collective-permute-start(bf16[144,128]{1,0:T(8,128)(2,1)S(1)} %kept.1.refs_0_), channel_id=1, source_target_pairs={{0,16},{4,20},{8,24},{12,28},{16,0},{20,4},{24,8},{28,12},{1,17},{... | collective-permute-start | bytes 110600 | tf_op jit(solution)/shard_map/ppermute | solution.py:24
  47.5 3.7 %collective-permute-start.18 = (bf16[144,128]{1,0:T(8,128)(2,1)S(1)}, bf16[144,128]{1,0:T(8,128)(2,1)S(1)}, u32[]{:S(2)}, u32[]{:S(2)}) collective-permute-start(bf16[144,128]{1,0:T(8,128)(2,1)S(1)} %kept.1.refs_0_), channel_id=1, source_target_pairs={{0,8},{4,12},{8,0},{12,4},{16,24},{20,28},{24,16},{28,20},{1,9},{5... | collective-permute-start | bytes 110600 | tf_op jit(solution)/shard_map/ppermute | solution.py:24
  51.2 10.9 %collective-permute-start.19 = (bf16[576,128]{1,0:T(8,128)(2,1)S(1)}, bf16[576,128]{1,0:T(8,128)(2,1)S(1)}, u32[]{:S(2)}, u32[]{:S(2)}) collective-permute-start(bf16[576,128]{1,0:T(8,128)(2,1)S(1)} %join.5.group), channel_id=1, source_target_pairs={{0,4},{4,0},{8,12},{12,8},{16,20},{20,16},{24,28},{28,24},{1,5},{5... | collective-permute-start | bytes 442376 | tf_op jit(solution)/shard_map/ppermute | solution.py:24

commit v20 on v17

--- a/solution.py
+++ b/solution.py
@@ -436,7 +436,8 @@
     order_near = [(k, low, high) for low, high in spans for k in range(len(near))]
     wide = gather(slopes[:n_far], order_far, xg_far)
     message = kept(slopes[n_far:], order_near, wide, xg_near, fbk, slot_row)
-    same_core = [swap(message, "rep", n_rep, d) for d in range(n_rep - 2, 0, -2)]
+    chips = [4, *range(n_rep - 2, 4, -2), 2] if n_rep > 4 else list(range(2, n_rep, 2))
+    same_core = [swap(message, "rep", n_rep, d) for d in chips]
     order = order_far + [(n_far + k, low, high) for k, low, high in order_near]
     new_feedback, token = residue(slopes, order, [xt_far, xt_near], fb, keep)
     joined, after = message, [token]

time: 57.4 us -> 57.3 us (level)
  no operation moved by 1% of the time
where the time goes in v20:
time: 57.3 us; the launch traced here: 57 us
  starting transfers between devices  24 us (42%)
  waiting for transfers between devices  15.6 us (27%)
  Pallas kernels  11.6 us (20%)
  local copies, waits for them, and re-layouts  4.28 us (7%)
  between operations  1.53 us (3%)
    ppermute x20, starting transfers between devices, swap(): return lax.ppermute(x, axis, [(i, i ^ d) for i in range(n)])  24 us
    ppermute x20, waiting for transfers between devices, swap(): return lax.ppermute(x, axis, [(i, i ^ d) for i in range(n)])  15.6 us
    unnamed x14, local copies, waits for them, and re-layouts  3.2 us
    pallas_call x1, Pallas kernels, outer(): pl.pallas_call(functools.partial(outer_kernel, cap, kw // LANES, tile, n)...  2.54 us
    pallas_call x1, Pallas kernels, residue(): pl.pallas_call(functools.partial(residue_kernel, order, tile), out_shape=...  2.38 us
    pallas_call x3, Pallas kernels, project(): pl.pallas_call(functools.partial(project_kernel, n, len(outs)), out_shape...  1.62 us
    pallas_call x1, Pallas kernels, outer(): pl.pallas_call(functools.partial(half_kernel, cap, kw // LANES, tile), ou...  1.41 us
    pallas_call x2, Pallas kernels, prepare(): pl.pallas_call(functools.partial(prepare_kernel, per_row, len(xs)), out_s...  1.2 us
  transfers between devices with their start and end apart: 20, of which 9 were waited for; matrix products, arithmetic and copies ran while one was open for 0% of the time, Pallas kernels for 15%

profile of v20, /device:TPU:1, one launch (start us, length us, event | category | flops | bytes accessed | tf_op | source)
XLA Modules:
  0.0 57.0 jit_solution(6094349291448238460)
XLA Ops:
  0.6 1.1 %dynamic-slice_bitcast_fusion = (bf16[64,2048]{1,0:T(8,128)(2,1)S(1)}, bf16[64,2048]{1,0:T(8,128)(2,1)S(1)}) fusion(bf16[1,128,8192]{2,1,0:T(8,128)(2,1)} %param.6, s32[]{:T(128)S(6)} %select_n.4), kind=kLoop, calls=%fused_computation | loop fusion | bytes 1048580 | tf_op jit(solution)/shard_map/dynamic_slice | solution.py:392
  1.7 2.1 %collective-permute-start.1 = (bf16[64,2048]{1,0:T(8,128)(2,1)S(1)}, bf16[64,2048]{1,0:T(8,128)(2,1)S(1)}, u32[]{:S(2)}, u32[]{:S(2)}) collective-permute-start(bf16[64,2048]{1,0:T(8,128)(2,1)S(1)} %get-tuple-element.56), channel_id=1, source_target_pairs={{0,2},{1,3},{2,0},{3,1},{4,6},{5,7},{6,4},{7,5},{8,10},{9,11},{10,... | collective-permute-start | bytes 786440 | tf_op jit(solution)/shard_map/ppermute | solution.py:24
  3.9 1.2 %collective-permute-start = (bf16[64,2048]{1,0:T(8,128)(2,1)S(1)}, bf16[64,2048]{1,0:T(8,128)(2,1)S(1)}, u32[]{:S(2)}, u32[]{:S(2)}) collective-permute-start(bf16[64,2048]{1,0:T(8,128)(2,1)S(1)} %get-tuple-element.57.refs_0_), channel_id=1, source_target_pairs={{0,1},{1,0},{2,3},{3,2},{4,5},{5,4},{6,7},{7,6},{8,9},{9,8},{10,11... | collective-permute-start | bytes 786440 | tf_op jit(solution)/shard_map/ppermute | solution.py:24
  5.1 1.6 %copy-done = bf16[1,128,8192]{2,1,0:T(8,128)(2,1)S(1)} copy-done((bf16[1,128,8192]{2,1,0:T(8,128)(2,1)S(1)}, bf16[1,128,8192]{2,1,0:T(8,128)(2,1)}, u32[]{:S(2)}) %copy-start) | copy-done | bytes 2097176
  7.1 2.8 %collective-permute-done.1.refs_2_ = bf16[64,2048]{1,0:T(8,128)(2,1)S(1)} collective-permute-done((bf16[64,2048]{1,0:T(8,128)(2,1)S(1)}, bf16[64,2048]{1,0:T(8,128)(2,1)S(1)}, u32[]{:S(2)}, u32[]{:S(2)}) %collective-permute-start.1) | collective-permute-done | bytes 262176 | tf_op jit(solution)/shard_map/ppermute | solution.py:24
  9.9 1.1 %collective-permute-start.3 = (bf16[64,2048]{1,0:T(8,128)(2,1)S(1)}, bf16[64,2048]{1,0:T(8,128)(2,1)S(1)}, u32[]{:S(2)}, u32[]{:S(2)}) collective-permute-start(bf16[64,2048]{1,0:T(8,128)(2,1)S(1)} %collective-permute-done.1.refs_2_), channel_id=1, source_target_pairs={{0,1},{1,0},{2,3},{3,2},{4,5},{5,4},{6,7},{7,6},{8,9},{9,8},{10,11... | collective-permute-start | bytes 786440 | tf_op jit(solution)/shard_map/ppermute | solution.py:24
  11.0 1.2 %collective-permute-start.2 = (bf16[64,2048]{1,0:T(8,128)(2,1)S(1)}, bf16[64,2048]{1,0:T(8,128)(2,1)S(1)}, u32[]{:S(2)}, u32[]{:S(2)}) collective-permute-start(bf16[64,2048]{1,0:T(8,128)(2,1)S(1)} %collective-permute-done.refs_1_), channel_id=1, source_target_pairs={{0,2},{1,3},{2,0},{3,1},{4,6},{5,7},{6,4},{7,5},{8,10},{9,11},{10,... | collective-permute-start | bytes 786440 | tf_op jit(solution)/shard_map/ppermute | solution.py:24
  12.9 1.6 %copy-done.3 = bf16[1,2048,512]{2,1,0:T(8,128)(2,1)S(1)} copy-done((bf16[1,2048,512]{2,1,0:T(8,128)(2,1)S(1)}, bf16[1,2048,512]{2,1,0:T(8,128)(2,1)}, u32[]{:S(2)}) %copy-start.3) | copy-done | bytes 2097176
  14.5 1.1 %early.1 = (f32[128,128]{1,0:T(8,128)S(1)}, bf16[2048,512]{1,0:T(8,128)(2,1)S(1)}, f32[8,128]{1,0:T(8,128)S(1)}) custom-call(s32[1,128]{1,0:T(1,128)S(1)} %bitcast.19, s32[1,1]{1,0:T(1,128)S(6)} %copy.8.count.refs_2_.refs_3_, bf16[2048,512]{1,0:T(8,128)(2,1)S(1)} %bitcast.16, f32[8,128]{1,0:T(8,128)S(1)} %get-tuple-element.29.after), custom_call_target="tpu_custom_call" | custom-call | flops 1000 | bytes 1000 | tf_op jit(solution)/shard_map/early/pallas_call | solution.py:145
  16.3 0.6 %collective-permute-start.9 = (bf16[64,2048]{1,0:T(8,128)(2,1)S(1)}, bf16[64,2048]{1,0:T(8,128)(2,1)S(1)}, u32[]{:S(2)}, u32[]{:S(2)}) collective-permute-start(bf16[64,2048]{1,0:T(8,128)(2,1)S(1)} %get-tuple-element.40), channel_id=1, source_target_pairs={{0,2},{1,3},{2,0},{3,1},{4,6},{5,7},{6,4},{7,5},{8,10},{9,11},{10,... | collective-permute-start | bytes 786440 | tf_op jit(solution)/shard_map/ppermute | solution.py:24
  16.9 0.6 %cut.5 = (bf16[128,2048]{1,0:T(8,128)(2,1)S(1)}, f32[8,128]{1,0:T(8,128)}) custom-call(bf16[128,8192]{1,0:T(8,128)(2,1)S(1)} %bitcast.12, f32[8,128]{1,0:T(8,128)S(1)} %get-tuple-element.31.refs_0_), custom_call_target="tpu_custom_call" | custom-call | flops 1000 | bytes 1000 | tf_op jit(solution)/shard_map/cut/pallas_call | solution.py:43
  18.1 3.9 %collective-permute-done.3.refs_2_ = bf16[64,2048]{1,0:T(8,128)(2,1)S(1)} collective-permute-done((bf16[64,2048]{1,0:T(8,128)(2,1)S(1)}, bf16[64,2048]{1,0:T(8,128)(2,1)S(1)}, u32[]{:S(2)}, u32[]{:S(2)}) %collective-permute-start.3) | collective-permute-done | bytes 262176 | tf_op jit(solution)/shard_map/ppermute | solution.py:24
  22.0 0.7 %project.4 = (f32[128,512]{1,0:T(8,128)S(1)}, bf16[128,512]{1,0:T(8,128)(2,1)S(1)}, bf16[256,2048]{1,0:T(8,128)(2,1)S(1)}) custom-call(bf16[128,2048]{1,0:T(8,128)(2,1)S(1)} %get-tuple-element.32.refs_0_, bf16[64,2048]{1,0:T(8,128)(2,1)S(1)} %collective-permute-done.2.refs_1_, bf16[64,2048]{1,0:T(8,128)(2,1)S(1)} %collective-permute-done.3.refs_2_, ...), custom_call_target="tpu_custom_call" | custom-call | flops 1000 | bytes 1000 | tf_op jit(solution)/shard_map/project/pallas_call | solution.py:73
  22.7 1.3 %collective-permute-start.6 = (bf16[128,512]{1,0:T(8,128)(2,1)S(1)}, bf16[128,512]{1,0:T(8,128)(2,1)S(1)}, u32[]{:S(2)}, u32[]{:S(2)}) collective-permute-start(bf16[128,512]{1,0:T(8,128)(2,1)S(1)} %get-tuple-element.37.refs_3_), channel_id=1, source_target_pairs={{0,3},{1,2},{2,1},{3,0},{4,7},{5,6},{6,5},{7,4},{8,11},{9,10},{10,... | collective-permute-start | bytes 393224 | tf_op jit(solution)/shard_map/ppermute | solution.py:24
  24.0 1.2 %collective-permute-start.11 = (bf16[64,512]{1,0:T(8,128)(2,1)S(1)}, bf16[64,512]{1,0:T(8,128)(2,1)S(1)}, u32[]{:S(2)}, u32[]{:S(2)}) collective-permute-start(bf16[64,512]{1,0:T(8,128)(2,1)S(1)} %get-tuple-element.35.refs_4_), channel_id=1, source_target_pairs={{0,2},{1,3},{2,0},{3,1},{4,6},{5,7},{6,4},{7,5},{8,10},{9,11},{10,... | collective-permute-start | bytes 196616 | tf_op jit(solution)/shard_map/ppermute | solution.py:24
  25.4 0.6 %prepare.2 = (bf16[128,256]{1,0:T(8,128)(2,1)S(1)}, bf16[2048,256]{1,0:T(8,128)(2,1)S(1)}, f32[8,128]{1,0:T(8,128)S(1)}) custom-call(bf16[256,2048]{1,0:T(8,128)(2,1)S(1)} %get-tuple-element.41.refs_0_, s32[1,128]{1,0:T(1,128)S(1)} %bitcast.20, s32[1,1]{1,0:T(1,128)S(6)} %copy.8.count.refs_2_.refs_3_, bf16[128,512]{1,0:T(8,128)(2,1)S(1)} %get-tuple-element.37.refs_3_), custom_call_target="tpu_custom_call" | custom-call | flops 1000 | bytes 1000 | tf_op jit(solution)/shard_map/prepare/pallas_call | solution.py:181
  26.0 1.6 %collective-permute-done.8.refs_0_ = bf16[64,2048]{1,0:T(8,128)(2,1)S(1)} collective-permute-done((bf16[64,2048]{1,0:T(8,128)(2,1)S(1)}, bf16[64,2048]{1,0:T(8,128)(2,1)S(1)}, u32[]{:S(2)}, u32[]{:S(2)}) %collective-permute-start.8) | collective-permute-done | bytes 262176 | tf_op jit(solution)/shard_map/ppermute | solution.py:24
  28.5 1.1 %collective-permute-start.10 = (bf16[64,512]{1,0:T(8,128)(2,1)S(1)}, bf16[64,512]{1,0:T(8,128)(2,1)S(1)}, u32[]{:S(2)}, u32[]{:S(2)}) collective-permute-start(bf16[64,512]{1,0:T(8,128)(2,1)S(1)} %get-tuple-element.43.refs_4_), channel_id=1, source_target_pairs={{0,1},{1,0},{2,3},{3,2},{4,5},{5,4},{6,7},{7,6},{8,9},{9,8},{10,11... | collective-permute-start | bytes 196616 | tf_op jit(solution)/shard_map/ppermute | solution.py:24
  29.6 0.6 %prepare.3 = (bf16[128,256]{1,0:T(8,128)(2,1)S(1)}, bf16[2048,256]{1,0:T(8,128)(2,1)S(1)}, f32[8,128]{1,0:T(8,128)S(1)}) custom-call(bf16[128,2048]{1,0:T(8,128)(2,1)S(1)} %get-tuple-element.45.refs_0_, bf16[128,2048]{1,0:T(8,128)(2,1)S(1)} %get-tuple-element.46.refs_1_, s32[1,128]{1,0:T(1,128)S(1)} %bitcast.21, s32[1,1]{1,0:T(1,128)S(6)} %copy.8.count.refs_2_.refs_3_, ...), custom_call_target="tpu_custom_call" | custom-call | flops 1000 | bytes 1000 | tf_op jit(solution)/shard_map/prepare/pallas_call | solution.py:181
  30.2 1.5 %collective-permute-done.7.refs_3_ = bf16[64,512]{1,0:T(8,128)(2,1)S(1)} collective-permute-done((bf16[64,512]{1,0:T(8,128)(2,1)S(1)}, bf16[64,512]{1,0:T(8,128)(2,1)S(1)}, u32[]{:S(2)}, u32[]{:S(2)}) %collective-permute-start.7) | collective-permute-done | bytes 65568 | tf_op jit(solution)/shard_map/ppermute | solution.py:24
  31.8 1.4 %collective-permute-done.12.refs_6_ = bf16[64,512]{1,0:T(8,128)(2,1)S(1)} collective-permute-done((bf16[64,512]{1,0:T(8,128)(2,1)S(1)}, bf16[64,512]{1,0:T(8,128)(2,1)S(1)}, u32[]{:S(2)}, u32[]{:S(2)}) %collective-permute-start.12) | collective-permute-done | bytes 65568 | tf_op jit(solution)/shard_map/ppermute | solution.py:24
  33.3 1.6 %collective-permute-start.15 = (bf16[128,512]{1,0:T(8,128)(2,1)S(1)}, bf16[128,512]{1,0:T(8,128)(2,1)S(1)}, u32[]{:S(2)}, u32[]{:S(2)}) collective-permute-start(bf16[128,512]{1,0:T(8,128)(2,1)S(1)} %slope.1.refs_0_), channel_id=1, source_target_pairs={{0,3},{1,2},{2,1},{3,0},{4,7},{5,6},{6,5},{7,4},{8,11},{9,10},{10,... | collective-permute-start | bytes 393224 | tf_op jit(solution)/shard_map/ppermute | solution.py:24
  34.8 0.6 %collective-permute-start.14 = (bf16[128,512]{1,0:T(8,128)(2,1)S(1)}, bf16[128,512]{1,0:T(8,128)(2,1)S(1)}, u32[]{:S(2)}, u32[]{:S(2)}) collective-permute-start(bf16[128,512]{1,0:T(8,128)(2,1)S(1)} %slope.1.refs_0_), channel_id=1, source_target_pairs={{0,2},{1,3},{2,0},{3,1},{4,6},{5,7},{6,4},{7,5},{8,10},{9,11},{10,... | collective-permute-start | bytes 393224 | tf_op jit(solution)/shard_map/ppermute | solution.py:24
  36.0 2.2 %collective-permute-done.15.refs_1_ = bf16[128,512]{1,0:T(8,128)(2,1)S(1)} collective-permute-done((bf16[128,512]{1,0:T(8,128)(2,1)S(1)}, bf16[128,512]{1,0:T(8,128)(2,1)S(1)}, u32[]{:S(2)}, u32[]{:S(2)}) %collective-permute-start.15) | collective-permute-done | bytes 131104 | tf_op jit(solution)/shard_map/ppermute | solution.py:24
  38.3 1.1 %collective-permute-done.14.refs_1_.refs_3_ = bf16[128,512]{1,0:T(8,128)(2,1)S(1)} collective-permute-done((bf16[128,512]{1,0:T(8,128)(2,1)S(1)}, bf16[128,512]{1,0:T(8,128)(2,1)S(1)}, u32[]{:S(2)}, u32[]{:S(2)}) %collective-permute-start.14) | collective-permute-done | bytes 131104 | tf_op jit(solution)/shard_map/ppermute | solution.py:24
  39.7 2.6 %collective-permute-start.16 = (bf16[144,128]{1,0:T(8,128)(2,1)S(1)}, bf16[144,128]{1,0:T(8,128)(2,1)S(1)}, u32[]{:S(2)}, u32[]{:S(2)}) collective-permute-start(bf16[144,128]{1,0:T(8,128)(2,1)S(1)} %kept.1.refs_0_), channel_id=1, source_target_pairs={{0,16},{4,20},{8,24},{12,28},{16,0},{20,4},{24,8},{28,12},{1,17},{... | collective-permute-start | bytes 110600 | tf_op jit(solution)/shard_map/ppermute | solution.py:24
  42.3 1.1 %collective-permute-start.17 = (bf16[144,128]{1,0:T(8,128)(2,1)S(1)}, bf16[144,128]{1,0:T(8,128)(2,1)S(1)}, u32[]{:S(2)}, u32[]{:S(2)}) collective-permute-start(bf16[144,128]{1,0:T(8,128)(2,1)S(1)} %kept.1.refs_0_), channel_id=1, source_target_pairs={{0,24},{4,28},{8,16},{12,20},{16,8},{20,12},{24,0},{28,4},{1,25},{... | collective-permute-start | bytes 110600 | tf_op jit(solution)/shard_map/ppermute | solution.py:24
  43.6 2.4 %residue.1 = (bf16[2048,512]{1,0:T(8,128)(2,1)}, f32[8,128]{1,0:T(8,128)S(1)}) custom-call(bf16[128,512]{1,0:T(8,128)(2,1)S(1)} %slope.1.refs_0_, bf16[128,512]{1,0:T(8,128)(2,1)S(1)} %collective-permute-done.15.refs_1_, bf16[128,512]{1,0:T(8,128)(2,1)S(1)} %collective-permute-done.13.refs_0_.refs_2_, ...), custom_call_target="tpu_custom_call" | custom-call | flops 1000 | bytes 1000 | tf_op jit(solution)/shard_map/residue/pallas_call | solution.py:274
  46.0 0.9 %collective-permute-done.17.refs_1_ = bf16[144,128]{1,0:T(8,128)(2,1)S(1)} collective-permute-done((bf16[144,128]{1,0:T(8,128)(2,1)S(1)}, bf16[144,128]{1,0:T(8,128)(2,1)S(1)}, u32[]{:S(2)}, u32[]{:S(2)}) %collective-permute-start.17) | collective-permute-done | bytes 36896 | tf_op jit(solution)/shard_map/ppermute | solution.py:24
  47.0 6.1 %collective-permute-start.19 = (bf16[576,128]{1,0:T(8,128)(2,1)S(1)}, bf16[576,128]{1,0:T(8,128)(2,1)S(1)}, u32[]{:S(2)}, u32[]{:S(2)}) collective-permute-start(bf16[576,128]{1,0:T(8,128)(2,1)S(1)} %join.5.group), channel_id=1, source_target_pairs={{0,4},{4,0},{8,12},{12,8},{16,20},{20,16},{24,28},{28,24},{1,5},{5... | collective-permute-start | bytes 442376 | tf_op jit(solution)/shard_map/ppermute | solution.py:24
  53.1 1.4 %half.1 = f32[2048,512]{1,0:T(8,128)S(1)} custom-call(bf16[576,128]{1,0:T(8,128)(2,1)S(1)} %join.5.group), custom_call_target="tpu_custom_call" | custom-call | flops 1000 | bytes 1000 | tf_op jit(solution)/shard_map/half/pallas_call | solution.py:356
  54.5 2.5 %outer.1 = f32[2048,512]{1,0:T(8,128)} custom-call(bf16[576,128]{1,0:T(8,128)(2,1)S(1)} %collective-permute-done.19.group, f32[2048,512]{1,0:T(8,128)S(1)} %half.1), custom_call_target="tpu_custom_call" | custom-call | flops 1000 | bytes 1000 | tf_op jit(solution)/shard_map/outer/pallas_call | solution.py:364
  (41 shorter events, 4.1 us)
Async XLA Ops:
  0.6 12.3 %copy-start.6 = (s32[1,1,128]{2,1,0:T(1,128)S(1)}, s32[1,1,128]{2,1,0:T(1,128)}, u32[]{:S(2)}) copy-start(s32[1,1,128]{2,1,0:T(1,128)} %param.11) | copy-start | bytes 1540
  1.7 8.2 %collective-permute-start.1 = (bf16[64,2048]{1,0:T(8,128)(2,1)S(1)}, bf16[64,2048]{1,0:T(8,128)(2,1)S(1)}, u32[]{:S(2)}, u32[]{:S(2)}) collective-permute-start(bf16[64,2048]{1,0:T(8,128)(2,1)S(1)} %get-tuple-element.56), channel_id=1, source_target_pairs={{0,2},{1,3},{2,0},{3,1},{4,6},{5,7},{6,4},{7,5},{8,10},{9,11},{10,... | collective-permute-start | bytes 786440 | tf_op jit(solution)/shard_map/ppermute | solution.py:24
  3.9 7.1 %collective-permute-start = (bf16[64,2048]{1,0:T(8,128)(2,1)S(1)}, bf16[64,2048]{1,0:T(8,128)(2,1)S(1)}, u32[]{:S(2)}, u32[]{:S(2)}) collective-permute-start(bf16[64,2048]{1,0:T(8,128)(2,1)S(1)} %get-tuple-element.57.refs_0_), channel_id=1, source_target_pairs={{0,1},{1,0},{2,3},{3,2},{4,5},{5,4},{6,7},{7,6},{8,9},{9,8},{10,11... | collective-permute-start | bytes 786440 | tf_op jit(solution)/shard_map/ppermute | solution.py:24
  5.1 1.6 %copy-start = (bf16[1,128,8192]{2,1,0:T(8,128)(2,1)S(1)}, bf16[1,128,8192]{2,1,0:T(8,128)(2,1)}, u32[]{:S(2)}) copy-start(bf16[1,128,8192]{2,1,0:T(8,128)(2,1)} %param.6) | copy-start | bytes 6291460
  6.7 9.0 %copy-start.1 = (bf16[1,128,8192]{2,1,0:T(8,128)(2,1)S(1)}, bf16[1,128,8192]{2,1,0:T(8,128)(2,1)}, u32[]{:S(2)}) copy-start(bf16[1,128,8192]{2,1,0:T(8,128)(2,1)} %param.6) | copy-start | bytes 6291460
  6.7 9.6 %collective-permute-start.4 = (bf16[64,2048]{1,0:T(8,128)(2,1)S(1)}, bf16[64,2048]{1,0:T(8,128)(2,1)S(1)}, u32[]{:S(2)}, u32[]{:S(2)}) collective-permute-start(bf16[64,2048]{1,0:T(8,128)(2,1)S(1)} %get-tuple-element.33), channel_id=1, source_target_pairs={{0,1},{1,0},{2,3},{3,2},{4,5},{5,4},{6,7},{7,6},{8,9},{9,8},{10,11... | collective-permute-start | bytes 786440 | tf_op jit(solution)/shard_map/ppermute | solution.py:24
  7.1 10.5 %collective-permute-start.5 = (bf16[64,2048]{1,0:T(8,128)(2,1)S(1)}, bf16[64,2048]{1,0:T(8,128)(2,1)S(1)}, u32[]{:S(2)}, u32[]{:S(2)}) collective-permute-start(bf16[64,2048]{1,0:T(8,128)(2,1)S(1)} %get-tuple-element.34), channel_id=1, source_target_pairs={{0,2},{1,3},{2,0},{3,1},{4,6},{5,7},{6,4},{7,5},{8,10},{9,11},{10,... | collective-permute-start | bytes 786440 | tf_op jit(solution)/shard_map/ppermute | solution.py:24
  9.9 12.1 %collective-permute-start.3 = (bf16[64,2048]{1,0:T(8,128)(2,1)S(1)}, bf16[64,2048]{1,0:T(8,128)(2,1)S(1)}, u32[]{:S(2)}, u32[]{:S(2)}) collective-permute-start(bf16[64,2048]{1,0:T(8,128)(2,1)S(1)} %collective-permute-done.1.refs_2_), channel_id=1, source_target_pairs={{0,1},{1,0},{2,3},{3,2},{4,5},{5,4},{6,7},{7,6},{8,9},{9,8},{10,11... | collective-permute-start | bytes 786440 | tf_op jit(solution)/shard_map/ppermute | solution.py:24
  11.0 10.9 %collective-permute-start.2 = (bf16[64,2048]{1,0:T(8,128)(2,1)S(1)}, bf16[64,2048]{1,0:T(8,128)(2,1)S(1)}, u32[]{:S(2)}, u32[]{:S(2)}) collective-permute-start(bf16[64,2048]{1,0:T(8,128)(2,1)S(1)} %collective-permute-done.refs_1_), channel_id=1, source_target_pairs={{0,2},{1,3},{2,0},{3,1},{4,6},{5,7},{6,4},{7,5},{8,10},{9,11},{10,... | collective-permute-start | bytes 786440 | tf_op jit(solution)/shard_map/ppermute | solution.py:24
  12.9 1.6 %copy-start.3 = (bf16[1,2048,512]{2,1,0:T(8,128)(2,1)S(1)}, bf16[1,2048,512]{2,1,0:T(8,128)(2,1)}, u32[]{:S(2)}) copy-start(bf16[1,2048,512]{2,1,0:T(8,128)(2,1)} %param.9) | copy-start | bytes 6291460
  15.6 2.0 %copy-start.2 = (bf16[1,2048,512]{2,1,0:T(8,128)(2,1)S(1)}, bf16[1,2048,512]{2,1,0:T(8,128)(2,1)}, u32[]{:S(2)}) copy-start(bf16[1,2048,512]{2,1,0:T(8,128)(2,1)} %param.8) | copy-start | bytes 6291460
  15.7 11.8 %collective-permute-start.8 = (bf16[64,2048]{1,0:T(8,128)(2,1)S(1)}, bf16[64,2048]{1,0:T(8,128)(2,1)S(1)}, u32[]{:S(2)}, u32[]{:S(2)}) collective-permute-start(bf16[64,2048]{1,0:T(8,128)(2,1)S(1)} %get-tuple-element.39), channel_id=1, source_target_pairs={{0,1},{1,0},{2,3},{3,2},{4,5},{5,4},{6,7},{7,6},{8,9},{9,8},{10,11... | collective-permute-start | bytes 786440 | tf_op jit(solution)/shard_map/ppermute | solution.py:24
  16.3 11.2 %collective-permute-start.9 = (bf16[64,2048]{1,0:T(8,128)(2,1)S(1)}, bf16[64,2048]{1,0:T(8,128)(2,1)S(1)}, u32[]{:S(2)}, u32[]{:S(2)}) collective-permute-start(bf16[64,2048]{1,0:T(8,128)(2,1)S(1)} %get-tuple-element.40), channel_id=1, source_target_pairs={{0,2},{1,3},{2,0},{3,1},{4,6},{5,7},{6,4},{7,5},{8,10},{9,11},{10,... | collective-permute-start | bytes 786440 | tf_op jit(solution)/shard_map/ppermute | solution.py:24
  22.7 10.5 %collective-permute-start.6 = (bf16[128,512]{1,0:T(8,128)(2,1)S(1)}, bf16[128,512]{1,0:T(8,128)(2,1)S(1)}, u32[]{:S(2)}, u32[]{:S(2)}) collective-permute-start(bf16[128,512]{1,0:T(8,128)(2,1)S(1)} %get-tuple-element.37.refs_3_), channel_id=1, source_target_pairs={{0,3},{1,2},{2,1},{3,0},{4,7},{5,6},{6,5},{7,4},{8,11},{9,10},{10,... | collective-permute-start | bytes 393224 | tf_op jit(solution)/shard_map/ppermute | solution.py:24
  24.0 7.8 %collective-permute-start.11 = (bf16[64,512]{1,0:T(8,128)(2,1)S(1)}, bf16[64,512]{1,0:T(8,128)(2,1)S(1)}, u32[]{:S(2)}, u32[]{:S(2)}) collective-permute-start(bf16[64,512]{1,0:T(8,128)(2,1)S(1)} %get-tuple-element.35.refs_4_), channel_id=1, source_target_pairs={{0,2},{1,3},{2,0},{3,1},{4,6},{5,7},{6,4},{7,5},{8,10},{9,11},{10,... | collective-permute-start | bytes 196616 | tf_op jit(solution)/shard_map/ppermute | solution.py:24
  25.1 6.6 %collective-permute-start.7 = (bf16[64,512]{1,0:T(8,128)(2,1)S(1)}, bf16[64,512]{1,0:T(8,128)(2,1)S(1)}, u32[]{:S(2)}, u32[]{:S(2)}) collective-permute-start(bf16[64,512]{1,0:T(8,128)(2,1)S(1)} %get-tuple-element.38), channel_id=1, source_target_pairs={{0,1},{1,0},{2,3},{3,2},{4,5},{5,4},{6,7},{7,6},{8,9},{9,8},{10,11... | collective-permute-start | bytes 196616 | tf_op jit(solution)/shard_map/ppermute | solution.py:24
  26.0 7.2 %copy-start.5 = (bf16[1,128,512]{2,1,0:T(8,128)(2,1)S(1)}, bf16[1,128,512]{2,1,0:T(8,128)(2,1)}, u32[]{:S(2)}) copy-start(bf16[1,128,512]{2,1,0:T(8,128)(2,1)} %param.7) | copy-start | bytes 393220
  28.0 15.6 %copy-start.4 = (bf16[1,2048,512]{2,1,0:T(8,128)(2,1)S(1)}, bf16[1,2048,512]{2,1,0:T(8,128)(2,1)}, u32[]{:S(2)}) copy-start(bf16[1,2048,512]{2,1,0:T(8,128)(2,1)} %param.9) | copy-start | bytes 6291460
  28.0 5.1 %collective-permute-start.12 = (bf16[64,512]{1,0:T(8,128)(2,1)S(1)}, bf16[64,512]{1,0:T(8,128)(2,1)S(1)}, u32[]{:S(2)}, u32[]{:S(2)}) collective-permute-start(bf16[64,512]{1,0:T(8,128)(2,1)S(1)} %get-tuple-element.44), channel_id=1, source_target_pairs={{0,2},{1,3},{2,0},{3,1},{4,6},{5,7},{6,4},{7,5},{8,10},{9,11},{10,... | collective-permute-start | bytes 196616 | tf_op jit(solution)/shard_map/ppermute | solution.py:24
  28.5 4.7 %collective-permute-start.10 = (bf16[64,512]{1,0:T(8,128)(2,1)S(1)}, bf16[64,512]{1,0:T(8,128)(2,1)S(1)}, u32[]{:S(2)}, u32[]{:S(2)}) collective-permute-start(bf16[64,512]{1,0:T(8,128)(2,1)S(1)} %get-tuple-element.43.refs_4_), channel_id=1, source_target_pairs={{0,1},{1,0},{2,3},{3,2},{4,5},{5,4},{6,7},{7,6},{8,9},{9,8},{10,11... | collective-permute-start | bytes 196616 | tf_op jit(solution)/shard_map/ppermute | solution.py:24
  33.3 4.9 %collective-permute-start.15 = (bf16[128,512]{1,0:T(8,128)(2,1)S(1)}, bf16[128,512]{1,0:T(8,128)(2,1)S(1)}, u32[]{:S(2)}, u32[]{:S(2)}) collective-permute-start(bf16[128,512]{1,0:T(8,128)(2,1)S(1)} %slope.1.refs_0_), channel_id=1, source_target_pairs={{0,3},{1,2},{2,1},{3,0},{4,7},{5,6},{6,5},{7,4},{8,11},{9,10},{10,... | collective-permute-start | bytes 393224 | tf_op jit(solution)/shard_map/ppermute | solution.py:24
  34.8 4.6 %collective-permute-start.14 = (bf16[128,512]{1,0:T(8,128)(2,1)S(1)}, bf16[128,512]{1,0:T(8,128)(2,1)S(1)}, u32[]{:S(2)}, u32[]{:S(2)}) collective-permute-start(bf16[128,512]{1,0:T(8,128)(2,1)S(1)} %slope.1.refs_0_), channel_id=1, source_target_pairs={{0,2},{1,3},{2,0},{3,1},{4,6},{5,7},{6,4},{7,5},{8,10},{9,11},{10,... | collective-permute-start | bytes 393224 | tf_op jit(solution)/shard_map/ppermute | solution.py:24
  35.5 4.0 %collective-permute-start.13 = (bf16[128,512]{1,0:T(8,128)(2,1)S(1)}, bf16[128,512]{1,0:T(8,128)(2,1)S(1)}, u32[]{:S(2)}, u32[]{:S(2)}) collective-permute-start(bf16[128,512]{1,0:T(8,128)(2,1)S(1)} %slope.1.refs_0_), channel_id=1, source_target_pairs={{0,1},{1,0},{2,3},{3,2},{4,5},{5,4},{6,7},{7,6},{8,9},{9,8},{10,11... | collective-permute-start | bytes 393224 | tf_op jit(solution)/shard_map/ppermute | solution.py:24
  39.7 6.3 %collective-permute-start.16 = (bf16[144,128]{1,0:T(8,128)(2,1)S(1)}, bf16[144,128]{1,0:T(8,128)(2,1)S(1)}, u32[]{:S(2)}, u32[]{:S(2)}) collective-permute-start(bf16[144,128]{1,0:T(8,128)(2,1)S(1)} %kept.1.refs_0_), channel_id=1, source_target_pairs={{0,16},{4,20},{8,24},{12,28},{16,0},{20,4},{24,8},{28,12},{1,17},{... | collective-permute-start | bytes 110600 | tf_op jit(solution)/shard_map/ppermute | solution.py:24
  42.3 4.6 %collective-permute-start.17 = (bf16[144,128]{1,0:T(8,128)(2,1)S(1)}, bf16[144,128]{1,0:T(8,128)(2,1)S(1)}, u32[]{:S(2)}, u32[]{:S(2)}) collective-permute-start(bf16[144,128]{1,0:T(8,128)(2,1)S(1)} %kept.1.refs_0_), channel_id=1, source_target_pairs={{0,24},{4,28},{8,16},{12,20},{16,8},{20,12},{24,0},{28,4},{1,25},{... | collective-permute-start | bytes 110600 | tf_op jit(solution)/shard_map/ppermute | solution.py:24
  43.4 3.5 %collective-permute-start.18 = (bf16[144,128]{1,0:T(8,128)(2,1)S(1)}, bf16[144,128]{1,0:T(8,128)(2,1)S(1)}, u32[]{:S(2)}, u32[]{:S(2)}) collective-permute-start(bf16[144,128]{1,0:T(8,128)(2,1)S(1)} %kept.1.refs_0_), channel_id=1, source_target_pairs={{0,8},{4,12},{8,0},{12,4},{16,24},{20,28},{24,16},{28,20},{1,9},{5... | collective-permute-start | bytes 110600 | tf_op jit(solution)/shard_map/ppermute | solution.py:24
  47.0 7.5 %collective-permute-start.19 = (bf16[576,128]{1,0:T(8,128)(2,1)S(1)}, bf16[576,128]{1,0:T(8,128)(2,1)S(1)}, u32[]{:S(2)}, u32[]{:S(2)}) collective-permute-start(bf16[576,128]{1,0:T(8,128)(2,1)S(1)} %join.5.group), channel_id=1, source_target_pairs={{0,4},{4,0},{8,12},{12,8},{16,20},{20,16},{24,28},{28,24},{1,5},{5... | collective-permute-start | bytes 442376 | tf_op jit(solution)/shard_map/ppermute | solution.py:24

commit v21 on v20

--- a/solution.py
+++ b/solution.py
@@ -406,9 +406,7 @@
     for low, high in spans:
         *out, token = cut(tokens, depth, [(d, low, high - low) for d in near], after)
         near_out.append(out)
-        if low == 0:
-            fbk, keep, token = early(slot_row, counts, fb, token)
-            after = [token] + hops
+        after = [token] + hops
     near_in = [[swap(x, "shard", n_shard, d) for x, d in zip(out, near)] for out in near_out]
 
     own, _ = cut(tokens, depth, [(0, 0, tok_dev)], [token])
@@ -429,6 +427,7 @@
     xg_near, xt_near, token = prepare(x_near, slot_row, counts, per_row, late_near[:1])
     shares = [share[k] for k in range(len(near)) for share in shares]
     slopes = slope(target[0], mine, whole, shares, spans, token)
+    fbk, keep, _ = early(slot_row, counts, fb, slopes)
     slopes = [slopes] + [swap(slopes, "shard", n_shard, d) for d in far + near]
 
     n_far = 1 + len(far)

time: 57.3 us -> 57.3 us (level)
  waiting for transfers between devices: 15.6 us -> 17.4 us
  local copies, waits for them, and re-layouts: 4.28 us -> 2.68 us
    ppermute x20, waiting for transfers between devices: 15.6 us -> 17.4 us  [swap(): return lax.ppermute(x, axis, [(i, i ^ d) for i in range(n)])]
    unnamed x14 -> x10, local copies, waits for them, and re-layouts: 3.2 us -> 1.61 us
  transfers between devices with their start and end apart: 20 -> 20, of which waited for: 9 -> 10; matrix products, arithmetic and copies ran while one was open for 0% -> 0% of each run, Pallas kernels for 15% -> 15%
where the time goes in v21:
time: 57.3 us; the launch traced here: 57.1 us
  starting transfers between devices  24 us (42%)
  waiting for transfers between devices  17.4 us (30%)
  Pallas kernels  11.5 us (20%)
  local copies, waits for them, and re-layouts  2.68 us (5%)
  between operations  1.49 us (3%)
    ppermute x20, starting transfers between devices, swap(): return lax.ppermute(x, axis, [(i, i ^ d) for i in range(n)])  24 us
    ppermute x20, waiting for transfers between devices, swap(): return lax.ppermute(x, axis, [(i, i ^ d) for i in range(n)])  17.4 us
    pallas_call x1, Pallas kernels, outer(): pl.pallas_call(functools.partial(outer_kernel, cap, kw // LANES, tile, n)...  2.54 us
    pallas_call x1, Pallas kernels, residue(): pl.pallas_call(functools.partial(residue_kernel, order, tile), out_shape=...  2.33 us
    pallas_call x3, Pallas kernels, project(): pl.pallas_call(functools.partial(project_kernel, n, len(outs)), out_shape...  1.62 us
    unnamed x10, local copies, waits for them, and re-layouts  1.61 us
    pallas_call x1, Pallas kernels, outer(): pl.pallas_call(functools.partial(half_kernel, cap, kw // LANES, tile), ou...  1.41 us
    pallas_call x2, Pallas kernels, prepare(): pl.pallas_call(functools.partial(prepare_kernel, per_row, len(xs)), out_s...  1.21 us
  transfers between devices with their start and end apart: 20, of which 10 were waited for; matrix products, arithmetic and copies ran while one was open for 0% of the time, Pallas kernels for 15%

profile of v21, /device:TPU:1, one launch (start us, length us, event | category | flops | bytes accessed | tf_op | source)
XLA Modules:
  0.0 57.1 jit_solution(7642059662073946911)
XLA Ops:
  0.6 1.1 %dynamic-slice_bitcast_fusion = (bf16[64,2048]{1,0:T(8,128)(2,1)S(1)}, bf16[64,2048]{1,0:T(8,128)(2,1)S(1)}) fusion(bf16[1,128,8192]{2,1,0:T(8,128)(2,1)} %param.6, s32[]{:T(128)S(6)} %select_n.4), kind=kLoop, calls=%fused_computation | loop fusion | bytes 1048580 | tf_op jit(solution)/shard_map/dynamic_slice | solution.py:392
  1.7 2.1 %collective-permute-start.1 = (bf16[64,2048]{1,0:T(8,128)(2,1)S(1)}, bf16[64,2048]{1,0:T(8,128)(2,1)S(1)}, u32[]{:S(2)}, u32[]{:S(2)}) collective-permute-start(bf16[64,2048]{1,0:T(8,128)(2,1)S(1)} %get-tuple-element.54), channel_id=1, source_target_pairs={{0,2},{1,3},{2,0},{3,1},{4,6},{5,7},{6,4},{7,5},{8,10},{9,11},{10,... | collective-permute-start | bytes 786440 | tf_op jit(solution)/shard_map/ppermute | solution.py:24
  3.9 1.2 %collective-permute-start = (bf16[64,2048]{1,0:T(8,128)(2,1)S(1)}, bf16[64,2048]{1,0:T(8,128)(2,1)S(1)}, u32[]{:S(2)}, u32[]{:S(2)}) collective-permute-start(bf16[64,2048]{1,0:T(8,128)(2,1)S(1)} %get-tuple-element.55.refs_0_), channel_id=1, source_target_pairs={{0,1},{1,0},{2,3},{3,2},{4,5},{5,4},{6,7},{7,6},{8,9},{9,8},{10,11... | collective-permute-start | bytes 786440 | tf_op jit(solution)/shard_map/ppermute | solution.py:24
  5.1 1.6 %copy-done = bf16[1,128,8192]{2,1,0:T(8,128)(2,1)S(1)} copy-done((bf16[1,128,8192]{2,1,0:T(8,128)(2,1)S(1)}, bf16[1,128,8192]{2,1,0:T(8,128)(2,1)}, u32[]{:S(2)}) %copy-start) | copy-done | bytes 2097176
  7.1 2.8 %collective-permute-done.1.refs_2_ = bf16[64,2048]{1,0:T(8,128)(2,1)S(1)} collective-permute-done((bf16[64,2048]{1,0:T(8,128)(2,1)S(1)}, bf16[64,2048]{1,0:T(8,128)(2,1)S(1)}, u32[]{:S(2)}, u32[]{:S(2)}) %collective-permute-start.1) | collective-permute-done | bytes 262176 | tf_op jit(solution)/shard_map/ppermute | solution.py:24
  9.9 1.1 %collective-permute-start.3 = (bf16[64,2048]{1,0:T(8,128)(2,1)S(1)}, bf16[64,2048]{1,0:T(8,128)(2,1)S(1)}, u32[]{:S(2)}, u32[]{:S(2)}) collective-permute-start(bf16[64,2048]{1,0:T(8,128)(2,1)S(1)} %collective-permute-done.1.refs_2_), channel_id=1, source_target_pairs={{0,1},{1,0},{2,3},{3,2},{4,5},{5,4},{6,7},{7,6},{8,9},{9,8},{10,11... | collective-permute-start | bytes 786440 | tf_op jit(solution)/shard_map/ppermute | solution.py:24
  11.0 1.2 %collective-permute-start.2 = (bf16[64,2048]{1,0:T(8,128)(2,1)S(1)}, bf16[64,2048]{1,0:T(8,128)(2,1)S(1)}, u32[]{:S(2)}, u32[]{:S(2)}) collective-permute-start(bf16[64,2048]{1,0:T(8,128)(2,1)S(1)} %collective-permute-done.refs_1_), channel_id=1, source_target_pairs={{0,2},{1,3},{2,0},{3,1},{4,6},{5,7},{6,4},{7,5},{8,10},{9,11},{10,... | collective-permute-start | bytes 786440 | tf_op jit(solution)/shard_map/ppermute | solution.py:24
  12.6 3.7 %collective-permute-done.4.refs_0_ = bf16[64,2048]{1,0:T(8,128)(2,1)S(1)} collective-permute-done((bf16[64,2048]{1,0:T(8,128)(2,1)S(1)}, bf16[64,2048]{1,0:T(8,128)(2,1)S(1)}, u32[]{:S(2)}, u32[]{:S(2)}) %collective-permute-start.4) | collective-permute-done | bytes 262176 | tf_op jit(solution)/shard_map/ppermute | solution.py:24
  16.7 0.6 %cut.5 = (bf16[128,2048]{1,0:T(8,128)(2,1)S(1)}, f32[8,128]{1,0:T(8,128)}) custom-call(bf16[128,8192]{1,0:T(8,128)(2,1)S(1)} %bitcast.12, f32[8,128]{1,0:T(8,128)S(1)} %get-tuple-element.29.refs_0_), custom_call_target="tpu_custom_call" | custom-call | flops 1000 | bytes 1000 | tf_op jit(solution)/shard_map/cut/pallas_call | solution.py:43
  17.9 4.1 %collective-permute-done.3.refs_2_ = bf16[64,2048]{1,0:T(8,128)(2,1)S(1)} collective-permute-done((bf16[64,2048]{1,0:T(8,128)(2,1)S(1)}, bf16[64,2048]{1,0:T(8,128)(2,1)S(1)}, u32[]{:S(2)}, u32[]{:S(2)}) %collective-permute-start.3) | collective-permute-done | bytes 262176 | tf_op jit(solution)/shard_map/ppermute | solution.py:24
  21.9 0.7 %project.4 = (f32[128,512]{1,0:T(8,128)S(1)}, bf16[128,512]{1,0:T(8,128)(2,1)S(1)}, bf16[256,2048]{1,0:T(8,128)(2,1)S(1)}) custom-call(bf16[128,2048]{1,0:T(8,128)(2,1)S(1)} %get-tuple-element.30.refs_0_, bf16[64,2048]{1,0:T(8,128)(2,1)S(1)} %collective-permute-done.2.refs_1_, bf16[64,2048]{1,0:T(8,128)(2,1)S(1)} %collective-permute-done.3.refs_2_, ...), custom_call_target="tpu_custom_call" | custom-call | flops 1000 | bytes 1000 | tf_op jit(solution)/shard_map/project/pallas_call | solution.py:73
  22.7 1.3 %collective-permute-start.6 = (bf16[128,512]{1,0:T(8,128)(2,1)S(1)}, bf16[128,512]{1,0:T(8,128)(2,1)S(1)}, u32[]{:S(2)}, u32[]{:S(2)}) collective-permute-start(bf16[128,512]{1,0:T(8,128)(2,1)S(1)} %get-tuple-element.35.refs_3_), channel_id=1, source_target_pairs={{0,3},{1,2},{2,1},{3,0},{4,7},{5,6},{6,5},{7,4},{8,11},{9,10},{10,... | collective-permute-start | bytes 393224 | tf_op jit(solution)/shard_map/ppermute | solution.py:24
  24.6 1.2 %collective-permute-start.11 = (bf16[64,512]{1,0:T(8,128)(2,1)S(1)}, bf16[64,512]{1,0:T(8,128)(2,1)S(1)}, u32[]{:S(2)}, u32[]{:S(2)}) collective-permute-start(bf16[64,512]{1,0:T(8,128)(2,1)S(1)} %get-tuple-element.33.refs_4_), channel_id=1, source_target_pairs={{0,2},{1,3},{2,0},{3,1},{4,6},{5,7},{6,4},{7,5},{8,10},{9,11},{10,... | collective-permute-start | bytes 196616 | tf_op jit(solution)/shard_map/ppermute | solution.py:24
  26.1 0.6 %prepare.2 = (bf16[128,256]{1,0:T(8,128)(2,1)S(1)}, bf16[2048,256]{1,0:T(8,128)(2,1)S(1)}, f32[8,128]{1,0:T(8,128)S(1)}) custom-call(bf16[256,2048]{1,0:T(8,128)(2,1)S(1)} %get-tuple-element.39.refs_0_, s32[1,128]{1,0:T(1,128)S(1)} %bitcast.19, s32[1,1]{1,0:T(1,128)S(6)} %copy.8.refs_2_.refs_3_.count, bf16[128,512]{1,0:T(8,128)(2,1)S(1)} %get-tuple-element.35.refs_3_), custom_call_target="tpu_custom_call" | custom-call | flops 1000 | bytes 1000 | tf_op jit(solution)/shard_map/prepare/pallas_call | solution.py:181
  26.7 0.8 %collective-permute-done.8.refs_0_ = bf16[64,2048]{1,0:T(8,128)(2,1)S(1)} collective-permute-done((bf16[64,2048]{1,0:T(8,128)(2,1)S(1)}, bf16[64,2048]{1,0:T(8,128)(2,1)S(1)}, u32[]{:S(2)}, u32[]{:S(2)}) %collective-permute-start.8) | collective-permute-done | bytes 262176 | tf_op jit(solution)/shard_map/ppermute | solution.py:24
  28.5 1.1 %collective-permute-start.10 = (bf16[64,512]{1,0:T(8,128)(2,1)S(1)}, bf16[64,512]{1,0:T(8,128)(2,1)S(1)}, u32[]{:S(2)}, u32[]{:S(2)}) collective-permute-start(bf16[64,512]{1,0:T(8,128)(2,1)S(1)} %get-tuple-element.41.refs_4_), channel_id=1, source_target_pairs={{0,1},{1,0},{2,3},{3,2},{4,5},{5,4},{6,7},{7,6},{8,9},{9,8},{10,11... | collective-permute-start | bytes 196616 | tf_op jit(solution)/shard_map/ppermute | solution.py:24
  29.6 0.6 %prepare.3 = (bf16[128,256]{1,0:T(8,128)(2,1)S(1)}, bf16[2048,256]{1,0:T(8,128)(2,1)S(1)}, f32[8,128]{1,0:T(8,128)S(1)}) custom-call(bf16[128,2048]{1,0:T(8,128)(2,1)S(1)} %get-tuple-element.43.refs_0_, bf16[128,2048]{1,0:T(8,128)(2,1)S(1)} %get-tuple-element.44.refs_1_, s32[1,128]{1,0:T(1,128)S(1)} %bitcast.20, s32[1,1]{1,0:T(1,128)S(6)} %copy.8.refs_2_.refs_3_.count, ...), custom_call_target="tpu_custom_call" | custom-call | flops 1000 | bytes 1000 | tf_op jit(solution)/shard_map/prepare/pallas_call | solution.py:181
  30.2 1.5 %collective-permute-done.7.refs_3_ = bf16[64,512]{1,0:T(8,128)(2,1)S(1)} collective-permute-done((bf16[64,512]{1,0:T(8,128)(2,1)S(1)}, bf16[64,512]{1,0:T(8,128)(2,1)S(1)}, u32[]{:S(2)}, u32[]{:S(2)}) %collective-permute-start.7) | collective-permute-done | bytes 65568 | tf_op jit(solution)/shard_map/ppermute | solution.py:24
  31.8 1.2 %collective-permute-done.12.refs_6_ = bf16[64,512]{1,0:T(8,128)(2,1)S(1)} collective-permute-done((bf16[64,512]{1,0:T(8,128)(2,1)S(1)}, bf16[64,512]{1,0:T(8,128)(2,1)S(1)}, u32[]{:S(2)}, u32[]{:S(2)}) %collective-permute-start.12) | collective-permute-done | bytes 65568 | tf_op jit(solution)/shard_map/ppermute | solution.py:24
  33.3 1.5 %collective-permute-start.15 = (bf16[128,512]{1,0:T(8,128)(2,1)S(1)}, bf16[128,512]{1,0:T(8,128)(2,1)S(1)}, u32[]{:S(2)}, u32[]{:S(2)}) collective-permute-start(bf16[128,512]{1,0:T(8,128)(2,1)S(1)} %slope.1.refs_0_.after), channel_id=1, source_target_pairs={{0,3},{1,2},{2,1},{3,0},{4,7},{5,6},{6,5},{7,4},{8,11},{9,10},{10,... | collective-permute-start | bytes 393224 | tf_op jit(solution)/shard_map/ppermute | solution.py:24
  34.8 0.7 %collective-permute-start.14 = (bf16[128,512]{1,0:T(8,128)(2,1)S(1)}, bf16[128,512]{1,0:T(8,128)(2,1)S(1)}, u32[]{:S(2)}, u32[]{:S(2)}) collective-permute-start(bf16[128,512]{1,0:T(8,128)(2,1)S(1)} %slope.1.refs_0_.after), channel_id=1, source_target_pairs={{0,2},{1,3},{2,0},{3,1},{4,6},{5,7},{6,4},{7,5},{8,10},{9,11},{10,... | collective-permute-start | bytes 393224 | tf_op jit(solution)/shard_map/ppermute | solution.py:24
  35.5 0.5 collective-permute-start.13
  36.0 1.1 %early.1 = (f32[128,128]{1,0:T(8,128)S(1)}, bf16[2048,512]{1,0:T(8,128)(2,1)S(1)}, f32[8,128]{1,0:T(8,128)}) custom-call(s32[1,128]{1,0:T(1,128)S(1)} %bitcast.21, s32[1,1]{1,0:T(1,128)S(6)} %copy.8.refs_2_.refs_3_.count, bf16[2048,512]{1,0:T(8,128)(2,1)S(1)} %bitcast.16, bf16[128,512]{1,0:T(8,128)(2,1)S(1)} %slope.1.refs_0_.after), custom_call_target="tpu_custom_call" | custom-call | flops 1000 | bytes 1000 | tf_op jit(solution)/shard_map/early/pallas_call | solution.py:145
  37.1 1.0 %collective-permute-done.15.refs_1_ = bf16[128,512]{1,0:T(8,128)(2,1)S(1)} collective-permute-done((bf16[128,512]{1,0:T(8,128)(2,1)S(1)}, bf16[128,512]{1,0:T(8,128)(2,1)S(1)}, u32[]{:S(2)}, u32[]{:S(2)}) %collective-permute-start.15) | collective-permute-done | bytes 131104 | tf_op jit(solution)/shard_map/ppermute | solution.py:24
  38.3 1.1 %collective-permute-done.14.refs_1_.refs_3_ = bf16[128,512]{1,0:T(8,128)(2,1)S(1)} collective-permute-done((bf16[128,512]{1,0:T(8,128)(2,1)S(1)}, bf16[128,512]{1,0:T(8,128)(2,1)S(1)}, u32[]{:S(2)}, u32[]{:S(2)}) %collective-permute-start.14) | collective-permute-done | bytes 131104 | tf_op jit(solution)/shard_map/ppermute | solution.py:24
  39.7 2.4 %collective-permute-start.16 = (bf16[144,128]{1,0:T(8,128)(2,1)S(1)}, bf16[144,128]{1,0:T(8,128)(2,1)S(1)}, u32[]{:S(2)}, u32[]{:S(2)}) collective-permute-start(bf16[144,128]{1,0:T(8,128)(2,1)S(1)} %kept.1.refs_0_), channel_id=1, source_target_pairs={{0,16},{4,20},{8,24},{12,28},{16,0},{20,4},{24,8},{28,12},{1,17},{... | collective-permute-start | bytes 110600 | tf_op jit(solution)/shard_map/ppermute | solution.py:24
  42.1 1.1 %collective-permute-start.17 = (bf16[144,128]{1,0:T(8,128)(2,1)S(1)}, bf16[144,128]{1,0:T(8,128)(2,1)S(1)}, u32[]{:S(2)}, u32[]{:S(2)}) collective-permute-start(bf16[144,128]{1,0:T(8,128)(2,1)S(1)} %kept.1.refs_0_), channel_id=1, source_target_pairs={{0,24},{4,28},{8,16},{12,20},{16,8},{20,12},{24,0},{28,4},{1,25},{... | collective-permute-start | bytes 110600 | tf_op jit(solution)/shard_map/ppermute | solution.py:24
  43.4 2.3 %residue.1 = (bf16[2048,512]{1,0:T(8,128)(2,1)}, f32[8,128]{1,0:T(8,128)S(1)}) custom-call(bf16[128,512]{1,0:T(8,128)(2,1)S(1)} %slope.1.refs_0_.after, bf16[128,512]{1,0:T(8,128)(2,1)S(1)} %collective-permute-done.15.refs_1_, bf16[128,512]{1,0:T(8,128)(2,1)S(1)} %collective-permute-done.13.refs_0_.refs_2_, ...), custom_call_target="tpu_custom_call" | custom-call | flops 1000 | bytes 1000 | tf_op jit(solution)/shard_map/residue/pallas_call | solution.py:274
  45.8 0.9 %collective-permute-done.17.refs_1_ = bf16[144,128]{1,0:T(8,128)(2,1)S(1)} collective-permute-done((bf16[144,128]{1,0:T(8,128)(2,1)S(1)}, bf16[144,128]{1,0:T(8,128)(2,1)S(1)}, u32[]{:S(2)}, u32[]{:S(2)}) %collective-permute-start.17) | collective-permute-done | bytes 36896 | tf_op jit(solution)/shard_map/ppermute | solution.py:24
  46.8 6.4 %collective-permute-start.19 = (bf16[576,128]{1,0:T(8,128)(2,1)S(1)}, bf16[576,128]{1,0:T(8,128)(2,1)S(1)}, u32[]{:S(2)}, u32[]{:S(2)}) collective-permute-start(bf16[576,128]{1,0:T(8,128)(2,1)S(1)} %join.5.group), channel_id=1, source_target_pairs={{0,4},{4,0},{8,12},{12,8},{16,20},{20,16},{24,28},{28,24},{1,5},{5... | collective-permute-start | bytes 442376 | tf_op jit(solution)/shard_map/ppermute | solution.py:24
  53.1 1.4 %half.1 = f32[2048,512]{1,0:T(8,128)S(1)} custom-call(bf16[576,128]{1,0:T(8,128)(2,1)S(1)} %join.5.group), custom_call_target="tpu_custom_call" | custom-call | flops 1000 | bytes 1000 | tf_op jit(solution)/shard_map/half/pallas_call | solution.py:356
  54.6 2.5 %outer.1 = f32[2048,512]{1,0:T(8,128)} custom-call(bf16[576,128]{1,0:T(8,128)(2,1)S(1)} %collective-permute-done.19.group, f32[2048,512]{1,0:T(8,128)S(1)} %half.1), custom_call_target="tpu_custom_call" | custom-call | flops 1000 | bytes 1000 | tf_op jit(solution)/shard_map/outer/pallas_call | solution.py:364
  (37 shorter events, 3.8 us)
Async XLA Ops:
  1.7 8.2 %collective-permute-start.1 = (bf16[64,2048]{1,0:T(8,128)(2,1)S(1)}, bf16[64,2048]{1,0:T(8,128)(2,1)S(1)}, u32[]{:S(2)}, u32[]{:S(2)}) collective-permute-start(bf16[64,2048]{1,0:T(8,128)(2,1)S(1)} %get-tuple-element.54), channel_id=1, source_target_pairs={{0,2},{1,3},{2,0},{3,1},{4,6},{5,7},{6,4},{7,5},{8,10},{9,11},{10,... | collective-permute-start | bytes 786440 | tf_op jit(solution)/shard_map/ppermute | solution.py:24
  3.9 7.1 %collective-permute-start = (bf16[64,2048]{1,0:T(8,128)(2,1)S(1)}, bf16[64,2048]{1,0:T(8,128)(2,1)S(1)}, u32[]{:S(2)}, u32[]{:S(2)}) collective-permute-start(bf16[64,2048]{1,0:T(8,128)(2,1)S(1)} %get-tuple-element.55.refs_0_), channel_id=1, source_target_pairs={{0,1},{1,0},{2,3},{3,2},{4,5},{5,4},{6,7},{7,6},{8,9},{9,8},{10,11... | collective-permute-start | bytes 786440 | tf_op jit(solution)/shard_map/ppermute | solution.py:24
  5.1 1.6 %copy-start = (bf16[1,128,8192]{2,1,0:T(8,128)(2,1)S(1)}, bf16[1,128,8192]{2,1,0:T(8,128)(2,1)}, u32[]{:S(2)}) copy-start(bf16[1,128,8192]{2,1,0:T(8,128)(2,1)} %param.6) | copy-start | bytes 6291460
  6.7 9.6 %collective-permute-start.4 = (bf16[64,2048]{1,0:T(8,128)(2,1)S(1)}, bf16[64,2048]{1,0:T(8,128)(2,1)S(1)}, u32[]{:S(2)}, u32[]{:S(2)}) collective-permute-start(bf16[64,2048]{1,0:T(8,128)(2,1)S(1)} %get-tuple-element.31), channel_id=1, source_target_pairs={{0,1},{1,0},{2,3},{3,2},{4,5},{5,4},{6,7},{7,6},{8,9},{9,8},{10,11... | collective-permute-start | bytes 786440 | tf_op jit(solution)/shard_map/ppermute | solution.py:24
  7.0 10.3 %collective-permute-start.5 = (bf16[64,2048]{1,0:T(8,128)(2,1)S(1)}, bf16[64,2048]{1,0:T(8,128)(2,1)S(1)}, u32[]{:S(2)}, u32[]{:S(2)}) collective-permute-start(bf16[64,2048]{1,0:T(8,128)(2,1)S(1)} %get-tuple-element.32), channel_id=1, source_target_pairs={{0,2},{1,3},{2,0},{3,1},{4,6},{5,7},{6,4},{7,5},{8,10},{9,11},{10,... | collective-permute-start | bytes 786440 | tf_op jit(solution)/shard_map/ppermute | solution.py:24
  9.9 12.1 %collective-permute-start.3 = (bf16[64,2048]{1,0:T(8,128)(2,1)S(1)}, bf16[64,2048]{1,0:T(8,128)(2,1)S(1)}, u32[]{:S(2)}, u32[]{:S(2)}) collective-permute-start(bf16[64,2048]{1,0:T(8,128)(2,1)S(1)} %collective-permute-done.1.refs_2_), channel_id=1, source_target_pairs={{0,1},{1,0},{2,3},{3,2},{4,5},{5,4},{6,7},{7,6},{8,9},{9,8},{10,11... | collective-permute-start | bytes 786440 | tf_op jit(solution)/shard_map/ppermute | solution.py:24
  11.0 10.9 %collective-permute-start.2 = (bf16[64,2048]{1,0:T(8,128)(2,1)S(1)}, bf16[64,2048]{1,0:T(8,128)(2,1)S(1)}, u32[]{:S(2)}, u32[]{:S(2)}) collective-permute-start(bf16[64,2048]{1,0:T(8,128)(2,1)S(1)} %collective-permute-done.refs_1_), channel_id=1, source_target_pairs={{0,2},{1,3},{2,0},{3,1},{4,6},{5,7},{6,4},{7,5},{8,10},{9,11},{10,... | collective-permute-start | bytes 786440 | tf_op jit(solution)/shard_map/ppermute | solution.py:24
  12.2 5.1 %copy-start.1 = (bf16[1,2048,512]{2,1,0:T(8,128)(2,1)S(1)}, bf16[1,2048,512]{2,1,0:T(8,128)(2,1)}, u32[]{:S(2)}) copy-start(bf16[1,2048,512]{2,1,0:T(8,128)(2,1)} %param.8) | copy-start | bytes 6291460
  12.3 15.3 %collective-permute-start.8 = (bf16[64,2048]{1,0:T(8,128)(2,1)S(1)}, bf16[64,2048]{1,0:T(8,128)(2,1)S(1)}, u32[]{:S(2)}, u32[]{:S(2)}) collective-permute-start(bf16[64,2048]{1,0:T(8,128)(2,1)S(1)} %get-tuple-element.37), channel_id=1, source_target_pairs={{0,1},{1,0},{2,3},{3,2},{4,5},{5,4},{6,7},{7,6},{8,9},{9,8},{10,11... | collective-permute-start | bytes 786440 | tf_op jit(solution)/shard_map/ppermute | solution.py:24
  16.3 11.2 %collective-permute-start.9 = (bf16[64,2048]{1,0:T(8,128)(2,1)S(1)}, bf16[64,2048]{1,0:T(8,128)(2,1)S(1)}, u32[]{:S(2)}, u32[]{:S(2)}) collective-permute-start(bf16[64,2048]{1,0:T(8,128)(2,1)S(1)} %get-tuple-element.38), channel_id=1, source_target_pairs={{0,2},{1,3},{2,0},{3,1},{4,6},{5,7},{6,4},{7,5},{8,10},{9,11},{10,... | collective-permute-start | bytes 786440 | tf_op jit(solution)/shard_map/ppermute | solution.py:24
  17.9 8.2 %copy-start.4 = (s32[1,1,128]{2,1,0:T(1,128)S(1)}, s32[1,1,128]{2,1,0:T(1,128)}, u32[]{:S(2)}) copy-start(s32[1,1,128]{2,1,0:T(1,128)} %param.11) | copy-start | bytes 1540
  22.7 10.5 %collective-permute-start.6 = (bf16[128,512]{1,0:T(8,128)(2,1)S(1)}, bf16[128,512]{1,0:T(8,128)(2,1)S(1)}, u32[]{:S(2)}, u32[]{:S(2)}) collective-permute-start(bf16[128,512]{1,0:T(8,128)(2,1)S(1)} %get-tuple-element.35.refs_3_), channel_id=1, source_target_pairs={{0,3},{1,2},{2,1},{3,0},{4,7},{5,6},{6,5},{7,4},{8,11},{9,10},{10,... | collective-permute-start | bytes 393224 | tf_op jit(solution)/shard_map/ppermute | solution.py:24
  24.6 7.2 %collective-permute-start.11 = (bf16[64,512]{1,0:T(8,128)(2,1)S(1)}, bf16[64,512]{1,0:T(8,128)(2,1)S(1)}, u32[]{:S(2)}, u32[]{:S(2)}) collective-permute-start(bf16[64,512]{1,0:T(8,128)(2,1)S(1)} %get-tuple-element.33.refs_4_), channel_id=1, source_target_pairs={{0,2},{1,3},{2,0},{3,1},{4,6},{5,7},{6,4},{7,5},{8,10},{9,11},{10,... | collective-permute-start | bytes 196616 | tf_op jit(solution)/shard_map/ppermute | solution.py:24
  25.8 5.9 %collective-permute-start.7 = (bf16[64,512]{1,0:T(8,128)(2,1)S(1)}, bf16[64,512]{1,0:T(8,128)(2,1)S(1)}, u32[]{:S(2)}, u32[]{:S(2)}) collective-permute-start(bf16[64,512]{1,0:T(8,128)(2,1)S(1)} %get-tuple-element.36), channel_id=1, source_target_pairs={{0,1},{1,0},{2,3},{3,2},{4,5},{5,4},{6,7},{7,6},{8,9},{9,8},{10,11... | collective-permute-start | bytes 196616 | tf_op jit(solution)/shard_map/ppermute | solution.py:24
  26.7 6.5 %copy-start.3 = (bf16[1,128,512]{2,1,0:T(8,128)(2,1)S(1)}, bf16[1,128,512]{2,1,0:T(8,128)(2,1)}, u32[]{:S(2)}) copy-start(bf16[1,128,512]{2,1,0:T(8,128)(2,1)} %param.7) | copy-start | bytes 393220
  27.6 8.4 %copy-start.2 = (bf16[1,2048,512]{2,1,0:T(8,128)(2,1)S(1)}, bf16[1,2048,512]{2,1,0:T(8,128)(2,1)}, u32[]{:S(2)}) copy-start(bf16[1,2048,512]{2,1,0:T(8,128)(2,1)} %param.9) | copy-start | bytes 6291460
  28.0 5.0 %collective-permute-start.12 = (bf16[64,512]{1,0:T(8,128)(2,1)S(1)}, bf16[64,512]{1,0:T(8,128)(2,1)S(1)}, u32[]{:S(2)}, u32[]{:S(2)}) collective-permute-start(bf16[64,512]{1,0:T(8,128)(2,1)S(1)} %get-tuple-element.42), channel_id=1, source_target_pairs={{0,2},{1,3},{2,0},{3,1},{4,6},{5,7},{6,4},{7,5},{8,10},{9,11},{10,... | collective-permute-start | bytes 196616 | tf_op jit(solution)/shard_map/ppermute | solution.py:24
  28.5 4.7 %collective-permute-start.10 = (bf16[64,512]{1,0:T(8,128)(2,1)S(1)}, bf16[64,512]{1,0:T(8,128)(2,1)S(1)}, u32[]{:S(2)}, u32[]{:S(2)}) collective-permute-start(bf16[64,512]{1,0:T(8,128)(2,1)S(1)} %get-tuple-element.41.refs_4_), channel_id=1, source_target_pairs={{0,1},{1,0},{2,3},{3,2},{4,5},{5,4},{6,7},{7,6},{8,9},{9,8},{10,11... | collective-permute-start | bytes 196616 | tf_op jit(solution)/shard_map/ppermute | solution.py:24
  33.3 4.9 %collective-permute-start.15 = (bf16[128,512]{1,0:T(8,128)(2,1)S(1)}, bf16[128,512]{1,0:T(8,128)(2,1)S(1)}, u32[]{:S(2)}, u32[]{:S(2)}) collective-permute-start(bf16[128,512]{1,0:T(8,128)(2,1)S(1)} %slope.1.refs_0_.after), channel_id=1, source_target_pairs={{0,3},{1,2},{2,1},{3,0},{4,7},{5,6},{6,5},{7,4},{8,11},{9,10},{10,... | collective-permute-start | bytes 393224 | tf_op jit(solution)/shard_map/ppermute | solution.py:24
  34.8 4.6 %collective-permute-start.14 = (bf16[128,512]{1,0:T(8,128)(2,1)S(1)}, bf16[128,512]{1,0:T(8,128)(2,1)S(1)}, u32[]{:S(2)}, u32[]{:S(2)}) collective-permute-start(bf16[128,512]{1,0:T(8,128)(2,1)S(1)} %slope.1.refs_0_.after), channel_id=1, source_target_pairs={{0,2},{1,3},{2,0},{3,1},{4,6},{5,7},{6,4},{7,5},{8,10},{9,11},{10,... | collective-permute-start | bytes 393224 | tf_op jit(solution)/shard_map/ppermute | solution.py:24
  35.5 4.0 %collective-permute-start.13 = (bf16[128,512]{1,0:T(8,128)(2,1)S(1)}, bf16[128,512]{1,0:T(8,128)(2,1)S(1)}, u32[]{:S(2)}, u32[]{:S(2)}) collective-permute-start(bf16[128,512]{1,0:T(8,128)(2,1)S(1)} %slope.1.refs_0_.after), channel_id=1, source_target_pairs={{0,1},{1,0},{2,3},{3,2},{4,5},{5,4},{6,7},{7,6},{8,9},{9,8},{10,11... | collective-permute-start | bytes 393224 | tf_op jit(solution)/shard_map/ppermute | solution.py:24
  39.7 6.0 %collective-permute-start.16 = (bf16[144,128]{1,0:T(8,128)(2,1)S(1)}, bf16[144,128]{1,0:T(8,128)(2,1)S(1)}, u32[]{:S(2)}, u32[]{:S(2)}) collective-permute-start(bf16[144,128]{1,0:T(8,128)(2,1)S(1)} %kept.1.refs_0_), channel_id=1, source_target_pairs={{0,16},{4,20},{8,24},{12,28},{16,0},{20,4},{24,8},{28,12},{1,17},{... | collective-permute-start | bytes 110600 | tf_op jit(solution)/shard_map/ppermute | solution.py:24
  42.1 4.6 %collective-permute-start.17 = (bf16[144,128]{1,0:T(8,128)(2,1)S(1)}, bf16[144,128]{1,0:T(8,128)(2,1)S(1)}, u32[]{:S(2)}, u32[]{:S(2)}) collective-permute-start(bf16[144,128]{1,0:T(8,128)(2,1)S(1)} %kept.1.refs_0_), channel_id=1, source_target_pairs={{0,24},{4,28},{8,16},{12,20},{16,8},{20,12},{24,0},{28,4},{1,25},{... | collective-permute-start | bytes 110600 | tf_op jit(solution)/shard_map/ppermute | solution.py:24
  43.2 3.5 %collective-permute-start.18 = (bf16[144,128]{1,0:T(8,128)(2,1)S(1)}, bf16[144,128]{1,0:T(8,128)(2,1)S(1)}, u32[]{:S(2)}, u32[]{:S(2)}) collective-permute-start(bf16[144,128]{1,0:T(8,128)(2,1)S(1)} %kept.1.refs_0_), channel_id=1, source_target_pairs={{0,8},{4,12},{8,0},{12,4},{16,24},{20,28},{24,16},{28,20},{1,9},{5... | collective-permute-start | bytes 110600 | tf_op jit(solution)/shard_map/ppermute | solution.py:24
  46.8 7.8 %collective-permute-start.19 = (bf16[576,128]{1,0:T(8,128)(2,1)S(1)}, bf16[576,128]{1,0:T(8,128)(2,1)S(1)}, u32[]{:S(2)}, u32[]{:S(2)}) collective-permute-start(bf16[576,128]{1,0:T(8,128)(2,1)S(1)} %join.5.group), channel_id=1, source_target_pairs={{0,4},{4,0},{8,12},{12,8},{16,20},{20,16},{24,28},{28,24},{1,5},{5... | collective-permute-start | bytes 442376 | tf_op jit(solution)/shard_map/ppermute | solution.py:24

commit v22 on v21

--- a/solution.py
+++ b/solution.py
@@ -330,8 +330,31 @@
     return jnp.dot(hot, wide[...], preferred_element_type=jnp.float32)
 
 
-def half_kernel(cap, per_row, tile, group, out, wide, lines):
-    spread(group, wide, lines, cap, per_row)
+def unpack_kernel(cap, per_row, message, *refs):
+    wide, lines = refs[-2:]
+    spread(message, wide, lines, cap, per_row)
+
+
+def unpack(message, cap, kw, after):
+    return pl.pallas_call(
+        functools.partial(unpack_kernel, cap, kw // LANES),
+        out_shape=[
+            jax.ShapeDtypeStruct((cap, kw), jnp.bfloat16),
+            jax.ShapeDtypeStruct((8, cap), jnp.int32),
+        ],
+        in_specs=[VMEM] + [ANY] * len(after),
+        compiler_params=params(4),
+        cost_estimate=BRIEF,
+        name="unpack",
+    )(message, *after)
+
+
+def half_kernel(tile, n, *refs):
+    wides, rows_of, (out, wide, lines) = refs[:n], refs[n : 2 * n], refs[2 * n :]
+    cap = wides[0].shape[0]
+    for k in range(n):
+        wide[k * cap : (k + 1) * cap, :] = wides[k][...]
+        lines[:, k * cap : (k + 1) * cap] = rows_of[k][...]
     for t in range(out.shape[0] // tile):
         out[t * tile : (t + 1) * tile, :] = place(lines, wide, t, tile)
 
@@ -347,20 +370,20 @@
         send_out(held, out, sems, t, tile).wait()
 
 
-def outer(groups, cap, depth, kw):
-    slots = groups[0].shape[0] // (cap + 16) * cap
+def outer(group, unpacked, cap, depth, kw):
+    slots = len(unpacked) * cap
     n = 2 * slots // cap
     tile = min(depth, 256)
     shape = jax.ShapeDtypeStruct((depth, kw), jnp.float32)
     scratch = [pltpu.VMEM((slots, kw), jnp.bfloat16), pltpu.VMEM((8, slots), jnp.int32)]
     half = pl.pallas_call(
-        functools.partial(half_kernel, cap, kw // LANES, tile),
+        functools.partial(half_kernel, min(depth, 512), len(unpacked)),
         out_shape=shape,
         scratch_shapes=scratch,
         compiler_params=params(14),
         cost_estimate=BRIEF,
         name="half",
-    )(groups[0])
+    )(*[wide for wide, _ in unpacked], *[lines for _, lines in unpacked])
     return pl.pallas_call(
         functools.partial(outer_kernel, cap, kw // LANES, tile, n),
         out_shape=shape,
@@ -370,7 +393,7 @@
         compiler_params=params(14),
         cost_estimate=BRIEF,
         name="outer",
-    )(groups[1], half)
+    )(group, half)
 
 
 def on_device(inputs, target, weights, feedback, counts, blocks):
@@ -439,11 +462,13 @@
     same_core = [swap(message, "rep", n_rep, d) for d in chips]
     order = order_far + [(n_far + k, low, high) for k, low, high in order_near]
     new_feedback, token = residue(slopes, order, [xt_far, xt_near], fb, keep)
-    joined, after = message, [token]
+    cap = slot_row.shape[1]
+    joined, after, unpacked = message, [token], [unpack(message, cap, kw, [token])]
     for received in same_core:
-        joined, after = join([joined, received], after), []
-    groups = [joined, swap(joined, "rep", n_rep, 1)]
-    return outer(groups, message.shape[0] - 16, depth, kw), new_feedback[None]
+        joined, after = join([joined, received], after + [unpacked[-1][1]]), []
+        unpacked.append(unpack(received, cap, kw, [token]))
+    group = swap(joined, "rep", n_rep, 1)
+    return outer(group, unpacked, cap, depth, kw), new_feedback[None]
 
 
 def solution(mesh):

time: 57.3 us -> 57.4 us (level)
    pallas_call x1 -> x5, Pallas kernels: 1.41 us -> 1.72 us  [the longest x1 1.26 us: outer(): pl.pallas_call(functools.partial(half_kernel, min(depth, 512), len(unpack...]
  transfers between devices with their start and end apart: 20 -> 20, of which waited for: 10 -> 10; matrix products, arithmetic and copies ran while one was open for 0% -> 0% of each run, Pallas kernels for 15% -> 16%
where the time goes in v22:
time: 57.4 us; the launch traced here: 57.2 us
  starting transfers between devices  24 us (42%)
  waiting for transfers between devices  17.2 us (30%)
  Pallas kernels  11.8 us (21%)
  local copies, waits for them, and re-layouts  2.68 us (5%)
  between operations  1.52 us (3%)
    ppermute x20, starting transfers between devices, swap(): return lax.ppermute(x, axis, [(i, i ^ d) for i in range(n)])  24 us
    ppermute x20, waiting for transfers between devices, swap(): return lax.ppermute(x, axis, [(i, i ^ d) for i in range(n)])  17.2 us
    pallas_call x1, Pallas kernels, outer(): pl.pallas_call(functools.partial(outer_kernel, cap, kw // LANES, tile, n)...  2.54 us
    pallas_call x1, Pallas kernels, residue(): pl.pallas_call(functools.partial(residue_kernel, order, tile), out_shape=...  2.33 us
    pallas_call x3, Pallas kernels, project(): pl.pallas_call(functools.partial(project_kernel, n, len(outs)), out_shape...  1.62 us
    unnamed x10, local copies, waits for them, and re-layouts  1.61 us
    pallas_call x1, Pallas kernels, outer(): pl.pallas_call(functools.partial(half_kernel, min(depth, 512), len(unpack...  1.26 us
    pallas_call x2, Pallas kernels, prepare(): pl.pallas_call(functools.partial(prepare_kernel, per_row, len(xs)), out_s...  1.21 us
  transfers between devices with their start and end apart: 20, of which 10 were waited for; matrix products, arithmetic and copies ran while one was open for 0% of the time, Pallas kernels for 16%

profile of v22, /device:TPU:1, one launch (start us, length us, event | category | flops | bytes accessed | tf_op | source)
XLA Modules:
  0.0 57.2 jit_solution(5176702937065617903)
XLA Ops:
  0.6 1.1 %dynamic-slice_bitcast_fusion = (bf16[64,2048]{1,0:T(8,128)(2,1)S(1)}, bf16[64,2048]{1,0:T(8,128)(2,1)S(1)}) fusion(bf16[1,128,8192]{2,1,0:T(8,128)(2,1)} %param.6, s32[]{:T(128)S(6)} %select_n.4), kind=kLoop, calls=%fused_computation | loop fusion | bytes 1048580 | tf_op jit(solution)/shard_map/dynamic_slice | solution.py:415
  1.7 2.1 %collective-permute-start.1 = (bf16[64,2048]{1,0:T(8,128)(2,1)S(1)}, bf16[64,2048]{1,0:T(8,128)(2,1)S(1)}, u32[]{:S(2)}, u32[]{:S(2)}) collective-permute-start(bf16[64,2048]{1,0:T(8,128)(2,1)S(1)} %get-tuple-element.70), channel_id=1, source_target_pairs={{0,2},{1,3},{2,0},{3,1},{4,6},{5,7},{6,4},{7,5},{8,10},{9,11},{10,... | collective-permute-start | bytes 786440 | tf_op jit(solution)/shard_map/ppermute | solution.py:24
  3.9 1.2 %collective-permute-start = (bf16[64,2048]{1,0:T(8,128)(2,1)S(1)}, bf16[64,2048]{1,0:T(8,128)(2,1)S(1)}, u32[]{:S(2)}, u32[]{:S(2)}) collective-permute-start(bf16[64,2048]{1,0:T(8,128)(2,1)S(1)} %get-tuple-element.71.refs_0_), channel_id=1, source_target_pairs={{0,1},{1,0},{2,3},{3,2},{4,5},{5,4},{6,7},{7,6},{8,9},{9,8},{10,11... | collective-permute-start | bytes 786440 | tf_op jit(solution)/shard_map/ppermute | solution.py:24
  5.1 1.6 %copy-done = bf16[1,128,8192]{2,1,0:T(8,128)(2,1)S(1)} copy-done((bf16[1,128,8192]{2,1,0:T(8,128)(2,1)S(1)}, bf16[1,128,8192]{2,1,0:T(8,128)(2,1)}, u32[]{:S(2)}) %copy-start) | copy-done | bytes 2097176
  7.1 2.8 %collective-permute-done.1.refs_2_ = bf16[64,2048]{1,0:T(8,128)(2,1)S(1)} collective-permute-done((bf16[64,2048]{1,0:T(8,128)(2,1)S(1)}, bf16[64,2048]{1,0:T(8,128)(2,1)S(1)}, u32[]{:S(2)}, u32[]{:S(2)}) %collective-permute-start.1) | collective-permute-done | bytes 262176 | tf_op jit(solution)/shard_map/ppermute | solution.py:24
  9.9 1.1 %collective-permute-start.3 = (bf16[64,2048]{1,0:T(8,128)(2,1)S(1)}, bf16[64,2048]{1,0:T(8,128)(2,1)S(1)}, u32[]{:S(2)}, u32[]{:S(2)}) collective-permute-start(bf16[64,2048]{1,0:T(8,128)(2,1)S(1)} %collective-permute-done.1.refs_2_), channel_id=1, source_target_pairs={{0,1},{1,0},{2,3},{3,2},{4,5},{5,4},{6,7},{7,6},{8,9},{9,8},{10,11... | collective-permute-start | bytes 786440 | tf_op jit(solution)/shard_map/ppermute | solution.py:24
  11.0 1.2 %collective-permute-start.2 = (bf16[64,2048]{1,0:T(8,128)(2,1)S(1)}, bf16[64,2048]{1,0:T(8,128)(2,1)S(1)}, u32[]{:S(2)}, u32[]{:S(2)}) collective-permute-start(bf16[64,2048]{1,0:T(8,128)(2,1)S(1)} %collective-permute-done.refs_1_), channel_id=1, source_target_pairs={{0,2},{1,3},{2,0},{3,1},{4,6},{5,7},{6,4},{7,5},{8,10},{9,11},{10,... | collective-permute-start | bytes 786440 | tf_op jit(solution)/shard_map/ppermute | solution.py:24
  12.6 3.7 %collective-permute-done.4.refs_0_ = bf16[64,2048]{1,0:T(8,128)(2,1)S(1)} collective-permute-done((bf16[64,2048]{1,0:T(8,128)(2,1)S(1)}, bf16[64,2048]{1,0:T(8,128)(2,1)S(1)}, u32[]{:S(2)}, u32[]{:S(2)}) %collective-permute-start.4) | collective-permute-done | bytes 262176 | tf_op jit(solution)/shard_map/ppermute | solution.py:24
  16.7 0.6 %cut.5 = (bf16[128,2048]{1,0:T(8,128)(2,1)S(1)}, f32[8,128]{1,0:T(8,128)}) custom-call(bf16[128,8192]{1,0:T(8,128)(2,1)S(1)} %bitcast.12, f32[8,128]{1,0:T(8,128)S(1)} %get-tuple-element.37.refs_0_), custom_call_target="tpu_custom_call" | custom-call | flops 1000 | bytes 1000 | tf_op jit(solution)/shard_map/cut/pallas_call | solution.py:43
  17.9 4.1 %collective-permute-done.3.refs_2_ = bf16[64,2048]{1,0:T(8,128)(2,1)S(1)} collective-permute-done((bf16[64,2048]{1,0:T(8,128)(2,1)S(1)}, bf16[64,2048]{1,0:T(8,128)(2,1)S(1)}, u32[]{:S(2)}, u32[]{:S(2)}) %collective-permute-start.3) | collective-permute-done | bytes 262176 | tf_op jit(solution)/shard_map/ppermute | solution.py:24
  21.9 0.7 %project.4 = (f32[128,512]{1,0:T(8,128)S(1)}, bf16[128,512]{1,0:T(8,128)(2,1)S(1)}, bf16[256,2048]{1,0:T(8,128)(2,1)S(1)}) custom-call(bf16[128,2048]{1,0:T(8,128)(2,1)S(1)} %get-tuple-element.38.refs_0_, bf16[64,2048]{1,0:T(8,128)(2,1)S(1)} %collective-permute-done.2.refs_1_, bf16[64,2048]{1,0:T(8,128)(2,1)S(1)} %collective-permute-done.3.refs_2_, ...), custom_call_target="tpu_custom_call" | custom-call | flops 1000 | bytes 1000 | tf_op jit(solution)/shard_map/project/pallas_call | solution.py:73
  22.7 1.3 %collective-permute-start.6 = (bf16[128,512]{1,0:T(8,128)(2,1)S(1)}, bf16[128,512]{1,0:T(8,128)(2,1)S(1)}, u32[]{:S(2)}, u32[]{:S(2)}) collective-permute-start(bf16[128,512]{1,0:T(8,128)(2,1)S(1)} %get-tuple-element.43.refs_3_), channel_id=1, source_target_pairs={{0,3},{1,2},{2,1},{3,0},{4,7},{5,6},{6,5},{7,4},{8,11},{9,10},{10,... | collective-permute-start | bytes 393224 | tf_op jit(solution)/shard_map/ppermute | solution.py:24
  24.6 1.2 %collective-permute-start.11 = (bf16[64,512]{1,0:T(8,128)(2,1)S(1)}, bf16[64,512]{1,0:T(8,128)(2,1)S(1)}, u32[]{:S(2)}, u32[]{:S(2)}) collective-permute-start(bf16[64,512]{1,0:T(8,128)(2,1)S(1)} %get-tuple-element.41.refs_4_), channel_id=1, source_target_pairs={{0,2},{1,3},{2,0},{3,1},{4,6},{5,7},{6,4},{7,5},{8,10},{9,11},{10,... | collective-permute-start | bytes 196616 | tf_op jit(solution)/shard_map/ppermute | solution.py:24
  26.1 0.6 %prepare.2 = (bf16[128,256]{1,0:T(8,128)(2,1)S(1)}, bf16[2048,256]{1,0:T(8,128)(2,1)S(1)}, f32[8,128]{1,0:T(8,128)S(1)}) custom-call(bf16[256,2048]{1,0:T(8,128)(2,1)S(1)} %get-tuple-element.47.refs_0_, s32[1,128]{1,0:T(1,128)S(1)} %bitcast.19, s32[1,1]{1,0:T(1,128)S(6)} %copy.8.refs_2_.refs_3_.count, bf16[128,512]{1,0:T(8,128)(2,1)S(1)} %get-tuple-element.43.refs_3_), custom_call_target="tpu_custom_call" | custom-call | flops 1000 | bytes 1000 | tf_op jit(solution)/shard_map/prepare/pallas_call | solution.py:181
  26.7 0.8 %collective-permute-done.8.refs_0_ = bf16[64,2048]{1,0:T(8,128)(2,1)S(1)} collective-permute-done((bf16[64,2048]{1,0:T(8,128)(2,1)S(1)}, bf16[64,2048]{1,0:T(8,128)(2,1)S(1)}, u32[]{:S(2)}, u32[]{:S(2)}) %collective-permute-start.8) | collective-permute-done | bytes 262176 | tf_op jit(solution)/shard_map/ppermute | solution.py:24
  28.5 1.1 %collective-permute-start.10 = (bf16[64,512]{1,0:T(8,128)(2,1)S(1)}, bf16[64,512]{1,0:T(8,128)(2,1)S(1)}, u32[]{:S(2)}, u32[]{:S(2)}) collective-permute-start(bf16[64,512]{1,0:T(8,128)(2,1)S(1)} %get-tuple-element.49.refs_4_), channel_id=1, source_target_pairs={{0,1},{1,0},{2,3},{3,2},{4,5},{5,4},{6,7},{7,6},{8,9},{9,8},{10,11... | collective-permute-start | bytes 196616 | tf_op jit(solution)/shard_map/ppermute | solution.py:24
  29.6 0.6 %prepare.3 = (bf16[128,256]{1,0:T(8,128)(2,1)S(1)}, bf16[2048,256]{1,0:T(8,128)(2,1)S(1)}, f32[8,128]{1,0:T(8,128)S(1)}) custom-call(bf16[128,2048]{1,0:T(8,128)(2,1)S(1)} %get-tuple-element.51.refs_0_, bf16[128,2048]{1,0:T(8,128)(2,1)S(1)} %get-tuple-element.52.refs_1_, s32[1,128]{1,0:T(1,128)S(1)} %bitcast.20, s32[1,1]{1,0:T(1,128)S(6)} %copy.8.refs_2_.refs_3_.count, ...), custom_call_target="tpu_custom_call" | custom-call | flops 1000 | bytes 1000 | tf_op jit(solution)/shard_map/prepare/pallas_call | solution.py:181
  30.2 1.5 %collective-permute-done.7.refs_3_ = bf16[64,512]{1,0:T(8,128)(2,1)S(1)} collective-permute-done((bf16[64,512]{1,0:T(8,128)(2,1)S(1)}, bf16[64,512]{1,0:T(8,128)(2,1)S(1)}, u32[]{:S(2)}, u32[]{:S(2)}) %collective-permute-start.7) | collective-permute-done | bytes 65568 | tf_op jit(solution)/shard_map/ppermute | solution.py:24
  31.8 1.2 %collective-permute-done.12.refs_6_ = bf16[64,512]{1,0:T(8,128)(2,1)S(1)} collective-permute-done((bf16[64,512]{1,0:T(8,128)(2,1)S(1)}, bf16[64,512]{1,0:T(8,128)(2,1)S(1)}, u32[]{:S(2)}, u32[]{:S(2)}) %collective-permute-start.12) | collective-permute-done | bytes 65568 | tf_op jit(solution)/shard_map/ppermute | solution.py:24
  33.3 1.5 %collective-permute-start.15 = (bf16[128,512]{1,0:T(8,128)(2,1)S(1)}, bf16[128,512]{1,0:T(8,128)(2,1)S(1)}, u32[]{:S(2)}, u32[]{:S(2)}) collective-permute-start(bf16[128,512]{1,0:T(8,128)(2,1)S(1)} %slope.1.refs_0_.after), channel_id=1, source_target_pairs={{0,3},{1,2},{2,1},{3,0},{4,7},{5,6},{6,5},{7,4},{8,11},{9,10},{10,... | collective-permute-start | bytes 393224 | tf_op jit(solution)/shard_map/ppermute | solution.py:24
  34.8 0.7 %collective-permute-start.14 = (bf16[128,512]{1,0:T(8,128)(2,1)S(1)}, bf16[128,512]{1,0:T(8,128)(2,1)S(1)}, u32[]{:S(2)}, u32[]{:S(2)}) collective-permute-start(bf16[128,512]{1,0:T(8,128)(2,1)S(1)} %slope.1.refs_0_.after), channel_id=1, source_target_pairs={{0,2},{1,3},{2,0},{3,1},{4,6},{5,7},{6,4},{7,5},{8,10},{9,11},{10,... | collective-permute-start | bytes 393224 | tf_op jit(solution)/shard_map/ppermute | solution.py:24
  35.5 0.5 collective-permute-start.13
  36.0 1.1 %early.1 = (f32[128,128]{1,0:T(8,128)S(1)}, bf16[2048,512]{1,0:T(8,128)(2,1)S(1)}, f32[8,128]{1,0:T(8,128)}) custom-call(s32[1,128]{1,0:T(1,128)S(1)} %bitcast.21, s32[1,1]{1,0:T(1,128)S(6)} %copy.8.refs_2_.refs_3_.count, bf16[2048,512]{1,0:T(8,128)(2,1)S(1)} %bitcast.16, bf16[128,512]{1,0:T(8,128)(2,1)S(1)} %slope.1.refs_0_.after), custom_call_target="tpu_custom_call" | custom-call | flops 1000 | bytes 1000 | tf_op jit(solution)/shard_map/early/pallas_call | solution.py:145
  37.1 1.0 %collective-permute-done.15.refs_1_ = bf16[128,512]{1,0:T(8,128)(2,1)S(1)} collective-permute-done((bf16[128,512]{1,0:T(8,128)(2,1)S(1)}, bf16[128,512]{1,0:T(8,128)(2,1)S(1)}, u32[]{:S(2)}, u32[]{:S(2)}) %collective-permute-start.15) | collective-permute-done | bytes 131104 | tf_op jit(solution)/shard_map/ppermute | solution.py:24
  38.3 1.1 %collective-permute-done.14.refs_1_.refs_3_ = bf16[128,512]{1,0:T(8,128)(2,1)S(1)} collective-permute-done((bf16[128,512]{1,0:T(8,128)(2,1)S(1)}, bf16[128,512]{1,0:T(8,128)(2,1)S(1)}, u32[]{:S(2)}, u32[]{:S(2)}) %collective-permute-start.14) | collective-permute-done | bytes 131104 | tf_op jit(solution)/shard_map/ppermute | solution.py:24
  39.7 2.4 %collective-permute-start.16 = (bf16[144,128]{1,0:T(8,128)(2,1)S(1)}, bf16[144,128]{1,0:T(8,128)(2,1)S(1)}, u32[]{:S(2)}, u32[]{:S(2)}) collective-permute-start(bf16[144,128]{1,0:T(8,128)(2,1)S(1)} %kept.1.message.refs_0_), channel_id=1, source_target_pairs={{0,16},{4,20},{8,24},{12,28},{16,0},{20,4},{24,8},{28,12},{1,17},{... | collective-permute-start | bytes 110600 | tf_op jit(solution)/shard_map/ppermute | solution.py:24
  42.1 1.1 %collective-permute-start.17 = (bf16[144,128]{1,0:T(8,128)(2,1)S(1)}, bf16[144,128]{1,0:T(8,128)(2,1)S(1)}, u32[]{:S(2)}, u32[]{:S(2)}) collective-permute-start(bf16[144,128]{1,0:T(8,128)(2,1)S(1)} %kept.1.message.refs_0_), channel_id=1, source_target_pairs={{0,24},{4,28},{8,16},{12,20},{16,8},{20,12},{24,0},{28,4},{1,25},{... | collective-permute-start | bytes 110600 | tf_op jit(solution)/shard_map/ppermute | solution.py:24
  43.4 2.3 %residue.1 = (bf16[2048,512]{1,0:T(8,128)(2,1)}, f32[8,128]{1,0:T(8,128)S(1)}) custom-call(bf16[128,512]{1,0:T(8,128)(2,1)S(1)} %slope.1.refs_0_.after, bf16[128,512]{1,0:T(8,128)(2,1)S(1)} %collective-permute-done.15.refs_1_, bf16[128,512]{1,0:T(8,128)(2,1)S(1)} %collective-permute-done.13.refs_0_.refs_2_, ...), custom_call_target="tpu_custom_call" | custom-call | flops 1000 | bytes 1000 | tf_op jit(solution)/shard_map/residue/pallas_call | solution.py:274
  46.0 0.7 %collective-permute-done.17.refs_1_.message = bf16[144,128]{1,0:T(8,128)(2,1)S(1)} collective-permute-done((bf16[144,128]{1,0:T(8,128)(2,1)S(1)}, bf16[144,128]{1,0:T(8,128)(2,1)S(1)}, u32[]{:S(2)}, u32[]{:S(2)}) %collective-permute-start.17) | collective-permute-done | bytes 36896 | tf_op jit(solution)/shard_map/ppermute | solution.py:24
  46.9 6.4 %collective-permute-start.19 = (bf16[576,128]{1,0:T(8,128)(2,1)S(1)}, bf16[576,128]{1,0:T(8,128)(2,1)S(1)}, u32[]{:S(2)}, u32[]{:S(2)}) collective-permute-start(bf16[576,128]{1,0:T(8,128)(2,1)S(1)} %join.5), channel_id=1, source_target_pairs={{0,4},{4,0},{8,12},{12,8},{16,20},{20,16},{24,28},{28,24},{1,5},{5... | collective-permute-start | bytes 442376 | tf_op jit(solution)/shard_map/ppermute | solution.py:24
  53.4 1.3 %half.1 = f32[2048,512]{1,0:T(8,128)S(1)} custom-call(bf16[128,512]{1,0:T(8,128)(2,1)S(1)} %get-tuple-element.64.refs_0_, bf16[128,512]{1,0:T(8,128)(2,1)S(1)} %get-tuple-element.65.refs_1_, bf16[128,512]{1,0:T(8,128)(2,1)S(1)} %get-tuple-element.66.refs_2_, bf16[128,512]{1,0:T(8,128)(2,1)S(1)} %get-tuple-element.67.refs_3_, ...), custom_call_target="tpu_custom_call" | custom-call | flops 1000 | bytes 1000 | tf_op jit(solution)/shard_map/half/pallas_call | solution.py:379
  54.7 2.5 %outer.1 = f32[2048,512]{1,0:T(8,128)} custom-call(bf16[576,128]{1,0:T(8,128)(2,1)S(1)} %collective-permute-done.19.group, f32[2048,512]{1,0:T(8,128)S(1)} %half.1), custom_call_target="tpu_custom_call" | custom-call | flops 1000 | bytes 1000 | tf_op jit(solution)/shard_map/outer/pallas_call | solution.py:387
  (41 shorter events, 4.3 us)
Async XLA Ops:
  1.7 8.2 %collective-permute-start.1 = (bf16[64,2048]{1,0:T(8,128)(2,1)S(1)}, bf16[64,2048]{1,0:T(8,128)(2,1)S(1)}, u32[]{:S(2)}, u32[]{:S(2)}) collective-permute-start(bf16[64,2048]{1,0:T(8,128)(2,1)S(1)} %get-tuple-element.70), channel_id=1, source_target_pairs={{0,2},{1,3},{2,0},{3,1},{4,6},{5,7},{6,4},{7,5},{8,10},{9,11},{10,... | collective-permute-start | bytes 786440 | tf_op jit(solution)/shard_map/ppermute | solution.py:24
  3.9 7.1 %collective-permute-start = (bf16[64,2048]{1,0:T(8,128)(2,1)S(1)}, bf16[64,2048]{1,0:T(8,128)(2,1)S(1)}, u32[]{:S(2)}, u32[]{:S(2)}) collective-permute-start(bf16[64,2048]{1,0:T(8,128)(2,1)S(1)} %get-tuple-element.71.refs_0_), channel_id=1, source_target_pairs={{0,1},{1,0},{2,3},{3,2},{4,5},{5,4},{6,7},{7,6},{8,9},{9,8},{10,11... | collective-permute-start | bytes 786440 | tf_op jit(solution)/shard_map/ppermute | solution.py:24
  5.1 1.6 %copy-start = (bf16[1,128,8192]{2,1,0:T(8,128)(2,1)S(1)}, bf16[1,128,8192]{2,1,0:T(8,128)(2,1)}, u32[]{:S(2)}) copy-start(bf16[1,128,8192]{2,1,0:T(8,128)(2,1)} %param.6) | copy-start | bytes 6291460
  6.7 9.6 %collective-permute-start.4 = (bf16[64,2048]{1,0:T(8,128)(2,1)S(1)}, bf16[64,2048]{1,0:T(8,128)(2,1)S(1)}, u32[]{:S(2)}, u32[]{:S(2)}) collective-permute-start(bf16[64,2048]{1,0:T(8,128)(2,1)S(1)} %get-tuple-element.39), channel_id=1, source_target_pairs={{0,1},{1,0},{2,3},{3,2},{4,5},{5,4},{6,7},{7,6},{8,9},{9,8},{10,11... | collective-permute-start | bytes 786440 | tf_op jit(solution)/shard_map/ppermute | solution.py:24
  7.0 10.3 %collective-permute-start.5 = (bf16[64,2048]{1,0:T(8,128)(2,1)S(1)}, bf16[64,2048]{1,0:T(8,128)(2,1)S(1)}, u32[]{:S(2)}, u32[]{:S(2)}) collective-permute-start(bf16[64,2048]{1,0:T(8,128)(2,1)S(1)} %get-tuple-element.40), channel_id=1, source_target_pairs={{0,2},{1,3},{2,0},{3,1},{4,6},{5,7},{6,4},{7,5},{8,10},{9,11},{10,... | collective-permute-start | bytes 786440 | tf_op jit(solution)/shard_map/ppermute | solution.py:24
  9.9 12.1 %collective-permute-start.3 = (bf16[64,2048]{1,0:T(8,128)(2,1)S(1)}, bf16[64,2048]{1,0:T(8,128)(2,1)S(1)}, u32[]{:S(2)}, u32[]{:S(2)}) collective-permute-start(bf16[64,2048]{1,0:T(8,128)(2,1)S(1)} %collective-permute-done.1.refs_2_), channel_id=1, source_target_pairs={{0,1},{1,0},{2,3},{3,2},{4,5},{5,4},{6,7},{7,6},{8,9},{9,8},{10,11... | collective-permute-start | bytes 786440 | tf_op jit(solution)/shard_map/ppermute | solution.py:24
  11.0 10.9 %collective-permute-start.2 = (bf16[64,2048]{1,0:T(8,128)(2,1)S(1)}, bf16[64,2048]{1,0:T(8,128)(2,1)S(1)}, u32[]{:S(2)}, u32[]{:S(2)}) collective-permute-start(bf16[64,2048]{1,0:T(8,128)(2,1)S(1)} %collective-permute-done.refs_1_), channel_id=1, source_target_pairs={{0,2},{1,3},{2,0},{3,1},{4,6},{5,7},{6,4},{7,5},{8,10},{9,11},{10,... | collective-permute-start | bytes 786440 | tf_op jit(solution)/shard_map/ppermute | solution.py:24
  12.2 5.1 %copy-start.1 = (bf16[1,2048,512]{2,1,0:T(8,128)(2,1)S(1)}, bf16[1,2048,512]{2,1,0:T(8,128)(2,1)}, u32[]{:S(2)}) copy-start(bf16[1,2048,512]{2,1,0:T(8,128)(2,1)} %param.8) | copy-start | bytes 6291460
  12.3 15.3 %collective-permute-start.8 = (bf16[64,2048]{1,0:T(8,128)(2,1)S(1)}, bf16[64,2048]{1,0:T(8,128)(2,1)S(1)}, u32[]{:S(2)}, u32[]{:S(2)}) collective-permute-start(bf16[64,2048]{1,0:T(8,128)(2,1)S(1)} %get-tuple-element.45), channel_id=1, source_target_pairs={{0,1},{1,0},{2,3},{3,2},{4,5},{5,4},{6,7},{7,6},{8,9},{9,8},{10,11... | collective-permute-start | bytes 786440 | tf_op jit(solution)/shard_map/ppermute | solution.py:24
  16.3 11.2 %collective-permute-start.9 = (bf16[64,2048]{1,0:T(8,128)(2,1)S(1)}, bf16[64,2048]{1,0:T(8,128)(2,1)S(1)}, u32[]{:S(2)}, u32[]{:S(2)}) collective-permute-start(bf16[64,2048]{1,0:T(8,128)(2,1)S(1)} %get-tuple-element.46), channel_id=1, source_target_pairs={{0,2},{1,3},{2,0},{3,1},{4,6},{5,7},{6,4},{7,5},{8,10},{9,11},{10,... | collective-permute-start | bytes 786440 | tf_op jit(solution)/shard_map/ppermute | solution.py:24
  17.9 8.2 %copy-start.4 = (s32[1,1,128]{2,1,0:T(1,128)S(1)}, s32[1,1,128]{2,1,0:T(1,128)}, u32[]{:S(2)}) copy-start(s32[1,1,128]{2,1,0:T(1,128)} %param.11) | copy-start | bytes 1540
  22.7 10.5 %collective-permute-start.6 = (bf16[128,512]{1,0:T(8,128)(2,1)S(1)}, bf16[128,512]{1,0:T(8,128)(2,1)S(1)}, u32[]{:S(2)}, u32[]{:S(2)}) collective-permute-start(bf16[128,512]{1,0:T(8,128)(2,1)S(1)} %get-tuple-element.43.refs_3_), channel_id=1, source_target_pairs={{0,3},{1,2},{2,1},{3,0},{4,7},{5,6},{6,5},{7,4},{8,11},{9,10},{10,... | collective-permute-start | bytes 393224 | tf_op jit(solution)/shard_map/ppermute | solution.py:24
  24.6 7.2 %collective-permute-start.11 = (bf16[64,512]{1,0:T(8,128)(2,1)S(1)}, bf16[64,512]{1,0:T(8,128)(2,1)S(1)}, u32[]{:S(2)}, u32[]{:S(2)}) collective-permute-start(bf16[64,512]{1,0:T(8,128)(2,1)S(1)} %get-tuple-element.41.refs_4_), channel_id=1, source_target_pairs={{0,2},{1,3},{2,0},{3,1},{4,6},{5,7},{6,4},{7,5},{8,10},{9,11},{10,... | collective-permute-start | bytes 196616 | tf_op jit(solution)/shard_map/ppermute | solution.py:24
  25.8 5.9 %collective-permute-start.7 = (bf16[64,512]{1,0:T(8,128)(2,1)S(1)}, bf16[64,512]{1,0:T(8,128)(2,1)S(1)}, u32[]{:S(2)}, u32[]{:S(2)}) collective-permute-start(bf16[64,512]{1,0:T(8,128)(2,1)S(1)} %get-tuple-element.44), channel_id=1, source_target_pairs={{0,1},{1,0},{2,3},{3,2},{4,5},{5,4},{6,7},{7,6},{8,9},{9,8},{10,11... | collective-permute-start | bytes 196616 | tf_op jit(solution)/shard_map/ppermute | solution.py:24
  26.7 6.5 %copy-start.3 = (bf16[1,128,512]{2,1,0:T(8,128)(2,1)S(1)}, bf16[1,128,512]{2,1,0:T(8,128)(2,1)}, u32[]{:S(2)}) copy-start(bf16[1,128,512]{2,1,0:T(8,128)(2,1)} %param.7) | copy-start | bytes 393220
  27.6 8.4 %copy-start.2 = (bf16[1,2048,512]{2,1,0:T(8,128)(2,1)S(1)}, bf16[1,2048,512]{2,1,0:T(8,128)(2,1)}, u32[]{:S(2)}) copy-start(bf16[1,2048,512]{2,1,0:T(8,128)(2,1)} %param.9) | copy-start | bytes 6291460
  28.0 5.0 %collective-permute-start.12 = (bf16[64,512]{1,0:T(8,128)(2,1)S(1)}, bf16[64,512]{1,0:T(8,128)(2,1)S(1)}, u32[]{:S(2)}, u32[]{:S(2)}) collective-permute-start(bf16[64,512]{1,0:T(8,128)(2,1)S(1)} %get-tuple-element.50), channel_id=1, source_target_pairs={{0,2},{1,3},{2,0},{3,1},{4,6},{5,7},{6,4},{7,5},{8,10},{9,11},{10,... | collective-permute-start | bytes 196616 | tf_op jit(solution)/shard_map/ppermute | solution.py:24
  28.5 4.7 %collective-permute-start.10 = (bf16[64,512]{1,0:T(8,128)(2,1)S(1)}, bf16[64,512]{1,0:T(8,128)(2,1)S(1)}, u32[]{:S(2)}, u32[]{:S(2)}) collective-permute-start(bf16[64,512]{1,0:T(8,128)(2,1)S(1)} %get-tuple-element.49.refs_4_), channel_id=1, source_target_pairs={{0,1},{1,0},{2,3},{3,2},{4,5},{5,4},{6,7},{7,6},{8,9},{9,8},{10,11... | collective-permute-start | bytes 196616 | tf_op jit(solution)/shard_map/ppermute | solution.py:24
  33.3 4.9 %collective-permute-start.15 = (bf16[128,512]{1,0:T(8,128)(2,1)S(1)}, bf16[128,512]{1,0:T(8,128)(2,1)S(1)}, u32[]{:S(2)}, u32[]{:S(2)}) collective-permute-start(bf16[128,512]{1,0:T(8,128)(2,1)S(1)} %slope.1.refs_0_.after), channel_id=1, source_target_pairs={{0,3},{1,2},{2,1},{3,0},{4,7},{5,6},{6,5},{7,4},{8,11},{9,10},{10,... | collective-permute-start | bytes 393224 | tf_op jit(solution)/shard_map/ppermute | solution.py:24
  34.8 4.6 %collective-permute-start.14 = (bf16[128,512]{1,0:T(8,128)(2,1)S(1)}, bf16[128,512]{1,0:T(8,128)(2,1)S(1)}, u32[]{:S(2)}, u32[]{:S(2)}) collective-permute-start(bf16[128,512]{1,0:T(8,128)(2,1)S(1)} %slope.1.refs_0_.after), channel_id=1, source_target_pairs={{0,2},{1,3},{2,0},{3,1},{4,6},{5,7},{6,4},{7,5},{8,10},{9,11},{10,... | collective-permute-start | bytes 393224 | tf_op jit(solution)/shard_map/ppermute | solution.py:24
  35.5 4.0 %collective-permute-start.13 = (bf16[128,512]{1,0:T(8,128)(2,1)S(1)}, bf16[128,512]{1,0:T(8,128)(2,1)S(1)}, u32[]{:S(2)}, u32[]{:S(2)}) collective-permute-start(bf16[128,512]{1,0:T(8,128)(2,1)S(1)} %slope.1.refs_0_.after), channel_id=1, source_target_pairs={{0,1},{1,0},{2,3},{3,2},{4,5},{5,4},{6,7},{7,6},{8,9},{9,8},{10,11... | collective-permute-start | bytes 393224 | tf_op jit(solution)/shard_map/ppermute | solution.py:24
  39.7 6.1 %collective-permute-start.16 = (bf16[144,128]{1,0:T(8,128)(2,1)S(1)}, bf16[144,128]{1,0:T(8,128)(2,1)S(1)}, u32[]{:S(2)}, u32[]{:S(2)}) collective-permute-start(bf16[144,128]{1,0:T(8,128)(2,1)S(1)} %kept.1.message.refs_0_), channel_id=1, source_target_pairs={{0,16},{4,20},{8,24},{12,28},{16,0},{20,4},{24,8},{28,12},{1,17},{... | collective-permute-start | bytes 110600 | tf_op jit(solution)/shard_map/ppermute | solution.py:24
  42.1 4.6 %collective-permute-start.17 = (bf16[144,128]{1,0:T(8,128)(2,1)S(1)}, bf16[144,128]{1,0:T(8,128)(2,1)S(1)}, u32[]{:S(2)}, u32[]{:S(2)}) collective-permute-start(bf16[144,128]{1,0:T(8,128)(2,1)S(1)} %kept.1.message.refs_0_), channel_id=1, source_target_pairs={{0,24},{4,28},{8,16},{12,20},{16,8},{20,12},{24,0},{28,4},{1,25},{... | collective-permute-start | bytes 110600 | tf_op jit(solution)/shard_map/ppermute | solution.py:24
  43.2 3.7 %collective-permute-start.18 = (bf16[144,128]{1,0:T(8,128)(2,1)S(1)}, bf16[144,128]{1,0:T(8,128)(2,1)S(1)}, u32[]{:S(2)}, u32[]{:S(2)}) collective-permute-start(bf16[144,128]{1,0:T(8,128)(2,1)S(1)} %kept.1.message.refs_0_), channel_id=1, source_target_pairs={{0,8},{4,12},{8,0},{12,4},{16,24},{20,28},{24,16},{28,20},{1,9},{5... | collective-permute-start | bytes 110600 | tf_op jit(solution)/shard_map/ppermute | solution.py:24
  46.9 7.8 %collective-permute-start.19 = (bf16[576,128]{1,0:T(8,128)(2,1)S(1)}, bf16[576,128]{1,0:T(8,128)(2,1)S(1)}, u32[]{:S(2)}, u32[]{:S(2)}) collective-permute-start(bf16[576,128]{1,0:T(8,128)(2,1)S(1)} %join.5), channel_id=1, source_target_pairs={{0,4},{4,0},{8,12},{12,8},{16,20},{20,16},{24,28},{28,24},{1,5},{5... | collective-permute-start | bytes 442376 | tf_op jit(solution)/shard_map/ppermute | solution.py:24

commit v23 on v21

--- a/solution.py
+++ b/solution.py
@@ -350,7 +350,7 @@
 def outer(groups, cap, depth, kw):
     slots = groups[0].shape[0] // (cap + 16) * cap
     n = 2 * slots // cap
-    tile = min(depth, 256)
+    tile = min(depth, 128)
     shape = jax.ShapeDtypeStruct((depth, kw), jnp.float32)
     scratch = [pltpu.VMEM((slots, kw), jnp.bfloat16), pltpu.VMEM((8, slots), jnp.int32)]
     half = pl.pallas_call(

time: 57.3 us -> 57.3 us (level)
  no operation moved by 1% of the time
where the time goes in v23:
time: 57.3 us; the launch traced here: 57.1 us
  starting transfers between devices  24 us (42%)
  waiting for transfers between devices  17.4 us (30%)
  Pallas kernels  11.6 us (20%)
  local copies, waits for them, and re-layouts  2.68 us (5%)
  between operations  1.49 us (3%)
    ppermute x20, starting transfers between devices, swap(): return lax.ppermute(x, axis, [(i, i ^ d) for i in range(n)])  24 us
    ppermute x20, waiting for transfers between devices, swap(): return lax.ppermute(x, axis, [(i, i ^ d) for i in range(n)])  17.4 us
    pallas_call x1, Pallas kernels, outer(): pl.pallas_call(functools.partial(outer_kernel, cap, kw // LANES, tile, n)...  2.55 us
    pallas_call x1, Pallas kernels, residue(): pl.pallas_call(functools.partial(residue_kernel, order, tile), out_shape=...  2.33 us
    pallas_call x3, Pallas kernels, project(): pl.pallas_call(functools.partial(project_kernel, n, len(outs)), out_shape...  1.62 us
    unnamed x10, local copies, waits for them, and re-layouts  1.61 us
    pallas_call x1, Pallas kernels, outer(): pl.pallas_call(functools.partial(half_kernel, cap, kw // LANES, tile), ou...  1.43 us
    pallas_call x2, Pallas kernels, prepare(): pl.pallas_call(functools.partial(prepare_kernel, per_row, len(xs)), out_s...  1.21 us
  transfers between devices with their start and end apart: 20, of which 10 were waited for; matrix products, arithmetic and copies ran while one was open for 0% of the time, Pallas kernels for 15%

profile of v23, /device:TPU:1, one launch (start us, length us, event | category | flops | bytes accessed | tf_op | source)
XLA Modules:
  0.0 57.1 jit_solution(6590783373233832742)
XLA Ops:
  0.6 1.1 %dynamic-slice_bitcast_fusion = (bf16[64,2048]{1,0:T(8,128)(2,1)S(1)}, bf16[64,2048]{1,0:T(8,128)(2,1)S(1)}) fusion(bf16[1,128,8192]{2,1,0:T(8,128)(2,1)} %param.6, s32[]{:T(128)S(6)} %select_n.4), kind=kLoop, calls=%fused_computation | loop fusion | bytes 1048580 | tf_op jit(solution)/shard_map/dynamic_slice | solution.py:392
  1.7 2.1 %collective-permute-start.1 = (bf16[64,2048]{1,0:T(8,128)(2,1)S(1)}, bf16[64,2048]{1,0:T(8,128)(2,1)S(1)}, u32[]{:S(2)}, u32[]{:S(2)}) collective-permute-start(bf16[64,2048]{1,0:T(8,128)(2,1)S(1)} %get-tuple-element.54), channel_id=1, source_target_pairs={{0,2},{1,3},{2,0},{3,1},{4,6},{5,7},{6,4},{7,5},{8,10},{9,11},{10,... | collective-permute-start | bytes 786440 | tf_op jit(solution)/shard_map/ppermute | solution.py:24
  3.9 1.2 %collective-permute-start = (bf16[64,2048]{1,0:T(8,128)(2,1)S(1)}, bf16[64,2048]{1,0:T(8,128)(2,1)S(1)}, u32[]{:S(2)}, u32[]{:S(2)}) collective-permute-start(bf16[64,2048]{1,0:T(8,128)(2,1)S(1)} %get-tuple-element.55.refs_0_), channel_id=1, source_target_pairs={{0,1},{1,0},{2,3},{3,2},{4,5},{5,4},{6,7},{7,6},{8,9},{9,8},{10,11... | collective-permute-start | bytes 786440 | tf_op jit(solution)/shard_map/ppermute | solution.py:24
  5.1 1.6 %copy-done = bf16[1,128,8192]{2,1,0:T(8,128)(2,1)S(1)} copy-done((bf16[1,128,8192]{2,1,0:T(8,128)(2,1)S(1)}, bf16[1,128,8192]{2,1,0:T(8,128)(2,1)}, u32[]{:S(2)}) %copy-start) | copy-done | bytes 2097176
  7.1 2.8 %collective-permute-done.1.refs_2_ = bf16[64,2048]{1,0:T(8,128)(2,1)S(1)} collective-permute-done((bf16[64,2048]{1,0:T(8,128)(2,1)S(1)}, bf16[64,2048]{1,0:T(8,128)(2,1)S(1)}, u32[]{:S(2)}, u32[]{:S(2)}) %collective-permute-start.1) | collective-permute-done | bytes 262176 | tf_op jit(solution)/shard_map/ppermute | solution.py:24
  9.9 1.1 %collective-permute-start.3 = (bf16[64,2048]{1,0:T(8,128)(2,1)S(1)}, bf16[64,2048]{1,0:T(8,128)(2,1)S(1)}, u32[]{:S(2)}, u32[]{:S(2)}) collective-permute-start(bf16[64,2048]{1,0:T(8,128)(2,1)S(1)} %collective-permute-done.1.refs_2_), channel_id=1, source_target_pairs={{0,1},{1,0},{2,3},{3,2},{4,5},{5,4},{6,7},{7,6},{8,9},{9,8},{10,11... | collective-permute-start | bytes 786440 | tf_op jit(solution)/shard_map/ppermute | solution.py:24
  11.0 1.2 %collective-permute-start.2 = (bf16[64,2048]{1,0:T(8,128)(2,1)S(1)}, bf16[64,2048]{1,0:T(8,128)(2,1)S(1)}, u32[]{:S(2)}, u32[]{:S(2)}) collective-permute-start(bf16[64,2048]{1,0:T(8,128)(2,1)S(1)} %collective-permute-done.refs_1_), channel_id=1, source_target_pairs={{0,2},{1,3},{2,0},{3,1},{4,6},{5,7},{6,4},{7,5},{8,10},{9,11},{10,... | collective-permute-start | bytes 786440 | tf_op jit(solution)/shard_map/ppermute | solution.py:24
  12.6 3.7 %collective-permute-done.4.refs_0_ = bf16[64,2048]{1,0:T(8,128)(2,1)S(1)} collective-permute-done((bf16[64,2048]{1,0:T(8,128)(2,1)S(1)}, bf16[64,2048]{1,0:T(8,128)(2,1)S(1)}, u32[]{:S(2)}, u32[]{:S(2)}) %collective-permute-start.4) | collective-permute-done | bytes 262176 | tf_op jit(solution)/shard_map/ppermute | solution.py:24
  16.7 0.6 %cut.5 = (bf16[128,2048]{1,0:T(8,128)(2,1)S(1)}, f32[8,128]{1,0:T(8,128)}) custom-call(bf16[128,8192]{1,0:T(8,128)(2,1)S(1)} %bitcast.12, f32[8,128]{1,0:T(8,128)S(1)} %get-tuple-element.29.refs_0_), custom_call_target="tpu_custom_call" | custom-call | flops 1000 | bytes 1000 | tf_op jit(solution)/shard_map/cut/pallas_call | solution.py:43
  17.9 4.1 %collective-permute-done.3.refs_2_ = bf16[64,2048]{1,0:T(8,128)(2,1)S(1)} collective-permute-done((bf16[64,2048]{1,0:T(8,128)(2,1)S(1)}, bf16[64,2048]{1,0:T(8,128)(2,1)S(1)}, u32[]{:S(2)}, u32[]{:S(2)}) %collective-permute-start.3) | collective-permute-done | bytes 262176 | tf_op jit(solution)/shard_map/ppermute | solution.py:24
  21.9 0.7 %project.4 = (f32[128,512]{1,0:T(8,128)S(1)}, bf16[128,512]{1,0:T(8,128)(2,1)S(1)}, bf16[256,2048]{1,0:T(8,128)(2,1)S(1)}) custom-call(bf16[128,2048]{1,0:T(8,128)(2,1)S(1)} %get-tuple-element.30.refs_0_, bf16[64,2048]{1,0:T(8,128)(2,1)S(1)} %collective-permute-done.2.refs_1_, bf16[64,2048]{1,0:T(8,128)(2,1)S(1)} %collective-permute-done.3.refs_2_, ...), custom_call_target="tpu_custom_call" | custom-call | flops 1000 | bytes 1000 | tf_op jit(solution)/shard_map/project/pallas_call | solution.py:73
  22.7 1.3 %collective-permute-start.6 = (bf16[128,512]{1,0:T(8,128)(2,1)S(1)}, bf16[128,512]{1,0:T(8,128)(2,1)S(1)}, u32[]{:S(2)}, u32[]{:S(2)}) collective-permute-start(bf16[128,512]{1,0:T(8,128)(2,1)S(1)} %get-tuple-element.35.refs_3_), channel_id=1, source_target_pairs={{0,3},{1,2},{2,1},{3,0},{4,7},{5,6},{6,5},{7,4},{8,11},{9,10},{10,... | collective-permute-start | bytes 393224 | tf_op jit(solution)/shard_map/ppermute | solution.py:24
  24.6 1.2 %collective-permute-start.11 = (bf16[64,512]{1,0:T(8,128)(2,1)S(1)}, bf16[64,512]{1,0:T(8,128)(2,1)S(1)}, u32[]{:S(2)}, u32[]{:S(2)}) collective-permute-start(bf16[64,512]{1,0:T(8,128)(2,1)S(1)} %get-tuple-element.33.refs_4_), channel_id=1, source_target_pairs={{0,2},{1,3},{2,0},{3,1},{4,6},{5,7},{6,4},{7,5},{8,10},{9,11},{10,... | collective-permute-start | bytes 196616 | tf_op jit(solution)/shard_map/ppermute | solution.py:24
  26.1 0.6 %prepare.2 = (bf16[128,256]{1,0:T(8,128)(2,1)S(1)}, bf16[2048,256]{1,0:T(8,128)(2,1)S(1)}, f32[8,128]{1,0:T(8,128)S(1)}) custom-call(bf16[256,2048]{1,0:T(8,128)(2,1)S(1)} %get-tuple-element.39.refs_0_, s32[1,128]{1,0:T(1,128)S(1)} %bitcast.19, s32[1,1]{1,0:T(1,128)S(6)} %copy.8.refs_2_.refs_3_.count, bf16[128,512]{1,0:T(8,128)(2,1)S(1)} %get-tuple-element.35.refs_3_), custom_call_target="tpu_custom_call" | custom-call | flops 1000 | bytes 1000 | tf_op jit(solution)/shard_map/prepare/pallas_call | solution.py:181
  26.7 0.8 %collective-permute-done.8.refs_0_ = bf16[64,2048]{1,0:T(8,128)(2,1)S(1)} collective-permute-done((bf16[64,2048]{1,0:T(8,128)(2,1)S(1)}, bf16[64,2048]{1,0:T(8,128)(2,1)S(1)}, u32[]{:S(2)}, u32[]{:S(2)}) %collective-permute-start.8) | collective-permute-done | bytes 262176 | tf_op jit(solution)/shard_map/ppermute | solution.py:24
  28.5 1.1 %collective-permute-start.10 = (bf16[64,512]{1,0:T(8,128)(2,1)S(1)}, bf16[64,512]{1,0:T(8,128)(2,1)S(1)}, u32[]{:S(2)}, u32[]{:S(2)}) collective-permute-start(bf16[64,512]{1,0:T(8,128)(2,1)S(1)} %get-tuple-element.41.refs_4_), channel_id=1, source_target_pairs={{0,1},{1,0},{2,3},{3,2},{4,5},{5,4},{6,7},{7,6},{8,9},{9,8},{10,11... | collective-permute-start | bytes 196616 | tf_op jit(solution)/shard_map/ppermute | solution.py:24
  29.6 0.6 %prepare.3 = (bf16[128,256]{1,0:T(8,128)(2,1)S(1)}, bf16[2048,256]{1,0:T(8,128)(2,1)S(1)}, f32[8,128]{1,0:T(8,128)S(1)}) custom-call(bf16[128,2048]{1,0:T(8,128)(2,1)S(1)} %get-tuple-element.43.refs_0_, bf16[128,2048]{1,0:T(8,128)(2,1)S(1)} %get-tuple-element.44.refs_1_, s32[1,128]{1,0:T(1,128)S(1)} %bitcast.20, s32[1,1]{1,0:T(1,128)S(6)} %copy.8.refs_2_.refs_3_.count, ...), custom_call_target="tpu_custom_call" | custom-call | flops 1000 | bytes 1000 | tf_op jit(solution)/shard_map/prepare/pallas_call | solution.py:181
  30.2 1.5 %collective-permute-done.7.refs_3_ = bf16[64,512]{1,0:T(8,128)(2,1)S(1)} collective-permute-done((bf16[64,512]{1,0:T(8,128)(2,1)S(1)}, bf16[64,512]{1,0:T(8,128)(2,1)S(1)}, u32[]{:S(2)}, u32[]{:S(2)}) %collective-permute-start.7) | collective-permute-done | bytes 65568 | tf_op jit(solution)/shard_map/ppermute | solution.py:24
  31.8 1.2 %collective-permute-done.12.refs_6_ = bf16[64,512]{1,0:T(8,128)(2,1)S(1)} collective-permute-done((bf16[64,512]{1,0:T(8,128)(2,1)S(1)}, bf16[64,512]{1,0:T(8,128)(2,1)S(1)}, u32[]{:S(2)}, u32[]{:S(2)}) %collective-permute-start.12) | collective-permute-done | bytes 65568 | tf_op jit(solution)/shard_map/ppermute | solution.py:24
  33.3 1.5 %collective-permute-start.15 = (bf16[128,512]{1,0:T(8,128)(2,1)S(1)}, bf16[128,512]{1,0:T(8,128)(2,1)S(1)}, u32[]{:S(2)}, u32[]{:S(2)}) collective-permute-start(bf16[128,512]{1,0:T(8,128)(2,1)S(1)} %slope.1.refs_0_.after), channel_id=1, source_target_pairs={{0,3},{1,2},{2,1},{3,0},{4,7},{5,6},{6,5},{7,4},{8,11},{9,10},{10,... | collective-permute-start | bytes 393224 | tf_op jit(solution)/shard_map/ppermute | solution.py:24
  34.8 0.7 %collective-permute-start.14 = (bf16[128,512]{1,0:T(8,128)(2,1)S(1)}, bf16[128,512]{1,0:T(8,128)(2,1)S(1)}, u32[]{:S(2)}, u32[]{:S(2)}) collective-permute-start(bf16[128,512]{1,0:T(8,128)(2,1)S(1)} %slope.1.refs_0_.after), channel_id=1, source_target_pairs={{0,2},{1,3},{2,0},{3,1},{4,6},{5,7},{6,4},{7,5},{8,10},{9,11},{10,... | collective-permute-start | bytes 393224 | tf_op jit(solution)/shard_map/ppermute | solution.py:24
  35.5 0.5 collective-permute-start.13
  36.0 1.1 %early.1 = (f32[128,128]{1,0:T(8,128)S(1)}, bf16[2048,512]{1,0:T(8,128)(2,1)S(1)}, f32[8,128]{1,0:T(8,128)}) custom-call(s32[1,128]{1,0:T(1,128)S(1)} %bitcast.21, s32[1,1]{1,0:T(1,128)S(6)} %copy.8.refs_2_.refs_3_.count, bf16[2048,512]{1,0:T(8,128)(2,1)S(1)} %bitcast.16, bf16[128,512]{1,0:T(8,128)(2,1)S(1)} %slope.1.refs_0_.after), custom_call_target="tpu_custom_call" | custom-call | flops 1000 | bytes 1000 | tf_op jit(solution)/shard_map/early/pallas_call | solution.py:145
  37.1 1.0 %collective-permute-done.15.refs_1_ = bf16[128,512]{1,0:T(8,128)(2,1)S(1)} collective-permute-done((bf16[128,512]{1,0:T(8,128)(2,1)S(1)}, bf16[128,512]{1,0:T(8,128)(2,1)S(1)}, u32[]{:S(2)}, u32[]{:S(2)}) %collective-permute-start.15) | collective-permute-done | bytes 131104 | tf_op jit(solution)/shard_map/ppermute | solution.py:24
  38.3 1.1 %collective-permute-done.14.refs_1_.refs_3_ = bf16[128,512]{1,0:T(8,128)(2,1)S(1)} collective-permute-done((bf16[128,512]{1,0:T(8,128)(2,1)S(1)}, bf16[128,512]{1,0:T(8,128)(2,1)S(1)}, u32[]{:S(2)}, u32[]{:S(2)}) %collective-permute-start.14) | collective-permute-done | bytes 131104 | tf_op jit(solution)/shard_map/ppermute | solution.py:24
  39.7 2.4 %collective-permute-start.16 = (bf16[144,128]{1,0:T(8,128)(2,1)S(1)}, bf16[144,128]{1,0:T(8,128)(2,1)S(1)}, u32[]{:S(2)}, u32[]{:S(2)}) collective-permute-start(bf16[144,128]{1,0:T(8,128)(2,1)S(1)} %kept.1.refs_0_), channel_id=1, source_target_pairs={{0,16},{4,20},{8,24},{12,28},{16,0},{20,4},{24,8},{28,12},{1,17},{... | collective-permute-start | bytes 110600 | tf_op jit(solution)/shard_map/ppermute | solution.py:24
  42.1 1.1 %collective-permute-start.17 = (bf16[144,128]{1,0:T(8,128)(2,1)S(1)}, bf16[144,128]{1,0:T(8,128)(2,1)S(1)}, u32[]{:S(2)}, u32[]{:S(2)}) collective-permute-start(bf16[144,128]{1,0:T(8,128)(2,1)S(1)} %kept.1.refs_0_), channel_id=1, source_target_pairs={{0,24},{4,28},{8,16},{12,20},{16,8},{20,12},{24,0},{28,4},{1,25},{... | collective-permute-start | bytes 110600 | tf_op jit(solution)/shard_map/ppermute | solution.py:24
  43.4 2.3 %residue.1 = (bf16[2048,512]{1,0:T(8,128)(2,1)}, f32[8,128]{1,0:T(8,128)S(1)}) custom-call(bf16[128,512]{1,0:T(8,128)(2,1)S(1)} %slope.1.refs_0_.after, bf16[128,512]{1,0:T(8,128)(2,1)S(1)} %collective-permute-done.15.refs_1_, bf16[128,512]{1,0:T(8,128)(2,1)S(1)} %collective-permute-done.13.refs_0_.refs_2_, ...), custom_call_target="tpu_custom_call" | custom-call | flops 1000 | bytes 1000 | tf_op jit(solution)/shard_map/residue/pallas_call | solution.py:274
  45.8 0.9 %collective-permute-done.17.refs_1_ = bf16[144,128]{1,0:T(8,128)(2,1)S(1)} collective-permute-done((bf16[144,128]{1,0:T(8,128)(2,1)S(1)}, bf16[144,128]{1,0:T(8,128)(2,1)S(1)}, u32[]{:S(2)}, u32[]{:S(2)}) %collective-permute-start.17) | collective-permute-done | bytes 36896 | tf_op jit(solution)/shard_map/ppermute | solution.py:24
  46.8 6.4 %collective-permute-start.19 = (bf16[576,128]{1,0:T(8,128)(2,1)S(1)}, bf16[576,128]{1,0:T(8,128)(2,1)S(1)}, u32[]{:S(2)}, u32[]{:S(2)}) collective-permute-start(bf16[576,128]{1,0:T(8,128)(2,1)S(1)} %join.5.group), channel_id=1, source_target_pairs={{0,4},{4,0},{8,12},{12,8},{16,20},{20,16},{24,28},{28,24},{1,5},{5... | collective-permute-start | bytes 442376 | tf_op jit(solution)/shard_map/ppermute | solution.py:24
  53.1 1.4 %half.1 = f32[2048,512]{1,0:T(8,128)S(1)} custom-call(bf16[576,128]{1,0:T(8,128)(2,1)S(1)} %join.5.group), custom_call_target="tpu_custom_call" | custom-call | flops 1000 | bytes 1000 | tf_op jit(solution)/shard_map/half/pallas_call | solution.py:356
  54.6 2.5 %outer.1 = f32[2048,512]{1,0:T(8,128)} custom-call(bf16[576,128]{1,0:T(8,128)(2,1)S(1)} %collective-permute-done.19.group, f32[2048,512]{1,0:T(8,128)S(1)} %half.1), custom_call_target="tpu_custom_call" | custom-call | flops 1000 | bytes 1000 | tf_op jit(solution)/shard_map/outer/pallas_call | solution.py:364
  (37 shorter events, 3.8 us)
Async XLA Ops:
  1.7 8.2 %collective-permute-start.1 = (bf16[64,2048]{1,0:T(8,128)(2,1)S(1)}, bf16[64,2048]{1,0:T(8,128)(2,1)S(1)}, u32[]{:S(2)}, u32[]{:S(2)}) collective-permute-start(bf16[64,2048]{1,0:T(8,128)(2,1)S(1)} %get-tuple-element.54), channel_id=1, source_target_pairs={{0,2},{1,3},{2,0},{3,1},{4,6},{5,7},{6,4},{7,5},{8,10},{9,11},{10,... | collective-permute-start | bytes 786440 | tf_op jit(solution)/shard_map/ppermute | solution.py:24
  3.9 7.1 %collective-permute-start = (bf16[64,2048]{1,0:T(8,128)(2,1)S(1)}, bf16[64,2048]{1,0:T(8,128)(2,1)S(1)}, u32[]{:S(2)}, u32[]{:S(2)}) collective-permute-start(bf16[64,2048]{1,0:T(8,128)(2,1)S(1)} %get-tuple-element.55.refs_0_), channel_id=1, source_target_pairs={{0,1},{1,0},{2,3},{3,2},{4,5},{5,4},{6,7},{7,6},{8,9},{9,8},{10,11... | collective-permute-start | bytes 786440 | tf_op jit(solution)/shard_map/ppermute | solution.py:24
  5.1 1.6 %copy-start = (bf16[1,128,8192]{2,1,0:T(8,128)(2,1)S(1)}, bf16[1,128,8192]{2,1,0:T(8,128)(2,1)}, u32[]{:S(2)}) copy-start(bf16[1,128,8192]{2,1,0:T(8,128)(2,1)} %param.6) | copy-start | bytes 6291460
  6.7 9.6 %collective-permute-start.4 = (bf16[64,2048]{1,0:T(8,128)(2,1)S(1)}, bf16[64,2048]{1,0:T(8,128)(2,1)S(1)}, u32[]{:S(2)}, u32[]{:S(2)}) collective-permute-start(bf16[64,2048]{1,0:T(8,128)(2,1)S(1)} %get-tuple-element.31), channel_id=1, source_target_pairs={{0,1},{1,0},{2,3},{3,2},{4,5},{5,4},{6,7},{7,6},{8,9},{9,8},{10,11... | collective-permute-start | bytes 786440 | tf_op jit(solution)/shard_map/ppermute | solution.py:24
  7.0 10.3 %collective-permute-start.5 = (bf16[64,2048]{1,0:T(8,128)(2,1)S(1)}, bf16[64,2048]{1,0:T(8,128)(2,1)S(1)}, u32[]{:S(2)}, u32[]{:S(2)}) collective-permute-start(bf16[64,2048]{1,0:T(8,128)(2,1)S(1)} %get-tuple-element.32), channel_id=1, source_target_pairs={{0,2},{1,3},{2,0},{3,1},{4,6},{5,7},{6,4},{7,5},{8,10},{9,11},{10,... | collective-permute-start | bytes 786440 | tf_op jit(solution)/shard_map/ppermute | solution.py:24
  9.9 12.1 %collective-permute-start.3 = (bf16[64,2048]{1,0:T(8,128)(2,1)S(1)}, bf16[64,2048]{1,0:T(8,128)(2,1)S(1)}, u32[]{:S(2)}, u32[]{:S(2)}) collective-permute-start(bf16[64,2048]{1,0:T(8,128)(2,1)S(1)} %collective-permute-done.1.refs_2_), channel_id=1, source_target_pairs={{0,1},{1,0},{2,3},{3,2},{4,5},{5,4},{6,7},{7,6},{8,9},{9,8},{10,11... | collective-permute-start | bytes 786440 | tf_op jit(solution)/shard_map/ppermute | solution.py:24
  11.0 10.9 %collective-permute-start.2 = (bf16[64,2048]{1,0:T(8,128)(2,1)S(1)}, bf16[64,2048]{1,0:T(8,128)(2,1)S(1)}, u32[]{:S(2)}, u32[]{:S(2)}) collective-permute-start(bf16[64,2048]{1,0:T(8,128)(2,1)S(1)} %collective-permute-done.refs_1_), channel_id=1, source_target_pairs={{0,2},{1,3},{2,0},{3,1},{4,6},{5,7},{6,4},{7,5},{8,10},{9,11},{10,... | collective-permute-start | bytes 786440 | tf_op jit(solution)/shard_map/ppermute | solution.py:24
  12.2 5.1 %copy-start.1 = (bf16[1,2048,512]{2,1,0:T(8,128)(2,1)S(1)}, bf16[1,2048,512]{2,1,0:T(8,128)(2,1)}, u32[]{:S(2)}) copy-start(bf16[1,2048,512]{2,1,0:T(8,128)(2,1)} %param.8) | copy-start | bytes 6291460
  12.3 15.3 %collective-permute-start.8 = (bf16[64,2048]{1,0:T(8,128)(2,1)S(1)}, bf16[64,2048]{1,0:T(8,128)(2,1)S(1)}, u32[]{:S(2)}, u32[]{:S(2)}) collective-permute-start(bf16[64,2048]{1,0:T(8,128)(2,1)S(1)} %get-tuple-element.37), channel_id=1, source_target_pairs={{0,1},{1,0},{2,3},{3,2},{4,5},{5,4},{6,7},{7,6},{8,9},{9,8},{10,11... | collective-permute-start | bytes 786440 | tf_op jit(solution)/shard_map/ppermute | solution.py:24
  16.3 11.2 %collective-permute-start.9 = (bf16[64,2048]{1,0:T(8,128)(2,1)S(1)}, bf16[64,2048]{1,0:T(8,128)(2,1)S(1)}, u32[]{:S(2)}, u32[]{:S(2)}) collective-permute-start(bf16[64,2048]{1,0:T(8,128)(2,1)S(1)} %get-tuple-element.38), channel_id=1, source_target_pairs={{0,2},{1,3},{2,0},{3,1},{4,6},{5,7},{6,4},{7,5},{8,10},{9,11},{10,... | collective-permute-start | bytes 786440 | tf_op jit(solution)/shard_map/ppermute | solution.py:24
  17.9 8.2 %copy-start.4 = (s32[1,1,128]{2,1,0:T(1,128)S(1)}, s32[1,1,128]{2,1,0:T(1,128)}, u32[]{:S(2)}) copy-start(s32[1,1,128]{2,1,0:T(1,128)} %param.11) | copy-start | bytes 1540
  22.7 10.5 %collective-permute-start.6 = (bf16[128,512]{1,0:T(8,128)(2,1)S(1)}, bf16[128,512]{1,0:T(8,128)(2,1)S(1)}, u32[]{:S(2)}, u32[]{:S(2)}) collective-permute-start(bf16[128,512]{1,0:T(8,128)(2,1)S(1)} %get-tuple-element.35.refs_3_), channel_id=1, source_target_pairs={{0,3},{1,2},{2,1},{3,0},{4,7},{5,6},{6,5},{7,4},{8,11},{9,10},{10,... | collective-permute-start | bytes 393224 | tf_op jit(solution)/shard_map/ppermute | solution.py:24
  24.6 7.2 %collective-permute-start.11 = (bf16[64,512]{1,0:T(8,128)(2,1)S(1)}, bf16[64,512]{1,0:T(8,128)(2,1)S(1)}, u32[]{:S(2)}, u32[]{:S(2)}) collective-permute-start(bf16[64,512]{1,0:T(8,128)(2,1)S(1)} %get-tuple-element.33.refs_4_), channel_id=1, source_target_pairs={{0,2},{1,3},{2,0},{3,1},{4,6},{5,7},{6,4},{7,5},{8,10},{9,11},{10,... | collective-permute-start | bytes 196616 | tf_op jit(solution)/shard_map/ppermute | solution.py:24
  25.8 5.9 %collective-permute-start.7 = (bf16[64,512]{1,0:T(8,128)(2,1)S(1)}, bf16[64,512]{1,0:T(8,128)(2,1)S(1)}, u32[]{:S(2)}, u32[]{:S(2)}) collective-permute-start(bf16[64,512]{1,0:T(8,128)(2,1)S(1)} %get-tuple-element.36), channel_id=1, source_target_pairs={{0,1},{1,0},{2,3},{3,2},{4,5},{5,4},{6,7},{7,6},{8,9},{9,8},{10,11... | collective-permute-start | bytes 196616 | tf_op jit(solution)/shard_map/ppermute | solution.py:24
  26.7 6.5 %copy-start.3 = (bf16[1,128,512]{2,1,0:T(8,128)(2,1)S(1)}, bf16[1,128,512]{2,1,0:T(8,128)(2,1)}, u32[]{:S(2)}) copy-start(bf16[1,128,512]{2,1,0:T(8,128)(2,1)} %param.7) | copy-start | bytes 393220
  27.6 8.4 %copy-start.2 = (bf16[1,2048,512]{2,1,0:T(8,128)(2,1)S(1)}, bf16[1,2048,512]{2,1,0:T(8,128)(2,1)}, u32[]{:S(2)}) copy-start(bf16[1,2048,512]{2,1,0:T(8,128)(2,1)} %param.9) | copy-start | bytes 6291460
  28.0 5.0 %collective-permute-start.12 = (bf16[64,512]{1,0:T(8,128)(2,1)S(1)}, bf16[64,512]{1,0:T(8,128)(2,1)S(1)}, u32[]{:S(2)}, u32[]{:S(2)}) collective-permute-start(bf16[64,512]{1,0:T(8,128)(2,1)S(1)} %get-tuple-element.42), channel_id=1, source_target_pairs={{0,2},{1,3},{2,0},{3,1},{4,6},{5,7},{6,4},{7,5},{8,10},{9,11},{10,... | collective-permute-start | bytes 196616 | tf_op jit(solution)/shard_map/ppermute | solution.py:24
  28.5 4.7 %collective-permute-start.10 = (bf16[64,512]{1,0:T(8,128)(2,1)S(1)}, bf16[64,512]{1,0:T(8,128)(2,1)S(1)}, u32[]{:S(2)}, u32[]{:S(2)}) collective-permute-start(bf16[64,512]{1,0:T(8,128)(2,1)S(1)} %get-tuple-element.41.refs_4_), channel_id=1, source_target_pairs={{0,1},{1,0},{2,3},{3,2},{4,5},{5,4},{6,7},{7,6},{8,9},{9,8},{10,11... | collective-permute-start | bytes 196616 | tf_op jit(solution)/shard_map/ppermute | solution.py:24
  33.3 4.9 %collective-permute-start.15 = (bf16[128,512]{1,0:T(8,128)(2,1)S(1)}, bf16[128,512]{1,0:T(8,128)(2,1)S(1)}, u32[]{:S(2)}, u32[]{:S(2)}) collective-permute-start(bf16[128,512]{1,0:T(8,128)(2,1)S(1)} %slope.1.refs_0_.after), channel_id=1, source_target_pairs={{0,3},{1,2},{2,1},{3,0},{4,7},{5,6},{6,5},{7,4},{8,11},{9,10},{10,... | collective-permute-start | bytes 393224 | tf_op jit(solution)/shard_map/ppermute | solution.py:24
  34.8 4.6 %collective-permute-start.14 = (bf16[128,512]{1,0:T(8,128)(2,1)S(1)}, bf16[128,512]{1,0:T(8,128)(2,1)S(1)}, u32[]{:S(2)}, u32[]{:S(2)}) collective-permute-start(bf16[128,512]{1,0:T(8,128)(2,1)S(1)} %slope.1.refs_0_.after), channel_id=1, source_target_pairs={{0,2},{1,3},{2,0},{3,1},{4,6},{5,7},{6,4},{7,5},{8,10},{9,11},{10,... | collective-permute-start | bytes 393224 | tf_op jit(solution)/shard_map/ppermute | solution.py:24
  35.5 4.0 %collective-permute-start.13 = (bf16[128,512]{1,0:T(8,128)(2,1)S(1)}, bf16[128,512]{1,0:T(8,128)(2,1)S(1)}, u32[]{:S(2)}, u32[]{:S(2)}) collective-permute-start(bf16[128,512]{1,0:T(8,128)(2,1)S(1)} %slope.1.refs_0_.after), channel_id=1, source_target_pairs={{0,1},{1,0},{2,3},{3,2},{4,5},{5,4},{6,7},{7,6},{8,9},{9,8},{10,11... | collective-permute-start | bytes 393224 | tf_op jit(solution)/shard_map/ppermute | solution.py:24
  39.7 6.0 %collective-permute-start.16 = (bf16[144,128]{1,0:T(8,128)(2,1)S(1)}, bf16[144,128]{1,0:T(8,128)(2,1)S(1)}, u32[]{:S(2)}, u32[]{:S(2)}) collective-permute-start(bf16[144,128]{1,0:T(8,128)(2,1)S(1)} %kept.1.refs_0_), channel_id=1, source_target_pairs={{0,16},{4,20},{8,24},{12,28},{16,0},{20,4},{24,8},{28,12},{1,17},{... | collective-permute-start | bytes 110600 | tf_op jit(solution)/shard_map/ppermute | solution.py:24
  42.1 4.6 %collective-permute-start.17 = (bf16[144,128]{1,0:T(8,128)(2,1)S(1)}, bf16[144,128]{1,0:T(8,128)(2,1)S(1)}, u32[]{:S(2)}, u32[]{:S(2)}) collective-permute-start(bf16[144,128]{1,0:T(8,128)(2,1)S(1)} %kept.1.refs_0_), channel_id=1, source_target_pairs={{0,24},{4,28},{8,16},{12,20},{16,8},{20,12},{24,0},{28,4},{1,25},{... | collective-permute-start | bytes 110600 | tf_op jit(solution)/shard_map/ppermute | solution.py:24
  43.2 3.5 %collective-permute-start.18 = (bf16[144,128]{1,0:T(8,128)(2,1)S(1)}, bf16[144,128]{1,0:T(8,128)(2,1)S(1)}, u32[]{:S(2)}, u32[]{:S(2)}) collective-permute-start(bf16[144,128]{1,0:T(8,128)(2,1)S(1)} %kept.1.refs_0_), channel_id=1, source_target_pairs={{0,8},{4,12},{8,0},{12,4},{16,24},{20,28},{24,16},{28,20},{1,9},{5... | collective-permute-start | bytes 110600 | tf_op jit(solution)/shard_map/ppermute | solution.py:24
  46.8 7.8 %collective-permute-start.19 = (bf16[576,128]{1,0:T(8,128)(2,1)S(1)}, bf16[576,128]{1,0:T(8,128)(2,1)S(1)}, u32[]{:S(2)}, u32[]{:S(2)}) collective-permute-start(bf16[576,128]{1,0:T(8,128)(2,1)S(1)} %join.5.group), channel_id=1, source_target_pairs={{0,4},{4,0},{8,12},{12,8},{16,20},{20,16},{24,28},{28,24},{1,5},{5... | collective-permute-start | bytes 442376 | tf_op jit(solution)/shard_map/ppermute | solution.py:24
